TPU v7x, 32 devices: a whole 2x2x4 slice. The times are simulated.
32 devices in a mesh: head: 2 (over core), seq: 16 (over z, y, x).
Axes of the slice: x: 2, y: 2, z: 4, core: 2. Of those that a mesh axis runs over, the one named last changes fastest.
Arguments:
- query_matrix: bfloat16 [32, 2048, 128], P(None, ('seq', 'head')), may hold values from -6 to 6
- key_matrix: bfloat16 [8, 2048, 128], P(None, ('seq', 'head')), may hold values from -6 to 6
- value_matrix: bfloat16 [8, 2048, 128], P(None, ('seq', 'head')), may hold values from -6 to 6
- output_gradient: bfloat16 [32, 2048, 128], P(None, ('seq', 'head')), may hold values from -6 to 6
- query_head_spans: int32 [32], replicated, may hold values from 64 to 256, as said below
- slab_offset: int32 [1], replicated, may hold values from 0 to 8191
Outputs:
- attn_out: bfloat16 [32, 2048, 128], P(None, ('seq', 'head'))
- query_grad: bfloat16 [32, 2048, 128], P(None, ('seq', 'head'))
- key_grad: bfloat16 [8, 2048, 128], P(None, ('seq', 'head'))
- value_grad: bfloat16 [8, 2048, 128], P(None, ('seq', 'head'))
Inputs may be any that keep to these rules, and one draw needn't show every extreme that they name: `query_head_spans`: every span is a multiple of 64; some head has the span 4 * 64 and some head the span 64.
All inputs are finite; a program needn't handle non-finite values.
Results may differ from a plain program's by a relative error of at most 0.019.
Values may be sent and summed in bfloat16 or wider, within the bound.
No kernel may reach another device: no remote copies, remote signals or barrier semaphores. Data moves between devices by JAX's collectives and lax.ppermute only.
A program may use at most 64 MiB of HBM per device.

v0:
```python
import jax
import jax.numpy as jnp
from jax import lax
from jax.sharding import PartitionSpec as P

REACH = 2
SEGMENT = 512


masked_score = -1e30


def shifted(block, axis, distance):
    devices = range(lax.axis_size(axis))
    route = [(i - distance, i) for i in devices if i - distance in devices]
    return lax.ppermute(block, axis, route)


def shards(query_matrix, key_matrix, value_matrix, output_gradient, query_head_spans, slab_offset):
    queries, keys_local, values_local, grads_in = (
        lax.all_to_all(query_matrix, "head", split_axis=0, concat_axis=1, tiled=True),
        lax.all_to_all(key_matrix, "head", split_axis=0, concat_axis=1, tiled=True),
        lax.all_to_all(value_matrix, "head", split_axis=0, concat_axis=1, tiled=True),
        lax.all_to_all(output_gradient, "head", split_axis=0, concat_axis=1, tiled=True),
    )
    heads_here = queries.shape[0]
    groups_here = keys_local.shape[0]
    heads_per_group = heads_here // groups_here
    block_length = queries.shape[1]
    head_size = queries.shape[2]
    score_scale = head_size ** (-0.5)
    head_index = lax.axis_index("head")
    seq_index = lax.axis_index("seq")
    span_per_row = lax.dynamic_slice_in_dim(
        query_head_spans, head_index * heads_here, heads_here
    ).reshape(groups_here, heads_per_group, 1, 1)
    doc_offset = slab_offset[0]
    query_grid = queries.reshape(groups_here, heads_per_group, block_length, head_size)
    grad_grid = grads_in.reshape(groups_here, heads_per_group, block_length, head_size)
    query_pos = seq_index * block_length + jnp.arange(block_length, dtype=jnp.int32)

    def visible_at(blocks_back):
        key_pos = (seq_index - blocks_back) * block_length + jnp.arange(
            block_length, dtype=jnp.int32
        )
        distance = query_pos[:, None] - key_pos[None, :]
        same_segment = (doc_offset + key_pos[None, :]) // SEGMENT == (
            doc_offset + query_pos[:, None]
        ) // SEGMENT
        inside = (distance >= 0) & (key_pos[None, :] >= 0) & same_segment
        return inside[None, None] & (distance[None, None] < span_per_row)

    def forward_step(online, key_block, value_block, blocks_back):
        visible = visible_at(blocks_back)

        def attend(carried):
            row_max, row_sum, weighted = carried
            scores = (
                jnp.einsum(
                    "gaqd,gkd->gaqk", query_grid, key_block, preferred_element_type=jnp.float32
                )
                * score_scale
            )
            new_max = jnp.maximum(
                row_max, jnp.max(jnp.where(visible, scores, masked_score), axis=-1, keepdims=True)
            )
            weights = jnp.where(visible, jnp.exp(scores - new_max), 0.0)
            factor = jnp.exp(row_max - new_max)
            row_sum = row_sum * factor + jnp.sum(weights, axis=-1, keepdims=True)
            weighted = weighted * factor + jnp.einsum(
                "gaqk,gkd->gaqd",
                weights.astype(jnp.bfloat16),
                value_block,
                preferred_element_type=jnp.float32,
            )
            return (new_max, row_sum, weighted)

        return lax.cond(jnp.any(visible), attend, lambda carried: carried, online)

    stat_shape = (groups_here, heads_per_group, block_length, 1)
    online = (
        jnp.full(stat_shape, masked_score, jnp.float32),
        jnp.zeros(stat_shape, jnp.float32),
        jnp.zeros(query_grid.shape, jnp.float32),
    )
    online = forward_step(online, keys_local, values_local, 0)
    offsets = [0]
    kept_keys = [keys_local]
    kept_values = [values_local]
    for bit_level in reversed(range(REACH.bit_length())):
        stride = 1 << bit_level
        chosen = [
            slot_index
            for slot_index in range(len(offsets))
            if offsets[slot_index] + stride <= REACH
        ]
        arrived = shifted(
            (
                jnp.stack([kept_keys[slot_index] for slot_index in chosen]),
                jnp.stack([kept_values[slot_index] for slot_index in chosen]),
            ),
            "seq",
            stride,
        )
        for slot_rank, slot_index in enumerate(chosen):
            kept_keys.append(arrived[0][slot_rank])
            kept_values.append(arrived[1][slot_rank])
            offsets.append(offsets[slot_index] + stride)
    ordering = [offsets.index(blocks_back) for blocks_back in range(REACH + 1)]
    window_keys = jnp.stack([kept_keys[slot_index] for slot_index in ordering])
    window_values = jnp.stack([kept_values[slot_index] for slot_index in ordering])
    online = lax.fori_loop(
        1,
        REACH + 1,
        lambda blocks_back, carried: forward_step(
            carried, window_keys[blocks_back], window_values[blocks_back], blocks_back
        ),
        online,
    )
    row_max, row_sum, weighted = online
    attn_grid = (weighted / row_sum).astype(jnp.bfloat16)
    log_total = row_max + jnp.log(row_sum)
    attn_out = lax.all_to_all(
        attn_grid.reshape(heads_here, block_length, head_size),
        "head",
        split_axis=1,
        concat_axis=0,
        tiled=True,
    )
    row_delta = jnp.sum(
        grad_grid.astype(jnp.float32) * attn_grid.astype(jnp.float32), axis=-1, keepdims=True
    )

    def backward_step(blocks_back, carried):
        visible = visible_at(blocks_back)
        key_block = window_keys[blocks_back]
        value_block = window_values[blocks_back]

        def differentiate(inner):
            query_acc, key_parts, value_parts = inner
            scores = (
                jnp.einsum(
                    "gaqd,gkd->gaqk", query_grid, key_block, preferred_element_type=jnp.float32
                )
                * score_scale
            )
            prob_rows = jnp.where(visible, jnp.exp(scores - log_total), 0.0)
            value_part = jnp.einsum(
                "gaqk,gaqd->gkd",
                prob_rows.astype(jnp.bfloat16),
                grad_grid,
                preferred_element_type=jnp.float32,
            )
            prob_grad = jnp.einsum(
                "gaqd,gkd->gaqk", grad_grid, value_block, preferred_element_type=jnp.float32
            )
            score_grad = (prob_rows * (prob_grad - row_delta) * score_scale).astype(jnp.bfloat16)
            query_acc = query_acc + jnp.einsum(
                "gaqk,gkd->gaqd", score_grad, key_block, preferred_element_type=jnp.float32
            )
            key_part = jnp.einsum(
                "gaqk,gaqd->gkd", score_grad, query_grid, preferred_element_type=jnp.float32
            )
            return (
                query_acc,
                key_parts.at[blocks_back].set(key_part),
                value_parts.at[blocks_back].set(value_part),
            )

        return lax.cond(jnp.any(visible), differentiate, lambda inner: inner, carried)

    part_shape = (REACH + 1, groups_here, block_length, head_size)
    query_acc, key_parts, value_parts = lax.fori_loop(
        0,
        REACH + 1,
        backward_step,
        (
            jnp.zeros(query_grid.shape, jnp.float32),
            jnp.zeros(part_shape, jnp.float32),
            jnp.zeros(part_shape, jnp.float32),
        ),
    )
    pending = list(range(REACH + 1))
    key_slots = [key_parts[blocks_back] for blocks_back in pending]
    value_slots = [value_parts[blocks_back] for blocks_back in pending]
    for bit_level in range(REACH.bit_length()):
        stride = 1 << bit_level
        senders = [blocks_back for blocks_back in pending if blocks_back // stride % 2 == 1]
        arrived = (
            shifted(
                jnp.stack([key_slots[blocks_back] for blocks_back in senders]).astype(jnp.bfloat16),
                "seq",
                -stride,
            ).astype(jnp.float32),
            shifted(
                jnp.stack([value_slots[blocks_back] for blocks_back in senders]).astype(
                    jnp.bfloat16
                ),
                "seq",
                -stride,
            ).astype(jnp.float32),
        )
        for slot_rank, blocks_back in enumerate(senders):
            key_slots[blocks_back - stride] = (
                key_slots[blocks_back - stride] + arrived[0][slot_rank]
            )
            value_slots[blocks_back - stride] = (
                value_slots[blocks_back - stride] + arrived[1][slot_rank]
            )
        pending = [blocks_back for blocks_back in pending if blocks_back not in senders]
    key_total = key_slots[0]
    value_total = value_slots[0]
    query_grad, key_grad, value_grad = (
        lax.all_to_all(
            query_acc.reshape(heads_here, block_length, head_size).astype(jnp.bfloat16),
            "head",
            split_axis=1,
            concat_axis=0,
            tiled=True,
        ),
        lax.all_to_all(
            key_total.astype(jnp.bfloat16), "head", split_axis=1, concat_axis=0, tiled=True
        ),
        lax.all_to_all(
            value_total.astype(jnp.bfloat16), "head", split_axis=1, concat_axis=0, tiled=True
        ),
    )
    return (attn_out, query_grad, key_grad, value_grad)


def solution(mesh):
    return jax.shard_map(
        shards,
        mesh=mesh,
        in_specs=(
            P(None, ("seq", "head"), None),
            P(None, ("seq", "head"), None),
            P(None, ("seq", "head"), None),
            P(None, ("seq", "head"), None),
            P(),
            P(),
        ),
        out_specs=(
            P(None, ("seq", "head"), None),
            P(None, ("seq", "head"), None),
            P(None, ("seq", "head"), None),
            P(None, ("seq", "head"), None),
        ),
        check_vma=False,
    )
```

profile of v0, /device:TPU:19, one launch (start us, length us, event | category | flops | bytes accessed | tf_op | source)
XLA Modules:
  0.0 117.9 jit_solution(4380437072795093184)
XLA Ops:
  0.6 5.2 %all_to_all.138 = bf16[8,64,128]{2,1,0:T(8,128)(2,1)S(1)} all-to-all(bf16[8,64,128]{2,1,0:T(8,128)(2,1)} %param.21), channel_id=1, replica_groups=mesh['head'=2,'seq'=16] {'head'}, dimensions={0} | all-to-all | bytes 262144 | tf_op jit(solution)/shard_map/all_to_all | solution.py:22
  5.8 3.3 %collective-permute-start.1 = (bf16[1,4,128,128]{3,2,1,0:T(8,128)(2,1)S(1)}, bf16[1,4,128,128]{3,2,1,0:T(8,128)(2,1)S(1)}, u32[]{:S(2)}, u32[]{:S(2)}) collective-permute-start(bf16[1,4,128,128]{3,2,1,0:T(8,128)(2,1)S(1)} %bitcast.169), channel_id=1, source_target_pairs={{0,2},{1,3},{2,4},{3,5},{4,6},{5,7},{6,8},{7,9},{8,10},{9,11},{10,... | collective-permute-start | bytes 393224 | tf_op jit(solution)/shard_map/ppermute | solution.py:16
  9.1 3.1 %collective-permute-start = (bf16[1,4,128,128]{3,2,1,0:T(8,128)(2,1)S(1)}, bf16[1,4,128,128]{3,2,1,0:T(8,128)(2,1)}, u32[]{:S(2)}, u32[]{:S(2)}) collective-permute-start(bf16[1,4,128,128]{3,2,1,0:T(8,128)(2,1)S(1)} %bitcast.170), channel_id=1, source_target_pairs={{0,1},{1,2},{2,3},{3,4},{4,5},{5,6},{6,7},{7,8},{8,9},{9,10},{10,1... | collective-permute-start | bytes 393224 | tf_op jit(solution)/shard_map/ppermute | solution.py:16
  12.2 4.4 %all_to_all.139 = bf16[8,64,128]{2,1,0:T(8,128)(2,1)S(1)} all-to-all(bf16[8,64,128]{2,1,0:T(8,128)(2,1)S(1)} %copy-done.7), channel_id=1, replica_groups=mesh['head'=2,'seq'=16] {'head'}, dimensions={0} | all-to-all | bytes 262144 | tf_op jit(solution)/shard_map/all_to_all | solution.py:23
  16.6 3.1 %collective-permute-start.3 = (bf16[1,4,128,128]{3,2,1,0:T(8,128)(2,1)S(1)}, bf16[1,4,128,128]{3,2,1,0:T(8,128)(2,1)S(1)}, u32[]{:S(2)}, u32[]{:S(2)}) collective-permute-start(bf16[1,4,128,128]{3,2,1,0:T(8,128)(2,1)S(1)} %bitcast.172), channel_id=1, source_target_pairs={{0,2},{1,3},{2,4},{3,5},{4,6},{5,7},{6,8},{7,9},{8,10},{9,11},{10,... | collective-permute-start | bytes 393224 | tf_op jit(solution)/shard_map/ppermute | solution.py:16
  19.8 3.1 %collective-permute-start.2 = (bf16[1,4,128,128]{3,2,1,0:T(8,128)(2,1)S(1)}, bf16[1,4,128,128]{3,2,1,0:T(8,128)(2,1)}, u32[]{:S(2)}, u32[]{:S(2)}) collective-permute-start(bf16[1,4,128,128]{3,2,1,0:T(8,128)(2,1)S(1)} %bitcast.173), channel_id=1, source_target_pairs={{0,1},{1,2},{2,3},{3,4},{4,5},{5,6},{6,7},{7,8},{8,9},{9,10},{10,1... | collective-permute-start | bytes 393224 | tf_op jit(solution)/shard_map/ppermute | solution.py:16
  22.9 4.4 %all-to-all-start.1 = ((bf16[32,64,128]{2,1,0:T(8,128)(2,1)}), bf16[32,64,128]{2,1,0:T(8,128)(2,1)S(1)}, u32[]{:S(2)}, u32[]{:S(2)}) async-start(bf16[32,64,128]{2,1,0:T(8,128)(2,1)} %param.20), calls=%async_computation.1 | async-start | bytes 1048576 | tf_op jit(solution)/shard_map/all_to_all | solution.py:21
  30.1 3.5 %all-to-all-start.4 = ((bf16[32,64,128]{2,1,0:T(8,128)(2,1)}), bf16[32,64,128]{2,1,0:T(8,128)(2,1)S(1)}, u32[]{:S(2)}, u32[]{:S(2)}) async-start(bf16[32,64,128]{2,1,0:T(8,128)(2,1)} %param.23), calls=%async_computation.4 | async-start | bytes 1048576 | tf_op jit(solution)/shard_map/all_to_all | solution.py:24
  39.1 8.1 %while.45 = (s32[]{:T(128)}, f32[4,4,128,1]{2,1,0,3:T(4,128)S(1)}, f32[4,4,128,1]{2,1,0,3:T(4,128)S(1)}, f32[4,4,128,128]{3,2,1,0:T(8,128)S(1)}, s32[]{:T(128)},...) while((s32[]{:T(128)}, f32[4,4,128,1]{2,1,0,3:T(4,128)S(1)}, ...), condition=%wide.region_11.12_spmd.clone, body=%wide.region_5.11_spmd.clone.sunk | while | flops 137997056 | bytes 7378597 | solution.py:112
  49.7 29.8 %while.46 = (s32[]{:T(128)}, f32[4,4,128,128]{3,2,1,0:T(8,128)S(1)}, f32[3,4,128,128]{3,2,1,0:T(8,128)S(1)}, f32[3,4,128,128]{3,2,1,0:T(8,128)}, s32[]{:T(128)},...) while((s32[]{:T(128)}, ...), condition=%wide.region_18.19_spmd.clone, body=%wide.region_13.18_spmd.clone.sunk | while | flops 338924320 | bytes 17357756 | solution.py:173
  51.2 1.7 %fusion.72 = (pred[]{:T(512)}, pred[4,4,128,128]{2,3,1,0:T(32,128)(4,1)S(1)}) fusion(s32[4,4]{1,0:T(4,128)} %bitcast.181, s32[128,128]{0,1:T(8,128)S(1)} %broadcast_subtract_fusion.6, pred[128,128]{0,1:T(8,128)(4,1)S(1)} %compare_and_fusion.12), kind=kLoop, calls=%fused_computation.116.clone.1 | loop fusion | flops 786431 | bytes 344129 | tf_op jit(solution)/shard_map/while/body/eval_jaxpr/reduce_or | solution.py:170
  53.5 5.5 %conditional.9 = ((f32[4,4,128,128]{3,2,1,0:T(8,128)S(1)}, f32[3,4,128,128]{3,2,1,0:T(8,128)S(1)}, f32[3,4,128,128]{3,2,1,0:T(8,128)})) conditional(s32[]{:T(128)} %convert_element_type.139, (f32[4,4,128,128]{3,2,1,0:T(8,128)S(1)}, f32[3,4,128,128]{3,2,1,0:T(8,128)S(1)}, f32[3,4,128,128]{3,2,1,0:T(8,128)}) %tuple.183, (s32[]{:T(128)}, ...), branch_computations={%region_15.15_spmd, %region_16.17_spmd} | conditional | flops 338034720 | bytes 16925440 | solution.py:170
  63.5 5.5 %conditional.9 = ((f32[4,4,128,128]{3,2,1,0:T(8,128)S(1)}, f32[3,4,128,128]{3,2,1,0:T(8,128)S(1)}, f32[3,4,128,128]{3,2,1,0:T(8,128)})) conditional(s32[]{:T(128)} %convert_element_type.139, (f32[4,4,128,128]{3,2,1,0:T(8,128)S(1)}, f32[3,4,128,128]{3,2,1,0:T(8,128)S(1)}, f32[3,4,128,128]{3,2,1,0:T(8,128)}) %tuple.183, (s32[]{:T(128)}, ...), branch_computations={%region_15.15_spmd, %region_16.17_spmd} | conditional | flops 338034720 | bytes 16925440 | solution.py:170
  73.4 5.5 %conditional.9 = ((f32[4,4,128,128]{3,2,1,0:T(8,128)S(1)}, f32[3,4,128,128]{3,2,1,0:T(8,128)S(1)}, f32[3,4,128,128]{3,2,1,0:T(8,128)})) conditional(s32[]{:T(128)} %convert_element_type.139, (f32[4,4,128,128]{3,2,1,0:T(8,128)S(1)}, f32[3,4,128,128]{3,2,1,0:T(8,128)S(1)}, f32[3,4,128,128]{3,2,1,0:T(8,128)}) %tuple.183, (s32[]{:T(128)}, ...), branch_computations={%region_15.15_spmd, %region_16.17_spmd} | conditional | flops 338034720 | bytes 16925440 | solution.py:170
  79.6 1.7 %copy.75 = bf16[3,4,128,128]{3,1,2,0:T(4,128)(2,1)S(1)} copy(f32[3,4,128,128]{3,2,1,0:T(8,128)} %get-tuple-element.1073) | data formatting | bytes 1179648 | tf_op jit(solution)/shard_map/while | solution.py:173
  83.8 4.2 %all_to_all.140 = bf16[16,128,128]{2,0,1:T(8,128)(2,1)S(1)} all-to-all(bf16[16,128,128]{2,0,1:T(8,128)(2,1)S(1)} %bitcast.153), channel_id=1, replica_groups=mesh['head'=2,'seq'=16] {'head'}, dimensions={1} | all-to-all | bytes 1048576 | tf_op jit(solution)/shard_map/all_to_all | solution.py:123
  89.4 4.2 %all_to_all.141 = bf16[16,128,128]{2,0,1:T(8,128)(2,1)S(1)} all-to-all(bf16[16,128,128]{2,0,1:T(8,128)(2,1)S(1)} %bitcast.155), channel_id=1, replica_groups=mesh['head'=2,'seq'=16] {'head'}, dimensions={1} | all-to-all | bytes 1048576 | tf_op jit(solution)/shard_map/all_to_all | solution.py:214
  94.6 2.2 %collective-permute-start.6 = (bf16[1,4,128,128]{3,1,2,0:T(4,128)(2,1)S(1)}, bf16[1,4,128,128]{3,1,2,0:T(4,128)(2,1)S(1)}, u32[]{:S(2)}, u32[]{:S(2)}) collective-permute-start(bf16[1,4,128,128]{3,1,2,0:T(4,128)(2,1)S(1)} %get-tuple-element.1224), channel_id=1, source_target_pairs={{1,0},{2,1},{3,2},{4,3},{5,4},{6,5},{7,6},{8,7},{9,8},{10,9},{11,1... | collective-permute-start | bytes 393224 | tf_op jit(solution)/shard_map/ppermute | solution.py:16
  96.7 3.0 %collective-permute-start.7 = (bf16[1,4,128,128]{3,1,2,0:T(4,128)(2,1)S(1)}, bf16[1,4,128,128]{3,1,2,0:T(4,128)(2,1)S(1)}, u32[]{:S(2)}, u32[]{:S(2)}) collective-permute-start(bf16[1,4,128,128]{3,1,2,0:T(4,128)(2,1)S(1)} %get-tuple-element.1225), channel_id=1, source_target_pairs={{2,0},{3,1},{4,2},{5,3},{6,4},{7,5},{8,6},{9,7},{10,8},{11,9},{12,... | collective-permute-start | bytes 393224 | tf_op jit(solution)/shard_map/ppermute | solution.py:16
  99.9 3.1 %collective-permute-start.4 = (bf16[1,4,128,128]{3,1,2,0:T(4,128)(2,1)S(1)}, bf16[1,4,128,128]{3,1,2,0:T(4,128)(2,1)S(1)}, u32[]{:S(2)}, u32[]{:S(2)}) collective-permute-start(bf16[1,4,128,128]{3,1,2,0:T(4,128)(2,1)S(1)} %get-tuple-element.1226), channel_id=1, source_target_pairs={{1,0},{2,1},{3,2},{4,3},{5,4},{6,5},{7,6},{8,7},{9,8},{10,9},{11,1... | collective-permute-start | bytes 393224 | tf_op jit(solution)/shard_map/ppermute | solution.py:16
  102.9 1.9 %collective-permute-start.5 = (bf16[1,4,128,128]{3,1,2,0:T(4,128)(2,1)S(1)}, bf16[1,4,128,128]{3,1,2,0:T(4,128)(2,1)S(1)}, u32[]{:S(2)}, u32[]{:S(2)}) collective-permute-start(bf16[1,4,128,128]{3,1,2,0:T(4,128)(2,1)S(1)} %get-tuple-element.1227), channel_id=1, source_target_pairs={{2,0},{3,1},{4,2},{5,3},{6,4},{7,5},{8,6},{9,7},{10,8},{11,9},{12,... | collective-permute-start | bytes 393224 | tf_op jit(solution)/shard_map/ppermute | solution.py:16
  104.9 3.5 %collective-permute-done.7 = bf16[1,4,128,128]{3,1,2,0:T(4,128)(2,1)S(1)} collective-permute-done((bf16[1,4,128,128]{3,1,2,0:T(4,128)(2,1)S(1)}, bf16[1,4,128,128]{3,1,2,0:T(4,128)(2,1)S(1)}, u32[]{:S(2)}, u32[]{:S(2)}) %collective-permute-start.7) | collective-permute-done | bytes 131104 | tf_op jit(solution)/shard_map/ppermute | solution.py:16
  108.5 4.1 %all_to_all.142 = bf16[4,128,128]{2,0,1:T(4,128)(2,1)S(1)} all-to-all(bf16[4,128,128]{2,0,1:T(4,128)(2,1)S(1)} %fusion.52), channel_id=1, replica_groups=mesh['head'=2,'seq'=16] {'head'}, dimensions={1} | all-to-all | bytes 262144 | tf_op jit(solution)/shard_map/all_to_all | solution.py:224
  113.4 3.8 %all_to_all.143 = bf16[4,128,128]{2,0,1:T(4,128)(2,1)S(1)} all-to-all(bf16[4,128,128]{2,0,1:T(4,128)(2,1)S(1)} %fusion.51), channel_id=1, replica_groups=mesh['head'=2,'seq'=16] {'head'}, dimensions={1} | all-to-all | bytes 262144 | tf_op jit(solution)/shard_map/all_to_all | solution.py:221
  (151 shorter events, 52.7 us)
Async XLA Ops:
  5.8 6.4 %copy-start.7 = (bf16[8,64,128]{2,1,0:T(8,128)(2,1)S(1)}, bf16[8,64,128]{2,1,0:T(8,128)(2,1)}, u32[]{:S(2)}) copy-start(bf16[8,64,128]{2,1,0:T(8,128)(2,1)} %param.22) | copy-start | bytes 393220
  5.8 31.4 %collective-permute-start.1 = (bf16[1,4,128,128]{3,2,1,0:T(8,128)(2,1)S(1)}, bf16[1,4,128,128]{3,2,1,0:T(8,128)(2,1)S(1)}, u32[]{:S(2)}, u32[]{:S(2)}) collective-permute-start(bf16[1,4,128,128]{3,2,1,0:T(8,128)(2,1)S(1)} %bitcast.169), channel_id=1, source_target_pairs={{0,2},{1,3},{2,4},{3,5},{4,6},{5,7},{6,8},{7,9},{8,10},{9,11},{10,... | collective-permute-start | bytes 393224 | tf_op jit(solution)/shard_map/ppermute | solution.py:16
  9.1 28.1 %collective-permute-start = (bf16[1,4,128,128]{3,2,1,0:T(8,128)(2,1)S(1)}, bf16[1,4,128,128]{3,2,1,0:T(8,128)(2,1)}, u32[]{:S(2)}, u32[]{:S(2)}) collective-permute-start(bf16[1,4,128,128]{3,2,1,0:T(8,128)(2,1)S(1)} %bitcast.170), channel_id=1, source_target_pairs={{0,1},{1,2},{2,3},{3,4},{4,5},{5,6},{6,7},{7,8},{8,9},{9,10},{10,1... | collective-permute-start | bytes 393224 | tf_op jit(solution)/shard_map/ppermute | solution.py:16
  16.6 21.5 %collective-permute-start.3 = (bf16[1,4,128,128]{3,2,1,0:T(8,128)(2,1)S(1)}, bf16[1,4,128,128]{3,2,1,0:T(8,128)(2,1)S(1)}, u32[]{:S(2)}, u32[]{:S(2)}) collective-permute-start(bf16[1,4,128,128]{3,2,1,0:T(8,128)(2,1)S(1)} %bitcast.172), channel_id=1, source_target_pairs={{0,2},{1,3},{2,4},{3,5},{4,6},{5,7},{6,8},{7,9},{8,10},{9,11},{10,... | collective-permute-start | bytes 393224 | tf_op jit(solution)/shard_map/ppermute | solution.py:16
  19.8 18.3 %collective-permute-start.2 = (bf16[1,4,128,128]{3,2,1,0:T(8,128)(2,1)S(1)}, bf16[1,4,128,128]{3,2,1,0:T(8,128)(2,1)}, u32[]{:S(2)}, u32[]{:S(2)}) collective-permute-start(bf16[1,4,128,128]{3,2,1,0:T(8,128)(2,1)S(1)} %bitcast.173), channel_id=1, source_target_pairs={{0,1},{1,2},{2,3},{3,4},{4,5},{5,6},{6,7},{7,8},{8,9},{9,10},{10,1... | collective-permute-start | bytes 393224 | tf_op jit(solution)/shard_map/ppermute | solution.py:16
  22.9 7.2 %all-to-all-start.1 = ((bf16[32,64,128]{2,1,0:T(8,128)(2,1)}), bf16[32,64,128]{2,1,0:T(8,128)(2,1)S(1)}, u32[]{:S(2)}, u32[]{:S(2)}) async-start(bf16[32,64,128]{2,1,0:T(8,128)(2,1)} %param.20), calls=%async_computation.1 | async-start | bytes 1048576 | tf_op jit(solution)/shard_map/all_to_all | solution.py:21
  30.1 4.9 %all-to-all-start.4 = ((bf16[32,64,128]{2,1,0:T(8,128)(2,1)}), bf16[32,64,128]{2,1,0:T(8,128)(2,1)S(1)}, u32[]{:S(2)}, u32[]{:S(2)}) async-start(bf16[32,64,128]{2,1,0:T(8,128)(2,1)} %param.23), calls=%async_computation.4 | async-start | bytes 1048576 | tf_op jit(solution)/shard_map/all_to_all | solution.py:24
  47.2 1.4 %copy-start.3 = (bf16[3,4,128,128]{3,2,1,0:T(8,128)(2,1)}, bf16[3,4,128,128]{3,2,1,0:T(8,128)(2,1)S(1)}, u32[]{:S(2)}) copy-start(bf16[3,4,128,128]{3,2,1,0:T(8,128)(2,1)S(1)} %get-tuple-element.1531) | copy-start | bytes 1179652
  55.4 1.3 %copy-start = (f32[3,4,128,128]{3,2,1,0:T(8,128)S(1)}, f32[3,4,128,128]{3,2,1,0:T(8,128)}, u32[]{:S(2)}) copy-start(f32[3,4,128,128]{3,2,1,0:T(8,128)} %get-tuple-element.1033) | copy-start | bytes 2359300 | tf_op jit(solution)/shard_map/while/body/eval_jaxpr/cond
  57.6 0.9 copy-start.1
  59.0 0.7 copy-start.6
  63.5 0.7 copy-start.8
  65.3 1.3 %copy-start = (f32[3,4,128,128]{3,2,1,0:T(8,128)S(1)}, f32[3,4,128,128]{3,2,1,0:T(8,128)}, u32[]{:S(2)}) copy-start(f32[3,4,128,128]{3,2,1,0:T(8,128)} %get-tuple-element.1033) | copy-start | bytes 2359300 | tf_op jit(solution)/shard_map/while/body/eval_jaxpr/cond
  67.5 0.9 copy-start.1
  68.9 0.7 copy-start.6
  75.2 1.3 %copy-start = (f32[3,4,128,128]{3,2,1,0:T(8,128)S(1)}, f32[3,4,128,128]{3,2,1,0:T(8,128)}, u32[]{:S(2)}) copy-start(f32[3,4,128,128]{3,2,1,0:T(8,128)} %get-tuple-element.1033) | copy-start | bytes 2359300 | tf_op jit(solution)/shard_map/while/body/eval_jaxpr/cond
  77.5 0.9 copy-start.1
  78.9 0.7 copy-start.6
  79.6 1.7 %copy-start.2 = (f32[3,4,128,128]{3,2,1,0:T(8,128)S(1)}, f32[3,4,128,128]{3,2,1,0:T(8,128)}, u32[]{:S(2)}) copy-start(f32[3,4,128,128]{3,2,1,0:T(8,128)} %get-tuple-element.1073) | copy-start | bytes 2359300
  82.3 1.0 copy-start.4
  94.6 10.3 %collective-permute-start.6 = (bf16[1,4,128,128]{3,1,2,0:T(4,128)(2,1)S(1)}, bf16[1,4,128,128]{3,1,2,0:T(4,128)(2,1)S(1)}, u32[]{:S(2)}, u32[]{:S(2)}) collective-permute-start(bf16[1,4,128,128]{3,1,2,0:T(4,128)(2,1)S(1)} %get-tuple-element.1224), channel_id=1, source_target_pairs={{1,0},{2,1},{3,2},{4,3},{5,4},{6,5},{7,6},{8,7},{9,8},{10,9},{11,1... | collective-permute-start | bytes 393224 | tf_op jit(solution)/shard_map/ppermute | solution.py:16
  96.7 11.7 %collective-permute-start.7 = (bf16[1,4,128,128]{3,1,2,0:T(4,128)(2,1)S(1)}, bf16[1,4,128,128]{3,1,2,0:T(4,128)(2,1)S(1)}, u32[]{:S(2)}, u32[]{:S(2)}) collective-permute-start(bf16[1,4,128,128]{3,1,2,0:T(4,128)(2,1)S(1)} %get-tuple-element.1225), channel_id=1, source_target_pairs={{2,0},{3,1},{4,2},{5,3},{6,4},{7,5},{8,6},{9,7},{10,8},{11,9},{12,... | collective-permute-start | bytes 393224 | tf_op jit(solution)/shard_map/ppermute | solution.py:16
  99.9 13.4 %collective-permute-start.4 = (bf16[1,4,128,128]{3,1,2,0:T(4,128)(2,1)S(1)}, bf16[1,4,128,128]{3,1,2,0:T(4,128)(2,1)S(1)}, u32[]{:S(2)}, u32[]{:S(2)}) collective-permute-start(bf16[1,4,128,128]{3,1,2,0:T(4,128)(2,1)S(1)} %get-tuple-element.1226), channel_id=1, source_target_pairs={{1,0},{2,1},{3,2},{4,3},{5,4},{6,5},{7,6},{8,7},{9,8},{10,9},{11,1... | collective-permute-start | bytes 393224 | tf_op jit(solution)/shard_map/ppermute | solution.py:16
  102.9 10.3 %collective-permute-start.5 = (bf16[1,4,128,128]{3,1,2,0:T(4,128)(2,1)S(1)}, bf16[1,4,128,128]{3,1,2,0:T(4,128)(2,1)S(1)}, u32[]{:S(2)}, u32[]{:S(2)}) collective-permute-start(bf16[1,4,128,128]{3,1,2,0:T(4,128)(2,1)S(1)} %get-tuple-element.1227), channel_id=1, source_target_pairs={{2,0},{3,1},{4,2},{5,3},{6,4},{7,5},{8,6},{9,7},{10,8},{11,9},{12,... | collective-permute-start | bytes 393224 | tf_op jit(solution)/shard_map/ppermute | solution.py:16
  (6 other events, 3.7 us)
where the time goes:
time: 119 us; the launch traced here: 118 us
  starting transfers between devices  30.8 us (26%)
  blocking collectives  25.8 us (22%)
  other arithmetic  19.2 us (16%)
  local copies, waits for them, and re-layouts  15.8 us (13%)
  matrix products  15.3 us (13%)
  waiting for transfers between devices  4.86 us (4%)
  loops' own time  3.89 us (3%)
  between operations  2.24 us (2%)
    ppermute x8, starting transfers between devices, shifted(): return lax.ppermute(block, axis, route)  22.8 us
    all_to_all x1, blocking collectives, shards(): lax.all_to_all(key_matrix, 'head', split_axis=0, concat_axis=1, tiled=True)  5.16 us
    reduce_or x3, other arithmetic, backward_step(): jnp.any(visible)  5.08 us
    all_to_all x1, starting transfers between devices, shards(): lax.all_to_all(query_matrix, 'head', split_axis=0, concat_axis=1, tiled=T...  4.4 us
    all_to_all x1, blocking collectives, shards(): lax.all_to_all(value_matrix, 'head', split_axis=0, concat_axis=1, tiled=T...  4.4 us
    all_to_all x1, blocking collectives, shards(): lax.all_to_all(attn_grid.reshape(heads_here, block_length, head_size), 'h...  4.16 us
    all_to_all x1, blocking collectives, shards(): lax.all_to_all(query_acc.reshape(heads_here, block_length, head_size).ast...  4.15 us
    all_to_all x1, blocking collectives, shards(): lax.all_to_all(value_total.astype(jnp.bfloat16), 'head', split_axis=1, co...  4.07 us
  transfers between devices with their start and end apart: 10, of which 2 were waited for; matrix products, arithmetic and copies ran while one was open for 4% of the time, Pallas kernels for 0%

commit v1 on v0

v1 whole, which is shorter than its diff:
```python
import math

import jax
import jax.numpy as jnp
from jax import lax
from jax.experimental import pallas as pl
from jax.experimental.pallas import tpu as pltpu
from jax.sharding import PartitionSpec as P

REACH = 2
SEGMENT = 512

masked_score = -1e30


def shifted(block, axis, distance):
    devices = range(lax.axis_size(axis))
    route = [(i - distance, i) for i in devices if i - distance in devices]
    return lax.ppermute(block, axis, route)


def swapped(block, axis):
    count = lax.axis_size(axis)
    return lax.ppermute(block, axis, [(i, count - 1 - i) for i in range(count)])


def matmul(left, right, contract):
    return lax.dot_general(
        left, right, ((contract[:1], contract[1:]), ((), ())), preferred_element_type=jnp.float32
    )


def attention_kernel(
    spans, offset, queries, keys, values, grads, back_two, back_four, back_odd,
    out, query_grad, odd_parts, own_part, two_part, four_part,
):
    groups, length, width = keys.shape
    per_group = queries.shape[0] // groups
    lanes = per_group * length
    scale = width ** (-0.5)
    start = (lax.axis_index("seq") * lax.axis_size("head") + lax.axis_index("head")) * length
    blocks = 2 * REACH + 1
    lane = lax.broadcasted_iota(jnp.int32, (1, lanes), 1)
    lane_head = lane // length
    lane_token = lane - lane_head * length
    row = lax.broadcasted_iota(jnp.int32, (length, lanes), 0)
    query_pos = start + lane_token
    doc_pos = offset[0] + query_pos
    segment_start = query_pos - lax.bitwise_and(doc_pos, SEGMENT - 1)
    floor = jnp.maximum(segment_start, 0)
    window_start = start - (blocks - 1) * length

    for g in range(groups):
        span = jnp.full((1, lanes), spans[g * per_group], jnp.int32)
        for a in range(1, per_group):
            span = jnp.where(lane_head == a, spans[g * per_group + a], span)
        first = jnp.maximum(floor, query_pos - span + 1) - window_start
        window_keys = jnp.concatenate(
            [back_four[0, g], back_odd[1, 0, g], back_two[0, g], back_odd[0, 0, g], keys[g]], axis=0
        )
        window_values = jnp.concatenate(
            [back_four[1, g], back_odd[1, 1, g], back_two[1, g], back_odd[0, 1, g], values[g]], axis=0
        )
        rows = pl.ds(g * per_group, per_group)
        query = queries[rows].reshape(lanes, width)
        grad = grads[rows].reshape(lanes, width)
        scores = matmul(window_keys, query, (1, 1)) * (scale * math.log2(math.e))
        parts = []
        for b in range(blocks):
            visible = row >= first - b * length
            if b == blocks - 1:
                visible = visible & (row <= lane_token)
            parts.append(
                jnp.where(visible, scores[b * length : (b + 1) * length], masked_score)
            )
        scores = jnp.concatenate(parts, axis=0)
        row_max = jnp.max(scores, axis=0, keepdims=True)
        weights = jnp.exp2(scores - row_max)
        inverse = 1.0 / jnp.sum(weights, axis=0, keepdims=True)
        weighted = matmul(window_values, weights.astype(jnp.bfloat16), (0, 0))
        attended = (weighted * inverse).astype(jnp.bfloat16)
        out[rows] = attended.T.reshape(per_group, length, width)
        delta = jnp.sum(
            grad.T.astype(jnp.float32) * attended.astype(jnp.float32), axis=0, keepdims=True
        )
        prob = weights * inverse
        value_part = matmul(prob.astype(jnp.bfloat16), grad, (1, 0))
        prob_grad = matmul(window_values, grad, (1, 1))
        score_grad = (prob * (prob_grad - delta) * scale).astype(jnp.bfloat16)
        key_part = matmul(score_grad, query, (1, 0))
        query_part = matmul(window_keys, score_grad, (0, 0)).astype(jnp.bfloat16)
        query_grad[rows] = query_part.T.reshape(per_group, length, width)
        for index, part in enumerate((key_part, value_part)):
            four, three, two, one, own = (
                part[b * length : (b + 1) * length] for b in range(blocks)
            )
            odd_parts[0, index, g] = one.astype(jnp.bfloat16)
            odd_parts[1, index, g] = three.astype(jnp.bfloat16)
            own_part[index, g] = own
            two_part[index, g] = two
            four_part[index, g] = four


def merge_kernel(odd_parts, own_part, two_part, four_part, own_sum, two_sum, four_sum):
    first_core = lax.axis_index("head") == 0

    @pl.when(first_core)
    def _():
        own_sum[...] = own_part[...] + odd_parts[0].astype(jnp.float32)
        two_sum[...] = (two_part[...] + odd_parts[1].astype(jnp.float32)).astype(jnp.bfloat16)
        four_sum[...] = four_part[...].astype(jnp.bfloat16)

    @pl.when(jnp.logical_not(first_core))
    def _():
        own_sum[...] = own_part[...]
        two_sum[...] = (two_part[...] + odd_parts[0].astype(jnp.float32)).astype(jnp.bfloat16)
        four_sum[...] = (four_part[...] + odd_parts[1].astype(jnp.float32)).astype(jnp.bfloat16)


def final_kernel(own_sum, two_sum, four_sum, key_grad, value_grad):
    for index, result in enumerate((key_grad, value_grad)):
        total = own_sum[index] + two_sum[index].astype(jnp.float32)
        result[...] = (total + four_sum[index].astype(jnp.float32)).astype(jnp.bfloat16)


def shards(query_matrix, key_matrix, value_matrix, output_gradient, query_head_spans, slab_offset):
    groups, length, width = key_matrix.shape
    pair_shape = (2, groups, length, width)
    smem = pl.BlockSpec(memory_space=pltpu.SMEM)
    vmem = pl.BlockSpec(memory_space=pltpu.VMEM)
    params = pltpu.CompilerParams(vmem_limit_bytes=48 * 1024 * 1024)
    own = jnp.stack([key_matrix, value_matrix])
    back_four = shifted(own, "seq", 2)
    back_two = shifted(own, "seq", 1)
    first_core = lax.axis_index("head") == 0
    back_odd = swapped(
        jnp.stack(
            [
                jnp.where(first_core, own, back_two),
                jnp.where(first_core, back_two, back_four),
            ]
        ),
        "head",
    )
    half = jax.ShapeDtypeStruct(pair_shape, jnp.bfloat16)
    full = jax.ShapeDtypeStruct(pair_shape, jnp.float32)
    attn_out, query_grad, odd_parts, own_part, two_part, four_part = pl.pallas_call(
        attention_kernel,
        out_shape=(
            jax.ShapeDtypeStruct(query_matrix.shape, jnp.bfloat16),
            jax.ShapeDtypeStruct(query_matrix.shape, jnp.bfloat16),
            jax.ShapeDtypeStruct((2,) + pair_shape, jnp.bfloat16),
            full,
            full,
            full,
        ),
        in_specs=[smem, smem] + [vmem] * 7,
        out_specs=(vmem,) * 6,
        compiler_params=params,
        name="attention",
    )(
        query_head_spans, slab_offset, query_matrix, key_matrix, value_matrix, output_gradient,
        back_two, back_four, back_odd,
    )
    own_sum, two_sum, four_sum = pl.pallas_call(
        merge_kernel,
        out_shape=(full, half, half),
        in_specs=[vmem] * 4,
        out_specs=(vmem,) * 3,
        compiler_params=params,
        name="merge",
    )(swapped(odd_parts, "head"), own_part, two_part, four_part)
    four_sum = shifted(four_sum, "seq", -2)
    two_sum = shifted(two_sum, "seq", -1)
    key_grad, value_grad = pl.pallas_call(
        final_kernel,
        out_shape=(jax.ShapeDtypeStruct(key_matrix.shape, jnp.bfloat16),) * 2,
        in_specs=[vmem] * 3,
        out_specs=(vmem,) * 2,
        compiler_params=params,
        name="total",
    )(own_sum, two_sum, four_sum)
    return (attn_out, query_grad, key_grad, value_grad)


def solution(mesh):
    tokens = P(None, ("seq", "head"), None)
    return jax.shard_map(
        shards,
        mesh=mesh,
        in_specs=(tokens, tokens, tokens, tokens, P(), P()),
        out_specs=(tokens, tokens, tokens, tokens),
        check_vma=False,
    )
```

time: 119 us -> 47.2 us (0.40)
  the two profiles are of different devices: /device:TPU:19 before, /device:TPU:4 now
where the time goes in v1:
time: 47.2 us; the launch traced here: 46.9 us
  waiting for transfers between devices  26.2 us (56%)
  starting transfers between devices  10.9 us (23%)
  Pallas kernels  7.24 us (15%)
  between operations  1.48 us (3%)
  other arithmetic  1.14 us (2%)
    ppermute x4, waiting for transfers between devices, shifted(): return lax.ppermute(block, axis, route)  23.2 us
    ppermute x4, starting transfers between devices, shifted(): return lax.ppermute(block, axis, route)  10.7 us
    pallas_call x1, Pallas kernels, shards(): pl.pallas_call(attention_kernel, out_shape=(jax.ShapeDtypeStruct(query_ma...  6.37 us
    ppermute x2, waiting for transfers between devices, swapped(): return lax.ppermute(block, axis, [(i, count - 1 - i) for i in range(count)])  2.95 us
    another operation x1, other arithmetic, shards(): own = jnp.stack([key_matrix, value_matrix])  1.04 us
  transfers between devices with their start and end apart: 6, of which 5 were waited for; matrix products, arithmetic and copies ran while one was open for 0% of the time, Pallas kernels for 0%

profile of v1, /device:TPU:4, one launch (start us, length us, event | category | flops | bytes accessed | tf_op | source)
XLA Modules:
  0.0 46.9 jit_solution(6890468292792384582)
XLA Ops:
  0.6 0.0 copy-start
  0.6 0.0 copy-start.1
  0.7 1.0 %pad_maximum_fusion.1 = bf16[2,8,64,128]{3,2,1,0:T(8,128)(2,1)S(1)} fusion(bf16[1,8,64,128]{3,2,1,0:T(8,128)(2,1)} %bitcast.8, bf16[1,8,64,128]{3,2,1,0:T(8,128)(2,1)} %bitcast.6), kind=kLoop, calls=%fused_computation.1 | loop fusion | flops 131072 | bytes 524288 | tf_op jit(solution)/shard_map/stack | solution.py:132
  1.7 3.4 %collective-permute-start.1 = (bf16[2,8,64,128]{3,2,1,0:T(8,128)(2,1)S(1)}, bf16[2,8,64,128]{3,2,1,0:T(8,128)(2,1)S(1)}, u32[]{:S(2)}, u32[]{:S(2)}) collective-permute-start(bf16[2,8,64,128]{3,2,1,0:T(8,128)(2,1)S(1)} %pad_maximum_fusion.1), channel_id=1, source_target_pairs={{0,2},{1,3},{2,4},{3,5},{4,6},{5,7},{6,8},{7,9},{8,10},{9,11},{10,... | collective-permute-start | bytes 786440 | tf_op jit(solution)/shard_map/ppermute | solution.py:19
  5.1 3.4 %collective-permute-start = (bf16[2,8,64,128]{3,2,1,0:T(8,128)(2,1)S(1)}, bf16[2,8,64,128]{3,2,1,0:T(8,128)(2,1)S(1)}, u32[]{:S(2)}, u32[]{:S(2)}) collective-permute-start(bf16[2,8,64,128]{3,2,1,0:T(8,128)(2,1)S(1)} %pad_maximum_fusion.1), channel_id=1, source_target_pairs={{0,1},{1,2},{2,3},{3,4},{4,5},{5,6},{6,7},{7,8},{8,9},{9,10},{10,1... | collective-permute-start | bytes 786440 | tf_op jit(solution)/shard_map/ppermute | solution.py:19
  8.5 8.7 %collective-permute-done.1.back_four = bf16[2,8,64,128]{3,2,1,0:T(8,128)(2,1)S(1)} collective-permute-done((bf16[2,8,64,128]{3,2,1,0:T(8,128)(2,1)S(1)}, bf16[2,8,64,128]{3,2,1,0:T(8,128)(2,1)S(1)}, u32[]{:S(2)}, u32[]{:S(2)}) %collective-permute-start.1) | collective-permute-done | bytes 262176 | tf_op jit(solution)/shard_map/ppermute | solution.py:19
  17.2 0.0 collective-permute-done.back_two
  17.2 0.0 copy-done
  17.3 0.0 copy-start.2
  17.3 0.0 copy-start.3
  17.3 0.1 pad_maximum_fusion
  17.4 0.0 copy-start.4
  17.4 0.1 collective-permute-start.2
  18.2 1.2 %collective-permute-done.2.back_odd = bf16[2,2,8,64,128]{4,3,2,1,0:T(8,128)(2,1)S(1)} collective-permute-done((bf16[2,2,8,64,128]{4,3,2,1,0:T(8,128)(2,1)S(1)}, bf16[2,2,8,64,128]{4,3,2,1,0:T(8,128)(2,1)S(1)}, u32[]{:S(2)}, u32[]{:S(2)}) %collective-permute-start.2) | collective-permute-done | bytes 524320 | tf_op jit(solution)/shard_map/ppermute | solution.py:24
  19.4 0.0 copy-done.4
  19.4 6.4 %attention.1 = (bf16[32,64,128]{2,1,0:T(8,128)(2,1)}, bf16[32,64,128]{2,1,0:T(8,128)(2,1)}, bf16[2,2,8,64,128]{4,3,2,1,0:T(8,128)(2,1)S(1)}, f32[2,8,64,128]{3,2...) custom-call(s32[32]{0:T(128)S(1)} %copy-done.4, s32[1]{0:T(128)S(6)} %copy.10.offset, ...), custom_call_target="tpu_custom_call" | custom-call | tf_op jit(solution)/shard_map/attention/pallas_call | solution.py:147
  25.8 0.1 collective-permute-start.3
  25.9 1.8 %collective-permute-done.3.odd_parts = bf16[2,2,8,64,128]{4,3,2,1,0:T(8,128)(2,1)S(1)} collective-permute-done((bf16[2,2,8,64,128]{4,3,2,1,0:T(8,128)(2,1)S(1)}, bf16[2,2,8,64,128]{4,3,2,1,0:T(8,128)(2,1)S(1)}, u32[]{:S(2)}, u32[]{:S(2)}) %collective-permute-start.3) | collective-permute-done | bytes 524320 | tf_op jit(solution)/shard_map/ppermute | solution.py:24
  27.7 0.1 merge.1
  27.8 1.9 %collective-permute-start.4 = (bf16[2,8,64,128]{3,2,1,0:T(8,128)(2,1)S(1)}, bf16[2,8,64,128]{3,2,1,0:T(8,128)(2,1)S(1)}, u32[]{:S(2)}, u32[]{:S(2)}) collective-permute-start(bf16[2,8,64,128]{3,2,1,0:T(8,128)(2,1)S(1)} %get-tuple-element.22), channel_id=1, source_target_pairs={{1,0},{2,1},{3,2},{4,3},{5,4},{6,5},{7,6},{8,7},{9,8},{10,9},{11,1... | collective-permute-start | bytes 786440 | tf_op jit(solution)/shard_map/ppermute | solution.py:19
  29.7 1.9 %collective-permute-start.5 = (bf16[2,8,64,128]{3,2,1,0:T(8,128)(2,1)S(1)}, bf16[2,8,64,128]{3,2,1,0:T(8,128)(2,1)S(1)}, u32[]{:S(2)}, u32[]{:S(2)}) collective-permute-start(bf16[2,8,64,128]{3,2,1,0:T(8,128)(2,1)S(1)} %get-tuple-element.23), channel_id=1, source_target_pairs={{2,0},{3,1},{4,2},{5,3},{6,4},{7,5},{8,6},{9,7},{10,8},{11,9},{12,... | collective-permute-start | bytes 786440 | tf_op jit(solution)/shard_map/ppermute | solution.py:19
  31.7 6.4 %collective-permute-done.4.two_sum = bf16[2,8,64,128]{3,2,1,0:T(8,128)(2,1)S(1)} collective-permute-done((bf16[2,8,64,128]{3,2,1,0:T(8,128)(2,1)S(1)}, bf16[2,8,64,128]{3,2,1,0:T(8,128)(2,1)S(1)}, u32[]{:S(2)}, u32[]{:S(2)}) %collective-permute-start.4) | collective-permute-done | bytes 262176 | tf_op jit(solution)/shard_map/ppermute | solution.py:19
  38.1 8.1 %collective-permute-done.5.four_sum = bf16[2,8,64,128]{3,2,1,0:T(8,128)(2,1)S(1)} collective-permute-done((bf16[2,8,64,128]{3,2,1,0:T(8,128)(2,1)S(1)}, bf16[2,8,64,128]{3,2,1,0:T(8,128)(2,1)S(1)}, u32[]{:S(2)}, u32[]{:S(2)}) %collective-permute-start.5) | collective-permute-done | bytes 262176 | tf_op jit(solution)/shard_map/ppermute | solution.py:19
  46.2 0.7 %total.1 = (bf16[8,64,128]{2,1,0:T(8,128)(2,1)}, bf16[8,64,128]{2,1,0:T(8,128)(2,1)}) custom-call(f32[2,8,64,128]{3,2,1,0:T(8,128)S(1)} %get-tuple-element.21.own_sum, bf16[2,8,64,128]{3,2,1,0:T(8,128)(2,1)S(1)} %collective-permute-done.4.two_sum, bf16[2,8,64,128]{3,2,1,0:T(8,128)(2,1)S(1)} %collective-permute-done.5.four_sum), custom_call_target="tpu_custom_call" | custom-call | tf_op jit(solution)/shard_map/total/pallas_call | solution.py:175
  (4 shorter events, 0.1 us)
Async XLA Ops:
  0.6 16.6 %copy-start = (bf16[8,64,128]{2,1,0:T(8,128)(2,1)S(1)}, bf16[8,64,128]{2,1,0:T(8,128)(2,1)}, u32[]{:S(2)}) copy-start(bf16[8,64,128]{2,1,0:T(8,128)(2,1)} %keys.1) | copy-start | bytes 393220
  0.6 16.6 %copy-start.1 = (bf16[8,64,128]{2,1,0:T(8,128)(2,1)S(1)}, bf16[8,64,128]{2,1,0:T(8,128)(2,1)}, u32[]{:S(2)}) copy-start(bf16[8,64,128]{2,1,0:T(8,128)(2,1)} %values.1) | copy-start | bytes 393220
  1.7 15.6 %collective-permute-start.1 = (bf16[2,8,64,128]{3,2,1,0:T(8,128)(2,1)S(1)}, bf16[2,8,64,128]{3,2,1,0:T(8,128)(2,1)S(1)}, u32[]{:S(2)}, u32[]{:S(2)}) collective-permute-start(bf16[2,8,64,128]{3,2,1,0:T(8,128)(2,1)S(1)} %pad_maximum_fusion.1), channel_id=1, source_target_pairs={{0,2},{1,3},{2,4},{3,5},{4,6},{5,7},{6,8},{7,9},{8,10},{9,11},{10,... | collective-permute-start | bytes 786440 | tf_op jit(solution)/shard_map/ppermute | solution.py:19
  5.1 12.1 %collective-permute-start = (bf16[2,8,64,128]{3,2,1,0:T(8,128)(2,1)S(1)}, bf16[2,8,64,128]{3,2,1,0:T(8,128)(2,1)S(1)}, u32[]{:S(2)}, u32[]{:S(2)}) collective-permute-start(bf16[2,8,64,128]{3,2,1,0:T(8,128)(2,1)S(1)} %pad_maximum_fusion.1), channel_id=1, source_target_pairs={{0,1},{1,2},{2,3},{3,4},{4,5},{5,6},{6,7},{7,8},{8,9},{9,10},{10,1... | collective-permute-start | bytes 786440 | tf_op jit(solution)/shard_map/ppermute | solution.py:19
  17.3 2.1 %copy-start.2 = (bf16[32,64,128]{2,1,0:T(8,128)(2,1)S(1)}, bf16[32,64,128]{2,1,0:T(8,128)(2,1)}, u32[]{:S(2)}) copy-start(bf16[32,64,128]{2,1,0:T(8,128)(2,1)} %queries.1) | copy-start | bytes 1572868
  17.3 2.1 %copy-start.3 = (bf16[32,64,128]{2,1,0:T(8,128)(2,1)S(1)}, bf16[32,64,128]{2,1,0:T(8,128)(2,1)}, u32[]{:S(2)}) copy-start(bf16[32,64,128]{2,1,0:T(8,128)(2,1)} %grads.1) | copy-start | bytes 1572868
  17.4 2.0 %copy-start.4 = (s32[32]{0:T(128)S(1)}, s32[32]{0:T(128)}, u32[]{:S(2)}) copy-start(s32[32]{0:T(128)} %spans.1) | copy-start | bytes 388
  17.4 2.0 %collective-permute-start.2 = (bf16[2,2,8,64,128]{4,3,2,1,0:T(8,128)(2,1)S(1)}, bf16[2,2,8,64,128]{4,3,2,1,0:T(8,128)(2,1)S(1)}, u32[]{:S(2)}, u32[]{:S(2)}) collective-permute-start(bf16[2,2,8,64,128]{4,3,2,1,0:T(8,128)(2,1)S(1)} %pad_maximum_fusion), channel_id=1, source_target_pairs={{0,16},{16,0},{1,17},{17,1},{2,18},{18,2},{3,19},{19,3},{4,20},{20... | collective-permute-start | bytes 1572872 | tf_op jit(solution)/shard_map/ppermute | solution.py:24
  25.8 1.9 %collective-permute-start.3 = (bf16[2,2,8,64,128]{4,3,2,1,0:T(8,128)(2,1)S(1)}, bf16[2,2,8,64,128]{4,3,2,1,0:T(8,128)(2,1)S(1)}, u32[]{:S(2)}, u32[]{:S(2)}) collective-permute-start(bf16[2,2,8,64,128]{4,3,2,1,0:T(8,128)(2,1)S(1)} %get-tuple-element.17), channel_id=1, source_target_pairs={{0,16},{16,0},{1,17},{17,1},{2,18},{18,2},{3,19},{19,3},{4,20},{20... | collective-permute-start | bytes 1572872 | tf_op jit(solution)/shard_map/ppermute | solution.py:24
  27.8 10.2 %collective-permute-start.4 = (bf16[2,8,64,128]{3,2,1,0:T(8,128)(2,1)S(1)}, bf16[2,8,64,128]{3,2,1,0:T(8,128)(2,1)S(1)}, u32[]{:S(2)}, u32[]{:S(2)}) collective-permute-start(bf16[2,8,64,128]{3,2,1,0:T(8,128)(2,1)S(1)} %get-tuple-element.22), channel_id=1, source_target_pairs={{1,0},{2,1},{3,2},{4,3},{5,4},{6,5},{7,6},{8,7},{9,8},{10,9},{11,1... | collective-permute-start | bytes 786440 | tf_op jit(solution)/shard_map/ppermute | solution.py:19
  29.7 16.4 %collective-permute-start.5 = (bf16[2,8,64,128]{3,2,1,0:T(8,128)(2,1)S(1)}, bf16[2,8,64,128]{3,2,1,0:T(8,128)(2,1)S(1)}, u32[]{:S(2)}, u32[]{:S(2)}) collective-permute-start(bf16[2,8,64,128]{3,2,1,0:T(8,128)(2,1)S(1)} %get-tuple-element.23), channel_id=1, source_target_pairs={{2,0},{3,1},{4,2},{5,3},{6,4},{7,5},{8,6},{9,7},{10,8},{11,9},{12,... | collective-permute-start | bytes 786440 | tf_op jit(solution)/shard_map/ppermute | solution.py:19

commit v2 on v1

v2 whole, which is shorter than its diff:
```python
import math

import jax
import jax.numpy as jnp
from jax import lax
from jax.experimental import pallas as pl
from jax.experimental.pallas import tpu as pltpu
from jax.sharding import PartitionSpec as P

REACH = 2
SEGMENT = 512

masked_score = -1e30


def shifted(block, axis, distance):
    devices = range(lax.axis_size(axis))
    route = [(i - distance, i) for i in devices if i - distance in devices]
    return lax.ppermute(block, axis, route)


def swapped(block, axis):
    count = lax.axis_size(axis)
    return lax.ppermute(block, axis, [(i, count - 1 - i) for i in range(count)])


def matmul(left, right, contract):
    return lax.dot_general(
        left, right, ((contract[:1], contract[1:]), ((), ())), preferred_element_type=jnp.float32
    )


def window(own, two, four, odd, index, g):
    return jnp.concatenate(
        [four[index, g], odd[1, index, g], two[index, g], odd[0, index, g], own[g]], axis=0
    )


def grouped(ref, g, per_group):
    _, length, width = ref.shape
    return ref[pl.ds(g * per_group, per_group)].reshape(per_group * length, width)


def first_visible(spans, offset, groups, per_group, length):
    lanes = per_group * length
    start = (lax.axis_index("seq") * lax.axis_size("head") + lax.axis_index("head")) * length
    lane = lax.broadcasted_iota(jnp.int32, (1, lanes), 1)
    lane_head = lane // length
    query_pos = start + lane - lane_head * length
    segment_start = query_pos - lax.bitwise_and(offset[0] + query_pos, SEGMENT - 1)
    floor = jnp.maximum(segment_start, 0)
    result = []
    for g in range(groups):
        span = jnp.full((1, lanes), spans[g * per_group], jnp.int32)
        for a in range(1, per_group):
            span = jnp.where(lane_head == a, spans[g * per_group + a], span)
        result.append(jnp.maximum(floor, query_pos - span + 1) - start)
    return result


def prepare_kernel(spans, offset, queries, keys, values, grads, own_scores, own_prob_grad, grad_rows):
    groups, length, width = keys.shape
    per_group = queries.shape[0] // groups
    lanes = per_group * length
    factor = width ** (-0.5) * math.log2(math.e)
    row = lax.broadcasted_iota(jnp.int32, (length, lanes), 0)
    lane_token = lax.broadcasted_iota(jnp.int32, (length, lanes), 1) % length
    first = first_visible(spans, offset, groups, per_group, length)
    for g in range(groups):
        query = grouped(queries, g, per_group)
        grad = grouped(grads, g, per_group)
        visible = (row >= first[g]) & (row <= lane_token)
        scores = matmul(keys[g], query, (1, 1)) * factor
        own_scores[g] = jnp.where(visible, scores, masked_score)
        own_prob_grad[g] = matmul(values[g], grad, (1, 1))
        grad_rows[g] = grad.T


def attention_kernel(
    spans, offset, queries, keys, values, grads, back_two, back_four, back_odd,
    own_scores, own_prob_grad, grad_rows,
    odd_parts, attended_rows, prob_half, score_grad_half,
):
    groups, length, width = keys.shape
    per_group = queries.shape[0] // groups
    lanes = per_group * length
    scale = width ** (-0.5)
    earlier = 2 * REACH
    row = lax.broadcasted_iota(jnp.int32, (length, lanes), 0)
    first = first_visible(spans, offset, groups, per_group, length)

    for g in range(groups):
        window_keys = window(keys, back_two, back_four, back_odd, 0, g)
        window_values = window(values, back_two, back_four, back_odd, 1, g)
        query = grouped(queries, g, per_group)
        grad = grouped(grads, g, per_group)
        scores = matmul(window_keys[: earlier * length], query, (1, 1)) * (scale * math.log2(math.e))
        scores = jnp.concatenate(
            [
                jnp.where(
                    row >= first[g] + (earlier - b) * length,
                    scores[b * length : (b + 1) * length],
                    masked_score,
                )
                for b in range(earlier)
            ]
            + [own_scores[g]],
            axis=0,
        )
        row_max = jnp.max(scores, axis=0, keepdims=True)
        weights = jnp.exp2(scores - row_max)
        inverse = 1.0 / jnp.sum(weights, axis=0, keepdims=True)
        weighted = matmul(window_values, weights.astype(jnp.bfloat16), (0, 0))
        attended = (weighted * inverse).astype(jnp.bfloat16)
        attended_rows[g] = attended
        delta = jnp.sum(
            grad_rows[g].astype(jnp.float32) * attended.astype(jnp.float32), axis=0, keepdims=True
        )
        prob = weights * inverse
        prob_grad = jnp.concatenate(
            [matmul(window_values[: earlier * length], grad, (1, 1)), own_prob_grad[g]], axis=0
        )
        half = prob.astype(jnp.bfloat16)
        score_grad = (prob * (prob_grad - delta) * scale).astype(jnp.bfloat16)
        prob_half[g] = half
        score_grad_half[g] = score_grad
        for slot, back in ((0, 1), (1, 3)):
            rows = slice((earlier - back) * length, (earlier - back + 1) * length)
            odd_parts[slot, 0, g] = matmul(score_grad[rows], query, (1, 0)).astype(jnp.bfloat16)
            odd_parts[slot, 1, g] = matmul(half[rows], grad, (1, 0)).astype(jnp.bfloat16)


def even_kernel(queries, grads, prob_half, score_grad_half, two_part, four_part):
    groups = prob_half.shape[0]
    per_group = queries.shape[0] // groups
    length = queries.shape[1]
    for g in range(groups):
        query = grouped(queries, g, per_group)
        grad = grouped(grads, g, per_group)
        for part, back in ((two_part, 2), (four_part, 4)):
            rows = pl.ds((2 * REACH - back) * length, length)
            part[0, g] = matmul(score_grad_half[g, rows], query, (1, 0))
            part[1, g] = matmul(prob_half[g, rows], grad, (1, 0))


def merge_kernel(odd_parts, two_part, four_part, two_sum, four_sum):
    first_core = lax.axis_index("head") == 0

    @pl.when(first_core)
    def _():
        two_sum[...] = (two_part[...] + odd_parts[1].astype(jnp.float32)).astype(jnp.bfloat16)
        four_sum[...] = four_part[...].astype(jnp.bfloat16)

    @pl.when(jnp.logical_not(first_core))
    def _():
        two_sum[...] = (two_part[...] + odd_parts[0].astype(jnp.float32)).astype(jnp.bfloat16)
        four_sum[...] = (four_part[...] + odd_parts[1].astype(jnp.float32)).astype(jnp.bfloat16)


def query_kernel(
    queries, keys, grads, back_two, back_four, back_odd, attended_rows, prob_half, score_grad_half,
    odd_parts, out, query_grad, own_sum,
):
    groups, length, width = keys.shape
    per_group = queries.shape[0] // groups
    first_core = lax.axis_index("head") == 0
    own_rows = pl.ds(2 * REACH * length, length)
    for g in range(groups):
        rows = pl.ds(g * per_group, per_group)
        out[rows] = attended_rows[g].T.reshape(per_group, length, width)
        window_keys = window(keys, back_two, back_four, back_odd, 0, g)
        query_part = matmul(window_keys, score_grad_half[g], (0, 0)).astype(jnp.bfloat16)
        query_grad[rows] = query_part.T.reshape(per_group, length, width)
        own_sum[0, g] = matmul(score_grad_half[g, own_rows], grouped(queries, g, per_group), (1, 0))
        own_sum[1, g] = matmul(prob_half[g, own_rows], grouped(grads, g, per_group), (1, 0))

    @pl.when(first_core)
    def _():
        own_sum[...] += odd_parts[0].astype(jnp.float32)


def final_kernel(own_sum, two_sum, four_sum, key_grad, value_grad):
    for index, result in enumerate((key_grad, value_grad)):
        total = own_sum[index] + two_sum[index].astype(jnp.float32)
        result[...] = (total + four_sum[index].astype(jnp.float32)).astype(jnp.bfloat16)


def shards(query_matrix, key_matrix, value_matrix, output_gradient, query_head_spans, slab_offset):
    groups, length, width = key_matrix.shape
    heads = query_matrix.shape[0]
    lanes = heads // groups * length
    keys_seen = (2 * REACH + 1) * length
    half, full = jnp.bfloat16, jnp.float32
    pair_shape = (2, groups, length, width)

    def call(kernel, name, outs, scalars, arrays, flops):
        smem = pl.BlockSpec(memory_space=pltpu.SMEM)
        vmem = pl.BlockSpec(memory_space=pltpu.VMEM)
        return pl.pallas_call(
            kernel,
            out_shape=tuple(jax.ShapeDtypeStruct(shape, kind) for shape, kind in outs),
            in_specs=[smem] * len(scalars) + [vmem] * len(arrays),
            out_specs=(vmem,) * len(outs),
            compiler_params=pltpu.CompilerParams(vmem_limit_bytes=40 * 1024 * 1024),
            cost_estimate=pl.CostEstimate(flops=flops, bytes_accessed=2**22, transcendentals=0),
            name=name,
        )(*scalars, *arrays)

    score_flops = 2 * heads * length * keys_seen * width
    scalars = (query_head_spans, slab_offset)
    own = jnp.stack([key_matrix, value_matrix])
    back_two = shifted(own, "seq", 1)
    back_four = shifted(own, "seq", 2)
    prepared = call(
        prepare_kernel,
        "prepare",
        [((groups, length, lanes), full)] * 2 + [((groups, width, lanes), half)],
        scalars,
        (query_matrix, key_matrix, value_matrix, output_gradient),
        score_flops,
    )
    back_two, back_four, *prepared = lax.optimization_barrier((back_two, back_four, *prepared))
    first_core = lax.axis_index("head") == 0
    back_odd = swapped(
        jnp.stack(
            [
                jnp.where(first_core, own, back_two),
                jnp.where(first_core, back_two, back_four),
            ]
        ),
        "head",
    )
    odd_parts, attended_rows, prob_half, score_grad_half = call(
        attention_kernel,
        "attention",
        [
            ((2,) + pair_shape, half),
            ((groups, width, lanes), half),
            ((groups, keys_seen, lanes), half),
            ((groups, keys_seen, lanes), half),
        ],
        scalars,
        (query_matrix, key_matrix, value_matrix, output_gradient, back_two, back_four, back_odd)
        + tuple(prepared),
        4 * score_flops,
    )
    odd_arrived = swapped(odd_parts, "head")
    two_part, four_part = call(
        even_kernel,
        "even_parts",
        [(pair_shape, full)] * 2,
        (),
        (query_matrix, output_gradient, prob_half, score_grad_half),
        score_flops,
    )
    two_sum, four_sum = call(
        merge_kernel, "merge", [(pair_shape, half)] * 2, (), (odd_arrived, two_part, four_part), 1000
    )
    four_total = shifted(four_sum, "seq", -2)
    two_total = shifted(two_sum, "seq", -1)
    attn_out, query_grad, own_sum = call(
        query_kernel,
        "query_grad",
        [(query_matrix.shape, half)] * 2 + [(pair_shape, full)],
        (),
        (
            query_matrix, key_matrix, output_gradient, back_two, back_four, back_odd,
            attended_rows, prob_half, score_grad_half, odd_arrived,
        ),
        2 * score_flops,
    )
    key_grad, value_grad = call(
        final_kernel,
        "total",
        [(key_matrix.shape, half)] * 2,
        (),
        (own_sum, two_total, four_total),
        1000,
    )
    return (attn_out, query_grad, key_grad, value_grad)


def solution(mesh):
    tokens = P(None, ("seq", "head"), None)
    return jax.shard_map(
        shards,
        mesh=mesh,
        in_specs=(tokens, tokens, tokens, tokens, P(), P()),
        out_specs=(tokens, tokens, tokens, tokens),
        check_vma=False,
    )
```

time: 47.2 us -> 45.2 us (0.958)
  the two profiles are of different devices: /device:TPU:4 before, /device:TPU:12 now
where the time goes in v2:
time: 45.2 us; the launch traced here: 44.8 us
  waiting for transfers between devices  16.2 us (36%)
  starting transfers between devices  13.3 us (29%)
  Pallas kernels  8.3 us (18%)
  local copies, waits for them, and re-layouts  4.56 us (10%)
  between operations  1.42 us (3%)
  other arithmetic  1.09 us (2%)
    ppermute x4, starting transfers between devices, shifted(): return lax.ppermute(block, axis, route)  13 us
    ppermute x4, waiting for transfers between devices, shifted(): return lax.ppermute(block, axis, route)  13 us
    pallas_call x6, Pallas kernels, call(): pl.pallas_call(kernel, out_shape=tuple((jax.ShapeDtypeStruct(shape, kind)...  8.3 us
    unnamed x16, local copies, waits for them, and re-layouts  4.56 us
    ppermute x2, waiting for transfers between devices, swapped(): return lax.ppermute(block, axis, [(i, count - 1 - i) for i in range(count)])  3.22 us
    another operation x1, other arithmetic, shards(): own = jnp.stack([key_matrix, value_matrix])  1 us
  transfers between devices with their start and end apart: 6, of which 5 were waited for; matrix products, arithmetic and copies ran while one was open for 0% of the time, Pallas kernels for 7%

profile of v2, /device:TPU:12, one launch (start us, length us, event | category | flops | bytes accessed | tf_op | source)
XLA Modules:
  0.0 44.8 jit_solution(1105188649309602335)
XLA Ops:
  0.6 1.0 %pad_maximum_fusion.1 = bf16[2,8,64,128]{3,2,1,0:T(8,128)(2,1)S(1)} fusion(bf16[1,8,64,128]{3,2,1,0:T(8,128)(2,1)} %bitcast.8, bf16[1,8,64,128]{3,2,1,0:T(8,128)(2,1)} %bitcast.6), kind=kLoop, calls=%fused_computation.1 | loop fusion | flops 131072 | bytes 524288 | tf_op jit(solution)/shard_map/stack | solution.py:211
  1.6 3.4 %collective-permute-start.1 = (bf16[2,8,64,128]{3,2,1,0:T(8,128)(2,1)S(1)}, bf16[2,8,64,128]{3,2,1,0:T(8,128)(2,1)S(1)}, u32[]{:S(2)}, u32[]{:S(2)}) collective-permute-start(bf16[2,8,64,128]{3,2,1,0:T(8,128)(2,1)S(1)} %pad_maximum_fusion.1), channel_id=1, source_target_pairs={{0,2},{1,3},{2,4},{3,5},{4,6},{5,7},{6,8},{7,9},{8,10},{9,11},{10,... | collective-permute-start | bytes 786440 | tf_op jit(solution)/shard_map/ppermute | solution.py:19
  5.1 3.4 %collective-permute-start = (bf16[2,8,64,128]{3,2,1,0:T(8,128)(2,1)S(1)}, bf16[2,8,64,128]{3,2,1,0:T(8,128)(2,1)S(1)}, u32[]{:S(2)}, u32[]{:S(2)}) collective-permute-start(bf16[2,8,64,128]{3,2,1,0:T(8,128)(2,1)S(1)} %pad_maximum_fusion.1), channel_id=1, source_target_pairs={{0,1},{1,2},{2,3},{3,4},{4,5},{5,6},{6,7},{7,8},{8,9},{9,10},{10,1... | collective-permute-start | bytes 786440 | tf_op jit(solution)/shard_map/ppermute | solution.py:19
  9.1 1.0 %copy-done = bf16[32,64,128]{2,1,0:T(8,128)(2,1)S(1)} copy-done((bf16[32,64,128]{2,1,0:T(8,128)(2,1)S(1)}, bf16[32,64,128]{2,1,0:T(8,128)(2,1)}, u32[]{:S(2)}) %copy-start) | copy-done | bytes 524312
  10.2 1.0 %copy-done.2 = bf16[32,64,128]{2,1,0:T(8,128)(2,1)S(1)} copy-done((bf16[32,64,128]{2,1,0:T(8,128)(2,1)S(1)}, bf16[32,64,128]{2,1,0:T(8,128)(2,1)}, u32[]{:S(2)}) %copy-start.2) | copy-done | bytes 524312
  11.2 0.9 %copy-done.4 = bf16[8,64,128]{2,1,0:T(8,128)(2,1)S(1)} copy-done((bf16[8,64,128]{2,1,0:T(8,128)(2,1)S(1)}, bf16[8,64,128]{2,1,0:T(8,128)(2,1)}, u32[]{:S(2)}) %copy-start.4) | copy-done | bytes 131096
  12.1 0.9 %copy-done.6 = bf16[8,64,128]{2,1,0:T(8,128)(2,1)S(1)} copy-done((bf16[8,64,128]{2,1,0:T(8,128)(2,1)S(1)}, bf16[8,64,128]{2,1,0:T(8,128)(2,1)}, u32[]{:S(2)}) %copy-start.6) | copy-done | bytes 131096
  13.0 0.7 %copy-done.7 = s32[32]{0:T(128)S(1)} copy-done((s32[32]{0:T(128)S(1)}, s32[32]{0:T(128)}, u32[]{:S(2)}) %copy-start.7) | copy-done | bytes 152
  13.7 1.0 %prepare.1 = (f32[8,64,256]{2,1,0:T(8,128)S(1)}, f32[8,64,256]{2,1,0:T(8,128)S(1)}, bf16[8,128,256]{2,1,0:T(8,128)(2,1)S(1)}) custom-call(s32[32]{0:T(128)S(1)} %copy-done.7, s32[1]{0:T(128)S(6)} %copy.10.offset, bf16[32,64,128]{2,1,0:T(8,128)(2,1)S(1)} %copy-done, bf16[8,64,128]{2,1,0:T(8,128)(2,1)S(1)} %copy-done.4, bf16[8,64,128]{2,1,0:T(8,128)(2,1)S(1)} %copy-done.6, ...), custom_call_target="tpu_custom_call" | custom-call | flops 167772160 | bytes 4194304 | tf_op jit(solution)/shard_map/prepare/pallas_call | solution.py:199
  14.7 2.5 %collective-permute-done.1.back_four = bf16[2,8,64,128]{3,2,1,0:T(8,128)(2,1)S(1)} collective-permute-done((bf16[2,8,64,128]{3,2,1,0:T(8,128)(2,1)S(1)}, bf16[2,8,64,128]{3,2,1,0:T(8,128)(2,1)S(1)}, u32[]{:S(2)}, u32[]{:S(2)}) %collective-permute-start.1) | collective-permute-done | bytes 262176 | tf_op jit(solution)/shard_map/ppermute | solution.py:19
  17.2 0.1 pad_maximum_fusion
  17.3 0.1 collective-permute-start.2
  17.4 1.9 %collective-permute-done.2.back_odd = bf16[2,2,8,64,128]{4,3,2,1,0:T(8,128)(2,1)S(1)} collective-permute-done((bf16[2,2,8,64,128]{4,3,2,1,0:T(8,128)(2,1)S(1)}, bf16[2,2,8,64,128]{4,3,2,1,0:T(8,128)(2,1)S(1)}, u32[]{:S(2)}, u32[]{:S(2)}) %collective-permute-start.2) | collective-permute-done | bytes 524320 | tf_op jit(solution)/shard_map/ppermute | solution.py:24
  19.3 4.3 %attention.1 = (bf16[2,2,8,64,128]{4,3,2,1,0:T(8,128)(2,1)S(1)}, bf16[8,128,256]{2,1,0:T(8,128)(2,1)S(1)}, bf16[8,320,256]{2,1,0:T(8,128)(2,1)S(1)}, bf16[8,320,256]{2,1,0:T(8,128)(2,1)S(1)}) custom-call(s32[32]{0:T(128)S(1)} %copy-done.7, s32[1]{0:T(128)S(6)} %copy.10.offset, bf16[32,64,128]{2,1,0:T(8,128)(2,1)S(1)} %copy-done, ...), custom_call_target="tpu_custom_call" | custom-call | flops 671088640 | bytes 4194304 | tf_op jit(solution)/shard_map/attention/pallas_call | solution.py:199
  23.6 0.2 collective-permute-start.3
  23.8 0.4 even_parts.1
  24.3 1.3 %collective-permute-done.3.odd_parts = bf16[2,2,8,64,128]{4,3,2,1,0:T(8,128)(2,1)S(1)} collective-permute-done((bf16[2,2,8,64,128]{4,3,2,1,0:T(8,128)(2,1)S(1)}, bf16[2,2,8,64,128]{4,3,2,1,0:T(8,128)(2,1)S(1)}, u32[]{:S(2)}, u32[]{:S(2)}) %collective-permute-start.3) | collective-permute-done | bytes 524320 | tf_op jit(solution)/shard_map/ppermute | solution.py:24
  25.6 0.1 merge.1
  25.7 1.9 %collective-permute-start.4 = (bf16[2,8,64,128]{3,2,1,0:T(8,128)(2,1)S(1)}, bf16[2,8,64,128]{3,2,1,0:T(8,128)(2,1)S(1)}, u32[]{:S(2)}, u32[]{:S(2)}) collective-permute-start(bf16[2,8,64,128]{3,2,1,0:T(8,128)(2,1)S(1)} %get-tuple-element.42), channel_id=1, source_target_pairs={{1,0},{2,1},{3,2},{4,3},{5,4},{6,5},{7,6},{8,7},{9,8},{10,9},{11,1... | collective-permute-start | bytes 786440 | tf_op jit(solution)/shard_map/ppermute | solution.py:19
  27.6 4.2 %collective-permute-start.5 = (bf16[2,8,64,128]{3,2,1,0:T(8,128)(2,1)S(1)}, bf16[2,8,64,128]{3,2,1,0:T(8,128)(2,1)S(1)}, u32[]{:S(2)}, u32[]{:S(2)}) collective-permute-start(bf16[2,8,64,128]{3,2,1,0:T(8,128)(2,1)S(1)} %get-tuple-element.43), channel_id=1, source_target_pairs={{2,0},{3,1},{4,2},{5,3},{6,4},{7,5},{8,6},{9,7},{10,8},{11,9},{12,... | collective-permute-start | bytes 786440 | tf_op jit(solution)/shard_map/ppermute | solution.py:19
  31.8 1.7 %query_grad.1 = (bf16[32,64,128]{2,1,0:T(8,128)(2,1)}, bf16[32,64,128]{2,1,0:T(8,128)(2,1)}, f32[2,8,64,128]{3,2,1,0:T(8,128)S(1)}) custom-call(bf16[32,64,128]{2,1,0:T(8,128)(2,1)S(1)} %copy-done.1, bf16[8,64,128]{2,1,0:T(8,128)(2,1)S(1)} %copy-done.5, bf16[32,64,128]{2,1,0:T(8,128)(2,1)S(1)} %copy-done.3, ...), custom_call_target="tpu_custom_call" | custom-call | flops 335544320 | bytes 4194304 | tf_op jit(solution)/shard_map/query_grad/pallas_call | solution.py:199
  33.6 2.3 %collective-permute-done.4.two_sum = bf16[2,8,64,128]{3,2,1,0:T(8,128)(2,1)S(1)} collective-permute-done((bf16[2,8,64,128]{3,2,1,0:T(8,128)(2,1)S(1)}, bf16[2,8,64,128]{3,2,1,0:T(8,128)(2,1)S(1)}, u32[]{:S(2)}, u32[]{:S(2)}) %collective-permute-start.4) | collective-permute-done | bytes 262176 | tf_op jit(solution)/shard_map/ppermute | solution.py:19
  35.9 8.2 %collective-permute-done.5.four_sum = bf16[2,8,64,128]{3,2,1,0:T(8,128)(2,1)S(1)} collective-permute-done((bf16[2,8,64,128]{3,2,1,0:T(8,128)(2,1)S(1)}, bf16[2,8,64,128]{3,2,1,0:T(8,128)(2,1)S(1)}, u32[]{:S(2)}, u32[]{:S(2)}) %collective-permute-start.5) | collective-permute-done | bytes 262176 | tf_op jit(solution)/shard_map/ppermute | solution.py:19
  44.1 0.7 %total.1 = (bf16[8,64,128]{2,1,0:T(8,128)(2,1)}, bf16[8,64,128]{2,1,0:T(8,128)(2,1)}) custom-call(f32[2,8,64,128]{3,2,1,0:T(8,128)S(1)} %get-tuple-element.39.own_sum, bf16[2,8,64,128]{3,2,1,0:T(8,128)(2,1)S(1)} %collective-permute-done.4.two_sum, bf16[2,8,64,128]{3,2,1,0:T(8,128)(2,1)S(1)} %collective-permute-done.5.four_sum), custom_call_target="tpu_custom_call" | custom-call | flops 1000 | bytes 4194304 | tf_op jit(solution)/shard_map/total/pallas_call | solution.py:199
  (13 shorter events, 0.1 us)
Async XLA Ops:
  1.6 15.6 %collective-permute-start.1 = (bf16[2,8,64,128]{3,2,1,0:T(8,128)(2,1)S(1)}, bf16[2,8,64,128]{3,2,1,0:T(8,128)(2,1)S(1)}, u32[]{:S(2)}, u32[]{:S(2)}) collective-permute-start(bf16[2,8,64,128]{3,2,1,0:T(8,128)(2,1)S(1)} %pad_maximum_fusion.1), channel_id=1, source_target_pairs={{0,2},{1,3},{2,4},{3,5},{4,6},{5,7},{6,8},{7,9},{8,10},{9,11},{10,... | collective-permute-start | bytes 786440 | tf_op jit(solution)/shard_map/ppermute | solution.py:19
  5.1 12.1 %collective-permute-start = (bf16[2,8,64,128]{3,2,1,0:T(8,128)(2,1)S(1)}, bf16[2,8,64,128]{3,2,1,0:T(8,128)(2,1)S(1)}, u32[]{:S(2)}, u32[]{:S(2)}) collective-permute-start(bf16[2,8,64,128]{3,2,1,0:T(8,128)(2,1)S(1)} %pad_maximum_fusion.1), channel_id=1, source_target_pairs={{0,1},{1,2},{2,3},{3,4},{4,5},{5,6},{6,7},{7,8},{8,9},{9,10},{10,1... | collective-permute-start | bytes 786440 | tf_op jit(solution)/shard_map/ppermute | solution.py:19
  9.1 1.0 %copy-start = (bf16[32,64,128]{2,1,0:T(8,128)(2,1)S(1)}, bf16[32,64,128]{2,1,0:T(8,128)(2,1)}, u32[]{:S(2)}) copy-start(bf16[32,64,128]{2,1,0:T(8,128)(2,1)} %queries.7) | copy-start | bytes 1572868
  10.2 1.0 %copy-start.2 = (bf16[32,64,128]{2,1,0:T(8,128)(2,1)S(1)}, bf16[32,64,128]{2,1,0:T(8,128)(2,1)}, u32[]{:S(2)}) copy-start(bf16[32,64,128]{2,1,0:T(8,128)(2,1)} %grads.7) | copy-start | bytes 1572868
  11.2 0.9 %copy-start.4 = (bf16[8,64,128]{2,1,0:T(8,128)(2,1)S(1)}, bf16[8,64,128]{2,1,0:T(8,128)(2,1)}, u32[]{:S(2)}) copy-start(bf16[8,64,128]{2,1,0:T(8,128)(2,1)} %keys.5) | copy-start | bytes 393220
  12.1 0.9 %copy-start.6 = (bf16[8,64,128]{2,1,0:T(8,128)(2,1)S(1)}, bf16[8,64,128]{2,1,0:T(8,128)(2,1)}, u32[]{:S(2)}) copy-start(bf16[8,64,128]{2,1,0:T(8,128)(2,1)} %values.3) | copy-start | bytes 393220
  13.0 0.7 %copy-start.7 = (s32[32]{0:T(128)S(1)}, s32[32]{0:T(128)}, u32[]{:S(2)}) copy-start(s32[32]{0:T(128)} %spans.3) | copy-start | bytes 388
  17.3 6.5 %copy-start.1 = (bf16[32,64,128]{2,1,0:T(8,128)(2,1)S(1)}, bf16[32,64,128]{2,1,0:T(8,128)(2,1)}, u32[]{:S(2)}) copy-start(bf16[32,64,128]{2,1,0:T(8,128)(2,1)} %queries.7) | copy-start | bytes 1572868
  17.3 6.5 %copy-start.3 = (bf16[32,64,128]{2,1,0:T(8,128)(2,1)S(1)}, bf16[32,64,128]{2,1,0:T(8,128)(2,1)}, u32[]{:S(2)}) copy-start(bf16[32,64,128]{2,1,0:T(8,128)(2,1)} %grads.7) | copy-start | bytes 1572868
  17.3 2.0 %collective-permute-start.2 = (bf16[2,2,8,64,128]{4,3,2,1,0:T(8,128)(2,1)S(1)}, bf16[2,2,8,64,128]{4,3,2,1,0:T(8,128)(2,1)S(1)}, u32[]{:S(2)}, u32[]{:S(2)}) collective-permute-start(bf16[2,2,8,64,128]{4,3,2,1,0:T(8,128)(2,1)S(1)} %pad_maximum_fusion), channel_id=1, source_target_pairs={{0,16},{16,0},{1,17},{17,1},{2,18},{18,2},{3,19},{19,3},{4,20},{20... | collective-permute-start | bytes 1572872 | tf_op jit(solution)/shard_map/ppermute | solution.py:24
  23.6 2.0 %collective-permute-start.3 = (bf16[2,2,8,64,128]{4,3,2,1,0:T(8,128)(2,1)S(1)}, bf16[2,2,8,64,128]{4,3,2,1,0:T(8,128)(2,1)S(1)}, u32[]{:S(2)}, u32[]{:S(2)}) collective-permute-start(bf16[2,2,8,64,128]{4,3,2,1,0:T(8,128)(2,1)S(1)} %get-tuple-element.36), channel_id=1, source_target_pairs={{0,16},{16,0},{1,17},{17,1},{2,18},{18,2},{3,19},{19,3},{4,20},{20... | collective-permute-start | bytes 1572872 | tf_op jit(solution)/shard_map/ppermute | solution.py:24
  24.3 7.6 %copy-start.5 = (bf16[8,64,128]{2,1,0:T(8,128)(2,1)S(1)}, bf16[8,64,128]{2,1,0:T(8,128)(2,1)}, u32[]{:S(2)}) copy-start(bf16[8,64,128]{2,1,0:T(8,128)(2,1)} %keys.5) | copy-start | bytes 393220
  25.7 10.3 %collective-permute-start.4 = (bf16[2,8,64,128]{3,2,1,0:T(8,128)(2,1)S(1)}, bf16[2,8,64,128]{3,2,1,0:T(8,128)(2,1)S(1)}, u32[]{:S(2)}, u32[]{:S(2)}) collective-permute-start(bf16[2,8,64,128]{3,2,1,0:T(8,128)(2,1)S(1)} %get-tuple-element.42), channel_id=1, source_target_pairs={{1,0},{2,1},{3,2},{4,3},{5,4},{6,5},{7,6},{8,7},{9,8},{10,9},{11,1... | collective-permute-start | bytes 786440 | tf_op jit(solution)/shard_map/ppermute | solution.py:19
  27.6 16.5 %collective-permute-start.5 = (bf16[2,8,64,128]{3,2,1,0:T(8,128)(2,1)S(1)}, bf16[2,8,64,128]{3,2,1,0:T(8,128)(2,1)S(1)}, u32[]{:S(2)}, u32[]{:S(2)}) collective-permute-start(bf16[2,8,64,128]{3,2,1,0:T(8,128)(2,1)S(1)} %get-tuple-element.43), channel_id=1, source_target_pairs={{2,0},{3,1},{4,2},{5,3},{6,4},{7,5},{8,6},{9,7},{10,8},{11,9},{12,... | collective-permute-start | bytes 786440 | tf_op jit(solution)/shard_map/ppermute | solution.py:19

commit v3 on v2

v3 whole, which is shorter than its diff:
```python
import math

import jax
import jax.numpy as jnp
from jax import lax
from jax.experimental import pallas as pl
from jax.experimental.pallas import tpu as pltpu
from jax.sharding import PartitionSpec as P

REACH = 2
SEGMENT = 512

masked_score = -1e30


def shifted(block, axis, distance):
    devices = range(lax.axis_size(axis))
    route = [(i - distance, i) for i in devices if i - distance in devices]
    return lax.ppermute(block, axis, route)


def swapped(block, axis):
    count = lax.axis_size(axis)
    return lax.ppermute(block, axis, [(i, count - 1 - i) for i in range(count)])


def matmul(left, right, contract):
    return lax.dot_general(
        left, right, ((contract[:1], contract[1:]), ((), ())), preferred_element_type=jnp.float32
    )


def grouped(ref, g, per_group):
    _, length, width = ref.shape
    return ref[pl.ds(g * per_group, per_group)].reshape(per_group * length, width)


def first_visible(spans, offset, groups, per_group, length):
    lanes = per_group * length
    start = (lax.axis_index("seq") * lax.axis_size("head") + lax.axis_index("head")) * length
    lane = lax.broadcasted_iota(jnp.int32, (1, lanes), 1)
    lane_head = lane // length
    query_pos = start + lane - lane_head * length
    segment_start = query_pos - lax.bitwise_and(offset[0] + query_pos, SEGMENT - 1)
    floor = jnp.maximum(segment_start, 0)
    result = []
    for g in range(groups):
        span = jnp.full((1, lanes), spans[g * per_group], jnp.int32)
        for a in range(1, per_group):
            span = jnp.where(lane_head == a, spans[g * per_group + a], span)
        result.append(jnp.maximum(floor, query_pos - span + 1) - start)
    return result


def join(*blocks):
    return jnp.concatenate(blocks, axis=0)


def masked(scores, first, backs, length):
    row = lax.broadcasted_iota(jnp.int32, (length, scores.shape[1]), 0)
    pieces = []
    for i, back in enumerate(backs):
        visible = row >= first + back * length
        if back == 0:
            lane = lax.broadcasted_iota(jnp.int32, row.shape, 1)
            visible &= row <= lane - lane // length * length
        pieces.append(jnp.where(visible, scores[i * length : (i + 1) * length], masked_score))
    return jnp.concatenate(pieces, axis=0)


def prepare_kernel(spans, offset, own, grads, own_copy, first, own_prob_grad, grad_rows):
    _, groups, length, width = own.shape
    per_group = grads.shape[0] // groups
    own_copy[...] = own[...]
    for g, rows in enumerate(first_visible(spans, offset, groups, per_group, length)):
        grad = grouped(grads, g, per_group)
        first[g] = rows
        own_prob_grad[g] = matmul(own[1, g], grad, (1, 1))
        grad_rows[g] = grad.T


def near_forward_kernel(
    first, queries, own, grads, one_keys, one_values, back_two, own_prob_grad,
    near_max, near_sum, near_out, near_weights, near_prob_grad,
):
    _, groups, length, width = own.shape
    per_group = queries.shape[0] // groups
    factor = width ** (-0.5) * math.log2(math.e)
    for g in range(groups):
        query = grouped(queries, g, per_group)
        grad = grouped(grads, g, per_group)
        scores = matmul(join(back_two[0, g], one_keys[g], own[0, g]), query, (1, 1)) * factor
        scores = masked(scores, first[g], (2, 1, 0), length)
        row_max = jnp.max(scores, axis=0, keepdims=True)
        weights = jnp.exp2(scores - row_max)
        near_max[g] = row_max
        near_sum[g] = jnp.sum(weights, axis=0, keepdims=True)
        near_weights[g] = weights
        near_out[g] = matmul(
            join(back_two[1, g], one_values[g], own[1, g]), weights.astype(jnp.bfloat16), (0, 0)
        )
        prob_grad = matmul(join(back_two[1, g], one_values[g]), grad, (1, 1))
        near_prob_grad[g] = jnp.concatenate([prob_grad, own_prob_grad[g]], axis=0)


def far_kernel(
    first, queries, grads, back_three, back_four, grad_rows, near_max, near_sum, near_out,
    attended_rows, row_delta, near_factor, prob_half, score_grad_half, three_part,
):
    _, groups, length, width = back_three.shape
    per_group = queries.shape[0] // groups
    scale = width ** (-0.5)
    for g in range(groups):
        query = grouped(queries, g, per_group)
        grad = grouped(grads, g, per_group)
        values = join(back_four[1, g], back_three[1, g])
        scores = matmul(join(back_four[0, g], back_three[0, g]), query, (1, 1))
        scores = masked(scores * (scale * math.log2(math.e)), first[g], (4, 3), length)
        row_max = jnp.maximum(near_max[g], jnp.max(scores, axis=0, keepdims=True))
        weights = jnp.exp2(scores - row_max)
        factor = jnp.exp2(near_max[g] - row_max)
        inverse = 1.0 / (near_sum[g] * factor + jnp.sum(weights, axis=0, keepdims=True))
        weighted = near_out[g] * factor + matmul(values, weights.astype(jnp.bfloat16), (0, 0))
        attended = (weighted * inverse).astype(jnp.bfloat16)
        delta = jnp.sum(
            grad_rows[g].astype(jnp.float32) * attended.astype(jnp.float32), axis=0, keepdims=True
        )
        prob = weights * inverse
        half = prob.astype(jnp.bfloat16)
        score_grad = (prob * (matmul(values, grad, (1, 1)) - delta) * scale).astype(jnp.bfloat16)
        attended_rows[g] = attended
        row_delta[g] = delta
        near_factor[g] = factor * inverse
        prob_half[g] = half
        score_grad_half[g] = score_grad
        three_part[0, g] = matmul(score_grad[length:], query, (1, 0)).astype(jnp.bfloat16)
        three_part[1, g] = matmul(half[length:], grad, (1, 0)).astype(jnp.bfloat16)


def four_kernel(queries, grads, prob_half, score_grad_half, four_part):
    groups = prob_half.shape[0]
    length = queries.shape[1]
    per_group = queries.shape[0] // groups
    for g in range(groups):
        four_part[0, g] = matmul(score_grad_half[g, :length], grouped(queries, g, per_group), (1, 0))
        four_part[1, g] = matmul(prob_half[g, :length], grouped(grads, g, per_group), (1, 0))


def four_sum_kernel(three_arrived, four_part, four_sum):
    first_core = lax.axis_index("head") == 0

    @pl.when(first_core)
    def _():
        four_sum[...] = four_part[...].astype(jnp.bfloat16)

    @pl.when(jnp.logical_not(first_core))
    def _():
        four_sum[...] = (four_part[...] + three_arrived[...].astype(jnp.float32)).astype(jnp.bfloat16)


def near_backward_kernel(
    queries, grads, near_weights, near_prob_grad, near_factor, row_delta,
    score_grad_half, one_keys, one_values, two_part, own_part,
):
    groups = near_weights.shape[0]
    length, width = queries.shape[1:]
    per_group = queries.shape[0] // groups
    for g in range(groups):
        query = grouped(queries, g, per_group)
        grad = grouped(grads, g, per_group)
        prob = near_weights[g] * near_factor[g]
        half = prob.astype(jnp.bfloat16)
        score_grad = prob * (near_prob_grad[g] - row_delta[g]) * width ** (-0.5)
        score_grad = score_grad.astype(jnp.bfloat16)
        score_grad_half[g] = score_grad
        key_part = matmul(score_grad, query, (1, 0))
        value_part = matmul(half, grad, (1, 0))
        for index, (part, one) in enumerate(((key_part, one_keys), (value_part, one_values))):
            two_part[index, g] = part[:length]
            one[g] = part[length : 2 * length].astype(jnp.bfloat16)
            own_part[index, g] = part[2 * length :]


def two_sum_kernel(one_keys, one_values, three_arrived, two_part, own_part, two_sum, own_sum):
    first_core = lax.axis_index("head") == 0
    ones = (one_keys, one_values)

    @pl.when(first_core)
    def _():
        two_sum[...] = (two_part[...] + three_arrived[...].astype(jnp.float32)).astype(jnp.bfloat16)
        for index, one in enumerate(ones):
            own_sum[index] = own_part[index] + one[...].astype(jnp.float32)

    @pl.when(jnp.logical_not(first_core))
    def _():
        for index, one in enumerate(ones):
            two_sum[index] = (two_part[index] + one[...].astype(jnp.float32)).astype(jnp.bfloat16)
        own_sum[...] = own_part[...]


def query_kernel(
    own, one_keys, back_two, back_three, back_four, attended_rows, far_grad, near_grad,
    own_sum, four_sum, out, query_grad, partial_sum,
):
    groups, length, width = own.shape[1:]
    per_group = out.shape[0] // groups
    partial_sum[...] = own_sum[...] + four_sum[...].astype(jnp.float32)
    for g in range(groups):
        rows = pl.ds(g * per_group, per_group)
        out[rows] = attended_rows[g].T.reshape(per_group, length, width)
        part = matmul(join(back_four[0, g], back_three[0, g]), far_grad[g], (0, 0))
        part += matmul(join(back_two[0, g], one_keys[g], own[0, g]), near_grad[g], (0, 0))
        query_grad[rows] = part.astype(jnp.bfloat16).T.reshape(per_group, length, width)


def final_kernel(partial_sum, two_sum, key_grad, value_grad):
    for index, result in enumerate((key_grad, value_grad)):
        total = partial_sum[index] + two_sum[index].astype(jnp.float32)
        result[...] = total.astype(jnp.bfloat16)


def shards(query_matrix, key_matrix, value_matrix, output_gradient, query_head_spans, slab_offset):
    groups, length, width = key_matrix.shape
    heads = query_matrix.shape[0]
    lanes = heads // groups * length
    half, full = jnp.bfloat16, jnp.float32
    vmem = pl.BlockSpec(memory_space=pltpu.VMEM)
    smem = pl.BlockSpec(memory_space=pltpu.SMEM)
    block_flops = 2 * heads * length * length * width

    def call(kernel, name, flops, outs, arrays, specs=None):
        return pl.pallas_call(
            kernel,
            out_shape=tuple(jax.ShapeDtypeStruct(shape, kind) for shape, kind in outs),
            in_specs=specs or [vmem] * len(arrays),
            out_specs=(vmem,) * len(outs),
            compiler_params=pltpu.CompilerParams(vmem_limit_bytes=40 * 1024 * 1024),
            cost_estimate=pl.CostEstimate(flops=flops, bytes_accessed=0, transcendentals=0),
            name=name,
        )(*arrays)

    def rows_of(count, kind):
        return ((groups, count, lanes), kind)

    single = (key_matrix.shape, half)
    pair = ((2, groups, length, width), half)
    wide_pair = ((2, groups, length, width), full)
    stat = rows_of(1, full)
    first_core = lax.axis_index("head") == 0

    own = jnp.stack([key_matrix, value_matrix])
    back_two = shifted(own, "seq", 1)
    queries, grads = query_matrix, output_gradient
    own_copy, first, own_prob_grad, grad_rows = call(
        prepare_kernel,
        "prepare",
        1,
        [
            pair, rows_of(1, jnp.int32), rows_of(length, full), rows_of(width, half),
        ],
        (query_head_spans, slab_offset, own, grads),
        specs=[smem, smem, vmem, vmem],
    )
    back_four = shifted(own_copy, "seq", 2)
    back_two, own_prob_grad = lax.optimization_barrier((back_two, own_prob_grad))
    back_one = [
        swapped(jnp.where(first_core, own[index], back_two[index]), "head") for index in range(2)
    ]
    near_max, near_sum, near_out, near_weights, near_prob_grad = call(
        near_forward_kernel,
        "near_forward",
        1,
        [stat, stat, rows_of(width, full), rows_of(3 * length, full), rows_of(3 * length, full)],
        (first, queries, own, grads, *back_one, back_two, own_prob_grad),
    )
    back_four, near_max = lax.optimization_barrier((back_four, near_max))
    back_three = swapped(jnp.where(first_core, back_two, back_four), "head")
    attended_rows, row_delta, near_factor, prob_half, far_grad, three_part = call(
        far_kernel,
        "far_forward_backward",
        1,
        [rows_of(width, half), stat, stat, rows_of(2 * length, half), rows_of(2 * length, half), pair],
        (first, queries, grads, back_three, back_four, grad_rows, near_max, near_sum, near_out),
    )
    three_arrived = swapped(three_part, "head")
    (four_part,) = call(
        four_kernel, "four_part", 1, [wide_pair], (queries, grads, prob_half, far_grad)
    )
    (four_sum,) = call(four_sum_kernel, "four_sum", 1000, [pair], (three_arrived, four_part))
    four_total = shifted(four_sum, "seq", -2)
    near_weights, four_sum = lax.optimization_barrier((near_weights, four_sum))
    near_grad, *one_parts, two_part, own_part = call(
        near_backward_kernel,
        "near_backward",
        6 * block_flops,
        [rows_of(3 * length, half), single, single, wide_pair, wide_pair],
        (queries, grads, near_weights, near_prob_grad, near_factor, row_delta),
    )
    one_arrived = [swapped(part, "head") for part in one_parts]
    two_sum, own_sum = call(
        two_sum_kernel,
        "two_sum",
        1000,
        [pair, wide_pair],
        (*one_arrived, three_arrived, two_part, own_part),
    )
    two_total = shifted(two_sum, "seq", -1)
    attn_out, query_grad, partial_sum = call(
        query_kernel,
        "query_grad",
        200 * block_flops,
        [(query_matrix.shape, half)] * 2 + [wide_pair],
        (own, back_one[0], back_two, back_three, back_four, attended_rows, far_grad, near_grad,
         own_sum, four_total),
    )
    key_grad, value_grad = call(
        final_kernel,
        "total",
        1000,
        [(key_matrix.shape, half)] * 2,
        (partial_sum, two_total),
    )
    return (attn_out, query_grad, key_grad, value_grad)


def solution(mesh):
    tokens = P(None, ("seq", "head"), None)
    return jax.shard_map(
        shards,
        mesh=mesh,
        in_specs=(tokens, tokens, tokens, tokens, P(), P()),
        out_specs=(tokens, tokens, tokens, tokens),
        check_vma=False,
    )
```

time: 45.2 us -> 42.2 us (0.934)
  the two profiles are of different devices: /device:TPU:12 before, /device:TPU:14 now
where the time goes in v3:
time: 42.2 us; the launch traced here: 41.9 us
  waiting for transfers between devices  14.3 us (34%)
  starting transfers between devices  14.2 us (34%)
  Pallas kernels  8.24 us (20%)
  other arithmetic  2.09 us (5%)
  local copies, waits for them, and re-layouts  1.7 us (4%)
  between operations  1.43 us (3%)
    ppermute x4, starting transfers between devices, shifted(): return lax.ppermute(block, axis, route)  12.8 us
    ppermute x4, waiting for transfers between devices, shifted(): return lax.ppermute(block, axis, route)  9.64 us
    pallas_call x9, Pallas kernels, call(): pl.pallas_call(kernel, out_shape=tuple((jax.ShapeDtypeStruct(shape, kind)...  8.24 us
    ppermute x6, waiting for transfers between devices, swapped(): return lax.ppermute(block, axis, [(i, count - 1 - i) for i in range(count)])  4.65 us
    unnamed x8, local copies, waits for them, and re-layouts  1.7 us
    ppermute x6, starting transfers between devices, swapped(): return lax.ppermute(block, axis, [(i, count - 1 - i) for i in range(count)])  1.41 us
    another operation x1, other arithmetic, shards(): own = jnp.stack([key_matrix, value_matrix])  1.05 us
    select_n x1, other arithmetic, shards(): jnp.where(first_core, own[index], back_two[index])  1 us
  transfers between devices with their start and end apart: 10, of which 9 were waited for; matrix products, arithmetic and copies ran while one was open for 2% of the time, Pallas kernels for 13%

profile of v3, /device:TPU:14, one launch (start us, length us, event | category | flops | bytes accessed | tf_op | source)
XLA Modules:
  0.0 41.9 jit_solution(9843975711064462717)
XLA Ops:
  0.6 1.1 %pad_maximum_fusion.own = bf16[2,8,64,128]{3,2,1,0:T(8,128)(2,1)S(1)} fusion(bf16[1,8,64,128]{3,2,1,0:T(8,128)(2,1)} %bitcast.6, bf16[1,8,64,128]{3,2,1,0:T(8,128)(2,1)} %bitcast.7), kind=kLoop, calls=%fused_computation | loop fusion | flops 131072 | bytes 524288 | tf_op jit(solution)/shard_map/stack | solution.py:251
  1.7 3.4 %collective-permute-start = (bf16[2,8,64,128]{3,2,1,0:T(8,128)(2,1)S(1)}, bf16[2,8,64,128]{3,2,1,0:T(8,128)(2,1)S(1)}, u32[]{:S(2)}, u32[]{:S(2)}) collective-permute-start(bf16[2,8,64,128]{3,2,1,0:T(8,128)(2,1)S(1)} %pad_maximum_fusion.own), channel_id=1, source_target_pairs={{0,1},{1,2},{2,3},{3,4},{4,5},{5,6},{6,7},{7,8},{8,9},{9,10},{10,1... | collective-permute-start | bytes 786440 | tf_op jit(solution)/shard_map/ppermute | solution.py:19
  5.8 1.0 %copy-done = bf16[32,64,128]{2,1,0:T(8,128)(2,1)S(1)} copy-done((bf16[32,64,128]{2,1,0:T(8,128)(2,1)S(1)}, bf16[32,64,128]{2,1,0:T(8,128)(2,1)}, u32[]{:S(2)}) %copy-start) | copy-done | bytes 524312
  6.8 0.7 %copy-done.3 = s32[32]{0:T(128)S(1)} copy-done((s32[32]{0:T(128)S(1)}, s32[32]{0:T(128)}, u32[]{:S(2)}) %copy-start.3) | copy-done | bytes 152
  7.5 0.9 %prepare.1 = (bf16[2,8,64,128]{3,2,1,0:T(8,128)(2,1)S(1)}, s32[8,1,256]{2,1,0:T(1,128)S(1)}, f32[8,64,256]{2,1,0:T(8,128)S(1)}, bf16[8,128,256]{2,1,0:T(8,128)(2,1)S(1)}) custom-call(s32[32]{0:T(128)S(1)} %copy-done.3, s32[1]{0:T(128)S(6)} %copy.10.offset, bf16[2,8,64,128]{3,2,1,0:T(8,128)(2,1)S(1)} %pad_maximum_fusion.own, bf16[32,64,128]{2,1,0:T(8,128)(2,1)S(1)} %copy-done), custom_call_target="tpu_custom_call" | custom-call | flops 1 | tf_op jit(solution)/shard_map/prepare/pallas_call | solution.py:232
  8.3 3.4 %collective-permute-start.2 = (bf16[2,8,64,128]{3,2,1,0:T(8,128)(2,1)S(1)}, bf16[2,8,64,128]{3,2,1,0:T(8,128)(2,1)S(1)}, u32[]{:S(2)}, u32[]{:S(2)}) collective-permute-start(bf16[2,8,64,128]{3,2,1,0:T(8,128)(2,1)S(1)} %get-tuple-element.38), channel_id=1, source_target_pairs={{0,2},{1,3},{2,4},{3,5},{4,6},{5,7},{6,8},{7,9},{8,10},{9,11},{10,... | collective-permute-start | bytes 786440 | tf_op jit(solution)/shard_map/ppermute | solution.py:19
  11.8 1.0 %bitcast_select_fusion = (bf16[8,64,128]{2,1,0:T(8,128)(2,1)S(1)}, bf16[8,64,128]{2,1,0:T(8,128)(2,1)S(1)}) fusion(bf16[8,64,128]{2,1,0:T(8,128)(2,1)} %param.8, bf16[2,8,64,128]{3,2,1,0:T(8,128)(2,1)S(1)} %collective-permute-done.back_two, pred[]{:T(512)S(6)} %eq.3, bf16[8,64,128]{2,1,0:T(8,128)(2,1)} %param.7), kind=kLoop, calls=%fused_computation.2 | loop fusion | flops 131072 | bytes 786433 | tf_op jit(solution)/shard_map/jit(_where)/select_n | solution.py:267
  12.9 0.5 %collective-permute-start.1 = (bf16[8,64,128]{2,1,0:T(8,128)(2,1)S(1)}, bf16[8,64,128]{2,1,0:T(8,128)(2,1)S(1)}, u32[]{:S(2)}, u32[]{:S(2)}) collective-permute-start(bf16[8,64,128]{2,1,0:T(8,128)(2,1)S(1)} %get-tuple-element.69), channel_id=1, source_target_pairs={{0,16},{16,0},{1,17},{17,1},{2,18},{18,2},{3,19},{19,3},{4,20},{20... | collective-permute-start | bytes 393224 | tf_op jit(solution)/shard_map/ppermute | solution.py:24
  13.3 0.8 %collective-permute-done.3.one_values = bf16[8,64,128]{2,1,0:T(8,128)(2,1)S(1)} collective-permute-done((bf16[8,64,128]{2,1,0:T(8,128)(2,1)S(1)}, bf16[8,64,128]{2,1,0:T(8,128)(2,1)S(1)}, u32[]{:S(2)}, u32[]{:S(2)}) %collective-permute-start.3) | collective-permute-done | bytes 131104 | tf_op jit(solution)/shard_map/ppermute | solution.py:24
  14.4 1.9 %near_forward.1 = (f32[8,1,256]{2,1,0:T(1,128)S(1)}, f32[8,1,256]{2,1,0:T(1,128)S(1)}, f32[8,128,256]{2,1,0:T(8,128)S(1)}, f32[8,192,256]{2,1,0:T(8,128)S(1)}, f32[8,192,256]{2,1,0:T(8,128)S(1)}) custom-call(s32[8,1,256]{2,1,0:T(1,128)S(1)} %get-tuple-element.39.first, bf16[32,64,128]{2,1,0:T(8,128)(2,1)S(1)} %copy-done.2, ...), custom_call_target="tpu_custom_call" | custom-call | flops 1 | tf_op jit(solution)/shard_map/near_forward/pallas_call | solution.py:232
  16.3 1.7 %collective-permute-done.2.back_four = bf16[2,8,64,128]{3,2,1,0:T(8,128)(2,1)S(1)} collective-permute-done((bf16[2,8,64,128]{3,2,1,0:T(8,128)(2,1)S(1)}, bf16[2,8,64,128]{3,2,1,0:T(8,128)(2,1)S(1)}, u32[]{:S(2)}, u32[]{:S(2)}) %collective-permute-start.2) | collective-permute-done | bytes 262176 | tf_op jit(solution)/shard_map/ppermute | solution.py:19
  18.1 1.5 %collective-permute-done.4.back_three = bf16[2,8,64,128]{3,2,1,0:T(8,128)(2,1)S(1)} collective-permute-done((bf16[2,8,64,128]{3,2,1,0:T(8,128)(2,1)S(1)}, bf16[2,8,64,128]{3,2,1,0:T(8,128)(2,1)S(1)}, u32[]{:S(2)}, u32[]{:S(2)}) %collective-permute-start.4) | collective-permute-done | bytes 262176 | tf_op jit(solution)/shard_map/ppermute | solution.py:24
  19.6 2.1 %far_forward_backward.1 = (bf16[8,128,256]{2,1,0:T(8,128)(2,1)S(1)}, f32[8,1,256]{2,1,0:T(1,128)S(1)}, f32[8,1,256]{2,1,0:T(1,128)S(1)}, bf16[8,128,256]{2,1,0:T...) custom-call(s32[8,1,256]{2,1,0:T(1,128)S(1)} %get-tuple-element.39.first, ...), custom_call_target="tpu_custom_call" | custom-call | flops 1 | tf_op jit(solution)/shard_map/far_forward_backward/pallas_call | solution.py:232
  21.9 0.3 four_part.1
  22.2 1.1 %collective-permute-done.5.three_arrived = bf16[2,8,64,128]{3,2,1,0:T(8,128)(2,1)S(1)} collective-permute-done((bf16[2,8,64,128]{3,2,1,0:T(8,128)(2,1)S(1)}, bf16[2,8,64,128]{3,2,1,0:T(8,128)(2,1)S(1)}, u32[]{:S(2)}, u32[]{:S(2)}) %collective-permute-start.5) | collective-permute-done | bytes 262176 | tf_op jit(solution)/shard_map/ppermute | solution.py:24
  23.3 3.3 %collective-permute-start.8 = (bf16[2,8,64,128]{3,2,1,0:T(8,128)(2,1)S(1)}, bf16[2,8,64,128]{3,2,1,0:T(8,128)(2,1)S(1)}, u32[]{:S(2)}, u32[]{:S(2)}) collective-permute-start(bf16[2,8,64,128]{3,2,1,0:T(8,128)(2,1)S(1)} %four_sum.1), channel_id=1, source_target_pairs={{2,0},{3,1},{4,2},{5,3},{6,4},{7,5},{8,6},{9,7},{10,8},{11,9},{12,... | collective-permute-start | bytes 786440 | tf_op jit(solution)/shard_map/ppermute | solution.py:19
  26.6 0.6 %near_backward.1 = (bf16[8,192,256]{2,1,0:T(8,128)(2,1)S(1)}, bf16[8,64,128]{2,1,0:T(8,128)(2,1)S(1)}, bf16[8,64,128]{2,1,0:T(8,128)(2,1)S(1)}, f32[2,8,64,128]{3,2,1,0:T(8,128)S(1)}, f32[2,8,64,128]{3,2,1,0:T(8,128)S(1)}) custom-call(bf16[32,64,128]{2,1,0:T(8,128)(2,1)S(1)} %copy-done.2, bf16[32,64,128]{2,1,0:T(8,128)(2,1)S(1)} %copy-done.1, ...), custom_call_target="tpu_custom_call" | custom-call | flops 201326592 | tf_op jit(solution)/shard_map/near_backward/pallas_call | solution.py:232
  27.4 0.5 %collective-permute-start.7 = (bf16[8,64,128]{2,1,0:T(8,128)(2,1)S(1)}, bf16[8,64,128]{2,1,0:T(8,128)(2,1)S(1)}, u32[]{:S(2)}, u32[]{:S(2)}) collective-permute-start(bf16[8,64,128]{2,1,0:T(8,128)(2,1)S(1)} %get-tuple-element.58), channel_id=1, source_target_pairs={{0,16},{16,0},{1,17},{17,1},{2,18},{18,2},{3,19},{19,3},{4,20},{20... | collective-permute-start | bytes 393224 | tf_op jit(solution)/shard_map/ppermute | solution.py:24
  27.9 0.8 %collective-permute-done.6.one_keys = bf16[8,64,128]{2,1,0:T(8,128)(2,1)S(1)} collective-permute-done((bf16[8,64,128]{2,1,0:T(8,128)(2,1)S(1)}, bf16[8,64,128]{2,1,0:T(8,128)(2,1)S(1)}, u32[]{:S(2)}, u32[]{:S(2)}) %collective-permute-start.6) | collective-permute-done | bytes 131104 | tf_op jit(solution)/shard_map/ppermute | solution.py:24
  29.0 2.6 %collective-permute-start.9 = (bf16[2,8,64,128]{3,2,1,0:T(8,128)(2,1)S(1)}, bf16[2,8,64,128]{3,2,1,0:T(8,128)(2,1)S(1)}, u32[]{:S(2)}, u32[]{:S(2)}) collective-permute-start(bf16[2,8,64,128]{3,2,1,0:T(8,128)(2,1)S(1)} %get-tuple-element.65), channel_id=1, source_target_pairs={{1,0},{2,1},{3,2},{4,3},{5,4},{6,5},{7,6},{8,7},{9,8},{10,9},{11,1... | collective-permute-start | bytes 786440 | tf_op jit(solution)/shard_map/ppermute | solution.py:19
  31.6 2.9 %collective-permute-done.8.four_sum = bf16[2,8,64,128]{3,2,1,0:T(8,128)(2,1)S(1)} collective-permute-done((bf16[2,8,64,128]{3,2,1,0:T(8,128)(2,1)S(1)}, bf16[2,8,64,128]{3,2,1,0:T(8,128)(2,1)S(1)}, u32[]{:S(2)}, u32[]{:S(2)}) %collective-permute-start.8) | collective-permute-done | bytes 262176 | tf_op jit(solution)/shard_map/ppermute | solution.py:19
  34.5 1.6 %query_grad.1 = (bf16[32,64,128]{2,1,0:T(8,128)(2,1)}, bf16[32,64,128]{2,1,0:T(8,128)(2,1)}, f32[2,8,64,128]{3,2,1,0:T(8,128)S(1)}) custom-call(bf16[2,8,64,128]{3,2,1,0:T(8,128)(2,1)S(1)} %pad_maximum_fusion.own, bf16[8,64,128]{2,1,0:T(8,128)(2,1)S(1)} %collective-permute-done.1.one_keys, bf16[2,8,64,128]{3,2,1,0:T(8,128)(2,1)S(1)} %collective-permute-done.back_two, ...), custom_call_target="tpu_custom_call" | custom-call | flops 6710886400 | tf_op jit(solution)/shard_map/query_grad/pallas_call | solution.py:232
  36.1 5.1 %collective-permute-done.9.two_sum = bf16[2,8,64,128]{3,2,1,0:T(8,128)(2,1)S(1)} collective-permute-done((bf16[2,8,64,128]{3,2,1,0:T(8,128)(2,1)S(1)}, bf16[2,8,64,128]{3,2,1,0:T(8,128)(2,1)S(1)}, u32[]{:S(2)}, u32[]{:S(2)}) %collective-permute-start.9) | collective-permute-done | bytes 262176 | tf_op jit(solution)/shard_map/ppermute | solution.py:19
  41.2 0.7 %total.1 = (bf16[8,64,128]{2,1,0:T(8,128)(2,1)}, bf16[8,64,128]{2,1,0:T(8,128)(2,1)}) custom-call(f32[2,8,64,128]{3,2,1,0:T(8,128)S(1)} %get-tuple-element.64.partial_sum, bf16[2,8,64,128]{3,2,1,0:T(8,128)(2,1)S(1)} %collective-permute-done.9.two_sum), custom_call_target="tpu_custom_call" | custom-call | flops 1000 | tf_op jit(solution)/shard_map/total/pallas_call | solution.py:232
  (16 shorter events, 1.0 us)
Async XLA Ops:
  0.6 13.7 %copy-start.1 = (bf16[32,64,128]{2,1,0:T(8,128)(2,1)S(1)}, bf16[32,64,128]{2,1,0:T(8,128)(2,1)}, u32[]{:S(2)}) copy-start(bf16[32,64,128]{2,1,0:T(8,128)(2,1)} %grads.9) | copy-start | bytes 1572868
  1.7 10.1 %collective-permute-start = (bf16[2,8,64,128]{3,2,1,0:T(8,128)(2,1)S(1)}, bf16[2,8,64,128]{3,2,1,0:T(8,128)(2,1)S(1)}, u32[]{:S(2)}, u32[]{:S(2)}) collective-permute-start(bf16[2,8,64,128]{3,2,1,0:T(8,128)(2,1)S(1)} %pad_maximum_fusion.own), channel_id=1, source_target_pairs={{0,1},{1,2},{2,3},{3,4},{4,5},{5,6},{6,7},{7,8},{8,9},{9,10},{10,1... | collective-permute-start | bytes 786440 | tf_op jit(solution)/shard_map/ppermute | solution.py:19
  5.8 1.0 %copy-start = (bf16[32,64,128]{2,1,0:T(8,128)(2,1)S(1)}, bf16[32,64,128]{2,1,0:T(8,128)(2,1)}, u32[]{:S(2)}) copy-start(bf16[32,64,128]{2,1,0:T(8,128)(2,1)} %grads.9) | copy-start | bytes 1572868
  6.8 0.7 %copy-start.3 = (s32[32]{0:T(128)S(1)}, s32[32]{0:T(128)}, u32[]{:S(2)}) copy-start(s32[32]{0:T(128)} %spans.1) | copy-start | bytes 388
  7.5 6.9 %copy-start.2 = (bf16[32,64,128]{2,1,0:T(8,128)(2,1)S(1)}, bf16[32,64,128]{2,1,0:T(8,128)(2,1)}, u32[]{:S(2)}) copy-start(bf16[32,64,128]{2,1,0:T(8,128)(2,1)} %queries.7) | copy-start | bytes 1572868
  8.3 9.7 %collective-permute-start.2 = (bf16[2,8,64,128]{3,2,1,0:T(8,128)(2,1)S(1)}, bf16[2,8,64,128]{3,2,1,0:T(8,128)(2,1)S(1)}, u32[]{:S(2)}, u32[]{:S(2)}) collective-permute-start(bf16[2,8,64,128]{3,2,1,0:T(8,128)(2,1)S(1)} %get-tuple-element.38), channel_id=1, source_target_pairs={{0,2},{1,3},{2,4},{3,5},{4,6},{5,7},{6,8},{7,9},{8,10},{9,11},{10,... | collective-permute-start | bytes 786440 | tf_op jit(solution)/shard_map/ppermute | solution.py:19
  12.8 1.4 %collective-permute-start.3 = (bf16[8,64,128]{2,1,0:T(8,128)(2,1)S(1)}, bf16[8,64,128]{2,1,0:T(8,128)(2,1)S(1)}, u32[]{:S(2)}, u32[]{:S(2)}) collective-permute-start(bf16[8,64,128]{2,1,0:T(8,128)(2,1)S(1)} %get-tuple-element.68), channel_id=1, source_target_pairs={{0,16},{16,0},{1,17},{17,1},{2,18},{18,2},{3,19},{19,3},{4,20},{20... | collective-permute-start | bytes 393224 | tf_op jit(solution)/shard_map/ppermute | solution.py:24
  12.9 1.5 %collective-permute-start.1 = (bf16[8,64,128]{2,1,0:T(8,128)(2,1)S(1)}, bf16[8,64,128]{2,1,0:T(8,128)(2,1)S(1)}, u32[]{:S(2)}, u32[]{:S(2)}) collective-permute-start(bf16[8,64,128]{2,1,0:T(8,128)(2,1)S(1)} %get-tuple-element.69), channel_id=1, source_target_pairs={{0,16},{16,0},{1,17},{17,1},{2,18},{18,2},{3,19},{19,3},{4,20},{20... | collective-permute-start | bytes 393224 | tf_op jit(solution)/shard_map/ppermute | solution.py:24
  18.0 1.6 %collective-permute-start.4 = (bf16[2,8,64,128]{3,2,1,0:T(8,128)(2,1)S(1)}, bf16[2,8,64,128]{3,2,1,0:T(8,128)(2,1)S(1)}, u32[]{:S(2)}, u32[]{:S(2)}) collective-permute-start(bf16[2,8,64,128]{3,2,1,0:T(8,128)(2,1)S(1)} %broadcast_select_fusion), channel_id=1, source_target_pairs={{0,16},{16,0},{1,17},{17,1},{2,18},{18,2},{3,19},{19,3},{4,20},{20... | collective-permute-start | bytes 786440 | tf_op jit(solution)/shard_map/ppermute | solution.py:24
  21.7 1.6 %collective-permute-start.5 = (bf16[2,8,64,128]{3,2,1,0:T(8,128)(2,1)S(1)}, bf16[2,8,64,128]{3,2,1,0:T(8,128)(2,1)S(1)}, u32[]{:S(2)}, u32[]{:S(2)}) collective-permute-start(bf16[2,8,64,128]{3,2,1,0:T(8,128)(2,1)S(1)} %get-tuple-element.50), channel_id=1, source_target_pairs={{0,16},{16,0},{1,17},{17,1},{2,18},{18,2},{3,19},{19,3},{4,20},{20... | collective-permute-start | bytes 786440 | tf_op jit(solution)/shard_map/ppermute | solution.py:24
  23.3 11.2 %collective-permute-start.8 = (bf16[2,8,64,128]{3,2,1,0:T(8,128)(2,1)S(1)}, bf16[2,8,64,128]{3,2,1,0:T(8,128)(2,1)S(1)}, u32[]{:S(2)}, u32[]{:S(2)}) collective-permute-start(bf16[2,8,64,128]{3,2,1,0:T(8,128)(2,1)S(1)} %four_sum.1), channel_id=1, source_target_pairs={{2,0},{3,1},{4,2},{5,3},{6,4},{7,5},{8,6},{9,7},{10,8},{11,9},{12,... | collective-permute-start | bytes 786440 | tf_op jit(solution)/shard_map/ppermute | solution.py:19
  27.3 1.4 %collective-permute-start.6 = (bf16[8,64,128]{2,1,0:T(8,128)(2,1)S(1)}, bf16[8,64,128]{2,1,0:T(8,128)(2,1)S(1)}, u32[]{:S(2)}, u32[]{:S(2)}) collective-permute-start(bf16[8,64,128]{2,1,0:T(8,128)(2,1)S(1)} %get-tuple-element.57), channel_id=1, source_target_pairs={{0,16},{16,0},{1,17},{17,1},{2,18},{18,2},{3,19},{19,3},{4,20},{20... | collective-permute-start | bytes 393224 | tf_op jit(solution)/shard_map/ppermute | solution.py:24
  27.4 1.5 %collective-permute-start.7 = (bf16[8,64,128]{2,1,0:T(8,128)(2,1)S(1)}, bf16[8,64,128]{2,1,0:T(8,128)(2,1)S(1)}, u32[]{:S(2)}, u32[]{:S(2)}) collective-permute-start(bf16[8,64,128]{2,1,0:T(8,128)(2,1)S(1)} %get-tuple-element.58), channel_id=1, source_target_pairs={{0,16},{16,0},{1,17},{17,1},{2,18},{18,2},{3,19},{19,3},{4,20},{20... | collective-permute-start | bytes 393224 | tf_op jit(solution)/shard_map/ppermute | solution.py:24
  29.0 12.2 %collective-permute-start.9 = (bf16[2,8,64,128]{3,2,1,0:T(8,128)(2,1)S(1)}, bf16[2,8,64,128]{3,2,1,0:T(8,128)(2,1)S(1)}, u32[]{:S(2)}, u32[]{:S(2)}) collective-permute-start(bf16[2,8,64,128]{3,2,1,0:T(8,128)(2,1)S(1)} %get-tuple-element.65), channel_id=1, source_target_pairs={{1,0},{2,1},{3,2},{4,3},{5,4},{6,5},{7,6},{8,7},{9,8},{10,9},{11,1... | collective-permute-start | bytes 786440 | tf_op jit(solution)/shard_map/ppermute | solution.py:19

commit v4 on v3

v4 whole, which is shorter than its diff:
```python
import math

import jax
import jax.numpy as jnp
from jax import lax
from jax.experimental import pallas as pl
from jax.experimental.pallas import tpu as pltpu
from jax.sharding import PartitionSpec as P

REACH = 2
SEGMENT = 512

masked_score = -1e30


def shifted(block, axis, distance):
    devices = range(lax.axis_size(axis))
    route = [(i - distance, i) for i in devices if i - distance in devices]
    return lax.ppermute(block, axis, route)


def swapped(block, axis):
    count = lax.axis_size(axis)
    return lax.ppermute(block, axis, [(i, count - 1 - i) for i in range(count)])


def matmul(left, right, contract):
    return lax.dot_general(
        left, right, ((contract[:1], contract[1:]), ((), ())), preferred_element_type=jnp.float32
    )


def grouped(ref, g, per_group):
    _, length, width = ref.shape
    return ref[pl.ds(g * per_group, per_group)].reshape(per_group * length, width)


def first_visible(spans, offset, groups, per_group, length):
    lanes = per_group * length
    start = (lax.axis_index("seq") * lax.axis_size("head") + lax.axis_index("head")) * length
    lane = lax.broadcasted_iota(jnp.int32, (1, lanes), 1)
    lane_head = lane // length
    query_pos = start + lane - lane_head * length
    segment_start = query_pos - lax.bitwise_and(offset[0] + query_pos, SEGMENT - 1)
    floor = jnp.maximum(segment_start, 0)
    result = []
    for g in range(groups):
        span = jnp.full((1, lanes), spans[g * per_group], jnp.int32)
        for a in range(1, per_group):
            span = jnp.where(lane_head == a, spans[g * per_group + a], span)
        result.append(jnp.maximum(floor, query_pos - span + 1) - start)
    return result


def join(*blocks):
    return jnp.concatenate(blocks, axis=0)


def masked(scores, first, backs, length):
    row = lax.broadcasted_iota(jnp.int32, (length, scores.shape[1]), 0)
    pieces = []
    for i, back in enumerate(backs):
        visible = row >= first + back * length
        if back == 0:
            lane = lax.broadcasted_iota(jnp.int32, row.shape, 1)
            visible &= row <= lane - lane // length * length
        pieces.append(jnp.where(visible, scores[i * length : (i + 1) * length], masked_score))
    return jnp.concatenate(pieces, axis=0)


def prepare_kernel(own, grads, own_copy, own_prob_grad, grad_rows):
    _, groups, length, width = own.shape
    per_group = grads.shape[0] // groups
    own_copy[...] = own[...]
    for g in range(groups):
        grad = grouped(grads, g, per_group)
        own_prob_grad[g] = matmul(own[1, g], grad, (1, 1))
        grad_rows[g] = grad.T


def own_kernel(spans, offset, queries, own, first, own_scores):
    _, groups, length, width = own.shape
    per_group = queries.shape[0] // groups
    factor = width ** (-0.5) * math.log2(math.e)
    for g, rows in enumerate(first_visible(spans, offset, groups, per_group, length)):
        first[g] = rows
        scores = matmul(own[0, g], grouped(queries, g, per_group), (1, 1)) * factor
        own_scores[g] = masked(scores, rows, (0,), length)


def near_forward_kernel(
    first, queries, own, grads, one_keys, one_values, back_two, own_scores, own_prob_grad,
    near_max, near_sum, near_out, near_weights, near_prob_grad,
):
    _, groups, length, width = own.shape
    per_group = queries.shape[0] // groups
    factor = width ** (-0.5) * math.log2(math.e)
    for g in range(groups):
        query = grouped(queries, g, per_group)
        grad = grouped(grads, g, per_group)
        scores = matmul(join(back_two[0, g], one_keys[g]), query, (1, 1)) * factor
        scores = join(masked(scores, first[g], (2, 1), length), own_scores[g])
        row_max = jnp.max(scores, axis=0, keepdims=True)
        weights = jnp.exp2(scores - row_max)
        near_max[g] = row_max
        near_sum[g] = jnp.sum(weights, axis=0, keepdims=True)
        near_weights[g] = weights
        near_out[g] = matmul(
            join(back_two[1, g], one_values[g], own[1, g]), weights.astype(jnp.bfloat16), (0, 0)
        )
        prob_grad = matmul(join(back_two[1, g], one_values[g]), grad, (1, 1))
        near_prob_grad[g] = join(prob_grad, own_prob_grad[g])


def four_forward_kernel(
    first, queries, grads, back_four, near_max, near_sum, near_out,
    most_max, most_sum, most_out, near_factor, four_weights, four_prob_grad,
):
    _, groups, length, width = back_four.shape
    per_group = queries.shape[0] // groups
    factor = width ** (-0.5) * math.log2(math.e)
    for g in range(groups):
        query = grouped(queries, g, per_group)
        grad = grouped(grads, g, per_group)
        scores = matmul(back_four[0, g], query, (1, 1)) * factor
        scores = masked(scores, first[g], (4,), length)
        row_max = jnp.maximum(near_max[g], jnp.max(scores, axis=0, keepdims=True))
        weights = jnp.exp2(scores - row_max)
        rescale = jnp.exp2(near_max[g] - row_max)
        most_max[g] = row_max
        most_sum[g] = near_sum[g] * rescale + jnp.sum(weights, axis=0, keepdims=True)
        most_out[g] = near_out[g] * rescale + matmul(
            back_four[1, g], weights.astype(jnp.bfloat16), (0, 0)
        )
        near_factor[g] = rescale
        four_weights[g] = weights
        four_prob_grad[g] = matmul(back_four[1, g], grad, (1, 1))


def three_kernel(
    first, queries, grads, back_three, grad_rows, most_max, most_sum, most_out,
    attended_rows, row_delta, most_factor, three_grad, three_part,
):
    _, groups, length, width = back_three.shape
    per_group = queries.shape[0] // groups
    scale = width ** (-0.5)
    for g in range(groups):
        query = grouped(queries, g, per_group)
        grad = grouped(grads, g, per_group)
        scores = matmul(back_three[0, g], query, (1, 1)) * (scale * math.log2(math.e))
        scores = masked(scores, first[g], (3,), length)
        row_max = jnp.maximum(most_max[g], jnp.max(scores, axis=0, keepdims=True))
        weights = jnp.exp2(scores - row_max)
        rescale = jnp.exp2(most_max[g] - row_max)
        inverse = 1.0 / (most_sum[g] * rescale + jnp.sum(weights, axis=0, keepdims=True))
        weighted = matmul(back_three[1, g], weights.astype(jnp.bfloat16), (0, 0))
        attended = ((most_out[g] * rescale + weighted) * inverse).astype(jnp.bfloat16)
        delta = jnp.sum(
            grad_rows[g].astype(jnp.float32) * attended.astype(jnp.float32), axis=0, keepdims=True
        )
        prob = weights * inverse
        prob_grad = matmul(back_three[1, g], grad, (1, 1))
        score_grad = (prob * (prob_grad - delta) * scale).astype(jnp.bfloat16)
        attended_rows[g] = attended
        row_delta[g] = delta
        most_factor[g] = rescale * inverse
        three_grad[g] = score_grad
        three_part[0, g] = matmul(score_grad, query, (1, 0)).astype(jnp.bfloat16)
        three_part[1, g] = matmul(prob.astype(jnp.bfloat16), grad, (1, 0)).astype(jnp.bfloat16)


def four_backward_kernel(
    queries, grads, four_weights, four_prob_grad, most_factor, row_delta, four_grad, four_part
):
    groups = four_weights.shape[0]
    length, width = queries.shape[1:]
    per_group = queries.shape[0] // groups
    for g in range(groups):
        prob = four_weights[g] * most_factor[g]
        score_grad = prob * (four_prob_grad[g] - row_delta[g]) * width ** (-0.5)
        score_grad = score_grad.astype(jnp.bfloat16)
        four_grad[g] = score_grad
        four_part[0, g] = matmul(score_grad, grouped(queries, g, per_group), (1, 0))
        four_part[1, g] = matmul(prob.astype(jnp.bfloat16), grouped(grads, g, per_group), (1, 0))


def four_sum_kernel(three_arrived, four_part, four_sum):
    first_core = lax.axis_index("head") == 0

    @pl.when(first_core)
    def _():
        four_sum[...] = four_part[...].astype(jnp.bfloat16)

    @pl.when(jnp.logical_not(first_core))
    def _():
        four_sum[...] = (four_part[...] + three_arrived[...].astype(jnp.float32)).astype(jnp.bfloat16)


def near_backward_kernel(
    queries, grads, near_weights, near_prob_grad, near_factor, most_factor, row_delta,
    score_grad_half, one_part, two_part, own_part,
):
    groups = near_weights.shape[0]
    length, width = queries.shape[1:]
    per_group = queries.shape[0] // groups
    for g in range(groups):
        query = grouped(queries, g, per_group)
        grad = grouped(grads, g, per_group)
        prob = near_weights[g] * (near_factor[g] * most_factor[g])
        half = prob.astype(jnp.bfloat16)
        score_grad = prob * (near_prob_grad[g] - row_delta[g]) * width ** (-0.5)
        score_grad = score_grad.astype(jnp.bfloat16)
        score_grad_half[g] = score_grad
        key_part = matmul(score_grad, query, (1, 0))
        value_part = matmul(half, grad, (1, 0))
        for index, part in enumerate((key_part, value_part)):
            two_part[index, g] = part[:length]
            one_part[index, g] = part[length : 2 * length].astype(jnp.bfloat16)
            own_part[index, g] = part[2 * length :]


def two_sum_kernel(one_arrived, three_arrived, two_part, own_part, two_sum, own_sum):
    first_core = lax.axis_index("head") == 0

    @pl.when(first_core)
    def _():
        two_sum[...] = (two_part[...] + three_arrived[...].astype(jnp.float32)).astype(jnp.bfloat16)
        own_sum[...] = own_part[...] + one_arrived[...].astype(jnp.float32)

    @pl.when(jnp.logical_not(first_core))
    def _():
        two_sum[...] = (two_part[...] + one_arrived[...].astype(jnp.float32)).astype(jnp.bfloat16)
        own_sum[...] = own_part[...]


def query_kernel(
    own, one_keys, back_two, back_three, back_four, attended_rows, four_grad, three_grad, near_grad,
    own_sum, four_sum, out, query_grad, partial_sum,
):
    groups, length, width = own.shape[1:]
    per_group = out.shape[0] // groups
    partial_sum[...] = own_sum[...] + four_sum[...].astype(jnp.float32)
    for g in range(groups):
        rows = pl.ds(g * per_group, per_group)
        out[rows] = attended_rows[g].T.reshape(per_group, length, width)
        part = matmul(
            join(back_four[0, g], back_three[0, g], back_two[0, g], one_keys[g], own[0, g]),
            join(four_grad[g], three_grad[g], near_grad[g]),
            (0, 0),
        )
        query_grad[rows] = part.astype(jnp.bfloat16).T.reshape(per_group, length, width)


def final_kernel(partial_sum, two_sum, key_grad, value_grad):
    for index, result in enumerate((key_grad, value_grad)):
        total = partial_sum[index] + two_sum[index].astype(jnp.float32)
        result[...] = total.astype(jnp.bfloat16)


def shards(query_matrix, key_matrix, value_matrix, output_gradient, query_head_spans, slab_offset):
    groups, length, width = key_matrix.shape
    heads = query_matrix.shape[0]
    lanes = heads // groups * length
    half, full = jnp.bfloat16, jnp.float32
    vmem = pl.BlockSpec(memory_space=pltpu.VMEM)
    smem = pl.BlockSpec(memory_space=pltpu.SMEM)
    block_flops = 2 * heads * length * length * width

    def call(kernel, name, flops, outs, arrays, specs=None):
        return pl.pallas_call(
            kernel,
            out_shape=tuple(jax.ShapeDtypeStruct(shape, kind) for shape, kind in outs),
            in_specs=specs or [vmem] * len(arrays),
            out_specs=(vmem,) * len(outs),
            compiler_params=pltpu.CompilerParams(vmem_limit_bytes=40 * 1024 * 1024),
            cost_estimate=pl.CostEstimate(flops=flops, bytes_accessed=0, transcendentals=0),
            name=name,
        )(*arrays)

    def rows_of(count, kind):
        return ((groups, count, lanes), kind)

    pair = ((2, groups, length, width), half)
    wide_pair = ((2, groups, length, width), full)
    stat = rows_of(1, full)
    first_core = lax.axis_index("head") == 0

    own = jnp.stack([key_matrix, value_matrix])
    back_two = shifted(own, "seq", 1)
    queries, grads = query_matrix, output_gradient
    own_copy, own_prob_grad, grad_rows = call(
        prepare_kernel,
        "prepare",
        1,
        [pair, rows_of(length, full), rows_of(width, half)],
        (own, grads),
    )
    back_four = shifted(own_copy, "seq", 2)
    query_head_spans, own_prob_grad = lax.optimization_barrier((query_head_spans, own_prob_grad))
    first, own_scores = call(
        own_kernel,
        "own_block",
        1,
        [rows_of(1, jnp.int32), rows_of(length, full)],
        (query_head_spans, slab_offset, queries, own_copy),
        specs=[smem, smem, vmem, vmem],
    )
    back_two, own_scores = lax.optimization_barrier((back_two, own_scores))
    back_one = [
        swapped(jnp.where(first_core, own_copy[index], back_two[index]), "head")
        for index in range(2)
    ]
    near_max, near_sum, near_out, near_weights, near_prob_grad = call(
        near_forward_kernel,
        "near_forward",
        1,
        [stat, stat, rows_of(width, full), rows_of(3 * length, full), rows_of(3 * length, full)],
        (first, queries, own_copy, grads, *back_one, back_two, own_scores, own_prob_grad),
    )
    back_four, near_max = lax.optimization_barrier((back_four, near_max))
    back_three = swapped(jnp.where(first_core, back_two, back_four), "head")
    most_max, most_sum, most_out, near_factor, four_weights, four_prob_grad = call(
        four_forward_kernel,
        "four_forward",
        1,
        [stat, stat, rows_of(width, full), stat, rows_of(length, full), rows_of(length, full)],
        (first, queries, grads, back_four, near_max, near_sum, near_out),
    )
    attended_rows, row_delta, most_factor, three_grad, three_part = call(
        three_kernel,
        "three_forward_backward",
        1,
        [rows_of(width, half), stat, stat, rows_of(length, half), pair],
        (first, queries, grads, back_three, grad_rows, most_max, most_sum, most_out),
    )
    three_arrived = swapped(three_part, "head")
    four_grad, four_part = call(
        four_backward_kernel,
        "four_backward",
        1,
        [rows_of(length, half), wide_pair],
        (queries, grads, four_weights, four_prob_grad, most_factor, row_delta),
    )
    near_grad, one_part, two_part, own_part = call(
        near_backward_kernel,
        "near_backward",
        1,
        [rows_of(3 * length, half), pair, wide_pair, wide_pair],
        (queries, grads, near_weights, near_prob_grad, near_factor, most_factor, row_delta),
    )
    one_arrived = swapped(one_part, "head")
    three_arrived, near_grad = lax.optimization_barrier((three_arrived, near_grad))
    (four_sum,) = call(four_sum_kernel, "four_sum", 1, [pair], (three_arrived, four_part))
    four_total = shifted(four_sum, "seq", -2)
    two_sum, own_sum = call(
        two_sum_kernel,
        "two_sum",
        1,
        [pair, wide_pair],
        (one_arrived, three_arrived, two_part, own_part),
    )
    two_total = shifted(two_sum, "seq", -1)
    attn_out, query_grad, partial_sum = call(
        query_kernel,
        "query_grad",
        200 * block_flops,
        [(query_matrix.shape, half)] * 2 + [wide_pair],
        (own_copy, back_one[0], back_two, back_three, back_four, attended_rows, four_grad,
         three_grad, near_grad, own_sum, four_total),
    )
    key_grad, value_grad = call(
        final_kernel,
        "total",
        1000,
        [(key_matrix.shape, half)] * 2,
        (partial_sum, two_total),
    )
    return (attn_out, query_grad, key_grad, value_grad)


def solution(mesh):
    tokens = P(None, ("seq", "head"), None)
    return jax.shard_map(
        shards,
        mesh=mesh,
        in_specs=(tokens, tokens, tokens, tokens, P(), P()),
        out_specs=(tokens, tokens, tokens, tokens),
        check_vma=False,
    )
```

time: 42.2 us -> 43.1 us (1.021)
  the two profiles are of different devices: /device:TPU:14 before, /device:TPU:2 now
where the time goes in v4:
time: 43.1 us; the launch traced here: 42.7 us
  waiting for transfers between devices  13.1 us (30%)
  starting transfers between devices  12.2 us (28%)
  Pallas kernels  10.3 us (24%)
  local copies, waits for them, and re-layouts  4.57 us (11%)
  between operations  1.46 us (3%)
  other arithmetic  1.11 us (3%)
    ppermute x4, waiting for transfers between devices, shifted(): return lax.ppermute(block, axis, route)  12.1 us
    ppermute x4, starting transfers between devices, shifted(): return lax.ppermute(block, axis, route)  10.6 us
    pallas_call x11, Pallas kernels, call(): pl.pallas_call(kernel, out_shape=tuple((jax.ShapeDtypeStruct(shape, kind)...  10.3 us
    unnamed x14, local copies, waits for them, and re-layouts  4.57 us
    ppermute x5, starting transfers between devices, swapped(): return lax.ppermute(block, axis, [(i, count - 1 - i) for i in range(count)])  1.59 us
    another operation x1, other arithmetic, shards(): own = jnp.stack([key_matrix, value_matrix])  1.05 us
    ppermute x5, waiting for transfers between devices, swapped(): return lax.ppermute(block, axis, [(i, count - 1 - i) for i in range(count)])  1.03 us
  transfers between devices with their start and end apart: 9, of which 3 were waited for; matrix products, arithmetic and copies ran while one was open for 0% of the time, Pallas kernels for 17%

profile of v4, /device:TPU:2, one launch (start us, length us, event | category | flops | bytes accessed | tf_op | source)
XLA Modules:
  0.0 42.7 jit_solution(13959732412973212903)
XLA Ops:
  0.6 1.1 %pad_maximum_fusion.own = bf16[2,8,64,128]{3,2,1,0:T(8,128)(2,1)S(1)} fusion(bf16[1,8,64,128]{3,2,1,0:T(8,128)(2,1)} %bitcast.6, bf16[1,8,64,128]{3,2,1,0:T(8,128)(2,1)} %bitcast.7), kind=kLoop, calls=%fused_computation | loop fusion | flops 131072 | bytes 524288 | tf_op jit(solution)/shard_map/stack | solution.py:288
  1.7 3.4 %collective-permute-start = (bf16[2,8,64,128]{3,2,1,0:T(8,128)(2,1)S(1)}, bf16[2,8,64,128]{3,2,1,0:T(8,128)(2,1)S(1)}, u32[]{:S(2)}, u32[]{:S(2)}) collective-permute-start(bf16[2,8,64,128]{3,2,1,0:T(8,128)(2,1)S(1)} %pad_maximum_fusion.own), channel_id=1, source_target_pairs={{0,1},{1,2},{2,3},{3,4},{4,5},{5,6},{6,7},{7,8},{8,9},{9,10},{10,1... | collective-permute-start | bytes 786440 | tf_op jit(solution)/shard_map/ppermute | solution.py:19
  5.1 1.0 %copy-done = bf16[32,64,128]{2,1,0:T(8,128)(2,1)S(1)} copy-done((bf16[32,64,128]{2,1,0:T(8,128)(2,1)S(1)}, bf16[32,64,128]{2,1,0:T(8,128)(2,1)}, u32[]{:S(2)}) %copy-start) | copy-done | bytes 524312
  6.2 0.3 prepare.1
  6.5 3.4 %collective-permute-start.2 = (bf16[2,8,64,128]{3,2,1,0:T(8,128)(2,1)S(1)}, bf16[2,8,64,128]{3,2,1,0:T(8,128)(2,1)S(1)}, u32[]{:S(2)}, u32[]{:S(2)}) collective-permute-start(bf16[2,8,64,128]{3,2,1,0:T(8,128)(2,1)S(1)} %get-tuple-element.46.own), channel_id=1, source_target_pairs={{0,2},{1,3},{2,4},{3,5},{4,6},{5,7},{6,8},{7,9},{8,10},{9,11},{10,... | collective-permute-start | bytes 786440 | tf_op jit(solution)/shard_map/ppermute | solution.py:19
  10.6 1.0 %copy-done.2 = bf16[32,64,128]{2,1,0:T(8,128)(2,1)S(1)} copy-done((bf16[32,64,128]{2,1,0:T(8,128)(2,1)S(1)}, bf16[32,64,128]{2,1,0:T(8,128)(2,1)}, u32[]{:S(2)}) %copy-start.2) | copy-done | bytes 524312
  11.6 0.7 %copy-done.6 = s32[32]{0:T(128)S(1)} copy-done((s32[32]{0:T(128)S(1)}, s32[32]{0:T(128)}, u32[]{:S(2)}) %copy-start.6) | copy-done | bytes 152
  12.2 0.8 %own_block.1 = (s32[8,1,256]{2,1,0:T(1,128)S(1)}, f32[8,64,256]{2,1,0:T(8,128)S(1)}) custom-call(s32[32]{0:T(128)S(1)} %copy-done.6, s32[1]{0:T(128)S(6)} %copy.10.offset, bf16[32,64,128]{2,1,0:T(8,128)(2,1)S(1)} %copy-done.2, bf16[2,8,64,128]{3,2,1,0:T(8,128)(2,1)S(1)} %get-tuple-element.46.own), custom_call_target="tpu_custom_call" | custom-call | flops 1 | tf_op jit(solution)/shard_map/own_block/pallas_call | solution.py:270
  13.1 0.8 %copy-done.4 = f32[8,64,256]{2,1,0:T(8,128)} copy-done((f32[8,64,256]{2,1,0:T(8,128)}, f32[8,64,256]{2,1,0:T(8,128)S(1)}, u32[]{:S(2)}) %copy-start.4) | copy-done | bytes 524312
  14.0 0.5 %collective-permute-start.3 = (bf16[8,64,128]{2,1,0:T(8,128)(2,1)S(1)}, bf16[8,64,128]{2,1,0:T(8,128)(2,1)S(1)}, u32[]{:S(2)}, u32[]{:S(2)}) collective-permute-start(bf16[8,64,128]{2,1,0:T(8,128)(2,1)S(1)} %get-tuple-element.88), channel_id=1, source_target_pairs={{0,16},{16,0},{1,17},{17,1},{2,18},{18,2},{3,19},{19,3},{4,20},{20... | collective-permute-start | bytes 393224 | tf_op jit(solution)/shard_map/ppermute | solution.py:24
  14.5 0.8 %collective-permute-done.1.one_keys = bf16[8,64,128]{2,1,0:T(8,128)(2,1)S(1)} collective-permute-done((bf16[8,64,128]{2,1,0:T(8,128)(2,1)S(1)}, bf16[8,64,128]{2,1,0:T(8,128)(2,1)S(1)}, u32[]{:S(2)}, u32[]{:S(2)}) %collective-permute-start.1) | collective-permute-done | bytes 131104 | tf_op jit(solution)/shard_map/ppermute | solution.py:24
  15.5 1.0 %copy-done.5 = f32[8,64,256]{2,1,0:T(8,128)S(1)} copy-done((f32[8,64,256]{2,1,0:T(8,128)S(1)}, f32[8,64,256]{2,1,0:T(8,128)}, u32[]{:S(2)}) %copy-start.5) | copy-done | bytes 524312
  16.6 1.9 %near_forward.1 = (f32[8,1,256]{2,1,0:T(1,128)S(1)}, f32[8,1,256]{2,1,0:T(1,128)S(1)}, f32[8,128,256]{2,1,0:T(8,128)S(1)}, f32[8,192,256]{2,1,0:T(8,128)S(1)}, f32[8,192,256]{2,1,0:T(8,128)S(1)}) custom-call(s32[8,1,256]{2,1,0:T(1,128)S(1)} %get-tuple-element.51.first, bf16[32,64,128]{2,1,0:T(8,128)(2,1)S(1)} %copy-done.3, ...), custom_call_target="tpu_custom_call" | custom-call | flops 1 | tf_op jit(solution)/shard_map/near_forward/pallas_call | solution.py:270
  18.5 0.4 collective-permute-start.4
  18.9 1.5 %four_forward.1 = (f32[8,1,256]{2,1,0:T(1,128)S(1)}, f32[8,1,256]{2,1,0:T(1,128)S(1)}, f32[8,128,256]{2,1,0:T(8,128)S(1)}, f32[8,1,256]{2,1,0:T(1,128)S(1)}, f32...) custom-call(s32[8,1,256]{2,1,0:T(1,128)S(1)} %get-tuple-element.51.first, bf16[32,64,128]{2,1,0:T(8,128)(2,1)S(1)} %copy-done.3, ...), custom_call_target="tpu_custom_call" | custom-call | flops 1 | tf_op jit(solution)/shard_map/four_forward/pallas_call | solution.py:270
  20.4 2.3 %three_forward_backward.1 = (bf16[8,128,256]{2,1,0:T(8,128)(2,1)S(1)}, f32[8,1,256]{2,1,0:T(1,128)S(1)}, f32[8,1,256]{2,1,0:T(1,128)S(1)}, bf16[8,64,256]{2,1,0:T(8,128)(2,1)S(1)}, bf16[2,8,64,128]{3,2,1,0:T(8,128)(2,1)S(1)}) custom-call(s32[8,1,256]{2,1,0:T(1,128)S(1)} %get-tuple-element.51.first, bf16[32,64,128]{2,1,0:T(8,128)(2,1)S(1)} %copy-done.3, ...), custom_call_target="tpu_custom_call" | custom-call | flops 1 | tf_op jit(solution)/shard_map/three_forward_backward/pallas_call | solution.py:270
  23.0 0.6 %near_backward.1 = (bf16[8,192,256]{2,1,0:T(8,128)(2,1)S(1)}, bf16[2,8,64,128]{3,2,1,0:T(8,128)(2,1)S(1)}, f32[2,8,64,128]{3,2,1,0:T(8,128)S(1)}, f32[2,8,64,128]{3,2,1,0:T(8,128)S(1)}) custom-call(bf16[32,64,128]{2,1,0:T(8,128)(2,1)S(1)} %copy-done.3, bf16[32,64,128]{2,1,0:T(8,128)(2,1)S(1)} %copy-done.1, ...), custom_call_target="tpu_custom_call" | custom-call | flops 1 | tf_op jit(solution)/shard_map/near_backward/pallas_call | solution.py:270
  23.7 0.4 collective-permute-start.6
  24.0 0.3 four_backward.1
  24.4 1.3 %collective-permute-start.7 = (bf16[2,8,64,128]{3,2,1,0:T(8,128)(2,1)S(1)}, bf16[2,8,64,128]{3,2,1,0:T(8,128)(2,1)S(1)}, u32[]{:S(2)}, u32[]{:S(2)}) collective-permute-start(bf16[2,8,64,128]{3,2,1,0:T(8,128)(2,1)S(1)} %four_sum.1), channel_id=1, source_target_pairs={{2,0},{3,1},{4,2},{5,3},{6,4},{7,5},{8,6},{9,7},{10,8},{11,9},{12,... | collective-permute-start | bytes 786440 | tf_op jit(solution)/shard_map/ppermute | solution.py:19
  25.9 2.4 %collective-permute-start.8 = (bf16[2,8,64,128]{3,2,1,0:T(8,128)(2,1)S(1)}, bf16[2,8,64,128]{3,2,1,0:T(8,128)(2,1)S(1)}, u32[]{:S(2)}, u32[]{:S(2)}) collective-permute-start(bf16[2,8,64,128]{3,2,1,0:T(8,128)(2,1)S(1)} %get-tuple-element.85), channel_id=1, source_target_pairs={{1,0},{2,1},{3,2},{4,3},{5,4},{6,5},{7,6},{8,7},{9,8},{10,9},{11,1... | collective-permute-start | bytes 786440 | tf_op jit(solution)/shard_map/ppermute | solution.py:19
  28.3 12.0 %collective-permute-done.7.four_sum = bf16[2,8,64,128]{3,2,1,0:T(8,128)(2,1)S(1)} collective-permute-done((bf16[2,8,64,128]{3,2,1,0:T(8,128)(2,1)S(1)}, bf16[2,8,64,128]{3,2,1,0:T(8,128)(2,1)S(1)}, u32[]{:S(2)}, u32[]{:S(2)}) %collective-permute-start.7) | collective-permute-done | bytes 262176 | tf_op jit(solution)/shard_map/ppermute | solution.py:19
  40.4 1.6 %query_grad.1 = (bf16[32,64,128]{2,1,0:T(8,128)(2,1)}, bf16[32,64,128]{2,1,0:T(8,128)(2,1)}, f32[2,8,64,128]{3,2,1,0:T(8,128)S(1)}) custom-call(bf16[2,8,64,128]{3,2,1,0:T(8,128)(2,1)S(1)} %get-tuple-element.46.own, bf16[8,64,128]{2,1,0:T(8,128)(2,1)S(1)} %collective-permute-done.1.one_keys, bf16[2,8,64,128]{3,2,1,0:T(8,128)(2,1)S(1)} %collective-permute-done.back_two, ...), custom_call_target="tpu_custom_call" | custom-call | flops 6710886400 | tf_op jit(solution)/shard_map/query_grad/pallas_call | solution.py:270
  42.0 0.7 %total.1 = (bf16[8,64,128]{2,1,0:T(8,128)(2,1)}, bf16[8,64,128]{2,1,0:T(8,128)(2,1)}) custom-call(f32[2,8,64,128]{3,2,1,0:T(8,128)S(1)} %get-tuple-element.84.partial_sum, bf16[2,8,64,128]{3,2,1,0:T(8,128)(2,1)S(1)} %collective-permute-done.8.two_sum), custom_call_target="tpu_custom_call" | custom-call | flops 1000 | tf_op jit(solution)/shard_map/total/pallas_call | solution.py:270
  (22 shorter events, 0.8 us)
Async XLA Ops:
  0.6 14.9 %copy-start.1 = (bf16[32,64,128]{2,1,0:T(8,128)(2,1)S(1)}, bf16[32,64,128]{2,1,0:T(8,128)(2,1)}, u32[]{:S(2)}) copy-start(bf16[32,64,128]{2,1,0:T(8,128)(2,1)} %grads.11) | copy-start | bytes 1572868
  1.7 12.2 %collective-permute-start = (bf16[2,8,64,128]{3,2,1,0:T(8,128)(2,1)S(1)}, bf16[2,8,64,128]{3,2,1,0:T(8,128)(2,1)S(1)}, u32[]{:S(2)}, u32[]{:S(2)}) collective-permute-start(bf16[2,8,64,128]{3,2,1,0:T(8,128)(2,1)S(1)} %pad_maximum_fusion.own), channel_id=1, source_target_pairs={{0,1},{1,2},{2,3},{3,4},{4,5},{5,6},{6,7},{7,8},{8,9},{9,10},{10,1... | collective-permute-start | bytes 786440 | tf_op jit(solution)/shard_map/ppermute | solution.py:19
  5.1 1.0 %copy-start = (bf16[32,64,128]{2,1,0:T(8,128)(2,1)S(1)}, bf16[32,64,128]{2,1,0:T(8,128)(2,1)}, u32[]{:S(2)}) copy-start(bf16[32,64,128]{2,1,0:T(8,128)(2,1)} %grads.11) | copy-start | bytes 1572868
  6.1 9.4 %copy-start.3 = (bf16[32,64,128]{2,1,0:T(8,128)(2,1)S(1)}, bf16[32,64,128]{2,1,0:T(8,128)(2,1)}, u32[]{:S(2)}) copy-start(bf16[32,64,128]{2,1,0:T(8,128)(2,1)} %queries.11) | copy-start | bytes 1572868
  6.5 12.1 %collective-permute-start.2 = (bf16[2,8,64,128]{3,2,1,0:T(8,128)(2,1)S(1)}, bf16[2,8,64,128]{3,2,1,0:T(8,128)(2,1)S(1)}, u32[]{:S(2)}, u32[]{:S(2)}) collective-permute-start(bf16[2,8,64,128]{3,2,1,0:T(8,128)(2,1)S(1)} %get-tuple-element.46.own), channel_id=1, source_target_pairs={{0,2},{1,3},{2,4},{3,5},{4,6},{5,7},{6,8},{7,9},{8,10},{9,11},{10,... | collective-permute-start | bytes 786440 | tf_op jit(solution)/shard_map/ppermute | solution.py:19
  10.5 1.0 %copy-start.2 = (bf16[32,64,128]{2,1,0:T(8,128)(2,1)S(1)}, bf16[32,64,128]{2,1,0:T(8,128)(2,1)}, u32[]{:S(2)}) copy-start(bf16[32,64,128]{2,1,0:T(8,128)(2,1)} %queries.11) | copy-start | bytes 1572868
  11.6 0.7 %copy-start.6 = (s32[32]{0:T(128)S(1)}, s32[32]{0:T(128)}, u32[]{:S(2)}) copy-start(s32[32]{0:T(128)} %spans) | copy-start | bytes 388
  13.1 0.8 %copy-start.4 = (f32[8,64,256]{2,1,0:T(8,128)}, f32[8,64,256]{2,1,0:T(8,128)S(1)}, u32[]{:S(2)}) copy-start(f32[8,64,256]{2,1,0:T(8,128)S(1)} %get-tuple-element.52.own_scores) | copy-start | bytes 1572868
  13.9 1.4 %collective-permute-start.1 = (bf16[8,64,128]{2,1,0:T(8,128)(2,1)S(1)}, bf16[8,64,128]{2,1,0:T(8,128)(2,1)S(1)}, u32[]{:S(2)}, u32[]{:S(2)}) collective-permute-start(bf16[8,64,128]{2,1,0:T(8,128)(2,1)S(1)} %get-tuple-element.89), channel_id=1, source_target_pairs={{0,16},{16,0},{1,17},{17,1},{2,18},{18,2},{3,19},{19,3},{4,20},{20... | collective-permute-start | bytes 393224 | tf_op jit(solution)/shard_map/ppermute | solution.py:24
  14.0 1.5 %collective-permute-start.3 = (bf16[8,64,128]{2,1,0:T(8,128)(2,1)S(1)}, bf16[8,64,128]{2,1,0:T(8,128)(2,1)S(1)}, u32[]{:S(2)}, u32[]{:S(2)}) collective-permute-start(bf16[8,64,128]{2,1,0:T(8,128)(2,1)S(1)} %get-tuple-element.88), channel_id=1, source_target_pairs={{0,16},{16,0},{1,17},{17,1},{2,18},{18,2},{3,19},{19,3},{4,20},{20... | collective-permute-start | bytes 393224 | tf_op jit(solution)/shard_map/ppermute | solution.py:24
  15.5 1.0 %copy-start.5 = (f32[8,64,256]{2,1,0:T(8,128)S(1)}, f32[8,64,256]{2,1,0:T(8,128)}, u32[]{:S(2)}) copy-start(f32[8,64,256]{2,1,0:T(8,128)} %copy-done.4) | copy-start | bytes 1572868
  18.5 1.9 %collective-permute-start.4 = (bf16[2,8,64,128]{3,2,1,0:T(8,128)(2,1)S(1)}, bf16[2,8,64,128]{3,2,1,0:T(8,128)(2,1)S(1)}, u32[]{:S(2)}, u32[]{:S(2)}) collective-permute-start(bf16[2,8,64,128]{3,2,1,0:T(8,128)(2,1)S(1)} %broadcast_select_fusion), channel_id=1, source_target_pairs={{0,16},{16,0},{1,17},{17,1},{2,18},{18,2},{3,19},{19,3},{4,20},{20... | collective-permute-start | bytes 786440 | tf_op jit(solution)/shard_map/ppermute | solution.py:24
  22.8 1.6 %collective-permute-start.5 = (bf16[2,8,64,128]{3,2,1,0:T(8,128)(2,1)S(1)}, bf16[2,8,64,128]{3,2,1,0:T(8,128)(2,1)S(1)}, u32[]{:S(2)}, u32[]{:S(2)}) collective-permute-start(bf16[2,8,64,128]{3,2,1,0:T(8,128)(2,1)S(1)} %get-tuple-element.70), channel_id=1, source_target_pairs={{0,16},{16,0},{1,17},{17,1},{2,18},{18,2},{3,19},{19,3},{4,20},{20... | collective-permute-start | bytes 786440 | tf_op jit(solution)/shard_map/ppermute | solution.py:24
  23.7 2.1 %collective-permute-start.6 = (bf16[2,8,64,128]{3,2,1,0:T(8,128)(2,1)S(1)}, bf16[2,8,64,128]{3,2,1,0:T(8,128)(2,1)S(1)}, u32[]{:S(2)}, u32[]{:S(2)}) collective-permute-start(bf16[2,8,64,128]{3,2,1,0:T(8,128)(2,1)S(1)} %get-tuple-element.76), channel_id=1, source_target_pairs={{0,16},{16,0},{1,17},{17,1},{2,18},{18,2},{3,19},{19,3},{4,20},{20... | collective-permute-start | bytes 786440 | tf_op jit(solution)/shard_map/ppermute | solution.py:24
  24.4 15.9 %collective-permute-start.7 = (bf16[2,8,64,128]{3,2,1,0:T(8,128)(2,1)S(1)}, bf16[2,8,64,128]{3,2,1,0:T(8,128)(2,1)S(1)}, u32[]{:S(2)}, u32[]{:S(2)}) collective-permute-start(bf16[2,8,64,128]{3,2,1,0:T(8,128)(2,1)S(1)} %four_sum.1), channel_id=1, source_target_pairs={{2,0},{3,1},{4,2},{5,3},{6,4},{7,5},{8,6},{9,7},{10,8},{11,9},{12,... | collective-permute-start | bytes 786440 | tf_op jit(solution)/shard_map/ppermute | solution.py:19
  25.9 16.1 %collective-permute-start.8 = (bf16[2,8,64,128]{3,2,1,0:T(8,128)(2,1)S(1)}, bf16[2,8,64,128]{3,2,1,0:T(8,128)(2,1)S(1)}, u32[]{:S(2)}, u32[]{:S(2)}) collective-permute-start(bf16[2,8,64,128]{3,2,1,0:T(8,128)(2,1)S(1)} %get-tuple-element.85), channel_id=1, source_target_pairs={{1,0},{2,1},{3,2},{4,3},{5,4},{6,5},{7,6},{8,7},{9,8},{10,9},{11,1... | collective-permute-start | bytes 786440 | tf_op jit(solution)/shard_map/ppermute | solution.py:19

commit v5 on v4

v5 whole, which is shorter than its diff:
```python
import math

import jax
import jax.numpy as jnp
from jax import lax
from jax.experimental import pallas as pl
from jax.experimental.pallas import tpu as pltpu
from jax.sharding import PartitionSpec as P

REACH = 2
SEGMENT = 512

masked_score = -1e30


def shifted(block, axis, distance):
    devices = range(lax.axis_size(axis))
    route = [(i - distance, i) for i in devices if i - distance in devices]
    return lax.ppermute(block, axis, route)


def swapped(block, axis):
    count = lax.axis_size(axis)
    return lax.ppermute(block, axis, [(i, count - 1 - i) for i in range(count)])


def matmul(left, right, contract):
    return lax.dot_general(
        left, right, ((contract[:1], contract[1:]), ((), ())), preferred_element_type=jnp.float32
    )


def grouped(ref, g, per_group):
    _, length, width = ref.shape
    return ref[pl.ds(g * per_group, per_group)].reshape(per_group * length, width)


def first_visible(spans, offset, groups, per_group, length):
    lanes = per_group * length
    start = (lax.axis_index("seq") * lax.axis_size("head") + lax.axis_index("head")) * length
    lane = lax.broadcasted_iota(jnp.int32, (1, lanes), 1)
    lane_head = lane // length
    query_pos = start + lane - lane_head * length
    segment_start = query_pos - lax.bitwise_and(offset[0] + query_pos, SEGMENT - 1)
    floor = jnp.maximum(segment_start, 0)
    result = []
    for g in range(groups):
        span = jnp.full((1, lanes), spans[g * per_group], jnp.int32)
        for a in range(1, per_group):
            span = jnp.where(lane_head == a, spans[g * per_group + a], span)
        result.append(jnp.maximum(floor, query_pos - span + 1) - start)
    return result


def join(*blocks):
    return jnp.concatenate(blocks, axis=0)


def masked(scores, first, backs, length):
    row = lax.broadcasted_iota(jnp.int32, (length, scores.shape[1]), 0)
    pieces = []
    for i, back in enumerate(backs):
        visible = row >= first + back * length
        if back == 0:
            lane = lax.broadcasted_iota(jnp.int32, row.shape, 1)
            visible &= row <= lane - lane // length * length
        pieces.append(jnp.where(visible, scores[i * length : (i + 1) * length], masked_score))
    return jnp.concatenate(pieces, axis=0)


def prepare_kernel(own, grads, own_copy, own_prob_grad, grad_rows):
    _, groups, length, width = own.shape
    per_group = grads.shape[0] // groups
    own_copy[...] = own[...]
    for g in range(groups):
        grad = grouped(grads, g, per_group)
        own_prob_grad[g] = matmul(own[1, g], grad, (1, 1))
        grad_rows[g] = grad.T


def own_kernel(spans, offset, queries, own, first, own_max, own_total, own_out, own_weights):
    _, groups, length, width = own.shape
    per_group = queries.shape[0] // groups
    factor = width ** (-0.5) * math.log2(math.e)
    for g, rows in enumerate(first_visible(spans, offset, groups, per_group, length)):
        first[g] = rows
        scores = matmul(own[0, g], grouped(queries, g, per_group), (1, 1)) * factor
        scores = masked(scores, rows, (0,), length)
        row_max = jnp.max(scores, axis=0, keepdims=True)
        weights = jnp.exp2(scores - row_max)
        own_max[g] = row_max
        own_total[g] = jnp.sum(weights, axis=0, keepdims=True)
        own_weights[g] = weights
        own_out[g] = matmul(own[1, g], weights.astype(jnp.bfloat16), (0, 0))


def near_forward_kernel(
    first, queries, grads, one_keys, one_values, back_two, own_max, own_total, own_out,
    near_max, near_total, near_out, near_weights, near_prob_grad, own_factor,
):
    _, groups, length, width = back_two.shape
    per_group = queries.shape[0] // groups
    factor = width ** (-0.5) * math.log2(math.e)
    for g in range(groups):
        query = grouped(queries, g, per_group)
        grad = grouped(grads, g, per_group)
        values = join(back_two[1, g], one_values[g])
        scores = matmul(join(back_two[0, g], one_keys[g]), query, (1, 1)) * factor
        scores = masked(scores, first[g], (2, 1), length)
        row_max = jnp.maximum(own_max[g], jnp.max(scores, axis=0, keepdims=True))
        weights = jnp.exp2(scores - row_max)
        rescale = jnp.exp2(own_max[g] - row_max)
        own_factor[g] = rescale
        near_max[g] = row_max
        near_total[g] = own_total[g] * rescale + jnp.sum(weights, axis=0, keepdims=True)
        near_weights[g] = weights
        near_out[g] = own_out[g] * rescale + matmul(values, weights.astype(jnp.bfloat16), (0, 0))
        near_prob_grad[g] = matmul(values, grad, (1, 1))


def four_kernel(first, queries, grads, back_four, four_scores, four_prob_grad):
    _, groups, length, width = back_four.shape
    per_group = queries.shape[0] // groups
    factor = width ** (-0.5) * math.log2(math.e)
    for g in range(groups):
        scores = matmul(back_four[0, g], grouped(queries, g, per_group), (1, 1)) * factor
        four_scores[g] = masked(scores, first[g], (4,), length)
        four_prob_grad[g] = matmul(back_four[1, g], grouped(grads, g, per_group), (1, 1))


def far_kernel(
    first, queries, grads, back_three, back_four, four_scores, four_prob_grad, grad_rows,
    near_max, near_total, near_out,
    attended_rows, row_delta, near_factor, prob_half, far_grad, three_part,
):
    _, groups, length, width = back_three.shape
    per_group = queries.shape[0] // groups
    scale = width ** (-0.5)
    for g in range(groups):
        query = grouped(queries, g, per_group)
        grad = grouped(grads, g, per_group)
        scores = matmul(back_three[0, g], query, (1, 1)) * (scale * math.log2(math.e))
        scores = join(four_scores[g], masked(scores, first[g], (3,), length))
        row_max = jnp.maximum(near_max[g], jnp.max(scores, axis=0, keepdims=True))
        weights = jnp.exp2(scores - row_max)
        rescale = jnp.exp2(near_max[g] - row_max)
        inverse = 1.0 / (near_total[g] * rescale + jnp.sum(weights, axis=0, keepdims=True))
        weighted = matmul(
            join(back_four[1, g], back_three[1, g]), weights.astype(jnp.bfloat16), (0, 0)
        )
        attended = ((near_out[g] * rescale + weighted) * inverse).astype(jnp.bfloat16)
        delta = jnp.sum(
            grad_rows[g].astype(jnp.float32) * attended.astype(jnp.float32), axis=0, keepdims=True
        )
        prob = weights * inverse
        half = prob.astype(jnp.bfloat16)
        prob_grad = join(four_prob_grad[g], matmul(back_three[1, g], grad, (1, 1)))
        score_grad = (prob * (prob_grad - delta) * scale).astype(jnp.bfloat16)
        attended_rows[g] = attended
        row_delta[g] = delta
        near_factor[g] = rescale * inverse
        prob_half[g] = half
        far_grad[g] = score_grad
        three_part[0, g] = matmul(score_grad[length:], query, (1, 0)).astype(jnp.bfloat16)
        three_part[1, g] = matmul(half[length:], grad, (1, 0)).astype(jnp.bfloat16)


def four_backward_kernel(queries, grads, prob_half, far_grad, four_part):
    groups = prob_half.shape[0]
    length = queries.shape[1]
    per_group = queries.shape[0] // groups
    for g in range(groups):
        four_part[0, g] = matmul(far_grad[g, :length], grouped(queries, g, per_group), (1, 0))
        four_part[1, g] = matmul(prob_half[g, :length], grouped(grads, g, per_group), (1, 0))


def four_sum_kernel(three_arrived, four_part, four_sum):
    first_core = lax.axis_index("head") == 0

    @pl.when(first_core)
    def _():
        four_sum[...] = four_part[...].astype(jnp.bfloat16)

    @pl.when(jnp.logical_not(first_core))
    def _():
        four_sum[...] = (four_part[...] + three_arrived[...].astype(jnp.float32)).astype(jnp.bfloat16)


def near_backward_kernel(
    queries, grads, near_weights, own_weights, near_prob_grad, own_prob_grad, near_factor,
    own_factor, row_delta, near_grad, one_part, two_part, own_part,
):
    groups = near_weights.shape[0]
    length, width = queries.shape[1:]
    per_group = queries.shape[0] // groups
    for g in range(groups):
        query = grouped(queries, g, per_group)
        grad = grouped(grads, g, per_group)
        prob = join(
            near_weights[g] * near_factor[g], own_weights[g] * (own_factor[g] * near_factor[g])
        )
        prob_grad = join(near_prob_grad[g], own_prob_grad[g])
        score_grad = (prob * (prob_grad - row_delta[g]) * width ** (-0.5)).astype(jnp.bfloat16)
        near_grad[g] = score_grad
        key_part = matmul(score_grad, query, (1, 0))
        value_part = matmul(prob.astype(jnp.bfloat16), grad, (1, 0))
        for index, part in enumerate((key_part, value_part)):
            two_part[index, g] = part[:length]
            one_part[index, g] = part[length : 2 * length].astype(jnp.bfloat16)
            own_part[index, g] = part[2 * length :]


def two_sum_kernel(one_arrived, three_arrived, two_part, own_part, two_sum, own_sum):
    first_core = lax.axis_index("head") == 0

    @pl.when(first_core)
    def _():
        two_sum[...] = (two_part[...] + three_arrived[...].astype(jnp.float32)).astype(jnp.bfloat16)
        own_sum[...] = own_part[...] + one_arrived[...].astype(jnp.float32)

    @pl.when(jnp.logical_not(first_core))
    def _():
        two_sum[...] = (two_part[...] + one_arrived[...].astype(jnp.float32)).astype(jnp.bfloat16)
        own_sum[...] = own_part[...]


def query_kernel(
    own, one_keys, back_two, back_three, back_four, attended_rows, far_grad, near_grad,
    out, query_grad,
):
    groups, length, width = own.shape[1:]
    per_group = out.shape[0] // groups
    for g in range(groups):
        rows = pl.ds(g * per_group, per_group)
        out[rows] = attended_rows[g].T.reshape(per_group, length, width)
        part = matmul(
            join(back_four[0, g], back_three[0, g], back_two[0, g], one_keys[g], own[0, g]),
            join(far_grad[g], near_grad[g]),
            (0, 0),
        )
        query_grad[rows] = part.astype(jnp.bfloat16).T.reshape(per_group, length, width)


def final_kernel(own_sum, two_sum, four_sum, key_grad, value_grad):
    for index, result in enumerate((key_grad, value_grad)):
        total = own_sum[index] + two_sum[index].astype(jnp.float32)
        result[...] = (total + four_sum[index].astype(jnp.float32)).astype(jnp.bfloat16)


def shards(query_matrix, key_matrix, value_matrix, output_gradient, query_head_spans, slab_offset):
    groups, length, width = key_matrix.shape
    heads = query_matrix.shape[0]
    lanes = heads // groups * length
    half, full = jnp.bfloat16, jnp.float32
    vmem = pl.BlockSpec(memory_space=pltpu.VMEM)
    smem = pl.BlockSpec(memory_space=pltpu.SMEM)
    block_flops = 2 * heads * length * length * width

    def call(kernel, name, flops, outs, arrays, specs=None):
        return pl.pallas_call(
            kernel,
            out_shape=tuple(jax.ShapeDtypeStruct(shape, kind) for shape, kind in outs),
            in_specs=specs or [vmem] * len(arrays),
            out_specs=(vmem,) * len(outs),
            compiler_params=pltpu.CompilerParams(vmem_limit_bytes=40 * 1024 * 1024),
            cost_estimate=pl.CostEstimate(flops=flops, bytes_accessed=0, transcendentals=0),
            name=name,
        )(*arrays)

    def rows_of(count, kind):
        return ((groups, count, lanes), kind)

    pair = ((2, groups, length, width), half)
    wide_pair = ((2, groups, length, width), full)
    stat = rows_of(1, full)
    first_core = lax.axis_index("head") == 0

    own = jnp.stack([key_matrix, value_matrix])
    back_two = shifted(own, "seq", 1)
    queries, grads = query_matrix, output_gradient
    own_copy, own_prob_grad, grad_rows = call(
        prepare_kernel,
        "prepare",
        1,
        [pair, rows_of(length, full), rows_of(width, half)],
        (own, grads),
    )
    back_four = shifted(own_copy, "seq", 2)
    first, own_max, own_total, own_out, own_weights = call(
        own_kernel,
        "own_block",
        1,
        [rows_of(1, jnp.int32), stat, stat, rows_of(width, full), rows_of(length, full)],
        (query_head_spans, slab_offset, queries, own_copy),
        specs=[smem, smem, vmem, vmem],
    )
    back_two, first = lax.optimization_barrier((back_two, first))
    back_one = [
        swapped(jnp.where(first_core, own_copy[index], back_two[index]), "head")
        for index in range(2)
    ]
    near_max, near_total, near_out, near_weights, near_prob_grad, own_factor = call(
        near_forward_kernel,
        "near_forward",
        1,
        [stat, stat, rows_of(width, full), rows_of(2 * length, full), rows_of(2 * length, full),
         stat],
        (first, queries, grads, *back_one, back_two, own_max, own_total, own_out),
    )
    back_four, near_max = lax.optimization_barrier((back_four, near_max))
    back_three = swapped(jnp.where(first_core, back_two, back_four), "head")
    four_scores, four_prob_grad = call(
        four_kernel,
        "four_block",
        1,
        [rows_of(length, full), rows_of(length, full)],
        (first, queries, grads, back_four),
    )
    attended_rows, row_delta, near_factor, prob_half, far_grad, three_part = call(
        far_kernel,
        "far_forward_backward",
        1,
        [rows_of(width, half), stat, stat, rows_of(2 * length, half), rows_of(2 * length, half),
         pair],
        (first, queries, grads, back_three, back_four, four_scores, four_prob_grad, grad_rows,
         near_max, near_total, near_out),
    )
    three_arrived = swapped(three_part, "head")
    (four_part,) = call(
        four_backward_kernel,
        "four_backward",
        1,
        [wide_pair],
        (queries, grads, prob_half, far_grad),
    )
    near_grad, one_part, two_part, own_part = call(
        near_backward_kernel,
        "near_backward",
        1,
        [rows_of(3 * length, half), pair, wide_pair, wide_pair],
        (queries, grads, near_weights, own_weights, near_prob_grad, own_prob_grad, near_factor,
         own_factor, row_delta),
    )
    one_arrived = swapped(one_part, "head")
    three_arrived, near_grad = lax.optimization_barrier((three_arrived, near_grad))
    (four_sum,) = call(four_sum_kernel, "four_sum", 1, [pair], (three_arrived, four_part))
    four_total = shifted(four_sum, "seq", -2)
    two_sum, own_sum = call(
        two_sum_kernel,
        "two_sum",
        1,
        [pair, wide_pair],
        (one_arrived, three_arrived, two_part, own_part),
    )
    two_total = shifted(two_sum, "seq", -1)
    attn_out, query_grad = call(
        query_kernel,
        "query_grad",
        200 * block_flops,
        [(query_matrix.shape, half)] * 2,
        (own_copy, back_one[0], back_two, back_three, back_four, attended_rows, far_grad,
         near_grad),
    )
    key_grad, value_grad = call(
        final_kernel,
        "total",
        1,
        [(key_matrix.shape, half)] * 2,
        (own_sum, two_total, four_total),
    )
    return (attn_out, query_grad, key_grad, value_grad)


def solution(mesh):
    tokens = P(None, ("seq", "head"), None)
    return jax.shard_map(
        shards,
        mesh=mesh,
        in_specs=(tokens, tokens, tokens, tokens, P(), P()),
        out_specs=(tokens, tokens, tokens, tokens),
        check_vma=False,
    )
```

time: 43.1 us -> 41.6 us (0.965)
  the two profiles are of different devices: /device:TPU:2 before, /device:TPU:22 now
where the time goes in v5:
time: 41.6 us; the launch traced here: 41.4 us
  starting transfers between devices  15.7 us (38%)
  waiting for transfers between devices  11 us (26%)
  Pallas kernels  9.69 us (23%)
  local copies, waits for them, and re-layouts  2.41 us (6%)
  between operations  1.48 us (4%)
  other arithmetic  1.11 us (3%)
    ppermute x4, starting transfers between devices, shifted(): return lax.ppermute(block, axis, route)  14.1 us
    pallas_call x11, Pallas kernels, call(): pl.pallas_call(kernel, out_shape=tuple((jax.ShapeDtypeStruct(shape, kind)...  9.69 us
    ppermute x4, waiting for transfers between devices, shifted(): return lax.ppermute(block, axis, route)  9.24 us
    unnamed x18, local copies, waits for them, and re-layouts  2.41 us
    ppermute x5, waiting for transfers between devices, swapped(): return lax.ppermute(block, axis, [(i, count - 1 - i) for i in range(count)])  1.78 us
    ppermute x5, starting transfers between devices, swapped(): return lax.ppermute(block, axis, [(i, count - 1 - i) for i in range(count)])  1.6 us
    another operation x1, other arithmetic, shards(): own = jnp.stack([key_matrix, value_matrix])  1.05 us
  transfers between devices with their start and end apart: 9, of which 5 were waited for; matrix products, arithmetic and copies ran while one was open for 0% of the time, Pallas kernels for 16%

profile of v5, /device:TPU:22, one launch (start us, length us, event | category | flops | bytes accessed | tf_op | source)
XLA Modules:
  0.0 41.4 jit_solution(3692754502750637141)
XLA Ops:
  0.6 1.1 %pad_maximum_fusion.own = bf16[2,8,64,128]{3,2,1,0:T(8,128)(2,1)S(1)} fusion(bf16[1,8,64,128]{3,2,1,0:T(8,128)(2,1)} %bitcast.6, bf16[1,8,64,128]{3,2,1,0:T(8,128)(2,1)} %bitcast.7), kind=kLoop, calls=%fused_computation | loop fusion | flops 131072 | bytes 524288 | tf_op jit(solution)/shard_map/stack | solution.py:278
  1.7 3.5 %collective-permute-start = (bf16[2,8,64,128]{3,2,1,0:T(8,128)(2,1)S(1)}, bf16[2,8,64,128]{3,2,1,0:T(8,128)(2,1)S(1)}, u32[]{:S(2)}, u32[]{:S(2)}) collective-permute-start(bf16[2,8,64,128]{3,2,1,0:T(8,128)(2,1)S(1)} %pad_maximum_fusion.own), channel_id=1, source_target_pairs={{0,1},{1,2},{2,3},{3,4},{4,5},{5,6},{6,7},{7,8},{8,9},{9,10},{10,1... | collective-permute-start | bytes 786440 | tf_op jit(solution)/shard_map/ppermute | solution.py:19
  5.3 0.3 prepare.1
  5.6 0.8 %copy-done.2 = f32[8,64,256]{2,1,0:T(8,128)} copy-done((f32[8,64,256]{2,1,0:T(8,128)}, f32[8,64,256]{2,1,0:T(8,128)S(1)}, u32[]{:S(2)}) %copy-start.2) | copy-done | bytes 524312
  6.4 0.8 %copy-done.6 = bf16[8,128,256]{2,1,0:T(8,128)(2,1)} copy-done((bf16[8,128,256]{2,1,0:T(8,128)(2,1)}, bf16[8,128,256]{2,1,0:T(8,128)(2,1)S(1)}, u32[]{:S(2)}) %copy-start.6) | copy-done | bytes 524312
  7.2 3.5 %collective-permute-start.2 = (bf16[2,8,64,128]{3,2,1,0:T(8,128)(2,1)S(1)}, bf16[2,8,64,128]{3,2,1,0:T(8,128)(2,1)S(1)}, u32[]{:S(2)}, u32[]{:S(2)}) collective-permute-start(bf16[2,8,64,128]{3,2,1,0:T(8,128)(2,1)S(1)} %get-tuple-element.42.own), channel_id=1, source_target_pairs={{0,2},{1,3},{2,4},{3,5},{4,6},{5,7},{6,8},{7,9},{8,10},{9,11},{10,... | collective-permute-start | bytes 786440 | tf_op jit(solution)/shard_map/ppermute | solution.py:19
  11.4 1.3 %own_block.1 = (s32[8,1,256]{2,1,0:T(1,128)S(1)}, f32[8,1,256]{2,1,0:T(1,128)S(1)}, f32[8,1,256]{2,1,0:T(1,128)S(1)}, f32[8,128,256]{2,1,0:T(8,128)S(1)}, f32[8,64,256]{2,1,0:T(8,128)S(1)}) custom-call(s32[32]{0:T(128)S(1)} %copy-done.8, s32[1]{0:T(128)S(6)} %copy.10.offset, bf16[32,64,128]{2,1,0:T(8,128)(2,1)S(1)} %copy-done.1, ...), custom_call_target="tpu_custom_call" | custom-call | flops 1 | tf_op jit(solution)/shard_map/own_block/pallas_call | solution.py:260
  12.7 0.8 %copy-done.4 = f32[8,64,256]{2,1,0:T(8,128)} copy-done((f32[8,64,256]{2,1,0:T(8,128)}, f32[8,64,256]{2,1,0:T(8,128)S(1)}, u32[]{:S(2)}) %copy-start.4) | copy-done | bytes 524312
  13.6 0.5 %collective-permute-start.1 = (bf16[8,64,128]{2,1,0:T(8,128)(2,1)S(1)}, bf16[8,64,128]{2,1,0:T(8,128)(2,1)S(1)}, u32[]{:S(2)}, u32[]{:S(2)}) collective-permute-start(bf16[8,64,128]{2,1,0:T(8,128)(2,1)S(1)} %get-tuple-element.81), channel_id=1, source_target_pairs={{0,16},{16,0},{1,17},{17,1},{2,18},{18,2},{3,19},{19,3},{4,20},{20... | collective-permute-start | bytes 393224 | tf_op jit(solution)/shard_map/ppermute | solution.py:24
  14.1 0.8 %collective-permute-done.3.one_values = bf16[8,64,128]{2,1,0:T(8,128)(2,1)S(1)} collective-permute-done((bf16[8,64,128]{2,1,0:T(8,128)(2,1)S(1)}, bf16[8,64,128]{2,1,0:T(8,128)(2,1)S(1)}, u32[]{:S(2)}, u32[]{:S(2)}) %collective-permute-start.3) | collective-permute-done | bytes 131104 | tf_op jit(solution)/shard_map/ppermute | solution.py:24
  15.1 1.9 %near_forward.1 = (f32[8,1,256]{2,1,0:T(1,128)S(1)}, f32[8,1,256]{2,1,0:T(1,128)S(1)}, f32[8,128,256]{2,1,0:T(8,128)S(1)}, f32[8,128,256]{2,1,0:T(8,128)S(1)}, f...) custom-call(s32[8,1,256]{2,1,0:T(1,128)S(1)} %get-tuple-element.45.first, bf16[32,64,128]{2,1,0:T(8,128)(2,1)S(1)} %copy-done.1, ...), custom_call_target="tpu_custom_call" | custom-call | flops 1 | tf_op jit(solution)/shard_map/near_forward/pallas_call | solution.py:260
  17.1 0.4 collective-permute-start.4
  17.5 0.5 %four_block.1 = (f32[8,64,256]{2,1,0:T(8,128)S(1)}, f32[8,64,256]{2,1,0:T(8,128)S(1)}) custom-call(s32[8,1,256]{2,1,0:T(1,128)S(1)} %get-tuple-element.45.first, bf16[32,64,128]{2,1,0:T(8,128)(2,1)S(1)} %copy-done.1, bf16[32,64,128]{2,1,0:T(8,128)(2,1)S(1)} %copy-done, bf16[2,8,64,128]{3,2,1,0:T(8,128)(2,1)S(1)} %collective-permute-done.2.back_four), custom_call_target="tpu_custom_call" | custom-call | flops 1 | tf_op jit(solution)/shard_map/four_block/pallas_call | solution.py:260
  17.9 0.7 %collective-permute-done.4.back_three = bf16[2,8,64,128]{3,2,1,0:T(8,128)(2,1)S(1)} collective-permute-done((bf16[2,8,64,128]{3,2,1,0:T(8,128)(2,1)S(1)}, bf16[2,8,64,128]{3,2,1,0:T(8,128)(2,1)S(1)}, u32[]{:S(2)}, u32[]{:S(2)}) %collective-permute-start.4) | collective-permute-done | bytes 262176 | tf_op jit(solution)/shard_map/ppermute | solution.py:24
  18.7 2.3 %far_forward_backward.1 = (bf16[8,128,256]{2,1,0:T(8,128)(2,1)S(1)}, f32[8,1,256]{2,1,0:T(1,128)S(1)}, f32[8,1,256]{2,1,0:T(1,128)S(1)}, bf16[8,128,256]{2,1,0:T...) custom-call(s32[8,1,256]{2,1,0:T(1,128)S(1)} %get-tuple-element.45.first, ...), custom_call_target="tpu_custom_call" | custom-call | flops 1 | tf_op jit(solution)/shard_map/far_forward_backward/pallas_call | solution.py:260
  21.0 0.4 collective-permute-start.5
  21.4 0.6 %near_backward.1 = (bf16[8,192,256]{2,1,0:T(8,128)(2,1)S(1)}, bf16[2,8,64,128]{3,2,1,0:T(8,128)(2,1)S(1)}, f32[2,8,64,128]{3,2,1,0:T(8,128)S(1)}, f32[2,8,64,128]{3,2,1,0:T(8,128)S(1)}) custom-call(bf16[32,64,128]{2,1,0:T(8,128)(2,1)S(1)} %copy-done.1, bf16[32,64,128]{2,1,0:T(8,128)(2,1)S(1)} %copy-done, f32[8,128,256]{2,1,0:T(8,128)S(1)} %get-tuple-element.60.near_weights, ...), custom_call_target="tpu_custom_call" | custom-call | flops 1 | tf_op jit(solution)/shard_map/near_backward/pallas_call | solution.py:260
  22.3 0.3 four_backward.1.four_part
  22.6 3.7 %collective-permute-start.8 = (bf16[2,8,64,128]{3,2,1,0:T(8,128)(2,1)S(1)}, bf16[2,8,64,128]{3,2,1,0:T(8,128)(2,1)S(1)}, u32[]{:S(2)}, u32[]{:S(2)}) collective-permute-start(bf16[2,8,64,128]{3,2,1,0:T(8,128)(2,1)S(1)} %four_sum.1), channel_id=1, source_target_pairs={{2,0},{3,1},{4,2},{5,3},{6,4},{7,5},{8,6},{9,7},{10,8},{11,9},{12,... | collective-permute-start | bytes 786440 | tf_op jit(solution)/shard_map/ppermute | solution.py:19
  26.4 3.4 %collective-permute-start.7 = (bf16[2,8,64,128]{3,2,1,0:T(8,128)(2,1)S(1)}, bf16[2,8,64,128]{3,2,1,0:T(8,128)(2,1)S(1)}, u32[]{:S(2)}, u32[]{:S(2)}) collective-permute-start(bf16[2,8,64,128]{3,2,1,0:T(8,128)(2,1)S(1)} %get-tuple-element.76), channel_id=1, source_target_pairs={{1,0},{2,1},{3,2},{4,3},{5,4},{6,5},{7,6},{8,7},{9,8},{10,9},{11,1... | collective-permute-start | bytes 786440 | tf_op jit(solution)/shard_map/ppermute | solution.py:19
  29.8 1.6 %query_grad.1 = (bf16[32,64,128]{2,1,0:T(8,128)(2,1)}, bf16[32,64,128]{2,1,0:T(8,128)(2,1)}) custom-call(bf16[2,8,64,128]{3,2,1,0:T(8,128)(2,1)S(1)} %get-tuple-element.42.own, bf16[8,64,128]{2,1,0:T(8,128)(2,1)S(1)} %collective-permute-done.1.one_keys, bf16[2,8,64,128]{3,2,1,0:T(8,128)(2,1)S(1)} %collective-permute-done.back_two, ...), custom_call_target="tpu_custom_call" | custom-call | flops 6710886400 | tf_op jit(solution)/shard_map/query_grad/pallas_call | solution.py:260
  31.4 6.4 %collective-permute-done.8.four_sum = bf16[2,8,64,128]{3,2,1,0:T(8,128)(2,1)S(1)} collective-permute-done((bf16[2,8,64,128]{3,2,1,0:T(8,128)(2,1)S(1)}, bf16[2,8,64,128]{3,2,1,0:T(8,128)(2,1)S(1)}, u32[]{:S(2)}, u32[]{:S(2)}) %collective-permute-start.8) | collective-permute-done | bytes 262176 | tf_op jit(solution)/shard_map/ppermute | solution.py:19
  37.8 2.9 %collective-permute-done.7.two_sum = bf16[2,8,64,128]{3,2,1,0:T(8,128)(2,1)S(1)} collective-permute-done((bf16[2,8,64,128]{3,2,1,0:T(8,128)(2,1)S(1)}, bf16[2,8,64,128]{3,2,1,0:T(8,128)(2,1)S(1)}, u32[]{:S(2)}, u32[]{:S(2)}) %collective-permute-start.7) | collective-permute-done | bytes 262176 | tf_op jit(solution)/shard_map/ppermute | solution.py:19
  40.7 0.7 %total.1 = (bf16[8,64,128]{2,1,0:T(8,128)(2,1)}, bf16[8,64,128]{2,1,0:T(8,128)(2,1)}) custom-call(f32[2,8,64,128]{3,2,1,0:T(8,128)S(1)} %get-tuple-element.75.own_sum, bf16[2,8,64,128]{3,2,1,0:T(8,128)(2,1)S(1)} %collective-permute-done.7.two_sum, bf16[2,8,64,128]{3,2,1,0:T(8,128)(2,1)S(1)} %collective-permute-done.8.four_sum), custom_call_target="tpu_custom_call" | custom-call | flops 1 | tf_op jit(solution)/shard_map/total/pallas_call | solution.py:260
  (26 shorter events, 0.8 us)
Async XLA Ops:
  0.6 4.6 %copy-start = (bf16[32,64,128]{2,1,0:T(8,128)(2,1)S(1)}, bf16[32,64,128]{2,1,0:T(8,128)(2,1)}, u32[]{:S(2)}) copy-start(bf16[32,64,128]{2,1,0:T(8,128)(2,1)} %grads.11) | copy-start | bytes 1572868
  1.7 9.7 %copy-start.1 = (bf16[32,64,128]{2,1,0:T(8,128)(2,1)S(1)}, bf16[32,64,128]{2,1,0:T(8,128)(2,1)}, u32[]{:S(2)}) copy-start(bf16[32,64,128]{2,1,0:T(8,128)(2,1)} %queries.11) | copy-start | bytes 1572868
  1.7 11.8 %collective-permute-start = (bf16[2,8,64,128]{3,2,1,0:T(8,128)(2,1)S(1)}, bf16[2,8,64,128]{3,2,1,0:T(8,128)(2,1)S(1)}, u32[]{:S(2)}, u32[]{:S(2)}) collective-permute-start(bf16[2,8,64,128]{3,2,1,0:T(8,128)(2,1)S(1)} %pad_maximum_fusion.own), channel_id=1, source_target_pairs={{0,1},{1,2},{2,3},{3,4},{4,5},{5,6},{6,7},{7,8},{8,9},{9,10},{10,1... | collective-permute-start | bytes 786440 | tf_op jit(solution)/shard_map/ppermute | solution.py:19
  5.6 0.8 %copy-start.2 = (f32[8,64,256]{2,1,0:T(8,128)}, f32[8,64,256]{2,1,0:T(8,128)S(1)}, u32[]{:S(2)}) copy-start(f32[8,64,256]{2,1,0:T(8,128)S(1)} %get-tuple-element.63.own_prob_grad) | copy-start | bytes 1572868
  6.4 0.8 %copy-start.6 = (bf16[8,128,256]{2,1,0:T(8,128)(2,1)}, bf16[8,128,256]{2,1,0:T(8,128)(2,1)S(1)}, u32[]{:S(2)}) copy-start(bf16[8,128,256]{2,1,0:T(8,128)(2,1)S(1)} %get-tuple-element.53.grad_rows) | copy-start | bytes 1572868
  7.2 4.2 %copy-start.8 = (s32[32]{0:T(128)S(1)}, s32[32]{0:T(128)}, u32[]{:S(2)}) copy-start(s32[32]{0:T(128)} %spans.1) | copy-start | bytes 388
  7.2 9.8 %collective-permute-start.2 = (bf16[2,8,64,128]{3,2,1,0:T(8,128)(2,1)S(1)}, bf16[2,8,64,128]{3,2,1,0:T(8,128)(2,1)S(1)}, u32[]{:S(2)}, u32[]{:S(2)}) collective-permute-start(bf16[2,8,64,128]{3,2,1,0:T(8,128)(2,1)S(1)} %get-tuple-element.42.own), channel_id=1, source_target_pairs={{0,2},{1,3},{2,4},{3,5},{4,6},{5,7},{6,8},{7,9},{8,10},{9,11},{10,... | collective-permute-start | bytes 786440 | tf_op jit(solution)/shard_map/ppermute | solution.py:19
  12.7 0.8 %copy-start.4 = (f32[8,64,256]{2,1,0:T(8,128)}, f32[8,64,256]{2,1,0:T(8,128)S(1)}, u32[]{:S(2)}) copy-start(f32[8,64,256]{2,1,0:T(8,128)S(1)} %get-tuple-element.61.own_weights) | copy-start | bytes 1572868
  13.5 1.4 %collective-permute-start.3 = (bf16[8,64,128]{2,1,0:T(8,128)(2,1)S(1)}, bf16[8,64,128]{2,1,0:T(8,128)(2,1)S(1)}, u32[]{:S(2)}, u32[]{:S(2)}) collective-permute-start(bf16[8,64,128]{2,1,0:T(8,128)(2,1)S(1)} %get-tuple-element.80), channel_id=1, source_target_pairs={{0,16},{16,0},{1,17},{17,1},{2,18},{18,2},{3,19},{19,3},{4,20},{20... | collective-permute-start | bytes 393224 | tf_op jit(solution)/shard_map/ppermute | solution.py:24
  13.6 1.5 %collective-permute-start.1 = (bf16[8,64,128]{2,1,0:T(8,128)(2,1)S(1)}, bf16[8,64,128]{2,1,0:T(8,128)(2,1)S(1)}, u32[]{:S(2)}, u32[]{:S(2)}) collective-permute-start(bf16[8,64,128]{2,1,0:T(8,128)(2,1)S(1)} %get-tuple-element.81), channel_id=1, source_target_pairs={{0,16},{16,0},{1,17},{17,1},{2,18},{18,2},{3,19},{19,3},{4,20},{20... | collective-permute-start | bytes 393224 | tf_op jit(solution)/shard_map/ppermute | solution.py:24
  17.1 1.6 %copy-start.7 = (bf16[8,128,256]{2,1,0:T(8,128)(2,1)S(1)}, bf16[8,128,256]{2,1,0:T(8,128)(2,1)}, u32[]{:S(2)}) copy-start(bf16[8,128,256]{2,1,0:T(8,128)(2,1)} %copy-done.6) | copy-start | bytes 1572868
  17.1 1.6 %collective-permute-start.4 = (bf16[2,8,64,128]{3,2,1,0:T(8,128)(2,1)S(1)}, bf16[2,8,64,128]{3,2,1,0:T(8,128)(2,1)S(1)}, u32[]{:S(2)}, u32[]{:S(2)}) collective-permute-start(bf16[2,8,64,128]{3,2,1,0:T(8,128)(2,1)S(1)} %broadcast_select_fusion), channel_id=1, source_target_pairs={{0,16},{16,0},{1,17},{17,1},{2,18},{18,2},{3,19},{19,3},{4,20},{20... | collective-permute-start | bytes 786440 | tf_op jit(solution)/shard_map/ppermute | solution.py:24
  18.7 2.7 %copy-start.3 = (f32[8,64,256]{2,1,0:T(8,128)S(1)}, f32[8,64,256]{2,1,0:T(8,128)}, u32[]{:S(2)}) copy-start(f32[8,64,256]{2,1,0:T(8,128)} %copy-done.2) | copy-start | bytes 1572868
  18.7 2.7 %copy-start.5 = (f32[8,64,256]{2,1,0:T(8,128)S(1)}, f32[8,64,256]{2,1,0:T(8,128)}, u32[]{:S(2)}) copy-start(f32[8,64,256]{2,1,0:T(8,128)} %copy-done.4) | copy-start | bytes 1572868
  21.0 1.6 %collective-permute-start.5 = (bf16[2,8,64,128]{3,2,1,0:T(8,128)(2,1)S(1)}, bf16[2,8,64,128]{3,2,1,0:T(8,128)(2,1)S(1)}, u32[]{:S(2)}, u32[]{:S(2)}) collective-permute-start(bf16[2,8,64,128]{3,2,1,0:T(8,128)(2,1)S(1)} %get-tuple-element.59), channel_id=1, source_target_pairs={{0,16},{16,0},{1,17},{17,1},{2,18},{18,2},{3,19},{19,3},{4,20},{20... | collective-permute-start | bytes 786440 | tf_op jit(solution)/shard_map/ppermute | solution.py:24
  22.0 4.3 %collective-permute-start.6 = (bf16[2,8,64,128]{3,2,1,0:T(8,128)(2,1)S(1)}, bf16[2,8,64,128]{3,2,1,0:T(8,128)(2,1)S(1)}, u32[]{:S(2)}, u32[]{:S(2)}) collective-permute-start(bf16[2,8,64,128]{3,2,1,0:T(8,128)(2,1)S(1)} %get-tuple-element.71), channel_id=1, source_target_pairs={{0,16},{16,0},{1,17},{17,1},{2,18},{18,2},{3,19},{19,3},{4,20},{20... | collective-permute-start | bytes 786440 | tf_op jit(solution)/shard_map/ppermute | solution.py:24
  22.6 15.1 %collective-permute-start.8 = (bf16[2,8,64,128]{3,2,1,0:T(8,128)(2,1)S(1)}, bf16[2,8,64,128]{3,2,1,0:T(8,128)(2,1)S(1)}, u32[]{:S(2)}, u32[]{:S(2)}) collective-permute-start(bf16[2,8,64,128]{3,2,1,0:T(8,128)(2,1)S(1)} %four_sum.1), channel_id=1, source_target_pairs={{2,0},{3,1},{4,2},{5,3},{6,4},{7,5},{8,6},{9,7},{10,8},{11,9},{12,... | collective-permute-start | bytes 786440 | tf_op jit(solution)/shard_map/ppermute | solution.py:19
  26.4 14.2 %collective-permute-start.7 = (bf16[2,8,64,128]{3,2,1,0:T(8,128)(2,1)S(1)}, bf16[2,8,64,128]{3,2,1,0:T(8,128)(2,1)S(1)}, u32[]{:S(2)}, u32[]{:S(2)}) collective-permute-start(bf16[2,8,64,128]{3,2,1,0:T(8,128)(2,1)S(1)} %get-tuple-element.76), channel_id=1, source_target_pairs={{1,0},{2,1},{3,2},{4,3},{5,4},{6,5},{7,6},{8,7},{9,8},{10,9},{11,1... | collective-permute-start | bytes 786440 | tf_op jit(solution)/shard_map/ppermute | solution.py:19

commit v6 on v1

v6 whole, which is shorter than its diff:
```python
import math

import jax
import jax.numpy as jnp
from jax import lax
from jax.experimental import pallas as pl
from jax.experimental.pallas import tpu as pltpu
from jax.sharding import PartitionSpec as P

REACH = 2
SEGMENT = 512

masked_score = -1e30


def shifted(block, axis, distance):
    devices = range(lax.axis_size(axis))
    route = [(i - distance, i) for i in devices if i - distance in devices]
    return lax.ppermute(block, axis, route)


def swapped(block, axis):
    count = lax.axis_size(axis)
    return lax.ppermute(block, axis, [(i, count - 1 - i) for i in range(count)])


def matmul(left, right, contract):
    return lax.dot_general(
        left, right, ((contract[:1], contract[1:]), ((), ())), preferred_element_type=jnp.float32
    )


def grouped(ref, n, count):
    _, length, width = ref.shape
    return ref[pl.ds(n * count, count)].reshape(count * length, width)


def join(*blocks):
    return jnp.concatenate(blocks, axis=0)


def core_offsets(length):
    core = lax.axis_index("head")
    return core * length, (1 - core) * length


def my_heads(count):
    return pl.ds(lax.axis_index("head") * count, count)


def other_heads(count):
    return pl.ds((1 - lax.axis_index("head")) * count, count)


def lane_tokens(count, length):
    lane = lax.broadcasted_iota(jnp.int32, (1, count * 2 * length), 1)
    token = lane - lane // (2 * length) * (2 * length)
    mine, other = core_offsets(length)
    return jnp.where(token < length, token + mine, token - length + other)


def first_visible(spans, offset, chunks, count, length):
    token = lane_tokens(count, length)
    lane_head = lax.broadcasted_iota(jnp.int32, token.shape, 1) // (2 * length)
    start = lax.axis_index("seq") * 2 * length
    segment_start = token - lax.bitwise_and(offset[0] + start + token, SEGMENT - 1)
    floor = jnp.maximum(segment_start, -start)
    base = lax.axis_index("head") * chunks * count
    result = []
    for n in range(chunks):
        span = jnp.full(token.shape, spans[base + n * count], jnp.int32)
        for a in range(1, count):
            span = jnp.where(lane_head == a, spans[base + n * count + a], span)
        result.append(jnp.maximum(floor, token - span + 1))
    return result


def masked(scores, first, chips_back, token=None):
    length = scores.shape[0] // 2
    row = lax.broadcasted_iota(jnp.int32, (length, scores.shape[1]), 0)
    pieces = []
    for part, offset in enumerate(core_offsets(length)):
        visible = row >= first + (chips_back * 2 * length - offset)
        if token is not None:
            visible &= row <= token - offset
        pieces.append(
            jnp.where(visible, scores[part * length : (part + 1) * length], masked_score)
        )
    return join(*pieces)


def split_kernel(block, *sends):
    for index, send in enumerate(sends):
        send[...] = block[index, other_heads(send.shape[0])]


def thirds(rows):
    return [2 * rows * (i + 1) // 3 - 2 * rows * i // 3 for i in range(3)]


def placed(pieces, rows):
    taken = 0
    for piece in pieces:
        count = piece.shape[0]
        for index in range(2):
            low = max(taken, index * rows)
            high = min(taken + count, (index + 1) * rows)
            if low < high:
                yield index, low - index * rows, piece.at[pl.ds(low - taken, high - low)], high - low
        taken += count


def split_rows_kernel(queries, grads, after, *sends):
    heads = queries.shape[0] // 2
    start = (1 - lax.axis_index("head")) * heads
    for index, row, piece, count in placed(sends, heads):
        piece[...] = (queries, grads)[index][pl.ds(start + row, count)]


def join_own_kernel(own, other_keys, other_values, own_head):
    groups, length = other_keys.shape[:2]
    own_head[:, :, pl.ds(0, length)] = own[:, my_heads(groups)]
    own_head[0, :, pl.ds(length, length)] = other_keys[...]
    own_head[1, :, pl.ds(length, length)] = other_values[...]


def own_kernel(
    spans, offset, queries, grads, first_third, second_third, last_third, own,
    query_head, grad_head, grad_rows, first, own_max, own_total, own_out, own_weights,
    own_prob_grad,
):
    heads, _, width = query_head.shape
    length = queries.shape[1]
    groups = own.shape[1]
    chunks = first.shape[0]
    count = heads // chunks
    query_head[:, pl.ds(0, length)] = queries[my_heads(heads)]
    grad_head[:, pl.ds(0, length)] = grads[my_heads(heads)]
    for index, row, piece, rows in placed((first_third, second_third, last_third), heads):
        (query_head, grad_head)[index][pl.ds(row, rows), pl.ds(length, length)] = piece[...]
    factor = width ** (-0.5) * math.log2(math.e)
    token = lane_tokens(count, length)
    for n, rows in enumerate(first_visible(spans, offset, chunks, count, length)):
        g = n * groups // chunks
        first[n] = rows
        grad = grouped(grad_head, n, count)
        scores = matmul(own[0, g], grouped(query_head, n, count), (1, 1)) * factor
        scores = masked(scores, rows, 0, token)
        row_max = jnp.max(scores, axis=0, keepdims=True)
        weights = jnp.exp2(scores - row_max)
        own_max[n] = row_max
        own_total[n] = jnp.sum(weights, axis=0, keepdims=True)
        own_weights[n] = weights
        own_out[n] = matmul(own[1, g], weights.astype(jnp.bfloat16), (0, 0))
        own_prob_grad[n] = matmul(own[1, g], grad, (1, 1))
        grad_rows[n] = grad.T


def one_back(back_one, one_other, index, g):
    base = lax.axis_index("head") * one_other[index].shape[0]
    return join(back_one[index, base + g], one_other[index][g])


def near_forward_kernel(
    first, query_head, grad_head, back_one, one_keys, one_values, own_max, own_total, own_out,
    near_max, near_total, near_out, near_weights, near_prob_grad, own_factor,
):
    groups = one_keys.shape[0]
    one_other = (one_keys, one_values)
    chunks = first.shape[0]
    heads, _, width = query_head.shape
    count = heads // chunks
    factor = width ** (-0.5) * math.log2(math.e)
    for n in range(chunks):
        g = n * groups // chunks
        values = one_back(back_one, one_other, 1, g)
        scores = matmul(
            one_back(back_one, one_other, 0, g), grouped(query_head, n, count), (1, 1)
        )
        scores = masked(scores * factor, first[n], 1)
        row_max = jnp.maximum(own_max[n], jnp.max(scores, axis=0, keepdims=True))
        weights = jnp.exp2(scores - row_max)
        rescale = jnp.exp2(own_max[n] - row_max)
        own_factor[n] = rescale
        near_max[n] = row_max
        near_total[n] = own_total[n] * rescale + jnp.sum(weights, axis=0, keepdims=True)
        near_weights[n] = weights
        near_out[n] = own_out[n] * rescale + matmul(values, weights.astype(jnp.bfloat16), (0, 0))
        near_prob_grad[n] = matmul(values, grouped(grad_head, n, count), (1, 1))


def far_kernel(
    first, query_head, grad_head, back_two, grad_rows, near_max, near_total, near_out,
    attended_rows, row_delta, near_factor, far_grad, far_part,
):
    groups = back_two.shape[1]
    chunks = first.shape[0]
    heads, _, width = query_head.shape
    count = heads // chunks
    scale = width ** (-0.5)
    parts = {}
    for n in range(chunks):
        g = n * groups // chunks
        query = grouped(query_head, n, count)
        grad = grouped(grad_head, n, count)
        scores = matmul(back_two[0, g], query, (1, 1)) * (scale * math.log2(math.e))
        scores = masked(scores, first[n], 2)
        row_max = jnp.maximum(near_max[n], jnp.max(scores, axis=0, keepdims=True))
        weights = jnp.exp2(scores - row_max)
        rescale = jnp.exp2(near_max[n] - row_max)
        inverse = 1.0 / (near_total[n] * rescale + jnp.sum(weights, axis=0, keepdims=True))
        weighted = matmul(back_two[1, g], weights.astype(jnp.bfloat16), (0, 0))
        attended = ((near_out[n] * rescale + weighted) * inverse).astype(jnp.bfloat16)
        delta = jnp.sum(
            grad_rows[n].astype(jnp.float32) * attended.astype(jnp.float32), axis=0, keepdims=True
        )
        prob = weights * inverse
        prob_grad = matmul(back_two[1, g], grad, (1, 1))
        score_grad = (prob * (prob_grad - delta) * scale).astype(jnp.bfloat16)
        attended_rows[n] = attended
        row_delta[n] = delta
        near_factor[n] = rescale * inverse
        far_grad[n] = score_grad
        pair = (
            matmul(score_grad, query, (1, 0)), matmul(prob.astype(jnp.bfloat16), grad, (1, 0)),
        )
        parts[g] = pair if g not in parts else (parts[g][0] + pair[0], parts[g][1] + pair[1])
        if (n + 1) * groups // chunks != g:
            for index in range(2):
                far_part[index, g] = parts[g][index].astype(jnp.bfloat16)


def near_backward_kernel(
    query_head, grad_head, near_weights, own_weights, near_prob_grad, own_prob_grad, near_factor,
    own_factor, row_delta, near_grad, one_mine, send_keys, send_values, own_part,
):
    chunks = near_weights.shape[0]
    groups, length, width = one_mine.shape[1:]
    count = query_head.shape[0] // chunks
    parts = {}
    for n in range(chunks):
        g = n * groups // chunks
        query = grouped(query_head, n, count)
        grad = grouped(grad_head, n, count)
        prob = join(
            near_weights[n] * near_factor[n], own_weights[n] * (own_factor[n] * near_factor[n])
        )
        prob_grad = join(near_prob_grad[n], own_prob_grad[n])
        score_grad = (prob * (prob_grad - row_delta[n]) * width ** (-0.5)).astype(jnp.bfloat16)
        near_grad[n] = score_grad
        pair = (
            matmul(score_grad, query, (1, 0)), matmul(prob.astype(jnp.bfloat16), grad, (1, 0)),
        )
        parts[g] = pair if g not in parts else (parts[g][0] + pair[0], parts[g][1] + pair[1])
        if (n + 1) * groups // chunks != g:
            for index in range(2):
                one_mine[index, g] = parts[g][index][:length].astype(jnp.bfloat16)
                send = (send_keys, send_values)[index]
                send[g] = parts[g][index][length : 2 * length].astype(jnp.bfloat16)
                own_part[index, g] = parts[g][index][2 * length :]


def join_one_kernel(one_mine, other_keys, other_values, one_part):
    groups = one_mine.shape[1]
    one_part[:, my_heads(groups)] = one_mine[...]
    one_part[0, other_heads(groups)] = other_keys[...]
    one_part[1, other_heads(groups)] = other_values[...]


def query_kernel(
    own, back_one, one_keys, back_two, attended_rows, far_grad, near_grad, after,
    out_mine, query_mine, first_third, second_third, last_third, query_send,
):
    sends = (first_third, second_third, last_third)
    groups = own.shape[1]
    chunks = far_grad.shape[0]
    heads, length, width = out_mine.shape
    count = heads // chunks
    for n in range(chunks):
        g = n * groups // chunks
        rows = pl.ds(n * count, count)
        keys = join(back_two[0, g], one_back(back_one, (one_keys,), 0, g), own[0, g])
        part = matmul(keys, join(far_grad[n], near_grad[n]), (0, 0)).astype(jnp.bfloat16)
        for index, (columns, mine) in enumerate(((attended_rows[n], out_mine), (part, query_mine))):
            block = columns.T.reshape(count, 2 * length, width)
            mine[rows] = block[:, :length]
            query_send[index, rows] = block[:, length:]
    for index, row, piece, taken in placed(sends, heads):
        piece[...] = query_send[index, pl.ds(row, taken)]


def assemble_kernel(
    out_mine, query_mine, first_third, second_third, last_third, out, query_grad, token
):
    heads = out_mine.shape[0]
    start = (1 - lax.axis_index("head")) * heads
    out[my_heads(heads)] = out_mine[...]
    query_grad[my_heads(heads)] = query_mine[...]
    for index, row, piece, count in placed((first_third, second_third, last_third), heads):
        (out, query_grad)[index][pl.ds(start + row, count)] = piece[...]
    token[...] = jnp.zeros(token.shape, token.dtype)


def own_sum_kernel(own_part, far_total, sum_mine, sum_send):
    length = sum_mine.shape[2]
    total = own_part[...] + far_total[...].astype(jnp.float32)
    sum_mine[...] = total[:, :, :length]
    sum_send[...] = total[:, :, length:].astype(jnp.bfloat16)


def final_kernel(sum_mine, sum_other, one_total, after, key_grad, value_grad):
    groups = sum_mine.shape[1]
    mine, other = my_heads(groups), other_heads(groups)
    for index, result in enumerate((key_grad, value_grad)):
        total = sum_mine[index] + one_total[index, mine].astype(jnp.float32)
        result[mine] = total.astype(jnp.bfloat16)
        total = sum_other[index].astype(jnp.float32) + one_total[index, other].astype(jnp.float32)
        result[other] = total.astype(jnp.bfloat16)


def shards(query_matrix, key_matrix, value_matrix, output_gradient, query_head_spans, slab_offset):
    groups, length, width = key_matrix.shape
    heads = query_matrix.shape[0]
    cores = lax.axis_size("head")
    tokens = cores * length
    groups_here, heads_here = groups // cores, heads // cores
    count = max(1, min(heads // groups, 256 // tokens))
    chunks = heads_here // count
    lanes = count * tokens
    half, full = jnp.bfloat16, jnp.float32
    vmem = pl.BlockSpec(memory_space=pltpu.VMEM)
    smem = pl.BlockSpec(memory_space=pltpu.SMEM)

    def call(kernel, name, outs, arrays, scalars=0, scratch=()):
        return pl.pallas_call(
            kernel,
            out_shape=tuple(jax.ShapeDtypeStruct(shape, kind) for shape, kind in outs),
            in_specs=[smem] * scalars + [vmem] * (len(arrays) - scalars),
            out_specs=(vmem,) * len(outs),
            scratch_shapes=scratch,
            compiler_params=pltpu.CompilerParams(vmem_limit_bytes=40 * 1024 * 1024),
            cost_estimate=pl.CostEstimate(flops=1, bytes_accessed=0, transcendentals=0),
            name=name,
        )(*arrays)

    def rows_of(rows, kind):
        return ((chunks, rows, lanes), kind)

    stat = rows_of(1, full)
    whole_pair = ((2, groups, length, width), half)
    half_block = ((groups_here, length, width), half)
    half_pair = ((2, groups_here, length, width), half)
    chip_pair = ((2, groups_here, tokens, width), half)
    half_rows = ((heads_here, length, width), half)
    third_rows = [((rows, length, width), half) for rows in thirds(heads_here)]
    chip_rows = ((heads_here, tokens, width), half)

    own = jnp.stack([key_matrix, value_matrix])
    back_one = shifted(own, "seq", 1)
    own_sends = call(split_kernel, "split_own", [half_block] * 2, (own,))
    (own_head,) = call(
        join_own_kernel, "join_own", [chip_pair], (own, *[swapped(send, "head") for send in own_sends])
    )
    back_two = shifted(own_head, "seq", 2)
    sends = call(
        split_rows_kernel,
        "split_rows",
        third_rows,
        (query_matrix, output_gradient, own),
    )
    (
        query_head, grad_head, grad_rows, first, own_max, own_total, own_out, own_weights,
        own_prob_grad,
    ) = call(
        own_kernel,
        "own_block",
        [
            chip_rows, chip_rows, rows_of(width, half), rows_of(1, jnp.int32), stat, stat,
            rows_of(width, full), rows_of(tokens, full), rows_of(tokens, full),
        ],
        (
            query_head_spans, slab_offset, query_matrix, output_gradient,
            *[swapped(send, "head") for send in sends], own_head,
        ),
        scalars=2,
    )
    back_one, first = lax.optimization_barrier((back_one, first))
    one_sends = call(split_kernel, "split_one", [half_block] * 2, (back_one,))
    one_other = [swapped(send, "head") for send in one_sends]
    near_max, near_total, near_out, near_weights, near_prob_grad, own_factor = call(
        near_forward_kernel,
        "near_forward",
        [stat, stat, rows_of(width, full), rows_of(tokens, full), rows_of(tokens, full), stat],
        (first, query_head, grad_head, back_one, *one_other, own_max, own_total, own_out),
    )
    back_two, near_max = lax.optimization_barrier((back_two, near_max))
    attended_rows, row_delta, near_factor, far_grad, far_part = call(
        far_kernel,
        "far_forward_backward",
        [rows_of(width, half), stat, stat, rows_of(tokens, half), chip_pair],
        (first, query_head, grad_head, back_two, grad_rows, near_max, near_total, near_out),
    )
    far_total = shifted(far_part, "seq", -2)
    near_grad, part_mine, *part_sends, own_part = call(
        near_backward_kernel,
        "near_backward",
        [rows_of(2 * tokens, half), half_pair, half_block, half_block, (chip_pair[0], full)],
        (
            query_head, grad_head, near_weights, own_weights, near_prob_grad, own_prob_grad,
            near_factor, own_factor, row_delta,
        ),
    )
    (one_part,) = call(
        join_one_kernel,
        "join_one",
        [whole_pair],
        (part_mine, *[swapped(send, "head") for send in part_sends]),
    )
    one_total = shifted(one_part, "seq", -1)
    out_mine, query_mine, *sends = call(
        query_kernel,
        "query_grad",
        [half_rows] * 2 + third_rows,
        (own_head, back_one, one_other[0], back_two, attended_rows, far_grad, near_grad, one_part),
        scratch=[pltpu.VMEM((2,) + half_rows[0], half)],
    )
    attn_out, query_grad, token = call(
        assemble_kernel,
        "assemble",
        [(query_matrix.shape, half)] * 2 + [((8, 128), full)],
        (out_mine, query_mine, *[swapped(send, "head") for send in sends]),
    )
    sum_mine, sum_send = call(
        own_sum_kernel, "own_sum", [(half_pair[0], full), half_pair], (own_part, far_total)
    )
    key_grad, value_grad = call(
        final_kernel,
        "total",
        [(key_matrix.shape, half)] * 2,
        (sum_mine, swapped(sum_send, "head"), one_total, token),
    )
    return (attn_out, query_grad, key_grad, value_grad)


def solution(mesh):
    tokens = P(None, ("seq", "head"), None)
    return jax.shard_map(
        shards,
        mesh=mesh,
        in_specs=(tokens, tokens, tokens, tokens, P(), P()),
        out_specs=(tokens, tokens, tokens, tokens),
        check_vma=False,
    )
```

time: 47.2 us -> 39.8 us (0.84)
  the two profiles are of different devices: /device:TPU:4 before, /device:TPU:3 now
where the time goes in v6:
time: 39.8 us; the launch traced here: 39.6 us
  starting transfers between devices  15.4 us (39%)
  waiting for transfers between devices  11.1 us (28%)
  Pallas kernels  10.6 us (27%)
  between operations  1.44 us (4%)
  other arithmetic  1.05 us (3%)
    pallas_call x13, Pallas kernels, call(): pl.pallas_call(kernel, out_shape=tuple((jax.ShapeDtypeStruct(shape, kind)...  10.6 us
    ppermute x4, starting transfers between devices, shifted(): return lax.ppermute(block, axis, route)  9.87 us
    ppermute x4, waiting for transfers between devices, shifted(): return lax.ppermute(block, axis, route)  7.41 us
    ppermute x13, starting transfers between devices, swapped(): return lax.ppermute(block, axis, [(i, count - 1 - i) for i in range(count)])  5.5 us
    ppermute x13, waiting for transfers between devices, swapped(): return lax.ppermute(block, axis, [(i, count - 1 - i) for i in range(count)])  3.68 us
    another operation x1, other arithmetic, shards(): own = jnp.stack([key_matrix, value_matrix])  1.05 us
  transfers between devices with their start and end apart: 17, of which 8 were waited for; matrix products, arithmetic and copies ran while one was open for 0% of the time, Pallas kernels for 18%

profile of v6, /device:TPU:3, one launch (start us, length us, event | category | flops | bytes accessed | tf_op | source)
XLA Modules:
  0.0 39.6 jit_solution(123435238088757296)
XLA Ops:
  0.6 1.1 %pad_maximum_fusion.block.own.after = bf16[2,8,64,128]{3,2,1,0:T(8,128)(2,1)S(1)} fusion(bf16[1,8,64,128]{3,2,1,0:T(8,128)(2,1)} %bitcast.2, bf16[1,8,64,128]{3,2,1,0:T(8,128)(2,1)} %bitcast.3), kind=kLoop, calls=%fused_computation | loop fusion | flops 131072 | bytes 524288 | tf_op jit(solution)/shard_map/stack | solution.py:358
  1.7 3.3 %collective-permute-start.2 = (bf16[2,8,64,128]{3,2,1,0:T(8,128)(2,1)S(1)}, bf16[2,8,64,128]{3,2,1,0:T(8,128)(2,1)S(1)}, u32[]{:S(2)}, u32[]{:S(2)}) collective-permute-start(bf16[2,8,64,128]{3,2,1,0:T(8,128)(2,1)S(1)} %pad_maximum_fusion.block.own.after), channel_id=1, source_target_pairs={{0,1},{1,2},{2,3},{3,4},{4,5},{5,6},{6,7},{7,8},{8,9},{9,10},{10,1... | collective-permute-start | bytes 786440 | tf_op jit(solution)/shard_map/ppermute | solution.py:19
  5.0 1.0 %collective-permute-start = (bf16[4,64,128]{2,1,0:T(8,128)(2,1)S(1)}, bf16[4,64,128]{2,1,0:T(8,128)(2,1)S(1)}, u32[]{:S(2)}, u32[]{:S(2)}) collective-permute-start(bf16[4,64,128]{2,1,0:T(8,128)(2,1)S(1)} %get-tuple-element.52), channel_id=1, source_target_pairs={{0,16},{16,0},{1,17},{17,1},{2,18},{18,2},{3,19},{19,3},{4,20},{20... | collective-permute-start | bytes 196616 | tf_op jit(solution)/shard_map/ppermute | solution.py:24
  6.1 0.8 %collective-permute-done.other_keys = bf16[4,64,128]{2,1,0:T(8,128)(2,1)S(1)} collective-permute-done((bf16[4,64,128]{2,1,0:T(8,128)(2,1)S(1)}, bf16[4,64,128]{2,1,0:T(8,128)(2,1)S(1)}, u32[]{:S(2)}, u32[]{:S(2)}) %collective-permute-start) | collective-permute-done | bytes 65568 | tf_op jit(solution)/shard_map/ppermute | solution.py:24
  6.9 0.4 collective-permute-done.1.other_values
  7.3 3.2 %collective-permute-start.7 = (bf16[2,4,128,128]{3,2,1,0:T(8,128)(2,1)S(1)}, bf16[2,4,128,128]{3,2,1,0:T(8,128)(2,1)S(1)}, u32[]{:S(2)}, u32[]{:S(2)}) collective-permute-start(bf16[2,4,128,128]{3,2,1,0:T(8,128)(2,1)S(1)} %join_own.1.own), channel_id=1, source_target_pairs={{0,2},{1,3},{2,4},{3,5},{4,6},{5,7},{6,8},{7,9},{8,10},{9,11},{10,... | collective-permute-start | bytes 786440 | tf_op jit(solution)/shard_map/ppermute | solution.py:19
  10.5 0.5 %collective-permute-start.4 = (bf16[11,64,128]{2,1,0:T(8,128)(2,1)S(1)}, bf16[11,64,128]{2,1,0:T(8,128)(2,1)S(1)}, u32[]{:S(2)}, u32[]{:S(2)}) collective-permute-start(bf16[11,64,128]{2,1,0:T(8,128)(2,1)S(1)} %get-tuple-element.55), channel_id=1, source_target_pairs={{0,16},{16,0},{1,17},{17,1},{2,18},{18,2},{3,19},{19,3},{4,20},{20... | collective-permute-start | bytes 540680 | tf_op jit(solution)/shard_map/ppermute | solution.py:24
  11.1 0.4 %collective-permute-start.3 = (bf16[10,64,128]{2,1,0:T(8,128)(2,1)S(1)}, bf16[10,64,128]{2,1,0:T(8,128)(2,1)S(1)}, u32[]{:S(2)}, u32[]{:S(2)}) collective-permute-start(bf16[10,64,128]{2,1,0:T(8,128)(2,1)S(1)} %get-tuple-element.54), channel_id=1, source_target_pairs={{0,16},{16,0},{1,17},{17,1},{2,18},{18,2},{3,19},{19,3},{4,20},{20... | collective-permute-start | bytes 491528 | tf_op jit(solution)/shard_map/ppermute | solution.py:24
  12.2 0.5 %collective-permute-done.3.first_third = bf16[10,64,128]{2,1,0:T(8,128)(2,1)S(1)} collective-permute-done((bf16[10,64,128]{2,1,0:T(8,128)(2,1)S(1)}, bf16[10,64,128]{2,1,0:T(8,128)(2,1)S(1)}, u32[]{:S(2)}, u32[]{:S(2)}) %collective-permute-start.3) | collective-permute-done | bytes 163872 | tf_op jit(solution)/shard_map/ppermute | solution.py:24
  12.7 2.4 %own_block.1 = (bf16[16,128,128]{2,1,0:T(8,128)(2,1)S(1)}, bf16[16,128,128]{2,1,0:T(8,128)(2,1)S(1)}, bf16[8,128,256]{2,1,0:T(8,128)(2,1)S(1)}, s32[8,1,256]{2,1...) custom-call(s32[32]{0:T(128)S(1)} %copy-done.2, ...), custom_call_target="tpu_custom_call" | custom-call | flops 1 | tf_op jit(solution)/shard_map/own_block/pallas_call | solution.py:335
  15.8 0.7 %collective-permute-done.6.one_keys = bf16[4,64,128]{2,1,0:T(8,128)(2,1)S(1)} collective-permute-done((bf16[4,64,128]{2,1,0:T(8,128)(2,1)S(1)}, bf16[4,64,128]{2,1,0:T(8,128)(2,1)S(1)}, u32[]{:S(2)}, u32[]{:S(2)}) %collective-permute-start.6) | collective-permute-done | bytes 65568 | tf_op jit(solution)/shard_map/ppermute | solution.py:24
  16.8 1.9 %near_forward.1 = (f32[8,1,256]{2,1,0:T(1,128)S(1)}, f32[8,1,256]{2,1,0:T(1,128)S(1)}, f32[8,128,256]{2,1,0:T(8,128)S(1)}, f32[8,128,256]{2,1,0:T(8,128)S(1)}, f...) custom-call(s32[8,1,256]{2,1,0:T(1,128)S(1)} %get-tuple-element.60.first, ...), custom_call_target="tpu_custom_call" | custom-call | flops 1 | tf_op jit(solution)/shard_map/near_forward/pallas_call | solution.py:335
  18.7 2.7 %far_forward_backward.1 = (bf16[8,128,256]{2,1,0:T(8,128)(2,1)S(1)}, f32[8,1,256]{2,1,0:T(1,128)S(1)}, f32[8,1,256]{2,1,0:T(1,128)S(1)}, bf16[8,128,256]{2,1,0:T(8,128)(2,1)S(1)}, bf16[2,4,128,128]{3,2,1,0:T(8,128)(2,1)S(1)}) custom-call(s32[8,1,256]{2,1,0:T(1,128)S(1)} %get-tuple-element.60.first, bf16[16,128,128]{2,1,0:T(8,128)(2,1)S(1)} %get-tuple-element.61.query_head, ...), custom_call_target="tpu_custom_call" | custom-call | flops 1 | tf_op jit(solution)/shard_map/far_forward_backward/pallas_call | solution.py:335
  21.4 1.3 %collective-permute-start.14 = (bf16[2,4,128,128]{3,2,1,0:T(8,128)(2,1)S(1)}, bf16[2,4,128,128]{3,2,1,0:T(8,128)(2,1)S(1)}, u32[]{:S(2)}, u32[]{:S(2)}) collective-permute-start(bf16[2,4,128,128]{3,2,1,0:T(8,128)(2,1)S(1)} %get-tuple-element.94), channel_id=1, source_target_pairs={{2,0},{3,1},{4,2},{5,3},{6,4},{7,5},{8,6},{9,7},{10,8},{11,9},{12,... | collective-permute-start | bytes 786440 | tf_op jit(solution)/shard_map/ppermute | solution.py:19
  22.7 0.8 %near_backward.1 = (bf16[8,256,256]{2,1,0:T(8,128)(2,1)S(1)}, bf16[2,4,64,128]{3,2,1,0:T(8,128)(2,1)S(1)}, bf16[4,64,128]{2,1,0:T(8,128)(2,1)S(1)}, bf16[4,64,12...) custom-call(bf16[16,128,128]{2,1,0:T(8,128)(2,1)S(1)} %get-tuple-element.61.query_head, ...), custom_call_target="tpu_custom_call" | custom-call | flops 1 | tf_op jit(solution)/shard_map/near_backward/pallas_call | solution.py:335
  24.1 0.7 %collective-permute-done.9.other_keys = bf16[4,64,128]{2,1,0:T(8,128)(2,1)S(1)} collective-permute-done((bf16[4,64,128]{2,1,0:T(8,128)(2,1)S(1)}, bf16[4,64,128]{2,1,0:T(8,128)(2,1)S(1)}, u32[]{:S(2)}, u32[]{:S(2)}) %collective-permute-start.9) | collective-permute-done | bytes 65568 | tf_op jit(solution)/shard_map/ppermute | solution.py:24
  25.1 2.2 %collective-permute-start.16 = (bf16[2,8,64,128]{3,2,1,0:T(8,128)(2,1)S(1)}, bf16[2,8,64,128]{3,2,1,0:T(8,128)(2,1)S(1)}, u32[]{:S(2)}, u32[]{:S(2)}) collective-permute-start(bf16[2,8,64,128]{3,2,1,0:T(8,128)(2,1)S(1)} %join_one.1.after), channel_id=1, source_target_pairs={{1,0},{2,1},{3,2},{4,3},{5,4},{6,5},{7,6},{8,7},{9,8},{10,9},{11,1... | collective-permute-start | bytes 786440 | tf_op jit(solution)/shard_map/ppermute | solution.py:19
  27.3 0.7 %query_grad.1 = (bf16[16,64,128]{2,1,0:T(8,128)(2,1)S(1)}, bf16[16,64,128]{2,1,0:T(8,128)(2,1)S(1)}, bf16[10,64,128]{2,1,0:T(8,128)(2,1)S(1)}, bf16[11,64,128]{2,1,0:T(8,128)(2,1)S(1)}, bf16[11,64,128]{2,1,0:T(8,128)(2,1)S(1)}) custom-call(bf16[2,4,128,128]{3,2,1,0:T(8,128)(2,1)S(1)} %join_own.1.own, ...), custom_call_target="tpu_custom_call" | custom-call | flops 1 | tf_op jit(solution)/shard_map/query_grad/pallas_call | solution.py:335
  28.0 0.6 %collective-permute-start.12 = (bf16[11,64,128]{2,1,0:T(8,128)(2,1)S(1)}, bf16[11,64,128]{2,1,0:T(8,128)(2,1)S(1)}, u32[]{:S(2)}, u32[]{:S(2)}) collective-permute-start(bf16[11,64,128]{2,1,0:T(8,128)(2,1)S(1)} %get-tuple-element.89), channel_id=1, source_target_pairs={{0,16},{16,0},{1,17},{17,1},{2,18},{18,2},{3,19},{19,3},{4,20},{20... | collective-permute-start | bytes 540680 | tf_op jit(solution)/shard_map/ppermute | solution.py:24
  28.7 0.4 %collective-permute-start.11 = (bf16[10,64,128]{2,1,0:T(8,128)(2,1)S(1)}, bf16[10,64,128]{2,1,0:T(8,128)(2,1)S(1)}, u32[]{:S(2)}, u32[]{:S(2)}) collective-permute-start(bf16[10,64,128]{2,1,0:T(8,128)(2,1)S(1)} %get-tuple-element.88), channel_id=1, source_target_pairs={{0,16},{16,0},{1,17},{17,1},{2,18},{18,2},{3,19},{19,3},{4,20},{20... | collective-permute-start | bytes 491528 | tf_op jit(solution)/shard_map/ppermute | solution.py:24
  29.1 7.4 %collective-permute-done.14.far_total = bf16[2,4,128,128]{3,2,1,0:T(8,128)(2,1)S(1)} collective-permute-done((bf16[2,4,128,128]{3,2,1,0:T(8,128)(2,1)S(1)}, bf16[2,4,128,128]{3,2,1,0:T(8,128)(2,1)S(1)}, u32[]{:S(2)}, u32[]{:S(2)}) %collective-permute-start.14) | collective-permute-done | bytes 262176 | tf_op jit(solution)/shard_map/ppermute | solution.py:19
  36.6 1.1 %collective-permute-start.15 = (bf16[2,4,64,128]{3,2,1,0:T(8,128)(2,1)S(1)}, bf16[2,4,64,128]{3,2,1,0:T(8,128)(2,1)S(1)}, u32[]{:S(2)}, u32[]{:S(2)}) collective-permute-start(bf16[2,4,64,128]{3,2,1,0:T(8,128)(2,1)S(1)} %get-tuple-element.96), channel_id=1, source_target_pairs={{0,16},{16,0},{1,17},{17,1},{2,18},{18,2},{3,19},{19,3},{4,20},{20... | collective-permute-start | bytes 393224 | tf_op jit(solution)/shard_map/ppermute | solution.py:24
  37.8 1.0 %assemble.1 = (bf16[32,64,128]{2,1,0:T(8,128)(2,1)}, bf16[32,64,128]{2,1,0:T(8,128)(2,1)}, f32[8,128]{1,0:T(8,128)S(1)}) custom-call(bf16[16,64,128]{2,1,0:T(8,128)(2,1)S(1)} %get-tuple-element.86.out_mine, bf16[16,64,128]{2,1,0:T(8,128)(2,1)S(1)} %get-tuple-element.87.query_mine, bf16[10,64,128]{2,1,0:T(8,128)(2,1)S(1)} %collective-permute-done.11.first_third, ...), custom_call_target="tpu_custom_call" | custom-call | flops 1 | tf_op jit(solution)/shard_map/assemble/pallas_call | solution.py:335
  38.8 0.7 %total.1 = (bf16[8,64,128]{2,1,0:T(8,128)(2,1)}, bf16[8,64,128]{2,1,0:T(8,128)(2,1)}) custom-call(f32[2,4,64,128]{3,2,1,0:T(8,128)S(1)} %get-tuple-element.95.sum_mine, bf16[2,4,64,128]{3,2,1,0:T(8,128)(2,1)S(1)} %collective-permute-done.15.sum_other, bf16[2,8,64,128]{3,2,1,0:T(8,128)(2,1)S(1)} %collective-permute-done.16.one_total, ...), custom_call_target="tpu_custom_call" | custom-call | flops 1 | tf_op jit(solution)/shard_map/total/pallas_call | solution.py:335
  (30 shorter events, 2.1 us)
Async XLA Ops:
  0.6 9.8 %copy-start.1 = (bf16[32,64,128]{2,1,0:T(8,128)(2,1)S(1)}, bf16[32,64,128]{2,1,0:T(8,128)(2,1)}, u32[]{:S(2)}) copy-start(bf16[32,64,128]{2,1,0:T(8,128)(2,1)} %grads.3) | copy-start | bytes 1572868
  1.7 8.8 %copy-start = (bf16[32,64,128]{2,1,0:T(8,128)(2,1)S(1)}, bf16[32,64,128]{2,1,0:T(8,128)(2,1)}, u32[]{:S(2)}) copy-start(bf16[32,64,128]{2,1,0:T(8,128)(2,1)} %queries.3) | copy-start | bytes 1572868
  1.7 13.4 %collective-permute-start.2 = (bf16[2,8,64,128]{3,2,1,0:T(8,128)(2,1)S(1)}, bf16[2,8,64,128]{3,2,1,0:T(8,128)(2,1)S(1)}, u32[]{:S(2)}, u32[]{:S(2)}) collective-permute-start(bf16[2,8,64,128]{3,2,1,0:T(8,128)(2,1)S(1)} %pad_maximum_fusion.block.own.after), channel_id=1, source_target_pairs={{0,1},{1,2},{2,3},{3,4},{4,5},{5,6},{6,7},{7,8},{8,9},{9,10},{10,1... | collective-permute-start | bytes 786440 | tf_op jit(solution)/shard_map/ppermute | solution.py:19
  5.0 1.9 %collective-permute-start = (bf16[4,64,128]{2,1,0:T(8,128)(2,1)S(1)}, bf16[4,64,128]{2,1,0:T(8,128)(2,1)S(1)}, u32[]{:S(2)}, u32[]{:S(2)}) collective-permute-start(bf16[4,64,128]{2,1,0:T(8,128)(2,1)S(1)} %get-tuple-element.52), channel_id=1, source_target_pairs={{0,16},{16,0},{1,17},{17,1},{2,18},{18,2},{3,19},{19,3},{4,20},{20... | collective-permute-start | bytes 196616 | tf_op jit(solution)/shard_map/ppermute | solution.py:24
  6.0 1.3 %collective-permute-start.1 = (bf16[4,64,128]{2,1,0:T(8,128)(2,1)S(1)}, bf16[4,64,128]{2,1,0:T(8,128)(2,1)S(1)}, u32[]{:S(2)}, u32[]{:S(2)}) collective-permute-start(bf16[4,64,128]{2,1,0:T(8,128)(2,1)S(1)} %get-tuple-element.53), channel_id=1, source_target_pairs={{0,16},{16,0},{1,17},{17,1},{2,18},{18,2},{3,19},{19,3},{4,20},{20... | collective-permute-start | bytes 196616 | tf_op jit(solution)/shard_map/ppermute | solution.py:24
  7.3 11.4 %collective-permute-start.7 = (bf16[2,4,128,128]{3,2,1,0:T(8,128)(2,1)S(1)}, bf16[2,4,128,128]{3,2,1,0:T(8,128)(2,1)S(1)}, u32[]{:S(2)}, u32[]{:S(2)}) collective-permute-start(bf16[2,4,128,128]{3,2,1,0:T(8,128)(2,1)S(1)} %join_own.1.own), channel_id=1, source_target_pairs={{0,2},{1,3},{2,4},{3,5},{4,6},{5,7},{6,8},{7,9},{8,10},{9,11},{10,... | collective-permute-start | bytes 786440 | tf_op jit(solution)/shard_map/ppermute | solution.py:19
  10.5 2.2 %collective-permute-start.4 = (bf16[11,64,128]{2,1,0:T(8,128)(2,1)S(1)}, bf16[11,64,128]{2,1,0:T(8,128)(2,1)S(1)}, u32[]{:S(2)}, u32[]{:S(2)}) collective-permute-start(bf16[11,64,128]{2,1,0:T(8,128)(2,1)S(1)} %get-tuple-element.55), channel_id=1, source_target_pairs={{0,16},{16,0},{1,17},{17,1},{2,18},{18,2},{3,19},{19,3},{4,20},{20... | collective-permute-start | bytes 540680 | tf_op jit(solution)/shard_map/ppermute | solution.py:24
  11.0 1.7 %collective-permute-start.5 = (bf16[11,64,128]{2,1,0:T(8,128)(2,1)S(1)}, bf16[11,64,128]{2,1,0:T(8,128)(2,1)S(1)}, u32[]{:S(2)}, u32[]{:S(2)}) collective-permute-start(bf16[11,64,128]{2,1,0:T(8,128)(2,1)S(1)} %get-tuple-element.56), channel_id=1, source_target_pairs={{0,16},{16,0},{1,17},{17,1},{2,18},{18,2},{3,19},{19,3},{4,20},{20... | collective-permute-start | bytes 540680 | tf_op jit(solution)/shard_map/ppermute | solution.py:24
  11.1 1.6 %copy-start.2 = (s32[32]{0:T(128)S(1)}, s32[32]{0:T(128)}, u32[]{:S(2)}) copy-start(s32[32]{0:T(128)} %spans.1) | copy-start | bytes 388
  11.1 1.6 %collective-permute-start.3 = (bf16[10,64,128]{2,1,0:T(8,128)(2,1)S(1)}, bf16[10,64,128]{2,1,0:T(8,128)(2,1)S(1)}, u32[]{:S(2)}, u32[]{:S(2)}) collective-permute-start(bf16[10,64,128]{2,1,0:T(8,128)(2,1)S(1)} %get-tuple-element.54), channel_id=1, source_target_pairs={{0,16},{16,0},{1,17},{17,1},{2,18},{18,2},{3,19},{19,3},{4,20},{20... | collective-permute-start | bytes 491528 | tf_op jit(solution)/shard_map/ppermute | solution.py:24
  15.2 1.3 %collective-permute-start.6 = (bf16[4,64,128]{2,1,0:T(8,128)(2,1)S(1)}, bf16[4,64,128]{2,1,0:T(8,128)(2,1)S(1)}, u32[]{:S(2)}, u32[]{:S(2)}) collective-permute-start(bf16[4,64,128]{2,1,0:T(8,128)(2,1)S(1)} %get-tuple-element.59), channel_id=1, source_target_pairs={{0,16},{16,0},{1,17},{17,1},{2,18},{18,2},{3,19},{19,3},{4,20},{20... | collective-permute-start | bytes 196616 | tf_op jit(solution)/shard_map/ppermute | solution.py:24
  15.5 1.3 %collective-permute-start.8 = (bf16[4,64,128]{2,1,0:T(8,128)(2,1)S(1)}, bf16[4,64,128]{2,1,0:T(8,128)(2,1)S(1)}, u32[]{:S(2)}, u32[]{:S(2)}) collective-permute-start(bf16[4,64,128]{2,1,0:T(8,128)(2,1)S(1)} %get-tuple-element.63), channel_id=1, source_target_pairs={{0,16},{16,0},{1,17},{17,1},{2,18},{18,2},{3,19},{19,3},{4,20},{20... | collective-permute-start | bytes 196616 | tf_op jit(solution)/shard_map/ppermute | solution.py:24
  21.4 15.2 %collective-permute-start.14 = (bf16[2,4,128,128]{3,2,1,0:T(8,128)(2,1)S(1)}, bf16[2,4,128,128]{3,2,1,0:T(8,128)(2,1)S(1)}, u32[]{:S(2)}, u32[]{:S(2)}) collective-permute-start(bf16[2,4,128,128]{3,2,1,0:T(8,128)(2,1)S(1)} %get-tuple-element.94), channel_id=1, source_target_pairs={{2,0},{3,1},{4,2},{5,3},{6,4},{7,5},{8,6},{9,7},{10,8},{11,9},{12,... | collective-permute-start | bytes 786440 | tf_op jit(solution)/shard_map/ppermute | solution.py:19
  23.5 1.3 %collective-permute-start.9 = (bf16[4,64,128]{2,1,0:T(8,128)(2,1)S(1)}, bf16[4,64,128]{2,1,0:T(8,128)(2,1)S(1)}, u32[]{:S(2)}, u32[]{:S(2)}) collective-permute-start(bf16[4,64,128]{2,1,0:T(8,128)(2,1)S(1)} %get-tuple-element.84), channel_id=1, source_target_pairs={{0,16},{16,0},{1,17},{17,1},{2,18},{18,2},{3,19},{19,3},{4,20},{20... | collective-permute-start | bytes 196616 | tf_op jit(solution)/shard_map/ppermute | solution.py:24
  23.8 1.3 %collective-permute-start.10 = (bf16[4,64,128]{2,1,0:T(8,128)(2,1)S(1)}, bf16[4,64,128]{2,1,0:T(8,128)(2,1)S(1)}, u32[]{:S(2)}, u32[]{:S(2)}) collective-permute-start(bf16[4,64,128]{2,1,0:T(8,128)(2,1)S(1)} %get-tuple-element.85), channel_id=1, source_target_pairs={{0,16},{16,0},{1,17},{17,1},{2,18},{18,2},{3,19},{19,3},{4,20},{20... | collective-permute-start | bytes 196616 | tf_op jit(solution)/shard_map/ppermute | solution.py:24
  25.1 13.7 %collective-permute-start.16 = (bf16[2,8,64,128]{3,2,1,0:T(8,128)(2,1)S(1)}, bf16[2,8,64,128]{3,2,1,0:T(8,128)(2,1)S(1)}, u32[]{:S(2)}, u32[]{:S(2)}) collective-permute-start(bf16[2,8,64,128]{3,2,1,0:T(8,128)(2,1)S(1)} %join_one.1.after), channel_id=1, source_target_pairs={{1,0},{2,1},{3,2},{4,3},{5,4},{6,5},{7,6},{8,7},{9,8},{10,9},{11,1... | collective-permute-start | bytes 786440 | tf_op jit(solution)/shard_map/ppermute | solution.py:19
  28.0 9.7 %collective-permute-start.12 = (bf16[11,64,128]{2,1,0:T(8,128)(2,1)S(1)}, bf16[11,64,128]{2,1,0:T(8,128)(2,1)S(1)}, u32[]{:S(2)}, u32[]{:S(2)}) collective-permute-start(bf16[11,64,128]{2,1,0:T(8,128)(2,1)S(1)} %get-tuple-element.89), channel_id=1, source_target_pairs={{0,16},{16,0},{1,17},{17,1},{2,18},{18,2},{3,19},{19,3},{4,20},{20... | collective-permute-start | bytes 540680 | tf_op jit(solution)/shard_map/ppermute | solution.py:24
  28.6 9.1 %collective-permute-start.13 = (bf16[11,64,128]{2,1,0:T(8,128)(2,1)S(1)}, bf16[11,64,128]{2,1,0:T(8,128)(2,1)S(1)}, u32[]{:S(2)}, u32[]{:S(2)}) collective-permute-start(bf16[11,64,128]{2,1,0:T(8,128)(2,1)S(1)} %get-tuple-element.90), channel_id=1, source_target_pairs={{0,16},{16,0},{1,17},{17,1},{2,18},{18,2},{3,19},{19,3},{4,20},{20... | collective-permute-start | bytes 540680 | tf_op jit(solution)/shard_map/ppermute | solution.py:24
  28.7 9.0 %collective-permute-start.11 = (bf16[10,64,128]{2,1,0:T(8,128)(2,1)S(1)}, bf16[10,64,128]{2,1,0:T(8,128)(2,1)S(1)}, u32[]{:S(2)}, u32[]{:S(2)}) collective-permute-start(bf16[10,64,128]{2,1,0:T(8,128)(2,1)S(1)} %get-tuple-element.88), channel_id=1, source_target_pairs={{0,16},{16,0},{1,17},{17,1},{2,18},{18,2},{3,19},{19,3},{4,20},{20... | collective-permute-start | bytes 491528 | tf_op jit(solution)/shard_map/ppermute | solution.py:24
  36.6 2.2 %collective-permute-start.15 = (bf16[2,4,64,128]{3,2,1,0:T(8,128)(2,1)S(1)}, bf16[2,4,64,128]{3,2,1,0:T(8,128)(2,1)S(1)}, u32[]{:S(2)}, u32[]{:S(2)}) collective-permute-start(bf16[2,4,64,128]{3,2,1,0:T(8,128)(2,1)S(1)} %get-tuple-element.96), channel_id=1, source_target_pairs={{0,16},{16,0},{1,17},{17,1},{2,18},{18,2},{3,19},{19,3},{4,20},{20... | collective-permute-start | bytes 393224 | tf_op jit(solution)/shard_map/ppermute | solution.py:24

commit v7 on v6

--- a/solution.py
+++ b/solution.py
@@ -141,19 +141,27 @@
     factor = width ** (-0.5) * math.log2(math.e)
     token = lane_tokens(count, length)
     for n, rows in enumerate(first_visible(spans, offset, chunks, count, length)):
+        first[n] = rows
+
+    def products(n):
         g = n * groups // chunks
-        first[n] = rows
-        grad = grouped(grad_head, n, count)
-        scores = matmul(own[0, g], grouped(query_head, n, count), (1, 1)) * factor
-        scores = masked(scores, rows, 0, token)
+        own_prob_grad[n] = matmul(own[1, g], grouped(grad_head, n, count), (1, 1))
+        return (matmul(own[0, g], grouped(query_head, n, count), (1, 1)),)
+
+    def softmax(n, scores):
+        scores = masked(scores * factor, first[n], 0, token)
         row_max = jnp.max(scores, axis=0, keepdims=True)
         weights = jnp.exp2(scores - row_max)
         own_max[n] = row_max
         own_total[n] = jnp.sum(weights, axis=0, keepdims=True)
         own_weights[n] = weights
-        own_out[n] = matmul(own[1, g], weights.astype(jnp.bfloat16), (0, 0))
-        own_prob_grad[n] = matmul(own[1, g], grad, (1, 1))
-        grad_rows[n] = grad.T
+        return (weights.astype(jnp.bfloat16),)
+
+    def weigh(n, halves):
+        own_out[n] = matmul(own[1, n * groups // chunks], halves, (0, 0))
+        grad_rows[n] = grouped(grad_head, n, count).T
+
+    pipelined(chunks, products, softmax, weigh)
 
 
 def one_back(back_one, one_other, index, g):
@@ -171,12 +179,15 @@
     heads, _, width = query_head.shape
     count = heads // chunks
     factor = width ** (-0.5) * math.log2(math.e)
-    for n in range(chunks):
+
+    def products(n):
         g = n * groups // chunks
+        keys = one_back(back_one, one_other, 0, g)
         values = one_back(back_one, one_other, 1, g)
-        scores = matmul(
-            one_back(back_one, one_other, 0, g), grouped(query_head, n, count), (1, 1)
-        )
+        near_prob_grad[n] = matmul(values, grouped(grad_head, n, count), (1, 1))
+        return (matmul(keys, grouped(query_head, n, count), (1, 1)),)
+
+    def softmax(n, scores):
         scores = masked(scores * factor, first[n], 1)
         row_max = jnp.maximum(own_max[n], jnp.max(scores, axis=0, keepdims=True))
         weights = jnp.exp2(scores - row_max)
@@ -185,8 +196,13 @@
         near_max[n] = row_max
         near_total[n] = own_total[n] * rescale + jnp.sum(weights, axis=0, keepdims=True)
         near_weights[n] = weights
-        near_out[n] = own_out[n] * rescale + matmul(values, weights.astype(jnp.bfloat16), (0, 0))
-        near_prob_grad[n] = matmul(values, grouped(grad_head, n, count), (1, 1))
+        return rescale, weights.astype(jnp.bfloat16)
+
+    def weigh(n, rescale, halves):
+        values = one_back(back_one, one_other, 1, n * groups // chunks)
+        near_out[n] = own_out[n] * rescale + matmul(values, halves, (0, 0))
+
+    pipelined(chunks, products, softmax, weigh)
 
 
 def far_kernel(
@@ -198,13 +214,16 @@
     heads, _, width = query_head.shape
     count = heads // chunks
     scale = width ** (-0.5)
-    parts = {}
-    for n in range(chunks):
+
+    def products(n):
         g = n * groups // chunks
-        query = grouped(query_head, n, count)
-        grad = grouped(grad_head, n, count)
-        scores = matmul(back_two[0, g], query, (1, 1)) * (scale * math.log2(math.e))
-        scores = masked(scores, first[n], 2)
+        scores = matmul(back_two[0, g], grouped(query_head, n, count), (1, 1))
+        prob_grad = matmul(back_two[1, g], grouped(grad_head, n, count), (1, 1))
+        return scores, prob_grad
+
+    def softmax(n, scores, prob_grad):
+        g = n * groups // chunks
+        scores = masked(scores * (scale * math.log2(math.e)), first[n], 2)
         row_max = jnp.maximum(near_max[n], jnp.max(scores, axis=0, keepdims=True))
         weights = jnp.exp2(scores - row_max)
         rescale = jnp.exp2(near_max[n] - row_max)
@@ -215,49 +234,90 @@
             grad_rows[n].astype(jnp.float32) * attended.astype(jnp.float32), axis=0, keepdims=True
         )
         prob = weights * inverse
-        prob_grad = matmul(back_two[1, g], grad, (1, 1))
-        score_grad = (prob * (prob_grad - delta) * scale).astype(jnp.bfloat16)
+        score_grad = (prob * (prob_grad - delta)).astype(jnp.bfloat16)
         attended_rows[n] = attended
         row_delta[n] = delta
         near_factor[n] = rescale * inverse
         far_grad[n] = score_grad
-        pair = (
-            matmul(score_grad, query, (1, 0)), matmul(prob.astype(jnp.bfloat16), grad, (1, 0)),
-        )
-        parts[g] = pair if g not in parts else (parts[g][0] + pair[0], parts[g][1] + pair[1])
+        return score_grad, prob.astype(jnp.bfloat16)
+
+    accumulate = accumulator(query_head, grad_head, chunks, groups)
+
+    def store(g, key_part, value_part):
+        far_part[0, g] = (key_part * scale).astype(jnp.bfloat16)
+        far_part[1, g] = value_part.astype(jnp.bfloat16)
+
+    pipelined(chunks, products, softmax, lambda n, *halves: accumulate(n, *halves, store))
+
+
+def pipelined(chunks, before, middle, after):
+    ready = before(0)
+    done = None
+    for n in range(chunks):
+        upcoming = before(n + 1) if n + 1 < chunks else None
+        result = middle(n, *ready)
+        if done is not None:
+            after(n - 1, *done)
+        ready, done = upcoming, result
+    after(chunks - 1, *done)
+
+
+def accumulator(query_head, grad_head, chunks, groups):
+    count = query_head.shape[0] // chunks
+    parts = {}
+
+    def accumulate(n, score_grad, half, store):
+        g = n * groups // chunks
+        key_part = matmul(score_grad, grouped(query_head, n, count), (1, 0))
+        value_part = matmul(half, grouped(grad_head, n, count), (1, 0))
+        if g in parts:
+            key_part, value_part = parts[g][0] + key_part, parts[g][1] + value_part
+        parts[g] = (key_part, value_part)
         if (n + 1) * groups // chunks != g:
-            for index in range(2):
-                far_part[index, g] = parts[g][index].astype(jnp.bfloat16)
-
-
-def near_backward_kernel(
-    query_head, grad_head, near_weights, own_weights, near_prob_grad, own_prob_grad, near_factor,
-    own_factor, row_delta, near_grad, one_mine, send_keys, send_values, own_part,
+            store(g, key_part, value_part)
+
+    return accumulate
+
+
+def one_backward_kernel(
+    query_head, grad_head, near_weights, near_prob_grad, near_factor, row_delta,
+    one_grad, one_mine, send_keys, send_values,
 ):
     chunks = near_weights.shape[0]
     groups, length, width = one_mine.shape[1:]
-    count = query_head.shape[0] // chunks
-    parts = {}
+    accumulate = accumulator(query_head, grad_head, chunks, groups)
+
+    def store(g, key_part, value_part):
+        for index, (part, send) in enumerate(
+            ((key_part * width ** (-0.5), send_keys), (value_part, send_values))
+        ):
+            one_mine[index, g] = part[:length].astype(jnp.bfloat16)
+            send[g] = part[length:].astype(jnp.bfloat16)
+
     for n in range(chunks):
-        g = n * groups // chunks
-        query = grouped(query_head, n, count)
-        grad = grouped(grad_head, n, count)
-        prob = join(
-            near_weights[n] * near_factor[n], own_weights[n] * (own_factor[n] * near_factor[n])
-        )
-        prob_grad = join(near_prob_grad[n], own_prob_grad[n])
-        score_grad = (prob * (prob_grad - row_delta[n]) * width ** (-0.5)).astype(jnp.bfloat16)
-        near_grad[n] = score_grad
-        pair = (
-            matmul(score_grad, query, (1, 0)), matmul(prob.astype(jnp.bfloat16), grad, (1, 0)),
-        )
-        parts[g] = pair if g not in parts else (parts[g][0] + pair[0], parts[g][1] + pair[1])
-        if (n + 1) * groups // chunks != g:
-            for index in range(2):
-                one_mine[index, g] = parts[g][index][:length].astype(jnp.bfloat16)
-                send = (send_keys, send_values)[index]
-                send[g] = parts[g][index][length : 2 * length].astype(jnp.bfloat16)
-                own_part[index, g] = parts[g][index][2 * length :]
+        prob = near_weights[n] * near_factor[n]
+        score_grad = (prob * (near_prob_grad[n] - row_delta[n])).astype(jnp.bfloat16)
+        one_grad[n] = score_grad
+        accumulate(n, score_grad, prob.astype(jnp.bfloat16), store)
+
+
+def own_backward_kernel(
+    query_head, grad_head, own_weights, own_prob_grad, near_factor, own_factor, row_delta,
+    after, own_grad, own_part,
+):
+    chunks = own_weights.shape[0]
+    groups, _, width = own_part.shape[1:]
+    accumulate = accumulator(query_head, grad_head, chunks, groups)
+
+    def store(g, key_part, value_part):
+        own_part[0, g] = key_part * width ** (-0.5)
+        own_part[1, g] = value_part
+
+    for n in range(chunks):
+        prob = own_weights[n] * (own_factor[n] * near_factor[n])
+        score_grad = (prob * (own_prob_grad[n] - row_delta[n])).astype(jnp.bfloat16)
+        own_grad[n] = score_grad
+        accumulate(n, score_grad, prob.astype(jnp.bfloat16), store)
 
 
 def join_one_kernel(one_mine, other_keys, other_values, one_part):
@@ -268,7 +328,7 @@
 
 
 def query_kernel(
-    own, back_one, one_keys, back_two, attended_rows, far_grad, near_grad, after,
+    own, back_one, one_keys, back_two, attended_rows, far_grad, one_grad, own_grad,
     out_mine, query_mine, first_third, second_third, last_third, query_send,
 ):
     sends = (first_third, second_third, last_third)
@@ -280,7 +340,8 @@
         g = n * groups // chunks
         rows = pl.ds(n * count, count)
         keys = join(back_two[0, g], one_back(back_one, (one_keys,), 0, g), own[0, g])
-        part = matmul(keys, join(far_grad[n], near_grad[n]), (0, 0)).astype(jnp.bfloat16)
+        part = matmul(keys, join(far_grad[n], one_grad[n], own_grad[n]), (0, 0))
+        part = (part * width ** (-0.5)).astype(jnp.bfloat16)
         for index, (columns, mine) in enumerate(((attended_rows[n], out_mine), (part, query_mine))):
             block = columns.T.reshape(count, 2 * length, width)
             mine[rows] = block[:, :length]
@@ -401,14 +462,11 @@
         (first, query_head, grad_head, back_two, grad_rows, near_max, near_total, near_out),
     )
     far_total = shifted(far_part, "seq", -2)
-    near_grad, part_mine, *part_sends, own_part = call(
-        near_backward_kernel,
-        "near_backward",
-        [rows_of(2 * tokens, half), half_pair, half_block, half_block, (chip_pair[0], full)],
-        (
-            query_head, grad_head, near_weights, own_weights, near_prob_grad, own_prob_grad,
-            near_factor, own_factor, row_delta,
-        ),
+    one_grad, part_mine, *part_sends = call(
+        one_backward_kernel,
+        "one_backward",
+        [rows_of(tokens, half), half_pair, half_block, half_block],
+        (query_head, grad_head, near_weights, near_prob_grad, near_factor, row_delta),
     )
     (one_part,) = call(
         join_one_kernel,
@@ -417,11 +475,20 @@
         (part_mine, *[swapped(send, "head") for send in part_sends]),
     )
     one_total = shifted(one_part, "seq", -1)
+    own_grad, own_part = call(
+        own_backward_kernel,
+        "own_backward",
+        [rows_of(tokens, half), (chip_pair[0], full)],
+        (
+            query_head, grad_head, own_weights, own_prob_grad, near_factor, own_factor, row_delta,
+            one_part,
+        ),
+    )
     out_mine, query_mine, *sends = call(
         query_kernel,
         "query_grad",
         [half_rows] * 2 + third_rows,
-        (own_head, back_one, one_other[0], back_two, attended_rows, far_grad, near_grad, one_part),
+        (own_head, back_one, one_other[0], back_two, attended_rows, far_grad, one_grad, own_grad),
         scratch=[pltpu.VMEM((2,) + half_rows[0], half)],
     )
     attn_out, query_grad, token = call(

time: 39.8 us -> 37.6 us (0.945)
  the two profiles are of different devices: /device:TPU:3 before, /device:TPU:14 now
where the time goes in v7:
time: 37.6 us; the launch traced here: 37.3 us
  starting transfers between devices  17.3 us (46%)
  waiting for transfers between devices  9.75 us (26%)
  Pallas kernels  7.76 us (21%)
  between operations  1.46 us (4%)
  other arithmetic  1.05 us (3%)
    ppermute x4, starting transfers between devices, shifted(): return lax.ppermute(block, axis, route)  13.8 us
    pallas_call x14, Pallas kernels, call(): pl.pallas_call(kernel, out_shape=tuple((jax.ShapeDtypeStruct(shape, kind)...  7.76 us
    ppermute x4, waiting for transfers between devices, shifted(): return lax.ppermute(block, axis, route)  5.52 us
    ppermute x13, waiting for transfers between devices, swapped(): return lax.ppermute(block, axis, [(i, count - 1 - i) for i in range(count)])  4.24 us
    ppermute x13, starting transfers between devices, swapped(): return lax.ppermute(block, axis, [(i, count - 1 - i) for i in range(count)])  3.52 us
    another operation x1, other arithmetic, shards(): own = jnp.stack([key_matrix, value_matrix])  1.05 us
  transfers between devices with their start and end apart: 17, of which 10 were waited for; matrix products, arithmetic and copies ran while one was open for 0% of the time, Pallas kernels for 15%

profile of v7, /device:TPU:14, one launch (start us, length us, event | category | flops | bytes accessed | tf_op | source)
XLA Modules:
  0.0 37.3 jit_solution(6807649041820514708)
XLA Ops:
  0.6 1.1 %pad_maximum_fusion.block.own.after = bf16[2,8,64,128]{3,2,1,0:T(8,128)(2,1)S(1)} fusion(bf16[1,8,64,128]{3,2,1,0:T(8,128)(2,1)} %bitcast.2, bf16[1,8,64,128]{3,2,1,0:T(8,128)(2,1)} %bitcast.3), kind=kLoop, calls=%fused_computation | loop fusion | flops 131072 | bytes 524288 | tf_op jit(solution)/shard_map/stack | solution.py:419
  1.7 3.5 %collective-permute-start.2 = (bf16[2,8,64,128]{3,2,1,0:T(8,128)(2,1)S(1)}, bf16[2,8,64,128]{3,2,1,0:T(8,128)(2,1)S(1)}, u32[]{:S(2)}, u32[]{:S(2)}) collective-permute-start(bf16[2,8,64,128]{3,2,1,0:T(8,128)(2,1)S(1)} %pad_maximum_fusion.block.own.after), channel_id=1, source_target_pairs={{0,1},{1,2},{2,3},{3,4},{4,5},{5,6},{6,7},{7,8},{8,9},{9,10},{10,1... | collective-permute-start | bytes 786440 | tf_op jit(solution)/shard_map/ppermute | solution.py:19
  5.4 0.5 %collective-permute-start.1 = (bf16[4,64,128]{2,1,0:T(8,128)(2,1)S(1)}, bf16[4,64,128]{2,1,0:T(8,128)(2,1)S(1)}, u32[]{:S(2)}, u32[]{:S(2)}) collective-permute-start(bf16[4,64,128]{2,1,0:T(8,128)(2,1)S(1)} %get-tuple-element.54), channel_id=1, source_target_pairs={{0,16},{16,0},{1,17},{17,1},{2,18},{18,2},{3,19},{19,3},{4,20},{20... | collective-permute-start | bytes 196616 | tf_op jit(solution)/shard_map/ppermute | solution.py:24
  5.9 0.7 %collective-permute-done.other_keys = bf16[4,64,128]{2,1,0:T(8,128)(2,1)S(1)} collective-permute-done((bf16[4,64,128]{2,1,0:T(8,128)(2,1)S(1)}, bf16[4,64,128]{2,1,0:T(8,128)(2,1)S(1)}, u32[]{:S(2)}, u32[]{:S(2)}) %collective-permute-start) | collective-permute-done | bytes 65568 | tf_op jit(solution)/shard_map/ppermute | solution.py:24
  6.8 3.4 %collective-permute-start.7 = (bf16[2,4,128,128]{3,2,1,0:T(8,128)(2,1)S(1)}, bf16[2,4,128,128]{3,2,1,0:T(8,128)(2,1)S(1)}, u32[]{:S(2)}, u32[]{:S(2)}) collective-permute-start(bf16[2,4,128,128]{3,2,1,0:T(8,128)(2,1)S(1)} %join_own.1.own), channel_id=1, source_target_pairs={{0,2},{1,3},{2,4},{3,5},{4,6},{5,7},{6,8},{7,9},{8,10},{9,11},{10,... | collective-permute-start | bytes 786440 | tf_op jit(solution)/shard_map/ppermute | solution.py:19
  11.6 0.7 %collective-permute-done.3.first_third = bf16[10,64,128]{2,1,0:T(8,128)(2,1)S(1)} collective-permute-done((bf16[10,64,128]{2,1,0:T(8,128)(2,1)S(1)}, bf16[10,64,128]{2,1,0:T(8,128)(2,1)S(1)}, u32[]{:S(2)}, u32[]{:S(2)}) %collective-permute-start.3) | collective-permute-done | bytes 163872 | tf_op jit(solution)/shard_map/ppermute | solution.py:24
  12.3 1.5 %own_block.1 = (bf16[16,128,128]{2,1,0:T(8,128)(2,1)S(1)}, bf16[16,128,128]{2,1,0:T(8,128)(2,1)S(1)}, bf16[8,128,256]{2,1,0:T(8,128)(2,1)S(1)}, s32[8,1,256]{2,1...) custom-call(s32[32]{0:T(128)S(1)} %copy-done.2, ...), custom_call_target="tpu_custom_call" | custom-call | flops 1 | tf_op jit(solution)/shard_map/own_block/pallas_call | solution.py:396
  14.4 0.7 %collective-permute-done.6.one_keys = bf16[4,64,128]{2,1,0:T(8,128)(2,1)S(1)} collective-permute-done((bf16[4,64,128]{2,1,0:T(8,128)(2,1)S(1)}, bf16[4,64,128]{2,1,0:T(8,128)(2,1)S(1)}, u32[]{:S(2)}, u32[]{:S(2)}) %collective-permute-start.6) | collective-permute-done | bytes 65568 | tf_op jit(solution)/shard_map/ppermute | solution.py:24
  15.4 0.9 %near_forward.1 = (f32[8,1,256]{2,1,0:T(1,128)S(1)}, f32[8,1,256]{2,1,0:T(1,128)S(1)}, f32[8,128,256]{2,1,0:T(8,128)S(1)}, f32[8,128,256]{2,1,0:T(8,128)S(1)}, f...) custom-call(s32[8,1,256]{2,1,0:T(1,128)S(1)} %get-tuple-element.61.first, ...), custom_call_target="tpu_custom_call" | custom-call | flops 1 | tf_op jit(solution)/shard_map/near_forward/pallas_call | solution.py:396
  16.4 0.9 %collective-permute-done.7.back_two = bf16[2,4,128,128]{3,2,1,0:T(8,128)(2,1)S(1)} collective-permute-done((bf16[2,4,128,128]{3,2,1,0:T(8,128)(2,1)S(1)}, bf16[2,4,128,128]{3,2,1,0:T(8,128)(2,1)S(1)}, u32[]{:S(2)}, u32[]{:S(2)}) %collective-permute-start.7) | collective-permute-done | bytes 262176 | tf_op jit(solution)/shard_map/ppermute | solution.py:19
  17.2 1.6 %far_forward_backward.1 = (bf16[8,128,256]{2,1,0:T(8,128)(2,1)S(1)}, f32[8,1,256]{2,1,0:T(1,128)S(1)}, f32[8,1,256]{2,1,0:T(1,128)S(1)}, bf16[8,128,256]{2,1,0:T(8,128)(2,1)S(1)}, bf16[2,4,128,128]{3,2,1,0:T(8,128)(2,1)S(1)}) custom-call(s32[8,1,256]{2,1,0:T(1,128)S(1)} %get-tuple-element.61.first, bf16[16,128,128]{2,1,0:T(8,128)(2,1)S(1)} %get-tuple-element.62.query_head, ...), custom_call_target="tpu_custom_call" | custom-call | flops 1 | tf_op jit(solution)/shard_map/far_forward_backward/pallas_call | solution.py:396
  18.8 3.5 %collective-permute-start.14 = (bf16[2,4,128,128]{3,2,1,0:T(8,128)(2,1)S(1)}, bf16[2,4,128,128]{3,2,1,0:T(8,128)(2,1)S(1)}, u32[]{:S(2)}, u32[]{:S(2)}) collective-permute-start(bf16[2,4,128,128]{3,2,1,0:T(8,128)(2,1)S(1)} %get-tuple-element.96), channel_id=1, source_target_pairs={{2,0},{3,1},{4,2},{5,3},{6,4},{7,5},{8,6},{9,7},{10,8},{11,9},{12,... | collective-permute-start | bytes 786440 | tf_op jit(solution)/shard_map/ppermute | solution.py:19
  22.3 0.5 %one_backward.1 = (bf16[8,128,256]{2,1,0:T(8,128)(2,1)S(1)}, bf16[2,4,64,128]{3,2,1,0:T(8,128)(2,1)S(1)}, bf16[4,64,128]{2,1,0:T(8,128)(2,1)S(1)}, bf16[4,64,128]{2,1,0:T(8,128)(2,1)S(1)}) custom-call(bf16[16,128,128]{2,1,0:T(8,128)(2,1)S(1)} %get-tuple-element.62.query_head, bf16[16,128,128]{2,1,0:T(8,128)(2,1)S(1)} %get-tuple-element.63.grad_head, ...), custom_call_target="tpu_custom_call" | custom-call | flops 1 | tf_op jit(solution)/shard_map/one_backward/pallas_call | solution.py:396
  22.9 0.5 %collective-permute-start.10 = (bf16[4,64,128]{2,1,0:T(8,128)(2,1)S(1)}, bf16[4,64,128]{2,1,0:T(8,128)(2,1)S(1)}, u32[]{:S(2)}, u32[]{:S(2)}) collective-permute-start(bf16[4,64,128]{2,1,0:T(8,128)(2,1)S(1)} %get-tuple-element.86), channel_id=1, source_target_pairs={{0,16},{16,0},{1,17},{17,1},{2,18},{18,2},{3,19},{19,3},{4,20},{20... | collective-permute-start | bytes 196616 | tf_op jit(solution)/shard_map/ppermute | solution.py:24
  23.4 0.7 %collective-permute-done.9.other_keys = bf16[4,64,128]{2,1,0:T(8,128)(2,1)S(1)} collective-permute-done((bf16[4,64,128]{2,1,0:T(8,128)(2,1)S(1)}, bf16[4,64,128]{2,1,0:T(8,128)(2,1)S(1)}, u32[]{:S(2)}, u32[]{:S(2)}) %collective-permute-start.9) | collective-permute-done | bytes 65568 | tf_op jit(solution)/shard_map/ppermute | solution.py:24
  24.3 3.4 %collective-permute-start.16 = (bf16[2,8,64,128]{3,2,1,0:T(8,128)(2,1)S(1)}, bf16[2,8,64,128]{3,2,1,0:T(8,128)(2,1)S(1)}, u32[]{:S(2)}, u32[]{:S(2)}) collective-permute-start(bf16[2,8,64,128]{3,2,1,0:T(8,128)(2,1)S(1)} %join_one.1.after), channel_id=1, source_target_pairs={{1,0},{2,1},{3,2},{4,3},{5,4},{6,5},{7,6},{8,7},{9,8},{10,9},{11,1... | collective-permute-start | bytes 786440 | tf_op jit(solution)/shard_map/ppermute | solution.py:19
  27.7 0.5 %own_backward.1 = (bf16[8,128,256]{2,1,0:T(8,128)(2,1)S(1)}, f32[2,4,128,128]{3,2,1,0:T(8,128)S(1)}) custom-call(bf16[16,128,128]{2,1,0:T(8,128)(2,1)S(1)} %get-tuple-element.62.query_head, bf16[16,128,128]{2,1,0:T(8,128)(2,1)S(1)} %get-tuple-element.63.grad_head, f32[8,128,256]{2,1,0:T(8,128)S(1)} %get-tuple-element.81.own_weights, ...), custom_call_target="tpu_custom_call" | custom-call | flops 1 | tf_op jit(solution)/shard_map/own_backward/pallas_call | solution.py:396
  28.2 0.7 %query_grad.1 = (bf16[16,64,128]{2,1,0:T(8,128)(2,1)S(1)}, bf16[16,64,128]{2,1,0:T(8,128)(2,1)S(1)}, bf16[10,64,128]{2,1,0:T(8,128)(2,1)S(1)}, bf16[11,64,128]{2,1,0:T(8,128)(2,1)S(1)}, bf16[11,64,128]{2,1,0:T(8,128)(2,1)S(1)}) custom-call(bf16[2,4,128,128]{3,2,1,0:T(8,128)(2,1)S(1)} %join_own.1.own, ...), custom_call_target="tpu_custom_call" | custom-call | flops 1 | tf_op jit(solution)/shard_map/query_grad/pallas_call | solution.py:396
  29.0 0.4 %collective-permute-start.13 = (bf16[11,64,128]{2,1,0:T(8,128)(2,1)S(1)}, bf16[11,64,128]{2,1,0:T(8,128)(2,1)S(1)}, u32[]{:S(2)}, u32[]{:S(2)}) collective-permute-start(bf16[11,64,128]{2,1,0:T(8,128)(2,1)S(1)} %get-tuple-element.92), channel_id=1, source_target_pairs={{0,16},{16,0},{1,17},{17,1},{2,18},{18,2},{3,19},{19,3},{4,20},{20... | collective-permute-start | bytes 540680 | tf_op jit(solution)/shard_map/ppermute | solution.py:24
  29.6 0.5 %collective-permute-start.15 = (bf16[2,4,64,128]{3,2,1,0:T(8,128)(2,1)S(1)}, bf16[2,4,64,128]{3,2,1,0:T(8,128)(2,1)S(1)}, u32[]{:S(2)}, u32[]{:S(2)}) collective-permute-start(bf16[2,4,64,128]{3,2,1,0:T(8,128)(2,1)S(1)} %get-tuple-element.98), channel_id=1, source_target_pairs={{0,16},{16,0},{1,17},{17,1},{2,18},{18,2},{3,19},{19,3},{4,20},{20... | collective-permute-start | bytes 393224 | tf_op jit(solution)/shard_map/ppermute | solution.py:24
  30.1 0.8 %collective-permute-done.11.first_third = bf16[10,64,128]{2,1,0:T(8,128)(2,1)S(1)} collective-permute-done((bf16[10,64,128]{2,1,0:T(8,128)(2,1)S(1)}, bf16[10,64,128]{2,1,0:T(8,128)(2,1)S(1)}, u32[]{:S(2)}, u32[]{:S(2)}) %collective-permute-start.11) | collective-permute-done | bytes 163872 | tf_op jit(solution)/shard_map/ppermute | solution.py:24
  30.9 1.0 %assemble.1 = (bf16[32,64,128]{2,1,0:T(8,128)(2,1)}, bf16[32,64,128]{2,1,0:T(8,128)(2,1)}, f32[8,128]{1,0:T(8,128)S(1)}) custom-call(bf16[16,64,128]{2,1,0:T(8,128)(2,1)S(1)} %get-tuple-element.88.out_mine, bf16[16,64,128]{2,1,0:T(8,128)(2,1)S(1)} %get-tuple-element.89.query_mine, bf16[10,64,128]{2,1,0:T(8,128)(2,1)S(1)} %collective-permute-done.11.first_third, ...), custom_call_target="tpu_custom_call" | custom-call | flops 1 | tf_op jit(solution)/shard_map/assemble/pallas_call | solution.py:396
  31.9 4.6 %collective-permute-done.16.one_total = bf16[2,8,64,128]{3,2,1,0:T(8,128)(2,1)S(1)} collective-permute-done((bf16[2,8,64,128]{3,2,1,0:T(8,128)(2,1)S(1)}, bf16[2,8,64,128]{3,2,1,0:T(8,128)(2,1)S(1)}, u32[]{:S(2)}, u32[]{:S(2)}) %collective-permute-start.16) | collective-permute-done | bytes 262176 | tf_op jit(solution)/shard_map/ppermute | solution.py:19
  36.6 0.8 %total.1 = (bf16[8,64,128]{2,1,0:T(8,128)(2,1)}, bf16[8,64,128]{2,1,0:T(8,128)(2,1)}) custom-call(f32[2,4,64,128]{3,2,1,0:T(8,128)S(1)} %get-tuple-element.97.sum_mine, bf16[2,4,64,128]{3,2,1,0:T(8,128)(2,1)S(1)} %collective-permute-done.15.sum_other, bf16[2,8,64,128]{3,2,1,0:T(8,128)(2,1)S(1)} %collective-permute-done.16.one_total, ...), custom_call_target="tpu_custom_call" | custom-call | flops 1 | tf_op jit(solution)/shard_map/total/pallas_call | solution.py:396
  (31 shorter events, 2.4 us)
Async XLA Ops:
  0.6 9.6 %copy-start.1 = (bf16[32,64,128]{2,1,0:T(8,128)(2,1)S(1)}, bf16[32,64,128]{2,1,0:T(8,128)(2,1)}, u32[]{:S(2)}) copy-start(bf16[32,64,128]{2,1,0:T(8,128)(2,1)} %grads.3) | copy-start | bytes 1572868
  1.7 8.5 %copy-start = (bf16[32,64,128]{2,1,0:T(8,128)(2,1)S(1)}, bf16[32,64,128]{2,1,0:T(8,128)(2,1)}, u32[]{:S(2)}) copy-start(bf16[32,64,128]{2,1,0:T(8,128)(2,1)} %queries.3) | copy-start | bytes 1572868
  1.7 12.1 %collective-permute-start.2 = (bf16[2,8,64,128]{3,2,1,0:T(8,128)(2,1)S(1)}, bf16[2,8,64,128]{3,2,1,0:T(8,128)(2,1)S(1)}, u32[]{:S(2)}, u32[]{:S(2)}) collective-permute-start(bf16[2,8,64,128]{3,2,1,0:T(8,128)(2,1)S(1)} %pad_maximum_fusion.block.own.after), channel_id=1, source_target_pairs={{0,1},{1,2},{2,3},{3,4},{4,5},{5,6},{6,7},{7,8},{8,9},{9,10},{10,1... | collective-permute-start | bytes 786440 | tf_op jit(solution)/shard_map/ppermute | solution.py:19
  5.3 1.3 %collective-permute-start = (bf16[4,64,128]{2,1,0:T(8,128)(2,1)S(1)}, bf16[4,64,128]{2,1,0:T(8,128)(2,1)S(1)}, u32[]{:S(2)}, u32[]{:S(2)}) collective-permute-start(bf16[4,64,128]{2,1,0:T(8,128)(2,1)S(1)} %get-tuple-element.53), channel_id=1, source_target_pairs={{0,16},{16,0},{1,17},{17,1},{2,18},{18,2},{3,19},{19,3},{4,20},{20... | collective-permute-start | bytes 196616 | tf_op jit(solution)/shard_map/ppermute | solution.py:24
  5.4 1.4 %collective-permute-start.1 = (bf16[4,64,128]{2,1,0:T(8,128)(2,1)S(1)}, bf16[4,64,128]{2,1,0:T(8,128)(2,1)S(1)}, u32[]{:S(2)}, u32[]{:S(2)}) collective-permute-start(bf16[4,64,128]{2,1,0:T(8,128)(2,1)S(1)} %get-tuple-element.54), channel_id=1, source_target_pairs={{0,16},{16,0},{1,17},{17,1},{2,18},{18,2},{3,19},{19,3},{4,20},{20... | collective-permute-start | bytes 196616 | tf_op jit(solution)/shard_map/ppermute | solution.py:24
  6.8 10.5 %collective-permute-start.7 = (bf16[2,4,128,128]{3,2,1,0:T(8,128)(2,1)S(1)}, bf16[2,4,128,128]{3,2,1,0:T(8,128)(2,1)S(1)}, u32[]{:S(2)}, u32[]{:S(2)}) collective-permute-start(bf16[2,4,128,128]{3,2,1,0:T(8,128)(2,1)S(1)} %join_own.1.own), channel_id=1, source_target_pairs={{0,2},{1,3},{2,4},{3,5},{4,6},{5,7},{6,8},{7,9},{8,10},{9,11},{10,... | collective-permute-start | bytes 786440 | tf_op jit(solution)/shard_map/ppermute | solution.py:19
  10.3 2.0 %collective-permute-start.4 = (bf16[11,64,128]{2,1,0:T(8,128)(2,1)S(1)}, bf16[11,64,128]{2,1,0:T(8,128)(2,1)S(1)}, u32[]{:S(2)}, u32[]{:S(2)}) collective-permute-start(bf16[11,64,128]{2,1,0:T(8,128)(2,1)S(1)} %get-tuple-element.56), channel_id=1, source_target_pairs={{0,16},{16,0},{1,17},{17,1},{2,18},{18,2},{3,19},{19,3},{4,20},{20... | collective-permute-start | bytes 540680 | tf_op jit(solution)/shard_map/ppermute | solution.py:24
  10.4 1.8 %collective-permute-start.5 = (bf16[11,64,128]{2,1,0:T(8,128)(2,1)S(1)}, bf16[11,64,128]{2,1,0:T(8,128)(2,1)S(1)}, u32[]{:S(2)}, u32[]{:S(2)}) collective-permute-start(bf16[11,64,128]{2,1,0:T(8,128)(2,1)S(1)} %get-tuple-element.57), channel_id=1, source_target_pairs={{0,16},{16,0},{1,17},{17,1},{2,18},{18,2},{3,19},{19,3},{4,20},{20... | collective-permute-start | bytes 540680 | tf_op jit(solution)/shard_map/ppermute | solution.py:24
  10.9 1.4 %copy-start.2 = (s32[32]{0:T(128)S(1)}, s32[32]{0:T(128)}, u32[]{:S(2)}) copy-start(s32[32]{0:T(128)} %spans.1) | copy-start | bytes 388
  10.9 1.4 %collective-permute-start.3 = (bf16[10,64,128]{2,1,0:T(8,128)(2,1)S(1)}, bf16[10,64,128]{2,1,0:T(8,128)(2,1)S(1)}, u32[]{:S(2)}, u32[]{:S(2)}) collective-permute-start(bf16[10,64,128]{2,1,0:T(8,128)(2,1)S(1)} %get-tuple-element.55), channel_id=1, source_target_pairs={{0,16},{16,0},{1,17},{17,1},{2,18},{18,2},{3,19},{19,3},{4,20},{20... | collective-permute-start | bytes 491528 | tf_op jit(solution)/shard_map/ppermute | solution.py:24
  13.9 1.3 %collective-permute-start.6 = (bf16[4,64,128]{2,1,0:T(8,128)(2,1)S(1)}, bf16[4,64,128]{2,1,0:T(8,128)(2,1)S(1)}, u32[]{:S(2)}, u32[]{:S(2)}) collective-permute-start(bf16[4,64,128]{2,1,0:T(8,128)(2,1)S(1)} %get-tuple-element.60), channel_id=1, source_target_pairs={{0,16},{16,0},{1,17},{17,1},{2,18},{18,2},{3,19},{19,3},{4,20},{20... | collective-permute-start | bytes 196616 | tf_op jit(solution)/shard_map/ppermute | solution.py:24
  14.2 1.3 %collective-permute-start.8 = (bf16[4,64,128]{2,1,0:T(8,128)(2,1)S(1)}, bf16[4,64,128]{2,1,0:T(8,128)(2,1)S(1)}, u32[]{:S(2)}, u32[]{:S(2)}) collective-permute-start(bf16[4,64,128]{2,1,0:T(8,128)(2,1)S(1)} %get-tuple-element.64), channel_id=1, source_target_pairs={{0,16},{16,0},{1,17},{17,1},{2,18},{18,2},{3,19},{19,3},{4,20},{20... | collective-permute-start | bytes 196616 | tf_op jit(solution)/shard_map/ppermute | solution.py:24
  18.8 10.7 %collective-permute-start.14 = (bf16[2,4,128,128]{3,2,1,0:T(8,128)(2,1)S(1)}, bf16[2,4,128,128]{3,2,1,0:T(8,128)(2,1)S(1)}, u32[]{:S(2)}, u32[]{:S(2)}) collective-permute-start(bf16[2,4,128,128]{3,2,1,0:T(8,128)(2,1)S(1)} %get-tuple-element.96), channel_id=1, source_target_pairs={{2,0},{3,1},{4,2},{5,3},{6,4},{7,5},{8,6},{9,7},{10,8},{11,9},{12,... | collective-permute-start | bytes 786440 | tf_op jit(solution)/shard_map/ppermute | solution.py:19
  22.8 1.3 %collective-permute-start.9 = (bf16[4,64,128]{2,1,0:T(8,128)(2,1)S(1)}, bf16[4,64,128]{2,1,0:T(8,128)(2,1)S(1)}, u32[]{:S(2)}, u32[]{:S(2)}) collective-permute-start(bf16[4,64,128]{2,1,0:T(8,128)(2,1)S(1)} %get-tuple-element.85), channel_id=1, source_target_pairs={{0,16},{16,0},{1,17},{17,1},{2,18},{18,2},{3,19},{19,3},{4,20},{20... | collective-permute-start | bytes 196616 | tf_op jit(solution)/shard_map/ppermute | solution.py:24
  22.9 1.4 %collective-permute-start.10 = (bf16[4,64,128]{2,1,0:T(8,128)(2,1)S(1)}, bf16[4,64,128]{2,1,0:T(8,128)(2,1)S(1)}, u32[]{:S(2)}, u32[]{:S(2)}) collective-permute-start(bf16[4,64,128]{2,1,0:T(8,128)(2,1)S(1)} %get-tuple-element.86), channel_id=1, source_target_pairs={{0,16},{16,0},{1,17},{17,1},{2,18},{18,2},{3,19},{19,3},{4,20},{20... | collective-permute-start | bytes 196616 | tf_op jit(solution)/shard_map/ppermute | solution.py:24
  24.3 12.3 %collective-permute-start.16 = (bf16[2,8,64,128]{3,2,1,0:T(8,128)(2,1)S(1)}, bf16[2,8,64,128]{3,2,1,0:T(8,128)(2,1)S(1)}, u32[]{:S(2)}, u32[]{:S(2)}) collective-permute-start(bf16[2,8,64,128]{3,2,1,0:T(8,128)(2,1)S(1)} %join_one.1.after), channel_id=1, source_target_pairs={{1,0},{2,1},{3,2},{4,3},{5,4},{6,5},{7,6},{8,7},{9,8},{10,9},{11,1... | collective-permute-start | bytes 786440 | tf_op jit(solution)/shard_map/ppermute | solution.py:19
  28.9 2.0 %collective-permute-start.12 = (bf16[11,64,128]{2,1,0:T(8,128)(2,1)S(1)}, bf16[11,64,128]{2,1,0:T(8,128)(2,1)S(1)}, u32[]{:S(2)}, u32[]{:S(2)}) collective-permute-start(bf16[11,64,128]{2,1,0:T(8,128)(2,1)S(1)} %get-tuple-element.91), channel_id=1, source_target_pairs={{0,16},{16,0},{1,17},{17,1},{2,18},{18,2},{3,19},{19,3},{4,20},{20... | collective-permute-start | bytes 540680 | tf_op jit(solution)/shard_map/ppermute | solution.py:24
  29.0 1.8 %collective-permute-start.13 = (bf16[11,64,128]{2,1,0:T(8,128)(2,1)S(1)}, bf16[11,64,128]{2,1,0:T(8,128)(2,1)S(1)}, u32[]{:S(2)}, u32[]{:S(2)}) collective-permute-start(bf16[11,64,128]{2,1,0:T(8,128)(2,1)S(1)} %get-tuple-element.92), channel_id=1, source_target_pairs={{0,16},{16,0},{1,17},{17,1},{2,18},{18,2},{3,19},{19,3},{4,20},{20... | collective-permute-start | bytes 540680 | tf_op jit(solution)/shard_map/ppermute | solution.py:24
  29.5 1.4 %collective-permute-start.11 = (bf16[10,64,128]{2,1,0:T(8,128)(2,1)S(1)}, bf16[10,64,128]{2,1,0:T(8,128)(2,1)S(1)}, u32[]{:S(2)}, u32[]{:S(2)}) collective-permute-start(bf16[10,64,128]{2,1,0:T(8,128)(2,1)S(1)} %get-tuple-element.90), channel_id=1, source_target_pairs={{0,16},{16,0},{1,17},{17,1},{2,18},{18,2},{3,19},{19,3},{4,20},{20... | collective-permute-start | bytes 491528 | tf_op jit(solution)/shard_map/ppermute | solution.py:24
  29.6 6.9 %collective-permute-start.15 = (bf16[2,4,64,128]{3,2,1,0:T(8,128)(2,1)S(1)}, bf16[2,4,64,128]{3,2,1,0:T(8,128)(2,1)S(1)}, u32[]{:S(2)}, u32[]{:S(2)}) collective-permute-start(bf16[2,4,64,128]{3,2,1,0:T(8,128)(2,1)S(1)} %get-tuple-element.98), channel_id=1, source_target_pairs={{0,16},{16,0},{1,17},{17,1},{2,18},{18,2},{3,19},{19,3},{4,20},{20... | collective-permute-start | bytes 393224 | tf_op jit(solution)/shard_map/ppermute | solution.py:24

commit v8 on v7

--- a/solution.py
+++ b/solution.py
@@ -164,17 +164,17 @@
     pipelined(chunks, products, softmax, weigh)
 
 
-def one_back(back_one, one_other, index, g):
-    base = lax.axis_index("head") * one_other[index].shape[0]
-    return join(back_one[index, base + g], one_other[index][g])
+def two_back(back_two, two_other, index, g):
+    base = lax.axis_index("head") * two_other[index].shape[0]
+    return join(back_two[index, base + g], two_other[index][g])
 
 
 def near_forward_kernel(
-    first, query_head, grad_head, back_one, one_keys, one_values, own_max, own_total, own_out,
+    first, query_head, grad_head, back_two, two_keys, two_values, own_max, own_total, own_out,
     near_max, near_total, near_out, near_weights, near_prob_grad, own_factor,
 ):
-    groups = one_keys.shape[0]
-    one_other = (one_keys, one_values)
+    groups = two_keys.shape[0]
+    two_other = (two_keys, two_values)
     chunks = first.shape[0]
     heads, _, width = query_head.shape
     count = heads // chunks
@@ -182,13 +182,13 @@
 
     def products(n):
         g = n * groups // chunks
-        keys = one_back(back_one, one_other, 0, g)
-        values = one_back(back_one, one_other, 1, g)
+        keys = two_back(back_two, two_other, 0, g)
+        values = two_back(back_two, two_other, 1, g)
         near_prob_grad[n] = matmul(values, grouped(grad_head, n, count), (1, 1))
         return (matmul(keys, grouped(query_head, n, count), (1, 1)),)
 
     def softmax(n, scores):
-        scores = masked(scores * factor, first[n], 1)
+        scores = masked(scores * factor, first[n], 2)
         row_max = jnp.maximum(own_max[n], jnp.max(scores, axis=0, keepdims=True))
         weights = jnp.exp2(scores - row_max)
         rescale = jnp.exp2(own_max[n] - row_max)
@@ -199,17 +199,17 @@
         return rescale, weights.astype(jnp.bfloat16)
 
     def weigh(n, rescale, halves):
-        values = one_back(back_one, one_other, 1, n * groups // chunks)
+        values = two_back(back_two, two_other, 1, n * groups // chunks)
         near_out[n] = own_out[n] * rescale + matmul(values, halves, (0, 0))
 
     pipelined(chunks, products, softmax, weigh)
 
 
-def far_kernel(
-    first, query_head, grad_head, back_two, grad_rows, near_max, near_total, near_out,
-    attended_rows, row_delta, near_factor, far_grad, far_part,
-):
-    groups = back_two.shape[1]
+def last_kernel(
+    first, query_head, grad_head, back_one, grad_rows, near_max, near_total, near_out,
+    attended_rows, row_delta, near_factor, one_grad, one_part,
+):
+    groups = back_one.shape[1]
     chunks = first.shape[0]
     heads, _, width = query_head.shape
     count = heads // chunks
@@ -217,18 +217,18 @@
 
     def products(n):
         g = n * groups // chunks
-        scores = matmul(back_two[0, g], grouped(query_head, n, count), (1, 1))
-        prob_grad = matmul(back_two[1, g], grouped(grad_head, n, count), (1, 1))
+        scores = matmul(back_one[0, g], grouped(query_head, n, count), (1, 1))
+        prob_grad = matmul(back_one[1, g], grouped(grad_head, n, count), (1, 1))
         return scores, prob_grad
 
     def softmax(n, scores, prob_grad):
         g = n * groups // chunks
-        scores = masked(scores * (scale * math.log2(math.e)), first[n], 2)
+        scores = masked(scores * (scale * math.log2(math.e)), first[n], 1)
         row_max = jnp.maximum(near_max[n], jnp.max(scores, axis=0, keepdims=True))
         weights = jnp.exp2(scores - row_max)
         rescale = jnp.exp2(near_max[n] - row_max)
         inverse = 1.0 / (near_total[n] * rescale + jnp.sum(weights, axis=0, keepdims=True))
-        weighted = matmul(back_two[1, g], weights.astype(jnp.bfloat16), (0, 0))
+        weighted = matmul(back_one[1, g], weights.astype(jnp.bfloat16), (0, 0))
         attended = ((near_out[n] * rescale + weighted) * inverse).astype(jnp.bfloat16)
         delta = jnp.sum(
             grad_rows[n].astype(jnp.float32) * attended.astype(jnp.float32), axis=0, keepdims=True
@@ -238,14 +238,14 @@
         attended_rows[n] = attended
         row_delta[n] = delta
         near_factor[n] = rescale * inverse
-        far_grad[n] = score_grad
+        one_grad[n] = score_grad
         return score_grad, prob.astype(jnp.bfloat16)
 
     accumulate = accumulator(query_head, grad_head, chunks, groups)
 
     def store(g, key_part, value_part):
-        far_part[0, g] = (key_part * scale).astype(jnp.bfloat16)
-        far_part[1, g] = value_part.astype(jnp.bfloat16)
+        one_part[0, g] = (key_part * scale).astype(jnp.bfloat16)
+        one_part[1, g] = value_part.astype(jnp.bfloat16)
 
     pipelined(chunks, products, softmax, lambda n, *halves: accumulate(n, *halves, store))
 
@@ -279,25 +279,22 @@
     return accumulate
 
 
-def one_backward_kernel(
+def two_backward_kernel(
     query_head, grad_head, near_weights, near_prob_grad, near_factor, row_delta,
-    one_grad, one_mine, send_keys, send_values,
+    two_grad, two_part,
 ):
     chunks = near_weights.shape[0]
-    groups, length, width = one_mine.shape[1:]
+    groups, _, width = two_part.shape[1:]
     accumulate = accumulator(query_head, grad_head, chunks, groups)
 
     def store(g, key_part, value_part):
-        for index, (part, send) in enumerate(
-            ((key_part * width ** (-0.5), send_keys), (value_part, send_values))
-        ):
-            one_mine[index, g] = part[:length].astype(jnp.bfloat16)
-            send[g] = part[length:].astype(jnp.bfloat16)
+        two_part[0, g] = (key_part * width ** (-0.5)).astype(jnp.bfloat16)
+        two_part[1, g] = value_part.astype(jnp.bfloat16)
 
     for n in range(chunks):
         prob = near_weights[n] * near_factor[n]
         score_grad = (prob * (near_prob_grad[n] - row_delta[n])).astype(jnp.bfloat16)
-        one_grad[n] = score_grad
+        two_grad[n] = score_grad
         accumulate(n, score_grad, prob.astype(jnp.bfloat16), store)
 
 
@@ -320,27 +317,27 @@
         accumulate(n, score_grad, prob.astype(jnp.bfloat16), store)
 
 
-def join_one_kernel(one_mine, other_keys, other_values, one_part):
-    groups = one_mine.shape[1]
-    one_part[:, my_heads(groups)] = one_mine[...]
-    one_part[0, other_heads(groups)] = other_keys[...]
-    one_part[1, other_heads(groups)] = other_values[...]
+def join_one_kernel(one_part, one_other, one_joined):
+    groups, tokens = one_part.shape[1:3]
+    length = tokens // 2
+    one_joined[:, my_heads(groups)] = one_part[:, :, pl.ds(0, length)]
+    one_joined[:, other_heads(groups)] = one_other[:, :, pl.ds(length, length)]
 
 
 def query_kernel(
-    own, back_one, one_keys, back_two, attended_rows, far_grad, one_grad, own_grad,
+    own, back_one, back_two, two_keys, attended_rows, two_grad, one_grad, own_grad,
     out_mine, query_mine, first_third, second_third, last_third, query_send,
 ):
     sends = (first_third, second_third, last_third)
     groups = own.shape[1]
-    chunks = far_grad.shape[0]
+    chunks = own_grad.shape[0]
     heads, length, width = out_mine.shape
     count = heads // chunks
     for n in range(chunks):
         g = n * groups // chunks
         rows = pl.ds(n * count, count)
-        keys = join(back_two[0, g], one_back(back_one, (one_keys,), 0, g), own[0, g])
-        part = matmul(keys, join(far_grad[n], one_grad[n], own_grad[n]), (0, 0))
+        keys = join(two_back(back_two, (two_keys,), 0, g), back_one[0, g], own[0, g])
+        part = matmul(keys, join(two_grad[n], one_grad[n], own_grad[n]), (0, 0))
         part = (part * width ** (-0.5)).astype(jnp.bfloat16)
         for index, (columns, mine) in enumerate(((attended_rows[n], out_mine), (part, query_mine))):
             block = columns.T.reshape(count, 2 * length, width)
@@ -362,9 +359,9 @@
     token[...] = jnp.zeros(token.shape, token.dtype)
 
 
-def own_sum_kernel(own_part, far_total, sum_mine, sum_send):
+def own_sum_kernel(own_part, two_total, sum_mine, sum_send):
     length = sum_mine.shape[2]
-    total = own_part[...] + far_total[...].astype(jnp.float32)
+    total = own_part[...] + two_total[...].astype(jnp.float32)
     sum_mine[...] = total[:, :, :length]
     sum_send[...] = total[:, :, length:].astype(jnp.bfloat16)
 
@@ -417,12 +414,12 @@
     chip_rows = ((heads_here, tokens, width), half)
 
     own = jnp.stack([key_matrix, value_matrix])
-    back_one = shifted(own, "seq", 1)
+    back_two = shifted(own, "seq", 2)
     own_sends = call(split_kernel, "split_own", [half_block] * 2, (own,))
     (own_head,) = call(
         join_own_kernel, "join_own", [chip_pair], (own, *[swapped(send, "head") for send in own_sends])
     )
-    back_two = shifted(own_head, "seq", 2)
+    back_one = shifted(own_head, "seq", 1)
     sends = call(
         split_rows_kernel,
         "split_rows",
@@ -445,35 +442,31 @@
         ),
         scalars=2,
     )
-    back_one, first = lax.optimization_barrier((back_one, first))
-    one_sends = call(split_kernel, "split_one", [half_block] * 2, (back_one,))
-    one_other = [swapped(send, "head") for send in one_sends]
+    back_two, first = lax.optimization_barrier((back_two, first))
+    two_sends = call(split_kernel, "split_two", [half_block] * 2, (back_two,))
+    two_other = [swapped(send, "head") for send in two_sends]
     near_max, near_total, near_out, near_weights, near_prob_grad, own_factor = call(
         near_forward_kernel,
         "near_forward",
         [stat, stat, rows_of(width, full), rows_of(tokens, full), rows_of(tokens, full), stat],
-        (first, query_head, grad_head, back_one, *one_other, own_max, own_total, own_out),
-    )
-    back_two, near_max = lax.optimization_barrier((back_two, near_max))
-    attended_rows, row_delta, near_factor, far_grad, far_part = call(
-        far_kernel,
-        "far_forward_backward",
+        (first, query_head, grad_head, back_two, *two_other, own_max, own_total, own_out),
+    )
+    back_one, near_max = lax.optimization_barrier((back_one, near_max))
+    attended_rows, row_delta, near_factor, one_grad, chip_part = call(
+        last_kernel,
+        "last_forward_backward",
         [rows_of(width, half), stat, stat, rows_of(tokens, half), chip_pair],
-        (first, query_head, grad_head, back_two, grad_rows, near_max, near_total, near_out),
-    )
-    far_total = shifted(far_part, "seq", -2)
-    one_grad, part_mine, *part_sends = call(
-        one_backward_kernel,
-        "one_backward",
-        [rows_of(tokens, half), half_pair, half_block, half_block],
+        (first, query_head, grad_head, back_one, grad_rows, near_max, near_total, near_out),
+    )
+    chip_other = swapped(chip_part, "head")
+    two_grad, two_part = call(
+        two_backward_kernel,
+        "two_backward",
+        [rows_of(tokens, half), chip_pair],
         (query_head, grad_head, near_weights, near_prob_grad, near_factor, row_delta),
     )
-    (one_part,) = call(
-        join_one_kernel,
-        "join_one",
-        [whole_pair],
-        (part_mine, *[swapped(send, "head") for send in part_sends]),
-    )
+    two_total = shifted(two_part, "seq", -2)
+    (one_part,) = call(join_one_kernel, "join_one", [whole_pair], (chip_part, chip_other))
     one_total = shifted(one_part, "seq", -1)
     own_grad, own_part = call(
         own_backward_kernel,
@@ -488,7 +481,7 @@
         query_kernel,
         "query_grad",
         [half_rows] * 2 + third_rows,
-        (own_head, back_one, one_other[0], back_two, attended_rows, far_grad, one_grad, own_grad),
+        (own_head, back_one, back_two, two_other[0], attended_rows, two_grad, one_grad, own_grad),
         scratch=[pltpu.VMEM((2,) + half_rows[0], half)],
     )
     attn_out, query_grad, token = call(
@@ -498,7 +491,7 @@
         (out_mine, query_mine, *[swapped(send, "head") for send in sends]),
     )
     sum_mine, sum_send = call(
-        own_sum_kernel, "own_sum", [(half_pair[0], full), half_pair], (own_part, far_total)
+        own_sum_kernel, "own_sum", [(half_pair[0], full), half_pair], (own_part, two_total)
     )
     key_grad, value_grad = call(
         final_kernel,

time: 37.6 us -> 38.5 us (1.024)
  the two profiles are of different devices: /device:TPU:14 before, /device:TPU:3 now
where the time goes in v8:
time: 38.5 us; the launch traced here: 38.3 us
  starting transfers between devices  14.8 us (38%)
  waiting for transfers between devices  13.2 us (34%)
  Pallas kernels  7.75 us (20%)
  between operations  1.46 us (4%)
  other arithmetic  1.05 us (3%)
    ppermute x4, waiting for transfers between devices, shifted(): return lax.ppermute(block, axis, route)  10.5 us
    ppermute x4, starting transfers between devices, shifted(): return lax.ppermute(block, axis, route)  9.61 us
    pallas_call x14, Pallas kernels, call(): pl.pallas_call(kernel, out_shape=tuple((jax.ShapeDtypeStruct(shape, kind)...  7.75 us
    ppermute x12, starting transfers between devices, swapped(): return lax.ppermute(block, axis, [(i, count - 1 - i) for i in range(count)])  5.23 us
    ppermute x12, waiting for transfers between devices, swapped(): return lax.ppermute(block, axis, [(i, count - 1 - i) for i in range(count)])  2.68 us
    another operation x1, other arithmetic, shards(): own = jnp.stack([key_matrix, value_matrix])  1.05 us
  transfers between devices with their start and end apart: 16, of which 7 were waited for; matrix products, arithmetic and copies ran while one was open for 0% of the time, Pallas kernels for 14%

profile of v8, /device:TPU:3, one launch (start us, length us, event | category | flops | bytes accessed | tf_op | source)
XLA Modules:
  0.0 38.3 jit_solution(5851173010047469414)
XLA Ops:
  0.6 1.1 %pad_maximum_fusion.block.own.after = bf16[2,8,64,128]{3,2,1,0:T(8,128)(2,1)S(1)} fusion(bf16[1,8,64,128]{3,2,1,0:T(8,128)(2,1)} %bitcast.2, bf16[1,8,64,128]{3,2,1,0:T(8,128)(2,1)} %bitcast.3), kind=kLoop, calls=%fused_computation | loop fusion | flops 131072 | bytes 524288 | tf_op jit(solution)/shard_map/stack | solution.py:416
  1.7 3.3 %collective-permute-start.3 = (bf16[2,8,64,128]{3,2,1,0:T(8,128)(2,1)S(1)}, bf16[2,8,64,128]{3,2,1,0:T(8,128)(2,1)S(1)}, u32[]{:S(2)}, u32[]{:S(2)}) collective-permute-start(bf16[2,8,64,128]{3,2,1,0:T(8,128)(2,1)S(1)} %pad_maximum_fusion.block.own.after), channel_id=1, source_target_pairs={{0,2},{1,3},{2,4},{3,5},{4,6},{5,7},{6,8},{7,9},{8,10},{9,11},{10,... | collective-permute-start | bytes 786440 | tf_op jit(solution)/shard_map/ppermute | solution.py:19
  5.0 1.0 %collective-permute-start = (bf16[4,64,128]{2,1,0:T(8,128)(2,1)S(1)}, bf16[4,64,128]{2,1,0:T(8,128)(2,1)S(1)}, u32[]{:S(2)}, u32[]{:S(2)}) collective-permute-start(bf16[4,64,128]{2,1,0:T(8,128)(2,1)S(1)} %get-tuple-element.51), channel_id=1, source_target_pairs={{0,16},{16,0},{1,17},{17,1},{2,18},{18,2},{3,19},{19,3},{4,20},{20... | collective-permute-start | bytes 196616 | tf_op jit(solution)/shard_map/ppermute | solution.py:24
  6.1 0.8 %collective-permute-done.other_keys = bf16[4,64,128]{2,1,0:T(8,128)(2,1)S(1)} collective-permute-done((bf16[4,64,128]{2,1,0:T(8,128)(2,1)S(1)}, bf16[4,64,128]{2,1,0:T(8,128)(2,1)S(1)}, u32[]{:S(2)}, u32[]{:S(2)}) %collective-permute-start) | collective-permute-done | bytes 65568 | tf_op jit(solution)/shard_map/ppermute | solution.py:24
  7.0 0.4 collective-permute-done.1.other_values
  7.3 3.1 %collective-permute-start.2 = (bf16[2,4,128,128]{3,2,1,0:T(8,128)(2,1)S(1)}, bf16[2,4,128,128]{3,2,1,0:T(8,128)(2,1)S(1)}, u32[]{:S(2)}, u32[]{:S(2)}) collective-permute-start(bf16[2,4,128,128]{3,2,1,0:T(8,128)(2,1)S(1)} %join_own.1.own), channel_id=1, source_target_pairs={{0,1},{1,2},{2,3},{3,4},{4,5},{5,6},{6,7},{7,8},{8,9},{9,10},{10,1... | collective-permute-start | bytes 786440 | tf_op jit(solution)/shard_map/ppermute | solution.py:19
  10.5 0.5 %collective-permute-start.5 = (bf16[11,64,128]{2,1,0:T(8,128)(2,1)S(1)}, bf16[11,64,128]{2,1,0:T(8,128)(2,1)S(1)}, u32[]{:S(2)}, u32[]{:S(2)}) collective-permute-start(bf16[11,64,128]{2,1,0:T(8,128)(2,1)S(1)} %get-tuple-element.54), channel_id=1, source_target_pairs={{0,16},{16,0},{1,17},{17,1},{2,18},{18,2},{3,19},{19,3},{4,20},{20... | collective-permute-start | bytes 540680 | tf_op jit(solution)/shard_map/ppermute | solution.py:24
  11.1 0.4 %collective-permute-start.4 = (bf16[10,64,128]{2,1,0:T(8,128)(2,1)S(1)}, bf16[10,64,128]{2,1,0:T(8,128)(2,1)S(1)}, u32[]{:S(2)}, u32[]{:S(2)}) collective-permute-start(bf16[10,64,128]{2,1,0:T(8,128)(2,1)S(1)} %get-tuple-element.53), channel_id=1, source_target_pairs={{0,16},{16,0},{1,17},{17,1},{2,18},{18,2},{3,19},{19,3},{4,20},{20... | collective-permute-start | bytes 491528 | tf_op jit(solution)/shard_map/ppermute | solution.py:24
  12.2 0.5 %collective-permute-done.4.first_third = bf16[10,64,128]{2,1,0:T(8,128)(2,1)S(1)} collective-permute-done((bf16[10,64,128]{2,1,0:T(8,128)(2,1)S(1)}, bf16[10,64,128]{2,1,0:T(8,128)(2,1)S(1)}, u32[]{:S(2)}, u32[]{:S(2)}) %collective-permute-start.4) | collective-permute-done | bytes 163872 | tf_op jit(solution)/shard_map/ppermute | solution.py:24
  12.7 1.5 %own_block.1 = (bf16[16,128,128]{2,1,0:T(8,128)(2,1)S(1)}, bf16[16,128,128]{2,1,0:T(8,128)(2,1)S(1)}, bf16[8,128,256]{2,1,0:T(8,128)(2,1)S(1)}, s32[8,1,256]{2,1...) custom-call(s32[32]{0:T(128)S(1)} %copy-done.2, ...), custom_call_target="tpu_custom_call" | custom-call | flops 1 | tf_op jit(solution)/shard_map/own_block/pallas_call | solution.py:393
  14.8 0.7 %collective-permute-done.7.two_keys = bf16[4,64,128]{2,1,0:T(8,128)(2,1)S(1)} collective-permute-done((bf16[4,64,128]{2,1,0:T(8,128)(2,1)S(1)}, bf16[4,64,128]{2,1,0:T(8,128)(2,1)S(1)}, u32[]{:S(2)}, u32[]{:S(2)}) %collective-permute-start.7) | collective-permute-done | bytes 65568 | tf_op jit(solution)/shard_map/ppermute | solution.py:24
  15.8 0.9 %near_forward.1 = (f32[8,1,256]{2,1,0:T(1,128)S(1)}, f32[8,1,256]{2,1,0:T(1,128)S(1)}, f32[8,128,256]{2,1,0:T(8,128)S(1)}, f32[8,128,256]{2,1,0:T(8,128)S(1)}, f...) custom-call(s32[8,1,256]{2,1,0:T(1,128)S(1)} %get-tuple-element.57.first, ...), custom_call_target="tpu_custom_call" | custom-call | flops 1 | tf_op jit(solution)/shard_map/near_forward/pallas_call | solution.py:393
  17.0 1.6 %last_forward_backward.1 = (bf16[8,128,256]{2,1,0:T(8,128)(2,1)S(1)}, f32[8,1,256]{2,1,0:T(1,128)S(1)}, f32[8,1,256]{2,1,0:T(1,128)S(1)}, bf16[8,128,256]{2,1,0:T(8,128)(2,1)S(1)}, bf16[2,4,128,128]{3,2,1,0:T(8,128)(2,1)S(1)}) custom-call(s32[8,1,256]{2,1,0:T(1,128)S(1)} %get-tuple-element.57.first, bf16[16,128,128]{2,1,0:T(8,128)(2,1)S(1)} %get-tuple-element.58.query_head, ...), custom_call_target="tpu_custom_call" | custom-call | flops 1 | tf_op jit(solution)/shard_map/last_forward_backward/pallas_call | solution.py:393
  18.6 1.0 %collective-permute-start.9 = (bf16[2,4,128,128]{3,2,1,0:T(8,128)(2,1)S(1)}, bf16[2,4,128,128]{3,2,1,0:T(8,128)(2,1)S(1)}, u32[]{:S(2)}, u32[]{:S(2)}) collective-permute-start(bf16[2,4,128,128]{3,2,1,0:T(8,128)(2,1)S(1)} %get-tuple-element.82.one_part), channel_id=1, source_target_pairs={{0,16},{16,0},{1,17},{17,1},{2,18},{18,2},{3,19},{19,3},{4,20},{20... | collective-permute-start | bytes 786440 | tf_op jit(solution)/shard_map/ppermute | solution.py:24
  19.6 0.5 %two_backward.1 = (bf16[8,128,256]{2,1,0:T(8,128)(2,1)S(1)}, bf16[2,4,128,128]{3,2,1,0:T(8,128)(2,1)S(1)}) custom-call(bf16[16,128,128]{2,1,0:T(8,128)(2,1)S(1)} %get-tuple-element.58.query_head, bf16[16,128,128]{2,1,0:T(8,128)(2,1)S(1)} %get-tuple-element.59.grad_head, f32[8,128,256]{2,1,0:T(8,128)S(1)} %get-tuple-element.73.near_weights, ...), custom_call_target="tpu_custom_call" | custom-call | flops 1 | tf_op jit(solution)/shard_map/two_backward/pallas_call | solution.py:393
  20.1 1.3 %collective-permute-start.13 = (bf16[2,4,128,128]{3,2,1,0:T(8,128)(2,1)S(1)}, bf16[2,4,128,128]{3,2,1,0:T(8,128)(2,1)S(1)}, u32[]{:S(2)}, u32[]{:S(2)}) collective-permute-start(bf16[2,4,128,128]{3,2,1,0:T(8,128)(2,1)S(1)} %get-tuple-element.92), channel_id=1, source_target_pairs={{2,0},{3,1},{4,2},{5,3},{6,4},{7,5},{8,6},{9,7},{10,8},{11,9},{12,... | collective-permute-start | bytes 786440 | tf_op jit(solution)/shard_map/ppermute | solution.py:19
  21.5 1.9 %collective-permute-start.15 = (bf16[2,8,64,128]{3,2,1,0:T(8,128)(2,1)S(1)}, bf16[2,8,64,128]{3,2,1,0:T(8,128)(2,1)S(1)}, u32[]{:S(2)}, u32[]{:S(2)}) collective-permute-start(bf16[2,8,64,128]{3,2,1,0:T(8,128)(2,1)S(1)} %join_one.1.after), channel_id=1, source_target_pairs={{1,0},{2,1},{3,2},{4,3},{5,4},{6,5},{7,6},{8,7},{9,8},{10,9},{11,1... | collective-permute-start | bytes 786440 | tf_op jit(solution)/shard_map/ppermute | solution.py:19
  23.4 0.5 %own_backward.1 = (bf16[8,128,256]{2,1,0:T(8,128)(2,1)S(1)}, f32[2,4,128,128]{3,2,1,0:T(8,128)S(1)}) custom-call(bf16[16,128,128]{2,1,0:T(8,128)(2,1)S(1)} %get-tuple-element.58.query_head, bf16[16,128,128]{2,1,0:T(8,128)(2,1)S(1)} %get-tuple-element.59.grad_head, f32[8,128,256]{2,1,0:T(8,128)S(1)} %get-tuple-element.79.own_weights, ...), custom_call_target="tpu_custom_call" | custom-call | flops 1 | tf_op jit(solution)/shard_map/own_backward/pallas_call | solution.py:393
  23.9 0.8 %query_grad.1 = (bf16[16,64,128]{2,1,0:T(8,128)(2,1)S(1)}, bf16[16,64,128]{2,1,0:T(8,128)(2,1)S(1)}, bf16[10,64,128]{2,1,0:T(8,128)(2,1)S(1)}, bf16[11,64,128]{2,1,0:T(8,128)(2,1)S(1)}, bf16[11,64,128]{2,1,0:T(8,128)(2,1)S(1)}) custom-call(bf16[2,4,128,128]{3,2,1,0:T(8,128)(2,1)S(1)} %join_own.1.own, ...), custom_call_target="tpu_custom_call" | custom-call | flops 1 | tf_op jit(solution)/shard_map/query_grad/pallas_call | solution.py:393
  24.7 0.5 %collective-permute-start.12 = (bf16[11,64,128]{2,1,0:T(8,128)(2,1)S(1)}, bf16[11,64,128]{2,1,0:T(8,128)(2,1)S(1)}, u32[]{:S(2)}, u32[]{:S(2)}) collective-permute-start(bf16[11,64,128]{2,1,0:T(8,128)(2,1)S(1)} %get-tuple-element.88), channel_id=1, source_target_pairs={{0,16},{16,0},{1,17},{17,1},{2,18},{18,2},{3,19},{19,3},{4,20},{20... | collective-permute-start | bytes 540680 | tf_op jit(solution)/shard_map/ppermute | solution.py:24
  25.3 10.3 %collective-permute-done.13.two_total = bf16[2,4,128,128]{3,2,1,0:T(8,128)(2,1)S(1)} collective-permute-done((bf16[2,4,128,128]{3,2,1,0:T(8,128)(2,1)S(1)}, bf16[2,4,128,128]{3,2,1,0:T(8,128)(2,1)S(1)}, u32[]{:S(2)}, u32[]{:S(2)}) %collective-permute-start.13) | collective-permute-done | bytes 262176 | tf_op jit(solution)/shard_map/ppermute | solution.py:19
  35.6 0.9 %collective-permute-start.14 = (bf16[2,4,64,128]{3,2,1,0:T(8,128)(2,1)S(1)}, bf16[2,4,64,128]{3,2,1,0:T(8,128)(2,1)S(1)}, u32[]{:S(2)}, u32[]{:S(2)}) collective-permute-start(bf16[2,4,64,128]{3,2,1,0:T(8,128)(2,1)S(1)} %get-tuple-element.94), channel_id=1, source_target_pairs={{0,16},{16,0},{1,17},{17,1},{2,18},{18,2},{3,19},{19,3},{4,20},{20... | collective-permute-start | bytes 393224 | tf_op jit(solution)/shard_map/ppermute | solution.py:24
  36.5 1.0 %assemble.1 = (bf16[32,64,128]{2,1,0:T(8,128)(2,1)}, bf16[32,64,128]{2,1,0:T(8,128)(2,1)}, f32[8,128]{1,0:T(8,128)S(1)}) custom-call(bf16[16,64,128]{2,1,0:T(8,128)(2,1)S(1)} %get-tuple-element.84.out_mine, bf16[16,64,128]{2,1,0:T(8,128)(2,1)S(1)} %get-tuple-element.85.query_mine, bf16[10,64,128]{2,1,0:T(8,128)(2,1)S(1)} %collective-permute-done.10.first_third, ...), custom_call_target="tpu_custom_call" | custom-call | flops 1 | tf_op jit(solution)/shard_map/assemble/pallas_call | solution.py:393
  37.6 0.7 %total.1 = (bf16[8,64,128]{2,1,0:T(8,128)(2,1)}, bf16[8,64,128]{2,1,0:T(8,128)(2,1)}) custom-call(f32[2,4,64,128]{3,2,1,0:T(8,128)S(1)} %get-tuple-element.93.sum_mine, bf16[2,4,64,128]{3,2,1,0:T(8,128)(2,1)S(1)} %collective-permute-done.14.sum_other, bf16[2,8,64,128]{3,2,1,0:T(8,128)(2,1)S(1)} %collective-permute-done.15.one_total, ...), custom_call_target="tpu_custom_call" | custom-call | flops 1 | tf_op jit(solution)/shard_map/total/pallas_call | solution.py:393
  (29 shorter events, 1.6 us)
Async XLA Ops:
  0.6 9.8 %copy-start.1 = (bf16[32,64,128]{2,1,0:T(8,128)(2,1)S(1)}, bf16[32,64,128]{2,1,0:T(8,128)(2,1)}, u32[]{:S(2)}) copy-start(bf16[32,64,128]{2,1,0:T(8,128)(2,1)} %grads.3) | copy-start | bytes 1572868
  1.7 8.8 %copy-start = (bf16[32,64,128]{2,1,0:T(8,128)(2,1)S(1)}, bf16[32,64,128]{2,1,0:T(8,128)(2,1)}, u32[]{:S(2)}) copy-start(bf16[32,64,128]{2,1,0:T(8,128)(2,1)} %queries.3) | copy-start | bytes 1572868
  1.7 12.5 %collective-permute-start.3 = (bf16[2,8,64,128]{3,2,1,0:T(8,128)(2,1)S(1)}, bf16[2,8,64,128]{3,2,1,0:T(8,128)(2,1)S(1)}, u32[]{:S(2)}, u32[]{:S(2)}) collective-permute-start(bf16[2,8,64,128]{3,2,1,0:T(8,128)(2,1)S(1)} %pad_maximum_fusion.block.own.after), channel_id=1, source_target_pairs={{0,2},{1,3},{2,4},{3,5},{4,6},{5,7},{6,8},{7,9},{8,10},{9,11},{10,... | collective-permute-start | bytes 786440 | tf_op jit(solution)/shard_map/ppermute | solution.py:19
  5.0 1.9 %collective-permute-start = (bf16[4,64,128]{2,1,0:T(8,128)(2,1)S(1)}, bf16[4,64,128]{2,1,0:T(8,128)(2,1)S(1)}, u32[]{:S(2)}, u32[]{:S(2)}) collective-permute-start(bf16[4,64,128]{2,1,0:T(8,128)(2,1)S(1)} %get-tuple-element.51), channel_id=1, source_target_pairs={{0,16},{16,0},{1,17},{17,1},{2,18},{18,2},{3,19},{19,3},{4,20},{20... | collective-permute-start | bytes 196616 | tf_op jit(solution)/shard_map/ppermute | solution.py:24
  6.1 1.3 %collective-permute-start.1 = (bf16[4,64,128]{2,1,0:T(8,128)(2,1)S(1)}, bf16[4,64,128]{2,1,0:T(8,128)(2,1)S(1)}, u32[]{:S(2)}, u32[]{:S(2)}) collective-permute-start(bf16[4,64,128]{2,1,0:T(8,128)(2,1)S(1)} %get-tuple-element.52), channel_id=1, source_target_pairs={{0,16},{16,0},{1,17},{17,1},{2,18},{18,2},{3,19},{19,3},{4,20},{20... | collective-permute-start | bytes 196616 | tf_op jit(solution)/shard_map/ppermute | solution.py:24
  7.3 9.7 %collective-permute-start.2 = (bf16[2,4,128,128]{3,2,1,0:T(8,128)(2,1)S(1)}, bf16[2,4,128,128]{3,2,1,0:T(8,128)(2,1)S(1)}, u32[]{:S(2)}, u32[]{:S(2)}) collective-permute-start(bf16[2,4,128,128]{3,2,1,0:T(8,128)(2,1)S(1)} %join_own.1.own), channel_id=1, source_target_pairs={{0,1},{1,2},{2,3},{3,4},{4,5},{5,6},{6,7},{7,8},{8,9},{9,10},{10,1... | collective-permute-start | bytes 786440 | tf_op jit(solution)/shard_map/ppermute | solution.py:19
  10.5 2.2 %collective-permute-start.5 = (bf16[11,64,128]{2,1,0:T(8,128)(2,1)S(1)}, bf16[11,64,128]{2,1,0:T(8,128)(2,1)S(1)}, u32[]{:S(2)}, u32[]{:S(2)}) collective-permute-start(bf16[11,64,128]{2,1,0:T(8,128)(2,1)S(1)} %get-tuple-element.54), channel_id=1, source_target_pairs={{0,16},{16,0},{1,17},{17,1},{2,18},{18,2},{3,19},{19,3},{4,20},{20... | collective-permute-start | bytes 540680 | tf_op jit(solution)/shard_map/ppermute | solution.py:24
  11.0 1.7 %collective-permute-start.6 = (bf16[11,64,128]{2,1,0:T(8,128)(2,1)S(1)}, bf16[11,64,128]{2,1,0:T(8,128)(2,1)S(1)}, u32[]{:S(2)}, u32[]{:S(2)}) collective-permute-start(bf16[11,64,128]{2,1,0:T(8,128)(2,1)S(1)} %get-tuple-element.55), channel_id=1, source_target_pairs={{0,16},{16,0},{1,17},{17,1},{2,18},{18,2},{3,19},{19,3},{4,20},{20... | collective-permute-start | bytes 540680 | tf_op jit(solution)/shard_map/ppermute | solution.py:24
  11.1 1.6 %copy-start.2 = (s32[32]{0:T(128)S(1)}, s32[32]{0:T(128)}, u32[]{:S(2)}) copy-start(s32[32]{0:T(128)} %spans.1) | copy-start | bytes 388
  11.1 1.6 %collective-permute-start.4 = (bf16[10,64,128]{2,1,0:T(8,128)(2,1)S(1)}, bf16[10,64,128]{2,1,0:T(8,128)(2,1)S(1)}, u32[]{:S(2)}, u32[]{:S(2)}) collective-permute-start(bf16[10,64,128]{2,1,0:T(8,128)(2,1)S(1)} %get-tuple-element.53), channel_id=1, source_target_pairs={{0,16},{16,0},{1,17},{17,1},{2,18},{18,2},{3,19},{19,3},{4,20},{20... | collective-permute-start | bytes 491528 | tf_op jit(solution)/shard_map/ppermute | solution.py:24
  14.3 1.3 %collective-permute-start.7 = (bf16[4,64,128]{2,1,0:T(8,128)(2,1)S(1)}, bf16[4,64,128]{2,1,0:T(8,128)(2,1)S(1)}, u32[]{:S(2)}, u32[]{:S(2)}) collective-permute-start(bf16[4,64,128]{2,1,0:T(8,128)(2,1)S(1)} %get-tuple-element.61), channel_id=1, source_target_pairs={{0,16},{16,0},{1,17},{17,1},{2,18},{18,2},{3,19},{19,3},{4,20},{20... | collective-permute-start | bytes 196616 | tf_op jit(solution)/shard_map/ppermute | solution.py:24
  14.6 1.3 %collective-permute-start.8 = (bf16[4,64,128]{2,1,0:T(8,128)(2,1)S(1)}, bf16[4,64,128]{2,1,0:T(8,128)(2,1)S(1)}, u32[]{:S(2)}, u32[]{:S(2)}) collective-permute-start(bf16[4,64,128]{2,1,0:T(8,128)(2,1)S(1)} %get-tuple-element.62), channel_id=1, source_target_pairs={{0,16},{16,0},{1,17},{17,1},{2,18},{18,2},{3,19},{19,3},{4,20},{20... | collective-permute-start | bytes 196616 | tf_op jit(solution)/shard_map/ppermute | solution.py:24
  18.6 2.8 %collective-permute-start.9 = (bf16[2,4,128,128]{3,2,1,0:T(8,128)(2,1)S(1)}, bf16[2,4,128,128]{3,2,1,0:T(8,128)(2,1)S(1)}, u32[]{:S(2)}, u32[]{:S(2)}) collective-permute-start(bf16[2,4,128,128]{3,2,1,0:T(8,128)(2,1)S(1)} %get-tuple-element.82.one_part), channel_id=1, source_target_pairs={{0,16},{16,0},{1,17},{17,1},{2,18},{18,2},{3,19},{19,3},{4,20},{20... | collective-permute-start | bytes 786440 | tf_op jit(solution)/shard_map/ppermute | solution.py:24
  20.1 15.4 %collective-permute-start.13 = (bf16[2,4,128,128]{3,2,1,0:T(8,128)(2,1)S(1)}, bf16[2,4,128,128]{3,2,1,0:T(8,128)(2,1)S(1)}, u32[]{:S(2)}, u32[]{:S(2)}) collective-permute-start(bf16[2,4,128,128]{3,2,1,0:T(8,128)(2,1)S(1)} %get-tuple-element.92), channel_id=1, source_target_pairs={{2,0},{3,1},{4,2},{5,3},{6,4},{7,5},{8,6},{9,7},{10,8},{11,9},{12,... | collective-permute-start | bytes 786440 | tf_op jit(solution)/shard_map/ppermute | solution.py:19
  21.5 16.1 %collective-permute-start.15 = (bf16[2,8,64,128]{3,2,1,0:T(8,128)(2,1)S(1)}, bf16[2,8,64,128]{3,2,1,0:T(8,128)(2,1)S(1)}, u32[]{:S(2)}, u32[]{:S(2)}) collective-permute-start(bf16[2,8,64,128]{3,2,1,0:T(8,128)(2,1)S(1)} %join_one.1.after), channel_id=1, source_target_pairs={{1,0},{2,1},{3,2},{4,3},{5,4},{6,5},{7,6},{8,7},{9,8},{10,9},{11,1... | collective-permute-start | bytes 786440 | tf_op jit(solution)/shard_map/ppermute | solution.py:19
  24.6 11.9 %collective-permute-start.11 = (bf16[11,64,128]{2,1,0:T(8,128)(2,1)S(1)}, bf16[11,64,128]{2,1,0:T(8,128)(2,1)S(1)}, u32[]{:S(2)}, u32[]{:S(2)}) collective-permute-start(bf16[11,64,128]{2,1,0:T(8,128)(2,1)S(1)} %get-tuple-element.87), channel_id=1, source_target_pairs={{0,16},{16,0},{1,17},{17,1},{2,18},{18,2},{3,19},{19,3},{4,20},{20... | collective-permute-start | bytes 540680 | tf_op jit(solution)/shard_map/ppermute | solution.py:24
  24.7 11.8 %collective-permute-start.12 = (bf16[11,64,128]{2,1,0:T(8,128)(2,1)S(1)}, bf16[11,64,128]{2,1,0:T(8,128)(2,1)S(1)}, u32[]{:S(2)}, u32[]{:S(2)}) collective-permute-start(bf16[11,64,128]{2,1,0:T(8,128)(2,1)S(1)} %get-tuple-element.88), channel_id=1, source_target_pairs={{0,16},{16,0},{1,17},{17,1},{2,18},{18,2},{3,19},{19,3},{4,20},{20... | collective-permute-start | bytes 540680 | tf_op jit(solution)/shard_map/ppermute | solution.py:24
  25.2 11.3 %collective-permute-start.10 = (bf16[10,64,128]{2,1,0:T(8,128)(2,1)S(1)}, bf16[10,64,128]{2,1,0:T(8,128)(2,1)S(1)}, u32[]{:S(2)}, u32[]{:S(2)}) collective-permute-start(bf16[10,64,128]{2,1,0:T(8,128)(2,1)S(1)} %get-tuple-element.86), channel_id=1, source_target_pairs={{0,16},{16,0},{1,17},{17,1},{2,18},{18,2},{3,19},{19,3},{4,20},{20... | collective-permute-start | bytes 491528 | tf_op jit(solution)/shard_map/ppermute | solution.py:24
  35.6 1.9 %collective-permute-start.14 = (bf16[2,4,64,128]{3,2,1,0:T(8,128)(2,1)S(1)}, bf16[2,4,64,128]{3,2,1,0:T(8,128)(2,1)S(1)}, u32[]{:S(2)}, u32[]{:S(2)}) collective-permute-start(bf16[2,4,64,128]{3,2,1,0:T(8,128)(2,1)S(1)} %get-tuple-element.94), channel_id=1, source_target_pairs={{0,16},{16,0},{1,17},{17,1},{2,18},{18,2},{3,19},{19,3},{4,20},{20... | collective-permute-start | bytes 393224 | tf_op jit(solution)/shard_map/ppermute | solution.py:24

commit v9 on v7

--- a/solution.py
+++ b/solution.py
@@ -94,29 +94,6 @@
         send[...] = block[index, other_heads(send.shape[0])]
 
 
-def thirds(rows):
-    return [2 * rows * (i + 1) // 3 - 2 * rows * i // 3 for i in range(3)]
-
-
-def placed(pieces, rows):
-    taken = 0
-    for piece in pieces:
-        count = piece.shape[0]
-        for index in range(2):
-            low = max(taken, index * rows)
-            high = min(taken + count, (index + 1) * rows)
-            if low < high:
-                yield index, low - index * rows, piece.at[pl.ds(low - taken, high - low)], high - low
-        taken += count
-
-
-def split_rows_kernel(queries, grads, after, *sends):
-    heads = queries.shape[0] // 2
-    start = (1 - lax.axis_index("head")) * heads
-    for index, row, piece, count in placed(sends, heads):
-        piece[...] = (queries, grads)[index][pl.ds(start + row, count)]
-
-
 def join_own_kernel(own, other_keys, other_values, own_head):
     groups, length = other_keys.shape[:2]
     own_head[:, :, pl.ds(0, length)] = own[:, my_heads(groups)]
@@ -125,7 +102,7 @@
 
 
 def own_kernel(
-    spans, offset, queries, grads, first_third, second_third, last_third, own,
+    spans, offset, queries, grads, queries_other, grads_other, own,
     query_head, grad_head, grad_rows, first, own_max, own_total, own_out, own_weights,
     own_prob_grad,
 ):
@@ -134,10 +111,11 @@
     groups = own.shape[1]
     chunks = first.shape[0]
     count = heads // chunks
-    query_head[:, pl.ds(0, length)] = queries[my_heads(heads)]
-    grad_head[:, pl.ds(0, length)] = grads[my_heads(heads)]
-    for index, row, piece, rows in placed((first_third, second_third, last_third), heads):
-        (query_head, grad_head)[index][pl.ds(row, rows), pl.ds(length, length)] = piece[...]
+    mine = my_heads(heads)
+    query_head[:, pl.ds(0, length)] = queries[mine]
+    query_head[:, pl.ds(length, length)] = queries_other[mine]
+    grad_head[:, pl.ds(0, length)] = grads[mine]
+    grad_head[:, pl.ds(length, length)] = grads_other[mine]
     factor = width ** (-0.5) * math.log2(math.e)
     token = lane_tokens(count, length)
     for n, rows in enumerate(first_visible(spans, offset, chunks, count, length)):
@@ -303,7 +281,7 @@
 
 def own_backward_kernel(
     query_head, grad_head, own_weights, own_prob_grad, near_factor, own_factor, row_delta,
-    after, own_grad, own_part,
+    own_grad, own_part,
 ):
     chunks = own_weights.shape[0]
     groups, _, width = own_part.shape[1:]
@@ -320,7 +298,7 @@
         accumulate(n, score_grad, prob.astype(jnp.bfloat16), store)
 
 
-def join_one_kernel(one_mine, other_keys, other_values, one_part):
+def join_one_kernel(one_mine, other_keys, other_values, after, one_part):
     groups = one_mine.shape[1]
     one_part[:, my_heads(groups)] = one_mine[...]
     one_part[0, other_heads(groups)] = other_keys[...]
@@ -329,9 +307,8 @@
 
 def query_kernel(
     own, back_one, one_keys, back_two, attended_rows, far_grad, one_grad, own_grad,
-    out_mine, query_mine, first_third, second_third, last_third, query_send,
-):
-    sends = (first_third, second_third, last_third)
+    out_mine, query_mine, out_send, query_send,
+):
     groups = own.shape[1]
     chunks = far_grad.shape[0]
     heads, length, width = out_mine.shape
@@ -342,23 +319,22 @@
         keys = join(back_two[0, g], one_back(back_one, (one_keys,), 0, g), own[0, g])
         part = matmul(keys, join(far_grad[n], one_grad[n], own_grad[n]), (0, 0))
         part = (part * width ** (-0.5)).astype(jnp.bfloat16)
-        for index, (columns, mine) in enumerate(((attended_rows[n], out_mine), (part, query_mine))):
+        for columns, mine, send in (
+            (attended_rows[n], out_mine, out_send), (part, query_mine, query_send),
+        ):
             block = columns.T.reshape(count, 2 * length, width)
             mine[rows] = block[:, :length]
-            query_send[index, rows] = block[:, length:]
-    for index, row, piece, taken in placed(sends, heads):
-        piece[...] = query_send[index, pl.ds(row, taken)]
+            send[rows] = block[:, length:]
 
 
 def assemble_kernel(
-    out_mine, query_mine, first_third, second_third, last_third, out, query_grad, token
-):
-    heads = out_mine.shape[0]
-    start = (1 - lax.axis_index("head")) * heads
-    out[my_heads(heads)] = out_mine[...]
-    query_grad[my_heads(heads)] = query_mine[...]
-    for index, row, piece, count in placed((first_third, second_third, last_third), heads):
-        (out, query_grad)[index][pl.ds(start + row, count)] = piece[...]
+    out_mine, query_mine, out_other, query_other, out, query_grad, token
+):
+    mine, other = my_heads(out_mine.shape[0]), other_heads(out_mine.shape[0])
+    out[mine] = out_mine[...]
+    out[other] = out_other[...]
+    query_grad[mine] = query_mine[...]
+    query_grad[other] = query_other[...]
     token[...] = jnp.zeros(token.shape, token.dtype)
 
 
@@ -413,7 +389,6 @@
     half_pair = ((2, groups_here, length, width), half)
     chip_pair = ((2, groups_here, tokens, width), half)
     half_rows = ((heads_here, length, width), half)
-    third_rows = [((rows, length, width), half) for rows in thirds(heads_here)]
     chip_rows = ((heads_here, tokens, width), half)
 
     own = jnp.stack([key_matrix, value_matrix])
@@ -423,12 +398,6 @@
         join_own_kernel, "join_own", [chip_pair], (own, *[swapped(send, "head") for send in own_sends])
     )
     back_two = shifted(own_head, "seq", 2)
-    sends = call(
-        split_rows_kernel,
-        "split_rows",
-        third_rows,
-        (query_matrix, output_gradient, own),
-    )
     (
         query_head, grad_head, grad_rows, first, own_max, own_total, own_out, own_weights,
         own_prob_grad,
@@ -441,7 +410,7 @@
         ],
         (
             query_head_spans, slab_offset, query_matrix, output_gradient,
-            *[swapped(send, "head") for send in sends], own_head,
+            swapped(query_matrix, "head"), swapped(output_gradient, "head"), own_head,
         ),
         scalars=2,
     )
@@ -468,34 +437,33 @@
         [rows_of(tokens, half), half_pair, half_block, half_block],
         (query_head, grad_head, near_weights, near_prob_grad, near_factor, row_delta),
     )
-    (one_part,) = call(
-        join_one_kernel,
-        "join_one",
-        [whole_pair],
-        (part_mine, *[swapped(send, "head") for send in part_sends]),
-    )
-    one_total = shifted(one_part, "seq", -1)
+    one_arrived = [swapped(send, "head") for send in part_sends]
     own_grad, own_part = call(
         own_backward_kernel,
         "own_backward",
         [rows_of(tokens, half), (chip_pair[0], full)],
         (
             query_head, grad_head, own_weights, own_prob_grad, near_factor, own_factor, row_delta,
-            one_part,
         ),
     )
-    out_mine, query_mine, *sends = call(
+    out_mine, query_mine, out_send, query_send = call(
         query_kernel,
         "query_grad",
-        [half_rows] * 2 + third_rows,
+        [half_rows] * 4,
         (own_head, back_one, one_other[0], back_two, attended_rows, far_grad, one_grad, own_grad),
-        scratch=[pltpu.VMEM((2,) + half_rows[0], half)],
-    )
+    )
+    (one_part,) = call(
+        join_one_kernel,
+        "join_one",
+        [whole_pair],
+        (part_mine, *one_arrived, query_send),
+    )
+    one_total = shifted(one_part, "seq", -1)
     attn_out, query_grad, token = call(
         assemble_kernel,
         "assemble",
         [(query_matrix.shape, half)] * 2 + [((8, 128), full)],
-        (out_mine, query_mine, *[swapped(send, "head") for send in sends]),
+        (out_mine, query_mine, swapped(out_send, "head"), swapped(query_send, "head")),
     )
     sum_mine, sum_send = call(
         own_sum_kernel, "own_sum", [(half_pair[0], full), half_pair], (own_part, far_total)

time: 37.6 us -> 38.9 us (1.035)
  waiting for transfers between devices: 9.75 us -> 11.6 us
  starting transfers between devices: 17.3 us -> 16.9 us
    ppermute x4, waiting for transfers between devices: 5.52 us -> 9.73 us  [shifted(): return lax.ppermute(block, axis, route)]
    ppermute x13 -> x11, waiting for transfers between devices: 4.24 us -> 1.82 us  [swapped(): return lax.ppermute(block, axis, [(i, count - 1 - i) for i in range(count)])]
    ppermute x13 -> x11, starting transfers between devices: 3.52 us -> 2.93 us  [swapped(): return lax.ppermute(block, axis, [(i, count - 1 - i) for i in range(count)])]
    pallas_call x14 -> x13, Pallas kernels: 7.76 us -> 7.64 us  [call(): pl.pallas_call(kernel, out_shape=tuple((jax.ShapeDtypeStruct(shape, kind)...]
  transfers between devices with their start and end apart: 17 -> 15, of which waited for: 10 -> 7; matrix products, arithmetic and copies ran while one was open for 0% -> 3% of each run, Pallas kernels for 15% -> 14%
where the time goes in v9:
time: 38.9 us; the launch traced here: 38.7 us
  starting transfers between devices  16.9 us (43%)
  waiting for transfers between devices  11.6 us (30%)
  Pallas kernels  7.64 us (20%)
  between operations  1.5 us (4%)
  other arithmetic  1.05 us (3%)
    ppermute x4, starting transfers between devices, shifted(): return lax.ppermute(block, axis, route)  14 us
    ppermute x4, waiting for transfers between devices, shifted(): return lax.ppermute(block, axis, route)  9.73 us
    pallas_call x13, Pallas kernels, call(): pl.pallas_call(kernel, out_shape=tuple((jax.ShapeDtypeStruct(shape, kind)...  7.64 us
    ppermute x11, starting transfers between devices, swapped(): return lax.ppermute(block, axis, [(i, count - 1 - i) for i in range(count)])  2.93 us
    ppermute x11, waiting for transfers between devices, swapped(): return lax.ppermute(block, axis, [(i, count - 1 - i) for i in range(count)])  1.82 us
    another operation x1, other arithmetic, shards(): own = jnp.stack([key_matrix, value_matrix])  1.05 us
  transfers between devices with their start and end apart: 15, of which 7 were waited for; matrix products, arithmetic and copies ran while one was open for 3% of the time, Pallas kernels for 14%

profile of v9, /device:TPU:14, one launch (start us, length us, event | category | flops | bytes accessed | tf_op | source)
XLA Modules:
  0.0 38.7 jit_solution(3973767469969477291)
XLA Ops:
  0.7 0.5 %collective-permute-start.4 = (bf16[32,64,128]{2,1,0:T(8,128)(2,1)}, bf16[32,64,128]{2,1,0:T(8,128)(2,1)S(1)}, u32[]{:S(2)}, u32[]{:S(2)}) collective-permute-start(bf16[32,64,128]{2,1,0:T(8,128)(2,1)} %grads.1), channel_id=1, source_target_pairs={{0,16},{16,0},{1,17},{17,1},{2,18},{18,2},{3,19},{19,3},{4,20},{20... | collective-permute-start | bytes 1572872 | tf_op jit(solution)/shard_map/ppermute | solution.py:24
  1.2 1.1 %pad_maximum_fusion.block.own = bf16[2,8,64,128]{3,2,1,0:T(8,128)(2,1)S(1)} fusion(bf16[1,8,64,128]{3,2,1,0:T(8,128)(2,1)} %bitcast.2, bf16[1,8,64,128]{3,2,1,0:T(8,128)(2,1)} %bitcast.3), kind=kLoop, calls=%fused_computation | loop fusion | flops 131072 | bytes 524288 | tf_op jit(solution)/shard_map/stack | solution.py:394
  2.3 3.5 %collective-permute-start.2 = (bf16[2,8,64,128]{3,2,1,0:T(8,128)(2,1)S(1)}, bf16[2,8,64,128]{3,2,1,0:T(8,128)(2,1)S(1)}, u32[]{:S(2)}, u32[]{:S(2)}) collective-permute-start(bf16[2,8,64,128]{3,2,1,0:T(8,128)(2,1)S(1)} %pad_maximum_fusion.block.own), channel_id=1, source_target_pairs={{0,1},{1,2},{2,3},{3,4},{4,5},{5,6},{6,7},{7,8},{8,9},{9,10},{10,1... | collective-permute-start | bytes 786440 | tf_op jit(solution)/shard_map/ppermute | solution.py:19
  5.9 0.5 %collective-permute-start.1 = (bf16[4,64,128]{2,1,0:T(8,128)(2,1)S(1)}, bf16[4,64,128]{2,1,0:T(8,128)(2,1)S(1)}, u32[]{:S(2)}, u32[]{:S(2)}) collective-permute-start(bf16[4,64,128]{2,1,0:T(8,128)(2,1)S(1)} %get-tuple-element.50), channel_id=1, source_target_pairs={{0,16},{16,0},{1,17},{17,1},{2,18},{18,2},{3,19},{19,3},{4,20},{20... | collective-permute-start | bytes 196616 | tf_op jit(solution)/shard_map/ppermute | solution.py:24
  6.4 0.7 %collective-permute-done.other_keys = bf16[4,64,128]{2,1,0:T(8,128)(2,1)S(1)} collective-permute-done((bf16[4,64,128]{2,1,0:T(8,128)(2,1)S(1)}, bf16[4,64,128]{2,1,0:T(8,128)(2,1)S(1)}, u32[]{:S(2)}, u32[]{:S(2)}) %collective-permute-start) | collective-permute-done | bytes 65568 | tf_op jit(solution)/shard_map/ppermute | solution.py:24
  7.2 0.2 collective-permute-done.1.other_values
  7.4 3.4 %collective-permute-start.6 = (bf16[2,4,128,128]{3,2,1,0:T(8,128)(2,1)S(1)}, bf16[2,4,128,128]{3,2,1,0:T(8,128)(2,1)S(1)}, u32[]{:S(2)}, u32[]{:S(2)}) collective-permute-start(bf16[2,4,128,128]{3,2,1,0:T(8,128)(2,1)S(1)} %join_own.1.own), channel_id=1, source_target_pairs={{0,2},{1,3},{2,4},{3,5},{4,6},{5,7},{6,8},{7,9},{8,10},{9,11},{10,... | collective-permute-start | bytes 786440 | tf_op jit(solution)/shard_map/ppermute | solution.py:19
  11.5 1.5 %own_block.1 = (bf16[16,128,128]{2,1,0:T(8,128)(2,1)S(1)}, bf16[16,128,128]{2,1,0:T(8,128)(2,1)S(1)}, bf16[8,128,256]{2,1,0:T(8,128)(2,1)S(1)}, s32[8,1,256]{2,1...) custom-call(s32[32]{0:T(128)S(1)} %copy-done.2, ...), custom_call_target="tpu_custom_call" | custom-call | flops 1 | tf_op jit(solution)/shard_map/own_block/pallas_call | solution.py:372
  13.2 0.4 %collective-permute-start.7 = (bf16[4,64,128]{2,1,0:T(8,128)(2,1)S(1)}, bf16[4,64,128]{2,1,0:T(8,128)(2,1)S(1)}, u32[]{:S(2)}, u32[]{:S(2)}) collective-permute-start(bf16[4,64,128]{2,1,0:T(8,128)(2,1)S(1)} %get-tuple-element.57), channel_id=1, source_target_pairs={{0,16},{16,0},{1,17},{17,1},{2,18},{18,2},{3,19},{19,3},{4,20},{20... | collective-permute-start | bytes 196616 | tf_op jit(solution)/shard_map/ppermute | solution.py:24
  13.6 0.7 %collective-permute-done.5.one_keys = bf16[4,64,128]{2,1,0:T(8,128)(2,1)S(1)} collective-permute-done((bf16[4,64,128]{2,1,0:T(8,128)(2,1)S(1)}, bf16[4,64,128]{2,1,0:T(8,128)(2,1)S(1)}, u32[]{:S(2)}, u32[]{:S(2)}) %collective-permute-start.5) | collective-permute-done | bytes 65568 | tf_op jit(solution)/shard_map/ppermute | solution.py:24
  14.5 0.9 %near_forward.1 = (f32[8,1,256]{2,1,0:T(1,128)S(1)}, f32[8,1,256]{2,1,0:T(1,128)S(1)}, f32[8,128,256]{2,1,0:T(8,128)S(1)}, f32[8,128,256]{2,1,0:T(8,128)S(1)}, f...) custom-call(s32[8,1,256]{2,1,0:T(1,128)S(1)} %get-tuple-element.54.first, ...), custom_call_target="tpu_custom_call" | custom-call | flops 1 | tf_op jit(solution)/shard_map/near_forward/pallas_call | solution.py:372
  15.5 2.3 %collective-permute-done.6.back_two = bf16[2,4,128,128]{3,2,1,0:T(8,128)(2,1)S(1)} collective-permute-done((bf16[2,4,128,128]{3,2,1,0:T(8,128)(2,1)S(1)}, bf16[2,4,128,128]{3,2,1,0:T(8,128)(2,1)S(1)}, u32[]{:S(2)}, u32[]{:S(2)}) %collective-permute-start.6) | collective-permute-done | bytes 262176 | tf_op jit(solution)/shard_map/ppermute | solution.py:19
  17.8 1.6 %far_forward_backward.1 = (bf16[8,128,256]{2,1,0:T(8,128)(2,1)S(1)}, f32[8,1,256]{2,1,0:T(1,128)S(1)}, f32[8,1,256]{2,1,0:T(1,128)S(1)}, bf16[8,128,256]{2,1,0:T(8,128)(2,1)S(1)}, bf16[2,4,128,128]{3,2,1,0:T(8,128)(2,1)S(1)}) custom-call(s32[8,1,256]{2,1,0:T(1,128)S(1)} %get-tuple-element.54.first, bf16[16,128,128]{2,1,0:T(8,128)(2,1)S(1)} %get-tuple-element.55.query_head, ...), custom_call_target="tpu_custom_call" | custom-call | flops 1 | tf_op jit(solution)/shard_map/far_forward_backward/pallas_call | solution.py:372
  19.4 3.7 %collective-permute-start.10 = (bf16[2,4,128,128]{3,2,1,0:T(8,128)(2,1)S(1)}, bf16[2,4,128,128]{3,2,1,0:T(8,128)(2,1)S(1)}, u32[]{:S(2)}, u32[]{:S(2)}) collective-permute-start(bf16[2,4,128,128]{3,2,1,0:T(8,128)(2,1)S(1)} %get-tuple-element.85), channel_id=1, source_target_pairs={{2,0},{3,1},{4,2},{5,3},{6,4},{7,5},{8,6},{9,7},{10,8},{11,9},{12,... | collective-permute-start | bytes 786440 | tf_op jit(solution)/shard_map/ppermute | solution.py:19
  23.1 0.5 %one_backward.1 = (bf16[8,128,256]{2,1,0:T(8,128)(2,1)S(1)}, bf16[2,4,64,128]{3,2,1,0:T(8,128)(2,1)S(1)}, bf16[4,64,128]{2,1,0:T(8,128)(2,1)S(1)}, bf16[4,64,128]{2,1,0:T(8,128)(2,1)S(1)}) custom-call(bf16[16,128,128]{2,1,0:T(8,128)(2,1)S(1)} %get-tuple-element.55.query_head, bf16[16,128,128]{2,1,0:T(8,128)(2,1)S(1)} %get-tuple-element.56.grad_head, ...), custom_call_target="tpu_custom_call" | custom-call | flops 1 | tf_op jit(solution)/shard_map/one_backward/pallas_call | solution.py:372
  23.7 0.5 %collective-permute-start.13 = (bf16[4,64,128]{2,1,0:T(8,128)(2,1)S(1)}, bf16[4,64,128]{2,1,0:T(8,128)(2,1)S(1)}, u32[]{:S(2)}, u32[]{:S(2)}) collective-permute-start(bf16[4,64,128]{2,1,0:T(8,128)(2,1)S(1)} %get-tuple-element.90), channel_id=1, source_target_pairs={{0,16},{16,0},{1,17},{17,1},{2,18},{18,2},{3,19},{19,3},{4,20},{20... | collective-permute-start | bytes 196616 | tf_op jit(solution)/shard_map/ppermute | solution.py:24
  24.2 0.5 %own_backward.1 = (bf16[8,128,256]{2,1,0:T(8,128)(2,1)S(1)}, f32[2,4,128,128]{3,2,1,0:T(8,128)S(1)}) custom-call(bf16[16,128,128]{2,1,0:T(8,128)(2,1)S(1)} %get-tuple-element.55.query_head, bf16[16,128,128]{2,1,0:T(8,128)(2,1)S(1)} %get-tuple-element.56.grad_head, f32[8,128,256]{2,1,0:T(8,128)S(1)} %get-tuple-element.74.own_weights, ...), custom_call_target="tpu_custom_call" | custom-call | flops 1 | tf_op jit(solution)/shard_map/own_backward/pallas_call | solution.py:372
  24.7 0.7 %query_grad.1 = (bf16[16,64,128]{2,1,0:T(8,128)(2,1)S(1)}, bf16[16,64,128]{2,1,0:T(8,128)(2,1)S(1)}, bf16[16,64,128]{2,1,0:T(8,128)(2,1)S(1)}, bf16[16,64,128]{2,1,0:T(8,128)(2,1)S(1)}) custom-call(bf16[2,4,128,128]{3,2,1,0:T(8,128)(2,1)S(1)} %join_own.1.own, bf16[2,8,64,128]{3,2,1,0:T(8,128)(2,1)S(1)} %collective-permute-done.2.block.back_one, ...), custom_call_target="tpu_custom_call" | custom-call | flops 1 | tf_op jit(solution)/shard_map/query_grad/pallas_call | solution.py:372
  25.5 0.4 %collective-permute-start.9 = (bf16[16,64,128]{2,1,0:T(8,128)(2,1)S(1)}, bf16[16,64,128]{2,1,0:T(8,128)(2,1)S(1)}, u32[]{:S(2)}, u32[]{:S(2)}) collective-permute-start(bf16[16,64,128]{2,1,0:T(8,128)(2,1)S(1)} %get-tuple-element.81.after), channel_id=1, source_target_pairs={{0,16},{16,0},{1,17},{17,1},{2,18},{18,2},{3,19},{19,3},{4,20},{20... | collective-permute-start | bytes 786440 | tf_op jit(solution)/shard_map/ppermute | solution.py:24
  26.0 3.4 %collective-permute-start.14 = (bf16[2,8,64,128]{3,2,1,0:T(8,128)(2,1)S(1)}, bf16[2,8,64,128]{3,2,1,0:T(8,128)(2,1)S(1)}, u32[]{:S(2)}, u32[]{:S(2)}) collective-permute-start(bf16[2,8,64,128]{3,2,1,0:T(8,128)(2,1)S(1)} %join_one.1), channel_id=1, source_target_pairs={{1,0},{2,1},{3,2},{4,3},{5,4},{6,5},{7,6},{8,7},{9,8},{10,9},{11,1... | collective-permute-start | bytes 786440 | tf_op jit(solution)/shard_map/ppermute | solution.py:19
  29.3 1.1 %collective-permute-done.10.far_total = bf16[2,4,128,128]{3,2,1,0:T(8,128)(2,1)S(1)} collective-permute-done((bf16[2,4,128,128]{3,2,1,0:T(8,128)(2,1)S(1)}, bf16[2,4,128,128]{3,2,1,0:T(8,128)(2,1)S(1)}, u32[]{:S(2)}, u32[]{:S(2)}) %collective-permute-start.10) | collective-permute-done | bytes 262176 | tf_op jit(solution)/shard_map/ppermute | solution.py:19
  30.6 1.0 %assemble.1 = (bf16[32,64,128]{2,1,0:T(8,128)(2,1)}, bf16[32,64,128]{2,1,0:T(8,128)(2,1)}, f32[8,128]{1,0:T(8,128)S(1)}) custom-call(bf16[16,64,128]{2,1,0:T(8,128)(2,1)S(1)} %get-tuple-element.78.out_mine, bf16[16,64,128]{2,1,0:T(8,128)(2,1)S(1)} %get-tuple-element.79.query_mine, bf16[16,64,128]{2,1,0:T(8,128)(2,1)S(1)} %collective-permute-done.8.out_other, ...), custom_call_target="tpu_custom_call" | custom-call | flops 1 | tf_op jit(solution)/shard_map/assemble/pallas_call | solution.py:372
  31.6 6.3 %collective-permute-done.14.one_total = bf16[2,8,64,128]{3,2,1,0:T(8,128)(2,1)S(1)} collective-permute-done((bf16[2,8,64,128]{3,2,1,0:T(8,128)(2,1)S(1)}, bf16[2,8,64,128]{3,2,1,0:T(8,128)(2,1)S(1)}, u32[]{:S(2)}, u32[]{:S(2)}) %collective-permute-start.14) | collective-permute-done | bytes 262176 | tf_op jit(solution)/shard_map/ppermute | solution.py:19
  37.9 0.7 %total.1 = (bf16[8,64,128]{2,1,0:T(8,128)(2,1)}, bf16[8,64,128]{2,1,0:T(8,128)(2,1)}) custom-call(f32[2,4,64,128]{3,2,1,0:T(8,128)S(1)} %get-tuple-element.86.sum_mine, bf16[2,4,64,128]{3,2,1,0:T(8,128)(2,1)S(1)} %collective-permute-done.11.sum_other, bf16[2,8,64,128]{3,2,1,0:T(8,128)(2,1)S(1)} %collective-permute-done.14.one_total, ...), custom_call_target="tpu_custom_call" | custom-call | flops 1 | tf_op jit(solution)/shard_map/total/pallas_call | solution.py:372
  (26 shorter events, 0.9 us)
Async XLA Ops:
  0.6 10.8 %collective-permute-start.3 = (bf16[32,64,128]{2,1,0:T(8,128)(2,1)}, bf16[32,64,128]{2,1,0:T(8,128)(2,1)S(1)}, u32[]{:S(2)}, u32[]{:S(2)}) collective-permute-start(bf16[32,64,128]{2,1,0:T(8,128)(2,1)} %queries.1), channel_id=1, source_target_pairs={{0,16},{16,0},{1,17},{17,1},{2,18},{18,2},{3,19},{19,3},{4,20},{20... | collective-permute-start | bytes 1572872 | tf_op jit(solution)/shard_map/ppermute | solution.py:24
  0.7 10.7 %collective-permute-start.4 = (bf16[32,64,128]{2,1,0:T(8,128)(2,1)}, bf16[32,64,128]{2,1,0:T(8,128)(2,1)S(1)}, u32[]{:S(2)}, u32[]{:S(2)}) collective-permute-start(bf16[32,64,128]{2,1,0:T(8,128)(2,1)} %grads.1), channel_id=1, source_target_pairs={{0,16},{16,0},{1,17},{17,1},{2,18},{18,2},{3,19},{19,3},{4,20},{20... | collective-permute-start | bytes 1572872 | tf_op jit(solution)/shard_map/ppermute | solution.py:24
  1.2 10.3 %copy-start.1 = (bf16[32,64,128]{2,1,0:T(8,128)(2,1)S(1)}, bf16[32,64,128]{2,1,0:T(8,128)(2,1)}, u32[]{:S(2)}) copy-start(bf16[32,64,128]{2,1,0:T(8,128)(2,1)} %grads.1) | copy-start | bytes 1572868
  2.3 9.2 %copy-start = (bf16[32,64,128]{2,1,0:T(8,128)(2,1)S(1)}, bf16[32,64,128]{2,1,0:T(8,128)(2,1)}, u32[]{:S(2)}) copy-start(bf16[32,64,128]{2,1,0:T(8,128)(2,1)} %queries.1) | copy-start | bytes 1572868
  2.3 10.8 %collective-permute-start.2 = (bf16[2,8,64,128]{3,2,1,0:T(8,128)(2,1)S(1)}, bf16[2,8,64,128]{3,2,1,0:T(8,128)(2,1)S(1)}, u32[]{:S(2)}, u32[]{:S(2)}) collective-permute-start(bf16[2,8,64,128]{3,2,1,0:T(8,128)(2,1)S(1)} %pad_maximum_fusion.block.own), channel_id=1, source_target_pairs={{0,1},{1,2},{2,3},{3,4},{4,5},{5,6},{6,7},{7,8},{8,9},{9,10},{10,1... | collective-permute-start | bytes 786440 | tf_op jit(solution)/shard_map/ppermute | solution.py:19
  5.8 1.3 %collective-permute-start = (bf16[4,64,128]{2,1,0:T(8,128)(2,1)S(1)}, bf16[4,64,128]{2,1,0:T(8,128)(2,1)S(1)}, u32[]{:S(2)}, u32[]{:S(2)}) collective-permute-start(bf16[4,64,128]{2,1,0:T(8,128)(2,1)S(1)} %get-tuple-element.49), channel_id=1, source_target_pairs={{0,16},{16,0},{1,17},{17,1},{2,18},{18,2},{3,19},{19,3},{4,20},{20... | collective-permute-start | bytes 196616 | tf_op jit(solution)/shard_map/ppermute | solution.py:24
  5.9 1.4 %collective-permute-start.1 = (bf16[4,64,128]{2,1,0:T(8,128)(2,1)S(1)}, bf16[4,64,128]{2,1,0:T(8,128)(2,1)S(1)}, u32[]{:S(2)}, u32[]{:S(2)}) collective-permute-start(bf16[4,64,128]{2,1,0:T(8,128)(2,1)S(1)} %get-tuple-element.50), channel_id=1, source_target_pairs={{0,16},{16,0},{1,17},{17,1},{2,18},{18,2},{3,19},{19,3},{4,20},{20... | collective-permute-start | bytes 196616 | tf_op jit(solution)/shard_map/ppermute | solution.py:24
  7.3 4.1 %copy-start.2 = (s32[32]{0:T(128)S(1)}, s32[32]{0:T(128)}, u32[]{:S(2)}) copy-start(s32[32]{0:T(128)} %spans.1) | copy-start | bytes 388
  7.4 10.5 %collective-permute-start.6 = (bf16[2,4,128,128]{3,2,1,0:T(8,128)(2,1)S(1)}, bf16[2,4,128,128]{3,2,1,0:T(8,128)(2,1)S(1)}, u32[]{:S(2)}, u32[]{:S(2)}) collective-permute-start(bf16[2,4,128,128]{3,2,1,0:T(8,128)(2,1)S(1)} %join_own.1.own), channel_id=1, source_target_pairs={{0,2},{1,3},{2,4},{3,5},{4,6},{5,7},{6,8},{7,9},{8,10},{9,11},{10,... | collective-permute-start | bytes 786440 | tf_op jit(solution)/shard_map/ppermute | solution.py:19
  13.1 1.3 %collective-permute-start.5 = (bf16[4,64,128]{2,1,0:T(8,128)(2,1)S(1)}, bf16[4,64,128]{2,1,0:T(8,128)(2,1)S(1)}, u32[]{:S(2)}, u32[]{:S(2)}) collective-permute-start(bf16[4,64,128]{2,1,0:T(8,128)(2,1)S(1)} %get-tuple-element.53), channel_id=1, source_target_pairs={{0,16},{16,0},{1,17},{17,1},{2,18},{18,2},{3,19},{19,3},{4,20},{20... | collective-permute-start | bytes 196616 | tf_op jit(solution)/shard_map/ppermute | solution.py:24
  13.2 1.3 %collective-permute-start.7 = (bf16[4,64,128]{2,1,0:T(8,128)(2,1)S(1)}, bf16[4,64,128]{2,1,0:T(8,128)(2,1)S(1)}, u32[]{:S(2)}, u32[]{:S(2)}) collective-permute-start(bf16[4,64,128]{2,1,0:T(8,128)(2,1)S(1)} %get-tuple-element.57), channel_id=1, source_target_pairs={{0,16},{16,0},{1,17},{17,1},{2,18},{18,2},{3,19},{19,3},{4,20},{20... | collective-permute-start | bytes 196616 | tf_op jit(solution)/shard_map/ppermute | solution.py:24
  19.4 11.0 %collective-permute-start.10 = (bf16[2,4,128,128]{3,2,1,0:T(8,128)(2,1)S(1)}, bf16[2,4,128,128]{3,2,1,0:T(8,128)(2,1)S(1)}, u32[]{:S(2)}, u32[]{:S(2)}) collective-permute-start(bf16[2,4,128,128]{3,2,1,0:T(8,128)(2,1)S(1)} %get-tuple-element.85), channel_id=1, source_target_pairs={{2,0},{3,1},{4,2},{5,3},{6,4},{7,5},{8,6},{9,7},{10,8},{11,9},{12,... | collective-permute-start | bytes 786440 | tf_op jit(solution)/shard_map/ppermute | solution.py:19
  23.6 2.3 %collective-permute-start.12 = (bf16[4,64,128]{2,1,0:T(8,128)(2,1)S(1)}, bf16[4,64,128]{2,1,0:T(8,128)(2,1)S(1)}, u32[]{:S(2)}, u32[]{:S(2)}) collective-permute-start(bf16[4,64,128]{2,1,0:T(8,128)(2,1)S(1)} %get-tuple-element.89), channel_id=1, source_target_pairs={{0,16},{16,0},{1,17},{17,1},{2,18},{18,2},{3,19},{19,3},{4,20},{20... | collective-permute-start | bytes 196616 | tf_op jit(solution)/shard_map/ppermute | solution.py:24
  23.7 2.2 %collective-permute-start.13 = (bf16[4,64,128]{2,1,0:T(8,128)(2,1)S(1)}, bf16[4,64,128]{2,1,0:T(8,128)(2,1)S(1)}, u32[]{:S(2)}, u32[]{:S(2)}) collective-permute-start(bf16[4,64,128]{2,1,0:T(8,128)(2,1)S(1)} %get-tuple-element.90), channel_id=1, source_target_pairs={{0,16},{16,0},{1,17},{17,1},{2,18},{18,2},{3,19},{19,3},{4,20},{20... | collective-permute-start | bytes 196616 | tf_op jit(solution)/shard_map/ppermute | solution.py:24
  25.3 5.2 %collective-permute-start.8 = (bf16[16,64,128]{2,1,0:T(8,128)(2,1)S(1)}, bf16[16,64,128]{2,1,0:T(8,128)(2,1)S(1)}, u32[]{:S(2)}, u32[]{:S(2)}) collective-permute-start(bf16[16,64,128]{2,1,0:T(8,128)(2,1)S(1)} %get-tuple-element.80), channel_id=1, source_target_pairs={{0,16},{16,0},{1,17},{17,1},{2,18},{18,2},{3,19},{19,3},{4,20},{20... | collective-permute-start | bytes 786440 | tf_op jit(solution)/shard_map/ppermute | solution.py:24
  25.5 5.1 %collective-permute-start.9 = (bf16[16,64,128]{2,1,0:T(8,128)(2,1)S(1)}, bf16[16,64,128]{2,1,0:T(8,128)(2,1)S(1)}, u32[]{:S(2)}, u32[]{:S(2)}) collective-permute-start(bf16[16,64,128]{2,1,0:T(8,128)(2,1)S(1)} %get-tuple-element.81.after), channel_id=1, source_target_pairs={{0,16},{16,0},{1,17},{17,1},{2,18},{18,2},{3,19},{19,3},{4,20},{20... | collective-permute-start | bytes 786440 | tf_op jit(solution)/shard_map/ppermute | solution.py:24
  26.0 12.0 %collective-permute-start.14 = (bf16[2,8,64,128]{3,2,1,0:T(8,128)(2,1)S(1)}, bf16[2,8,64,128]{3,2,1,0:T(8,128)(2,1)S(1)}, u32[]{:S(2)}, u32[]{:S(2)}) collective-permute-start(bf16[2,8,64,128]{3,2,1,0:T(8,128)(2,1)S(1)} %join_one.1), channel_id=1, source_target_pairs={{1,0},{2,1},{3,2},{4,3},{5,4},{6,5},{7,6},{8,7},{9,8},{10,9},{11,1... | collective-permute-start | bytes 786440 | tf_op jit(solution)/shard_map/ppermute | solution.py:19
  30.5 7.5 %collective-permute-start.11 = (bf16[2,4,64,128]{3,2,1,0:T(8,128)(2,1)S(1)}, bf16[2,4,64,128]{3,2,1,0:T(8,128)(2,1)S(1)}, u32[]{:S(2)}, u32[]{:S(2)}) collective-permute-start(bf16[2,4,64,128]{3,2,1,0:T(8,128)(2,1)S(1)} %get-tuple-element.87), channel_id=1, source_target_pairs={{0,16},{16,0},{1,17},{17,1},{2,18},{18,2},{3,19},{19,3},{4,20},{20... | collective-permute-start | bytes 393224 | tf_op jit(solution)/shard_map/ppermute | solution.py:24

commit v10 on v8

--- a/solution.py
+++ b/solution.py
@@ -117,11 +117,14 @@
         piece[...] = (queries, grads)[index][pl.ds(start + row, count)]
 
 
-def join_own_kernel(own, other_keys, other_values, own_head):
-    groups, length = other_keys.shape[:2]
+def split_own_kernel(own, own_send):
+    own_send[...] = own[:, other_heads(own_send.shape[1])]
+
+
+def join_own_kernel(own, own_other, own_head):
+    groups, length = own_other.shape[1:3]
     own_head[:, :, pl.ds(0, length)] = own[:, my_heads(groups)]
-    own_head[0, :, pl.ds(length, length)] = other_keys[...]
-    own_head[1, :, pl.ds(length, length)] = other_values[...]
+    own_head[:, :, pl.ds(length, length)] = own_other[...]
 
 
 def own_kernel(
@@ -415,9 +418,9 @@
 
     own = jnp.stack([key_matrix, value_matrix])
     back_two = shifted(own, "seq", 2)
-    own_sends = call(split_kernel, "split_own", [half_block] * 2, (own,))
+    (own_send,) = call(split_own_kernel, "split_own", [half_pair], (own,))
     (own_head,) = call(
-        join_own_kernel, "join_own", [chip_pair], (own, *[swapped(send, "head") for send in own_sends])
+        join_own_kernel, "join_own", [chip_pair], (own, swapped(own_send, "head"))
     )
     back_one = shifted(own_head, "seq", 1)
     sends = call(

time: 38.5 us -> 40.6 us (1.055)
  the two profiles are of different devices: /device:TPU:3 before, /device:TPU:6 now
where the time goes in v10:
time: 40.6 us; the launch traced here: 40.4 us
  starting transfers between devices  17.2 us (42%)
  waiting for transfers between devices  13 us (32%)
  Pallas kernels  7.74 us (19%)
  between operations  1.52 us (4%)
  other arithmetic  0.99 us (2%)
    ppermute x4, starting transfers between devices, shifted(): return lax.ppermute(block, axis, route)  15.1 us
    ppermute x4, waiting for transfers between devices, shifted(): return lax.ppermute(block, axis, route)  11.1 us
    pallas_call x14, Pallas kernels, call(): pl.pallas_call(kernel, out_shape=tuple((jax.ShapeDtypeStruct(shape, kind)...  7.74 us
    ppermute x11, starting transfers between devices, swapped(): return lax.ppermute(block, axis, [(i, count - 1 - i) for i in range(count)])  2.08 us
    ppermute x11, waiting for transfers between devices, swapped(): return lax.ppermute(block, axis, [(i, count - 1 - i) for i in range(count)])  1.94 us
    another operation x1, other arithmetic, shards(): own = jnp.stack([key_matrix, value_matrix])  0.99 us
  transfers between devices with their start and end apart: 15, of which 7 were waited for; matrix products, arithmetic and copies ran while one was open for 0% of the time, Pallas kernels for 13%

profile of v10, /device:TPU:6, one launch (start us, length us, event | category | flops | bytes accessed | tf_op | source)
XLA Modules:
  0.0 40.4 jit_solution(1235034736981823876)
XLA Ops:
  0.6 1.0 %pad_maximum_fusion.own.after = bf16[2,8,64,128]{3,2,1,0:T(8,128)(2,1)S(1)} fusion(bf16[1,8,64,128]{3,2,1,0:T(8,128)(2,1)} %bitcast.2, bf16[1,8,64,128]{3,2,1,0:T(8,128)(2,1)} %bitcast.3), kind=kLoop, calls=%fused_computation | loop fusion | flops 131072 | bytes 524288 | tf_op jit(solution)/shard_map/stack | solution.py:419
  1.8 3.6 %collective-permute-start.2 = (bf16[2,8,64,128]{3,2,1,0:T(8,128)(2,1)S(1)}, bf16[2,8,64,128]{3,2,1,0:T(8,128)(2,1)S(1)}, u32[]{:S(2)}, u32[]{:S(2)}) collective-permute-start(bf16[2,8,64,128]{3,2,1,0:T(8,128)(2,1)S(1)} %pad_maximum_fusion.own.after), channel_id=1, source_target_pairs={{0,2},{1,3},{2,4},{3,5},{4,6},{5,7},{6,8},{7,9},{8,10},{9,11},{10,... | collective-permute-start | bytes 786440 | tf_op jit(solution)/shard_map/ppermute | solution.py:19
  5.4 3.4 %collective-permute-start.1 = (bf16[2,4,128,128]{3,2,1,0:T(8,128)(2,1)S(1)}, bf16[2,4,128,128]{3,2,1,0:T(8,128)(2,1)S(1)}, u32[]{:S(2)}, u32[]{:S(2)}) collective-permute-start(bf16[2,4,128,128]{3,2,1,0:T(8,128)(2,1)S(1)} %join_own.1.own), channel_id=1, source_target_pairs={{0,1},{1,2},{2,3},{3,4},{4,5},{5,6},{6,7},{7,8},{8,9},{9,10},{10,1... | collective-permute-start | bytes 786440 | tf_op jit(solution)/shard_map/ppermute | solution.py:19
  8.9 0.5 %collective-permute-start.5 = (bf16[11,64,128]{2,1,0:T(8,128)(2,1)S(1)}, bf16[11,64,128]{2,1,0:T(8,128)(2,1)S(1)}, u32[]{:S(2)}, u32[]{:S(2)}) collective-permute-start(bf16[11,64,128]{2,1,0:T(8,128)(2,1)S(1)} %get-tuple-element.51), channel_id=1, source_target_pairs={{0,16},{16,0},{1,17},{17,1},{2,18},{18,2},{3,19},{19,3},{4,20},{20... | collective-permute-start | bytes 540680 | tf_op jit(solution)/shard_map/ppermute | solution.py:24
  10.2 0.7 %collective-permute-done.3.first_third = bf16[10,64,128]{2,1,0:T(8,128)(2,1)S(1)} collective-permute-done((bf16[10,64,128]{2,1,0:T(8,128)(2,1)S(1)}, bf16[10,64,128]{2,1,0:T(8,128)(2,1)S(1)}, u32[]{:S(2)}, u32[]{:S(2)}) %collective-permute-start.3) | collective-permute-done | bytes 163872 | tf_op jit(solution)/shard_map/ppermute | solution.py:24
  10.8 1.5 %own_block.1 = (bf16[16,128,128]{2,1,0:T(8,128)(2,1)S(1)}, bf16[16,128,128]{2,1,0:T(8,128)(2,1)S(1)}, bf16[8,128,256]{2,1,0:T(8,128)(2,1)S(1)}, s32[8,1,256]{2,1...) custom-call(s32[32]{0:T(128)S(1)} %copy-done.2, ...), custom_call_target="tpu_custom_call" | custom-call | flops 1 | tf_op jit(solution)/shard_map/own_block/pallas_call | solution.py:396
  12.4 0.3 collective-permute-start.6
  12.7 0.3 collective-permute-start.7
  13.0 0.7 %collective-permute-done.6.two_keys = bf16[4,64,128]{2,1,0:T(8,128)(2,1)S(1)} collective-permute-done((bf16[4,64,128]{2,1,0:T(8,128)(2,1)S(1)}, bf16[4,64,128]{2,1,0:T(8,128)(2,1)S(1)}, u32[]{:S(2)}, u32[]{:S(2)}) %collective-permute-start.6) | collective-permute-done | bytes 65568 | tf_op jit(solution)/shard_map/ppermute | solution.py:24
  13.7 0.3 collective-permute-done.7.two_values
  14.0 0.9 %near_forward.1 = (f32[8,1,256]{2,1,0:T(1,128)S(1)}, f32[8,1,256]{2,1,0:T(1,128)S(1)}, f32[8,128,256]{2,1,0:T(8,128)S(1)}, f32[8,128,256]{2,1,0:T(8,128)S(1)}, f...) custom-call(s32[8,1,256]{2,1,0:T(1,128)S(1)} %get-tuple-element.53.first, ...), custom_call_target="tpu_custom_call" | custom-call | flops 1 | tf_op jit(solution)/shard_map/near_forward/pallas_call | solution.py:396
  14.9 2.1 %collective-permute-done.1.back_one = bf16[2,4,128,128]{3,2,1,0:T(8,128)(2,1)S(1)} collective-permute-done((bf16[2,4,128,128]{3,2,1,0:T(8,128)(2,1)S(1)}, bf16[2,4,128,128]{3,2,1,0:T(8,128)(2,1)S(1)}, u32[]{:S(2)}, u32[]{:S(2)}) %collective-permute-start.1) | collective-permute-done | bytes 262176 | tf_op jit(solution)/shard_map/ppermute | solution.py:19
  17.0 1.6 %last_forward_backward.1 = (bf16[8,128,256]{2,1,0:T(8,128)(2,1)S(1)}, f32[8,1,256]{2,1,0:T(1,128)S(1)}, f32[8,1,256]{2,1,0:T(1,128)S(1)}, bf16[8,128,256]{2,1,0:T(8,128)(2,1)S(1)}, bf16[2,4,128,128]{3,2,1,0:T(8,128)(2,1)S(1)}) custom-call(s32[8,1,256]{2,1,0:T(1,128)S(1)} %get-tuple-element.53.first, bf16[16,128,128]{2,1,0:T(8,128)(2,1)S(1)} %get-tuple-element.54.query_head, ...), custom_call_target="tpu_custom_call" | custom-call | flops 1 | tf_op jit(solution)/shard_map/last_forward_backward/pallas_call | solution.py:396
  18.7 0.5 %two_backward.1 = (bf16[8,128,256]{2,1,0:T(8,128)(2,1)S(1)}, bf16[2,4,128,128]{3,2,1,0:T(8,128)(2,1)S(1)}) custom-call(bf16[16,128,128]{2,1,0:T(8,128)(2,1)S(1)} %get-tuple-element.54.query_head, bf16[16,128,128]{2,1,0:T(8,128)(2,1)S(1)} %get-tuple-element.55.grad_head, f32[8,128,256]{2,1,0:T(8,128)S(1)} %get-tuple-element.69.near_weights, ...), custom_call_target="tpu_custom_call" | custom-call | flops 1 | tf_op jit(solution)/shard_map/two_backward/pallas_call | solution.py:396
  19.2 1.9 %collective-permute-start.12 = (bf16[2,4,128,128]{3,2,1,0:T(8,128)(2,1)S(1)}, bf16[2,4,128,128]{3,2,1,0:T(8,128)(2,1)S(1)}, u32[]{:S(2)}, u32[]{:S(2)}) collective-permute-start(bf16[2,4,128,128]{3,2,1,0:T(8,128)(2,1)S(1)} %get-tuple-element.88), channel_id=1, source_target_pairs={{2,0},{3,1},{4,2},{5,3},{6,4},{7,5},{8,6},{9,7},{10,8},{11,9},{12,... | collective-permute-start | bytes 786440 | tf_op jit(solution)/shard_map/ppermute | solution.py:19
  21.2 6.2 %collective-permute-start.14 = (bf16[2,8,64,128]{3,2,1,0:T(8,128)(2,1)S(1)}, bf16[2,8,64,128]{3,2,1,0:T(8,128)(2,1)S(1)}, u32[]{:S(2)}, u32[]{:S(2)}) collective-permute-start(bf16[2,8,64,128]{3,2,1,0:T(8,128)(2,1)S(1)} %join_one.1.after), channel_id=1, source_target_pairs={{1,0},{2,1},{3,2},{4,3},{5,4},{6,5},{7,6},{8,7},{9,8},{10,9},{11,1... | collective-permute-start | bytes 786440 | tf_op jit(solution)/shard_map/ppermute | solution.py:19
  27.4 0.5 %own_backward.1 = (bf16[8,128,256]{2,1,0:T(8,128)(2,1)S(1)}, f32[2,4,128,128]{3,2,1,0:T(8,128)S(1)}) custom-call(bf16[16,128,128]{2,1,0:T(8,128)(2,1)S(1)} %get-tuple-element.54.query_head, bf16[16,128,128]{2,1,0:T(8,128)(2,1)S(1)} %get-tuple-element.55.grad_head, f32[8,128,256]{2,1,0:T(8,128)S(1)} %get-tuple-element.75.own_weights, ...), custom_call_target="tpu_custom_call" | custom-call | flops 1 | tf_op jit(solution)/shard_map/own_backward/pallas_call | solution.py:396
  27.8 0.8 %query_grad.1 = (bf16[16,64,128]{2,1,0:T(8,128)(2,1)S(1)}, bf16[16,64,128]{2,1,0:T(8,128)(2,1)S(1)}, bf16[10,64,128]{2,1,0:T(8,128)(2,1)S(1)}, bf16[11,64,128]{2,1,0:T(8,128)(2,1)S(1)}, bf16[11,64,128]{2,1,0:T(8,128)(2,1)S(1)}) custom-call(bf16[2,4,128,128]{3,2,1,0:T(8,128)(2,1)S(1)} %join_own.1.own, ...), custom_call_target="tpu_custom_call" | custom-call | flops 1 | tf_op jit(solution)/shard_map/query_grad/pallas_call | solution.py:396
  28.7 0.5 %collective-permute-start.11 = (bf16[11,64,128]{2,1,0:T(8,128)(2,1)S(1)}, bf16[11,64,128]{2,1,0:T(8,128)(2,1)S(1)}, u32[]{:S(2)}, u32[]{:S(2)}) collective-permute-start(bf16[11,64,128]{2,1,0:T(8,128)(2,1)S(1)} %get-tuple-element.84), channel_id=1, source_target_pairs={{0,16},{16,0},{1,17},{17,1},{2,18},{18,2},{3,19},{19,3},{4,20},{20... | collective-permute-start | bytes 540680 | tf_op jit(solution)/shard_map/ppermute | solution.py:24
  29.2 1.5 %collective-permute-done.12.two_total = bf16[2,4,128,128]{3,2,1,0:T(8,128)(2,1)S(1)} collective-permute-done((bf16[2,4,128,128]{3,2,1,0:T(8,128)(2,1)S(1)}, bf16[2,4,128,128]{3,2,1,0:T(8,128)(2,1)S(1)}, u32[]{:S(2)}, u32[]{:S(2)}) %collective-permute-start.12) | collective-permute-done | bytes 262176 | tf_op jit(solution)/shard_map/ppermute | solution.py:19
  30.9 1.0 %assemble.1 = (bf16[32,64,128]{2,1,0:T(8,128)(2,1)}, bf16[32,64,128]{2,1,0:T(8,128)(2,1)}, f32[8,128]{1,0:T(8,128)S(1)}) custom-call(bf16[16,64,128]{2,1,0:T(8,128)(2,1)S(1)} %get-tuple-element.80.out_mine, bf16[16,64,128]{2,1,0:T(8,128)(2,1)S(1)} %get-tuple-element.81.query_mine, bf16[10,64,128]{2,1,0:T(8,128)(2,1)S(1)} %collective-permute-done.9.first_third, ...), custom_call_target="tpu_custom_call" | custom-call | flops 1 | tf_op jit(solution)/shard_map/assemble/pallas_call | solution.py:396
  31.9 0.3 collective-permute-done.13.sum_other
  32.2 7.5 %collective-permute-done.14.one_total = bf16[2,8,64,128]{3,2,1,0:T(8,128)(2,1)S(1)} collective-permute-done((bf16[2,8,64,128]{3,2,1,0:T(8,128)(2,1)S(1)}, bf16[2,8,64,128]{3,2,1,0:T(8,128)(2,1)S(1)}, u32[]{:S(2)}, u32[]{:S(2)}) %collective-permute-start.14) | collective-permute-done | bytes 262176 | tf_op jit(solution)/shard_map/ppermute | solution.py:19
  39.7 0.7 %total.1 = (bf16[8,64,128]{2,1,0:T(8,128)(2,1)}, bf16[8,64,128]{2,1,0:T(8,128)(2,1)}) custom-call(f32[2,4,64,128]{3,2,1,0:T(8,128)S(1)} %get-tuple-element.89.sum_mine, bf16[2,4,64,128]{3,2,1,0:T(8,128)(2,1)S(1)} %collective-permute-done.13.sum_other, bf16[2,8,64,128]{3,2,1,0:T(8,128)(2,1)S(1)} %collective-permute-done.14.one_total, ...), custom_call_target="tpu_custom_call" | custom-call | flops 1 | tf_op jit(solution)/shard_map/total/pallas_call | solution.py:396
  (27 shorter events, 0.8 us)
Async XLA Ops:
  1.6 7.1 %copy-start = (bf16[32,64,128]{2,1,0:T(8,128)(2,1)S(1)}, bf16[32,64,128]{2,1,0:T(8,128)(2,1)}, u32[]{:S(2)}) copy-start(bf16[32,64,128]{2,1,0:T(8,128)(2,1)} %queries.3) | copy-start | bytes 1572868
  1.6 7.1 %copy-start.1 = (bf16[32,64,128]{2,1,0:T(8,128)(2,1)S(1)}, bf16[32,64,128]{2,1,0:T(8,128)(2,1)}, u32[]{:S(2)}) copy-start(bf16[32,64,128]{2,1,0:T(8,128)(2,1)} %grads.3) | copy-start | bytes 1572868
  1.7 3.6 %collective-permute-start = (bf16[2,4,64,128]{3,2,1,0:T(8,128)(2,1)S(1)}, bf16[2,4,64,128]{3,2,1,0:T(8,128)(2,1)S(1)}, u32[]{:S(2)}, u32[]{:S(2)}) collective-permute-start(bf16[2,4,64,128]{3,2,1,0:T(8,128)(2,1)S(1)} %split_own.1), channel_id=1, source_target_pairs={{0,16},{16,0},{1,17},{17,1},{2,18},{18,2},{3,19},{19,3},{4,20},{20... | collective-permute-start | bytes 393224 | tf_op jit(solution)/shard_map/ppermute | solution.py:24
  1.8 10.6 %collective-permute-start.2 = (bf16[2,8,64,128]{3,2,1,0:T(8,128)(2,1)S(1)}, bf16[2,8,64,128]{3,2,1,0:T(8,128)(2,1)S(1)}, u32[]{:S(2)}, u32[]{:S(2)}) collective-permute-start(bf16[2,8,64,128]{3,2,1,0:T(8,128)(2,1)S(1)} %pad_maximum_fusion.own.after), channel_id=1, source_target_pairs={{0,2},{1,3},{2,4},{3,5},{4,6},{5,7},{6,8},{7,9},{8,10},{9,11},{10,... | collective-permute-start | bytes 786440 | tf_op jit(solution)/shard_map/ppermute | solution.py:19
  5.4 11.6 %collective-permute-start.1 = (bf16[2,4,128,128]{3,2,1,0:T(8,128)(2,1)S(1)}, bf16[2,4,128,128]{3,2,1,0:T(8,128)(2,1)S(1)}, u32[]{:S(2)}, u32[]{:S(2)}) collective-permute-start(bf16[2,4,128,128]{3,2,1,0:T(8,128)(2,1)S(1)} %join_own.1.own), channel_id=1, source_target_pairs={{0,1},{1,2},{2,3},{3,4},{4,5},{5,6},{6,7},{7,8},{8,9},{9,10},{10,1... | collective-permute-start | bytes 786440 | tf_op jit(solution)/shard_map/ppermute | solution.py:19
  8.8 2.0 %collective-permute-start.4 = (bf16[11,64,128]{2,1,0:T(8,128)(2,1)S(1)}, bf16[11,64,128]{2,1,0:T(8,128)(2,1)S(1)}, u32[]{:S(2)}, u32[]{:S(2)}) collective-permute-start(bf16[11,64,128]{2,1,0:T(8,128)(2,1)S(1)} %get-tuple-element.50), channel_id=1, source_target_pairs={{0,16},{16,0},{1,17},{17,1},{2,18},{18,2},{3,19},{19,3},{4,20},{20... | collective-permute-start | bytes 540680 | tf_op jit(solution)/shard_map/ppermute | solution.py:24
  8.9 1.9 %collective-permute-start.5 = (bf16[11,64,128]{2,1,0:T(8,128)(2,1)S(1)}, bf16[11,64,128]{2,1,0:T(8,128)(2,1)S(1)}, u32[]{:S(2)}, u32[]{:S(2)}) collective-permute-start(bf16[11,64,128]{2,1,0:T(8,128)(2,1)S(1)} %get-tuple-element.51), channel_id=1, source_target_pairs={{0,16},{16,0},{1,17},{17,1},{2,18},{18,2},{3,19},{19,3},{4,20},{20... | collective-permute-start | bytes 540680 | tf_op jit(solution)/shard_map/ppermute | solution.py:24
  9.4 1.4 %copy-start.2 = (s32[32]{0:T(128)S(1)}, s32[32]{0:T(128)}, u32[]{:S(2)}) copy-start(s32[32]{0:T(128)} %spans.1) | copy-start | bytes 388
  9.4 1.4 %collective-permute-start.3 = (bf16[10,64,128]{2,1,0:T(8,128)(2,1)S(1)}, bf16[10,64,128]{2,1,0:T(8,128)(2,1)S(1)}, u32[]{:S(2)}, u32[]{:S(2)}) collective-permute-start(bf16[10,64,128]{2,1,0:T(8,128)(2,1)S(1)} %get-tuple-element.49), channel_id=1, source_target_pairs={{0,16},{16,0},{1,17},{17,1},{2,18},{18,2},{3,19},{19,3},{4,20},{20... | collective-permute-start | bytes 491528 | tf_op jit(solution)/shard_map/ppermute | solution.py:24
  12.4 1.3 %collective-permute-start.6 = (bf16[4,64,128]{2,1,0:T(8,128)(2,1)S(1)}, bf16[4,64,128]{2,1,0:T(8,128)(2,1)S(1)}, u32[]{:S(2)}, u32[]{:S(2)}) collective-permute-start(bf16[4,64,128]{2,1,0:T(8,128)(2,1)S(1)} %get-tuple-element.57), channel_id=1, source_target_pairs={{0,16},{16,0},{1,17},{17,1},{2,18},{18,2},{3,19},{19,3},{4,20},{20... | collective-permute-start | bytes 196616 | tf_op jit(solution)/shard_map/ppermute | solution.py:24
  12.7 1.3 %collective-permute-start.7 = (bf16[4,64,128]{2,1,0:T(8,128)(2,1)S(1)}, bf16[4,64,128]{2,1,0:T(8,128)(2,1)S(1)}, u32[]{:S(2)}, u32[]{:S(2)}) collective-permute-start(bf16[4,64,128]{2,1,0:T(8,128)(2,1)S(1)} %get-tuple-element.58), channel_id=1, source_target_pairs={{0,16},{16,0},{1,17},{17,1},{2,18},{18,2},{3,19},{19,3},{4,20},{20... | collective-permute-start | bytes 196616 | tf_op jit(solution)/shard_map/ppermute | solution.py:24
  18.6 2.5 %collective-permute-start.8 = (bf16[2,4,128,128]{3,2,1,0:T(8,128)(2,1)S(1)}, bf16[2,4,128,128]{3,2,1,0:T(8,128)(2,1)S(1)}, u32[]{:S(2)}, u32[]{:S(2)}) collective-permute-start(bf16[2,4,128,128]{3,2,1,0:T(8,128)(2,1)S(1)} %get-tuple-element.78.one_part), channel_id=1, source_target_pairs={{0,16},{16,0},{1,17},{17,1},{2,18},{18,2},{3,19},{19,3},{4,20},{20... | collective-permute-start | bytes 786440 | tf_op jit(solution)/shard_map/ppermute | solution.py:24
  19.2 11.5 %collective-permute-start.12 = (bf16[2,4,128,128]{3,2,1,0:T(8,128)(2,1)S(1)}, bf16[2,4,128,128]{3,2,1,0:T(8,128)(2,1)S(1)}, u32[]{:S(2)}, u32[]{:S(2)}) collective-permute-start(bf16[2,4,128,128]{3,2,1,0:T(8,128)(2,1)S(1)} %get-tuple-element.88), channel_id=1, source_target_pairs={{2,0},{3,1},{4,2},{5,3},{6,4},{7,5},{8,6},{9,7},{10,8},{11,9},{12,... | collective-permute-start | bytes 786440 | tf_op jit(solution)/shard_map/ppermute | solution.py:19
  21.2 18.5 %collective-permute-start.14 = (bf16[2,8,64,128]{3,2,1,0:T(8,128)(2,1)S(1)}, bf16[2,8,64,128]{3,2,1,0:T(8,128)(2,1)S(1)}, u32[]{:S(2)}, u32[]{:S(2)}) collective-permute-start(bf16[2,8,64,128]{3,2,1,0:T(8,128)(2,1)S(1)} %join_one.1.after), channel_id=1, source_target_pairs={{1,0},{2,1},{3,2},{4,3},{5,4},{6,5},{7,6},{8,7},{9,8},{10,9},{11,1... | collective-permute-start | bytes 786440 | tf_op jit(solution)/shard_map/ppermute | solution.py:19
  28.6 2.3 %collective-permute-start.10 = (bf16[11,64,128]{2,1,0:T(8,128)(2,1)S(1)}, bf16[11,64,128]{2,1,0:T(8,128)(2,1)S(1)}, u32[]{:S(2)}, u32[]{:S(2)}) collective-permute-start(bf16[11,64,128]{2,1,0:T(8,128)(2,1)S(1)} %get-tuple-element.83), channel_id=1, source_target_pairs={{0,16},{16,0},{1,17},{17,1},{2,18},{18,2},{3,19},{19,3},{4,20},{20... | collective-permute-start | bytes 540680 | tf_op jit(solution)/shard_map/ppermute | solution.py:24
  28.7 2.2 %collective-permute-start.11 = (bf16[11,64,128]{2,1,0:T(8,128)(2,1)S(1)}, bf16[11,64,128]{2,1,0:T(8,128)(2,1)S(1)}, u32[]{:S(2)}, u32[]{:S(2)}) collective-permute-start(bf16[11,64,128]{2,1,0:T(8,128)(2,1)S(1)} %get-tuple-element.84), channel_id=1, source_target_pairs={{0,16},{16,0},{1,17},{17,1},{2,18},{18,2},{3,19},{19,3},{4,20},{20... | collective-permute-start | bytes 540680 | tf_op jit(solution)/shard_map/ppermute | solution.py:24
  29.2 1.7 %collective-permute-start.9 = (bf16[10,64,128]{2,1,0:T(8,128)(2,1)S(1)}, bf16[10,64,128]{2,1,0:T(8,128)(2,1)S(1)}, u32[]{:S(2)}, u32[]{:S(2)}) collective-permute-start(bf16[10,64,128]{2,1,0:T(8,128)(2,1)S(1)} %get-tuple-element.82), channel_id=1, source_target_pairs={{0,16},{16,0},{1,17},{17,1},{2,18},{18,2},{3,19},{19,3},{4,20},{20... | collective-permute-start | bytes 491528 | tf_op jit(solution)/shard_map/ppermute | solution.py:24
  30.8 1.4 %collective-permute-start.13 = (bf16[2,4,64,128]{3,2,1,0:T(8,128)(2,1)S(1)}, bf16[2,4,64,128]{3,2,1,0:T(8,128)(2,1)S(1)}, u32[]{:S(2)}, u32[]{:S(2)}) collective-permute-start(bf16[2,4,64,128]{3,2,1,0:T(8,128)(2,1)S(1)} %get-tuple-element.90), channel_id=1, source_target_pairs={{0,16},{16,0},{1,17},{17,1},{2,18},{18,2},{3,19},{19,3},{4,20},{20... | collective-permute-start | bytes 393224 | tf_op jit(solution)/shard_map/ppermute | solution.py:24

commit v11 on v7

--- a/solution.py
+++ b/solution.py
@@ -417,7 +417,11 @@
     chip_rows = ((heads_here, tokens, width), half)
 
     own = jnp.stack([key_matrix, value_matrix])
-    back_one = shifted(own, "seq", 1)
+    count_seq = lax.axis_size("seq")
+    pairs = [[i, i + 1] for i in range(0, count_seq, 2)]
+    gathered = lax.all_gather(own, "seq", axis_index_groups=pairs)
+    crossing = lax.ppermute(own, "seq", [(i - 1, i) for i in range(2, count_seq, 2)])
+    back_one = jnp.where(lax.bitwise_and(lax.axis_index("seq"), 1) == 1, gathered[0], crossing)
     own_sends = call(split_kernel, "split_own", [half_block] * 2, (own,))
     (own_head,) = call(
         join_own_kernel, "join_own", [chip_pair], (own, *[swapped(send, "head") for send in own_sends])

time: 37.6 us -> 47.5 us (1.26)
  blocking collectives: 0 us -> 9.31 us
  local copies, waits for them, and re-layouts: 0.01 us -> 1.05 us
  starting transfers between devices: 17.3 us -> 16.8 us
    all_gather x0 -> x1, blocking collectives: none -> 9.31 us  [shards(): gathered = lax.all_gather(own, 'seq', axis_index_groups=pairs)]
    ppermute x4 -> x3, starting transfers between devices: 13.8 us -> 9.94 us  [shifted(): return lax.ppermute(block, axis, route)]
    ppermute x0 -> x1, starting transfers between devices: none -> 3.41 us  [shards(): lax.ppermute(own, 'seq', [(i - 1, i) for i in range(2, count_seq, 2)])]
    ppermute x13, waiting for transfers between devices: 4.24 us -> 2.59 us  [swapped(): return lax.ppermute(block, axis, [(i, count - 1 - i) for i in range(count)])]
    ppermute x4 -> x3, waiting for transfers between devices: 5.52 us -> 7.08 us  [shifted(): return lax.ppermute(block, axis, route)]
    unnamed x6 -> x8, local copies, waits for them, and re-layouts: 0.01 us -> 1.05 us
  transfers between devices with their start and end apart: 17 -> 17, of which waited for: 10 -> 7; matrix products, arithmetic and copies ran while one was open for 0% -> 0% of each run, Pallas kernels for 15% -> 11%
where the time goes in v11:
time: 47.5 us; the launch traced here: 47.3 us
  starting transfers between devices  16.8 us (35%)
  waiting for transfers between devices  9.68 us (20%)
  blocking collectives  9.31 us (20%)
  Pallas kernels  7.72 us (16%)
  between operations  1.58 us (3%)
  other arithmetic  1.08 us (2%)
  local copies, waits for them, and re-layouts  1.05 us (2%)
    ppermute x3, starting transfers between devices, shifted(): return lax.ppermute(block, axis, route)  9.94 us
    all_gather x1, blocking collectives, shards(): gathered = lax.all_gather(own, 'seq', axis_index_groups=pairs)  9.31 us
    pallas_call x14, Pallas kernels, call(): pl.pallas_call(kernel, out_shape=tuple((jax.ShapeDtypeStruct(shape, kind)...  7.72 us
    ppermute x3, waiting for transfers between devices, shifted(): return lax.ppermute(block, axis, route)  7.08 us
    ppermute x13, starting transfers between devices, swapped(): return lax.ppermute(block, axis, [(i, count - 1 - i) for i in range(count)])  3.5 us
    ppermute x1, starting transfers between devices, shards(): lax.ppermute(own, 'seq', [(i - 1, i) for i in range(2, count_seq, 2)])  3.41 us
    ppermute x13, waiting for transfers between devices, swapped(): return lax.ppermute(block, axis, [(i, count - 1 - i) for i in range(count)])  2.59 us
    unnamed x8, local copies, waits for them, and re-layouts  1.05 us
  transfers between devices with their start and end apart: 17, of which 7 were waited for; matrix products, arithmetic and copies ran while one was open for 0% of the time, Pallas kernels for 11%

profile of v11, /device:TPU:14, one launch (start us, length us, event | category | flops | bytes accessed | tf_op | source)
XLA Modules:
  0.0 47.3 jit_solution(587568308981486123)
XLA Ops:
  0.6 1.1 %pad_maximum_fusion.block.own.after = bf16[2,8,64,128]{3,2,1,0:T(8,128)(2,1)S(1)} fusion(bf16[1,8,64,128]{3,2,1,0:T(8,128)(2,1)} %bitcast.2, bf16[1,8,64,128]{3,2,1,0:T(8,128)(2,1)} %bitcast.3), kind=kLoop, calls=%fused_computation.1 | loop fusion | flops 131072 | bytes 524288 | tf_op jit(solution)/shard_map/stack | solution.py:419
  1.7 3.4 %collective-permute-start.2 = (bf16[2,8,64,128]{3,2,1,0:T(8,128)(2,1)S(1)}, bf16[2,8,64,128]{3,2,1,0:T(8,128)(2,1)S(1)}, u32[]{:S(2)}, u32[]{:S(2)}) collective-permute-start(bf16[2,8,64,128]{3,2,1,0:T(8,128)(2,1)S(1)} %pad_maximum_fusion.block.own.after), channel_id=1, source_target_pairs={{1,2},{3,4},{5,6},{7,8},{9,10},{11,12},{13,14},{17,18},{19,20},{21... | collective-permute-start | bytes 786440 | tf_op jit(solution)/shard_map/ppermute | solution.py:423
  5.2 1.0 %copy-done.1 = bf16[32,64,128]{2,1,0:T(8,128)(2,1)S(1)} copy-done((bf16[32,64,128]{2,1,0:T(8,128)(2,1)S(1)}, bf16[32,64,128]{2,1,0:T(8,128)(2,1)}, u32[]{:S(2)}) %copy-start.1) | copy-done | bytes 524312
  6.3 0.6 %collective-permute-start.4 = (bf16[11,64,128]{2,1,0:T(8,128)(2,1)S(1)}, bf16[11,64,128]{2,1,0:T(8,128)(2,1)S(1)}, u32[]{:S(2)}, u32[]{:S(2)}) collective-permute-start(bf16[11,64,128]{2,1,0:T(8,128)(2,1)S(1)} %get-tuple-element.56), channel_id=1, source_target_pairs={{0,16},{16,0},{1,17},{17,1},{2,18},{18,2},{3,19},{19,3},{4,20},{20... | collective-permute-start | bytes 540680 | tf_op jit(solution)/shard_map/ppermute | solution.py:24
  7.5 9.3 %all-gather = bf16[4,8,64,128]{3,2,1,0:T(8,128)(2,1)S(1)} all-gather(bf16[2,8,64,128]{3,2,1,0:T(8,128)(2,1)S(1)} %pad_maximum_fusion.block.own.after), channel_id=2, replica_groups={{0,1},{2,3},{4,5},{6,7},{8,9},{10,11},{12,13},{14,15},{16,17},{18,19},{..., dimensions={0}, use_global_device_ids=true | all-gather | bytes 786432 | tf_op jit(solution)/shard_map/all_gather | solution.py:422
  17.5 3.4 %collective-permute-start.7 = (bf16[2,4,128,128]{3,2,1,0:T(8,128)(2,1)S(1)}, bf16[2,4,128,128]{3,2,1,0:T(8,128)(2,1)S(1)}, u32[]{:S(2)}, u32[]{:S(2)}) collective-permute-start(bf16[2,4,128,128]{3,2,1,0:T(8,128)(2,1)S(1)} %join_own.1.own), channel_id=1, source_target_pairs={{0,2},{1,3},{2,4},{3,5},{4,6},{5,7},{6,8},{7,9},{8,10},{9,11},{10,... | collective-permute-start | bytes 786440 | tf_op jit(solution)/shard_map/ppermute | solution.py:19
  21.0 1.5 %own_block.1 = (bf16[16,128,128]{2,1,0:T(8,128)(2,1)S(1)}, bf16[16,128,128]{2,1,0:T(8,128)(2,1)S(1)}, bf16[8,128,256]{2,1,0:T(8,128)(2,1)S(1)}, s32[8,1,256]{2,1...) custom-call(s32[32]{0:T(128)S(1)} %copy-done.3, ...), custom_call_target="tpu_custom_call" | custom-call | flops 1 | tf_op jit(solution)/shard_map/own_block/pallas_call | solution.py:396
  22.7 0.5 %collective-permute-start.8 = (bf16[4,64,128]{2,1,0:T(8,128)(2,1)S(1)}, bf16[4,64,128]{2,1,0:T(8,128)(2,1)S(1)}, u32[]{:S(2)}, u32[]{:S(2)}) collective-permute-start(bf16[4,64,128]{2,1,0:T(8,128)(2,1)S(1)} %get-tuple-element.64), channel_id=1, source_target_pairs={{0,16},{16,0},{1,17},{17,1},{2,18},{18,2},{3,19},{19,3},{4,20},{20... | collective-permute-start | bytes 196616 | tf_op jit(solution)/shard_map/ppermute | solution.py:24
  23.2 0.7 %collective-permute-done.6.one_keys = bf16[4,64,128]{2,1,0:T(8,128)(2,1)S(1)} collective-permute-done((bf16[4,64,128]{2,1,0:T(8,128)(2,1)S(1)}, bf16[4,64,128]{2,1,0:T(8,128)(2,1)S(1)}, u32[]{:S(2)}, u32[]{:S(2)}) %collective-permute-start.6) | collective-permute-done | bytes 65568 | tf_op jit(solution)/shard_map/ppermute | solution.py:24
  24.1 0.9 %near_forward.1 = (f32[8,1,256]{2,1,0:T(1,128)S(1)}, f32[8,1,256]{2,1,0:T(1,128)S(1)}, f32[8,128,256]{2,1,0:T(8,128)S(1)}, f32[8,128,256]{2,1,0:T(8,128)S(1)}, f...) custom-call(s32[8,1,256]{2,1,0:T(1,128)S(1)} %get-tuple-element.61.first, ...), custom_call_target="tpu_custom_call" | custom-call | flops 1 | tf_op jit(solution)/shard_map/near_forward/pallas_call | solution.py:396
  25.0 2.2 %collective-permute-done.7.back_two = bf16[2,4,128,128]{3,2,1,0:T(8,128)(2,1)S(1)} collective-permute-done((bf16[2,4,128,128]{3,2,1,0:T(8,128)(2,1)S(1)}, bf16[2,4,128,128]{3,2,1,0:T(8,128)(2,1)S(1)}, u32[]{:S(2)}, u32[]{:S(2)}) %collective-permute-start.7) | collective-permute-done | bytes 262176 | tf_op jit(solution)/shard_map/ppermute | solution.py:19
  27.3 1.6 %far_forward_backward.1 = (bf16[8,128,256]{2,1,0:T(8,128)(2,1)S(1)}, f32[8,1,256]{2,1,0:T(1,128)S(1)}, f32[8,1,256]{2,1,0:T(1,128)S(1)}, bf16[8,128,256]{2,1,0:T(8,128)(2,1)S(1)}, bf16[2,4,128,128]{3,2,1,0:T(8,128)(2,1)S(1)}) custom-call(s32[8,1,256]{2,1,0:T(1,128)S(1)} %get-tuple-element.61.first, bf16[16,128,128]{2,1,0:T(8,128)(2,1)S(1)} %get-tuple-element.62.query_head, ...), custom_call_target="tpu_custom_call" | custom-call | flops 1 | tf_op jit(solution)/shard_map/far_forward_backward/pallas_call | solution.py:396
  28.9 3.3 %collective-permute-start.14 = (bf16[2,4,128,128]{3,2,1,0:T(8,128)(2,1)S(1)}, bf16[2,4,128,128]{3,2,1,0:T(8,128)(2,1)S(1)}, u32[]{:S(2)}, u32[]{:S(2)}) collective-permute-start(bf16[2,4,128,128]{3,2,1,0:T(8,128)(2,1)S(1)} %get-tuple-element.96), channel_id=1, source_target_pairs={{2,0},{3,1},{4,2},{5,3},{6,4},{7,5},{8,6},{9,7},{10,8},{11,9},{12,... | collective-permute-start | bytes 786440 | tf_op jit(solution)/shard_map/ppermute | solution.py:19
  32.2 0.5 %one_backward.1 = (bf16[8,128,256]{2,1,0:T(8,128)(2,1)S(1)}, bf16[2,4,64,128]{3,2,1,0:T(8,128)(2,1)S(1)}, bf16[4,64,128]{2,1,0:T(8,128)(2,1)S(1)}, bf16[4,64,128]{2,1,0:T(8,128)(2,1)S(1)}) custom-call(bf16[16,128,128]{2,1,0:T(8,128)(2,1)S(1)} %get-tuple-element.62.query_head, bf16[16,128,128]{2,1,0:T(8,128)(2,1)S(1)} %get-tuple-element.63.grad_head, ...), custom_call_target="tpu_custom_call" | custom-call | flops 1 | tf_op jit(solution)/shard_map/one_backward/pallas_call | solution.py:396
  32.8 0.5 %collective-permute-start.10 = (bf16[4,64,128]{2,1,0:T(8,128)(2,1)S(1)}, bf16[4,64,128]{2,1,0:T(8,128)(2,1)S(1)}, u32[]{:S(2)}, u32[]{:S(2)}) collective-permute-start(bf16[4,64,128]{2,1,0:T(8,128)(2,1)S(1)} %get-tuple-element.86), channel_id=1, source_target_pairs={{0,16},{16,0},{1,17},{17,1},{2,18},{18,2},{3,19},{19,3},{4,20},{20... | collective-permute-start | bytes 196616 | tf_op jit(solution)/shard_map/ppermute | solution.py:24
  33.3 0.7 %collective-permute-done.9.other_keys = bf16[4,64,128]{2,1,0:T(8,128)(2,1)S(1)} collective-permute-done((bf16[4,64,128]{2,1,0:T(8,128)(2,1)S(1)}, bf16[4,64,128]{2,1,0:T(8,128)(2,1)S(1)}, u32[]{:S(2)}, u32[]{:S(2)}) %collective-permute-start.9) | collective-permute-done | bytes 65568 | tf_op jit(solution)/shard_map/ppermute | solution.py:24
  34.2 3.2 %collective-permute-start.16 = (bf16[2,8,64,128]{3,2,1,0:T(8,128)(2,1)S(1)}, bf16[2,8,64,128]{3,2,1,0:T(8,128)(2,1)S(1)}, u32[]{:S(2)}, u32[]{:S(2)}) collective-permute-start(bf16[2,8,64,128]{3,2,1,0:T(8,128)(2,1)S(1)} %join_one.1.after), channel_id=1, source_target_pairs={{1,0},{2,1},{3,2},{4,3},{5,4},{6,5},{7,6},{8,7},{9,8},{10,9},{11,1... | collective-permute-start | bytes 786440 | tf_op jit(solution)/shard_map/ppermute | solution.py:19
  37.4 0.5 own_backward.1
  37.9 0.7 %query_grad.1 = (bf16[16,64,128]{2,1,0:T(8,128)(2,1)S(1)}, bf16[16,64,128]{2,1,0:T(8,128)(2,1)S(1)}, bf16[10,64,128]{2,1,0:T(8,128)(2,1)S(1)}, bf16[11,64,128]{2,1,0:T(8,128)(2,1)S(1)}, bf16[11,64,128]{2,1,0:T(8,128)(2,1)S(1)}) custom-call(bf16[2,4,128,128]{3,2,1,0:T(8,128)(2,1)S(1)} %join_own.1.own, ...), custom_call_target="tpu_custom_call" | custom-call | flops 1 | tf_op jit(solution)/shard_map/query_grad/pallas_call | solution.py:396
  39.4 0.5 %collective-permute-start.15 = (bf16[2,4,64,128]{3,2,1,0:T(8,128)(2,1)S(1)}, bf16[2,4,64,128]{3,2,1,0:T(8,128)(2,1)S(1)}, u32[]{:S(2)}, u32[]{:S(2)}) collective-permute-start(bf16[2,4,64,128]{3,2,1,0:T(8,128)(2,1)S(1)} %get-tuple-element.98), channel_id=1, source_target_pairs={{0,16},{16,0},{1,17},{17,1},{2,18},{18,2},{3,19},{19,3},{4,20},{20... | collective-permute-start | bytes 393224 | tf_op jit(solution)/shard_map/ppermute | solution.py:24
  39.8 0.8 %collective-permute-done.11.first_third = bf16[10,64,128]{2,1,0:T(8,128)(2,1)S(1)} collective-permute-done((bf16[10,64,128]{2,1,0:T(8,128)(2,1)S(1)}, bf16[10,64,128]{2,1,0:T(8,128)(2,1)S(1)}, u32[]{:S(2)}, u32[]{:S(2)}) %collective-permute-start.11) | collective-permute-done | bytes 163872 | tf_op jit(solution)/shard_map/ppermute | solution.py:24
  40.6 1.0 %assemble.1 = (bf16[32,64,128]{2,1,0:T(8,128)(2,1)}, bf16[32,64,128]{2,1,0:T(8,128)(2,1)}, f32[8,128]{1,0:T(8,128)S(1)}) custom-call(bf16[16,64,128]{2,1,0:T(8,128)(2,1)S(1)} %get-tuple-element.88.out_mine, bf16[16,64,128]{2,1,0:T(8,128)(2,1)S(1)} %get-tuple-element.89.query_mine, bf16[10,64,128]{2,1,0:T(8,128)(2,1)S(1)} %collective-permute-done.11.first_third, ...), custom_call_target="tpu_custom_call" | custom-call | flops 1 | tf_op jit(solution)/shard_map/assemble/pallas_call | solution.py:396
  41.7 4.8 %collective-permute-done.16.one_total = bf16[2,8,64,128]{3,2,1,0:T(8,128)(2,1)S(1)} collective-permute-done((bf16[2,8,64,128]{3,2,1,0:T(8,128)(2,1)S(1)}, bf16[2,8,64,128]{3,2,1,0:T(8,128)(2,1)S(1)}, u32[]{:S(2)}, u32[]{:S(2)}) %collective-permute-start.16) | collective-permute-done | bytes 262176 | tf_op jit(solution)/shard_map/ppermute | solution.py:19
  46.5 0.7 %total.1 = (bf16[8,64,128]{2,1,0:T(8,128)(2,1)}, bf16[8,64,128]{2,1,0:T(8,128)(2,1)}) custom-call(f32[2,4,64,128]{3,2,1,0:T(8,128)S(1)} %get-tuple-element.97.sum_mine, bf16[2,4,64,128]{3,2,1,0:T(8,128)(2,1)S(1)} %collective-permute-done.15.sum_other, bf16[2,8,64,128]{3,2,1,0:T(8,128)(2,1)S(1)} %collective-permute-done.16.one_total, ...), custom_call_target="tpu_custom_call" | custom-call | flops 1 | tf_op jit(solution)/shard_map/total/pallas_call | solution.py:396
  (35 shorter events, 2.0 us)
Async XLA Ops:
  0.6 4.6 %copy-start = (bf16[32,64,128]{2,1,0:T(8,128)(2,1)S(1)}, bf16[32,64,128]{2,1,0:T(8,128)(2,1)}, u32[]{:S(2)}) copy-start(bf16[32,64,128]{2,1,0:T(8,128)(2,1)} %queries.3) | copy-start | bytes 1572868
  1.7 20.9 %collective-permute-start.2 = (bf16[2,8,64,128]{3,2,1,0:T(8,128)(2,1)S(1)}, bf16[2,8,64,128]{3,2,1,0:T(8,128)(2,1)S(1)}, u32[]{:S(2)}, u32[]{:S(2)}) collective-permute-start(bf16[2,8,64,128]{3,2,1,0:T(8,128)(2,1)S(1)} %pad_maximum_fusion.block.own.after), channel_id=1, source_target_pairs={{1,2},{3,4},{5,6},{7,8},{9,10},{11,12},{13,14},{17,18},{19,20},{21... | collective-permute-start | bytes 786440 | tf_op jit(solution)/shard_map/ppermute | solution.py:423
  5.1 2.2 %collective-permute-start = (bf16[4,64,128]{2,1,0:T(8,128)(2,1)S(1)}, bf16[4,64,128]{2,1,0:T(8,128)(2,1)S(1)}, u32[]{:S(2)}, u32[]{:S(2)}) collective-permute-start(bf16[4,64,128]{2,1,0:T(8,128)(2,1)S(1)} %get-tuple-element.53), channel_id=1, source_target_pairs={{0,16},{16,0},{1,17},{17,1},{2,18},{18,2},{3,19},{19,3},{4,20},{20... | collective-permute-start | bytes 196616 | tf_op jit(solution)/shard_map/ppermute | solution.py:24
  5.2 1.0 %copy-start.1 = (bf16[32,64,128]{2,1,0:T(8,128)(2,1)S(1)}, bf16[32,64,128]{2,1,0:T(8,128)(2,1)}, u32[]{:S(2)}) copy-start(bf16[32,64,128]{2,1,0:T(8,128)(2,1)} %grads.3) | copy-start | bytes 1572868
  6.3 14.7 %collective-permute-start.4 = (bf16[11,64,128]{2,1,0:T(8,128)(2,1)S(1)}, bf16[11,64,128]{2,1,0:T(8,128)(2,1)S(1)}, u32[]{:S(2)}, u32[]{:S(2)}) collective-permute-start(bf16[11,64,128]{2,1,0:T(8,128)(2,1)S(1)} %get-tuple-element.56), channel_id=1, source_target_pairs={{0,16},{16,0},{1,17},{17,1},{2,18},{18,2},{3,19},{19,3},{4,20},{20... | collective-permute-start | bytes 540680 | tf_op jit(solution)/shard_map/ppermute | solution.py:24
  6.9 14.1 %collective-permute-start.5 = (bf16[11,64,128]{2,1,0:T(8,128)(2,1)S(1)}, bf16[11,64,128]{2,1,0:T(8,128)(2,1)S(1)}, u32[]{:S(2)}, u32[]{:S(2)}) collective-permute-start(bf16[11,64,128]{2,1,0:T(8,128)(2,1)S(1)} %get-tuple-element.57), channel_id=1, source_target_pairs={{0,16},{16,0},{1,17},{17,1},{2,18},{18,2},{3,19},{19,3},{4,20},{20... | collective-permute-start | bytes 540680 | tf_op jit(solution)/shard_map/ppermute | solution.py:24
  6.9 14.0 %collective-permute-start.3 = (bf16[10,64,128]{2,1,0:T(8,128)(2,1)S(1)}, bf16[10,64,128]{2,1,0:T(8,128)(2,1)S(1)}, u32[]{:S(2)}, u32[]{:S(2)}) collective-permute-start(bf16[10,64,128]{2,1,0:T(8,128)(2,1)S(1)} %get-tuple-element.55), channel_id=1, source_target_pairs={{0,16},{16,0},{1,17},{17,1},{2,18},{18,2},{3,19},{19,3},{4,20},{20... | collective-permute-start | bytes 491528 | tf_op jit(solution)/shard_map/ppermute | solution.py:24
  7.4 10.1 %collective-permute-start.1 = (bf16[4,64,128]{2,1,0:T(8,128)(2,1)S(1)}, bf16[4,64,128]{2,1,0:T(8,128)(2,1)S(1)}, u32[]{:S(2)}, u32[]{:S(2)}) collective-permute-start(bf16[4,64,128]{2,1,0:T(8,128)(2,1)S(1)} %get-tuple-element.54), channel_id=1, source_target_pairs={{0,16},{16,0},{1,17},{17,1},{2,18},{18,2},{3,19},{19,3},{4,20},{20... | collective-permute-start | bytes 196616 | tf_op jit(solution)/shard_map/ppermute | solution.py:24
  16.8 4.2 %copy-start.2 = (bf16[32,64,128]{2,1,0:T(8,128)(2,1)S(1)}, bf16[32,64,128]{2,1,0:T(8,128)(2,1)}, u32[]{:S(2)}) copy-start(bf16[32,64,128]{2,1,0:T(8,128)(2,1)} %grads.3) | copy-start | bytes 1572868
  17.5 3.5 %copy-start.3 = (s32[32]{0:T(128)S(1)}, s32[32]{0:T(128)}, u32[]{:S(2)}) copy-start(s32[32]{0:T(128)} %spans.1) | copy-start | bytes 388
  17.5 9.7 %collective-permute-start.7 = (bf16[2,4,128,128]{3,2,1,0:T(8,128)(2,1)S(1)}, bf16[2,4,128,128]{3,2,1,0:T(8,128)(2,1)S(1)}, u32[]{:S(2)}, u32[]{:S(2)}) collective-permute-start(bf16[2,4,128,128]{3,2,1,0:T(8,128)(2,1)S(1)} %join_own.1.own), channel_id=1, source_target_pairs={{0,2},{1,3},{2,4},{3,5},{4,6},{5,7},{6,8},{7,9},{8,10},{9,11},{10,... | collective-permute-start | bytes 786440 | tf_op jit(solution)/shard_map/ppermute | solution.py:19
  22.6 1.3 %collective-permute-start.6 = (bf16[4,64,128]{2,1,0:T(8,128)(2,1)S(1)}, bf16[4,64,128]{2,1,0:T(8,128)(2,1)S(1)}, u32[]{:S(2)}, u32[]{:S(2)}) collective-permute-start(bf16[4,64,128]{2,1,0:T(8,128)(2,1)S(1)} %get-tuple-element.60), channel_id=1, source_target_pairs={{0,16},{16,0},{1,17},{17,1},{2,18},{18,2},{3,19},{19,3},{4,20},{20... | collective-permute-start | bytes 196616 | tf_op jit(solution)/shard_map/ppermute | solution.py:24
  22.7 1.4 %collective-permute-start.8 = (bf16[4,64,128]{2,1,0:T(8,128)(2,1)S(1)}, bf16[4,64,128]{2,1,0:T(8,128)(2,1)S(1)}, u32[]{:S(2)}, u32[]{:S(2)}) collective-permute-start(bf16[4,64,128]{2,1,0:T(8,128)(2,1)S(1)} %get-tuple-element.64), channel_id=1, source_target_pairs={{0,16},{16,0},{1,17},{17,1},{2,18},{18,2},{3,19},{19,3},{4,20},{20... | collective-permute-start | bytes 196616 | tf_op jit(solution)/shard_map/ppermute | solution.py:24
  28.9 10.4 %collective-permute-start.14 = (bf16[2,4,128,128]{3,2,1,0:T(8,128)(2,1)S(1)}, bf16[2,4,128,128]{3,2,1,0:T(8,128)(2,1)S(1)}, u32[]{:S(2)}, u32[]{:S(2)}) collective-permute-start(bf16[2,4,128,128]{3,2,1,0:T(8,128)(2,1)S(1)} %get-tuple-element.96), channel_id=1, source_target_pairs={{2,0},{3,1},{4,2},{5,3},{6,4},{7,5},{8,6},{9,7},{10,8},{11,9},{12,... | collective-permute-start | bytes 786440 | tf_op jit(solution)/shard_map/ppermute | solution.py:19
  32.7 1.3 %collective-permute-start.9 = (bf16[4,64,128]{2,1,0:T(8,128)(2,1)S(1)}, bf16[4,64,128]{2,1,0:T(8,128)(2,1)S(1)}, u32[]{:S(2)}, u32[]{:S(2)}) collective-permute-start(bf16[4,64,128]{2,1,0:T(8,128)(2,1)S(1)} %get-tuple-element.85), channel_id=1, source_target_pairs={{0,16},{16,0},{1,17},{17,1},{2,18},{18,2},{3,19},{19,3},{4,20},{20... | collective-permute-start | bytes 196616 | tf_op jit(solution)/shard_map/ppermute | solution.py:24
  32.8 1.4 %collective-permute-start.10 = (bf16[4,64,128]{2,1,0:T(8,128)(2,1)S(1)}, bf16[4,64,128]{2,1,0:T(8,128)(2,1)S(1)}, u32[]{:S(2)}, u32[]{:S(2)}) collective-permute-start(bf16[4,64,128]{2,1,0:T(8,128)(2,1)S(1)} %get-tuple-element.86), channel_id=1, source_target_pairs={{0,16},{16,0},{1,17},{17,1},{2,18},{18,2},{3,19},{19,3},{4,20},{20... | collective-permute-start | bytes 196616 | tf_op jit(solution)/shard_map/ppermute | solution.py:24
  34.2 12.3 %collective-permute-start.16 = (bf16[2,8,64,128]{3,2,1,0:T(8,128)(2,1)S(1)}, bf16[2,8,64,128]{3,2,1,0:T(8,128)(2,1)S(1)}, u32[]{:S(2)}, u32[]{:S(2)}) collective-permute-start(bf16[2,8,64,128]{3,2,1,0:T(8,128)(2,1)S(1)} %join_one.1.after), channel_id=1, source_target_pairs={{1,0},{2,1},{3,2},{4,3},{5,4},{6,5},{7,6},{8,7},{9,8},{10,9},{11,1... | collective-permute-start | bytes 786440 | tf_op jit(solution)/shard_map/ppermute | solution.py:19
  38.6 2.0 %collective-permute-start.12 = (bf16[11,64,128]{2,1,0:T(8,128)(2,1)S(1)}, bf16[11,64,128]{2,1,0:T(8,128)(2,1)S(1)}, u32[]{:S(2)}, u32[]{:S(2)}) collective-permute-start(bf16[11,64,128]{2,1,0:T(8,128)(2,1)S(1)} %get-tuple-element.91), channel_id=1, source_target_pairs={{0,16},{16,0},{1,17},{17,1},{2,18},{18,2},{3,19},{19,3},{4,20},{20... | collective-permute-start | bytes 540680 | tf_op jit(solution)/shard_map/ppermute | solution.py:24
  38.8 1.8 %collective-permute-start.13 = (bf16[11,64,128]{2,1,0:T(8,128)(2,1)S(1)}, bf16[11,64,128]{2,1,0:T(8,128)(2,1)S(1)}, u32[]{:S(2)}, u32[]{:S(2)}) collective-permute-start(bf16[11,64,128]{2,1,0:T(8,128)(2,1)S(1)} %get-tuple-element.92), channel_id=1, source_target_pairs={{0,16},{16,0},{1,17},{17,1},{2,18},{18,2},{3,19},{19,3},{4,20},{20... | collective-permute-start | bytes 540680 | tf_op jit(solution)/shard_map/ppermute | solution.py:24
  39.2 1.4 %collective-permute-start.11 = (bf16[10,64,128]{2,1,0:T(8,128)(2,1)S(1)}, bf16[10,64,128]{2,1,0:T(8,128)(2,1)S(1)}, u32[]{:S(2)}, u32[]{:S(2)}) collective-permute-start(bf16[10,64,128]{2,1,0:T(8,128)(2,1)S(1)} %get-tuple-element.90), channel_id=1, source_target_pairs={{0,16},{16,0},{1,17},{17,1},{2,18},{18,2},{3,19},{19,3},{4,20},{20... | collective-permute-start | bytes 491528 | tf_op jit(solution)/shard_map/ppermute | solution.py:24
  39.4 7.2 %collective-permute-start.15 = (bf16[2,4,64,128]{3,2,1,0:T(8,128)(2,1)S(1)}, bf16[2,4,64,128]{3,2,1,0:T(8,128)(2,1)S(1)}, u32[]{:S(2)}, u32[]{:S(2)}) collective-permute-start(bf16[2,4,64,128]{3,2,1,0:T(8,128)(2,1)S(1)} %get-tuple-element.98), channel_id=1, source_target_pairs={{0,16},{16,0},{1,17},{17,1},{2,18},{18,2},{3,19},{19,3},{4,20},{20... | collective-permute-start | bytes 393224 | tf_op jit(solution)/shard_map/ppermute | solution.py:24

commit v12 on v8

--- a/solution.py
+++ b/solution.py
@@ -222,13 +222,18 @@
         return scores, prob_grad
 
     def softmax(n, scores, prob_grad):
-        g = n * groups // chunks
         scores = masked(scores * (scale * math.log2(math.e)), first[n], 1)
         row_max = jnp.maximum(near_max[n], jnp.max(scores, axis=0, keepdims=True))
         weights = jnp.exp2(scores - row_max)
         rescale = jnp.exp2(near_max[n] - row_max)
         inverse = 1.0 / (near_total[n] * rescale + jnp.sum(weights, axis=0, keepdims=True))
-        weighted = matmul(back_one[1, g], weights.astype(jnp.bfloat16), (0, 0))
+        weighted = matmul(
+            back_one[1, n * groups // chunks], weights.astype(jnp.bfloat16), (0, 0)
+        )
+        near_factor[n] = rescale * inverse
+        return prob_grad, weights, weighted, rescale, inverse
+
+    def differentiate(n, prob_grad, weights, weighted, rescale, inverse):
         attended = ((near_out[n] * rescale + weighted) * inverse).astype(jnp.bfloat16)
         delta = jnp.sum(
             grad_rows[n].astype(jnp.float32) * attended.astype(jnp.float32), axis=0, keepdims=True
@@ -237,36 +242,31 @@
         score_grad = (prob * (prob_grad - delta)).astype(jnp.bfloat16)
         attended_rows[n] = attended
         row_delta[n] = delta
-        near_factor[n] = rescale * inverse
         one_grad[n] = score_grad
         return score_grad, prob.astype(jnp.bfloat16)
-
-    accumulate = accumulator(query_head, grad_head, chunks, groups)
 
     def store(g, key_part, value_part):
         one_part[0, g] = (key_part * scale).astype(jnp.bfloat16)
         one_part[1, g] = value_part.astype(jnp.bfloat16)
 
-    pipelined(chunks, products, softmax, lambda n, *halves: accumulate(n, *halves, store))
-
-
-def pipelined(chunks, before, middle, after):
-    ready = before(0)
-    done = None
-    for n in range(chunks):
-        upcoming = before(n + 1) if n + 1 < chunks else None
-        result = middle(n, *ready)
-        if done is not None:
-            after(n - 1, *done)
-        ready, done = upcoming, result
-    after(chunks - 1, *done)
-
-
-def accumulator(query_head, grad_head, chunks, groups):
+    accumulate = accumulator(query_head, grad_head, chunks, groups, store)
+    pipelined(chunks, products, softmax, differentiate, accumulate)
+
+
+def pipelined(chunks, *stages):
+    ready = [{} for _ in range(len(stages) + 1)]
+    for step in range(chunks + len(stages) - 1):
+        for depth, stage in enumerate(stages):
+            n = step - depth
+            if 0 <= n < chunks:
+                ready[depth + 1][n] = stage(n, *ready[depth].pop(n, ())) or ()
+
+
+def accumulator(query_head, grad_head, chunks, groups, store):
     count = query_head.shape[0] // chunks
     parts = {}
 
-    def accumulate(n, score_grad, half, store):
+    def accumulate(n, score_grad, half):
         g = n * groups // chunks
         key_part = matmul(score_grad, grouped(query_head, n, count), (1, 0))
         value_part = matmul(half, grouped(grad_head, n, count), (1, 0))
@@ -281,21 +281,26 @@
 
 def two_backward_kernel(
     query_head, grad_head, near_weights, near_prob_grad, near_factor, row_delta,
-    two_grad, two_part,
+    two_grad, two_mine, send_keys, send_values,
 ):
     chunks = near_weights.shape[0]
-    groups, _, width = two_part.shape[1:]
-    accumulate = accumulator(query_head, grad_head, chunks, groups)
-
-    def store(g, key_part, value_part):
-        two_part[0, g] = (key_part * width ** (-0.5)).astype(jnp.bfloat16)
-        two_part[1, g] = value_part.astype(jnp.bfloat16)
-
-    for n in range(chunks):
+    groups, length, width = two_mine.shape[1:]
+
+    def differentiate(n):
         prob = near_weights[n] * near_factor[n]
         score_grad = (prob * (near_prob_grad[n] - row_delta[n])).astype(jnp.bfloat16)
         two_grad[n] = score_grad
-        accumulate(n, score_grad, prob.astype(jnp.bfloat16), store)
+        return score_grad, prob.astype(jnp.bfloat16)
+
+    def store(g, key_part, value_part):
+        for index, (part, send) in enumerate(
+            ((key_part * width ** (-0.5), send_keys), (value_part, send_values))
+        ):
+            two_mine[index, g] = part[:length].astype(jnp.bfloat16)
+            send[g] = part[length:].astype(jnp.bfloat16)
+
+    accumulate = accumulator(query_head, grad_head, chunks, groups, store)
+    pipelined(chunks, differentiate, accumulate)
 
 
 def own_backward_kernel(
@@ -304,24 +309,26 @@
 ):
     chunks = own_weights.shape[0]
     groups, _, width = own_part.shape[1:]
-    accumulate = accumulator(query_head, grad_head, chunks, groups)
+
+    def differentiate(n):
+        prob = own_weights[n] * (own_factor[n] * near_factor[n])
+        score_grad = (prob * (own_prob_grad[n] - row_delta[n])).astype(jnp.bfloat16)
+        own_grad[n] = score_grad
+        return score_grad, prob.astype(jnp.bfloat16)
 
     def store(g, key_part, value_part):
         own_part[0, g] = key_part * width ** (-0.5)
         own_part[1, g] = value_part
 
-    for n in range(chunks):
-        prob = own_weights[n] * (own_factor[n] * near_factor[n])
-        score_grad = (prob * (own_prob_grad[n] - row_delta[n])).astype(jnp.bfloat16)
-        own_grad[n] = score_grad
-        accumulate(n, score_grad, prob.astype(jnp.bfloat16), store)
-
-
-def join_one_kernel(one_part, one_other, one_joined):
-    groups, tokens = one_part.shape[1:3]
-    length = tokens // 2
-    one_joined[:, my_heads(groups)] = one_part[:, :, pl.ds(0, length)]
-    one_joined[:, other_heads(groups)] = one_other[:, :, pl.ds(length, length)]
+    accumulate = accumulator(query_head, grad_head, chunks, groups, store)
+    pipelined(chunks, differentiate, accumulate)
+
+
+def join_two_kernel(two_mine, other_keys, other_values, two_part):
+    groups = two_mine.shape[1]
+    two_part[:, my_heads(groups)] = two_mine[...]
+    two_part[0, other_heads(groups)] = other_keys[...]
+    two_part[1, other_heads(groups)] = other_values[...]
 
 
 def query_kernel(
@@ -359,20 +366,20 @@
     token[...] = jnp.zeros(token.shape, token.dtype)
 
 
-def own_sum_kernel(own_part, two_total, sum_mine, sum_send):
+def own_sum_kernel(own_part, one_total, sum_mine, sum_send):
     length = sum_mine.shape[2]
-    total = own_part[...] + two_total[...].astype(jnp.float32)
+    total = own_part[...] + one_total[...].astype(jnp.float32)
     sum_mine[...] = total[:, :, :length]
     sum_send[...] = total[:, :, length:].astype(jnp.bfloat16)
 
 
-def final_kernel(sum_mine, sum_other, one_total, after, key_grad, value_grad):
+def final_kernel(sum_mine, sum_other, two_total, after, key_grad, value_grad):
     groups = sum_mine.shape[1]
     mine, other = my_heads(groups), other_heads(groups)
     for index, result in enumerate((key_grad, value_grad)):
-        total = sum_mine[index] + one_total[index, mine].astype(jnp.float32)
+        total = sum_mine[index] + two_total[index, mine].astype(jnp.float32)
         result[mine] = total.astype(jnp.bfloat16)
-        total = sum_other[index].astype(jnp.float32) + one_total[index, other].astype(jnp.float32)
+        total = sum_other[index].astype(jnp.float32) + two_total[index, other].astype(jnp.float32)
         result[other] = total.astype(jnp.bfloat16)
 
 
@@ -452,29 +459,33 @@
         (first, query_head, grad_head, back_two, *two_other, own_max, own_total, own_out),
     )
     back_one, near_max = lax.optimization_barrier((back_one, near_max))
-    attended_rows, row_delta, near_factor, one_grad, chip_part = call(
+    attended_rows, row_delta, near_factor, one_grad, one_part = call(
         last_kernel,
         "last_forward_backward",
         [rows_of(width, half), stat, stat, rows_of(tokens, half), chip_pair],
         (first, query_head, grad_head, back_one, grad_rows, near_max, near_total, near_out),
     )
-    chip_other = swapped(chip_part, "head")
-    two_grad, two_part = call(
+    one_total = shifted(one_part, "seq", -1)
+    two_grad, part_mine, *part_sends = call(
         two_backward_kernel,
         "two_backward",
-        [rows_of(tokens, half), chip_pair],
+        [rows_of(tokens, half), half_pair, half_block, half_block],
         (query_head, grad_head, near_weights, near_prob_grad, near_factor, row_delta),
     )
+    (two_part,) = call(
+        join_two_kernel,
+        "join_two",
+        [whole_pair],
+        (part_mine, *[swapped(send, "head") for send in part_sends]),
+    )
     two_total = shifted(two_part, "seq", -2)
-    (one_part,) = call(join_one_kernel, "join_one", [whole_pair], (chip_part, chip_other))
-    one_total = shifted(one_part, "seq", -1)
     own_grad, own_part = call(
         own_backward_kernel,
         "own_backward",
         [rows_of(tokens, half), (chip_pair[0], full)],
         (
             query_head, grad_head, own_weights, own_prob_grad, near_factor, own_factor, row_delta,
-            one_part,
+            two_part,
         ),
     )
     out_mine, query_mine, *sends = call(
@@ -491,13 +502,13 @@
         (out_mine, query_mine, *[swapped(send, "head") for send in sends]),
     )
     sum_mine, sum_send = call(
-        own_sum_kernel, "own_sum", [(half_pair[0], full), half_pair], (own_part, two_total)
+        own_sum_kernel, "own_sum", [(half_pair[0], full), half_pair], (own_part, one_total)
     )
     key_grad, value_grad = call(
         final_kernel,
         "total",
         [(key_matrix.shape, half)] * 2,
-        (sum_mine, swapped(sum_send, "head"), one_total, token),
+        (sum_mine, swapped(sum_send, "head"), two_total, token),
     )
     return (attn_out, query_grad, key_grad, value_grad)
 

time: 38.5 us -> 38.4 us (level)
  the two profiles are of different devices: /device:TPU:3 before, /device:TPU:27 now
where the time goes in v12:
time: 38.4 us; the launch traced here: 38.2 us
  starting transfers between devices  17.1 us (45%)
  waiting for transfers between devices  10.8 us (28%)
  Pallas kernels  7.71 us (20%)
  between operations  1.45 us (4%)
  other arithmetic  1.05 us (3%)
    ppermute x4, starting transfers between devices, shifted(): return lax.ppermute(block, axis, route)  11.8 us
    pallas_call x14, Pallas kernels, call(): pl.pallas_call(kernel, out_shape=tuple((jax.ShapeDtypeStruct(shape, kind)...  7.71 us
    ppermute x4, waiting for transfers between devices, shifted(): return lax.ppermute(block, axis, route)  6.69 us
    ppermute x13, starting transfers between devices, swapped(): return lax.ppermute(block, axis, [(i, count - 1 - i) for i in range(count)])  5.35 us
    ppermute x13, waiting for transfers between devices, swapped(): return lax.ppermute(block, axis, [(i, count - 1 - i) for i in range(count)])  4.13 us
    another operation x1, other arithmetic, shards(): own = jnp.stack([key_matrix, value_matrix])  1.05 us
  transfers between devices with their start and end apart: 17, of which 10 were waited for; matrix products, arithmetic and copies ran while one was open for 0% of the time, Pallas kernels for 14%

profile of v12, /device:TPU:27, one launch (start us, length us, event | category | flops | bytes accessed | tf_op | source)
XLA Modules:
  0.0 38.2 jit_solution(17691124770836101803)
XLA Ops:
  0.6 1.1 %pad_maximum_fusion.block.own.after = bf16[2,8,64,128]{3,2,1,0:T(8,128)(2,1)S(1)} fusion(bf16[1,8,64,128]{3,2,1,0:T(8,128)(2,1)} %bitcast.2, bf16[1,8,64,128]{3,2,1,0:T(8,128)(2,1)} %bitcast.3), kind=kLoop, calls=%fused_computation | loop fusion | flops 131072 | bytes 524288 | tf_op jit(solution)/shard_map/stack | solution.py:423
  1.7 3.3 %collective-permute-start.3 = (bf16[2,8,64,128]{3,2,1,0:T(8,128)(2,1)S(1)}, bf16[2,8,64,128]{3,2,1,0:T(8,128)(2,1)S(1)}, u32[]{:S(2)}, u32[]{:S(2)}) collective-permute-start(bf16[2,8,64,128]{3,2,1,0:T(8,128)(2,1)S(1)} %pad_maximum_fusion.block.own.after), channel_id=1, source_target_pairs={{0,2},{1,3},{2,4},{3,5},{4,6},{5,7},{6,8},{7,9},{8,10},{9,11},{10,... | collective-permute-start | bytes 786440 | tf_op jit(solution)/shard_map/ppermute | solution.py:19
  5.0 1.0 %collective-permute-start = (bf16[4,64,128]{2,1,0:T(8,128)(2,1)S(1)}, bf16[4,64,128]{2,1,0:T(8,128)(2,1)S(1)}, u32[]{:S(2)}, u32[]{:S(2)}) collective-permute-start(bf16[4,64,128]{2,1,0:T(8,128)(2,1)S(1)} %get-tuple-element.53), channel_id=1, source_target_pairs={{0,16},{16,0},{1,17},{17,1},{2,18},{18,2},{3,19},{19,3},{4,20},{20... | collective-permute-start | bytes 196616 | tf_op jit(solution)/shard_map/ppermute | solution.py:24
  6.1 0.8 %collective-permute-done.other_keys = bf16[4,64,128]{2,1,0:T(8,128)(2,1)S(1)} collective-permute-done((bf16[4,64,128]{2,1,0:T(8,128)(2,1)S(1)}, bf16[4,64,128]{2,1,0:T(8,128)(2,1)S(1)}, u32[]{:S(2)}, u32[]{:S(2)}) %collective-permute-start) | collective-permute-done | bytes 65568 | tf_op jit(solution)/shard_map/ppermute | solution.py:24
  7.3 1.9 %collective-permute-start.2 = (bf16[2,4,128,128]{3,2,1,0:T(8,128)(2,1)S(1)}, bf16[2,4,128,128]{3,2,1,0:T(8,128)(2,1)S(1)}, u32[]{:S(2)}, u32[]{:S(2)}) collective-permute-start(bf16[2,4,128,128]{3,2,1,0:T(8,128)(2,1)S(1)} %join_own.1.own), channel_id=1, source_target_pairs={{0,1},{1,2},{2,3},{3,4},{4,5},{5,6},{6,7},{7,8},{8,9},{9,10},{10,1... | collective-permute-start | bytes 786440 | tf_op jit(solution)/shard_map/ppermute | solution.py:19
  10.7 0.6 %collective-permute-done.4.first_third = bf16[10,64,128]{2,1,0:T(8,128)(2,1)S(1)} collective-permute-done((bf16[10,64,128]{2,1,0:T(8,128)(2,1)S(1)}, bf16[10,64,128]{2,1,0:T(8,128)(2,1)S(1)}, u32[]{:S(2)}, u32[]{:S(2)}) %collective-permute-start.4) | collective-permute-done | bytes 163872 | tf_op jit(solution)/shard_map/ppermute | solution.py:24
  11.3 1.5 %own_block.1 = (bf16[16,128,128]{2,1,0:T(8,128)(2,1)S(1)}, bf16[16,128,128]{2,1,0:T(8,128)(2,1)S(1)}, bf16[8,128,256]{2,1,0:T(8,128)(2,1)S(1)}, s32[8,1,256]{2,1...) custom-call(s32[32]{0:T(128)S(1)} %copy-done.2, ...), custom_call_target="tpu_custom_call" | custom-call | flops 1 | tf_op jit(solution)/shard_map/own_block/pallas_call | solution.py:400
  12.9 0.6 %collective-permute-start.7 = (bf16[4,64,128]{2,1,0:T(8,128)(2,1)S(1)}, bf16[4,64,128]{2,1,0:T(8,128)(2,1)S(1)}, u32[]{:S(2)}, u32[]{:S(2)}) collective-permute-start(bf16[4,64,128]{2,1,0:T(8,128)(2,1)S(1)} %get-tuple-element.63), channel_id=1, source_target_pairs={{0,16},{16,0},{1,17},{17,1},{2,18},{18,2},{3,19},{19,3},{4,20},{20... | collective-permute-start | bytes 196616 | tf_op jit(solution)/shard_map/ppermute | solution.py:24
  13.6 0.8 %collective-permute-done.7.two_keys = bf16[4,64,128]{2,1,0:T(8,128)(2,1)S(1)} collective-permute-done((bf16[4,64,128]{2,1,0:T(8,128)(2,1)S(1)}, bf16[4,64,128]{2,1,0:T(8,128)(2,1)S(1)}, u32[]{:S(2)}, u32[]{:S(2)}) %collective-permute-start.7) | collective-permute-done | bytes 65568 | tf_op jit(solution)/shard_map/ppermute | solution.py:24
  14.8 0.9 %near_forward.1 = (f32[8,1,256]{2,1,0:T(1,128)S(1)}, f32[8,1,256]{2,1,0:T(1,128)S(1)}, f32[8,128,256]{2,1,0:T(8,128)S(1)}, f32[8,128,256]{2,1,0:T(8,128)S(1)}, f...) custom-call(s32[8,1,256]{2,1,0:T(1,128)S(1)} %get-tuple-element.59.first, ...), custom_call_target="tpu_custom_call" | custom-call | flops 1 | tf_op jit(solution)/shard_map/near_forward/pallas_call | solution.py:400
  15.7 1.3 %collective-permute-done.2.back_one = bf16[2,4,128,128]{3,2,1,0:T(8,128)(2,1)S(1)} collective-permute-done((bf16[2,4,128,128]{3,2,1,0:T(8,128)(2,1)S(1)}, bf16[2,4,128,128]{3,2,1,0:T(8,128)(2,1)S(1)}, u32[]{:S(2)}, u32[]{:S(2)}) %collective-permute-start.2) | collective-permute-done | bytes 262176 | tf_op jit(solution)/shard_map/ppermute | solution.py:19
  17.0 1.5 %last_forward_backward.1 = (bf16[8,128,256]{2,1,0:T(8,128)(2,1)S(1)}, f32[8,1,256]{2,1,0:T(1,128)S(1)}, f32[8,1,256]{2,1,0:T(1,128)S(1)}, bf16[8,128,256]{2,1,0:T(8,128)(2,1)S(1)}, bf16[2,4,128,128]{3,2,1,0:T(8,128)(2,1)S(1)}) custom-call(s32[8,1,256]{2,1,0:T(1,128)S(1)} %get-tuple-element.59.first, bf16[16,128,128]{2,1,0:T(8,128)(2,1)S(1)} %get-tuple-element.60.query_head, ...), custom_call_target="tpu_custom_call" | custom-call | flops 1 | tf_op jit(solution)/shard_map/last_forward_backward/pallas_call | solution.py:400
  18.5 4.6 %collective-permute-start.14 = (bf16[2,4,128,128]{3,2,1,0:T(8,128)(2,1)S(1)}, bf16[2,4,128,128]{3,2,1,0:T(8,128)(2,1)S(1)}, u32[]{:S(2)}, u32[]{:S(2)}) collective-permute-start(bf16[2,4,128,128]{3,2,1,0:T(8,128)(2,1)S(1)} %get-tuple-element.96), channel_id=1, source_target_pairs={{1,0},{2,1},{3,2},{4,3},{5,4},{6,5},{7,6},{8,7},{9,8},{10,9},{11,1... | collective-permute-start | bytes 786440 | tf_op jit(solution)/shard_map/ppermute | solution.py:19
  23.1 0.5 %two_backward.1 = (bf16[8,128,256]{2,1,0:T(8,128)(2,1)S(1)}, bf16[2,4,64,128]{3,2,1,0:T(8,128)(2,1)S(1)}, bf16[4,64,128]{2,1,0:T(8,128)(2,1)S(1)}, bf16[4,64,128]{2,1,0:T(8,128)(2,1)S(1)}) custom-call(bf16[16,128,128]{2,1,0:T(8,128)(2,1)S(1)} %get-tuple-element.60.query_head, bf16[16,128,128]{2,1,0:T(8,128)(2,1)S(1)} %get-tuple-element.61.grad_head, ...), custom_call_target="tpu_custom_call" | custom-call | flops 1 | tf_op jit(solution)/shard_map/two_backward/pallas_call | solution.py:400
  23.7 0.8 %collective-permute-start.9 = (bf16[4,64,128]{2,1,0:T(8,128)(2,1)S(1)}, bf16[4,64,128]{2,1,0:T(8,128)(2,1)S(1)}, u32[]{:S(2)}, u32[]{:S(2)}) collective-permute-start(bf16[4,64,128]{2,1,0:T(8,128)(2,1)S(1)} %get-tuple-element.85), channel_id=1, source_target_pairs={{0,16},{16,0},{1,17},{17,1},{2,18},{18,2},{3,19},{19,3},{4,20},{20... | collective-permute-start | bytes 196616 | tf_op jit(solution)/shard_map/ppermute | solution.py:24
  24.5 0.8 %collective-permute-done.9.other_keys = bf16[4,64,128]{2,1,0:T(8,128)(2,1)S(1)} collective-permute-done((bf16[4,64,128]{2,1,0:T(8,128)(2,1)S(1)}, bf16[4,64,128]{2,1,0:T(8,128)(2,1)S(1)}, u32[]{:S(2)}, u32[]{:S(2)}) %collective-permute-start.9) | collective-permute-done | bytes 65568 | tf_op jit(solution)/shard_map/ppermute | solution.py:24
  25.8 2.0 %collective-permute-start.16 = (bf16[2,8,64,128]{3,2,1,0:T(8,128)(2,1)S(1)}, bf16[2,8,64,128]{3,2,1,0:T(8,128)(2,1)S(1)}, u32[]{:S(2)}, u32[]{:S(2)}) collective-permute-start(bf16[2,8,64,128]{3,2,1,0:T(8,128)(2,1)S(1)} %join_two.1.after), channel_id=1, source_target_pairs={{2,0},{3,1},{4,2},{5,3},{6,4},{7,5},{8,6},{9,7},{10,8},{11,9},{12,... | collective-permute-start | bytes 786440 | tf_op jit(solution)/shard_map/ppermute | solution.py:19
  28.2 0.8 %query_grad.1 = (bf16[16,64,128]{2,1,0:T(8,128)(2,1)S(1)}, bf16[16,64,128]{2,1,0:T(8,128)(2,1)S(1)}, bf16[10,64,128]{2,1,0:T(8,128)(2,1)S(1)}, bf16[11,64,128]{2,1,0:T(8,128)(2,1)S(1)}, bf16[11,64,128]{2,1,0:T(8,128)(2,1)S(1)}) custom-call(bf16[2,4,128,128]{3,2,1,0:T(8,128)(2,1)S(1)} %join_own.1.own, ...), custom_call_target="tpu_custom_call" | custom-call | flops 1 | tf_op jit(solution)/shard_map/query_grad/pallas_call | solution.py:400
  29.0 0.5 %collective-permute-start.12 = (bf16[11,64,128]{2,1,0:T(8,128)(2,1)S(1)}, bf16[11,64,128]{2,1,0:T(8,128)(2,1)S(1)}, u32[]{:S(2)}, u32[]{:S(2)}) collective-permute-start(bf16[11,64,128]{2,1,0:T(8,128)(2,1)S(1)} %get-tuple-element.91), channel_id=1, source_target_pairs={{0,16},{16,0},{1,17},{17,1},{2,18},{18,2},{3,19},{19,3},{4,20},{20... | collective-permute-start | bytes 540680 | tf_op jit(solution)/shard_map/ppermute | solution.py:24
  30.0 1.6 %collective-permute-done.14.one_total = bf16[2,4,128,128]{3,2,1,0:T(8,128)(2,1)S(1)} collective-permute-done((bf16[2,4,128,128]{3,2,1,0:T(8,128)(2,1)S(1)}, bf16[2,4,128,128]{3,2,1,0:T(8,128)(2,1)S(1)}, u32[]{:S(2)}, u32[]{:S(2)}) %collective-permute-start.14) | collective-permute-done | bytes 262176 | tf_op jit(solution)/shard_map/ppermute | solution.py:19
  31.6 0.9 %collective-permute-start.15 = (bf16[2,4,64,128]{3,2,1,0:T(8,128)(2,1)S(1)}, bf16[2,4,64,128]{3,2,1,0:T(8,128)(2,1)S(1)}, u32[]{:S(2)}, u32[]{:S(2)}) collective-permute-start(bf16[2,4,64,128]{3,2,1,0:T(8,128)(2,1)S(1)} %get-tuple-element.98), channel_id=1, source_target_pairs={{0,16},{16,0},{1,17},{17,1},{2,18},{18,2},{3,19},{19,3},{4,20},{20... | collective-permute-start | bytes 393224 | tf_op jit(solution)/shard_map/ppermute | solution.py:24
  32.5 1.0 %assemble.1 = (bf16[32,64,128]{2,1,0:T(8,128)(2,1)}, bf16[32,64,128]{2,1,0:T(8,128)(2,1)}, f32[8,128]{1,0:T(8,128)S(1)}) custom-call(bf16[16,64,128]{2,1,0:T(8,128)(2,1)S(1)} %get-tuple-element.88.out_mine, bf16[16,64,128]{2,1,0:T(8,128)(2,1)S(1)} %get-tuple-element.89.query_mine, bf16[10,64,128]{2,1,0:T(8,128)(2,1)S(1)} %collective-permute-done.11.first_third, ...), custom_call_target="tpu_custom_call" | custom-call | flops 1 | tf_op jit(solution)/shard_map/assemble/pallas_call | solution.py:400
  33.6 3.9 %collective-permute-done.16.two_total = bf16[2,8,64,128]{3,2,1,0:T(8,128)(2,1)S(1)} collective-permute-done((bf16[2,8,64,128]{3,2,1,0:T(8,128)(2,1)S(1)}, bf16[2,8,64,128]{3,2,1,0:T(8,128)(2,1)S(1)}, u32[]{:S(2)}, u32[]{:S(2)}) %collective-permute-start.16) | collective-permute-done | bytes 262176 | tf_op jit(solution)/shard_map/ppermute | solution.py:19
  37.4 0.8 %total.1 = (bf16[8,64,128]{2,1,0:T(8,128)(2,1)}, bf16[8,64,128]{2,1,0:T(8,128)(2,1)}) custom-call(f32[2,4,64,128]{3,2,1,0:T(8,128)S(1)} %get-tuple-element.97.sum_mine, bf16[2,4,64,128]{3,2,1,0:T(8,128)(2,1)S(1)} %collective-permute-done.15.sum_other, bf16[2,8,64,128]{3,2,1,0:T(8,128)(2,1)S(1)} %collective-permute-done.16.two_total, ...), custom_call_target="tpu_custom_call" | custom-call | flops 1 | tf_op jit(solution)/shard_map/total/pallas_call | solution.py:400
  (31 shorter events, 3.2 us)
Async XLA Ops:
  0.6 8.6 %copy-start.1 = (bf16[32,64,128]{2,1,0:T(8,128)(2,1)S(1)}, bf16[32,64,128]{2,1,0:T(8,128)(2,1)}, u32[]{:S(2)}) copy-start(bf16[32,64,128]{2,1,0:T(8,128)(2,1)} %grads.3) | copy-start | bytes 1572868
  1.7 7.6 %copy-start = (bf16[32,64,128]{2,1,0:T(8,128)(2,1)S(1)}, bf16[32,64,128]{2,1,0:T(8,128)(2,1)}, u32[]{:S(2)}) copy-start(bf16[32,64,128]{2,1,0:T(8,128)(2,1)} %queries.3) | copy-start | bytes 1572868
  1.7 11.1 %collective-permute-start.3 = (bf16[2,8,64,128]{3,2,1,0:T(8,128)(2,1)S(1)}, bf16[2,8,64,128]{3,2,1,0:T(8,128)(2,1)S(1)}, u32[]{:S(2)}, u32[]{:S(2)}) collective-permute-start(bf16[2,8,64,128]{3,2,1,0:T(8,128)(2,1)S(1)} %pad_maximum_fusion.block.own.after), channel_id=1, source_target_pairs={{0,2},{1,3},{2,4},{3,5},{4,6},{5,7},{6,8},{7,9},{8,10},{9,11},{10,... | collective-permute-start | bytes 786440 | tf_op jit(solution)/shard_map/ppermute | solution.py:19
  5.0 1.9 %collective-permute-start = (bf16[4,64,128]{2,1,0:T(8,128)(2,1)S(1)}, bf16[4,64,128]{2,1,0:T(8,128)(2,1)S(1)}, u32[]{:S(2)}, u32[]{:S(2)}) collective-permute-start(bf16[4,64,128]{2,1,0:T(8,128)(2,1)S(1)} %get-tuple-element.53), channel_id=1, source_target_pairs={{0,16},{16,0},{1,17},{17,1},{2,18},{18,2},{3,19},{19,3},{4,20},{20... | collective-permute-start | bytes 196616 | tf_op jit(solution)/shard_map/ppermute | solution.py:24
  6.0 1.3 %collective-permute-start.1 = (bf16[4,64,128]{2,1,0:T(8,128)(2,1)S(1)}, bf16[4,64,128]{2,1,0:T(8,128)(2,1)S(1)}, u32[]{:S(2)}, u32[]{:S(2)}) collective-permute-start(bf16[4,64,128]{2,1,0:T(8,128)(2,1)S(1)} %get-tuple-element.54), channel_id=1, source_target_pairs={{0,16},{16,0},{1,17},{17,1},{2,18},{18,2},{3,19},{19,3},{4,20},{20... | collective-permute-start | bytes 196616 | tf_op jit(solution)/shard_map/ppermute | solution.py:24
  7.3 9.7 %collective-permute-start.2 = (bf16[2,4,128,128]{3,2,1,0:T(8,128)(2,1)S(1)}, bf16[2,4,128,128]{3,2,1,0:T(8,128)(2,1)S(1)}, u32[]{:S(2)}, u32[]{:S(2)}) collective-permute-start(bf16[2,4,128,128]{3,2,1,0:T(8,128)(2,1)S(1)} %join_own.1.own), channel_id=1, source_target_pairs={{0,1},{1,2},{2,3},{3,4},{4,5},{5,6},{6,7},{7,8},{8,9},{9,10},{10,1... | collective-permute-start | bytes 786440 | tf_op jit(solution)/shard_map/ppermute | solution.py:19
  9.3 2.0 %collective-permute-start.5 = (bf16[11,64,128]{2,1,0:T(8,128)(2,1)S(1)}, bf16[11,64,128]{2,1,0:T(8,128)(2,1)S(1)}, u32[]{:S(2)}, u32[]{:S(2)}) collective-permute-start(bf16[11,64,128]{2,1,0:T(8,128)(2,1)S(1)} %get-tuple-element.56), channel_id=1, source_target_pairs={{0,16},{16,0},{1,17},{17,1},{2,18},{18,2},{3,19},{19,3},{4,20},{20... | collective-permute-start | bytes 540680 | tf_op jit(solution)/shard_map/ppermute | solution.py:24
  9.6 1.8 %collective-permute-start.6 = (bf16[11,64,128]{2,1,0:T(8,128)(2,1)S(1)}, bf16[11,64,128]{2,1,0:T(8,128)(2,1)S(1)}, u32[]{:S(2)}, u32[]{:S(2)}) collective-permute-start(bf16[11,64,128]{2,1,0:T(8,128)(2,1)S(1)} %get-tuple-element.57), channel_id=1, source_target_pairs={{0,16},{16,0},{1,17},{17,1},{2,18},{18,2},{3,19},{19,3},{4,20},{20... | collective-permute-start | bytes 540680 | tf_op jit(solution)/shard_map/ppermute | solution.py:24
  9.9 1.4 %copy-start.2 = (s32[32]{0:T(128)S(1)}, s32[32]{0:T(128)}, u32[]{:S(2)}) copy-start(s32[32]{0:T(128)} %spans.1) | copy-start | bytes 388
  9.9 1.4 %collective-permute-start.4 = (bf16[10,64,128]{2,1,0:T(8,128)(2,1)S(1)}, bf16[10,64,128]{2,1,0:T(8,128)(2,1)S(1)}, u32[]{:S(2)}, u32[]{:S(2)}) collective-permute-start(bf16[10,64,128]{2,1,0:T(8,128)(2,1)S(1)} %get-tuple-element.55), channel_id=1, source_target_pairs={{0,16},{16,0},{1,17},{17,1},{2,18},{18,2},{3,19},{19,3},{4,20},{20... | collective-permute-start | bytes 491528 | tf_op jit(solution)/shard_map/ppermute | solution.py:24
  12.9 1.5 %collective-permute-start.7 = (bf16[4,64,128]{2,1,0:T(8,128)(2,1)S(1)}, bf16[4,64,128]{2,1,0:T(8,128)(2,1)S(1)}, u32[]{:S(2)}, u32[]{:S(2)}) collective-permute-start(bf16[4,64,128]{2,1,0:T(8,128)(2,1)S(1)} %get-tuple-element.63), channel_id=1, source_target_pairs={{0,16},{16,0},{1,17},{17,1},{2,18},{18,2},{3,19},{19,3},{4,20},{20... | collective-permute-start | bytes 196616 | tf_op jit(solution)/shard_map/ppermute | solution.py:24
  13.5 1.3 %collective-permute-start.8 = (bf16[4,64,128]{2,1,0:T(8,128)(2,1)S(1)}, bf16[4,64,128]{2,1,0:T(8,128)(2,1)S(1)}, u32[]{:S(2)}, u32[]{:S(2)}) collective-permute-start(bf16[4,64,128]{2,1,0:T(8,128)(2,1)S(1)} %get-tuple-element.64), channel_id=1, source_target_pairs={{0,16},{16,0},{1,17},{17,1},{2,18},{18,2},{3,19},{19,3},{4,20},{20... | collective-permute-start | bytes 196616 | tf_op jit(solution)/shard_map/ppermute | solution.py:24
  18.5 13.0 %collective-permute-start.14 = (bf16[2,4,128,128]{3,2,1,0:T(8,128)(2,1)S(1)}, bf16[2,4,128,128]{3,2,1,0:T(8,128)(2,1)S(1)}, u32[]{:S(2)}, u32[]{:S(2)}) collective-permute-start(bf16[2,4,128,128]{3,2,1,0:T(8,128)(2,1)S(1)} %get-tuple-element.96), channel_id=1, source_target_pairs={{1,0},{2,1},{3,2},{4,3},{5,4},{6,5},{7,6},{8,7},{9,8},{10,9},{11,1... | collective-permute-start | bytes 786440 | tf_op jit(solution)/shard_map/ppermute | solution.py:19
  23.7 1.7 %collective-permute-start.9 = (bf16[4,64,128]{2,1,0:T(8,128)(2,1)S(1)}, bf16[4,64,128]{2,1,0:T(8,128)(2,1)S(1)}, u32[]{:S(2)}, u32[]{:S(2)}) collective-permute-start(bf16[4,64,128]{2,1,0:T(8,128)(2,1)S(1)} %get-tuple-element.85), channel_id=1, source_target_pairs={{0,16},{16,0},{1,17},{17,1},{2,18},{18,2},{3,19},{19,3},{4,20},{20... | collective-permute-start | bytes 196616 | tf_op jit(solution)/shard_map/ppermute | solution.py:24
  24.5 1.3 %collective-permute-start.10 = (bf16[4,64,128]{2,1,0:T(8,128)(2,1)S(1)}, bf16[4,64,128]{2,1,0:T(8,128)(2,1)S(1)}, u32[]{:S(2)}, u32[]{:S(2)}) collective-permute-start(bf16[4,64,128]{2,1,0:T(8,128)(2,1)S(1)} %get-tuple-element.86), channel_id=1, source_target_pairs={{0,16},{16,0},{1,17},{17,1},{2,18},{18,2},{3,19},{19,3},{4,20},{20... | collective-permute-start | bytes 196616 | tf_op jit(solution)/shard_map/ppermute | solution.py:24
  25.8 11.7 %collective-permute-start.16 = (bf16[2,8,64,128]{3,2,1,0:T(8,128)(2,1)S(1)}, bf16[2,8,64,128]{3,2,1,0:T(8,128)(2,1)S(1)}, u32[]{:S(2)}, u32[]{:S(2)}) collective-permute-start(bf16[2,8,64,128]{3,2,1,0:T(8,128)(2,1)S(1)} %join_two.1.after), channel_id=1, source_target_pairs={{2,0},{3,1},{4,2},{5,3},{6,4},{7,5},{8,6},{9,7},{10,8},{11,9},{12,... | collective-permute-start | bytes 786440 | tf_op jit(solution)/shard_map/ppermute | solution.py:19
  29.0 3.5 %collective-permute-start.12 = (bf16[11,64,128]{2,1,0:T(8,128)(2,1)S(1)}, bf16[11,64,128]{2,1,0:T(8,128)(2,1)S(1)}, u32[]{:S(2)}, u32[]{:S(2)}) collective-permute-start(bf16[11,64,128]{2,1,0:T(8,128)(2,1)S(1)} %get-tuple-element.91), channel_id=1, source_target_pairs={{0,16},{16,0},{1,17},{17,1},{2,18},{18,2},{3,19},{19,3},{4,20},{20... | collective-permute-start | bytes 540680 | tf_op jit(solution)/shard_map/ppermute | solution.py:24
  29.5 3.0 %collective-permute-start.13 = (bf16[11,64,128]{2,1,0:T(8,128)(2,1)S(1)}, bf16[11,64,128]{2,1,0:T(8,128)(2,1)S(1)}, u32[]{:S(2)}, u32[]{:S(2)}) collective-permute-start(bf16[11,64,128]{2,1,0:T(8,128)(2,1)S(1)} %get-tuple-element.92), channel_id=1, source_target_pairs={{0,16},{16,0},{1,17},{17,1},{2,18},{18,2},{3,19},{19,3},{4,20},{20... | collective-permute-start | bytes 540680 | tf_op jit(solution)/shard_map/ppermute | solution.py:24
  29.5 3.0 %collective-permute-start.11 = (bf16[10,64,128]{2,1,0:T(8,128)(2,1)S(1)}, bf16[10,64,128]{2,1,0:T(8,128)(2,1)S(1)}, u32[]{:S(2)}, u32[]{:S(2)}) collective-permute-start(bf16[10,64,128]{2,1,0:T(8,128)(2,1)S(1)} %get-tuple-element.90), channel_id=1, source_target_pairs={{0,16},{16,0},{1,17},{17,1},{2,18},{18,2},{3,19},{19,3},{4,20},{20... | collective-permute-start | bytes 491528 | tf_op jit(solution)/shard_map/ppermute | solution.py:24
  31.6 5.8 %collective-permute-start.15 = (bf16[2,4,64,128]{3,2,1,0:T(8,128)(2,1)S(1)}, bf16[2,4,64,128]{3,2,1,0:T(8,128)(2,1)S(1)}, u32[]{:S(2)}, u32[]{:S(2)}) collective-permute-start(bf16[2,4,64,128]{3,2,1,0:T(8,128)(2,1)S(1)} %get-tuple-element.98), channel_id=1, source_target_pairs={{0,16},{16,0},{1,17},{17,1},{2,18},{18,2},{3,19},{19,3},{4,20},{20... | collective-permute-start | bytes 393224 | tf_op jit(solution)/shard_map/ppermute | solution.py:24

commit v13 on v12

--- a/solution.py
+++ b/solution.py
@@ -421,7 +421,8 @@
     chip_rows = ((heads_here, tokens, width), half)
 
     own = jnp.stack([key_matrix, value_matrix])
-    back_two = shifted(own, "seq", 2)
+    chips = lax.axis_size("seq")
+    back_two = lax.ppermute(own, "seq", [(i, (i + 2) % chips) for i in range(chips)])
     own_sends = call(split_kernel, "split_own", [half_block] * 2, (own,))
     (own_head,) = call(
         join_own_kernel, "join_own", [chip_pair], (own, *[swapped(send, "head") for send in own_sends])

time: 38.4 us -> 36.4 us (0.948)
  starting transfers between devices: 17.1 us -> 15.2 us
    ppermute x4 -> x3, starting transfers between devices: 11.8 us -> 8.52 us  [shifted(): return lax.ppermute(block, axis, route)]
    ppermute x0 -> x1, starting transfers between devices: none -> 1.29 us  [shards(): lax.ppermute(own, 'seq', [(i, (i + 2) % chips) for i in range(chips)])]
    ppermute x4 -> x3, waiting for transfers between devices: 6.69 us -> 6.66 us  [shifted(): return lax.ppermute(block, axis, route)]
  transfers between devices with their start and end apart: 17 -> 17, of which waited for: 10 -> 10; matrix products, arithmetic and copies ran while one was open for 0% -> 0% of each run, Pallas kernels for 14% -> 15%
where the time goes in v13:
time: 36.4 us; the launch traced here: 36.2 us
  starting transfers between devices  15.2 us (42%)
  waiting for transfers between devices  10.8 us (30%)
  Pallas kernels  7.68 us (21%)
  between operations  1.44 us (4%)
  other arithmetic  1.05 us (3%)
    ppermute x3, starting transfers between devices, shifted(): return lax.ppermute(block, axis, route)  8.52 us
    pallas_call x14, Pallas kernels, call(): pl.pallas_call(kernel, out_shape=tuple((jax.ShapeDtypeStruct(shape, kind)...  7.68 us
    ppermute x3, waiting for transfers between devices, shifted(): return lax.ppermute(block, axis, route)  6.66 us
    ppermute x13, starting transfers between devices, swapped(): return lax.ppermute(block, axis, [(i, count - 1 - i) for i in range(count)])  5.43 us
    ppermute x13, waiting for transfers between devices, swapped(): return lax.ppermute(block, axis, [(i, count - 1 - i) for i in range(count)])  4.13 us
    ppermute x1, starting transfers between devices, shards(): lax.ppermute(own, 'seq', [(i, (i + 2) % chips) for i in range(chips)])  1.29 us
    another operation x1, other arithmetic, shards(): own = jnp.stack([key_matrix, value_matrix])  1.05 us
  transfers between devices with their start and end apart: 17, of which 10 were waited for; matrix products, arithmetic and copies ran while one was open for 0% of the time, Pallas kernels for 15%

profile of v13, /device:TPU:27, one launch (start us, length us, event | category | flops | bytes accessed | tf_op | source)
XLA Modules:
  0.0 36.2 jit_solution(979296842446454422)
XLA Ops:
  0.6 1.1 %pad_maximum_fusion.block.own.after = bf16[2,8,64,128]{3,2,1,0:T(8,128)(2,1)S(1)} fusion(bf16[1,8,64,128]{3,2,1,0:T(8,128)(2,1)} %bitcast.2, bf16[1,8,64,128]{3,2,1,0:T(8,128)(2,1)} %bitcast.3), kind=kLoop, calls=%fused_computation | loop fusion | flops 131072 | bytes 524288 | tf_op jit(solution)/shard_map/stack | solution.py:423
  1.7 1.3 %collective-permute-start.3 = (bf16[2,8,64,128]{3,2,1,0:T(8,128)(2,1)S(1)}, bf16[2,8,64,128]{3,2,1,0:T(8,128)(2,1)S(1)}, u32[]{:S(2)}, u32[]{:S(2)}) collective-permute-start(bf16[2,8,64,128]{3,2,1,0:T(8,128)(2,1)S(1)} %pad_maximum_fusion.block.own.after), channel_id=1, source_target_pairs={{0,2},{1,3},{2,4},{3,5},{4,6},{5,7},{6,8},{7,9},{8,10},{9,11},{10,... | collective-permute-start | bytes 786440 | tf_op jit(solution)/shard_map/ppermute | solution.py:425
  3.0 1.0 %collective-permute-start = (bf16[4,64,128]{2,1,0:T(8,128)(2,1)S(1)}, bf16[4,64,128]{2,1,0:T(8,128)(2,1)S(1)}, u32[]{:S(2)}, u32[]{:S(2)}) collective-permute-start(bf16[4,64,128]{2,1,0:T(8,128)(2,1)S(1)} %get-tuple-element.53), channel_id=1, source_target_pairs={{0,16},{16,0},{1,17},{17,1},{2,18},{18,2},{3,19},{19,3},{4,20},{20... | collective-permute-start | bytes 196616 | tf_op jit(solution)/shard_map/ppermute | solution.py:24
  4.1 0.8 %collective-permute-done.other_keys = bf16[4,64,128]{2,1,0:T(8,128)(2,1)S(1)} collective-permute-done((bf16[4,64,128]{2,1,0:T(8,128)(2,1)S(1)}, bf16[4,64,128]{2,1,0:T(8,128)(2,1)S(1)}, u32[]{:S(2)}, u32[]{:S(2)}) %collective-permute-start) | collective-permute-done | bytes 65568 | tf_op jit(solution)/shard_map/ppermute | solution.py:24
  5.3 1.9 %collective-permute-start.2 = (bf16[2,4,128,128]{3,2,1,0:T(8,128)(2,1)S(1)}, bf16[2,4,128,128]{3,2,1,0:T(8,128)(2,1)S(1)}, u32[]{:S(2)}, u32[]{:S(2)}) collective-permute-start(bf16[2,4,128,128]{3,2,1,0:T(8,128)(2,1)S(1)} %join_own.1.own), channel_id=1, source_target_pairs={{0,1},{1,2},{2,3},{3,4},{4,5},{5,6},{6,7},{7,8},{8,9},{9,10},{10,1... | collective-permute-start | bytes 786440 | tf_op jit(solution)/shard_map/ppermute | solution.py:19
  8.7 0.6 %collective-permute-done.4.first_third = bf16[10,64,128]{2,1,0:T(8,128)(2,1)S(1)} collective-permute-done((bf16[10,64,128]{2,1,0:T(8,128)(2,1)S(1)}, bf16[10,64,128]{2,1,0:T(8,128)(2,1)S(1)}, u32[]{:S(2)}, u32[]{:S(2)}) %collective-permute-start.4) | collective-permute-done | bytes 163872 | tf_op jit(solution)/shard_map/ppermute | solution.py:24
  9.3 1.5 %own_block.1 = (bf16[16,128,128]{2,1,0:T(8,128)(2,1)S(1)}, bf16[16,128,128]{2,1,0:T(8,128)(2,1)S(1)}, bf16[8,128,256]{2,1,0:T(8,128)(2,1)S(1)}, s32[8,1,256]{2,1...) custom-call(s32[32]{0:T(128)S(1)} %copy-done.2, ...), custom_call_target="tpu_custom_call" | custom-call | flops 1 | tf_op jit(solution)/shard_map/own_block/pallas_call | solution.py:400
  10.9 0.7 %collective-permute-start.7 = (bf16[4,64,128]{2,1,0:T(8,128)(2,1)S(1)}, bf16[4,64,128]{2,1,0:T(8,128)(2,1)S(1)}, u32[]{:S(2)}, u32[]{:S(2)}) collective-permute-start(bf16[4,64,128]{2,1,0:T(8,128)(2,1)S(1)} %get-tuple-element.63), channel_id=1, source_target_pairs={{0,16},{16,0},{1,17},{17,1},{2,18},{18,2},{3,19},{19,3},{4,20},{20... | collective-permute-start | bytes 196616 | tf_op jit(solution)/shard_map/ppermute | solution.py:24
  11.7 0.8 %collective-permute-done.7.two_keys = bf16[4,64,128]{2,1,0:T(8,128)(2,1)S(1)} collective-permute-done((bf16[4,64,128]{2,1,0:T(8,128)(2,1)S(1)}, bf16[4,64,128]{2,1,0:T(8,128)(2,1)S(1)}, u32[]{:S(2)}, u32[]{:S(2)}) %collective-permute-start.7) | collective-permute-done | bytes 65568 | tf_op jit(solution)/shard_map/ppermute | solution.py:24
  12.8 0.9 %near_forward.1 = (f32[8,1,256]{2,1,0:T(1,128)S(1)}, f32[8,1,256]{2,1,0:T(1,128)S(1)}, f32[8,128,256]{2,1,0:T(8,128)S(1)}, f32[8,128,256]{2,1,0:T(8,128)S(1)}, f...) custom-call(s32[8,1,256]{2,1,0:T(1,128)S(1)} %get-tuple-element.59.first, ...), custom_call_target="tpu_custom_call" | custom-call | flops 1 | tf_op jit(solution)/shard_map/near_forward/pallas_call | solution.py:400
  13.8 1.2 %collective-permute-done.2.back_one = bf16[2,4,128,128]{3,2,1,0:T(8,128)(2,1)S(1)} collective-permute-done((bf16[2,4,128,128]{3,2,1,0:T(8,128)(2,1)S(1)}, bf16[2,4,128,128]{3,2,1,0:T(8,128)(2,1)S(1)}, u32[]{:S(2)}, u32[]{:S(2)}) %collective-permute-start.2) | collective-permute-done | bytes 262176 | tf_op jit(solution)/shard_map/ppermute | solution.py:19
  15.0 1.5 %last_forward_backward.1 = (bf16[8,128,256]{2,1,0:T(8,128)(2,1)S(1)}, f32[8,1,256]{2,1,0:T(1,128)S(1)}, f32[8,1,256]{2,1,0:T(1,128)S(1)}, bf16[8,128,256]{2,1,0:T(8,128)(2,1)S(1)}, bf16[2,4,128,128]{3,2,1,0:T(8,128)(2,1)S(1)}) custom-call(s32[8,1,256]{2,1,0:T(1,128)S(1)} %get-tuple-element.59.first, bf16[16,128,128]{2,1,0:T(8,128)(2,1)S(1)} %get-tuple-element.60.query_head, ...), custom_call_target="tpu_custom_call" | custom-call | flops 1 | tf_op jit(solution)/shard_map/last_forward_backward/pallas_call | solution.py:400
  16.5 4.7 %collective-permute-start.14 = (bf16[2,4,128,128]{3,2,1,0:T(8,128)(2,1)S(1)}, bf16[2,4,128,128]{3,2,1,0:T(8,128)(2,1)S(1)}, u32[]{:S(2)}, u32[]{:S(2)}) collective-permute-start(bf16[2,4,128,128]{3,2,1,0:T(8,128)(2,1)S(1)} %get-tuple-element.96), channel_id=1, source_target_pairs={{1,0},{2,1},{3,2},{4,3},{5,4},{6,5},{7,6},{8,7},{9,8},{10,9},{11,1... | collective-permute-start | bytes 786440 | tf_op jit(solution)/shard_map/ppermute | solution.py:19
  21.2 0.5 %two_backward.1 = (bf16[8,128,256]{2,1,0:T(8,128)(2,1)S(1)}, bf16[2,4,64,128]{3,2,1,0:T(8,128)(2,1)S(1)}, bf16[4,64,128]{2,1,0:T(8,128)(2,1)S(1)}, bf16[4,64,128]{2,1,0:T(8,128)(2,1)S(1)}) custom-call(bf16[16,128,128]{2,1,0:T(8,128)(2,1)S(1)} %get-tuple-element.60.query_head, bf16[16,128,128]{2,1,0:T(8,128)(2,1)S(1)} %get-tuple-element.61.grad_head, ...), custom_call_target="tpu_custom_call" | custom-call | flops 1 | tf_op jit(solution)/shard_map/two_backward/pallas_call | solution.py:400
  21.7 0.8 %collective-permute-start.9 = (bf16[4,64,128]{2,1,0:T(8,128)(2,1)S(1)}, bf16[4,64,128]{2,1,0:T(8,128)(2,1)S(1)}, u32[]{:S(2)}, u32[]{:S(2)}) collective-permute-start(bf16[4,64,128]{2,1,0:T(8,128)(2,1)S(1)} %get-tuple-element.85), channel_id=1, source_target_pairs={{0,16},{16,0},{1,17},{17,1},{2,18},{18,2},{3,19},{19,3},{4,20},{20... | collective-permute-start | bytes 196616 | tf_op jit(solution)/shard_map/ppermute | solution.py:24
  22.6 0.8 %collective-permute-done.9.other_keys = bf16[4,64,128]{2,1,0:T(8,128)(2,1)S(1)} collective-permute-done((bf16[4,64,128]{2,1,0:T(8,128)(2,1)S(1)}, bf16[4,64,128]{2,1,0:T(8,128)(2,1)S(1)}, u32[]{:S(2)}, u32[]{:S(2)}) %collective-permute-start.9) | collective-permute-done | bytes 65568 | tf_op jit(solution)/shard_map/ppermute | solution.py:24
  23.8 1.9 %collective-permute-start.16 = (bf16[2,8,64,128]{3,2,1,0:T(8,128)(2,1)S(1)}, bf16[2,8,64,128]{3,2,1,0:T(8,128)(2,1)S(1)}, u32[]{:S(2)}, u32[]{:S(2)}) collective-permute-start(bf16[2,8,64,128]{3,2,1,0:T(8,128)(2,1)S(1)} %join_two.1.after), channel_id=1, source_target_pairs={{2,0},{3,1},{4,2},{5,3},{6,4},{7,5},{8,6},{9,7},{10,8},{11,9},{12,... | collective-permute-start | bytes 786440 | tf_op jit(solution)/shard_map/ppermute | solution.py:19
  26.2 0.8 %query_grad.1 = (bf16[16,64,128]{2,1,0:T(8,128)(2,1)S(1)}, bf16[16,64,128]{2,1,0:T(8,128)(2,1)S(1)}, bf16[10,64,128]{2,1,0:T(8,128)(2,1)S(1)}, bf16[11,64,128]{2,1,0:T(8,128)(2,1)S(1)}, bf16[11,64,128]{2,1,0:T(8,128)(2,1)S(1)}) custom-call(bf16[2,4,128,128]{3,2,1,0:T(8,128)(2,1)S(1)} %join_own.1.own, ...), custom_call_target="tpu_custom_call" | custom-call | flops 1 | tf_op jit(solution)/shard_map/query_grad/pallas_call | solution.py:400
  27.0 0.5 %collective-permute-start.12 = (bf16[11,64,128]{2,1,0:T(8,128)(2,1)S(1)}, bf16[11,64,128]{2,1,0:T(8,128)(2,1)S(1)}, u32[]{:S(2)}, u32[]{:S(2)}) collective-permute-start(bf16[11,64,128]{2,1,0:T(8,128)(2,1)S(1)} %get-tuple-element.91), channel_id=1, source_target_pairs={{0,16},{16,0},{1,17},{17,1},{2,18},{18,2},{3,19},{19,3},{4,20},{20... | collective-permute-start | bytes 540680 | tf_op jit(solution)/shard_map/ppermute | solution.py:24
  28.0 1.6 %collective-permute-done.14.one_total = bf16[2,4,128,128]{3,2,1,0:T(8,128)(2,1)S(1)} collective-permute-done((bf16[2,4,128,128]{3,2,1,0:T(8,128)(2,1)S(1)}, bf16[2,4,128,128]{3,2,1,0:T(8,128)(2,1)S(1)}, u32[]{:S(2)}, u32[]{:S(2)}) %collective-permute-start.14) | collective-permute-done | bytes 262176 | tf_op jit(solution)/shard_map/ppermute | solution.py:19
  29.6 0.9 %collective-permute-start.15 = (bf16[2,4,64,128]{3,2,1,0:T(8,128)(2,1)S(1)}, bf16[2,4,64,128]{3,2,1,0:T(8,128)(2,1)S(1)}, u32[]{:S(2)}, u32[]{:S(2)}) collective-permute-start(bf16[2,4,64,128]{3,2,1,0:T(8,128)(2,1)S(1)} %get-tuple-element.98), channel_id=1, source_target_pairs={{0,16},{16,0},{1,17},{17,1},{2,18},{18,2},{3,19},{19,3},{4,20},{20... | collective-permute-start | bytes 393224 | tf_op jit(solution)/shard_map/ppermute | solution.py:24
  30.5 1.0 %assemble.1 = (bf16[32,64,128]{2,1,0:T(8,128)(2,1)}, bf16[32,64,128]{2,1,0:T(8,128)(2,1)}, f32[8,128]{1,0:T(8,128)S(1)}) custom-call(bf16[16,64,128]{2,1,0:T(8,128)(2,1)S(1)} %get-tuple-element.88.out_mine, bf16[16,64,128]{2,1,0:T(8,128)(2,1)S(1)} %get-tuple-element.89.query_mine, bf16[10,64,128]{2,1,0:T(8,128)(2,1)S(1)} %collective-permute-done.11.first_third, ...), custom_call_target="tpu_custom_call" | custom-call | flops 1 | tf_op jit(solution)/shard_map/assemble/pallas_call | solution.py:400
  31.6 3.9 %collective-permute-done.16.two_total = bf16[2,8,64,128]{3,2,1,0:T(8,128)(2,1)S(1)} collective-permute-done((bf16[2,8,64,128]{3,2,1,0:T(8,128)(2,1)S(1)}, bf16[2,8,64,128]{3,2,1,0:T(8,128)(2,1)S(1)}, u32[]{:S(2)}, u32[]{:S(2)}) %collective-permute-start.16) | collective-permute-done | bytes 262176 | tf_op jit(solution)/shard_map/ppermute | solution.py:19
  35.5 0.8 %total.1 = (bf16[8,64,128]{2,1,0:T(8,128)(2,1)}, bf16[8,64,128]{2,1,0:T(8,128)(2,1)}) custom-call(f32[2,4,64,128]{3,2,1,0:T(8,128)S(1)} %get-tuple-element.97.sum_mine, bf16[2,4,64,128]{3,2,1,0:T(8,128)(2,1)S(1)} %collective-permute-done.15.sum_other, bf16[2,8,64,128]{3,2,1,0:T(8,128)(2,1)S(1)} %collective-permute-done.16.two_total, ...), custom_call_target="tpu_custom_call" | custom-call | flops 1 | tf_op jit(solution)/shard_map/total/pallas_call | solution.py:400
  (31 shorter events, 3.2 us)
Async XLA Ops:
  0.6 6.6 %copy-start.1 = (bf16[32,64,128]{2,1,0:T(8,128)(2,1)S(1)}, bf16[32,64,128]{2,1,0:T(8,128)(2,1)}, u32[]{:S(2)}) copy-start(bf16[32,64,128]{2,1,0:T(8,128)(2,1)} %grads.3) | copy-start | bytes 1572868
  1.7 5.6 %copy-start = (bf16[32,64,128]{2,1,0:T(8,128)(2,1)S(1)}, bf16[32,64,128]{2,1,0:T(8,128)(2,1)}, u32[]{:S(2)}) copy-start(bf16[32,64,128]{2,1,0:T(8,128)(2,1)} %queries.3) | copy-start | bytes 1572868
  1.7 9.1 %collective-permute-start.3 = (bf16[2,8,64,128]{3,2,1,0:T(8,128)(2,1)S(1)}, bf16[2,8,64,128]{3,2,1,0:T(8,128)(2,1)S(1)}, u32[]{:S(2)}, u32[]{:S(2)}) collective-permute-start(bf16[2,8,64,128]{3,2,1,0:T(8,128)(2,1)S(1)} %pad_maximum_fusion.block.own.after), channel_id=1, source_target_pairs={{0,2},{1,3},{2,4},{3,5},{4,6},{5,7},{6,8},{7,9},{8,10},{9,11},{10,... | collective-permute-start | bytes 786440 | tf_op jit(solution)/shard_map/ppermute | solution.py:425
  3.0 1.9 %collective-permute-start = (bf16[4,64,128]{2,1,0:T(8,128)(2,1)S(1)}, bf16[4,64,128]{2,1,0:T(8,128)(2,1)S(1)}, u32[]{:S(2)}, u32[]{:S(2)}) collective-permute-start(bf16[4,64,128]{2,1,0:T(8,128)(2,1)S(1)} %get-tuple-element.53), channel_id=1, source_target_pairs={{0,16},{16,0},{1,17},{17,1},{2,18},{18,2},{3,19},{19,3},{4,20},{20... | collective-permute-start | bytes 196616 | tf_op jit(solution)/shard_map/ppermute | solution.py:24
  4.0 1.3 %collective-permute-start.1 = (bf16[4,64,128]{2,1,0:T(8,128)(2,1)S(1)}, bf16[4,64,128]{2,1,0:T(8,128)(2,1)S(1)}, u32[]{:S(2)}, u32[]{:S(2)}) collective-permute-start(bf16[4,64,128]{2,1,0:T(8,128)(2,1)S(1)} %get-tuple-element.54), channel_id=1, source_target_pairs={{0,16},{16,0},{1,17},{17,1},{2,18},{18,2},{3,19},{19,3},{4,20},{20... | collective-permute-start | bytes 196616 | tf_op jit(solution)/shard_map/ppermute | solution.py:24
  5.3 9.7 %collective-permute-start.2 = (bf16[2,4,128,128]{3,2,1,0:T(8,128)(2,1)S(1)}, bf16[2,4,128,128]{3,2,1,0:T(8,128)(2,1)S(1)}, u32[]{:S(2)}, u32[]{:S(2)}) collective-permute-start(bf16[2,4,128,128]{3,2,1,0:T(8,128)(2,1)S(1)} %join_own.1.own), channel_id=1, source_target_pairs={{0,1},{1,2},{2,3},{3,4},{4,5},{5,6},{6,7},{7,8},{8,9},{9,10},{10,1... | collective-permute-start | bytes 786440 | tf_op jit(solution)/shard_map/ppermute | solution.py:19
  7.3 2.0 %collective-permute-start.5 = (bf16[11,64,128]{2,1,0:T(8,128)(2,1)S(1)}, bf16[11,64,128]{2,1,0:T(8,128)(2,1)S(1)}, u32[]{:S(2)}, u32[]{:S(2)}) collective-permute-start(bf16[11,64,128]{2,1,0:T(8,128)(2,1)S(1)} %get-tuple-element.56), channel_id=1, source_target_pairs={{0,16},{16,0},{1,17},{17,1},{2,18},{18,2},{3,19},{19,3},{4,20},{20... | collective-permute-start | bytes 540680 | tf_op jit(solution)/shard_map/ppermute | solution.py:24
  7.5 1.8 %collective-permute-start.6 = (bf16[11,64,128]{2,1,0:T(8,128)(2,1)S(1)}, bf16[11,64,128]{2,1,0:T(8,128)(2,1)S(1)}, u32[]{:S(2)}, u32[]{:S(2)}) collective-permute-start(bf16[11,64,128]{2,1,0:T(8,128)(2,1)S(1)} %get-tuple-element.57), channel_id=1, source_target_pairs={{0,16},{16,0},{1,17},{17,1},{2,18},{18,2},{3,19},{19,3},{4,20},{20... | collective-permute-start | bytes 540680 | tf_op jit(solution)/shard_map/ppermute | solution.py:24
  7.9 1.4 %copy-start.2 = (s32[32]{0:T(128)S(1)}, s32[32]{0:T(128)}, u32[]{:S(2)}) copy-start(s32[32]{0:T(128)} %spans.1) | copy-start | bytes 388
  7.9 1.4 %collective-permute-start.4 = (bf16[10,64,128]{2,1,0:T(8,128)(2,1)S(1)}, bf16[10,64,128]{2,1,0:T(8,128)(2,1)S(1)}, u32[]{:S(2)}, u32[]{:S(2)}) collective-permute-start(bf16[10,64,128]{2,1,0:T(8,128)(2,1)S(1)} %get-tuple-element.55), channel_id=1, source_target_pairs={{0,16},{16,0},{1,17},{17,1},{2,18},{18,2},{3,19},{19,3},{4,20},{20... | collective-permute-start | bytes 491528 | tf_op jit(solution)/shard_map/ppermute | solution.py:24
  10.9 1.6 %collective-permute-start.7 = (bf16[4,64,128]{2,1,0:T(8,128)(2,1)S(1)}, bf16[4,64,128]{2,1,0:T(8,128)(2,1)S(1)}, u32[]{:S(2)}, u32[]{:S(2)}) collective-permute-start(bf16[4,64,128]{2,1,0:T(8,128)(2,1)S(1)} %get-tuple-element.63), channel_id=1, source_target_pairs={{0,16},{16,0},{1,17},{17,1},{2,18},{18,2},{3,19},{19,3},{4,20},{20... | collective-permute-start | bytes 196616 | tf_op jit(solution)/shard_map/ppermute | solution.py:24
  11.6 1.3 %collective-permute-start.8 = (bf16[4,64,128]{2,1,0:T(8,128)(2,1)S(1)}, bf16[4,64,128]{2,1,0:T(8,128)(2,1)S(1)}, u32[]{:S(2)}, u32[]{:S(2)}) collective-permute-start(bf16[4,64,128]{2,1,0:T(8,128)(2,1)S(1)} %get-tuple-element.64), channel_id=1, source_target_pairs={{0,16},{16,0},{1,17},{17,1},{2,18},{18,2},{3,19},{19,3},{4,20},{20... | collective-permute-start | bytes 196616 | tf_op jit(solution)/shard_map/ppermute | solution.py:24
  16.5 13.1 %collective-permute-start.14 = (bf16[2,4,128,128]{3,2,1,0:T(8,128)(2,1)S(1)}, bf16[2,4,128,128]{3,2,1,0:T(8,128)(2,1)S(1)}, u32[]{:S(2)}, u32[]{:S(2)}) collective-permute-start(bf16[2,4,128,128]{3,2,1,0:T(8,128)(2,1)S(1)} %get-tuple-element.96), channel_id=1, source_target_pairs={{1,0},{2,1},{3,2},{4,3},{5,4},{6,5},{7,6},{8,7},{9,8},{10,9},{11,1... | collective-permute-start | bytes 786440 | tf_op jit(solution)/shard_map/ppermute | solution.py:19
  21.7 1.7 %collective-permute-start.9 = (bf16[4,64,128]{2,1,0:T(8,128)(2,1)S(1)}, bf16[4,64,128]{2,1,0:T(8,128)(2,1)S(1)}, u32[]{:S(2)}, u32[]{:S(2)}) collective-permute-start(bf16[4,64,128]{2,1,0:T(8,128)(2,1)S(1)} %get-tuple-element.85), channel_id=1, source_target_pairs={{0,16},{16,0},{1,17},{17,1},{2,18},{18,2},{3,19},{19,3},{4,20},{20... | collective-permute-start | bytes 196616 | tf_op jit(solution)/shard_map/ppermute | solution.py:24
  22.5 1.3 %collective-permute-start.10 = (bf16[4,64,128]{2,1,0:T(8,128)(2,1)S(1)}, bf16[4,64,128]{2,1,0:T(8,128)(2,1)S(1)}, u32[]{:S(2)}, u32[]{:S(2)}) collective-permute-start(bf16[4,64,128]{2,1,0:T(8,128)(2,1)S(1)} %get-tuple-element.86), channel_id=1, source_target_pairs={{0,16},{16,0},{1,17},{17,1},{2,18},{18,2},{3,19},{19,3},{4,20},{20... | collective-permute-start | bytes 196616 | tf_op jit(solution)/shard_map/ppermute | solution.py:24
  23.8 11.7 %collective-permute-start.16 = (bf16[2,8,64,128]{3,2,1,0:T(8,128)(2,1)S(1)}, bf16[2,8,64,128]{3,2,1,0:T(8,128)(2,1)S(1)}, u32[]{:S(2)}, u32[]{:S(2)}) collective-permute-start(bf16[2,8,64,128]{3,2,1,0:T(8,128)(2,1)S(1)} %join_two.1.after), channel_id=1, source_target_pairs={{2,0},{3,1},{4,2},{5,3},{6,4},{7,5},{8,6},{9,7},{10,8},{11,9},{12,... | collective-permute-start | bytes 786440 | tf_op jit(solution)/shard_map/ppermute | solution.py:19
  27.0 3.6 %collective-permute-start.12 = (bf16[11,64,128]{2,1,0:T(8,128)(2,1)S(1)}, bf16[11,64,128]{2,1,0:T(8,128)(2,1)S(1)}, u32[]{:S(2)}, u32[]{:S(2)}) collective-permute-start(bf16[11,64,128]{2,1,0:T(8,128)(2,1)S(1)} %get-tuple-element.91), channel_id=1, source_target_pairs={{0,16},{16,0},{1,17},{17,1},{2,18},{18,2},{3,19},{19,3},{4,20},{20... | collective-permute-start | bytes 540680 | tf_op jit(solution)/shard_map/ppermute | solution.py:24
  27.5 3.1 %collective-permute-start.13 = (bf16[11,64,128]{2,1,0:T(8,128)(2,1)S(1)}, bf16[11,64,128]{2,1,0:T(8,128)(2,1)S(1)}, u32[]{:S(2)}, u32[]{:S(2)}) collective-permute-start(bf16[11,64,128]{2,1,0:T(8,128)(2,1)S(1)} %get-tuple-element.92), channel_id=1, source_target_pairs={{0,16},{16,0},{1,17},{17,1},{2,18},{18,2},{3,19},{19,3},{4,20},{20... | collective-permute-start | bytes 540680 | tf_op jit(solution)/shard_map/ppermute | solution.py:24
  27.5 3.0 %collective-permute-start.11 = (bf16[10,64,128]{2,1,0:T(8,128)(2,1)S(1)}, bf16[10,64,128]{2,1,0:T(8,128)(2,1)S(1)}, u32[]{:S(2)}, u32[]{:S(2)}) collective-permute-start(bf16[10,64,128]{2,1,0:T(8,128)(2,1)S(1)} %get-tuple-element.90), channel_id=1, source_target_pairs={{0,16},{16,0},{1,17},{17,1},{2,18},{18,2},{3,19},{19,3},{4,20},{20... | collective-permute-start | bytes 491528 | tf_op jit(solution)/shard_map/ppermute | solution.py:24
  29.6 5.8 %collective-permute-start.15 = (bf16[2,4,64,128]{3,2,1,0:T(8,128)(2,1)S(1)}, bf16[2,4,64,128]{3,2,1,0:T(8,128)(2,1)S(1)}, u32[]{:S(2)}, u32[]{:S(2)}) collective-permute-start(bf16[2,4,64,128]{3,2,1,0:T(8,128)(2,1)S(1)} %get-tuple-element.98), channel_id=1, source_target_pairs={{0,16},{16,0},{1,17},{17,1},{2,18},{18,2},{3,19},{19,3},{4,20},{20... | collective-permute-start | bytes 393224 | tf_op jit(solution)/shard_map/ppermute | solution.py:24

commit v14 on v12

--- a/solution.py
+++ b/solution.py
@@ -14,9 +14,8 @@
 
 
 def shifted(block, axis, distance):
-    devices = range(lax.axis_size(axis))
-    route = [(i - distance, i) for i in devices if i - distance in devices]
-    return lax.ppermute(block, axis, route)
+    count = lax.axis_size(axis)
+    return lax.ppermute(block, axis, [(i, (i + distance) % count) for i in range(count)])
 
 
 def swapped(block, axis):

time: 38.4 us -> 34.5 us (0.90)
  the two profiles are of different devices: /device:TPU:27 before, /device:TPU:0 now
where the time goes in v14:
time: 34.5 us; the launch traced here: 34.4 us
  waiting for transfers between devices  12.6 us (37%)
  starting transfers between devices  11.6 us (34%)
  Pallas kernels  7.67 us (22%)
  between operations  1.42 us (4%)
  other arithmetic  1.05 us (3%)
    ppermute x4, waiting for transfers between devices, shifted(): lax.ppermute(block, axis, [(i, (i + distance) % count) for i in range(cou...  8.48 us
    ppermute x4, starting transfers between devices, shifted(): lax.ppermute(block, axis, [(i, (i + distance) % count) for i in range(cou...  8.12 us
    pallas_call x14, Pallas kernels, call(): pl.pallas_call(kernel, out_shape=tuple((jax.ShapeDtypeStruct(shape, kind)...  7.67 us
    ppermute x13, waiting for transfers between devices, swapped(): return lax.ppermute(block, axis, [(i, count - 1 - i) for i in range(count)])  4.14 us
    ppermute x13, starting transfers between devices, swapped(): return lax.ppermute(block, axis, [(i, count - 1 - i) for i in range(count)])  3.5 us
    another operation x1, other arithmetic, shards(): own = jnp.stack([key_matrix, value_matrix])  1.05 us
  transfers between devices with their start and end apart: 17, of which 11 were waited for; matrix products, arithmetic and copies ran while one was open for 0% of the time, Pallas kernels for 16%

profile of v14, /device:TPU:0, one launch (start us, length us, event | category | flops | bytes accessed | tf_op | source)
XLA Modules:
  0.0 34.4 jit_solution(8439598175503799794)
XLA Ops:
  0.6 1.1 %pad_maximum_fusion.block.own.after = bf16[2,8,64,128]{3,2,1,0:T(8,128)(2,1)S(1)} fusion(bf16[1,8,64,128]{3,2,1,0:T(8,128)(2,1)} %bitcast.2, bf16[1,8,64,128]{3,2,1,0:T(8,128)(2,1)} %bitcast.3), kind=kLoop, calls=%fused_computation | loop fusion | flops 131072 | bytes 524288 | tf_op jit(solution)/shard_map/stack | solution.py:422
  1.7 3.0 %collective-permute-start.3 = (bf16[2,8,64,128]{3,2,1,0:T(8,128)(2,1)S(1)}, bf16[2,8,64,128]{3,2,1,0:T(8,128)(2,1)S(1)}, u32[]{:S(2)}, u32[]{:S(2)}) collective-permute-start(bf16[2,8,64,128]{3,2,1,0:T(8,128)(2,1)S(1)} %pad_maximum_fusion.block.own.after), channel_id=1, source_target_pairs={{0,2},{1,3},{2,4},{3,5},{4,6},{5,7},{6,8},{7,9},{8,10},{9,11},{10,... | collective-permute-start | bytes 786440 | tf_op jit(solution)/shard_map/ppermute | solution.py:18
  4.8 0.5 %collective-permute-start.1 = (bf16[4,64,128]{2,1,0:T(8,128)(2,1)S(1)}, bf16[4,64,128]{2,1,0:T(8,128)(2,1)S(1)}, u32[]{:S(2)}, u32[]{:S(2)}) collective-permute-start(bf16[4,64,128]{2,1,0:T(8,128)(2,1)S(1)} %get-tuple-element.54), channel_id=1, source_target_pairs={{0,16},{16,0},{1,17},{17,1},{2,18},{18,2},{3,19},{19,3},{4,20},{20... | collective-permute-start | bytes 196616 | tf_op jit(solution)/shard_map/ppermute | solution.py:23
  5.3 0.7 %collective-permute-done.other_keys = bf16[4,64,128]{2,1,0:T(8,128)(2,1)S(1)} collective-permute-done((bf16[4,64,128]{2,1,0:T(8,128)(2,1)S(1)}, bf16[4,64,128]{2,1,0:T(8,128)(2,1)S(1)}, u32[]{:S(2)}, u32[]{:S(2)}) %collective-permute-start) | collective-permute-done | bytes 65568 | tf_op jit(solution)/shard_map/ppermute | solution.py:23
  6.2 1.5 %collective-permute-start.2 = (bf16[2,4,128,128]{3,2,1,0:T(8,128)(2,1)S(1)}, bf16[2,4,128,128]{3,2,1,0:T(8,128)(2,1)S(1)}, u32[]{:S(2)}, u32[]{:S(2)}) collective-permute-start(bf16[2,4,128,128]{3,2,1,0:T(8,128)(2,1)S(1)} %join_own.1.own), channel_id=1, source_target_pairs={{0,1},{1,2},{2,3},{3,4},{4,5},{5,6},{6,7},{7,8},{8,9},{9,10},{10,1... | collective-permute-start | bytes 786440 | tf_op jit(solution)/shard_map/ppermute | solution.py:18
  9.1 0.7 %collective-permute-done.4.first_third = bf16[10,64,128]{2,1,0:T(8,128)(2,1)S(1)} collective-permute-done((bf16[10,64,128]{2,1,0:T(8,128)(2,1)S(1)}, bf16[10,64,128]{2,1,0:T(8,128)(2,1)S(1)}, u32[]{:S(2)}, u32[]{:S(2)}) %collective-permute-start.4) | collective-permute-done | bytes 163872 | tf_op jit(solution)/shard_map/ppermute | solution.py:23
  9.8 1.5 %own_block.1 = (bf16[16,128,128]{2,1,0:T(8,128)(2,1)S(1)}, bf16[16,128,128]{2,1,0:T(8,128)(2,1)S(1)}, bf16[8,128,256]{2,1,0:T(8,128)(2,1)S(1)}, s32[8,1,256]{2,1...) custom-call(s32[32]{0:T(128)S(1)} %copy-done.2, ...), custom_call_target="tpu_custom_call" | custom-call | flops 1 | tf_op jit(solution)/shard_map/own_block/pallas_call | solution.py:399
  11.4 4.6 %collective-permute-done.3.block.back_two = bf16[2,8,64,128]{3,2,1,0:T(8,128)(2,1)S(1)} collective-permute-done((bf16[2,8,64,128]{3,2,1,0:T(8,128)(2,1)S(1)}, bf16[2,8,64,128]{3,2,1,0:T(8,128)(2,1)S(1)}, u32[]{:S(2)}, u32[]{:S(2)}) %collective-permute-start.3) | collective-permute-done | bytes 262176 | tf_op jit(solution)/shard_map/ppermute | solution.py:18
  16.0 0.5 %collective-permute-start.8 = (bf16[4,64,128]{2,1,0:T(8,128)(2,1)S(1)}, bf16[4,64,128]{2,1,0:T(8,128)(2,1)S(1)}, u32[]{:S(2)}, u32[]{:S(2)}) collective-permute-start(bf16[4,64,128]{2,1,0:T(8,128)(2,1)S(1)} %get-tuple-element.64), channel_id=1, source_target_pairs={{0,16},{16,0},{1,17},{17,1},{2,18},{18,2},{3,19},{19,3},{4,20},{20... | collective-permute-start | bytes 196616 | tf_op jit(solution)/shard_map/ppermute | solution.py:23
  16.5 0.7 %collective-permute-done.7.two_keys = bf16[4,64,128]{2,1,0:T(8,128)(2,1)S(1)} collective-permute-done((bf16[4,64,128]{2,1,0:T(8,128)(2,1)S(1)}, bf16[4,64,128]{2,1,0:T(8,128)(2,1)S(1)}, u32[]{:S(2)}, u32[]{:S(2)}) %collective-permute-start.7) | collective-permute-done | bytes 65568 | tf_op jit(solution)/shard_map/ppermute | solution.py:23
  17.4 0.9 %near_forward.1 = (f32[8,1,256]{2,1,0:T(1,128)S(1)}, f32[8,1,256]{2,1,0:T(1,128)S(1)}, f32[8,128,256]{2,1,0:T(8,128)S(1)}, f32[8,128,256]{2,1,0:T(8,128)S(1)}, f...) custom-call(s32[8,1,256]{2,1,0:T(1,128)S(1)} %get-tuple-element.59.first, ...), custom_call_target="tpu_custom_call" | custom-call | flops 1 | tf_op jit(solution)/shard_map/near_forward/pallas_call | solution.py:399
  18.3 2.3 %collective-permute-done.2.back_one = bf16[2,4,128,128]{3,2,1,0:T(8,128)(2,1)S(1)} collective-permute-done((bf16[2,4,128,128]{3,2,1,0:T(8,128)(2,1)S(1)}, bf16[2,4,128,128]{3,2,1,0:T(8,128)(2,1)S(1)}, u32[]{:S(2)}, u32[]{:S(2)}) %collective-permute-start.2) | collective-permute-done | bytes 262176 | tf_op jit(solution)/shard_map/ppermute | solution.py:18
  20.6 1.5 %last_forward_backward.1 = (bf16[8,128,256]{2,1,0:T(8,128)(2,1)S(1)}, f32[8,1,256]{2,1,0:T(1,128)S(1)}, f32[8,1,256]{2,1,0:T(1,128)S(1)}, bf16[8,128,256]{2,1,0:T(8,128)(2,1)S(1)}, bf16[2,4,128,128]{3,2,1,0:T(8,128)(2,1)S(1)}) custom-call(s32[8,1,256]{2,1,0:T(1,128)S(1)} %get-tuple-element.59.first, bf16[16,128,128]{2,1,0:T(8,128)(2,1)S(1)} %get-tuple-element.60.query_head, ...), custom_call_target="tpu_custom_call" | custom-call | flops 1 | tf_op jit(solution)/shard_map/last_forward_backward/pallas_call | solution.py:399
  22.2 0.5 %two_backward.1 = (bf16[8,128,256]{2,1,0:T(8,128)(2,1)S(1)}, bf16[2,4,64,128]{3,2,1,0:T(8,128)(2,1)S(1)}, bf16[4,64,128]{2,1,0:T(8,128)(2,1)S(1)}, bf16[4,64,128]{2,1,0:T(8,128)(2,1)S(1)}) custom-call(bf16[16,128,128]{2,1,0:T(8,128)(2,1)S(1)} %get-tuple-element.60.query_head, bf16[16,128,128]{2,1,0:T(8,128)(2,1)S(1)} %get-tuple-element.61.grad_head, ...), custom_call_target="tpu_custom_call" | custom-call | flops 1 | tf_op jit(solution)/shard_map/two_backward/pallas_call | solution.py:399
  22.8 0.5 %collective-permute-start.10 = (bf16[4,64,128]{2,1,0:T(8,128)(2,1)S(1)}, bf16[4,64,128]{2,1,0:T(8,128)(2,1)S(1)}, u32[]{:S(2)}, u32[]{:S(2)}) collective-permute-start(bf16[4,64,128]{2,1,0:T(8,128)(2,1)S(1)} %get-tuple-element.86), channel_id=1, source_target_pairs={{0,16},{16,0},{1,17},{17,1},{2,18},{18,2},{3,19},{19,3},{4,20},{20... | collective-permute-start | bytes 196616 | tf_op jit(solution)/shard_map/ppermute | solution.py:23
  23.3 0.7 %collective-permute-done.9.other_keys = bf16[4,64,128]{2,1,0:T(8,128)(2,1)S(1)} collective-permute-done((bf16[4,64,128]{2,1,0:T(8,128)(2,1)S(1)}, bf16[4,64,128]{2,1,0:T(8,128)(2,1)S(1)}, u32[]{:S(2)}, u32[]{:S(2)}) %collective-permute-start.9) | collective-permute-done | bytes 65568 | tf_op jit(solution)/shard_map/ppermute | solution.py:23
  24.3 3.5 %collective-permute-start.16 = (bf16[2,8,64,128]{3,2,1,0:T(8,128)(2,1)S(1)}, bf16[2,8,64,128]{3,2,1,0:T(8,128)(2,1)S(1)}, u32[]{:S(2)}, u32[]{:S(2)}) collective-permute-start(bf16[2,8,64,128]{3,2,1,0:T(8,128)(2,1)S(1)} %join_two.1.after), channel_id=1, source_target_pairs={{0,14},{1,15},{2,0},{3,1},{4,2},{5,3},{6,4},{7,5},{8,6},{9,7},{10,... | collective-permute-start | bytes 786440 | tf_op jit(solution)/shard_map/ppermute | solution.py:18
  28.2 0.8 %query_grad.1 = (bf16[16,64,128]{2,1,0:T(8,128)(2,1)S(1)}, bf16[16,64,128]{2,1,0:T(8,128)(2,1)S(1)}, bf16[10,64,128]{2,1,0:T(8,128)(2,1)S(1)}, bf16[11,64,128]{2,1,0:T(8,128)(2,1)S(1)}, bf16[11,64,128]{2,1,0:T(8,128)(2,1)S(1)}) custom-call(bf16[2,4,128,128]{3,2,1,0:T(8,128)(2,1)S(1)} %join_own.1.own, ...), custom_call_target="tpu_custom_call" | custom-call | flops 1 | tf_op jit(solution)/shard_map/query_grad/pallas_call | solution.py:399
  29.0 0.5 %collective-permute-start.13 = (bf16[11,64,128]{2,1,0:T(8,128)(2,1)S(1)}, bf16[11,64,128]{2,1,0:T(8,128)(2,1)S(1)}, u32[]{:S(2)}, u32[]{:S(2)}) collective-permute-start(bf16[11,64,128]{2,1,0:T(8,128)(2,1)S(1)} %get-tuple-element.92), channel_id=1, source_target_pairs={{0,16},{16,0},{1,17},{17,1},{2,18},{18,2},{3,19},{19,3},{4,20},{20... | collective-permute-start | bytes 540680 | tf_op jit(solution)/shard_map/ppermute | solution.py:23
  29.7 0.5 %collective-permute-start.15 = (bf16[2,4,64,128]{3,2,1,0:T(8,128)(2,1)S(1)}, bf16[2,4,64,128]{3,2,1,0:T(8,128)(2,1)S(1)}, u32[]{:S(2)}, u32[]{:S(2)}) collective-permute-start(bf16[2,4,64,128]{3,2,1,0:T(8,128)(2,1)S(1)} %get-tuple-element.98), channel_id=1, source_target_pairs={{0,16},{16,0},{1,17},{17,1},{2,18},{18,2},{3,19},{19,3},{4,20},{20... | collective-permute-start | bytes 393224 | tf_op jit(solution)/shard_map/ppermute | solution.py:23
  30.2 0.8 %collective-permute-done.11.first_third = bf16[10,64,128]{2,1,0:T(8,128)(2,1)S(1)} collective-permute-done((bf16[10,64,128]{2,1,0:T(8,128)(2,1)S(1)}, bf16[10,64,128]{2,1,0:T(8,128)(2,1)S(1)}, u32[]{:S(2)}, u32[]{:S(2)}) %collective-permute-start.11) | collective-permute-done | bytes 163872 | tf_op jit(solution)/shard_map/ppermute | solution.py:23
  31.0 1.0 %assemble.1 = (bf16[32,64,128]{2,1,0:T(8,128)(2,1)}, bf16[32,64,128]{2,1,0:T(8,128)(2,1)}, f32[8,128]{1,0:T(8,128)S(1)}) custom-call(bf16[16,64,128]{2,1,0:T(8,128)(2,1)S(1)} %get-tuple-element.88.out_mine, bf16[16,64,128]{2,1,0:T(8,128)(2,1)S(1)} %get-tuple-element.89.query_mine, bf16[10,64,128]{2,1,0:T(8,128)(2,1)S(1)} %collective-permute-done.11.first_third, ...), custom_call_target="tpu_custom_call" | custom-call | flops 1 | tf_op jit(solution)/shard_map/assemble/pallas_call | solution.py:399
  32.0 1.6 %collective-permute-done.16.two_total = bf16[2,8,64,128]{3,2,1,0:T(8,128)(2,1)S(1)} collective-permute-done((bf16[2,8,64,128]{3,2,1,0:T(8,128)(2,1)S(1)}, bf16[2,8,64,128]{3,2,1,0:T(8,128)(2,1)S(1)}, u32[]{:S(2)}, u32[]{:S(2)}) %collective-permute-start.16) | collective-permute-done | bytes 262176 | tf_op jit(solution)/shard_map/ppermute | solution.py:18
  33.6 0.8 %total.1 = (bf16[8,64,128]{2,1,0:T(8,128)(2,1)}, bf16[8,64,128]{2,1,0:T(8,128)(2,1)}) custom-call(f32[2,4,64,128]{3,2,1,0:T(8,128)S(1)} %get-tuple-element.97.sum_mine, bf16[2,4,64,128]{3,2,1,0:T(8,128)(2,1)S(1)} %collective-permute-done.15.sum_other, bf16[2,8,64,128]{3,2,1,0:T(8,128)(2,1)S(1)} %collective-permute-done.16.two_total, ...), custom_call_target="tpu_custom_call" | custom-call | flops 1 | tf_op jit(solution)/shard_map/total/pallas_call | solution.py:399
  (31 shorter events, 2.2 us)
Async XLA Ops:
  0.6 7.2 %copy-start.1 = (bf16[32,64,128]{2,1,0:T(8,128)(2,1)S(1)}, bf16[32,64,128]{2,1,0:T(8,128)(2,1)}, u32[]{:S(2)}) copy-start(bf16[32,64,128]{2,1,0:T(8,128)(2,1)} %grads.3) | copy-start | bytes 1572868
  1.7 6.1 %copy-start = (bf16[32,64,128]{2,1,0:T(8,128)(2,1)S(1)}, bf16[32,64,128]{2,1,0:T(8,128)(2,1)}, u32[]{:S(2)}) copy-start(bf16[32,64,128]{2,1,0:T(8,128)(2,1)} %queries.3) | copy-start | bytes 1572868
  1.7 14.2 %collective-permute-start.3 = (bf16[2,8,64,128]{3,2,1,0:T(8,128)(2,1)S(1)}, bf16[2,8,64,128]{3,2,1,0:T(8,128)(2,1)S(1)}, u32[]{:S(2)}, u32[]{:S(2)}) collective-permute-start(bf16[2,8,64,128]{3,2,1,0:T(8,128)(2,1)S(1)} %pad_maximum_fusion.block.own.after), channel_id=1, source_target_pairs={{0,2},{1,3},{2,4},{3,5},{4,6},{5,7},{6,8},{7,9},{8,10},{9,11},{10,... | collective-permute-start | bytes 786440 | tf_op jit(solution)/shard_map/ppermute | solution.py:18
  4.7 1.3 %collective-permute-start = (bf16[4,64,128]{2,1,0:T(8,128)(2,1)S(1)}, bf16[4,64,128]{2,1,0:T(8,128)(2,1)S(1)}, u32[]{:S(2)}, u32[]{:S(2)}) collective-permute-start(bf16[4,64,128]{2,1,0:T(8,128)(2,1)S(1)} %get-tuple-element.53), channel_id=1, source_target_pairs={{0,16},{16,0},{1,17},{17,1},{2,18},{18,2},{3,19},{19,3},{4,20},{20... | collective-permute-start | bytes 196616 | tf_op jit(solution)/shard_map/ppermute | solution.py:23
  4.8 1.4 %collective-permute-start.1 = (bf16[4,64,128]{2,1,0:T(8,128)(2,1)S(1)}, bf16[4,64,128]{2,1,0:T(8,128)(2,1)S(1)}, u32[]{:S(2)}, u32[]{:S(2)}) collective-permute-start(bf16[4,64,128]{2,1,0:T(8,128)(2,1)S(1)} %get-tuple-element.54), channel_id=1, source_target_pairs={{0,16},{16,0},{1,17},{17,1},{2,18},{18,2},{3,19},{19,3},{4,20},{20... | collective-permute-start | bytes 196616 | tf_op jit(solution)/shard_map/ppermute | solution.py:23
  6.2 14.4 %collective-permute-start.2 = (bf16[2,4,128,128]{3,2,1,0:T(8,128)(2,1)S(1)}, bf16[2,4,128,128]{3,2,1,0:T(8,128)(2,1)S(1)}, u32[]{:S(2)}, u32[]{:S(2)}) collective-permute-start(bf16[2,4,128,128]{3,2,1,0:T(8,128)(2,1)S(1)} %join_own.1.own), channel_id=1, source_target_pairs={{0,1},{1,2},{2,3},{3,4},{4,5},{5,6},{6,7},{7,8},{8,9},{9,10},{10,1... | collective-permute-start | bytes 786440 | tf_op jit(solution)/shard_map/ppermute | solution.py:18
  7.8 2.0 %collective-permute-start.5 = (bf16[11,64,128]{2,1,0:T(8,128)(2,1)S(1)}, bf16[11,64,128]{2,1,0:T(8,128)(2,1)S(1)}, u32[]{:S(2)}, u32[]{:S(2)}) collective-permute-start(bf16[11,64,128]{2,1,0:T(8,128)(2,1)S(1)} %get-tuple-element.56), channel_id=1, source_target_pairs={{0,16},{16,0},{1,17},{17,1},{2,18},{18,2},{3,19},{19,3},{4,20},{20... | collective-permute-start | bytes 540680 | tf_op jit(solution)/shard_map/ppermute | solution.py:23
  8.0 1.8 %collective-permute-start.6 = (bf16[11,64,128]{2,1,0:T(8,128)(2,1)S(1)}, bf16[11,64,128]{2,1,0:T(8,128)(2,1)S(1)}, u32[]{:S(2)}, u32[]{:S(2)}) collective-permute-start(bf16[11,64,128]{2,1,0:T(8,128)(2,1)S(1)} %get-tuple-element.57), channel_id=1, source_target_pairs={{0,16},{16,0},{1,17},{17,1},{2,18},{18,2},{3,19},{19,3},{4,20},{20... | collective-permute-start | bytes 540680 | tf_op jit(solution)/shard_map/ppermute | solution.py:23
  8.4 1.4 %copy-start.2 = (s32[32]{0:T(128)S(1)}, s32[32]{0:T(128)}, u32[]{:S(2)}) copy-start(s32[32]{0:T(128)} %spans.1) | copy-start | bytes 388
  8.4 1.4 %collective-permute-start.4 = (bf16[10,64,128]{2,1,0:T(8,128)(2,1)S(1)}, bf16[10,64,128]{2,1,0:T(8,128)(2,1)S(1)}, u32[]{:S(2)}, u32[]{:S(2)}) collective-permute-start(bf16[10,64,128]{2,1,0:T(8,128)(2,1)S(1)} %get-tuple-element.55), channel_id=1, source_target_pairs={{0,16},{16,0},{1,17},{17,1},{2,18},{18,2},{3,19},{19,3},{4,20},{20... | collective-permute-start | bytes 491528 | tf_op jit(solution)/shard_map/ppermute | solution.py:23
  15.9 1.3 %collective-permute-start.7 = (bf16[4,64,128]{2,1,0:T(8,128)(2,1)S(1)}, bf16[4,64,128]{2,1,0:T(8,128)(2,1)S(1)}, u32[]{:S(2)}, u32[]{:S(2)}) collective-permute-start(bf16[4,64,128]{2,1,0:T(8,128)(2,1)S(1)} %get-tuple-element.63), channel_id=1, source_target_pairs={{0,16},{16,0},{1,17},{17,1},{2,18},{18,2},{3,19},{19,3},{4,20},{20... | collective-permute-start | bytes 196616 | tf_op jit(solution)/shard_map/ppermute | solution.py:23
  16.0 1.4 %collective-permute-start.8 = (bf16[4,64,128]{2,1,0:T(8,128)(2,1)S(1)}, bf16[4,64,128]{2,1,0:T(8,128)(2,1)S(1)}, u32[]{:S(2)}, u32[]{:S(2)}) collective-permute-start(bf16[4,64,128]{2,1,0:T(8,128)(2,1)S(1)} %get-tuple-element.64), channel_id=1, source_target_pairs={{0,16},{16,0},{1,17},{17,1},{2,18},{18,2},{3,19},{19,3},{4,20},{20... | collective-permute-start | bytes 196616 | tf_op jit(solution)/shard_map/ppermute | solution.py:23
  22.2 7.5 %collective-permute-start.14 = (bf16[2,4,128,128]{3,2,1,0:T(8,128)(2,1)S(1)}, bf16[2,4,128,128]{3,2,1,0:T(8,128)(2,1)S(1)}, u32[]{:S(2)}, u32[]{:S(2)}) collective-permute-start(bf16[2,4,128,128]{3,2,1,0:T(8,128)(2,1)S(1)} %get-tuple-element.96), channel_id=1, source_target_pairs={{0,15},{1,0},{2,1},{3,2},{4,3},{5,4},{6,5},{7,6},{8,7},{9,8},{10,9... | collective-permute-start | bytes 786440 | tf_op jit(solution)/shard_map/ppermute | solution.py:18
  22.7 1.3 %collective-permute-start.9 = (bf16[4,64,128]{2,1,0:T(8,128)(2,1)S(1)}, bf16[4,64,128]{2,1,0:T(8,128)(2,1)S(1)}, u32[]{:S(2)}, u32[]{:S(2)}) collective-permute-start(bf16[4,64,128]{2,1,0:T(8,128)(2,1)S(1)} %get-tuple-element.85), channel_id=1, source_target_pairs={{0,16},{16,0},{1,17},{17,1},{2,18},{18,2},{3,19},{19,3},{4,20},{20... | collective-permute-start | bytes 196616 | tf_op jit(solution)/shard_map/ppermute | solution.py:23
  22.8 1.4 %collective-permute-start.10 = (bf16[4,64,128]{2,1,0:T(8,128)(2,1)S(1)}, bf16[4,64,128]{2,1,0:T(8,128)(2,1)S(1)}, u32[]{:S(2)}, u32[]{:S(2)}) collective-permute-start(bf16[4,64,128]{2,1,0:T(8,128)(2,1)S(1)} %get-tuple-element.86), channel_id=1, source_target_pairs={{0,16},{16,0},{1,17},{17,1},{2,18},{18,2},{3,19},{19,3},{4,20},{20... | collective-permute-start | bytes 196616 | tf_op jit(solution)/shard_map/ppermute | solution.py:23
  24.3 9.4 %collective-permute-start.16 = (bf16[2,8,64,128]{3,2,1,0:T(8,128)(2,1)S(1)}, bf16[2,8,64,128]{3,2,1,0:T(8,128)(2,1)S(1)}, u32[]{:S(2)}, u32[]{:S(2)}) collective-permute-start(bf16[2,8,64,128]{3,2,1,0:T(8,128)(2,1)S(1)} %join_two.1.after), channel_id=1, source_target_pairs={{0,14},{1,15},{2,0},{3,1},{4,2},{5,3},{6,4},{7,5},{8,6},{9,7},{10,... | collective-permute-start | bytes 786440 | tf_op jit(solution)/shard_map/ppermute | solution.py:18
  29.0 2.0 %collective-permute-start.12 = (bf16[11,64,128]{2,1,0:T(8,128)(2,1)S(1)}, bf16[11,64,128]{2,1,0:T(8,128)(2,1)S(1)}, u32[]{:S(2)}, u32[]{:S(2)}) collective-permute-start(bf16[11,64,128]{2,1,0:T(8,128)(2,1)S(1)} %get-tuple-element.91), channel_id=1, source_target_pairs={{0,16},{16,0},{1,17},{17,1},{2,18},{18,2},{3,19},{19,3},{4,20},{20... | collective-permute-start | bytes 540680 | tf_op jit(solution)/shard_map/ppermute | solution.py:23
  29.0 1.9 %collective-permute-start.13 = (bf16[11,64,128]{2,1,0:T(8,128)(2,1)S(1)}, bf16[11,64,128]{2,1,0:T(8,128)(2,1)S(1)}, u32[]{:S(2)}, u32[]{:S(2)}) collective-permute-start(bf16[11,64,128]{2,1,0:T(8,128)(2,1)S(1)} %get-tuple-element.92), channel_id=1, source_target_pairs={{0,16},{16,0},{1,17},{17,1},{2,18},{18,2},{3,19},{19,3},{4,20},{20... | collective-permute-start | bytes 540680 | tf_op jit(solution)/shard_map/ppermute | solution.py:23
  29.5 1.4 %collective-permute-start.11 = (bf16[10,64,128]{2,1,0:T(8,128)(2,1)S(1)}, bf16[10,64,128]{2,1,0:T(8,128)(2,1)S(1)}, u32[]{:S(2)}, u32[]{:S(2)}) collective-permute-start(bf16[10,64,128]{2,1,0:T(8,128)(2,1)S(1)} %get-tuple-element.90), channel_id=1, source_target_pairs={{0,16},{16,0},{1,17},{17,1},{2,18},{18,2},{3,19},{19,3},{4,20},{20... | collective-permute-start | bytes 491528 | tf_op jit(solution)/shard_map/ppermute | solution.py:23
  29.7 3.9 %collective-permute-start.15 = (bf16[2,4,64,128]{3,2,1,0:T(8,128)(2,1)S(1)}, bf16[2,4,64,128]{3,2,1,0:T(8,128)(2,1)S(1)}, u32[]{:S(2)}, u32[]{:S(2)}) collective-permute-start(bf16[2,4,64,128]{3,2,1,0:T(8,128)(2,1)S(1)} %get-tuple-element.98), channel_id=1, source_target_pairs={{0,16},{16,0},{1,17},{17,1},{2,18},{18,2},{3,19},{19,3},{4,20},{20... | collective-permute-start | bytes 393224 | tf_op jit(solution)/shard_map/ppermute | solution.py:23

commit v15 on v14

v15 whole, which is shorter than its diff:
```python
import functools
import math

import jax
import jax.numpy as jnp
from jax import lax
from jax.experimental import pallas as pl
from jax.experimental.pallas import tpu as pltpu
from jax.sharding import PartitionSpec as P

REACH = 2
SEGMENT = 512

masked_score = -1e30


def shifted(block, axis, distance):
    count = lax.axis_size(axis)
    return lax.ppermute(block, axis, [(i, (i + distance) % count) for i in range(count)])


def swapped(block, axis):
    count = lax.axis_size(axis)
    return lax.ppermute(block, axis, [(i, count - 1 - i) for i in range(count)])


def matmul(left, right, contract):
    return lax.dot_general(
        left, right, ((contract[:1], contract[1:]), ((), ())), preferred_element_type=jnp.float32
    )


def grouped(ref, n, count):
    _, length, width = ref.shape
    return ref[pl.ds(n * count, count)].reshape(count * length, width)


def join(*blocks):
    return jnp.concatenate(blocks, axis=0)


def core_offsets(length):
    core = lax.axis_index("head")
    return core * length, (1 - core) * length


def my_heads(count):
    return pl.ds(lax.axis_index("head") * count, count)


def other_heads(count):
    return pl.ds((1 - lax.axis_index("head")) * count, count)


def lane_tokens(count, length):
    lane = lax.broadcasted_iota(jnp.int32, (1, count * 2 * length), 1)
    token = lane - lane // (2 * length) * (2 * length)
    mine, other = core_offsets(length)
    return jnp.where(token < length, token + mine, token - length + other)


def first_visible(spans, offset, chunks, count, length):
    token = lane_tokens(count, length)
    lane_head = lax.broadcasted_iota(jnp.int32, token.shape, 1) // (2 * length)
    start = lax.axis_index("seq") * 2 * length
    segment_start = token - lax.bitwise_and(offset[0] + start + token, SEGMENT - 1)
    floor = jnp.maximum(segment_start, -start)
    base = lax.axis_index("head") * chunks * count
    result = []
    for n in range(chunks):
        span = jnp.full(token.shape, spans[base + n * count], jnp.int32)
        for a in range(1, count):
            span = jnp.where(lane_head == a, spans[base + n * count + a], span)
        result.append(jnp.maximum(floor, token - span + 1))
    return result


def masked(scores, first, chips_back, token=None):
    length = scores.shape[0] // 2
    row = lax.broadcasted_iota(jnp.int32, (length, scores.shape[1]), 0)
    pieces = []
    for part, offset in enumerate(core_offsets(length)):
        visible = row >= first + (chips_back * 2 * length - offset)
        if token is not None:
            visible &= row <= token - offset
        pieces.append(
            jnp.where(visible, scores[part * length : (part + 1) * length], masked_score)
        )
    return join(*pieces)


def split_kernel(own, first_send, own_send):
    groups, part = own_send.shape[1], first_send.shape[2]
    for core in range(2):
        first_send[:, core] = own[:, core * groups : core * groups + part]
    own_send[...] = own[:, other_heads(groups)]


def join_own_kernel(own, own_other, *halves):
    groups, length = own_other.shape[1:3]
    part = halves[0].shape[1]
    start = lax.axis_index("head") * groups
    for index, target in enumerate(halves):
        target[:, :, pl.ds(0, length)] = own[:, pl.ds(start + index * part, part)]
        target[:, :, pl.ds(length, length)] = own_other[:, pl.ds(index * part, part)]


def split_two_kernel(back_two, *sends):
    for index, send in enumerate(sends):
        send[...] = back_two[index, 1 - lax.axis_index("head")]


def join_two_kernel(back_two, other_keys, other_values, target):
    length = other_keys.shape[1]
    target[:, :, pl.ds(0, length)] = back_two[:, lax.axis_index("head")]
    for index, other in enumerate((other_keys, other_values)):
        target[index, :, pl.ds(length, length)] = other[...]


def own_kernel(
    spans, offset, queries, grads, queries_other, grads_other, *refs
):
    (
        *halves, query_head, grad_head, grad_rows, first, own_max, own_total, own_out,
        own_weights, own_prob_grad,
    ) = refs
    heads, _, width = query_head.shape
    length = queries.shape[1]
    part = halves[0].shape[1]
    groups = part * len(halves)
    chunks = first.shape[0]
    count = heads // chunks
    mine = my_heads(heads)
    query_head[:, pl.ds(0, length)] = queries[mine]
    query_head[:, pl.ds(length, length)] = queries_other[mine]
    grad_head[:, pl.ds(0, length)] = grads[mine]
    grad_head[:, pl.ds(length, length)] = grads_other[mine]
    factor = width ** (-0.5) * math.log2(math.e)
    token = lane_tokens(count, length)
    for n, rows in enumerate(first_visible(spans, offset, chunks, count, length)):
        first[n] = rows

    def block(index, n):
        g = n * groups // chunks
        return halves[g // part][index, g % part]

    def products(n):
        own_prob_grad[n] = matmul(block(1, n), grouped(grad_head, n, count), (1, 1))
        return (matmul(block(0, n), grouped(query_head, n, count), (1, 1)),)

    def softmax(n, scores):
        scores = masked(scores * factor, first[n], 0, token)
        row_max = jnp.max(scores, axis=0, keepdims=True)
        weights = jnp.exp2(scores - row_max)
        own_max[n] = row_max
        own_total[n] = jnp.sum(weights, axis=0, keepdims=True)
        own_weights[n] = weights
        return (weights.astype(jnp.bfloat16),)

    def weigh(n, halved):
        own_out[n] = matmul(block(1, n), halved, (0, 0))
        grad_rows[n] = grouped(grad_head, n, count).T

    pipelined(chunks, products, softmax, weigh)


def near_kernel(
    base, first, query_head, grad_head, back_two, own_max, own_total, own_out, after,
    near_max, near_total, near_out, near_weights, near_prob_grad, own_factor,
):
    groups = back_two.shape[1]
    chunks = near_max.shape[0]
    heads, _, width = query_head.shape
    count = heads // first.shape[0]
    factor = width ** (-0.5) * math.log2(math.e)

    def products(n):
        g = n * groups // chunks
        near_prob_grad[n] = matmul(back_two[1, g], grouped(grad_head, base + n, count), (1, 1))
        return (matmul(back_two[0, g], grouped(query_head, base + n, count), (1, 1)),)

    def softmax(n, scores):
        scores = masked(scores * factor, first[base + n], 2)
        before = own_max[base + n]
        row_max = jnp.maximum(before, jnp.max(scores, axis=0, keepdims=True))
        weights = jnp.exp2(scores - row_max)
        rescale = jnp.exp2(before - row_max)
        own_factor[n] = rescale
        near_max[n] = row_max
        near_total[n] = own_total[base + n] * rescale + jnp.sum(weights, axis=0, keepdims=True)
        near_weights[n] = weights
        return rescale, weights.astype(jnp.bfloat16)

    def weigh(n, rescale, halved):
        weighted = matmul(back_two[1, n * groups // chunks], halved, (0, 0))
        near_out[n] = own_out[base + n] * rescale + weighted

    pipelined(chunks, products, softmax, weigh)


def last_kernel(
    base, first, query_head, grad_head, back_one, grad_rows, near_max, near_total, near_out,
    attended_rows, row_delta, near_factor, one_grad, *targets,
):
    groups = back_one.shape[1]
    chunks = near_max.shape[0]
    heads, _, width = query_head.shape
    count = heads // first.shape[0]
    scale = width ** (-0.5)

    def products(n):
        g = n * groups // chunks
        scores = matmul(back_one[0, g], grouped(query_head, base + n, count), (1, 1))
        prob_grad = matmul(back_one[1, g], grouped(grad_head, base + n, count), (1, 1))
        return scores, prob_grad

    def softmax(n, scores, prob_grad):
        scores = masked(scores * (scale * math.log2(math.e)), first[base + n], 1)
        row_max = jnp.maximum(near_max[n], jnp.max(scores, axis=0, keepdims=True))
        weights = jnp.exp2(scores - row_max)
        rescale = jnp.exp2(near_max[n] - row_max)
        inverse = 1.0 / (near_total[n] * rescale + jnp.sum(weights, axis=0, keepdims=True))
        weighted = matmul(
            back_one[1, n * groups // chunks], weights.astype(jnp.bfloat16), (0, 0)
        )
        near_factor[n] = rescale * inverse
        return prob_grad, weights, weighted, rescale, inverse

    def differentiate(n, prob_grad, weights, weighted, rescale, inverse):
        attended = ((near_out[n] * rescale + weighted) * inverse).astype(jnp.bfloat16)
        delta = jnp.sum(
            grad_rows[base + n].astype(jnp.float32) * attended.astype(jnp.float32),
            axis=0,
            keepdims=True,
        )
        prob = weights * inverse
        score_grad = (prob * (prob_grad - delta)).astype(jnp.bfloat16)
        attended_rows[n] = attended
        row_delta[n] = delta
        one_grad[n] = score_grad
        return score_grad, prob.astype(jnp.bfloat16)

    store = functools.partial(store_rows, targets, scale)
    accumulate = accumulator(query_head, grad_head, base, count, chunks, groups, store)
    pipelined(chunks, products, softmax, differentiate, accumulate)


def store_rows(targets, scale, g, key_part, value_part):
    length = targets[0].shape[2]
    for index, part in enumerate((key_part * scale, value_part)):
        for place, target in enumerate(targets):
            rows = part[place * length : (place + 1) * length]
            target[index, g] = rows.astype(target.dtype)


def pipelined(chunks, *stages):
    ready = [{} for _ in range(len(stages) + 1)]
    for step in range(chunks + len(stages) - 1):
        for depth, stage in enumerate(stages):
            n = step - depth
            if 0 <= n < chunks:
                ready[depth + 1][n] = stage(n, *ready[depth].pop(n, ())) or ()


def accumulator(query_head, grad_head, base, count, chunks, groups, store):
    parts = {}

    def accumulate(n, score_grad, half):
        g = n * groups // chunks
        key_part = matmul(score_grad, grouped(query_head, base + n, count), (1, 0))
        value_part = matmul(half, grouped(grad_head, base + n, count), (1, 0))
        if g in parts:
            key_part, value_part = parts[g][0] + key_part, parts[g][1] + value_part
        parts[g] = (key_part, value_part)
        if (n + 1) * groups // chunks != g:
            store(g, key_part, value_part)

    return accumulate


def two_backward_kernel(
    base, count, query_head, grad_head, near_weights, near_prob_grad, near_factor, row_delta,
    two_grad, *targets,
):
    chunks = near_weights.shape[0]
    groups, _, width = targets[0].shape[1:]

    def differentiate(n):
        prob = near_weights[n] * near_factor[n]
        score_grad = (prob * (near_prob_grad[n] - row_delta[n])).astype(jnp.bfloat16)
        two_grad[n] = score_grad
        return score_grad, prob.astype(jnp.bfloat16)

    store = functools.partial(store_rows, targets, width ** (-0.5))
    accumulate = accumulator(query_head, grad_head, base, count, chunks, groups, store)
    pipelined(chunks, differentiate, accumulate)


def own_backward_kernel(
    base, query_head, grad_head, own_weights, own_prob_grad, near_factor, own_factor, row_delta,
    own_grad, *targets,
):
    chunks = own_grad.shape[0]
    groups, _, width = targets[0].shape[1:]
    count = query_head.shape[0] // own_weights.shape[0]

    def differentiate(n):
        prob = own_weights[base + n] * (own_factor[n] * near_factor[n])
        score_grad = (prob * (own_prob_grad[base + n] - row_delta[n])).astype(jnp.bfloat16)
        own_grad[n] = score_grad
        return score_grad, prob.astype(jnp.bfloat16)

    store = functools.partial(store_rows, targets, width ** (-0.5))
    accumulate = accumulator(query_head, grad_head, base, count, chunks, groups, store)
    pipelined(chunks, differentiate, accumulate)


def pack_kernel(first, second, both):
    both[0] = first[...]
    both[1] = second[...]


def join_back_kernel(first, second, other, *targets):
    core = lax.axis_index("head")
    for index, (mine, target) in enumerate(zip((first, second), targets)):
        target[:, core] = mine[...]
        target[:, 1 - core] = other[index]


def query_kernel(
    own, back_one, back_two, attended_rows, own_grad, one_grad, two_grad, mine, send
):
    chunks, part = own_grad.shape[0], own.shape[1]
    heads, length, width = mine.shape[1:]
    count = heads // chunks
    for n in range(chunks):
        g = n * part // chunks
        rows = pl.ds(n * count, count)
        keys = join(back_two[0, g], back_one[0, g], own[0, g])
        total = matmul(keys, join(two_grad[n], one_grad[n], own_grad[n]), (0, 0))
        total = (total * width ** (-0.5)).astype(jnp.bfloat16)
        for index, columns in enumerate((attended_rows[n], total)):
            block = columns.T.reshape(count, 2 * length, width)
            mine[index, rows] = block[:, :length]
            send[index, rows] = block[:, length:]


def assemble_kernel(
    first_mine, first_other, second_mine, second_other, out, query_grad, token
):
    count = first_mine.shape[1]
    start = lax.axis_index("head") * 2 * count
    other_start = (1 - lax.axis_index("head")) * 2 * count
    for index, target in enumerate((out, query_grad)):
        target[pl.ds(start, count)] = first_mine[index]
        target[pl.ds(other_start, count)] = first_other[index]
        target[pl.ds(start + count, count)] = second_mine[index]
        target[pl.ds(other_start + count, count)] = second_other[index]
    token[...] = jnp.zeros(token.shape, token.dtype)


def sum_kernel(
    own_first, one_first, two_first, own_mine, own_send, sum_mine, sum_send
):
    length, part = sum_mine.shape[2], own_first.shape[1]
    arrived = one_first[...].astype(jnp.float32) + two_first[...].astype(jnp.float32)
    total = own_first[...] + arrived
    sum_mine[:, pl.ds(0, part)] = total[:, :, :length]
    sum_send[:, pl.ds(0, part)] = total[:, :, length:].astype(jnp.bfloat16)
    sum_mine[:, pl.ds(part, part)] = own_mine[...]
    sum_send[:, pl.ds(part, part)] = own_send[...]


def final_kernel(sum_mine, sum_other, one_total, two_total, after, key_grad, value_grad):
    groups, part = sum_mine.shape[1], two_total.shape[2]
    core = lax.axis_index("head")
    for index, result in enumerate((key_grad, value_grad)):
        for place, sums in ((core, sum_mine), (1 - core, sum_other)):
            start = place * groups
            first = sums[index, pl.ds(0, part)].astype(jnp.float32)
            second = sums[index, pl.ds(part, part)].astype(jnp.float32)
            second += one_total[index, place].astype(jnp.float32)
            second += two_total[index, place].astype(jnp.float32)
            result[pl.ds(start, part)] = first.astype(jnp.bfloat16)
            result[pl.ds(start + part, part)] = second.astype(jnp.bfloat16)


def shards(query_matrix, key_matrix, value_matrix, output_gradient, query_head_spans, slab_offset):
    groups, length, width = key_matrix.shape
    heads = query_matrix.shape[0]
    cores = lax.axis_size("head")
    tokens = cores * length
    groups_here, heads_here = groups // cores, heads // cores
    part = groups_here // 2
    count = max(1, min(heads // groups, 256 // tokens))
    chunks = heads_here // count
    each = chunks // 2
    lanes = count * tokens
    half, full = jnp.bfloat16, jnp.float32
    vmem = pl.BlockSpec(memory_space=pltpu.VMEM)
    smem = pl.BlockSpec(memory_space=pltpu.SMEM)

    def call(kernel, name, outs, arrays, scalars=0, flops=1):
        return pl.pallas_call(
            kernel,
            out_shape=tuple(jax.ShapeDtypeStruct(shape, kind) for shape, kind in outs),
            in_specs=[smem] * scalars + [vmem] * (len(arrays) - scalars),
            out_specs=(vmem,) * len(outs),
            compiler_params=pltpu.CompilerParams(vmem_limit_bytes=40 * 1024 * 1024),
            cost_estimate=pl.CostEstimate(flops=flops, bytes_accessed=0, transcendentals=0),
            name=name,
        )(*arrays)

    def rows_of(rows, kind, number=each):
        return ((number, rows, lanes), kind)

    stat = rows_of(1, full)
    pair = (2, groups_here, length, width)
    token_half = ((2, cores, part, length, width), half)
    small_half = ((2, part, length, width), half)
    chip_half = ((2, part, tokens, width), half)
    half_rows = ((heads_here, length, width), half)
    chip_rows = ((heads_here, tokens, width), half)

    queries_other = swapped(query_matrix, "head")
    grads_other = swapped(output_gradient, "head")
    own = jnp.stack([key_matrix, value_matrix])
    first_send, own_send = call(split_kernel, "split_own", [token_half, (pair, half)], (own,))
    back_two_first = shifted(first_send, "seq", 2)
    own_halves = call(
        join_own_kernel, "join_own", [chip_half] * 2, (own, swapped(own_send, "head"))
    )
    back_one = [shifted(own_halves[0], "seq", 1)]
    back_two = [None, shifted(own_halves[1], "seq", 2)]
    back_one.append(shifted(own_halves[1], "seq", 1))
    (
        query_head, grad_head, grad_rows, first, own_max, own_total, own_out, own_weights,
        own_prob_grad,
    ) = call(
        own_kernel,
        "own_block",
        [
            chip_rows, chip_rows, rows_of(width, half, chunks), rows_of(1, jnp.int32, chunks),
            rows_of(1, full, chunks), rows_of(1, full, chunks), rows_of(width, full, chunks),
            rows_of(tokens, full, chunks), rows_of(tokens, full, chunks),
        ],
        (
            query_head_spans, slab_offset, query_matrix, output_gradient, queries_other,
            grads_other, *own_halves,
        ),
        scalars=2,
    )
    back_two_first, first = lax.optimization_barrier((back_two_first, first))
    two_sends = call(
        split_two_kernel, "split_two", [((part, length, width), half)] * 2, (back_two_first,)
    )
    (back_two[0],) = call(
        join_two_kernel,
        "join_two",
        [chip_half],
        (back_two_first, *[swapped(send, "head") for send in two_sends]),
    )

    split_half = [small_half] * 2
    kept = []
    after = first
    for index in range(2):
        base = index * each
        label = "ab"[index]
        parts = [chip_half] if index == 0 else split_half
        near_max, near_total, near_out, near_weights, near_prob_grad, own_factor = call(
            functools.partial(near_kernel, base),
            "near_" + label,
            [stat, stat, rows_of(width, full), rows_of(tokens, full), rows_of(tokens, full), stat],
            (first, query_head, grad_head, back_two[index], own_max, own_total, own_out, after),
        )
        back_one[index], near_max = lax.optimization_barrier((back_one[index], near_max))
        attended_rows, row_delta, near_factor, one_grad, *one_parts = call(
            functools.partial(last_kernel, base),
            "last_" + label,
            [rows_of(width, half), stat, stat, rows_of(tokens, half)] + parts,
            (
                first, query_head, grad_head, back_one[index], grad_rows, near_max, near_total,
                near_out,
            ),
        )
        two_grad, *two_parts = call(
            functools.partial(two_backward_kernel, base, count),
            "two_back_" + label,
            [rows_of(tokens, half)] + parts,
            (query_head, grad_head, near_weights, near_prob_grad, near_factor, row_delta),
        )
        if index == 0:
            one_part, two_part = one_parts[0], two_parts[0]
            after = two_part
        else:
            (both,) = call(
                pack_kernel, "pack", [((2,) + small_half[0], half)], (one_parts[1], two_parts[1])
            )
            one_part, two_part = call(
                join_back_kernel,
                "join_back",
                [token_half] * 2,
                (one_parts[0], two_parts[0], swapped(both, "head")),
            )
        one_total = shifted(one_part, "seq", -1)
        two_total = shifted(two_part, "seq", -2)
        own_grad, *own_parts = call(
            functools.partial(own_backward_kernel, base),
            "own_back_" + label,
            [rows_of(tokens, half)]
            + ([(chip_half[0], full)] if index == 0 else [(small_half[0], full), small_half]),
            (
                query_head, grad_head, own_weights, own_prob_grad, near_factor, own_factor,
                row_delta,
            ),
        )
        rows_half = (heads_here // 2, length, width)
        mine, *sends = call(
            query_kernel,
            "query_" + label,
            [((2,) + rows_half, half)]
            + [((2,) + rows_half, half)],
            (
                own_halves[index], back_one[index], back_two[index], attended_rows, own_grad,
                one_grad, two_grad,
            ),
        )
        others = [swapped(send, "head") for send in sends]
        kept.append((one_total, two_total, own_parts, mine, others))
    token_shape = ((8, 128), full)
    attn_out, query_grad, token = call(
        assemble_kernel,
        "assemble",
        [(query_matrix.shape, half)] * 2 + [token_shape],
        (kept[0][3], kept[0][4][0], kept[1][3], kept[1][4][0]),
    )
    sum_mine, sum_send = call(
        sum_kernel,
        "sum",
        [(pair, full), (pair, half)],
        (*kept[0][2], kept[0][0], kept[0][1], *kept[1][2]),
        flops=10**8,
    )
    key_grad, value_grad = call(
        final_kernel,
        "total",
        [(key_matrix.shape, half)] * 2,
        (sum_mine, swapped(sum_send, "head"), kept[1][0], kept[1][1], token),
    )
    return (attn_out, query_grad, key_grad, value_grad)


def solution(mesh):
    tokens = P(None, ("seq", "head"), None)
    return jax.shard_map(
        shards,
        mesh=mesh,
        in_specs=(tokens, tokens, tokens, tokens, P(), P()),
        out_specs=(tokens, tokens, tokens, tokens),
        check_vma=False,
    )
```

time: 34.5 us -> 41 us (1.19)
  starting transfers between devices: 11.6 us -> 19.5 us
  waiting for transfers between devices: 12.6 us -> 10.2 us
  Pallas kernels: 7.67 us -> 8.69 us
    ppermute x4 -> x8, starting transfers between devices: 8.12 us -> 16.6 us  [shifted(): lax.ppermute(block, axis, [(i, (i + distance) % count) for i in range(cou...]
    ppermute x13 -> x9, waiting for transfers between devices: 4.14 us -> 0.88 us  [swapped(): return lax.ppermute(block, axis, [(i, count - 1 - i) for i in range(count)])]
    pallas_call x14 -> x20, Pallas kernels: 7.67 us -> 8.69 us  [call(): pl.pallas_call(kernel, out_shape=tuple((jax.ShapeDtypeStruct(shape, kind)...]
    ppermute x4 -> x8, waiting for transfers between devices: 8.48 us -> 9.3 us  [shifted(): lax.ppermute(block, axis, [(i, (i + distance) % count) for i in range(cou...]
    ppermute x13 -> x9, starting transfers between devices: 3.5 us -> 2.88 us  [swapped(): return lax.ppermute(block, axis, [(i, count - 1 - i) for i in range(count)])]
  transfers between devices with their start and end apart: 17 -> 17, of which waited for: 11 -> 6; matrix products, arithmetic and copies ran while one was open for 0% -> 3% of each run, Pallas kernels for 16% -> 19%
where the time goes in v15:
time: 41 us; the launch traced here: 40.9 us
  starting transfers between devices  19.5 us (48%)
  waiting for transfers between devices  10.2 us (25%)
  Pallas kernels  8.69 us (21%)
  between operations  1.46 us (4%)
  other arithmetic  1.08 us (3%)
    ppermute x8, starting transfers between devices, shifted(): lax.ppermute(block, axis, [(i, (i + distance) % count) for i in range(cou...  16.6 us
    ppermute x8, waiting for transfers between devices, shifted(): lax.ppermute(block, axis, [(i, (i + distance) % count) for i in range(cou...  9.3 us
    pallas_call x20, Pallas kernels, call(): pl.pallas_call(kernel, out_shape=tuple((jax.ShapeDtypeStruct(shape, kind)...  8.69 us
    ppermute x9, starting transfers between devices, swapped(): return lax.ppermute(block, axis, [(i, count - 1 - i) for i in range(count)])  2.88 us
    another operation x1, other arithmetic, shards(): own = jnp.stack([key_matrix, value_matrix])  1.08 us
    ppermute x9, waiting for transfers between devices, swapped(): return lax.ppermute(block, axis, [(i, count - 1 - i) for i in range(count)])  0.88 us
  transfers between devices with their start and end apart: 17, of which 6 were waited for; matrix products, arithmetic and copies ran while one was open for 3% of the time, Pallas kernels for 19%

profile of v15, /device:TPU:0, one launch (start us, length us, event | category | flops | bytes accessed | tf_op | source)
XLA Modules:
  0.0 40.9 jit_solution(7822328862760677962)
XLA Ops:
  0.6 0.5 %collective-permute-start.3 = (bf16[32,64,128]{2,1,0:T(8,128)(2,1)}, bf16[32,64,128]{2,1,0:T(8,128)(2,1)S(1)}, u32[]{:S(2)}, u32[]{:S(2)}) collective-permute-start(bf16[32,64,128]{2,1,0:T(8,128)(2,1)} %queries.1), channel_id=1, source_target_pairs={{0,16},{16,0},{1,17},{17,1},{2,18},{18,2},{3,19},{19,3},{4,20},{20... | collective-permute-start | bytes 1572872 | tf_op jit(solution)/shard_map/ppermute | solution.py:24
  1.2 1.1 %pad_maximum_fusion.own = bf16[2,8,64,128]{3,2,1,0:T(8,128)(2,1)S(1)} fusion(bf16[1,8,64,128]{3,2,1,0:T(8,128)(2,1)} %bitcast.2, bf16[1,8,64,128]{3,2,1,0:T(8,128)(2,1)} %bitcast.3), kind=kLoop, calls=%fused_computation | loop fusion | flops 131072 | bytes 524288 | tf_op jit(solution)/shard_map/stack | solution.py:427
  2.3 0.5 %collective-permute-start = (bf16[2,4,64,128]{3,2,1,0:T(8,128)(2,1)S(1)}, bf16[2,4,64,128]{3,2,1,0:T(8,128)(2,1)S(1)}, u32[]{:S(2)}, u32[]{:S(2)}) collective-permute-start(bf16[2,4,64,128]{3,2,1,0:T(8,128)(2,1)S(1)} %get-tuple-element.71), channel_id=1, source_target_pairs={{0,16},{16,0},{1,17},{17,1},{2,18},{18,2},{3,19},{19,3},{4,20},{20... | collective-permute-start | bytes 393224 | tf_op jit(solution)/shard_map/ppermute | solution.py:24
  2.8 2.6 %collective-permute-start.2 = (bf16[2,2,2,64,128]{4,3,2,1,0:T(8,128)(2,1)S(1)}, bf16[2,2,2,64,128]{4,3,2,1,0:T(8,128)(2,1)S(1)}, u32[]{:S(2)}, u32[]{:S(2)}) collective-permute-start(bf16[2,2,2,64,128]{4,3,2,1,0:T(8,128)(2,1)S(1)} %get-tuple-element.73), channel_id=1, source_target_pairs={{0,2},{1,3},{2,4},{3,5},{4,6},{5,7},{6,8},{7,9},{8,10},{9,11},{10,... | collective-permute-start | bytes 393224 | tf_op jit(solution)/shard_map/ppermute | solution.py:19
  5.5 1.5 %collective-permute-start.1 = (bf16[2,2,128,128]{3,2,1,0:T(8,128)(2,1)S(1)}, bf16[2,2,128,128]{3,2,1,0:T(8,128)(2,1)S(1)}, u32[]{:S(2)}, u32[]{:S(2)}) collective-permute-start(bf16[2,2,128,128]{3,2,1,0:T(8,128)(2,1)S(1)} %get-tuple-element.72.refs_0_.own), channel_id=1, source_target_pairs={{0,1},{1,2},{2,3},{3,4},{4,5},{5,6},{6,7},{7,8},{8,9},{9,10},{10,1... | collective-permute-start | bytes 393224 | tf_op jit(solution)/shard_map/ppermute | solution.py:19
  7.0 1.5 %collective-permute-start.9 = (bf16[2,2,128,128]{3,2,1,0:T(8,128)(2,1)S(1)}, bf16[2,2,128,128]{3,2,1,0:T(8,128)(2,1)S(1)}, u32[]{:S(2)}, u32[]{:S(2)}) collective-permute-start(bf16[2,2,128,128]{3,2,1,0:T(8,128)(2,1)S(1)} %get-tuple-element.74.refs_1_.own), channel_id=1, source_target_pairs={{0,2},{1,3},{2,4},{3,5},{4,6},{5,7},{6,8},{7,9},{8,10},{9,11},{10,... | collective-permute-start | bytes 393224 | tf_op jit(solution)/shard_map/ppermute | solution.py:19
  8.5 1.5 %collective-permute-start.8 = (bf16[2,2,128,128]{3,2,1,0:T(8,128)(2,1)S(1)}, bf16[2,2,128,128]{3,2,1,0:T(8,128)(2,1)S(1)}, u32[]{:S(2)}, u32[]{:S(2)}) collective-permute-start(bf16[2,2,128,128]{3,2,1,0:T(8,128)(2,1)S(1)} %get-tuple-element.74.refs_1_.own), channel_id=1, source_target_pairs={{0,1},{1,2},{2,3},{3,4},{4,5},{5,6},{6,7},{7,8},{8,9},{9,10},{10,1... | collective-permute-start | bytes 393224 | tf_op jit(solution)/shard_map/ppermute | solution.py:19
  10.7 1.5 %own_block.1 = (bf16[16,128,128]{2,1,0:T(8,128)(2,1)S(1)}, bf16[16,128,128]{2,1,0:T(8,128)(2,1)S(1)}, bf16[8,128,256]{2,1,0:T(8,128)(2,1)S(1)}, s32[8,1,256]{2,1...) custom-call(s32[32]{0:T(128)S(1)} %copy-done.2, ...), custom_call_target="tpu_custom_call" | custom-call | flops 1 | tf_op jit(solution)/shard_map/own_block/pallas_call | solution.py:404
  12.3 2.6 %collective-permute-done.2.back_two = bf16[2,2,2,64,128]{4,3,2,1,0:T(8,128)(2,1)S(1)} collective-permute-done((bf16[2,2,2,64,128]{4,3,2,1,0:T(8,128)(2,1)S(1)}, bf16[2,2,2,64,128]{4,3,2,1,0:T(8,128)(2,1)S(1)}, u32[]{:S(2)}, u32[]{:S(2)}) %collective-permute-start.2) | collective-permute-done | bytes 131104 | tf_op jit(solution)/shard_map/ppermute | solution.py:19
  14.9 0.5 %collective-permute-start.6 = (bf16[2,64,128]{2,1,0:T(8,128)(2,1)S(1)}, bf16[2,64,128]{2,1,0:T(8,128)(2,1)S(1)}, u32[]{:S(2)}, u32[]{:S(2)}) collective-permute-start(bf16[2,64,128]{2,1,0:T(8,128)(2,1)S(1)} %get-tuple-element.81), channel_id=1, source_target_pairs={{0,16},{16,0},{1,17},{17,1},{2,18},{18,2},{3,19},{19,3},{4,20},{20... | collective-permute-start | bytes 98312 | tf_op jit(solution)/shard_map/ppermute | solution.py:24
  15.4 0.7 %collective-permute-done.5.other_keys = bf16[2,64,128]{2,1,0:T(8,128)(2,1)S(1)} collective-permute-done((bf16[2,64,128]{2,1,0:T(8,128)(2,1)S(1)}, bf16[2,64,128]{2,1,0:T(8,128)(2,1)S(1)}, u32[]{:S(2)}, u32[]{:S(2)}) %collective-permute-start.5) | collective-permute-done | bytes 32800 | tf_op jit(solution)/shard_map/ppermute | solution.py:24
  16.3 0.7 %near_a.1 = (f32[4,1,256]{2,1,0:T(1,128)S(1)}, f32[4,1,256]{2,1,0:T(1,128)S(1)}, f32[4,128,256]{2,1,0:T(8,128)S(1)}, f32[4,128,256]{2,1,0:T(8,128)S(1)}, f32[4,1...) custom-call(s32[8,1,256]{2,1,0:T(1,128)S(1)} %get-tuple-element.76.first.after, ...), custom_call_target="tpu_custom_call" | custom-call | flops 1 | tf_op jit(solution)/shard_map/near_a/pallas_call | solution.py:404
  16.9 1.3 %collective-permute-done.1.back_one = bf16[2,2,128,128]{3,2,1,0:T(8,128)(2,1)S(1)} collective-permute-done((bf16[2,2,128,128]{3,2,1,0:T(8,128)(2,1)S(1)}, bf16[2,2,128,128]{3,2,1,0:T(8,128)(2,1)S(1)}, u32[]{:S(2)}, u32[]{:S(2)}) %collective-permute-start.1) | collective-permute-done | bytes 131104 | tf_op jit(solution)/shard_map/ppermute | solution.py:19
  18.2 0.9 %last_a.1 = (bf16[4,128,256]{2,1,0:T(8,128)(2,1)S(1)}, f32[4,1,256]{2,1,0:T(1,128)S(1)}, f32[4,1,256]{2,1,0:T(1,128)S(1)}, bf16[4,128,256]{2,1,0:T(8,128)(2,1)S(1)}, bf16[2,2,128,128]{3,2,1,0:T(8,128)(2,1)S(1)}) custom-call(s32[8,1,256]{2,1,0:T(1,128)S(1)} %get-tuple-element.76.first.after, bf16[16,128,128]{2,1,0:T(8,128)(2,1)S(1)} %get-tuple-element.77.query_head, ...), custom_call_target="tpu_custom_call" | custom-call | flops 1 | tf_op jit(solution)/shard_map/last_a/pallas_call | solution.py:404
  19.8 4.0 %collective-permute-start.12 = (bf16[2,2,128,128]{3,2,1,0:T(8,128)(2,1)S(1)}, bf16[2,2,128,128]{3,2,1,0:T(8,128)(2,1)S(1)}, u32[]{:S(2)}, u32[]{:S(2)}) collective-permute-start(bf16[2,2,128,128]{3,2,1,0:T(8,128)(2,1)S(1)} %get-tuple-element.104.after), channel_id=1, source_target_pairs={{0,14},{1,15},{2,0},{3,1},{4,2},{5,3},{6,4},{7,5},{8,6},{9,7},{10,... | collective-permute-start | bytes 393224 | tf_op jit(solution)/shard_map/ppermute | solution.py:19
  24.7 0.6 %near_b.1 = (f32[4,1,256]{2,1,0:T(1,128)S(1)}, f32[4,1,256]{2,1,0:T(1,128)S(1)}, f32[4,128,256]{2,1,0:T(8,128)S(1)}, f32[4,128,256]{2,1,0:T(8,128)S(1)}, f32[4,1...) custom-call(s32[8,1,256]{2,1,0:T(1,128)S(1)} %get-tuple-element.76.first.after, ...), custom_call_target="tpu_custom_call" | custom-call | flops 1 | tf_op jit(solution)/shard_map/near_b/pallas_call | solution.py:404
  25.4 0.9 %last_b.1 = (bf16[4,128,256]{2,1,0:T(8,128)(2,1)S(1)}, f32[4,1,256]{2,1,0:T(1,128)S(1)}, f32[4,1,256]{2,1,0:T(1,128)S(1)}, bf16[4,128,256]{2,1,0:T(8,128)(2,1)S(...) custom-call(s32[8,1,256]{2,1,0:T(1,128)S(1)} %get-tuple-element.76.first.after, ...), custom_call_target="tpu_custom_call" | custom-call | flops 1 | tf_op jit(solution)/shard_map/last_b/pallas_call | solution.py:404
  26.9 0.5 %collective-permute-start.14 = (bf16[2,2,2,64,128]{4,3,2,1,0:T(8,128)(2,1)S(1)}, bf16[2,2,2,64,128]{4,3,2,1,0:T(8,128)(2,1)S(1)}, u32[]{:S(2)}, u32[]{:S(2)}) collective-permute-start(bf16[2,2,2,64,128]{4,3,2,1,0:T(8,128)(2,1)S(1)} %pack.1), channel_id=1, source_target_pairs={{0,16},{16,0},{1,17},{17,1},{2,18},{18,2},{3,19},{19,3},{4,20},{20... | collective-permute-start | bytes 393224 | tf_op jit(solution)/shard_map/ppermute | solution.py:24
  28.1 0.5 %collective-permute-start.13 = (bf16[2,4,64,128]{3,2,1,0:T(8,128)(2,1)S(1)}, bf16[2,4,64,128]{3,2,1,0:T(8,128)(2,1)S(1)}, u32[]{:S(2)}, u32[]{:S(2)}) collective-permute-start(bf16[2,4,64,128]{3,2,1,0:T(8,128)(2,1)S(1)} %get-tuple-element.128), channel_id=1, source_target_pairs={{0,16},{16,0},{1,17},{17,1},{2,18},{18,2},{3,19},{19,3},{4,20},{20... | collective-permute-start | bytes 393224 | tf_op jit(solution)/shard_map/ppermute | solution.py:24
  28.6 5.0 %collective-permute-start.15 = (bf16[2,2,2,64,128]{4,3,2,1,0:T(8,128)(2,1)S(1)}, bf16[2,2,2,64,128]{4,3,2,1,0:T(8,128)(2,1)S(1)}, u32[]{:S(2)}, u32[]{:S(2)}) collective-permute-start(bf16[2,2,2,64,128]{4,3,2,1,0:T(8,128)(2,1)S(1)} %get-tuple-element.133), channel_id=1, source_target_pairs={{0,15},{1,0},{2,1},{3,2},{4,3},{5,4},{6,5},{7,6},{8,7},{9,8},{10,9... | collective-permute-start | bytes 393224 | tf_op jit(solution)/shard_map/ppermute | solution.py:19
  33.7 1.0 %assemble.1 = (bf16[32,64,128]{2,1,0:T(8,128)(2,1)}, bf16[32,64,128]{2,1,0:T(8,128)(2,1)}, f32[8,128]{1,0:T(8,128)S(1)}) custom-call(bf16[2,8,64,128]{3,2,1,0:T(8,128)(2,1)S(1)} %get-tuple-element.102.first_mine, bf16[2,8,64,128]{3,2,1,0:T(8,128)(2,1)S(1)} %collective-permute-done.7.first_other, bf16[2,8,64,128]{3,2,1,0:T(8,128)(2,1)S(1)} %get-tuple-element.119.second_mine, ...), custom_call_target="tpu_custom_call" | custom-call | flops 1 | tf_op jit(solution)/shard_map/assemble/pallas_call | solution.py:404
  34.7 2.7 %collective-permute-done.15.one_total = bf16[2,2,2,64,128]{4,3,2,1,0:T(8,128)(2,1)S(1)} collective-permute-done((bf16[2,2,2,64,128]{4,3,2,1,0:T(8,128)(2,1)S(1)}, bf16[2,2,2,64,128]{4,3,2,1,0:T(8,128)(2,1)S(1)}, u32[]{:S(2)}, u32[]{:S(2)}) %collective-permute-start.15) | collective-permute-done | bytes 131104 | tf_op jit(solution)/shard_map/ppermute | solution.py:19
  37.5 2.7 %collective-permute-done.16.two_total = bf16[2,2,2,64,128]{4,3,2,1,0:T(8,128)(2,1)S(1)} collective-permute-done((bf16[2,2,2,64,128]{4,3,2,1,0:T(8,128)(2,1)S(1)}, bf16[2,2,2,64,128]{4,3,2,1,0:T(8,128)(2,1)S(1)}, u32[]{:S(2)}, u32[]{:S(2)}) %collective-permute-start.16) | collective-permute-done | bytes 131104 | tf_op jit(solution)/shard_map/ppermute | solution.py:19
  40.1 0.7 %total.1 = (bf16[8,64,128]{2,1,0:T(8,128)(2,1)}, bf16[8,64,128]{2,1,0:T(8,128)(2,1)}) custom-call(f32[2,4,64,128]{3,2,1,0:T(8,128)S(1)} %get-tuple-element.127.sum_mine, bf16[2,4,64,128]{3,2,1,0:T(8,128)(2,1)S(1)} %collective-permute-done.13.sum_other, bf16[2,2,2,64,128]{4,3,2,1,0:T(8,128)(2,1)S(1)} %collective-permute-done.15.one_total, ...), custom_call_target="tpu_custom_call" | custom-call | flops 1 | tf_op jit(solution)/shard_map/total/pallas_call | solution.py:404
  (37 shorter events, 3.2 us)
Async XLA Ops:
  0.6 7.9 %collective-permute-start.3 = (bf16[32,64,128]{2,1,0:T(8,128)(2,1)}, bf16[32,64,128]{2,1,0:T(8,128)(2,1)S(1)}, u32[]{:S(2)}, u32[]{:S(2)}) collective-permute-start(bf16[32,64,128]{2,1,0:T(8,128)(2,1)} %queries.1), channel_id=1, source_target_pairs={{0,16},{16,0},{1,17},{17,1},{2,18},{18,2},{3,19},{19,3},{4,20},{20... | collective-permute-start | bytes 1572872 | tf_op jit(solution)/shard_map/ppermute | solution.py:24
  1.1 9.5 %collective-permute-start.4 = (bf16[32,64,128]{2,1,0:T(8,128)(2,1)}, bf16[32,64,128]{2,1,0:T(8,128)(2,1)S(1)}, u32[]{:S(2)}, u32[]{:S(2)}) collective-permute-start(bf16[32,64,128]{2,1,0:T(8,128)(2,1)} %grads.1), channel_id=1, source_target_pairs={{0,16},{16,0},{1,17},{17,1},{2,18},{18,2},{3,19},{19,3},{4,20},{20... | collective-permute-start | bytes 1572872 | tf_op jit(solution)/shard_map/ppermute | solution.py:24
  1.2 9.5 %copy-start = (bf16[32,64,128]{2,1,0:T(8,128)(2,1)S(1)}, bf16[32,64,128]{2,1,0:T(8,128)(2,1)}, u32[]{:S(2)}) copy-start(bf16[32,64,128]{2,1,0:T(8,128)(2,1)} %queries.1) | copy-start | bytes 1572868
  1.2 9.5 %copy-start.1 = (bf16[32,64,128]{2,1,0:T(8,128)(2,1)S(1)}, bf16[32,64,128]{2,1,0:T(8,128)(2,1)}, u32[]{:S(2)}) copy-start(bf16[32,64,128]{2,1,0:T(8,128)(2,1)} %grads.1) | copy-start | bytes 1572868
  2.3 3.1 %collective-permute-start = (bf16[2,4,64,128]{3,2,1,0:T(8,128)(2,1)S(1)}, bf16[2,4,64,128]{3,2,1,0:T(8,128)(2,1)S(1)}, u32[]{:S(2)}, u32[]{:S(2)}) collective-permute-start(bf16[2,4,64,128]{3,2,1,0:T(8,128)(2,1)S(1)} %get-tuple-element.71), channel_id=1, source_target_pairs={{0,16},{16,0},{1,17},{17,1},{2,18},{18,2},{3,19},{19,3},{4,20},{20... | collective-permute-start | bytes 393224 | tf_op jit(solution)/shard_map/ppermute | solution.py:24
  2.8 12.0 %collective-permute-start.2 = (bf16[2,2,2,64,128]{4,3,2,1,0:T(8,128)(2,1)S(1)}, bf16[2,2,2,64,128]{4,3,2,1,0:T(8,128)(2,1)S(1)}, u32[]{:S(2)}, u32[]{:S(2)}) collective-permute-start(bf16[2,2,2,64,128]{4,3,2,1,0:T(8,128)(2,1)S(1)} %get-tuple-element.73), channel_id=1, source_target_pairs={{0,2},{1,3},{2,4},{3,5},{4,6},{5,7},{6,8},{7,9},{8,10},{9,11},{10,... | collective-permute-start | bytes 393224 | tf_op jit(solution)/shard_map/ppermute | solution.py:19
  5.5 12.7 %collective-permute-start.1 = (bf16[2,2,128,128]{3,2,1,0:T(8,128)(2,1)S(1)}, bf16[2,2,128,128]{3,2,1,0:T(8,128)(2,1)S(1)}, u32[]{:S(2)}, u32[]{:S(2)}) collective-permute-start(bf16[2,2,128,128]{3,2,1,0:T(8,128)(2,1)S(1)} %get-tuple-element.72.refs_0_.own), channel_id=1, source_target_pairs={{0,1},{1,2},{2,3},{3,4},{4,5},{5,6},{6,7},{7,8},{8,9},{9,10},{10,1... | collective-permute-start | bytes 393224 | tf_op jit(solution)/shard_map/ppermute | solution.py:19
  7.0 3.7 %copy-start.2 = (s32[32]{0:T(128)S(1)}, s32[32]{0:T(128)}, u32[]{:S(2)}) copy-start(s32[32]{0:T(128)} %spans.1) | copy-start | bytes 388
  7.0 17.7 %collective-permute-start.9 = (bf16[2,2,128,128]{3,2,1,0:T(8,128)(2,1)S(1)}, bf16[2,2,128,128]{3,2,1,0:T(8,128)(2,1)S(1)}, u32[]{:S(2)}, u32[]{:S(2)}) collective-permute-start(bf16[2,2,128,128]{3,2,1,0:T(8,128)(2,1)S(1)} %get-tuple-element.74.refs_1_.own), channel_id=1, source_target_pairs={{0,2},{1,3},{2,4},{3,5},{4,6},{5,7},{6,8},{7,9},{8,10},{9,11},{10,... | collective-permute-start | bytes 393224 | tf_op jit(solution)/shard_map/ppermute | solution.py:19
  8.5 16.8 %collective-permute-start.8 = (bf16[2,2,128,128]{3,2,1,0:T(8,128)(2,1)S(1)}, bf16[2,2,128,128]{3,2,1,0:T(8,128)(2,1)S(1)}, u32[]{:S(2)}, u32[]{:S(2)}) collective-permute-start(bf16[2,2,128,128]{3,2,1,0:T(8,128)(2,1)S(1)} %get-tuple-element.74.refs_1_.own), channel_id=1, source_target_pairs={{0,1},{1,2},{2,3},{3,4},{4,5},{5,6},{6,7},{7,8},{8,9},{9,10},{10,1... | collective-permute-start | bytes 393224 | tf_op jit(solution)/shard_map/ppermute | solution.py:19
  14.9 1.2 %collective-permute-start.5 = (bf16[2,64,128]{2,1,0:T(8,128)(2,1)S(1)}, bf16[2,64,128]{2,1,0:T(8,128)(2,1)S(1)}, u32[]{:S(2)}, u32[]{:S(2)}) collective-permute-start(bf16[2,64,128]{2,1,0:T(8,128)(2,1)S(1)} %get-tuple-element.80), channel_id=1, source_target_pairs={{0,16},{16,0},{1,17},{17,1},{2,18},{18,2},{3,19},{19,3},{4,20},{20... | collective-permute-start | bytes 98312 | tf_op jit(solution)/shard_map/ppermute | solution.py:24
  14.9 1.4 %collective-permute-start.6 = (bf16[2,64,128]{2,1,0:T(8,128)(2,1)S(1)}, bf16[2,64,128]{2,1,0:T(8,128)(2,1)S(1)}, u32[]{:S(2)}, u32[]{:S(2)}) collective-permute-start(bf16[2,64,128]{2,1,0:T(8,128)(2,1)S(1)} %get-tuple-element.81), channel_id=1, source_target_pairs={{0,16},{16,0},{1,17},{17,1},{2,18},{18,2},{3,19},{19,3},{4,20},{20... | collective-permute-start | bytes 98312 | tf_op jit(solution)/shard_map/ppermute | solution.py:24
  19.1 8.9 %collective-permute-start.11 = (bf16[2,2,128,128]{3,2,1,0:T(8,128)(2,1)S(1)}, bf16[2,2,128,128]{3,2,1,0:T(8,128)(2,1)S(1)}, u32[]{:S(2)}, u32[]{:S(2)}) collective-permute-start(bf16[2,2,128,128]{3,2,1,0:T(8,128)(2,1)S(1)} %get-tuple-element.124), channel_id=1, source_target_pairs={{0,15},{1,0},{2,1},{3,2},{4,3},{5,4},{6,5},{7,6},{8,7},{9,8},{10,9... | collective-permute-start | bytes 393224 | tf_op jit(solution)/shard_map/ppermute | solution.py:19
  19.8 8.2 %collective-permute-start.12 = (bf16[2,2,128,128]{3,2,1,0:T(8,128)(2,1)S(1)}, bf16[2,2,128,128]{3,2,1,0:T(8,128)(2,1)S(1)}, u32[]{:S(2)}, u32[]{:S(2)}) collective-permute-start(bf16[2,2,128,128]{3,2,1,0:T(8,128)(2,1)S(1)} %get-tuple-element.104.after), channel_id=1, source_target_pairs={{0,14},{1,15},{2,0},{3,1},{4,2},{5,3},{6,4},{7,5},{8,6},{9,7},{10,... | collective-permute-start | bytes 393224 | tf_op jit(solution)/shard_map/ppermute | solution.py:19
  24.6 9.1 %collective-permute-start.7 = (bf16[2,8,64,128]{3,2,1,0:T(8,128)(2,1)S(1)}, bf16[2,8,64,128]{3,2,1,0:T(8,128)(2,1)S(1)}, u32[]{:S(2)}, u32[]{:S(2)}) collective-permute-start(bf16[2,8,64,128]{3,2,1,0:T(8,128)(2,1)S(1)} %get-tuple-element.103), channel_id=1, source_target_pairs={{0,16},{16,0},{1,17},{17,1},{2,18},{18,2},{3,19},{19,3},{4,20},{20... | collective-permute-start | bytes 786440 | tf_op jit(solution)/shard_map/ppermute | solution.py:24
  26.9 1.6 %collective-permute-start.14 = (bf16[2,2,2,64,128]{4,3,2,1,0:T(8,128)(2,1)S(1)}, bf16[2,2,2,64,128]{4,3,2,1,0:T(8,128)(2,1)S(1)}, u32[]{:S(2)}, u32[]{:S(2)}) collective-permute-start(bf16[2,2,2,64,128]{4,3,2,1,0:T(8,128)(2,1)S(1)} %pack.1), channel_id=1, source_target_pairs={{0,16},{16,0},{1,17},{17,1},{2,18},{18,2},{3,19},{19,3},{4,20},{20... | collective-permute-start | bytes 393224 | tf_op jit(solution)/shard_map/ppermute | solution.py:24
  27.9 5.8 %collective-permute-start.10 = (bf16[2,8,64,128]{3,2,1,0:T(8,128)(2,1)S(1)}, bf16[2,8,64,128]{3,2,1,0:T(8,128)(2,1)S(1)}, u32[]{:S(2)}, u32[]{:S(2)}) collective-permute-start(bf16[2,8,64,128]{3,2,1,0:T(8,128)(2,1)S(1)} %get-tuple-element.120), channel_id=1, source_target_pairs={{0,16},{16,0},{1,17},{17,1},{2,18},{18,2},{3,19},{19,3},{4,20},{20... | collective-permute-start | bytes 786440 | tf_op jit(solution)/shard_map/ppermute | solution.py:24
  28.1 6.7 %collective-permute-start.13 = (bf16[2,4,64,128]{3,2,1,0:T(8,128)(2,1)S(1)}, bf16[2,4,64,128]{3,2,1,0:T(8,128)(2,1)S(1)}, u32[]{:S(2)}, u32[]{:S(2)}) collective-permute-start(bf16[2,4,64,128]{3,2,1,0:T(8,128)(2,1)S(1)} %get-tuple-element.128), channel_id=1, source_target_pairs={{0,16},{16,0},{1,17},{17,1},{2,18},{18,2},{3,19},{19,3},{4,20},{20... | collective-permute-start | bytes 393224 | tf_op jit(solution)/shard_map/ppermute | solution.py:24
  28.6 8.9 %collective-permute-start.15 = (bf16[2,2,2,64,128]{4,3,2,1,0:T(8,128)(2,1)S(1)}, bf16[2,2,2,64,128]{4,3,2,1,0:T(8,128)(2,1)S(1)}, u32[]{:S(2)}, u32[]{:S(2)}) collective-permute-start(bf16[2,2,2,64,128]{4,3,2,1,0:T(8,128)(2,1)S(1)} %get-tuple-element.133), channel_id=1, source_target_pairs={{0,15},{1,0},{2,1},{3,2},{4,3},{5,4},{6,5},{7,6},{8,7},{9,8},{10,9... | collective-permute-start | bytes 393224 | tf_op jit(solution)/shard_map/ppermute | solution.py:19
  33.7 6.5 %collective-permute-start.16 = (bf16[2,2,2,64,128]{4,3,2,1,0:T(8,128)(2,1)S(1)}, bf16[2,2,2,64,128]{4,3,2,1,0:T(8,128)(2,1)S(1)}, u32[]{:S(2)}, u32[]{:S(2)}) collective-permute-start(bf16[2,2,2,64,128]{4,3,2,1,0:T(8,128)(2,1)S(1)} %get-tuple-element.134), channel_id=1, source_target_pairs={{0,14},{1,15},{2,0},{3,1},{4,2},{5,3},{6,4},{7,5},{8,6},{9,7},{10,... | collective-permute-start | bytes 393224 | tf_op jit(solution)/shard_map/ppermute | solution.py:19

commit v16 on v14

--- a/solution.py
+++ b/solution.py
@@ -13,9 +13,10 @@
 masked_score = -1e30
 
 
-def shifted(block, axis, distance):
+def shifted(block, axis, distance, ring=True):
     count = lax.axis_size(axis)
-    return lax.ppermute(block, axis, [(i, (i + distance) % count) for i in range(count)])
+    route = [(i, (i + distance) % count) for i in range(count) if ring or i + distance < count]
+    return lax.ppermute(block, axis, route)
 
 
 def swapped(block, axis):
@@ -425,7 +426,7 @@
     (own_head,) = call(
         join_own_kernel, "join_own", [chip_pair], (own, *[swapped(send, "head") for send in own_sends])
     )
-    back_one = shifted(own_head, "seq", 1)
+    back_one = shifted(own_head, "seq", 1, ring=False)
     sends = call(
         split_rows_kernel,
         "split_rows",

time: 34.5 us -> 34.6 us (level)
  waiting for transfers between devices: 12.6 us -> 6.59 us
  starting transfers between devices: 11.6 us -> 17.6 us
    ppermute x4, waiting for transfers between devices: 8.48 us -> 2.45 us  [shifted(): return lax.ppermute(block, axis, route)]
    ppermute x4, starting transfers between devices: 8.12 us -> 14.1 us  [shifted(): return lax.ppermute(block, axis, route)]
  transfers between devices with their start and end apart: 17 -> 17, of which waited for: 11 -> 10; matrix products, arithmetic and copies ran while one was open for 0% -> 0% of each run, Pallas kernels for 16% -> 16%
where the time goes in v16:
time: 34.6 us; the launch traced here: 34.4 us
  starting transfers between devices  17.6 us (51%)
  Pallas kernels  7.69 us (22%)
  waiting for transfers between devices  6.59 us (19%)
  between operations  1.44 us (4%)
  other arithmetic  1.05 us (3%)
    ppermute x4, starting transfers between devices, shifted(): return lax.ppermute(block, axis, route)  14.1 us
    pallas_call x14, Pallas kernels, call(): pl.pallas_call(kernel, out_shape=tuple((jax.ShapeDtypeStruct(shape, kind)...  7.69 us
    ppermute x13, waiting for transfers between devices, swapped(): return lax.ppermute(block, axis, [(i, count - 1 - i) for i in range(count)])  4.14 us
    ppermute x13, starting transfers between devices, swapped(): return lax.ppermute(block, axis, [(i, count - 1 - i) for i in range(count)])  3.5 us
    ppermute x4, waiting for transfers between devices, shifted(): return lax.ppermute(block, axis, route)  2.45 us
    another operation x1, other arithmetic, shards(): own = jnp.stack([key_matrix, value_matrix])  1.05 us
  transfers between devices with their start and end apart: 17, of which 10 were waited for; matrix products, arithmetic and copies ran while one was open for 0% of the time, Pallas kernels for 16%

profile of v16, /device:TPU:0, one launch (start us, length us, event | category | flops | bytes accessed | tf_op | source)
XLA Modules:
  0.0 34.4 jit_solution(14397481054136324815)
XLA Ops:
  0.6 1.1 %pad_maximum_fusion.block.own.after = bf16[2,8,64,128]{3,2,1,0:T(8,128)(2,1)S(1)} fusion(bf16[1,8,64,128]{3,2,1,0:T(8,128)(2,1)} %bitcast.2, bf16[1,8,64,128]{3,2,1,0:T(8,128)(2,1)} %bitcast.3), kind=kLoop, calls=%fused_computation | loop fusion | flops 131072 | bytes 524288 | tf_op jit(solution)/shard_map/stack | solution.py:423
  1.7 3.0 %collective-permute-start.3 = (bf16[2,8,64,128]{3,2,1,0:T(8,128)(2,1)S(1)}, bf16[2,8,64,128]{3,2,1,0:T(8,128)(2,1)S(1)}, u32[]{:S(2)}, u32[]{:S(2)}) collective-permute-start(bf16[2,8,64,128]{3,2,1,0:T(8,128)(2,1)S(1)} %pad_maximum_fusion.block.own.after), channel_id=1, source_target_pairs={{0,2},{1,3},{2,4},{3,5},{4,6},{5,7},{6,8},{7,9},{8,10},{9,11},{10,... | collective-permute-start | bytes 786440 | tf_op jit(solution)/shard_map/ppermute | solution.py:19
  4.8 0.5 %collective-permute-start.1 = (bf16[4,64,128]{2,1,0:T(8,128)(2,1)S(1)}, bf16[4,64,128]{2,1,0:T(8,128)(2,1)S(1)}, u32[]{:S(2)}, u32[]{:S(2)}) collective-permute-start(bf16[4,64,128]{2,1,0:T(8,128)(2,1)S(1)} %get-tuple-element.54), channel_id=1, source_target_pairs={{0,16},{16,0},{1,17},{17,1},{2,18},{18,2},{3,19},{19,3},{4,20},{20... | collective-permute-start | bytes 196616 | tf_op jit(solution)/shard_map/ppermute | solution.py:24
  5.3 0.7 %collective-permute-done.other_keys = bf16[4,64,128]{2,1,0:T(8,128)(2,1)S(1)} collective-permute-done((bf16[4,64,128]{2,1,0:T(8,128)(2,1)S(1)}, bf16[4,64,128]{2,1,0:T(8,128)(2,1)S(1)}, u32[]{:S(2)}, u32[]{:S(2)}) %collective-permute-start) | collective-permute-done | bytes 65568 | tf_op jit(solution)/shard_map/ppermute | solution.py:24
  6.2 3.4 %collective-permute-start.2 = (bf16[2,4,128,128]{3,2,1,0:T(8,128)(2,1)S(1)}, bf16[2,4,128,128]{3,2,1,0:T(8,128)(2,1)S(1)}, u32[]{:S(2)}, u32[]{:S(2)}) collective-permute-start(bf16[2,4,128,128]{3,2,1,0:T(8,128)(2,1)S(1)} %join_own.1.own), channel_id=1, source_target_pairs={{0,1},{1,2},{2,3},{3,4},{4,5},{5,6},{6,7},{7,8},{8,9},{9,10},{10,1... | collective-permute-start | bytes 786440 | tf_op jit(solution)/shard_map/ppermute | solution.py:19
  11.0 0.7 %collective-permute-done.4.first_third = bf16[10,64,128]{2,1,0:T(8,128)(2,1)S(1)} collective-permute-done((bf16[10,64,128]{2,1,0:T(8,128)(2,1)S(1)}, bf16[10,64,128]{2,1,0:T(8,128)(2,1)S(1)}, u32[]{:S(2)}, u32[]{:S(2)}) %collective-permute-start.4) | collective-permute-done | bytes 163872 | tf_op jit(solution)/shard_map/ppermute | solution.py:24
  11.7 1.5 %own_block.1 = (bf16[16,128,128]{2,1,0:T(8,128)(2,1)S(1)}, bf16[16,128,128]{2,1,0:T(8,128)(2,1)S(1)}, bf16[8,128,256]{2,1,0:T(8,128)(2,1)S(1)}, s32[8,1,256]{2,1...) custom-call(s32[32]{0:T(128)S(1)} %copy-done.2, ...), custom_call_target="tpu_custom_call" | custom-call | flops 1 | tf_op jit(solution)/shard_map/own_block/pallas_call | solution.py:400
  13.3 0.8 %collective-permute-done.3.block.back_two = bf16[2,8,64,128]{3,2,1,0:T(8,128)(2,1)S(1)} collective-permute-done((bf16[2,8,64,128]{3,2,1,0:T(8,128)(2,1)S(1)}, bf16[2,8,64,128]{3,2,1,0:T(8,128)(2,1)S(1)}, u32[]{:S(2)}, u32[]{:S(2)}) %collective-permute-start.3) | collective-permute-done | bytes 262176 | tf_op jit(solution)/shard_map/ppermute | solution.py:19
  14.2 0.5 %collective-permute-start.8 = (bf16[4,64,128]{2,1,0:T(8,128)(2,1)S(1)}, bf16[4,64,128]{2,1,0:T(8,128)(2,1)S(1)}, u32[]{:S(2)}, u32[]{:S(2)}) collective-permute-start(bf16[4,64,128]{2,1,0:T(8,128)(2,1)S(1)} %get-tuple-element.64), channel_id=1, source_target_pairs={{0,16},{16,0},{1,17},{17,1},{2,18},{18,2},{3,19},{19,3},{4,20},{20... | collective-permute-start | bytes 196616 | tf_op jit(solution)/shard_map/ppermute | solution.py:24
  14.7 0.7 %collective-permute-done.7.two_keys = bf16[4,64,128]{2,1,0:T(8,128)(2,1)S(1)} collective-permute-done((bf16[4,64,128]{2,1,0:T(8,128)(2,1)S(1)}, bf16[4,64,128]{2,1,0:T(8,128)(2,1)S(1)}, u32[]{:S(2)}, u32[]{:S(2)}) %collective-permute-start.7) | collective-permute-done | bytes 65568 | tf_op jit(solution)/shard_map/ppermute | solution.py:24
  15.6 0.9 %near_forward.1 = (f32[8,1,256]{2,1,0:T(1,128)S(1)}, f32[8,1,256]{2,1,0:T(1,128)S(1)}, f32[8,128,256]{2,1,0:T(8,128)S(1)}, f32[8,128,256]{2,1,0:T(8,128)S(1)}, f...) custom-call(s32[8,1,256]{2,1,0:T(1,128)S(1)} %get-tuple-element.59.first, ...), custom_call_target="tpu_custom_call" | custom-call | flops 1 | tf_op jit(solution)/shard_map/near_forward/pallas_call | solution.py:400
  16.5 1.5 %last_forward_backward.1 = (bf16[8,128,256]{2,1,0:T(8,128)(2,1)S(1)}, f32[8,1,256]{2,1,0:T(1,128)S(1)}, f32[8,1,256]{2,1,0:T(1,128)S(1)}, bf16[8,128,256]{2,1,0:T(8,128)(2,1)S(1)}, bf16[2,4,128,128]{3,2,1,0:T(8,128)(2,1)S(1)}) custom-call(s32[8,1,256]{2,1,0:T(1,128)S(1)} %get-tuple-element.59.first, bf16[16,128,128]{2,1,0:T(8,128)(2,1)S(1)} %get-tuple-element.60.query_head, ...), custom_call_target="tpu_custom_call" | custom-call | flops 1 | tf_op jit(solution)/shard_map/last_forward_backward/pallas_call | solution.py:400
  18.1 4.4 %collective-permute-start.14 = (bf16[2,4,128,128]{3,2,1,0:T(8,128)(2,1)S(1)}, bf16[2,4,128,128]{3,2,1,0:T(8,128)(2,1)S(1)}, u32[]{:S(2)}, u32[]{:S(2)}) collective-permute-start(bf16[2,4,128,128]{3,2,1,0:T(8,128)(2,1)S(1)} %get-tuple-element.96), channel_id=1, source_target_pairs={{0,15},{1,0},{2,1},{3,2},{4,3},{5,4},{6,5},{7,6},{8,7},{9,8},{10,9... | collective-permute-start | bytes 786440 | tf_op jit(solution)/shard_map/ppermute | solution.py:19
  22.4 0.5 %two_backward.1 = (bf16[8,128,256]{2,1,0:T(8,128)(2,1)S(1)}, bf16[2,4,64,128]{3,2,1,0:T(8,128)(2,1)S(1)}, bf16[4,64,128]{2,1,0:T(8,128)(2,1)S(1)}, bf16[4,64,128]{2,1,0:T(8,128)(2,1)S(1)}) custom-call(bf16[16,128,128]{2,1,0:T(8,128)(2,1)S(1)} %get-tuple-element.60.query_head, bf16[16,128,128]{2,1,0:T(8,128)(2,1)S(1)} %get-tuple-element.61.grad_head, ...), custom_call_target="tpu_custom_call" | custom-call | flops 1 | tf_op jit(solution)/shard_map/two_backward/pallas_call | solution.py:400
  23.0 0.5 %collective-permute-start.10 = (bf16[4,64,128]{2,1,0:T(8,128)(2,1)S(1)}, bf16[4,64,128]{2,1,0:T(8,128)(2,1)S(1)}, u32[]{:S(2)}, u32[]{:S(2)}) collective-permute-start(bf16[4,64,128]{2,1,0:T(8,128)(2,1)S(1)} %get-tuple-element.86), channel_id=1, source_target_pairs={{0,16},{16,0},{1,17},{17,1},{2,18},{18,2},{3,19},{19,3},{4,20},{20... | collective-permute-start | bytes 196616 | tf_op jit(solution)/shard_map/ppermute | solution.py:24
  23.5 0.7 %collective-permute-done.9.other_keys = bf16[4,64,128]{2,1,0:T(8,128)(2,1)S(1)} collective-permute-done((bf16[4,64,128]{2,1,0:T(8,128)(2,1)S(1)}, bf16[4,64,128]{2,1,0:T(8,128)(2,1)S(1)}, u32[]{:S(2)}, u32[]{:S(2)}) %collective-permute-start.9) | collective-permute-done | bytes 65568 | tf_op jit(solution)/shard_map/ppermute | solution.py:24
  24.4 3.3 %collective-permute-start.16 = (bf16[2,8,64,128]{3,2,1,0:T(8,128)(2,1)S(1)}, bf16[2,8,64,128]{3,2,1,0:T(8,128)(2,1)S(1)}, u32[]{:S(2)}, u32[]{:S(2)}) collective-permute-start(bf16[2,8,64,128]{3,2,1,0:T(8,128)(2,1)S(1)} %join_two.1.after), channel_id=1, source_target_pairs={{0,14},{1,15},{2,0},{3,1},{4,2},{5,3},{6,4},{7,5},{8,6},{9,7},{10,... | collective-permute-start | bytes 786440 | tf_op jit(solution)/shard_map/ppermute | solution.py:19
  28.2 0.8 %query_grad.1 = (bf16[16,64,128]{2,1,0:T(8,128)(2,1)S(1)}, bf16[16,64,128]{2,1,0:T(8,128)(2,1)S(1)}, bf16[10,64,128]{2,1,0:T(8,128)(2,1)S(1)}, bf16[11,64,128]{2,1,0:T(8,128)(2,1)S(1)}, bf16[11,64,128]{2,1,0:T(8,128)(2,1)S(1)}) custom-call(bf16[2,4,128,128]{3,2,1,0:T(8,128)(2,1)S(1)} %join_own.1.own, ...), custom_call_target="tpu_custom_call" | custom-call | flops 1 | tf_op jit(solution)/shard_map/query_grad/pallas_call | solution.py:400
  29.0 0.5 %collective-permute-start.13 = (bf16[11,64,128]{2,1,0:T(8,128)(2,1)S(1)}, bf16[11,64,128]{2,1,0:T(8,128)(2,1)S(1)}, u32[]{:S(2)}, u32[]{:S(2)}) collective-permute-start(bf16[11,64,128]{2,1,0:T(8,128)(2,1)S(1)} %get-tuple-element.92), channel_id=1, source_target_pairs={{0,16},{16,0},{1,17},{17,1},{2,18},{18,2},{3,19},{19,3},{4,20},{20... | collective-permute-start | bytes 540680 | tf_op jit(solution)/shard_map/ppermute | solution.py:24
  29.7 0.5 %collective-permute-start.15 = (bf16[2,4,64,128]{3,2,1,0:T(8,128)(2,1)S(1)}, bf16[2,4,64,128]{3,2,1,0:T(8,128)(2,1)S(1)}, u32[]{:S(2)}, u32[]{:S(2)}) collective-permute-start(bf16[2,4,64,128]{3,2,1,0:T(8,128)(2,1)S(1)} %get-tuple-element.98), channel_id=1, source_target_pairs={{0,16},{16,0},{1,17},{17,1},{2,18},{18,2},{3,19},{19,3},{4,20},{20... | collective-permute-start | bytes 393224 | tf_op jit(solution)/shard_map/ppermute | solution.py:24
  30.2 0.8 %collective-permute-done.11.first_third = bf16[10,64,128]{2,1,0:T(8,128)(2,1)S(1)} collective-permute-done((bf16[10,64,128]{2,1,0:T(8,128)(2,1)S(1)}, bf16[10,64,128]{2,1,0:T(8,128)(2,1)S(1)}, u32[]{:S(2)}, u32[]{:S(2)}) %collective-permute-start.11) | collective-permute-done | bytes 163872 | tf_op jit(solution)/shard_map/ppermute | solution.py:24
  31.0 1.0 %assemble.1 = (bf16[32,64,128]{2,1,0:T(8,128)(2,1)}, bf16[32,64,128]{2,1,0:T(8,128)(2,1)}, f32[8,128]{1,0:T(8,128)S(1)}) custom-call(bf16[16,64,128]{2,1,0:T(8,128)(2,1)S(1)} %get-tuple-element.88.out_mine, bf16[16,64,128]{2,1,0:T(8,128)(2,1)S(1)} %get-tuple-element.89.query_mine, bf16[10,64,128]{2,1,0:T(8,128)(2,1)S(1)} %collective-permute-done.11.first_third, ...), custom_call_target="tpu_custom_call" | custom-call | flops 1 | tf_op jit(solution)/shard_map/assemble/pallas_call | solution.py:400
  32.0 1.6 %collective-permute-done.16.two_total = bf16[2,8,64,128]{3,2,1,0:T(8,128)(2,1)S(1)} collective-permute-done((bf16[2,8,64,128]{3,2,1,0:T(8,128)(2,1)S(1)}, bf16[2,8,64,128]{3,2,1,0:T(8,128)(2,1)S(1)}, u32[]{:S(2)}, u32[]{:S(2)}) %collective-permute-start.16) | collective-permute-done | bytes 262176 | tf_op jit(solution)/shard_map/ppermute | solution.py:19
  33.6 0.8 %total.1 = (bf16[8,64,128]{2,1,0:T(8,128)(2,1)}, bf16[8,64,128]{2,1,0:T(8,128)(2,1)}) custom-call(f32[2,4,64,128]{3,2,1,0:T(8,128)S(1)} %get-tuple-element.97.sum_mine, bf16[2,4,64,128]{3,2,1,0:T(8,128)(2,1)S(1)} %collective-permute-done.15.sum_other, bf16[2,8,64,128]{3,2,1,0:T(8,128)(2,1)S(1)} %collective-permute-done.16.two_total, ...), custom_call_target="tpu_custom_call" | custom-call | flops 1 | tf_op jit(solution)/shard_map/total/pallas_call | solution.py:400
  (31 shorter events, 2.1 us)
Async XLA Ops:
  0.6 9.0 %copy-start.1 = (bf16[32,64,128]{2,1,0:T(8,128)(2,1)S(1)}, bf16[32,64,128]{2,1,0:T(8,128)(2,1)}, u32[]{:S(2)}) copy-start(bf16[32,64,128]{2,1,0:T(8,128)(2,1)} %grads.3) | copy-start | bytes 1572868
  1.7 8.0 %copy-start = (bf16[32,64,128]{2,1,0:T(8,128)(2,1)S(1)}, bf16[32,64,128]{2,1,0:T(8,128)(2,1)}, u32[]{:S(2)}) copy-start(bf16[32,64,128]{2,1,0:T(8,128)(2,1)} %queries.3) | copy-start | bytes 1572868
  1.7 12.4 %collective-permute-start.3 = (bf16[2,8,64,128]{3,2,1,0:T(8,128)(2,1)S(1)}, bf16[2,8,64,128]{3,2,1,0:T(8,128)(2,1)S(1)}, u32[]{:S(2)}, u32[]{:S(2)}) collective-permute-start(bf16[2,8,64,128]{3,2,1,0:T(8,128)(2,1)S(1)} %pad_maximum_fusion.block.own.after), channel_id=1, source_target_pairs={{0,2},{1,3},{2,4},{3,5},{4,6},{5,7},{6,8},{7,9},{8,10},{9,11},{10,... | collective-permute-start | bytes 786440 | tf_op jit(solution)/shard_map/ppermute | solution.py:19
  4.7 1.3 %collective-permute-start = (bf16[4,64,128]{2,1,0:T(8,128)(2,1)S(1)}, bf16[4,64,128]{2,1,0:T(8,128)(2,1)S(1)}, u32[]{:S(2)}, u32[]{:S(2)}) collective-permute-start(bf16[4,64,128]{2,1,0:T(8,128)(2,1)S(1)} %get-tuple-element.53), channel_id=1, source_target_pairs={{0,16},{16,0},{1,17},{17,1},{2,18},{18,2},{3,19},{19,3},{4,20},{20... | collective-permute-start | bytes 196616 | tf_op jit(solution)/shard_map/ppermute | solution.py:24
  4.8 1.4 %collective-permute-start.1 = (bf16[4,64,128]{2,1,0:T(8,128)(2,1)S(1)}, bf16[4,64,128]{2,1,0:T(8,128)(2,1)S(1)}, u32[]{:S(2)}, u32[]{:S(2)}) collective-permute-start(bf16[4,64,128]{2,1,0:T(8,128)(2,1)S(1)} %get-tuple-element.54), channel_id=1, source_target_pairs={{0,16},{16,0},{1,17},{17,1},{2,18},{18,2},{3,19},{19,3},{4,20},{20... | collective-permute-start | bytes 196616 | tf_op jit(solution)/shard_map/ppermute | solution.py:24
  6.2 10.3 %collective-permute-start.2 = (bf16[2,4,128,128]{3,2,1,0:T(8,128)(2,1)S(1)}, bf16[2,4,128,128]{3,2,1,0:T(8,128)(2,1)S(1)}, u32[]{:S(2)}, u32[]{:S(2)}) collective-permute-start(bf16[2,4,128,128]{3,2,1,0:T(8,128)(2,1)S(1)} %join_own.1.own), channel_id=1, source_target_pairs={{0,1},{1,2},{2,3},{3,4},{4,5},{5,6},{6,7},{7,8},{8,9},{9,10},{10,1... | collective-permute-start | bytes 786440 | tf_op jit(solution)/shard_map/ppermute | solution.py:19
  9.7 2.0 %collective-permute-start.5 = (bf16[11,64,128]{2,1,0:T(8,128)(2,1)S(1)}, bf16[11,64,128]{2,1,0:T(8,128)(2,1)S(1)}, u32[]{:S(2)}, u32[]{:S(2)}) collective-permute-start(bf16[11,64,128]{2,1,0:T(8,128)(2,1)S(1)} %get-tuple-element.56), channel_id=1, source_target_pairs={{0,16},{16,0},{1,17},{17,1},{2,18},{18,2},{3,19},{19,3},{4,20},{20... | collective-permute-start | bytes 540680 | tf_op jit(solution)/shard_map/ppermute | solution.py:24
  9.9 1.8 %collective-permute-start.6 = (bf16[11,64,128]{2,1,0:T(8,128)(2,1)S(1)}, bf16[11,64,128]{2,1,0:T(8,128)(2,1)S(1)}, u32[]{:S(2)}, u32[]{:S(2)}) collective-permute-start(bf16[11,64,128]{2,1,0:T(8,128)(2,1)S(1)} %get-tuple-element.57), channel_id=1, source_target_pairs={{0,16},{16,0},{1,17},{17,1},{2,18},{18,2},{3,19},{19,3},{4,20},{20... | collective-permute-start | bytes 540680 | tf_op jit(solution)/shard_map/ppermute | solution.py:24
  10.3 1.4 %copy-start.2 = (s32[32]{0:T(128)S(1)}, s32[32]{0:T(128)}, u32[]{:S(2)}) copy-start(s32[32]{0:T(128)} %spans.1) | copy-start | bytes 388
  10.3 1.4 %collective-permute-start.4 = (bf16[10,64,128]{2,1,0:T(8,128)(2,1)S(1)}, bf16[10,64,128]{2,1,0:T(8,128)(2,1)S(1)}, u32[]{:S(2)}, u32[]{:S(2)}) collective-permute-start(bf16[10,64,128]{2,1,0:T(8,128)(2,1)S(1)} %get-tuple-element.55), channel_id=1, source_target_pairs={{0,16},{16,0},{1,17},{17,1},{2,18},{18,2},{3,19},{19,3},{4,20},{20... | collective-permute-start | bytes 491528 | tf_op jit(solution)/shard_map/ppermute | solution.py:24
  14.1 1.3 %collective-permute-start.7 = (bf16[4,64,128]{2,1,0:T(8,128)(2,1)S(1)}, bf16[4,64,128]{2,1,0:T(8,128)(2,1)S(1)}, u32[]{:S(2)}, u32[]{:S(2)}) collective-permute-start(bf16[4,64,128]{2,1,0:T(8,128)(2,1)S(1)} %get-tuple-element.63), channel_id=1, source_target_pairs={{0,16},{16,0},{1,17},{17,1},{2,18},{18,2},{3,19},{19,3},{4,20},{20... | collective-permute-start | bytes 196616 | tf_op jit(solution)/shard_map/ppermute | solution.py:24
  14.2 1.4 %collective-permute-start.8 = (bf16[4,64,128]{2,1,0:T(8,128)(2,1)S(1)}, bf16[4,64,128]{2,1,0:T(8,128)(2,1)S(1)}, u32[]{:S(2)}, u32[]{:S(2)}) collective-permute-start(bf16[4,64,128]{2,1,0:T(8,128)(2,1)S(1)} %get-tuple-element.64), channel_id=1, source_target_pairs={{0,16},{16,0},{1,17},{17,1},{2,18},{18,2},{3,19},{19,3},{4,20},{20... | collective-permute-start | bytes 196616 | tf_op jit(solution)/shard_map/ppermute | solution.py:24
  18.1 11.6 %collective-permute-start.14 = (bf16[2,4,128,128]{3,2,1,0:T(8,128)(2,1)S(1)}, bf16[2,4,128,128]{3,2,1,0:T(8,128)(2,1)S(1)}, u32[]{:S(2)}, u32[]{:S(2)}) collective-permute-start(bf16[2,4,128,128]{3,2,1,0:T(8,128)(2,1)S(1)} %get-tuple-element.96), channel_id=1, source_target_pairs={{0,15},{1,0},{2,1},{3,2},{4,3},{5,4},{6,5},{7,6},{8,7},{9,8},{10,9... | collective-permute-start | bytes 786440 | tf_op jit(solution)/shard_map/ppermute | solution.py:19
  22.9 1.3 %collective-permute-start.9 = (bf16[4,64,128]{2,1,0:T(8,128)(2,1)S(1)}, bf16[4,64,128]{2,1,0:T(8,128)(2,1)S(1)}, u32[]{:S(2)}, u32[]{:S(2)}) collective-permute-start(bf16[4,64,128]{2,1,0:T(8,128)(2,1)S(1)} %get-tuple-element.85), channel_id=1, source_target_pairs={{0,16},{16,0},{1,17},{17,1},{2,18},{18,2},{3,19},{19,3},{4,20},{20... | collective-permute-start | bytes 196616 | tf_op jit(solution)/shard_map/ppermute | solution.py:24
  23.0 1.4 %collective-permute-start.10 = (bf16[4,64,128]{2,1,0:T(8,128)(2,1)S(1)}, bf16[4,64,128]{2,1,0:T(8,128)(2,1)S(1)}, u32[]{:S(2)}, u32[]{:S(2)}) collective-permute-start(bf16[4,64,128]{2,1,0:T(8,128)(2,1)S(1)} %get-tuple-element.86), channel_id=1, source_target_pairs={{0,16},{16,0},{1,17},{17,1},{2,18},{18,2},{3,19},{19,3},{4,20},{20... | collective-permute-start | bytes 196616 | tf_op jit(solution)/shard_map/ppermute | solution.py:24
  24.4 9.2 %collective-permute-start.16 = (bf16[2,8,64,128]{3,2,1,0:T(8,128)(2,1)S(1)}, bf16[2,8,64,128]{3,2,1,0:T(8,128)(2,1)S(1)}, u32[]{:S(2)}, u32[]{:S(2)}) collective-permute-start(bf16[2,8,64,128]{3,2,1,0:T(8,128)(2,1)S(1)} %join_two.1.after), channel_id=1, source_target_pairs={{0,14},{1,15},{2,0},{3,1},{4,2},{5,3},{6,4},{7,5},{8,6},{9,7},{10,... | collective-permute-start | bytes 786440 | tf_op jit(solution)/shard_map/ppermute | solution.py:19
  29.0 2.0 %collective-permute-start.12 = (bf16[11,64,128]{2,1,0:T(8,128)(2,1)S(1)}, bf16[11,64,128]{2,1,0:T(8,128)(2,1)S(1)}, u32[]{:S(2)}, u32[]{:S(2)}) collective-permute-start(bf16[11,64,128]{2,1,0:T(8,128)(2,1)S(1)} %get-tuple-element.91), channel_id=1, source_target_pairs={{0,16},{16,0},{1,17},{17,1},{2,18},{18,2},{3,19},{19,3},{4,20},{20... | collective-permute-start | bytes 540680 | tf_op jit(solution)/shard_map/ppermute | solution.py:24
  29.0 1.9 %collective-permute-start.13 = (bf16[11,64,128]{2,1,0:T(8,128)(2,1)S(1)}, bf16[11,64,128]{2,1,0:T(8,128)(2,1)S(1)}, u32[]{:S(2)}, u32[]{:S(2)}) collective-permute-start(bf16[11,64,128]{2,1,0:T(8,128)(2,1)S(1)} %get-tuple-element.92), channel_id=1, source_target_pairs={{0,16},{16,0},{1,17},{17,1},{2,18},{18,2},{3,19},{19,3},{4,20},{20... | collective-permute-start | bytes 540680 | tf_op jit(solution)/shard_map/ppermute | solution.py:24
  29.5 1.4 %collective-permute-start.11 = (bf16[10,64,128]{2,1,0:T(8,128)(2,1)S(1)}, bf16[10,64,128]{2,1,0:T(8,128)(2,1)S(1)}, u32[]{:S(2)}, u32[]{:S(2)}) collective-permute-start(bf16[10,64,128]{2,1,0:T(8,128)(2,1)S(1)} %get-tuple-element.90), channel_id=1, source_target_pairs={{0,16},{16,0},{1,17},{17,1},{2,18},{18,2},{3,19},{19,3},{4,20},{20... | collective-permute-start | bytes 491528 | tf_op jit(solution)/shard_map/ppermute | solution.py:24
  29.7 3.9 %collective-permute-start.15 = (bf16[2,4,64,128]{3,2,1,0:T(8,128)(2,1)S(1)}, bf16[2,4,64,128]{3,2,1,0:T(8,128)(2,1)S(1)}, u32[]{:S(2)}, u32[]{:S(2)}) collective-permute-start(bf16[2,4,64,128]{3,2,1,0:T(8,128)(2,1)S(1)} %get-tuple-element.98), channel_id=1, source_target_pairs={{0,16},{16,0},{1,17},{17,1},{2,18},{18,2},{3,19},{19,3},{4,20},{20... | collective-permute-start | bytes 393224 | tf_op jit(solution)/shard_map/ppermute | solution.py:24

commit v17 on v16

--- a/solution.py
+++ b/solution.py
@@ -1,3 +1,4 @@
+import functools
 import math
 
 import jax
@@ -110,43 +111,45 @@
         taken += count
 
 
-def split_rows_kernel(queries, grads, after, *sends):
-    heads = queries.shape[0] // 2
-    start = (1 - lax.axis_index("head")) * heads
-    for index, row, piece, count in placed(sends, heads):
-        piece[...] = (queries, grads)[index][pl.ds(start + row, count)]
-
-
-def join_own_kernel(own, other_keys, other_values, own_head):
+def join_own_kernel(own, other_keys, other_values, *halves):
     groups, length = other_keys.shape[:2]
-    own_head[:, :, pl.ds(0, length)] = own[:, my_heads(groups)]
-    own_head[0, :, pl.ds(length, length)] = other_keys[...]
-    own_head[1, :, pl.ds(length, length)] = other_values[...]
+    part = halves[0].shape[1]
+    start = lax.axis_index("head") * groups
+    for place, target in enumerate(halves):
+        target[:, :, pl.ds(0, length)] = own[:, pl.ds(start + place * part, part)]
+        for index, other in enumerate((other_keys, other_values)):
+            target[index, :, pl.ds(length, length)] = other[pl.ds(place * part, part)]
 
 
 def own_kernel(
-    spans, offset, queries, grads, first_third, second_third, last_third, own,
+    spans, offset, queries, grads, queries_other, grads_other, first_half, second_half,
     query_head, grad_head, grad_rows, first, own_max, own_total, own_out, own_weights,
     own_prob_grad,
 ):
     heads, _, width = query_head.shape
     length = queries.shape[1]
-    groups = own.shape[1]
+    part = first_half.shape[1]
+    groups = 2 * part
     chunks = first.shape[0]
     count = heads // chunks
-    query_head[:, pl.ds(0, length)] = queries[my_heads(heads)]
-    grad_head[:, pl.ds(0, length)] = grads[my_heads(heads)]
-    for index, row, piece, rows in placed((first_third, second_third, last_third), heads):
-        (query_head, grad_head)[index][pl.ds(row, rows), pl.ds(length, length)] = piece[...]
+    mine = my_heads(heads)
+    query_head[:, pl.ds(0, length)] = queries[mine]
+    query_head[:, pl.ds(length, length)] = queries_other[mine]
+    grad_head[:, pl.ds(0, length)] = grads[mine]
+    grad_head[:, pl.ds(length, length)] = grads_other[mine]
+
+    def block(index, n):
+        g = n * groups // chunks
+        return (first_half, second_half)[g // part][index, g % part]
+
     factor = width ** (-0.5) * math.log2(math.e)
     token = lane_tokens(count, length)
     for n, rows in enumerate(first_visible(spans, offset, chunks, count, length)):
         first[n] = rows
 
     def products(n):
-        g = n * groups // chunks
-        own_prob_grad[n] = matmul(own[1, g], grouped(grad_head, n, count), (1, 1))
-        return (matmul(own[0, g], grouped(query_head, n, count), (1, 1)),)
+        own_prob_grad[n] = matmul(block(1, n), grouped(grad_head, n, count), (1, 1))
+        return (matmul(block(0, n), grouped(query_head, n, count), (1, 1)),)
 
     def softmax(n, scores):
         scores = masked(scores * factor, first[n], 0, token)
@@ -158,7 +161,7 @@
         return (weights.astype(jnp.bfloat16),)
 
     def weigh(n, halves):
-        own_out[n] = matmul(own[1, n * groups // chunks], halves, (0, 0))
+        own_out[n] = matmul(block(1, n), halves, (0, 0))
         grad_rows[n] = grouped(grad_head, n, count).T
 
     pipelined(chunks, products, softmax, weigh)
@@ -206,27 +209,27 @@
 
 
 def last_kernel(
-    first, query_head, grad_head, back_one, grad_rows, near_max, near_total, near_out,
+    base, first, query_head, grad_head, back_one, grad_rows, near_max, near_total, near_out, after,
     attended_rows, row_delta, near_factor, one_grad, one_part,
 ):
     groups = back_one.shape[1]
-    chunks = first.shape[0]
+    chunks = row_delta.shape[0]
     heads, _, width = query_head.shape
-    count = heads // chunks
+    count = heads // first.shape[0]
     scale = width ** (-0.5)
 
     def products(n):
         g = n * groups // chunks
-        scores = matmul(back_one[0, g], grouped(query_head, n, count), (1, 1))
-        prob_grad = matmul(back_one[1, g], grouped(grad_head, n, count), (1, 1))
+        scores = matmul(back_one[0, g], grouped(query_head, base + n, count), (1, 1))
+        prob_grad = matmul(back_one[1, g], grouped(grad_head, base + n, count), (1, 1))
         return scores, prob_grad
 
     def softmax(n, scores, prob_grad):
-        scores = masked(scores * (scale * math.log2(math.e)), first[n], 1)
-        row_max = jnp.maximum(near_max[n], jnp.max(scores, axis=0, keepdims=True))
+        scores = masked(scores * (scale * math.log2(math.e)), first[base + n], 1)
+        row_max = jnp.maximum(near_max[base + n], jnp.max(scores, axis=0, keepdims=True))
         weights = jnp.exp2(scores - row_max)
-        rescale = jnp.exp2(near_max[n] - row_max)
-        inverse = 1.0 / (near_total[n] * rescale + jnp.sum(weights, axis=0, keepdims=True))
+        rescale = jnp.exp2(near_max[base + n] - row_max)
+        inverse = 1.0 / (near_total[base + n] * rescale + jnp.sum(weights, axis=0, keepdims=True))
         weighted = matmul(
             back_one[1, n * groups // chunks], weights.astype(jnp.bfloat16), (0, 0)
         )
@@ -234,9 +237,9 @@
         return prob_grad, weights, weighted, rescale, inverse
 
     def differentiate(n, prob_grad, weights, weighted, rescale, inverse):
-        attended = ((near_out[n] * rescale + weighted) * inverse).astype(jnp.bfloat16)
+        attended = ((near_out[base + n] * rescale + weighted) * inverse).astype(jnp.bfloat16)
         delta = jnp.sum(
-            grad_rows[n].astype(jnp.float32) * attended.astype(jnp.float32), axis=0, keepdims=True
+            grad_rows[base + n].astype(jnp.float32) * attended.astype(jnp.float32), axis=0, keepdims=True
         )
         prob = weights * inverse
         score_grad = (prob * (prob_grad - delta)).astype(jnp.bfloat16)
@@ -249,7 +252,7 @@
         one_part[0, g] = (key_part * scale).astype(jnp.bfloat16)
         one_part[1, g] = value_part.astype(jnp.bfloat16)
 
-    accumulate = accumulator(query_head, grad_head, chunks, groups, store)
+    accumulate = accumulator(query_head, grad_head, base, count, chunks, groups, store)
     pipelined(chunks, products, softmax, differentiate, accumulate)
 
 
@@ -262,14 +265,13 @@
                 ready[depth + 1][n] = stage(n, *ready[depth].pop(n, ())) or ()
 
 
-def accumulator(query_head, grad_head, chunks, groups, store):
-    count = query_head.shape[0] // chunks
+def accumulator(query_head, grad_head, base, count, chunks, groups, store):
     parts = {}
 
     def accumulate(n, score_grad, half):
         g = n * groups // chunks
-        key_part = matmul(score_grad, grouped(query_head, n, count), (1, 0))
-        value_part = matmul(half, grouped(grad_head, n, count), (1, 0))
+        key_part = matmul(score_grad, grouped(query_head, base + n, count), (1, 0))
+        value_part = matmul(half, grouped(grad_head, base + n, count), (1, 0))
         if g in parts:
             key_part, value_part = parts[g][0] + key_part, parts[g][1] + value_part
         parts[g] = (key_part, value_part)
@@ -279,16 +281,22 @@
     return accumulate
 
 
+def of_half(n, first, second):
+    each = first.shape[0]
+    return first[n] if n < each else second[n - each]
+
+
 def two_backward_kernel(
-    query_head, grad_head, near_weights, near_prob_grad, near_factor, row_delta,
+    query_head, grad_head, near_weights, near_prob_grad, factor_a, delta_a, factor_b, delta_b,
     two_grad, two_mine, send_keys, send_values,
 ):
     chunks = near_weights.shape[0]
     groups, length, width = two_mine.shape[1:]
 
     def differentiate(n):
-        prob = near_weights[n] * near_factor[n]
-        score_grad = (prob * (near_prob_grad[n] - row_delta[n])).astype(jnp.bfloat16)
+        prob = near_weights[n] * of_half(n, factor_a, factor_b)
+        score_grad = prob * (near_prob_grad[n] - of_half(n, delta_a, delta_b))
+        score_grad = score_grad.astype(jnp.bfloat16)
         two_grad[n] = score_grad
         return score_grad, prob.astype(jnp.bfloat16)
 
@@ -299,20 +307,21 @@
             two_mine[index, g] = part[:length].astype(jnp.bfloat16)
             send[g] = part[length:].astype(jnp.bfloat16)
 
-    accumulate = accumulator(query_head, grad_head, chunks, groups, store)
+    accumulate = accumulator(query_head, grad_head, 0, query_head.shape[0] // chunks, chunks, groups, store)
     pipelined(chunks, differentiate, accumulate)
 
 
 def own_backward_kernel(
-    query_head, grad_head, own_weights, own_prob_grad, near_factor, own_factor, row_delta,
-    after, own_grad, own_part,
+    query_head, grad_head, own_weights, own_prob_grad, own_factor, factor_a, delta_a, factor_b,
+    delta_b, after, own_grad, own_part,
 ):
     chunks = own_weights.shape[0]
     groups, _, width = own_part.shape[1:]
 
     def differentiate(n):
-        prob = own_weights[n] * (own_factor[n] * near_factor[n])
-        score_grad = (prob * (own_prob_grad[n] - row_delta[n])).astype(jnp.bfloat16)
+        prob = own_weights[n] * (own_factor[n] * of_half(n, factor_a, factor_b))
+        score_grad = prob * (own_prob_grad[n] - of_half(n, delta_a, delta_b))
+        score_grad = score_grad.astype(jnp.bfloat16)
         own_grad[n] = score_grad
         return score_grad, prob.astype(jnp.bfloat16)
 
@@ -320,7 +329,7 @@
         own_part[0, g] = key_part * width ** (-0.5)
         own_part[1, g] = value_part
 
-    accumulate = accumulator(query_head, grad_head, chunks, groups, store)
+    accumulate = accumulator(query_head, grad_head, 0, query_head.shape[0] // chunks, chunks, groups, store)
     pipelined(chunks, differentiate, accumulate)
 
 
@@ -332,25 +341,26 @@
 
 
 def query_kernel(
-    own, back_one, back_two, two_keys, attended_rows, two_grad, one_grad, own_grad,
-    out_mine, query_mine, first_third, second_third, last_third, query_send,
-):
-    sends = (first_third, second_third, last_third)
-    groups = own.shape[1]
-    chunks = own_grad.shape[0]
+    own_a, own_b, one_a, one_b, rows_a, rows_b, grad_a, grad_b, back_two, two_keys, two_grad,
+    own_grad, after, out_mine, query_mine, first_third, second_third, last_third, query_send,
+):
+    part, chunks = own_a.shape[1], own_grad.shape[0]
     heads, length, width = out_mine.shape
     count = heads // chunks
     for n in range(chunks):
-        g = n * groups // chunks
+        g = n * 2 * part // chunks
+        own, one = ((own_a, one_a), (own_b, one_b))[g // part]
         rows = pl.ds(n * count, count)
-        keys = join(two_back(back_two, (two_keys,), 0, g), back_one[0, g], own[0, g])
-        part = matmul(keys, join(two_grad[n], one_grad[n], own_grad[n]), (0, 0))
-        part = (part * width ** (-0.5)).astype(jnp.bfloat16)
-        for index, (columns, mine) in enumerate(((attended_rows[n], out_mine), (part, query_mine))):
+        keys = join(two_back(back_two, (two_keys,), 0, g), one[0, g % part], own[0, g % part])
+        total = matmul(keys, join(two_grad[n], of_half(n, grad_a, grad_b), own_grad[n]), (0, 0))
+        total = (total * width ** (-0.5)).astype(jnp.bfloat16)
+        for index, (columns, mine) in enumerate(
+            ((of_half(n, rows_a, rows_b), out_mine), (total, query_mine))
+        ):
             block = columns.T.reshape(count, 2 * length, width)
             mine[rows] = block[:, :length]
             query_send[index, rows] = block[:, length:]
-    for index, row, piece, taken in placed(sends, heads):
+    for index, row, piece, taken in placed((first_third, second_third, last_third), heads):
         piece[...] = query_send[index, pl.ds(row, taken)]
 
 
@@ -366,11 +376,18 @@
     token[...] = jnp.zeros(token.shape, token.dtype)
 
 
-def own_sum_kernel(own_part, one_total, sum_mine, sum_send):
-    length = sum_mine.shape[2]
-    total = own_part[...] + one_total[...].astype(jnp.float32)
-    sum_mine[...] = total[:, :, :length]
-    sum_send[...] = total[:, :, length:].astype(jnp.bfloat16)
+def first_sum_kernel(own_part, one_total, total, token):
+    total[...] = own_part[:, pl.ds(0, one_total.shape[1])] + one_total[...].astype(jnp.float32)
+    token[...] = jnp.zeros(token.shape, token.dtype)
+
+
+def own_sum_kernel(own_part, first_sum, one_total, sum_mine, sum_send):
+    length, part = sum_mine.shape[2], first_sum.shape[1]
+    second = own_part[:, pl.ds(part, part)] + one_total[...].astype(jnp.float32)
+    for index, total in enumerate((first_sum[...], second)):
+        groups = pl.ds(index * part, part)
+        sum_mine[:, groups] = total[:, :, :length]
+        sum_send[:, groups] = total[:, :, length:].astype(jnp.bfloat16)
 
 
 def final_kernel(sum_mine, sum_other, two_total, after, key_grad, value_grad):
@@ -396,7 +413,7 @@
     vmem = pl.BlockSpec(memory_space=pltpu.VMEM)
     smem = pl.BlockSpec(memory_space=pltpu.SMEM)
 
-    def call(kernel, name, outs, arrays, scalars=0, scratch=()):
+    def call(kernel, name, outs, arrays, scalars=0, scratch=(), flops=1):
         return pl.pallas_call(
             kernel,
             out_shape=tuple(jax.ShapeDtypeStruct(shape, kind) for shape, kind in outs),
@@ -404,7 +421,7 @@
             out_specs=(vmem,) * len(outs),
             scratch_shapes=scratch,
             compiler_params=pltpu.CompilerParams(vmem_limit_bytes=40 * 1024 * 1024),
-            cost_estimate=pl.CostEstimate(flops=1, bytes_accessed=0, transcendentals=0),
+            cost_estimate=pl.CostEstimate(flops=flops, bytes_accessed=0, transcendentals=0),
             name=name,
         )(*arrays)
 
@@ -417,22 +434,25 @@
     half_pair = ((2, groups_here, length, width), half)
     chip_pair = ((2, groups_here, tokens, width), half)
     half_rows = ((heads_here, length, width), half)
-    third_rows = [((rows, length, width), half) for rows in thirds(heads_here)]
+    part, each = groups_here // 2, chunks // 2
+    chip_half = ((2, part, tokens, width), half)
+    half_stat = ((each, 1, lanes), full)
     chip_rows = ((heads_here, tokens, width), half)
 
+    queries_other = swapped(query_matrix, "head")
+    grads_other = swapped(output_gradient, "head")
     own = jnp.stack([key_matrix, value_matrix])
     back_two = shifted(own, "seq", 2)
     own_sends = call(split_kernel, "split_own", [half_block] * 2, (own,))
-    (own_head,) = call(
-        join_own_kernel, "join_own", [chip_pair], (own, *[swapped(send, "head") for send in own_sends])
-    )
-    back_one = shifted(own_head, "seq", 1, ring=False)
-    sends = call(
-        split_rows_kernel,
-        "split_rows",
-        third_rows,
-        (query_matrix, output_gradient, own),
-    )
+    own_halves = call(
+        join_own_kernel,
+        "join_own",
+        [chip_half] * 2,
+        (own, *[swapped(send, "head") for send in own_sends]),
+    )
+    back_one = [
+        shifted(block, "seq", 1, ring=index == 0) for index, block in enumerate(own_halves)
+    ]
     (
         query_head, grad_head, grad_rows, first, own_max, own_total, own_out, own_weights,
         own_prob_grad,
@@ -445,7 +465,7 @@
         ],
         (
             query_head_spans, slab_offset, query_matrix, output_gradient,
-            *[swapped(send, "head") for send in sends], own_head,
+            queries_other, grads_other, *own_halves,
         ),
         scalars=2,
     )
@@ -458,19 +478,30 @@
         [stat, stat, rows_of(width, full), rows_of(tokens, full), rows_of(tokens, full), stat],
         (first, query_head, grad_head, back_two, *two_other, own_max, own_total, own_out),
     )
-    back_one, near_max = lax.optimization_barrier((back_one, near_max))
-    attended_rows, row_delta, near_factor, one_grad, one_part = call(
-        last_kernel,
-        "last_forward_backward",
-        [rows_of(width, half), stat, stat, rows_of(tokens, half), chip_pair],
-        (first, query_head, grad_head, back_one, grad_rows, near_max, near_total, near_out),
-    )
-    one_total = shifted(one_part, "seq", -1)
+    after = near_max
+    halves = []
+    for index in range(2):
+        back_one[index], after = lax.optimization_barrier((back_one[index], after))
+        rows, delta, factor, one_grad, one_part = call(
+            functools.partial(last_kernel, index * each),
+            "last_" + "ab"[index],
+            [
+                ((each, width, lanes), half), half_stat, half_stat, ((each, tokens, lanes), half),
+                chip_half,
+            ],
+            (
+                first, query_head, grad_head, back_one[index], grad_rows, near_max, near_total,
+                near_out, after,
+            ),
+        )
+        halves.append((factor, delta, rows, one_grad, shifted(one_part, "seq", -1)))
+        after = delta
+    stats = (*halves[0][:2], *halves[1][:2])
     two_grad, part_mine, *part_sends = call(
         two_backward_kernel,
         "two_backward",
         [rows_of(tokens, half), half_pair, half_block, half_block],
-        (query_head, grad_head, near_weights, near_prob_grad, near_factor, row_delta),
+        (query_head, grad_head, near_weights, near_prob_grad, *stats),
     )
     (two_part,) = call(
         join_two_kernel,
@@ -484,15 +515,24 @@
         "own_backward",
         [rows_of(tokens, half), (chip_pair[0], full)],
         (
-            query_head, grad_head, own_weights, own_prob_grad, near_factor, own_factor, row_delta,
-            two_part,
+            query_head, grad_head, own_weights, own_prob_grad, own_factor, *stats, two_part,
         ),
+    )
+    first_sum, sum_token = call(
+        first_sum_kernel,
+        "sum_a",
+        [(chip_half[0], full), ((8, 128), full)],
+        (own_part, halves[0][4]),
+        flops=5 * 10**8,
     )
     out_mine, query_mine, *sends = call(
         query_kernel,
         "query_grad",
-        [half_rows] * 2 + third_rows,
-        (own_head, back_one, back_two, two_other[0], attended_rows, two_grad, one_grad, own_grad),
+        [half_rows] * 2 + [((rows, length, width), half) for rows in thirds(heads_here)],
+        (
+            *own_halves, *back_one, halves[0][2], halves[1][2], halves[0][3], halves[1][3],
+            back_two, two_other[0], two_grad, own_grad, sum_token,
+        ),
         scratch=[pltpu.VMEM((2,) + half_rows[0], half)],
     )
     attn_out, query_grad, token = call(
@@ -502,7 +542,10 @@
         (out_mine, query_mine, *[swapped(send, "head") for send in sends]),
     )
     sum_mine, sum_send = call(
-        own_sum_kernel, "own_sum", [(half_pair[0], full), half_pair], (own_part, one_total)
+        own_sum_kernel,
+        "sum_b",
+        [(half_pair[0], full), half_pair],
+        (own_part, first_sum, halves[1][4]),
     )
     key_grad, value_grad = call(
         final_kernel,

time: 34.6 us -> 38.7 us (1.12)
  waiting for transfers between devices: 6.59 us -> 9.82 us
  starting transfers between devices: 17.6 us -> 18.2 us
    ppermute x4 -> x6, waiting for transfers between devices: 2.45 us -> 7.74 us  [shifted(): return lax.ppermute(block, axis, route)]
    ppermute x13 -> x12, waiting for transfers between devices: 4.14 us -> 2.08 us  [swapped(): return lax.ppermute(block, axis, [(i, count - 1 - i) for i in range(count)])]
    ppermute x4 -> x6, starting transfers between devices: 14.1 us -> 15.2 us  [shifted(): return lax.ppermute(block, axis, route)]
    ppermute x13 -> x12, starting transfers between devices: 3.5 us -> 3.02 us  [swapped(): return lax.ppermute(block, axis, [(i, count - 1 - i) for i in range(count)])]
    pallas_call x14 -> x15, Pallas kernels: 7.69 us -> 7.94 us  [call(): pl.pallas_call(kernel, out_shape=tuple((jax.ShapeDtypeStruct(shape, kind)...]
  transfers between devices with their start and end apart: 17 -> 18, of which waited for: 10 -> 8; matrix products, arithmetic and copies ran while one was open for 0% -> 3% of each run, Pallas kernels for 16% -> 19%
where the time goes in v17:
time: 38.7 us; the launch traced here: 38.5 us
  starting transfers between devices  18.2 us (47%)
  waiting for transfers between devices  9.82 us (25%)
  Pallas kernels  7.94 us (21%)
  between operations  1.48 us (4%)
  other arithmetic  1.08 us (3%)
    ppermute x6, starting transfers between devices, shifted(): return lax.ppermute(block, axis, route)  15.2 us
    pallas_call x15, Pallas kernels, call(): pl.pallas_call(kernel, out_shape=tuple((jax.ShapeDtypeStruct(shape, kind)...  7.94 us
    ppermute x6, waiting for transfers between devices, shifted(): return lax.ppermute(block, axis, route)  7.74 us
    ppermute x12, starting transfers between devices, swapped(): return lax.ppermute(block, axis, [(i, count - 1 - i) for i in range(count)])  3.02 us
    ppermute x12, waiting for transfers between devices, swapped(): return lax.ppermute(block, axis, [(i, count - 1 - i) for i in range(count)])  2.08 us
    another operation x1, other arithmetic, shards(): own = jnp.stack([key_matrix, value_matrix])  1.08 us
  transfers between devices with their start and end apart: 18, of which 8 were waited for; matrix products, arithmetic and copies ran while one was open for 3% of the time, Pallas kernels for 19%

profile of v17, /device:TPU:0, one launch (start us, length us, event | category | flops | bytes accessed | tf_op | source)
XLA Modules:
  0.0 38.5 jit_solution(9545767021681255024)
XLA Ops:
  0.6 0.5 %collective-permute-start.4 = (bf16[32,64,128]{2,1,0:T(8,128)(2,1)}, bf16[32,64,128]{2,1,0:T(8,128)(2,1)S(1)}, u32[]{:S(2)}, u32[]{:S(2)}) collective-permute-start(bf16[32,64,128]{2,1,0:T(8,128)(2,1)} %queries.1), channel_id=1, source_target_pairs={{0,16},{16,0},{1,17},{17,1},{2,18},{18,2},{3,19},{19,3},{4,20},{20... | collective-permute-start | bytes 1572872 | tf_op jit(solution)/shard_map/ppermute | solution.py:25
  1.2 1.1 %pad_maximum_fusion.block.own = bf16[2,8,64,128]{3,2,1,0:T(8,128)(2,1)S(1)} fusion(bf16[1,8,64,128]{3,2,1,0:T(8,128)(2,1)} %bitcast.2, bf16[1,8,64,128]{3,2,1,0:T(8,128)(2,1)} %bitcast.3), kind=kLoop, calls=%fused_computation | loop fusion | flops 131072 | bytes 524288 | tf_op jit(solution)/shard_map/stack | solution.py:444
  2.3 3.0 %collective-permute-start.3 = (bf16[2,8,64,128]{3,2,1,0:T(8,128)(2,1)S(1)}, bf16[2,8,64,128]{3,2,1,0:T(8,128)(2,1)S(1)}, u32[]{:S(2)}, u32[]{:S(2)}) collective-permute-start(bf16[2,8,64,128]{3,2,1,0:T(8,128)(2,1)S(1)} %pad_maximum_fusion.block.own), channel_id=1, source_target_pairs={{0,2},{1,3},{2,4},{3,5},{4,6},{5,7},{6,8},{7,9},{8,10},{9,11},{10,... | collective-permute-start | bytes 786440 | tf_op jit(solution)/shard_map/ppermute | solution.py:20
  5.4 0.5 %collective-permute-start.1 = (bf16[4,64,128]{2,1,0:T(8,128)(2,1)S(1)}, bf16[4,64,128]{2,1,0:T(8,128)(2,1)S(1)}, u32[]{:S(2)}, u32[]{:S(2)}) collective-permute-start(bf16[4,64,128]{2,1,0:T(8,128)(2,1)S(1)} %get-tuple-element.62), channel_id=1, source_target_pairs={{0,16},{16,0},{1,17},{17,1},{2,18},{18,2},{3,19},{19,3},{4,20},{20... | collective-permute-start | bytes 196616 | tf_op jit(solution)/shard_map/ppermute | solution.py:25
  5.9 0.7 %collective-permute-done.other_keys = bf16[4,64,128]{2,1,0:T(8,128)(2,1)S(1)} collective-permute-done((bf16[4,64,128]{2,1,0:T(8,128)(2,1)S(1)}, bf16[4,64,128]{2,1,0:T(8,128)(2,1)S(1)}, u32[]{:S(2)}, u32[]{:S(2)}) %collective-permute-start) | collective-permute-done | bytes 65568 | tf_op jit(solution)/shard_map/ppermute | solution.py:25
  6.8 1.5 %collective-permute-start.2 = (bf16[2,2,128,128]{3,2,1,0:T(8,128)(2,1)S(1)}, bf16[2,2,128,128]{3,2,1,0:T(8,128)(2,1)S(1)}, u32[]{:S(2)}, u32[]{:S(2)}) collective-permute-start(bf16[2,2,128,128]{3,2,1,0:T(8,128)(2,1)S(1)} %get-tuple-element.63.first_half.own_a), channel_id=1, source_target_pairs={{0,1},{1,2},{2,3},{3,4},{4,5},{5,6},{6,7},{7,8},{8,9},{9,10},{10,1... | collective-permute-start | bytes 393224 | tf_op jit(solution)/shard_map/ppermute | solution.py:20
  8.4 3.5 %collective-permute-start.8 = (bf16[2,2,128,128]{3,2,1,0:T(8,128)(2,1)S(1)}, bf16[2,2,128,128]{3,2,1,0:T(8,128)(2,1)S(1)}, u32[]{:S(2)}, u32[]{:S(2)}) collective-permute-start(bf16[2,2,128,128]{3,2,1,0:T(8,128)(2,1)S(1)} %get-tuple-element.64.second_half.own_b), channel_id=1, source_target_pairs={{0,1},{1,2},{2,3},{3,4},{4,5},{5,6},{6,7},{7,8},{8,9},{9,10},{10,1... | collective-permute-start | bytes 393224 | tf_op jit(solution)/shard_map/ppermute | solution.py:20
  12.6 1.5 %own_block.1 = (bf16[16,128,128]{2,1,0:T(8,128)(2,1)S(1)}, bf16[16,128,128]{2,1,0:T(8,128)(2,1)S(1)}, bf16[8,128,256]{2,1,0:T(8,128)(2,1)S(1)}, s32[8,1,256]{2,1...) custom-call(s32[32]{0:T(128)S(1)} %copy-done.2, ...), custom_call_target="tpu_custom_call" | custom-call | flops 1 | tf_op jit(solution)/shard_map/own_block/pallas_call | solution.py:417
  14.1 2.6 %collective-permute-done.3.block.back_two = bf16[2,8,64,128]{3,2,1,0:T(8,128)(2,1)S(1)} collective-permute-done((bf16[2,8,64,128]{3,2,1,0:T(8,128)(2,1)S(1)}, bf16[2,8,64,128]{3,2,1,0:T(8,128)(2,1)S(1)}, u32[]{:S(2)}, u32[]{:S(2)}) %collective-permute-start.3) | collective-permute-done | bytes 262176 | tf_op jit(solution)/shard_map/ppermute | solution.py:20
  16.8 0.5 %collective-permute-start.7 = (bf16[4,64,128]{2,1,0:T(8,128)(2,1)S(1)}, bf16[4,64,128]{2,1,0:T(8,128)(2,1)S(1)}, u32[]{:S(2)}, u32[]{:S(2)}) collective-permute-start(bf16[4,64,128]{2,1,0:T(8,128)(2,1)S(1)} %get-tuple-element.71), channel_id=1, source_target_pairs={{0,16},{16,0},{1,17},{17,1},{2,18},{18,2},{3,19},{19,3},{4,20},{20... | collective-permute-start | bytes 196616 | tf_op jit(solution)/shard_map/ppermute | solution.py:25
  17.3 0.7 %collective-permute-done.6.two_keys = bf16[4,64,128]{2,1,0:T(8,128)(2,1)S(1)} collective-permute-done((bf16[4,64,128]{2,1,0:T(8,128)(2,1)S(1)}, bf16[4,64,128]{2,1,0:T(8,128)(2,1)S(1)}, u32[]{:S(2)}, u32[]{:S(2)}) %collective-permute-start.6) | collective-permute-done | bytes 65568 | tf_op jit(solution)/shard_map/ppermute | solution.py:25
  18.2 0.9 %near_forward.1 = (f32[8,1,256]{2,1,0:T(1,128)S(1)}, f32[8,1,256]{2,1,0:T(1,128)S(1)}, f32[8,128,256]{2,1,0:T(8,128)S(1)}, f32[8,128,256]{2,1,0:T(8,128)S(1)}, f...) custom-call(s32[8,1,256]{2,1,0:T(1,128)S(1)} %get-tuple-element.66.first, ...), custom_call_target="tpu_custom_call" | custom-call | flops 1 | tf_op jit(solution)/shard_map/near_forward/pallas_call | solution.py:417
  19.2 0.9 %last_a.1 = (bf16[4,128,256]{2,1,0:T(8,128)(2,1)S(1)}, f32[4,1,256]{2,1,0:T(1,128)S(1)}, f32[4,1,256]{2,1,0:T(1,128)S(1)}, bf16[4,128,256]{2,1,0:T(8,128)(2,1)S(1)}, bf16[2,2,128,128]{3,2,1,0:T(8,128)(2,1)S(1)}) custom-call(s32[8,1,256]{2,1,0:T(1,128)S(1)} %get-tuple-element.66.first, bf16[16,128,128]{2,1,0:T(8,128)(2,1)S(1)} %get-tuple-element.67.query_head, ...), custom_call_target="tpu_custom_call" | custom-call | flops 1 | tf_op jit(solution)/shard_map/last_a/pallas_call | solution.py:417
  20.1 0.9 %collective-permute-start.11 = (bf16[2,2,128,128]{3,2,1,0:T(8,128)(2,1)S(1)}, bf16[2,2,128,128]{3,2,1,0:T(8,128)(2,1)S(1)}, u32[]{:S(2)}, u32[]{:S(2)}) collective-permute-start(bf16[2,2,128,128]{3,2,1,0:T(8,128)(2,1)S(1)} %get-tuple-element.102), channel_id=1, source_target_pairs={{0,15},{1,0},{2,1},{3,2},{4,3},{5,4},{6,5},{7,6},{8,7},{9,8},{10,9... | collective-permute-start | bytes 393224 | tf_op jit(solution)/shard_map/ppermute | solution.py:20
  21.0 0.9 %last_b.1 = (bf16[4,128,256]{2,1,0:T(8,128)(2,1)S(1)}, f32[4,1,256]{2,1,0:T(1,128)S(1)}, f32[4,1,256]{2,1,0:T(1,128)S(1)}, bf16[4,128,256]{2,1,0:T(8,128)(2,1)S(1)}, bf16[2,2,128,128]{3,2,1,0:T(8,128)(2,1)S(1)}) custom-call(s32[8,1,256]{2,1,0:T(1,128)S(1)} %get-tuple-element.66.first, bf16[16,128,128]{2,1,0:T(8,128)(2,1)S(1)} %get-tuple-element.67.query_head, ...), custom_call_target="tpu_custom_call" | custom-call | flops 1 | tf_op jit(solution)/shard_map/last_b/pallas_call | solution.py:417
  21.9 0.5 %two_backward.1 = (bf16[8,128,256]{2,1,0:T(8,128)(2,1)S(1)}, bf16[2,4,64,128]{3,2,1,0:T(8,128)(2,1)S(1)}, bf16[4,64,128]{2,1,0:T(8,128)(2,1)S(1)}, bf16[4,64,128]{2,1,0:T(8,128)(2,1)S(1)}) custom-call(bf16[16,128,128]{2,1,0:T(8,128)(2,1)S(1)} %get-tuple-element.67.query_head, bf16[16,128,128]{2,1,0:T(8,128)(2,1)S(1)} %get-tuple-element.68.grad_head, ...), custom_call_target="tpu_custom_call" | custom-call | flops 1 | tf_op jit(solution)/shard_map/two_backward/pallas_call | solution.py:417
  23.0 6.2 %collective-permute-start.15 = (bf16[2,2,128,128]{3,2,1,0:T(8,128)(2,1)S(1)}, bf16[2,2,128,128]{3,2,1,0:T(8,128)(2,1)S(1)}, u32[]{:S(2)}, u32[]{:S(2)}) collective-permute-start(bf16[2,2,128,128]{3,2,1,0:T(8,128)(2,1)S(1)} %get-tuple-element.112), channel_id=1, source_target_pairs={{0,15},{1,0},{2,1},{3,2},{4,3},{5,4},{6,5},{7,6},{8,7},{9,8},{10,9... | collective-permute-start | bytes 393224 | tf_op jit(solution)/shard_map/ppermute | solution.py:20
  29.2 0.5 %own_backward.1 = (bf16[8,128,256]{2,1,0:T(8,128)(2,1)S(1)}, f32[2,4,128,128]{3,2,1,0:T(8,128)S(1)}) custom-call(bf16[16,128,128]{2,1,0:T(8,128)(2,1)S(1)} %get-tuple-element.67.query_head, bf16[16,128,128]{2,1,0:T(8,128)(2,1)S(1)} %get-tuple-element.68.grad_head, f32[8,128,256]{2,1,0:T(8,128)S(1)} %get-tuple-element.94.own_weights, ...), custom_call_target="tpu_custom_call" | custom-call | flops 1 | tf_op jit(solution)/shard_map/own_backward/pallas_call | solution.py:417
  29.8 0.7 %query_grad.1 = (bf16[16,64,128]{2,1,0:T(8,128)(2,1)S(1)}, bf16[16,64,128]{2,1,0:T(8,128)(2,1)S(1)}, bf16[10,64,128]{2,1,0:T(8,128)(2,1)S(1)}, bf16[11,64,128]{2,1,0:T(8,128)(2,1)S(1)}, bf16[11,64,128]{2,1,0:T(8,128)(2,1)S(1)}) custom-call(bf16[2,2,128,128]{3,2,1,0:T(8,128)(2,1)S(1)} %get-tuple-element.63.first_half.own_a, ...), custom_call_target="tpu_custom_call" | custom-call | flops 1 | tf_op jit(solution)/shard_map/query_grad/pallas_call | solution.py:417
  30.6 0.5 %collective-permute-start.14 = (bf16[11,64,128]{2,1,0:T(8,128)(2,1)S(1)}, bf16[11,64,128]{2,1,0:T(8,128)(2,1)S(1)}, u32[]{:S(2)}, u32[]{:S(2)}) collective-permute-start(bf16[11,64,128]{2,1,0:T(8,128)(2,1)S(1)} %get-tuple-element.108), channel_id=1, source_target_pairs={{0,16},{16,0},{1,17},{17,1},{2,18},{18,2},{3,19},{19,3},{4,20},{20... | collective-permute-start | bytes 540680 | tf_op jit(solution)/shard_map/ppermute | solution.py:25
  31.2 1.9 %collective-permute-done.15.one_total = bf16[2,2,128,128]{3,2,1,0:T(8,128)(2,1)S(1)} collective-permute-done((bf16[2,2,128,128]{3,2,1,0:T(8,128)(2,1)S(1)}, bf16[2,2,128,128]{3,2,1,0:T(8,128)(2,1)S(1)}, u32[]{:S(2)}, u32[]{:S(2)}) %collective-permute-start.15) | collective-permute-done | bytes 131104 | tf_op jit(solution)/shard_map/ppermute | solution.py:20
  33.2 1.0 %assemble.1 = (bf16[32,64,128]{2,1,0:T(8,128)(2,1)}, bf16[32,64,128]{2,1,0:T(8,128)(2,1)}, f32[8,128]{1,0:T(8,128)S(1)}) custom-call(bf16[16,64,128]{2,1,0:T(8,128)(2,1)S(1)} %get-tuple-element.104.out_mine, bf16[16,64,128]{2,1,0:T(8,128)(2,1)S(1)} %get-tuple-element.105.query_mine, bf16[10,64,128]{2,1,0:T(8,128)(2,1)S(1)} %collective-permute-done.12.first_third, ...), custom_call_target="tpu_custom_call" | custom-call | flops 1 | tf_op jit(solution)/shard_map/assemble/pallas_call | solution.py:417
  34.5 3.3 %collective-permute-done.17.two_total = bf16[2,8,64,128]{3,2,1,0:T(8,128)(2,1)S(1)} collective-permute-done((bf16[2,8,64,128]{3,2,1,0:T(8,128)(2,1)S(1)}, bf16[2,8,64,128]{3,2,1,0:T(8,128)(2,1)S(1)}, u32[]{:S(2)}, u32[]{:S(2)}) %collective-permute-start.17) | collective-permute-done | bytes 262176 | tf_op jit(solution)/shard_map/ppermute | solution.py:20
  37.8 0.7 %total.1 = (bf16[8,64,128]{2,1,0:T(8,128)(2,1)}, bf16[8,64,128]{2,1,0:T(8,128)(2,1)}) custom-call(f32[2,4,64,128]{3,2,1,0:T(8,128)S(1)} %get-tuple-element.113.sum_mine, bf16[2,4,64,128]{3,2,1,0:T(8,128)(2,1)S(1)} %collective-permute-done.16.sum_other, bf16[2,8,64,128]{3,2,1,0:T(8,128)(2,1)S(1)} %collective-permute-done.17.two_total, ...), custom_call_target="tpu_custom_call" | custom-call | flops 1 | tf_op jit(solution)/shard_map/total/pallas_call | solution.py:417
  (34 shorter events, 1.8 us)
Async XLA Ops:
  0.6 11.9 %collective-permute-start.4 = (bf16[32,64,128]{2,1,0:T(8,128)(2,1)}, bf16[32,64,128]{2,1,0:T(8,128)(2,1)S(1)}, u32[]{:S(2)}, u32[]{:S(2)}) collective-permute-start(bf16[32,64,128]{2,1,0:T(8,128)(2,1)} %queries.1), channel_id=1, source_target_pairs={{0,16},{16,0},{1,17},{17,1},{2,18},{18,2},{3,19},{19,3},{4,20},{20... | collective-permute-start | bytes 1572872 | tf_op jit(solution)/shard_map/ppermute | solution.py:25
  1.1 11.4 %collective-permute-start.5 = (bf16[32,64,128]{2,1,0:T(8,128)(2,1)}, bf16[32,64,128]{2,1,0:T(8,128)(2,1)S(1)}, u32[]{:S(2)}, u32[]{:S(2)}) collective-permute-start(bf16[32,64,128]{2,1,0:T(8,128)(2,1)} %grads.1), channel_id=1, source_target_pairs={{0,16},{16,0},{1,17},{17,1},{2,18},{18,2},{3,19},{19,3},{4,20},{20... | collective-permute-start | bytes 1572872 | tf_op jit(solution)/shard_map/ppermute | solution.py:25
  1.2 11.3 %copy-start = (bf16[32,64,128]{2,1,0:T(8,128)(2,1)S(1)}, bf16[32,64,128]{2,1,0:T(8,128)(2,1)}, u32[]{:S(2)}) copy-start(bf16[32,64,128]{2,1,0:T(8,128)(2,1)} %queries.1) | copy-start | bytes 1572868
  1.2 11.4 %copy-start.1 = (bf16[32,64,128]{2,1,0:T(8,128)(2,1)S(1)}, bf16[32,64,128]{2,1,0:T(8,128)(2,1)}, u32[]{:S(2)}) copy-start(bf16[32,64,128]{2,1,0:T(8,128)(2,1)} %grads.1) | copy-start | bytes 1572868
  2.3 14.4 %collective-permute-start.3 = (bf16[2,8,64,128]{3,2,1,0:T(8,128)(2,1)S(1)}, bf16[2,8,64,128]{3,2,1,0:T(8,128)(2,1)S(1)}, u32[]{:S(2)}, u32[]{:S(2)}) collective-permute-start(bf16[2,8,64,128]{3,2,1,0:T(8,128)(2,1)S(1)} %pad_maximum_fusion.block.own), channel_id=1, source_target_pairs={{0,2},{1,3},{2,4},{3,5},{4,6},{5,7},{6,8},{7,9},{8,10},{9,11},{10,... | collective-permute-start | bytes 786440 | tf_op jit(solution)/shard_map/ppermute | solution.py:20
  5.3 1.3 %collective-permute-start = (bf16[4,64,128]{2,1,0:T(8,128)(2,1)S(1)}, bf16[4,64,128]{2,1,0:T(8,128)(2,1)S(1)}, u32[]{:S(2)}, u32[]{:S(2)}) collective-permute-start(bf16[4,64,128]{2,1,0:T(8,128)(2,1)S(1)} %get-tuple-element.61), channel_id=1, source_target_pairs={{0,16},{16,0},{1,17},{17,1},{2,18},{18,2},{3,19},{19,3},{4,20},{20... | collective-permute-start | bytes 196616 | tf_op jit(solution)/shard_map/ppermute | solution.py:25
  5.4 1.4 %collective-permute-start.1 = (bf16[4,64,128]{2,1,0:T(8,128)(2,1)S(1)}, bf16[4,64,128]{2,1,0:T(8,128)(2,1)S(1)}, u32[]{:S(2)}, u32[]{:S(2)}) collective-permute-start(bf16[4,64,128]{2,1,0:T(8,128)(2,1)S(1)} %get-tuple-element.62), channel_id=1, source_target_pairs={{0,16},{16,0},{1,17},{17,1},{2,18},{18,2},{3,19},{19,3},{4,20},{20... | collective-permute-start | bytes 196616 | tf_op jit(solution)/shard_map/ppermute | solution.py:25
  6.8 12.3 %collective-permute-start.2 = (bf16[2,2,128,128]{3,2,1,0:T(8,128)(2,1)S(1)}, bf16[2,2,128,128]{3,2,1,0:T(8,128)(2,1)S(1)}, u32[]{:S(2)}, u32[]{:S(2)}) collective-permute-start(bf16[2,2,128,128]{3,2,1,0:T(8,128)(2,1)S(1)} %get-tuple-element.63.first_half.own_a), channel_id=1, source_target_pairs={{0,1},{1,2},{2,3},{3,4},{4,5},{5,6},{6,7},{7,8},{8,9},{9,10},{10,1... | collective-permute-start | bytes 393224 | tf_op jit(solution)/shard_map/ppermute | solution.py:20
  8.4 4.2 %copy-start.2 = (s32[32]{0:T(128)S(1)}, s32[32]{0:T(128)}, u32[]{:S(2)}) copy-start(s32[32]{0:T(128)} %spans.1) | copy-start | bytes 388
  8.4 12.6 %collective-permute-start.8 = (bf16[2,2,128,128]{3,2,1,0:T(8,128)(2,1)S(1)}, bf16[2,2,128,128]{3,2,1,0:T(8,128)(2,1)S(1)}, u32[]{:S(2)}, u32[]{:S(2)}) collective-permute-start(bf16[2,2,128,128]{3,2,1,0:T(8,128)(2,1)S(1)} %get-tuple-element.64.second_half.own_b), channel_id=1, source_target_pairs={{0,1},{1,2},{2,3},{3,4},{4,5},{5,6},{6,7},{7,8},{8,9},{9,10},{10,1... | collective-permute-start | bytes 393224 | tf_op jit(solution)/shard_map/ppermute | solution.py:20
  16.8 1.3 %collective-permute-start.6 = (bf16[4,64,128]{2,1,0:T(8,128)(2,1)S(1)}, bf16[4,64,128]{2,1,0:T(8,128)(2,1)S(1)}, u32[]{:S(2)}, u32[]{:S(2)}) collective-permute-start(bf16[4,64,128]{2,1,0:T(8,128)(2,1)S(1)} %get-tuple-element.70), channel_id=1, source_target_pairs={{0,16},{16,0},{1,17},{17,1},{2,18},{18,2},{3,19},{19,3},{4,20},{20... | collective-permute-start | bytes 196616 | tf_op jit(solution)/shard_map/ppermute | solution.py:25
  16.8 1.4 %collective-permute-start.7 = (bf16[4,64,128]{2,1,0:T(8,128)(2,1)S(1)}, bf16[4,64,128]{2,1,0:T(8,128)(2,1)S(1)}, u32[]{:S(2)}, u32[]{:S(2)}) collective-permute-start(bf16[4,64,128]{2,1,0:T(8,128)(2,1)S(1)} %get-tuple-element.71), channel_id=1, source_target_pairs={{0,16},{16,0},{1,17},{17,1},{2,18},{18,2},{3,19},{19,3},{4,20},{20... | collective-permute-start | bytes 196616 | tf_op jit(solution)/shard_map/ppermute | solution.py:25
  20.1 9.6 %collective-permute-start.11 = (bf16[2,2,128,128]{3,2,1,0:T(8,128)(2,1)S(1)}, bf16[2,2,128,128]{3,2,1,0:T(8,128)(2,1)S(1)}, u32[]{:S(2)}, u32[]{:S(2)}) collective-permute-start(bf16[2,2,128,128]{3,2,1,0:T(8,128)(2,1)S(1)} %get-tuple-element.102), channel_id=1, source_target_pairs={{0,15},{1,0},{2,1},{3,2},{4,3},{5,4},{6,5},{7,6},{8,7},{9,8},{10,9... | collective-permute-start | bytes 393224 | tf_op jit(solution)/shard_map/ppermute | solution.py:20
  22.4 6.7 %collective-permute-start.9 = (bf16[4,64,128]{2,1,0:T(8,128)(2,1)S(1)}, bf16[4,64,128]{2,1,0:T(8,128)(2,1)S(1)}, u32[]{:S(2)}, u32[]{:S(2)}) collective-permute-start(bf16[4,64,128]{2,1,0:T(8,128)(2,1)S(1)} %get-tuple-element.98), channel_id=1, source_target_pairs={{0,16},{16,0},{1,17},{17,1},{2,18},{18,2},{3,19},{19,3},{4,20},{20... | collective-permute-start | bytes 196616 | tf_op jit(solution)/shard_map/ppermute | solution.py:25
  22.6 6.6 %collective-permute-start.10 = (bf16[4,64,128]{2,1,0:T(8,128)(2,1)S(1)}, bf16[4,64,128]{2,1,0:T(8,128)(2,1)S(1)}, u32[]{:S(2)}, u32[]{:S(2)}) collective-permute-start(bf16[4,64,128]{2,1,0:T(8,128)(2,1)S(1)} %get-tuple-element.99), channel_id=1, source_target_pairs={{0,16},{16,0},{1,17},{17,1},{2,18},{18,2},{3,19},{19,3},{4,20},{20... | collective-permute-start | bytes 196616 | tf_op jit(solution)/shard_map/ppermute | solution.py:25
  23.0 10.0 %collective-permute-start.15 = (bf16[2,2,128,128]{3,2,1,0:T(8,128)(2,1)S(1)}, bf16[2,2,128,128]{3,2,1,0:T(8,128)(2,1)S(1)}, u32[]{:S(2)}, u32[]{:S(2)}) collective-permute-start(bf16[2,2,128,128]{3,2,1,0:T(8,128)(2,1)S(1)} %get-tuple-element.112), channel_id=1, source_target_pairs={{0,15},{1,0},{2,1},{3,2},{4,3},{5,4},{6,5},{7,6},{8,7},{9,8},{10,9... | collective-permute-start | bytes 393224 | tf_op jit(solution)/shard_map/ppermute | solution.py:20
  29.2 8.6 %collective-permute-start.17 = (bf16[2,8,64,128]{3,2,1,0:T(8,128)(2,1)S(1)}, bf16[2,8,64,128]{3,2,1,0:T(8,128)(2,1)S(1)}, u32[]{:S(2)}, u32[]{:S(2)}) collective-permute-start(bf16[2,8,64,128]{3,2,1,0:T(8,128)(2,1)S(1)} %join_two.1.after), channel_id=1, source_target_pairs={{0,14},{1,15},{2,0},{3,1},{4,2},{5,3},{6,4},{7,5},{8,6},{9,7},{10,... | collective-permute-start | bytes 786440 | tf_op jit(solution)/shard_map/ppermute | solution.py:20
  30.5 2.6 %collective-permute-start.13 = (bf16[11,64,128]{2,1,0:T(8,128)(2,1)S(1)}, bf16[11,64,128]{2,1,0:T(8,128)(2,1)S(1)}, u32[]{:S(2)}, u32[]{:S(2)}) collective-permute-start(bf16[11,64,128]{2,1,0:T(8,128)(2,1)S(1)} %get-tuple-element.107), channel_id=1, source_target_pairs={{0,16},{16,0},{1,17},{17,1},{2,18},{18,2},{3,19},{19,3},{4,20},{20... | collective-permute-start | bytes 540680 | tf_op jit(solution)/shard_map/ppermute | solution.py:25
  30.6 2.6 %collective-permute-start.14 = (bf16[11,64,128]{2,1,0:T(8,128)(2,1)S(1)}, bf16[11,64,128]{2,1,0:T(8,128)(2,1)S(1)}, u32[]{:S(2)}, u32[]{:S(2)}) collective-permute-start(bf16[11,64,128]{2,1,0:T(8,128)(2,1)S(1)} %get-tuple-element.108), channel_id=1, source_target_pairs={{0,16},{16,0},{1,17},{17,1},{2,18},{18,2},{3,19},{19,3},{4,20},{20... | collective-permute-start | bytes 540680 | tf_op jit(solution)/shard_map/ppermute | solution.py:25
  31.1 2.1 %collective-permute-start.12 = (bf16[10,64,128]{2,1,0:T(8,128)(2,1)S(1)}, bf16[10,64,128]{2,1,0:T(8,128)(2,1)S(1)}, u32[]{:S(2)}, u32[]{:S(2)}) collective-permute-start(bf16[10,64,128]{2,1,0:T(8,128)(2,1)S(1)} %get-tuple-element.106), channel_id=1, source_target_pairs={{0,16},{16,0},{1,17},{17,1},{2,18},{18,2},{3,19},{19,3},{4,20},{20... | collective-permute-start | bytes 491528 | tf_op jit(solution)/shard_map/ppermute | solution.py:25
  33.1 1.4 %collective-permute-start.16 = (bf16[2,4,64,128]{3,2,1,0:T(8,128)(2,1)S(1)}, bf16[2,4,64,128]{3,2,1,0:T(8,128)(2,1)S(1)}, u32[]{:S(2)}, u32[]{:S(2)}) collective-permute-start(bf16[2,4,64,128]{3,2,1,0:T(8,128)(2,1)S(1)} %get-tuple-element.114), channel_id=1, source_target_pairs={{0,16},{16,0},{1,17},{17,1},{2,18},{18,2},{3,19},{19,3},{4,20},{20... | collective-permute-start | bytes 393224 | tf_op jit(solution)/shard_map/ppermute | solution.py:25

commit v18 on v16

--- a/solution.py
+++ b/solution.py
@@ -15,7 +15,7 @@
 
 def shifted(block, axis, distance, ring=True):
     count = lax.axis_size(axis)
-    route = [(i, (i + distance) % count) for i in range(count) if ring or i + distance < count]
+    route = [(i, (i + distance) % count) for i in range(count) if ring or 0 <= i + distance < count]
     return lax.ppermute(block, axis, route)
 
 
@@ -478,7 +478,7 @@
         [whole_pair],
         (part_mine, *[swapped(send, "head") for send in part_sends]),
     )
-    two_total = shifted(two_part, "seq", -2)
+    two_total = shifted(two_part, "seq", -2, ring=False)
     own_grad, own_part = call(
         own_backward_kernel,
         "own_backward",

time: 34.6 us -> 35.8 us (1.035)
  waiting for transfers between devices: 6.59 us -> 9.86 us
  starting transfers between devices: 17.6 us -> 15.6 us
    ppermute x4, waiting for transfers between devices: 2.45 us -> 5.63 us  [shifted(): return lax.ppermute(block, axis, route)]
    ppermute x4, starting transfers between devices: 14.1 us -> 12.1 us  [shifted(): return lax.ppermute(block, axis, route)]
  transfers between devices with their start and end apart: 17 -> 17, of which waited for: 10 -> 10; matrix products, arithmetic and copies ran while one was open for 0% -> 0% of each run, Pallas kernels for 16% -> 15%
where the time goes in v18:
time: 35.8 us; the launch traced here: 35.7 us
  starting transfers between devices  15.6 us (44%)
  waiting for transfers between devices  9.86 us (28%)
  Pallas kernels  7.69 us (21%)
  between operations  1.44 us (4%)
  other arithmetic  1.05 us (3%)
    ppermute x4, starting transfers between devices, shifted(): return lax.ppermute(block, axis, route)  12.1 us
    pallas_call x14, Pallas kernels, call(): pl.pallas_call(kernel, out_shape=tuple((jax.ShapeDtypeStruct(shape, kind)...  7.69 us
    ppermute x4, waiting for transfers between devices, shifted(): return lax.ppermute(block, axis, route)  5.63 us
    ppermute x13, waiting for transfers between devices, swapped(): return lax.ppermute(block, axis, [(i, count - 1 - i) for i in range(count)])  4.23 us
    ppermute x13, starting transfers between devices, swapped(): return lax.ppermute(block, axis, [(i, count - 1 - i) for i in range(count)])  3.51 us
    another operation x1, other arithmetic, shards(): own = jnp.stack([key_matrix, value_matrix])  1.05 us
  transfers between devices with their start and end apart: 17, of which 10 were waited for; matrix products, arithmetic and copies ran while one was open for 0% of the time, Pallas kernels for 15%

profile of v18, /device:TPU:0, one launch (start us, length us, event | category | flops | bytes accessed | tf_op | source)
XLA Modules:
  0.0 35.7 jit_solution(16974259615768912250)
XLA Ops:
  0.6 1.1 %pad_maximum_fusion.block.own.after = bf16[2,8,64,128]{3,2,1,0:T(8,128)(2,1)S(1)} fusion(bf16[1,8,64,128]{3,2,1,0:T(8,128)(2,1)} %bitcast.2, bf16[1,8,64,128]{3,2,1,0:T(8,128)(2,1)} %bitcast.3), kind=kLoop, calls=%fused_computation | loop fusion | flops 131072 | bytes 524288 | tf_op jit(solution)/shard_map/stack | solution.py:423
  1.7 3.0 %collective-permute-start.3 = (bf16[2,8,64,128]{3,2,1,0:T(8,128)(2,1)S(1)}, bf16[2,8,64,128]{3,2,1,0:T(8,128)(2,1)S(1)}, u32[]{:S(2)}, u32[]{:S(2)}) collective-permute-start(bf16[2,8,64,128]{3,2,1,0:T(8,128)(2,1)S(1)} %pad_maximum_fusion.block.own.after), channel_id=1, source_target_pairs={{0,2},{1,3},{2,4},{3,5},{4,6},{5,7},{6,8},{7,9},{8,10},{9,11},{10,... | collective-permute-start | bytes 786440 | tf_op jit(solution)/shard_map/ppermute | solution.py:19
  4.8 0.5 %collective-permute-start.1 = (bf16[4,64,128]{2,1,0:T(8,128)(2,1)S(1)}, bf16[4,64,128]{2,1,0:T(8,128)(2,1)S(1)}, u32[]{:S(2)}, u32[]{:S(2)}) collective-permute-start(bf16[4,64,128]{2,1,0:T(8,128)(2,1)S(1)} %get-tuple-element.54), channel_id=1, source_target_pairs={{0,16},{16,0},{1,17},{17,1},{2,18},{18,2},{3,19},{19,3},{4,20},{20... | collective-permute-start | bytes 196616 | tf_op jit(solution)/shard_map/ppermute | solution.py:24
  5.3 0.7 %collective-permute-done.other_keys = bf16[4,64,128]{2,1,0:T(8,128)(2,1)S(1)} collective-permute-done((bf16[4,64,128]{2,1,0:T(8,128)(2,1)S(1)}, bf16[4,64,128]{2,1,0:T(8,128)(2,1)S(1)}, u32[]{:S(2)}, u32[]{:S(2)}) %collective-permute-start) | collective-permute-done | bytes 65568 | tf_op jit(solution)/shard_map/ppermute | solution.py:24
  6.2 3.4 %collective-permute-start.2 = (bf16[2,4,128,128]{3,2,1,0:T(8,128)(2,1)S(1)}, bf16[2,4,128,128]{3,2,1,0:T(8,128)(2,1)S(1)}, u32[]{:S(2)}, u32[]{:S(2)}) collective-permute-start(bf16[2,4,128,128]{3,2,1,0:T(8,128)(2,1)S(1)} %join_own.1.own), channel_id=1, source_target_pairs={{0,1},{1,2},{2,3},{3,4},{4,5},{5,6},{6,7},{7,8},{8,9},{9,10},{10,1... | collective-permute-start | bytes 786440 | tf_op jit(solution)/shard_map/ppermute | solution.py:19
  9.9 0.4 %collective-permute-start.6 = (bf16[11,64,128]{2,1,0:T(8,128)(2,1)S(1)}, bf16[11,64,128]{2,1,0:T(8,128)(2,1)S(1)}, u32[]{:S(2)}, u32[]{:S(2)}) collective-permute-start(bf16[11,64,128]{2,1,0:T(8,128)(2,1)S(1)} %get-tuple-element.57), channel_id=1, source_target_pairs={{0,16},{16,0},{1,17},{17,1},{2,18},{18,2},{3,19},{19,3},{4,20},{20... | collective-permute-start | bytes 540680 | tf_op jit(solution)/shard_map/ppermute | solution.py:24
  11.0 0.7 %collective-permute-done.4.first_third = bf16[10,64,128]{2,1,0:T(8,128)(2,1)S(1)} collective-permute-done((bf16[10,64,128]{2,1,0:T(8,128)(2,1)S(1)}, bf16[10,64,128]{2,1,0:T(8,128)(2,1)S(1)}, u32[]{:S(2)}, u32[]{:S(2)}) %collective-permute-start.4) | collective-permute-done | bytes 163872 | tf_op jit(solution)/shard_map/ppermute | solution.py:24
  11.7 1.5 %own_block.1 = (bf16[16,128,128]{2,1,0:T(8,128)(2,1)S(1)}, bf16[16,128,128]{2,1,0:T(8,128)(2,1)S(1)}, bf16[8,128,256]{2,1,0:T(8,128)(2,1)S(1)}, s32[8,1,256]{2,1...) custom-call(s32[32]{0:T(128)S(1)} %copy-done.2, ...), custom_call_target="tpu_custom_call" | custom-call | flops 1 | tf_op jit(solution)/shard_map/own_block/pallas_call | solution.py:400
  13.3 0.8 %collective-permute-done.3.block.back_two = bf16[2,8,64,128]{3,2,1,0:T(8,128)(2,1)S(1)} collective-permute-done((bf16[2,8,64,128]{3,2,1,0:T(8,128)(2,1)S(1)}, bf16[2,8,64,128]{3,2,1,0:T(8,128)(2,1)S(1)}, u32[]{:S(2)}, u32[]{:S(2)}) %collective-permute-start.3) | collective-permute-done | bytes 262176 | tf_op jit(solution)/shard_map/ppermute | solution.py:19
  14.2 0.5 %collective-permute-start.8 = (bf16[4,64,128]{2,1,0:T(8,128)(2,1)S(1)}, bf16[4,64,128]{2,1,0:T(8,128)(2,1)S(1)}, u32[]{:S(2)}, u32[]{:S(2)}) collective-permute-start(bf16[4,64,128]{2,1,0:T(8,128)(2,1)S(1)} %get-tuple-element.64), channel_id=1, source_target_pairs={{0,16},{16,0},{1,17},{17,1},{2,18},{18,2},{3,19},{19,3},{4,20},{20... | collective-permute-start | bytes 196616 | tf_op jit(solution)/shard_map/ppermute | solution.py:24
  14.7 0.7 %collective-permute-done.7.two_keys = bf16[4,64,128]{2,1,0:T(8,128)(2,1)S(1)} collective-permute-done((bf16[4,64,128]{2,1,0:T(8,128)(2,1)S(1)}, bf16[4,64,128]{2,1,0:T(8,128)(2,1)S(1)}, u32[]{:S(2)}, u32[]{:S(2)}) %collective-permute-start.7) | collective-permute-done | bytes 65568 | tf_op jit(solution)/shard_map/ppermute | solution.py:24
  15.6 0.9 %near_forward.1 = (f32[8,1,256]{2,1,0:T(1,128)S(1)}, f32[8,1,256]{2,1,0:T(1,128)S(1)}, f32[8,128,256]{2,1,0:T(8,128)S(1)}, f32[8,128,256]{2,1,0:T(8,128)S(1)}, f...) custom-call(s32[8,1,256]{2,1,0:T(1,128)S(1)} %get-tuple-element.59.first, ...), custom_call_target="tpu_custom_call" | custom-call | flops 1 | tf_op jit(solution)/shard_map/near_forward/pallas_call | solution.py:400
  16.5 1.5 %last_forward_backward.1 = (bf16[8,128,256]{2,1,0:T(8,128)(2,1)S(1)}, f32[8,1,256]{2,1,0:T(1,128)S(1)}, f32[8,1,256]{2,1,0:T(1,128)S(1)}, bf16[8,128,256]{2,1,0:T(8,128)(2,1)S(1)}, bf16[2,4,128,128]{3,2,1,0:T(8,128)(2,1)S(1)}) custom-call(s32[8,1,256]{2,1,0:T(1,128)S(1)} %get-tuple-element.59.first, bf16[16,128,128]{2,1,0:T(8,128)(2,1)S(1)} %get-tuple-element.60.query_head, ...), custom_call_target="tpu_custom_call" | custom-call | flops 1 | tf_op jit(solution)/shard_map/last_forward_backward/pallas_call | solution.py:400
  18.1 4.4 %collective-permute-start.14 = (bf16[2,4,128,128]{3,2,1,0:T(8,128)(2,1)S(1)}, bf16[2,4,128,128]{3,2,1,0:T(8,128)(2,1)S(1)}, u32[]{:S(2)}, u32[]{:S(2)}) collective-permute-start(bf16[2,4,128,128]{3,2,1,0:T(8,128)(2,1)S(1)} %get-tuple-element.96), channel_id=1, source_target_pairs={{0,15},{1,0},{2,1},{3,2},{4,3},{5,4},{6,5},{7,6},{8,7},{9,8},{10,9... | collective-permute-start | bytes 786440 | tf_op jit(solution)/shard_map/ppermute | solution.py:19
  22.4 0.5 %two_backward.1 = (bf16[8,128,256]{2,1,0:T(8,128)(2,1)S(1)}, bf16[2,4,64,128]{3,2,1,0:T(8,128)(2,1)S(1)}, bf16[4,64,128]{2,1,0:T(8,128)(2,1)S(1)}, bf16[4,64,128]{2,1,0:T(8,128)(2,1)S(1)}) custom-call(bf16[16,128,128]{2,1,0:T(8,128)(2,1)S(1)} %get-tuple-element.60.query_head, bf16[16,128,128]{2,1,0:T(8,128)(2,1)S(1)} %get-tuple-element.61.grad_head, ...), custom_call_target="tpu_custom_call" | custom-call | flops 1 | tf_op jit(solution)/shard_map/two_backward/pallas_call | solution.py:400
  23.0 0.5 %collective-permute-start.10 = (bf16[4,64,128]{2,1,0:T(8,128)(2,1)S(1)}, bf16[4,64,128]{2,1,0:T(8,128)(2,1)S(1)}, u32[]{:S(2)}, u32[]{:S(2)}) collective-permute-start(bf16[4,64,128]{2,1,0:T(8,128)(2,1)S(1)} %get-tuple-element.86), channel_id=1, source_target_pairs={{0,16},{16,0},{1,17},{17,1},{2,18},{18,2},{3,19},{19,3},{4,20},{20... | collective-permute-start | bytes 196616 | tf_op jit(solution)/shard_map/ppermute | solution.py:24
  23.5 0.7 %collective-permute-done.9.other_keys = bf16[4,64,128]{2,1,0:T(8,128)(2,1)S(1)} collective-permute-done((bf16[4,64,128]{2,1,0:T(8,128)(2,1)S(1)}, bf16[4,64,128]{2,1,0:T(8,128)(2,1)S(1)}, u32[]{:S(2)}, u32[]{:S(2)}) %collective-permute-start.9) | collective-permute-done | bytes 65568 | tf_op jit(solution)/shard_map/ppermute | solution.py:24
  24.4 1.3 %collective-permute-start.16 = (bf16[2,8,64,128]{3,2,1,0:T(8,128)(2,1)S(1)}, bf16[2,8,64,128]{3,2,1,0:T(8,128)(2,1)S(1)}, u32[]{:S(2)}, u32[]{:S(2)}) collective-permute-start(bf16[2,8,64,128]{3,2,1,0:T(8,128)(2,1)S(1)} %join_two.1.after), channel_id=1, source_target_pairs={{2,0},{3,1},{4,2},{5,3},{6,4},{7,5},{8,6},{9,7},{10,8},{11,9},{12,... | collective-permute-start | bytes 786440 | tf_op jit(solution)/shard_map/ppermute | solution.py:19
  25.8 0.5 %own_backward.1 = (bf16[8,128,256]{2,1,0:T(8,128)(2,1)S(1)}, f32[2,4,128,128]{3,2,1,0:T(8,128)S(1)}) custom-call(bf16[16,128,128]{2,1,0:T(8,128)(2,1)S(1)} %get-tuple-element.60.query_head, bf16[16,128,128]{2,1,0:T(8,128)(2,1)S(1)} %get-tuple-element.61.grad_head, f32[8,128,256]{2,1,0:T(8,128)S(1)} %get-tuple-element.81.own_weights, ...), custom_call_target="tpu_custom_call" | custom-call | flops 1 | tf_op jit(solution)/shard_map/own_backward/pallas_call | solution.py:400
  26.2 0.8 %query_grad.1 = (bf16[16,64,128]{2,1,0:T(8,128)(2,1)S(1)}, bf16[16,64,128]{2,1,0:T(8,128)(2,1)S(1)}, bf16[10,64,128]{2,1,0:T(8,128)(2,1)S(1)}, bf16[11,64,128]{2,1,0:T(8,128)(2,1)S(1)}, bf16[11,64,128]{2,1,0:T(8,128)(2,1)S(1)}) custom-call(bf16[2,4,128,128]{3,2,1,0:T(8,128)(2,1)S(1)} %join_own.1.own, ...), custom_call_target="tpu_custom_call" | custom-call | flops 1 | tf_op jit(solution)/shard_map/query_grad/pallas_call | solution.py:400
  28.2 0.8 %collective-permute-done.11.first_third = bf16[10,64,128]{2,1,0:T(8,128)(2,1)S(1)} collective-permute-done((bf16[10,64,128]{2,1,0:T(8,128)(2,1)S(1)}, bf16[10,64,128]{2,1,0:T(8,128)(2,1)S(1)}, u32[]{:S(2)}, u32[]{:S(2)}) %collective-permute-start.11) | collective-permute-done | bytes 163872 | tf_op jit(solution)/shard_map/ppermute | solution.py:24
  29.0 1.0 %assemble.1 = (bf16[32,64,128]{2,1,0:T(8,128)(2,1)}, bf16[32,64,128]{2,1,0:T(8,128)(2,1)}, f32[8,128]{1,0:T(8,128)S(1)}) custom-call(bf16[16,64,128]{2,1,0:T(8,128)(2,1)S(1)} %get-tuple-element.88.out_mine, bf16[16,64,128]{2,1,0:T(8,128)(2,1)S(1)} %get-tuple-element.89.query_mine, bf16[10,64,128]{2,1,0:T(8,128)(2,1)S(1)} %collective-permute-done.11.first_third, ...), custom_call_target="tpu_custom_call" | custom-call | flops 1 | tf_op jit(solution)/shard_map/assemble/pallas_call | solution.py:400
  30.1 4.8 %collective-permute-done.16.two_total = bf16[2,8,64,128]{3,2,1,0:T(8,128)(2,1)S(1)} collective-permute-done((bf16[2,8,64,128]{3,2,1,0:T(8,128)(2,1)S(1)}, bf16[2,8,64,128]{3,2,1,0:T(8,128)(2,1)S(1)}, u32[]{:S(2)}, u32[]{:S(2)}) %collective-permute-start.16) | collective-permute-done | bytes 262176 | tf_op jit(solution)/shard_map/ppermute | solution.py:19
  34.9 0.8 %total.1 = (bf16[8,64,128]{2,1,0:T(8,128)(2,1)}, bf16[8,64,128]{2,1,0:T(8,128)(2,1)}) custom-call(f32[2,4,64,128]{3,2,1,0:T(8,128)S(1)} %get-tuple-element.97.sum_mine, bf16[2,4,64,128]{3,2,1,0:T(8,128)(2,1)S(1)} %collective-permute-done.15.sum_other, bf16[2,8,64,128]{3,2,1,0:T(8,128)(2,1)S(1)} %collective-permute-done.16.two_total, ...), custom_call_target="tpu_custom_call" | custom-call | flops 1 | tf_op jit(solution)/shard_map/total/pallas_call | solution.py:400
  (31 shorter events, 2.3 us)
Async XLA Ops:
  0.6 9.0 %copy-start.1 = (bf16[32,64,128]{2,1,0:T(8,128)(2,1)S(1)}, bf16[32,64,128]{2,1,0:T(8,128)(2,1)}, u32[]{:S(2)}) copy-start(bf16[32,64,128]{2,1,0:T(8,128)(2,1)} %grads.3) | copy-start | bytes 1572868
  1.7 8.0 %copy-start = (bf16[32,64,128]{2,1,0:T(8,128)(2,1)S(1)}, bf16[32,64,128]{2,1,0:T(8,128)(2,1)}, u32[]{:S(2)}) copy-start(bf16[32,64,128]{2,1,0:T(8,128)(2,1)} %queries.3) | copy-start | bytes 1572868
  1.7 12.4 %collective-permute-start.3 = (bf16[2,8,64,128]{3,2,1,0:T(8,128)(2,1)S(1)}, bf16[2,8,64,128]{3,2,1,0:T(8,128)(2,1)S(1)}, u32[]{:S(2)}, u32[]{:S(2)}) collective-permute-start(bf16[2,8,64,128]{3,2,1,0:T(8,128)(2,1)S(1)} %pad_maximum_fusion.block.own.after), channel_id=1, source_target_pairs={{0,2},{1,3},{2,4},{3,5},{4,6},{5,7},{6,8},{7,9},{8,10},{9,11},{10,... | collective-permute-start | bytes 786440 | tf_op jit(solution)/shard_map/ppermute | solution.py:19
  4.7 1.3 %collective-permute-start = (bf16[4,64,128]{2,1,0:T(8,128)(2,1)S(1)}, bf16[4,64,128]{2,1,0:T(8,128)(2,1)S(1)}, u32[]{:S(2)}, u32[]{:S(2)}) collective-permute-start(bf16[4,64,128]{2,1,0:T(8,128)(2,1)S(1)} %get-tuple-element.53), channel_id=1, source_target_pairs={{0,16},{16,0},{1,17},{17,1},{2,18},{18,2},{3,19},{19,3},{4,20},{20... | collective-permute-start | bytes 196616 | tf_op jit(solution)/shard_map/ppermute | solution.py:24
  4.8 1.4 %collective-permute-start.1 = (bf16[4,64,128]{2,1,0:T(8,128)(2,1)S(1)}, bf16[4,64,128]{2,1,0:T(8,128)(2,1)S(1)}, u32[]{:S(2)}, u32[]{:S(2)}) collective-permute-start(bf16[4,64,128]{2,1,0:T(8,128)(2,1)S(1)} %get-tuple-element.54), channel_id=1, source_target_pairs={{0,16},{16,0},{1,17},{17,1},{2,18},{18,2},{3,19},{19,3},{4,20},{20... | collective-permute-start | bytes 196616 | tf_op jit(solution)/shard_map/ppermute | solution.py:24
  6.2 10.3 %collective-permute-start.2 = (bf16[2,4,128,128]{3,2,1,0:T(8,128)(2,1)S(1)}, bf16[2,4,128,128]{3,2,1,0:T(8,128)(2,1)S(1)}, u32[]{:S(2)}, u32[]{:S(2)}) collective-permute-start(bf16[2,4,128,128]{3,2,1,0:T(8,128)(2,1)S(1)} %join_own.1.own), channel_id=1, source_target_pairs={{0,1},{1,2},{2,3},{3,4},{4,5},{5,6},{6,7},{7,8},{8,9},{9,10},{10,1... | collective-permute-start | bytes 786440 | tf_op jit(solution)/shard_map/ppermute | solution.py:19
  9.7 2.0 %collective-permute-start.5 = (bf16[11,64,128]{2,1,0:T(8,128)(2,1)S(1)}, bf16[11,64,128]{2,1,0:T(8,128)(2,1)S(1)}, u32[]{:S(2)}, u32[]{:S(2)}) collective-permute-start(bf16[11,64,128]{2,1,0:T(8,128)(2,1)S(1)} %get-tuple-element.56), channel_id=1, source_target_pairs={{0,16},{16,0},{1,17},{17,1},{2,18},{18,2},{3,19},{19,3},{4,20},{20... | collective-permute-start | bytes 540680 | tf_op jit(solution)/shard_map/ppermute | solution.py:24
  9.9 1.8 %collective-permute-start.6 = (bf16[11,64,128]{2,1,0:T(8,128)(2,1)S(1)}, bf16[11,64,128]{2,1,0:T(8,128)(2,1)S(1)}, u32[]{:S(2)}, u32[]{:S(2)}) collective-permute-start(bf16[11,64,128]{2,1,0:T(8,128)(2,1)S(1)} %get-tuple-element.57), channel_id=1, source_target_pairs={{0,16},{16,0},{1,17},{17,1},{2,18},{18,2},{3,19},{19,3},{4,20},{20... | collective-permute-start | bytes 540680 | tf_op jit(solution)/shard_map/ppermute | solution.py:24
  10.3 1.4 %copy-start.2 = (s32[32]{0:T(128)S(1)}, s32[32]{0:T(128)}, u32[]{:S(2)}) copy-start(s32[32]{0:T(128)} %spans.1) | copy-start | bytes 388
  10.3 1.4 %collective-permute-start.4 = (bf16[10,64,128]{2,1,0:T(8,128)(2,1)S(1)}, bf16[10,64,128]{2,1,0:T(8,128)(2,1)S(1)}, u32[]{:S(2)}, u32[]{:S(2)}) collective-permute-start(bf16[10,64,128]{2,1,0:T(8,128)(2,1)S(1)} %get-tuple-element.55), channel_id=1, source_target_pairs={{0,16},{16,0},{1,17},{17,1},{2,18},{18,2},{3,19},{19,3},{4,20},{20... | collective-permute-start | bytes 491528 | tf_op jit(solution)/shard_map/ppermute | solution.py:24
  14.1 1.3 %collective-permute-start.7 = (bf16[4,64,128]{2,1,0:T(8,128)(2,1)S(1)}, bf16[4,64,128]{2,1,0:T(8,128)(2,1)S(1)}, u32[]{:S(2)}, u32[]{:S(2)}) collective-permute-start(bf16[4,64,128]{2,1,0:T(8,128)(2,1)S(1)} %get-tuple-element.63), channel_id=1, source_target_pairs={{0,16},{16,0},{1,17},{17,1},{2,18},{18,2},{3,19},{19,3},{4,20},{20... | collective-permute-start | bytes 196616 | tf_op jit(solution)/shard_map/ppermute | solution.py:24
  14.2 1.4 %collective-permute-start.8 = (bf16[4,64,128]{2,1,0:T(8,128)(2,1)S(1)}, bf16[4,64,128]{2,1,0:T(8,128)(2,1)S(1)}, u32[]{:S(2)}, u32[]{:S(2)}) collective-permute-start(bf16[4,64,128]{2,1,0:T(8,128)(2,1)S(1)} %get-tuple-element.64), channel_id=1, source_target_pairs={{0,16},{16,0},{1,17},{17,1},{2,18},{18,2},{3,19},{19,3},{4,20},{20... | collective-permute-start | bytes 196616 | tf_op jit(solution)/shard_map/ppermute | solution.py:24
  18.1 9.8 %collective-permute-start.14 = (bf16[2,4,128,128]{3,2,1,0:T(8,128)(2,1)S(1)}, bf16[2,4,128,128]{3,2,1,0:T(8,128)(2,1)S(1)}, u32[]{:S(2)}, u32[]{:S(2)}) collective-permute-start(bf16[2,4,128,128]{3,2,1,0:T(8,128)(2,1)S(1)} %get-tuple-element.96), channel_id=1, source_target_pairs={{0,15},{1,0},{2,1},{3,2},{4,3},{5,4},{6,5},{7,6},{8,7},{9,8},{10,9... | collective-permute-start | bytes 786440 | tf_op jit(solution)/shard_map/ppermute | solution.py:19
  22.9 1.3 %collective-permute-start.9 = (bf16[4,64,128]{2,1,0:T(8,128)(2,1)S(1)}, bf16[4,64,128]{2,1,0:T(8,128)(2,1)S(1)}, u32[]{:S(2)}, u32[]{:S(2)}) collective-permute-start(bf16[4,64,128]{2,1,0:T(8,128)(2,1)S(1)} %get-tuple-element.85), channel_id=1, source_target_pairs={{0,16},{16,0},{1,17},{17,1},{2,18},{18,2},{3,19},{19,3},{4,20},{20... | collective-permute-start | bytes 196616 | tf_op jit(solution)/shard_map/ppermute | solution.py:24
  23.0 1.4 %collective-permute-start.10 = (bf16[4,64,128]{2,1,0:T(8,128)(2,1)S(1)}, bf16[4,64,128]{2,1,0:T(8,128)(2,1)S(1)}, u32[]{:S(2)}, u32[]{:S(2)}) collective-permute-start(bf16[4,64,128]{2,1,0:T(8,128)(2,1)S(1)} %get-tuple-element.86), channel_id=1, source_target_pairs={{0,16},{16,0},{1,17},{17,1},{2,18},{18,2},{3,19},{19,3},{4,20},{20... | collective-permute-start | bytes 196616 | tf_op jit(solution)/shard_map/ppermute | solution.py:24
  24.4 10.5 %collective-permute-start.16 = (bf16[2,8,64,128]{3,2,1,0:T(8,128)(2,1)S(1)}, bf16[2,8,64,128]{3,2,1,0:T(8,128)(2,1)S(1)}, u32[]{:S(2)}, u32[]{:S(2)}) collective-permute-start(bf16[2,8,64,128]{3,2,1,0:T(8,128)(2,1)S(1)} %join_two.1.after), channel_id=1, source_target_pairs={{2,0},{3,1},{4,2},{5,3},{6,4},{7,5},{8,6},{9,7},{10,8},{11,9},{12,... | collective-permute-start | bytes 786440 | tf_op jit(solution)/shard_map/ppermute | solution.py:19
  27.0 2.1 %collective-permute-start.12 = (bf16[11,64,128]{2,1,0:T(8,128)(2,1)S(1)}, bf16[11,64,128]{2,1,0:T(8,128)(2,1)S(1)}, u32[]{:S(2)}, u32[]{:S(2)}) collective-permute-start(bf16[11,64,128]{2,1,0:T(8,128)(2,1)S(1)} %get-tuple-element.91), channel_id=1, source_target_pairs={{0,16},{16,0},{1,17},{17,1},{2,18},{18,2},{3,19},{19,3},{4,20},{20... | collective-permute-start | bytes 540680 | tf_op jit(solution)/shard_map/ppermute | solution.py:24
  27.4 1.7 %collective-permute-start.13 = (bf16[11,64,128]{2,1,0:T(8,128)(2,1)S(1)}, bf16[11,64,128]{2,1,0:T(8,128)(2,1)S(1)}, u32[]{:S(2)}, u32[]{:S(2)}) collective-permute-start(bf16[11,64,128]{2,1,0:T(8,128)(2,1)S(1)} %get-tuple-element.92), channel_id=1, source_target_pairs={{0,16},{16,0},{1,17},{17,1},{2,18},{18,2},{3,19},{19,3},{4,20},{20... | collective-permute-start | bytes 540680 | tf_op jit(solution)/shard_map/ppermute | solution.py:24
  27.5 1.5 %collective-permute-start.11 = (bf16[10,64,128]{2,1,0:T(8,128)(2,1)S(1)}, bf16[10,64,128]{2,1,0:T(8,128)(2,1)S(1)}, u32[]{:S(2)}, u32[]{:S(2)}) collective-permute-start(bf16[10,64,128]{2,1,0:T(8,128)(2,1)S(1)} %get-tuple-element.90), channel_id=1, source_target_pairs={{0,16},{16,0},{1,17},{17,1},{2,18},{18,2},{3,19},{19,3},{4,20},{20... | collective-permute-start | bytes 491528 | tf_op jit(solution)/shard_map/ppermute | solution.py:24
  28.0 6.9 %collective-permute-start.15 = (bf16[2,4,64,128]{3,2,1,0:T(8,128)(2,1)S(1)}, bf16[2,4,64,128]{3,2,1,0:T(8,128)(2,1)S(1)}, u32[]{:S(2)}, u32[]{:S(2)}) collective-permute-start(bf16[2,4,64,128]{3,2,1,0:T(8,128)(2,1)S(1)} %get-tuple-element.98), channel_id=1, source_target_pairs={{0,16},{16,0},{1,17},{17,1},{2,18},{18,2},{3,19},{19,3},{4,20},{20... | collective-permute-start | bytes 393224 | tf_op jit(solution)/shard_map/ppermute | solution.py:24

commit v19 on v16

--- a/solution.py
+++ b/solution.py
@@ -281,10 +281,10 @@
 
 def two_backward_kernel(
     query_head, grad_head, near_weights, near_prob_grad, near_factor, row_delta,
-    two_grad, two_mine, send_keys, send_values,
+    two_grad, two_part,
 ):
     chunks = near_weights.shape[0]
-    groups, length, width = two_mine.shape[1:]
+    groups, _, width = two_part.shape[1:]
 
     def differentiate(n):
         prob = near_weights[n] * near_factor[n]
@@ -293,11 +293,8 @@
         return score_grad, prob.astype(jnp.bfloat16)
 
     def store(g, key_part, value_part):
-        for index, (part, send) in enumerate(
-            ((key_part * width ** (-0.5), send_keys), (value_part, send_values))
-        ):
-            two_mine[index, g] = part[:length].astype(jnp.bfloat16)
-            send[g] = part[length:].astype(jnp.bfloat16)
+        two_part[0, g] = (key_part * width ** (-0.5)).astype(jnp.bfloat16)
+        two_part[1, g] = value_part.astype(jnp.bfloat16)
 
     accumulate = accumulator(query_head, grad_head, chunks, groups, store)
     pipelined(chunks, differentiate, accumulate)
@@ -324,11 +321,11 @@
     pipelined(chunks, differentiate, accumulate)
 
 
-def join_two_kernel(two_mine, other_keys, other_values, two_part):
-    groups = two_mine.shape[1]
-    two_part[:, my_heads(groups)] = two_mine[...]
-    two_part[0, other_heads(groups)] = other_keys[...]
-    two_part[1, other_heads(groups)] = other_values[...]
+def join_one_kernel(one_part, one_other, joined):
+    groups, tokens = one_part.shape[1:3]
+    length = tokens // 2
+    joined[:, my_heads(groups)] = one_part[:, :, pl.ds(0, length)]
+    joined[:, other_heads(groups)] = one_other[:, :, pl.ds(length, length)]
 
 
 def query_kernel(
@@ -366,20 +363,20 @@
     token[...] = jnp.zeros(token.shape, token.dtype)
 
 
-def own_sum_kernel(own_part, one_total, sum_mine, sum_send):
+def own_sum_kernel(own_part, two_total, sum_mine, sum_send):
     length = sum_mine.shape[2]
-    total = own_part[...] + one_total[...].astype(jnp.float32)
+    total = own_part[...] + two_total[...].astype(jnp.float32)
     sum_mine[...] = total[:, :, :length]
     sum_send[...] = total[:, :, length:].astype(jnp.bfloat16)
 
 
-def final_kernel(sum_mine, sum_other, two_total, after, key_grad, value_grad):
+def final_kernel(sum_mine, sum_other, one_total, after, key_grad, value_grad):
     groups = sum_mine.shape[1]
     mine, other = my_heads(groups), other_heads(groups)
     for index, result in enumerate((key_grad, value_grad)):
-        total = sum_mine[index] + two_total[index, mine].astype(jnp.float32)
+        total = sum_mine[index] + one_total[index, mine].astype(jnp.float32)
         result[mine] = total.astype(jnp.bfloat16)
-        total = sum_other[index].astype(jnp.float32) + two_total[index, other].astype(jnp.float32)
+        total = sum_other[index].astype(jnp.float32) + one_total[index, other].astype(jnp.float32)
         result[other] = total.astype(jnp.bfloat16)
 
 
@@ -465,27 +462,23 @@
         [rows_of(width, half), stat, stat, rows_of(tokens, half), chip_pair],
         (first, query_head, grad_head, back_one, grad_rows, near_max, near_total, near_out),
     )
-    one_total = shifted(one_part, "seq", -1)
-    two_grad, part_mine, *part_sends = call(
+    one_other = swapped(one_part, "head")
+    two_grad, two_part = call(
         two_backward_kernel,
         "two_backward",
-        [rows_of(tokens, half), half_pair, half_block, half_block],
+        [rows_of(tokens, half), chip_pair],
         (query_head, grad_head, near_weights, near_prob_grad, near_factor, row_delta),
     )
-    (two_part,) = call(
-        join_two_kernel,
-        "join_two",
-        [whole_pair],
-        (part_mine, *[swapped(send, "head") for send in part_sends]),
-    )
     two_total = shifted(two_part, "seq", -2)
+    (joined,) = call(join_one_kernel, "join_one", [whole_pair], (one_part, one_other))
+    one_total = shifted(joined, "seq", -1)
     own_grad, own_part = call(
         own_backward_kernel,
         "own_backward",
         [rows_of(tokens, half), (chip_pair[0], full)],
         (
             query_head, grad_head, own_weights, own_prob_grad, near_factor, own_factor, row_delta,
-            two_part,
+            joined,
         ),
     )
     out_mine, query_mine, *sends = call(
@@ -502,13 +495,13 @@
         (out_mine, query_mine, *[swapped(send, "head") for send in sends]),
     )
     sum_mine, sum_send = call(
-        own_sum_kernel, "own_sum", [(half_pair[0], full), half_pair], (own_part, one_total)
+        own_sum_kernel, "own_sum", [(half_pair[0], full), half_pair], (own_part, two_total)
     )
     key_grad, value_grad = call(
         final_kernel,
         "total",
         [(key_matrix.shape, half)] * 2,
-        (sum_mine, swapped(sum_send, "head"), two_total, token),
+        (sum_mine, swapped(sum_send, "head"), one_total, token),
     )
     return (attn_out, query_grad, key_grad, value_grad)
 

time: 34.6 us -> 38.8 us (1.12)
  waiting for transfers between devices: 6.59 us -> 11.6 us
  starting transfers between devices: 17.6 us -> 16.8 us
    ppermute x4, waiting for transfers between devices: 2.45 us -> 8.86 us  [shifted(): return lax.ppermute(block, axis, route)]
    ppermute x13 -> x12, waiting for transfers between devices: 4.14 us -> 2.74 us  [swapped(): return lax.ppermute(block, axis, [(i, count - 1 - i) for i in range(count)])]
    ppermute x13 -> x12, starting transfers between devices: 3.5 us -> 2.92 us  [swapped(): return lax.ppermute(block, axis, [(i, count - 1 - i) for i in range(count)])]
  transfers between devices with their start and end apart: 17 -> 16, of which waited for: 10 -> 9; matrix products, arithmetic and copies ran while one was open for 0% -> 0% of each run, Pallas kernels for 16% -> 14%
where the time goes in v19:
time: 38.8 us; the launch traced here: 38.6 us
  starting transfers between devices  16.8 us (43%)
  waiting for transfers between devices  11.6 us (30%)
  Pallas kernels  7.67 us (20%)
  between operations  1.47 us (4%)
  other arithmetic  1.05 us (3%)
    ppermute x4, starting transfers between devices, shifted(): return lax.ppermute(block, axis, route)  13.9 us
    ppermute x4, waiting for transfers between devices, shifted(): return lax.ppermute(block, axis, route)  8.86 us
    pallas_call x14, Pallas kernels, call(): pl.pallas_call(kernel, out_shape=tuple((jax.ShapeDtypeStruct(shape, kind)...  7.67 us
    ppermute x12, starting transfers between devices, swapped(): return lax.ppermute(block, axis, [(i, count - 1 - i) for i in range(count)])  2.92 us
    ppermute x12, waiting for transfers between devices, swapped(): return lax.ppermute(block, axis, [(i, count - 1 - i) for i in range(count)])  2.74 us
    another operation x1, other arithmetic, shards(): own = jnp.stack([key_matrix, value_matrix])  1.05 us
  transfers between devices with their start and end apart: 16, of which 9 were waited for; matrix products, arithmetic and copies ran while one was open for 0% of the time, Pallas kernels for 14%

profile of v19, /device:TPU:0, one launch (start us, length us, event | category | flops | bytes accessed | tf_op | source)
XLA Modules:
  0.0 38.6 jit_solution(6690878042830405267)
XLA Ops:
  0.6 1.1 %pad_maximum_fusion.block.own.after = bf16[2,8,64,128]{3,2,1,0:T(8,128)(2,1)S(1)} fusion(bf16[1,8,64,128]{3,2,1,0:T(8,128)(2,1)} %bitcast.2, bf16[1,8,64,128]{3,2,1,0:T(8,128)(2,1)} %bitcast.3), kind=kLoop, calls=%fused_computation | loop fusion | flops 131072 | bytes 524288 | tf_op jit(solution)/shard_map/stack | solution.py:420
  1.7 3.0 %collective-permute-start.3 = (bf16[2,8,64,128]{3,2,1,0:T(8,128)(2,1)S(1)}, bf16[2,8,64,128]{3,2,1,0:T(8,128)(2,1)S(1)}, u32[]{:S(2)}, u32[]{:S(2)}) collective-permute-start(bf16[2,8,64,128]{3,2,1,0:T(8,128)(2,1)S(1)} %pad_maximum_fusion.block.own.after), channel_id=1, source_target_pairs={{0,2},{1,3},{2,4},{3,5},{4,6},{5,7},{6,8},{7,9},{8,10},{9,11},{10,... | collective-permute-start | bytes 786440 | tf_op jit(solution)/shard_map/ppermute | solution.py:19
  4.8 0.5 %collective-permute-start.1 = (bf16[4,64,128]{2,1,0:T(8,128)(2,1)S(1)}, bf16[4,64,128]{2,1,0:T(8,128)(2,1)S(1)}, u32[]{:S(2)}, u32[]{:S(2)}) collective-permute-start(bf16[4,64,128]{2,1,0:T(8,128)(2,1)S(1)} %get-tuple-element.52), channel_id=1, source_target_pairs={{0,16},{16,0},{1,17},{17,1},{2,18},{18,2},{3,19},{19,3},{4,20},{20... | collective-permute-start | bytes 196616 | tf_op jit(solution)/shard_map/ppermute | solution.py:24
  5.3 0.7 %collective-permute-done.other_keys = bf16[4,64,128]{2,1,0:T(8,128)(2,1)S(1)} collective-permute-done((bf16[4,64,128]{2,1,0:T(8,128)(2,1)S(1)}, bf16[4,64,128]{2,1,0:T(8,128)(2,1)S(1)}, u32[]{:S(2)}, u32[]{:S(2)}) %collective-permute-start) | collective-permute-done | bytes 65568 | tf_op jit(solution)/shard_map/ppermute | solution.py:24
  6.2 3.4 %collective-permute-start.2 = (bf16[2,4,128,128]{3,2,1,0:T(8,128)(2,1)S(1)}, bf16[2,4,128,128]{3,2,1,0:T(8,128)(2,1)S(1)}, u32[]{:S(2)}, u32[]{:S(2)}) collective-permute-start(bf16[2,4,128,128]{3,2,1,0:T(8,128)(2,1)S(1)} %join_own.1.own), channel_id=1, source_target_pairs={{0,1},{1,2},{2,3},{3,4},{4,5},{5,6},{6,7},{7,8},{8,9},{9,10},{10,1... | collective-permute-start | bytes 786440 | tf_op jit(solution)/shard_map/ppermute | solution.py:19
  9.9 0.4 %collective-permute-start.6 = (bf16[11,64,128]{2,1,0:T(8,128)(2,1)S(1)}, bf16[11,64,128]{2,1,0:T(8,128)(2,1)S(1)}, u32[]{:S(2)}, u32[]{:S(2)}) collective-permute-start(bf16[11,64,128]{2,1,0:T(8,128)(2,1)S(1)} %get-tuple-element.55), channel_id=1, source_target_pairs={{0,16},{16,0},{1,17},{17,1},{2,18},{18,2},{3,19},{19,3},{4,20},{20... | collective-permute-start | bytes 540680 | tf_op jit(solution)/shard_map/ppermute | solution.py:24
  11.0 0.7 %collective-permute-done.4.first_third = bf16[10,64,128]{2,1,0:T(8,128)(2,1)S(1)} collective-permute-done((bf16[10,64,128]{2,1,0:T(8,128)(2,1)S(1)}, bf16[10,64,128]{2,1,0:T(8,128)(2,1)S(1)}, u32[]{:S(2)}, u32[]{:S(2)}) %collective-permute-start.4) | collective-permute-done | bytes 163872 | tf_op jit(solution)/shard_map/ppermute | solution.py:24
  11.7 1.5 %own_block.1 = (bf16[16,128,128]{2,1,0:T(8,128)(2,1)S(1)}, bf16[16,128,128]{2,1,0:T(8,128)(2,1)S(1)}, bf16[8,128,256]{2,1,0:T(8,128)(2,1)S(1)}, s32[8,1,256]{2,1...) custom-call(s32[32]{0:T(128)S(1)} %copy-done.2, ...), custom_call_target="tpu_custom_call" | custom-call | flops 1 | tf_op jit(solution)/shard_map/own_block/pallas_call | solution.py:397
  13.3 0.8 %collective-permute-done.3.block.back_two = bf16[2,8,64,128]{3,2,1,0:T(8,128)(2,1)S(1)} collective-permute-done((bf16[2,8,64,128]{3,2,1,0:T(8,128)(2,1)S(1)}, bf16[2,8,64,128]{3,2,1,0:T(8,128)(2,1)S(1)}, u32[]{:S(2)}, u32[]{:S(2)}) %collective-permute-start.3) | collective-permute-done | bytes 262176 | tf_op jit(solution)/shard_map/ppermute | solution.py:19
  14.2 0.5 %collective-permute-start.8 = (bf16[4,64,128]{2,1,0:T(8,128)(2,1)S(1)}, bf16[4,64,128]{2,1,0:T(8,128)(2,1)S(1)}, u32[]{:S(2)}, u32[]{:S(2)}) collective-permute-start(bf16[4,64,128]{2,1,0:T(8,128)(2,1)S(1)} %get-tuple-element.62), channel_id=1, source_target_pairs={{0,16},{16,0},{1,17},{17,1},{2,18},{18,2},{3,19},{19,3},{4,20},{20... | collective-permute-start | bytes 196616 | tf_op jit(solution)/shard_map/ppermute | solution.py:24
  14.7 0.7 %collective-permute-done.7.two_keys = bf16[4,64,128]{2,1,0:T(8,128)(2,1)S(1)} collective-permute-done((bf16[4,64,128]{2,1,0:T(8,128)(2,1)S(1)}, bf16[4,64,128]{2,1,0:T(8,128)(2,1)S(1)}, u32[]{:S(2)}, u32[]{:S(2)}) %collective-permute-start.7) | collective-permute-done | bytes 65568 | tf_op jit(solution)/shard_map/ppermute | solution.py:24
  15.6 0.9 %near_forward.1 = (f32[8,1,256]{2,1,0:T(1,128)S(1)}, f32[8,1,256]{2,1,0:T(1,128)S(1)}, f32[8,128,256]{2,1,0:T(8,128)S(1)}, f32[8,128,256]{2,1,0:T(8,128)S(1)}, f...) custom-call(s32[8,1,256]{2,1,0:T(1,128)S(1)} %get-tuple-element.57.first, ...), custom_call_target="tpu_custom_call" | custom-call | flops 1 | tf_op jit(solution)/shard_map/near_forward/pallas_call | solution.py:397
  16.5 1.5 %last_forward_backward.1 = (bf16[8,128,256]{2,1,0:T(8,128)(2,1)S(1)}, f32[8,1,256]{2,1,0:T(1,128)S(1)}, f32[8,1,256]{2,1,0:T(1,128)S(1)}, bf16[8,128,256]{2,1,0:T(8,128)(2,1)S(1)}, bf16[2,4,128,128]{3,2,1,0:T(8,128)(2,1)S(1)}) custom-call(s32[8,1,256]{2,1,0:T(1,128)S(1)} %get-tuple-element.57.first, bf16[16,128,128]{2,1,0:T(8,128)(2,1)S(1)} %get-tuple-element.58.query_head, ...), custom_call_target="tpu_custom_call" | custom-call | flops 1 | tf_op jit(solution)/shard_map/last_forward_backward/pallas_call | solution.py:397
  18.1 0.4 %collective-permute-start.9 = (bf16[2,4,128,128]{3,2,1,0:T(8,128)(2,1)S(1)}, bf16[2,4,128,128]{3,2,1,0:T(8,128)(2,1)S(1)}, u32[]{:S(2)}, u32[]{:S(2)}) collective-permute-start(bf16[2,4,128,128]{3,2,1,0:T(8,128)(2,1)S(1)} %get-tuple-element.82.one_part), channel_id=1, source_target_pairs={{0,16},{16,0},{1,17},{17,1},{2,18},{18,2},{3,19},{19,3},{4,20},{20... | collective-permute-start | bytes 786440 | tf_op jit(solution)/shard_map/ppermute | solution.py:24
  18.5 0.5 %two_backward.1 = (bf16[8,128,256]{2,1,0:T(8,128)(2,1)S(1)}, bf16[2,4,128,128]{3,2,1,0:T(8,128)(2,1)S(1)}) custom-call(bf16[16,128,128]{2,1,0:T(8,128)(2,1)S(1)} %get-tuple-element.58.query_head, bf16[16,128,128]{2,1,0:T(8,128)(2,1)S(1)} %get-tuple-element.59.grad_head, f32[8,128,256]{2,1,0:T(8,128)S(1)} %get-tuple-element.73.near_weights, ...), custom_call_target="tpu_custom_call" | custom-call | flops 1 | tf_op jit(solution)/shard_map/two_backward/pallas_call | solution.py:397
  19.0 7.4 %collective-permute-start.13 = (bf16[2,4,128,128]{3,2,1,0:T(8,128)(2,1)S(1)}, bf16[2,4,128,128]{3,2,1,0:T(8,128)(2,1)S(1)}, u32[]{:S(2)}, u32[]{:S(2)}) collective-permute-start(bf16[2,4,128,128]{3,2,1,0:T(8,128)(2,1)S(1)} %get-tuple-element.92), channel_id=1, source_target_pairs={{0,14},{1,15},{2,0},{3,1},{4,2},{5,3},{6,4},{7,5},{8,6},{9,7},{10,... | collective-permute-start | bytes 786440 | tf_op jit(solution)/shard_map/ppermute | solution.py:19
  26.5 0.5 %own_backward.1 = (bf16[8,128,256]{2,1,0:T(8,128)(2,1)S(1)}, f32[2,4,128,128]{3,2,1,0:T(8,128)S(1)}) custom-call(bf16[16,128,128]{2,1,0:T(8,128)(2,1)S(1)} %get-tuple-element.58.query_head, bf16[16,128,128]{2,1,0:T(8,128)(2,1)S(1)} %get-tuple-element.59.grad_head, f32[8,128,256]{2,1,0:T(8,128)S(1)} %get-tuple-element.79.own_weights, ...), custom_call_target="tpu_custom_call" | custom-call | flops 1 | tf_op jit(solution)/shard_map/own_backward/pallas_call | solution.py:397
  27.0 0.8 %query_grad.1 = (bf16[16,64,128]{2,1,0:T(8,128)(2,1)S(1)}, bf16[16,64,128]{2,1,0:T(8,128)(2,1)S(1)}, bf16[10,64,128]{2,1,0:T(8,128)(2,1)S(1)}, bf16[11,64,128]{2,1,0:T(8,128)(2,1)S(1)}, bf16[11,64,128]{2,1,0:T(8,128)(2,1)S(1)}) custom-call(bf16[2,4,128,128]{3,2,1,0:T(8,128)(2,1)S(1)} %join_own.1.own, ...), custom_call_target="tpu_custom_call" | custom-call | flops 1 | tf_op jit(solution)/shard_map/query_grad/pallas_call | solution.py:397
  27.8 0.5 %collective-permute-start.12 = (bf16[11,64,128]{2,1,0:T(8,128)(2,1)S(1)}, bf16[11,64,128]{2,1,0:T(8,128)(2,1)S(1)}, u32[]{:S(2)}, u32[]{:S(2)}) collective-permute-start(bf16[11,64,128]{2,1,0:T(8,128)(2,1)S(1)} %get-tuple-element.88), channel_id=1, source_target_pairs={{0,16},{16,0},{1,17},{17,1},{2,18},{18,2},{3,19},{19,3},{4,20},{20... | collective-permute-start | bytes 540680 | tf_op jit(solution)/shard_map/ppermute | solution.py:24
  28.4 4.7 %collective-permute-done.13.two_total = bf16[2,4,128,128]{3,2,1,0:T(8,128)(2,1)S(1)} collective-permute-done((bf16[2,4,128,128]{3,2,1,0:T(8,128)(2,1)S(1)}, bf16[2,4,128,128]{3,2,1,0:T(8,128)(2,1)S(1)}, u32[]{:S(2)}, u32[]{:S(2)}) %collective-permute-start.13) | collective-permute-done | bytes 262176 | tf_op jit(solution)/shard_map/ppermute | solution.py:19
  33.2 1.0 %assemble.1 = (bf16[32,64,128]{2,1,0:T(8,128)(2,1)}, bf16[32,64,128]{2,1,0:T(8,128)(2,1)}, f32[8,128]{1,0:T(8,128)S(1)}) custom-call(bf16[16,64,128]{2,1,0:T(8,128)(2,1)S(1)} %get-tuple-element.84.out_mine, bf16[16,64,128]{2,1,0:T(8,128)(2,1)S(1)} %get-tuple-element.85.query_mine, bf16[10,64,128]{2,1,0:T(8,128)(2,1)S(1)} %collective-permute-done.10.first_third, ...), custom_call_target="tpu_custom_call" | custom-call | flops 1 | tf_op jit(solution)/shard_map/assemble/pallas_call | solution.py:397
  34.3 0.3 collective-permute-done.14.sum_other
  34.5 3.4 %collective-permute-done.15.one_total = bf16[2,8,64,128]{3,2,1,0:T(8,128)(2,1)S(1)} collective-permute-done((bf16[2,8,64,128]{3,2,1,0:T(8,128)(2,1)S(1)}, bf16[2,8,64,128]{3,2,1,0:T(8,128)(2,1)S(1)}, u32[]{:S(2)}, u32[]{:S(2)}) %collective-permute-start.15) | collective-permute-done | bytes 262176 | tf_op jit(solution)/shard_map/ppermute | solution.py:19
  37.9 0.7 %total.1 = (bf16[8,64,128]{2,1,0:T(8,128)(2,1)}, bf16[8,64,128]{2,1,0:T(8,128)(2,1)}) custom-call(f32[2,4,64,128]{3,2,1,0:T(8,128)S(1)} %get-tuple-element.93.sum_mine, bf16[2,4,64,128]{3,2,1,0:T(8,128)(2,1)S(1)} %collective-permute-done.14.sum_other, bf16[2,8,64,128]{3,2,1,0:T(8,128)(2,1)S(1)} %collective-permute-done.15.one_total, ...), custom_call_target="tpu_custom_call" | custom-call | flops 1 | tf_op jit(solution)/shard_map/total/pallas_call | solution.py:397
  (29 shorter events, 1.2 us)
Async XLA Ops:
  0.6 9.0 %copy-start.1 = (bf16[32,64,128]{2,1,0:T(8,128)(2,1)S(1)}, bf16[32,64,128]{2,1,0:T(8,128)(2,1)}, u32[]{:S(2)}) copy-start(bf16[32,64,128]{2,1,0:T(8,128)(2,1)} %grads.3) | copy-start | bytes 1572868
  1.7 8.0 %copy-start = (bf16[32,64,128]{2,1,0:T(8,128)(2,1)S(1)}, bf16[32,64,128]{2,1,0:T(8,128)(2,1)}, u32[]{:S(2)}) copy-start(bf16[32,64,128]{2,1,0:T(8,128)(2,1)} %queries.3) | copy-start | bytes 1572868
  1.7 12.4 %collective-permute-start.3 = (bf16[2,8,64,128]{3,2,1,0:T(8,128)(2,1)S(1)}, bf16[2,8,64,128]{3,2,1,0:T(8,128)(2,1)S(1)}, u32[]{:S(2)}, u32[]{:S(2)}) collective-permute-start(bf16[2,8,64,128]{3,2,1,0:T(8,128)(2,1)S(1)} %pad_maximum_fusion.block.own.after), channel_id=1, source_target_pairs={{0,2},{1,3},{2,4},{3,5},{4,6},{5,7},{6,8},{7,9},{8,10},{9,11},{10,... | collective-permute-start | bytes 786440 | tf_op jit(solution)/shard_map/ppermute | solution.py:19
  4.7 1.3 %collective-permute-start = (bf16[4,64,128]{2,1,0:T(8,128)(2,1)S(1)}, bf16[4,64,128]{2,1,0:T(8,128)(2,1)S(1)}, u32[]{:S(2)}, u32[]{:S(2)}) collective-permute-start(bf16[4,64,128]{2,1,0:T(8,128)(2,1)S(1)} %get-tuple-element.51), channel_id=1, source_target_pairs={{0,16},{16,0},{1,17},{17,1},{2,18},{18,2},{3,19},{19,3},{4,20},{20... | collective-permute-start | bytes 196616 | tf_op jit(solution)/shard_map/ppermute | solution.py:24
  4.8 1.4 %collective-permute-start.1 = (bf16[4,64,128]{2,1,0:T(8,128)(2,1)S(1)}, bf16[4,64,128]{2,1,0:T(8,128)(2,1)S(1)}, u32[]{:S(2)}, u32[]{:S(2)}) collective-permute-start(bf16[4,64,128]{2,1,0:T(8,128)(2,1)S(1)} %get-tuple-element.52), channel_id=1, source_target_pairs={{0,16},{16,0},{1,17},{17,1},{2,18},{18,2},{3,19},{19,3},{4,20},{20... | collective-permute-start | bytes 196616 | tf_op jit(solution)/shard_map/ppermute | solution.py:24
  6.2 10.3 %collective-permute-start.2 = (bf16[2,4,128,128]{3,2,1,0:T(8,128)(2,1)S(1)}, bf16[2,4,128,128]{3,2,1,0:T(8,128)(2,1)S(1)}, u32[]{:S(2)}, u32[]{:S(2)}) collective-permute-start(bf16[2,4,128,128]{3,2,1,0:T(8,128)(2,1)S(1)} %join_own.1.own), channel_id=1, source_target_pairs={{0,1},{1,2},{2,3},{3,4},{4,5},{5,6},{6,7},{7,8},{8,9},{9,10},{10,1... | collective-permute-start | bytes 786440 | tf_op jit(solution)/shard_map/ppermute | solution.py:19
  9.7 2.0 %collective-permute-start.5 = (bf16[11,64,128]{2,1,0:T(8,128)(2,1)S(1)}, bf16[11,64,128]{2,1,0:T(8,128)(2,1)S(1)}, u32[]{:S(2)}, u32[]{:S(2)}) collective-permute-start(bf16[11,64,128]{2,1,0:T(8,128)(2,1)S(1)} %get-tuple-element.54), channel_id=1, source_target_pairs={{0,16},{16,0},{1,17},{17,1},{2,18},{18,2},{3,19},{19,3},{4,20},{20... | collective-permute-start | bytes 540680 | tf_op jit(solution)/shard_map/ppermute | solution.py:24
  9.9 1.8 %collective-permute-start.6 = (bf16[11,64,128]{2,1,0:T(8,128)(2,1)S(1)}, bf16[11,64,128]{2,1,0:T(8,128)(2,1)S(1)}, u32[]{:S(2)}, u32[]{:S(2)}) collective-permute-start(bf16[11,64,128]{2,1,0:T(8,128)(2,1)S(1)} %get-tuple-element.55), channel_id=1, source_target_pairs={{0,16},{16,0},{1,17},{17,1},{2,18},{18,2},{3,19},{19,3},{4,20},{20... | collective-permute-start | bytes 540680 | tf_op jit(solution)/shard_map/ppermute | solution.py:24
  10.3 1.4 %copy-start.2 = (s32[32]{0:T(128)S(1)}, s32[32]{0:T(128)}, u32[]{:S(2)}) copy-start(s32[32]{0:T(128)} %spans.1) | copy-start | bytes 388
  10.3 1.4 %collective-permute-start.4 = (bf16[10,64,128]{2,1,0:T(8,128)(2,1)S(1)}, bf16[10,64,128]{2,1,0:T(8,128)(2,1)S(1)}, u32[]{:S(2)}, u32[]{:S(2)}) collective-permute-start(bf16[10,64,128]{2,1,0:T(8,128)(2,1)S(1)} %get-tuple-element.53), channel_id=1, source_target_pairs={{0,16},{16,0},{1,17},{17,1},{2,18},{18,2},{3,19},{19,3},{4,20},{20... | collective-permute-start | bytes 491528 | tf_op jit(solution)/shard_map/ppermute | solution.py:24
  14.1 1.3 %collective-permute-start.7 = (bf16[4,64,128]{2,1,0:T(8,128)(2,1)S(1)}, bf16[4,64,128]{2,1,0:T(8,128)(2,1)S(1)}, u32[]{:S(2)}, u32[]{:S(2)}) collective-permute-start(bf16[4,64,128]{2,1,0:T(8,128)(2,1)S(1)} %get-tuple-element.61), channel_id=1, source_target_pairs={{0,16},{16,0},{1,17},{17,1},{2,18},{18,2},{3,19},{19,3},{4,20},{20... | collective-permute-start | bytes 196616 | tf_op jit(solution)/shard_map/ppermute | solution.py:24
  14.2 1.4 %collective-permute-start.8 = (bf16[4,64,128]{2,1,0:T(8,128)(2,1)S(1)}, bf16[4,64,128]{2,1,0:T(8,128)(2,1)S(1)}, u32[]{:S(2)}, u32[]{:S(2)}) collective-permute-start(bf16[4,64,128]{2,1,0:T(8,128)(2,1)S(1)} %get-tuple-element.62), channel_id=1, source_target_pairs={{0,16},{16,0},{1,17},{17,1},{2,18},{18,2},{3,19},{19,3},{4,20},{20... | collective-permute-start | bytes 196616 | tf_op jit(solution)/shard_map/ppermute | solution.py:24
  18.1 8.3 %collective-permute-start.9 = (bf16[2,4,128,128]{3,2,1,0:T(8,128)(2,1)S(1)}, bf16[2,4,128,128]{3,2,1,0:T(8,128)(2,1)S(1)}, u32[]{:S(2)}, u32[]{:S(2)}) collective-permute-start(bf16[2,4,128,128]{3,2,1,0:T(8,128)(2,1)S(1)} %get-tuple-element.82.one_part), channel_id=1, source_target_pairs={{0,16},{16,0},{1,17},{17,1},{2,18},{18,2},{3,19},{19,3},{4,20},{20... | collective-permute-start | bytes 786440 | tf_op jit(solution)/shard_map/ppermute | solution.py:24
  19.0 14.1 %collective-permute-start.13 = (bf16[2,4,128,128]{3,2,1,0:T(8,128)(2,1)S(1)}, bf16[2,4,128,128]{3,2,1,0:T(8,128)(2,1)S(1)}, u32[]{:S(2)}, u32[]{:S(2)}) collective-permute-start(bf16[2,4,128,128]{3,2,1,0:T(8,128)(2,1)S(1)} %get-tuple-element.92), channel_id=1, source_target_pairs={{0,14},{1,15},{2,0},{3,1},{4,2},{5,3},{6,4},{7,5},{8,6},{9,7},{10,... | collective-permute-start | bytes 786440 | tf_op jit(solution)/shard_map/ppermute | solution.py:19
  26.4 11.5 %collective-permute-start.15 = (bf16[2,8,64,128]{3,2,1,0:T(8,128)(2,1)S(1)}, bf16[2,8,64,128]{3,2,1,0:T(8,128)(2,1)S(1)}, u32[]{:S(2)}, u32[]{:S(2)}) collective-permute-start(bf16[2,8,64,128]{3,2,1,0:T(8,128)(2,1)S(1)} %join_one.1.after), channel_id=1, source_target_pairs={{0,15},{1,0},{2,1},{3,2},{4,3},{5,4},{6,5},{7,6},{8,7},{9,8},{10,9... | collective-permute-start | bytes 786440 | tf_op jit(solution)/shard_map/ppermute | solution.py:19
  27.7 5.5 %collective-permute-start.11 = (bf16[11,64,128]{2,1,0:T(8,128)(2,1)S(1)}, bf16[11,64,128]{2,1,0:T(8,128)(2,1)S(1)}, u32[]{:S(2)}, u32[]{:S(2)}) collective-permute-start(bf16[11,64,128]{2,1,0:T(8,128)(2,1)S(1)} %get-tuple-element.87), channel_id=1, source_target_pairs={{0,16},{16,0},{1,17},{17,1},{2,18},{18,2},{3,19},{19,3},{4,20},{20... | collective-permute-start | bytes 540680 | tf_op jit(solution)/shard_map/ppermute | solution.py:24
  27.8 5.4 %collective-permute-start.12 = (bf16[11,64,128]{2,1,0:T(8,128)(2,1)S(1)}, bf16[11,64,128]{2,1,0:T(8,128)(2,1)S(1)}, u32[]{:S(2)}, u32[]{:S(2)}) collective-permute-start(bf16[11,64,128]{2,1,0:T(8,128)(2,1)S(1)} %get-tuple-element.88), channel_id=1, source_target_pairs={{0,16},{16,0},{1,17},{17,1},{2,18},{18,2},{3,19},{19,3},{4,20},{20... | collective-permute-start | bytes 540680 | tf_op jit(solution)/shard_map/ppermute | solution.py:24
  28.3 4.9 %collective-permute-start.10 = (bf16[10,64,128]{2,1,0:T(8,128)(2,1)S(1)}, bf16[10,64,128]{2,1,0:T(8,128)(2,1)S(1)}, u32[]{:S(2)}, u32[]{:S(2)}) collective-permute-start(bf16[10,64,128]{2,1,0:T(8,128)(2,1)S(1)} %get-tuple-element.86), channel_id=1, source_target_pairs={{0,16},{16,0},{1,17},{17,1},{2,18},{18,2},{3,19},{19,3},{4,20},{20... | collective-permute-start | bytes 491528 | tf_op jit(solution)/shard_map/ppermute | solution.py:24
  33.1 1.4 %collective-permute-start.14 = (bf16[2,4,64,128]{3,2,1,0:T(8,128)(2,1)S(1)}, bf16[2,4,64,128]{3,2,1,0:T(8,128)(2,1)S(1)}, u32[]{:S(2)}, u32[]{:S(2)}) collective-permute-start(bf16[2,4,64,128]{3,2,1,0:T(8,128)(2,1)S(1)} %get-tuple-element.94), channel_id=1, source_target_pairs={{0,16},{16,0},{1,17},{17,1},{2,18},{18,2},{3,19},{19,3},{4,20},{20... | collective-permute-start | bytes 393224 | tf_op jit(solution)/shard_map/ppermute | solution.py:24

commit v20 on v17

--- a/solution.py
+++ b/solution.py
@@ -111,45 +111,43 @@
         taken += count
 
 
-def join_own_kernel(own, other_keys, other_values, *halves):
+def split_rows_kernel(queries, grads, after, *sends):
+    heads = queries.shape[0] // 2
+    start = (1 - lax.axis_index("head")) * heads
+    for index, row, piece, count in placed(sends, heads):
+        piece[...] = (queries, grads)[index][pl.ds(start + row, count)]
+
+
+def join_own_kernel(own, other_keys, other_values, own_head):
     groups, length = other_keys.shape[:2]
-    part = halves[0].shape[1]
-    start = lax.axis_index("head") * groups
-    for place, target in enumerate(halves):
-        target[:, :, pl.ds(0, length)] = own[:, pl.ds(start + place * part, part)]
-        for index, other in enumerate((other_keys, other_values)):
-            target[index, :, pl.ds(length, length)] = other[pl.ds(place * part, part)]
+    own_head[:, :, pl.ds(0, length)] = own[:, my_heads(groups)]
+    own_head[0, :, pl.ds(length, length)] = other_keys[...]
+    own_head[1, :, pl.ds(length, length)] = other_values[...]
 
 
 def own_kernel(
-    spans, offset, queries, grads, queries_other, grads_other, first_half, second_half,
+    spans, offset, queries, grads, first_third, second_third, last_third, own,
     query_head, grad_head, grad_rows, first, own_max, own_total, own_out, own_weights,
     own_prob_grad,
 ):
     heads, _, width = query_head.shape
     length = queries.shape[1]
-    part = first_half.shape[1]
-    groups = 2 * part
+    groups = own.shape[1]
     chunks = first.shape[0]
     count = heads // chunks
-    mine = my_heads(heads)
-    query_head[:, pl.ds(0, length)] = queries[mine]
-    query_head[:, pl.ds(length, length)] = queries_other[mine]
-    grad_head[:, pl.ds(0, length)] = grads[mine]
-    grad_head[:, pl.ds(length, length)] = grads_other[mine]
-
-    def block(index, n):
-        g = n * groups // chunks
-        return (first_half, second_half)[g // part][index, g % part]
-
+    query_head[:, pl.ds(0, length)] = queries[my_heads(heads)]
+    grad_head[:, pl.ds(0, length)] = grads[my_heads(heads)]
+    for index, row, piece, rows in placed((first_third, second_third, last_third), heads):
+        (query_head, grad_head)[index][pl.ds(row, rows), pl.ds(length, length)] = piece[...]
     factor = width ** (-0.5) * math.log2(math.e)
     token = lane_tokens(count, length)
     for n, rows in enumerate(first_visible(spans, offset, chunks, count, length)):
         first[n] = rows
 
     def products(n):
-        own_prob_grad[n] = matmul(block(1, n), grouped(grad_head, n, count), (1, 1))
-        return (matmul(block(0, n), grouped(query_head, n, count), (1, 1)),)
+        g = n * groups // chunks
+        own_prob_grad[n] = matmul(own[1, g], grouped(grad_head, n, count), (1, 1))
+        return (matmul(own[0, g], grouped(query_head, n, count), (1, 1)),)
 
     def softmax(n, scores):
         scores = masked(scores * factor, first[n], 0, token)
@@ -161,7 +159,7 @@
         return (weights.astype(jnp.bfloat16),)
 
     def weigh(n, halves):
-        own_out[n] = matmul(block(1, n), halves, (0, 0))
+        own_out[n] = matmul(own[1, n * groups // chunks], halves, (0, 0))
         grad_rows[n] = grouped(grad_head, n, count).T
 
     pipelined(chunks, products, softmax, weigh)
@@ -212,7 +210,8 @@
     base, first, query_head, grad_head, back_one, grad_rows, near_max, near_total, near_out, after,
     attended_rows, row_delta, near_factor, one_grad, one_part,
 ):
-    groups = back_one.shape[1]
+    groups = one_part.shape[1]
+    g_base = base * back_one.shape[1] // first.shape[0]
     chunks = row_delta.shape[0]
     heads, _, width = query_head.shape
     count = heads // first.shape[0]
@@ -220,8 +219,8 @@
 
     def products(n):
         g = n * groups // chunks
-        scores = matmul(back_one[0, g], grouped(query_head, base + n, count), (1, 1))
-        prob_grad = matmul(back_one[1, g], grouped(grad_head, base + n, count), (1, 1))
+        scores = matmul(back_one[0, g_base + g], grouped(query_head, base + n, count), (1, 1))
+        prob_grad = matmul(back_one[1, g_base + g], grouped(grad_head, base + n, count), (1, 1))
         return scores, prob_grad
 
     def softmax(n, scores, prob_grad):
@@ -231,7 +230,7 @@
         rescale = jnp.exp2(near_max[base + n] - row_max)
         inverse = 1.0 / (near_total[base + n] * rescale + jnp.sum(weights, axis=0, keepdims=True))
         weighted = matmul(
-            back_one[1, n * groups // chunks], weights.astype(jnp.bfloat16), (0, 0)
+            back_one[1, g_base + n * groups // chunks], weights.astype(jnp.bfloat16), (0, 0)
         )
         near_factor[n] = rescale * inverse
         return prob_grad, weights, weighted, rescale, inverse
@@ -341,26 +340,27 @@
 
 
 def query_kernel(
-    own_a, own_b, one_a, one_b, rows_a, rows_b, grad_a, grad_b, back_two, two_keys, two_grad,
-    own_grad, after, out_mine, query_mine, first_third, second_third, last_third, query_send,
-):
-    part, chunks = own_a.shape[1], own_grad.shape[0]
+    own, back_one, back_two, two_keys, rows_a, rows_b, two_grad, grad_a, grad_b, own_grad, after,
+    out_mine, query_mine, first_third, second_third, last_third, query_send,
+):
+    sends = (first_third, second_third, last_third)
+    groups = own.shape[1]
+    chunks = own_grad.shape[0]
     heads, length, width = out_mine.shape
     count = heads // chunks
     for n in range(chunks):
-        g = n * 2 * part // chunks
-        own, one = ((own_a, one_a), (own_b, one_b))[g // part]
+        g = n * groups // chunks
         rows = pl.ds(n * count, count)
-        keys = join(two_back(back_two, (two_keys,), 0, g), one[0, g % part], own[0, g % part])
-        total = matmul(keys, join(two_grad[n], of_half(n, grad_a, grad_b), own_grad[n]), (0, 0))
-        total = (total * width ** (-0.5)).astype(jnp.bfloat16)
+        keys = join(two_back(back_two, (two_keys,), 0, g), back_one[0, g], own[0, g])
+        part = matmul(keys, join(two_grad[n], of_half(n, grad_a, grad_b), own_grad[n]), (0, 0))
+        part = (part * width ** (-0.5)).astype(jnp.bfloat16)
         for index, (columns, mine) in enumerate(
-            ((of_half(n, rows_a, rows_b), out_mine), (total, query_mine))
+            ((of_half(n, rows_a, rows_b), out_mine), (part, query_mine))
         ):
             block = columns.T.reshape(count, 2 * length, width)
             mine[rows] = block[:, :length]
             query_send[index, rows] = block[:, length:]
-    for index, row, piece, taken in placed((first_third, second_third, last_third), heads):
+    for index, row, piece, taken in placed(sends, heads):
         piece[...] = query_send[index, pl.ds(row, taken)]
 
 
@@ -434,25 +434,25 @@
     half_pair = ((2, groups_here, length, width), half)
     chip_pair = ((2, groups_here, tokens, width), half)
     half_rows = ((heads_here, length, width), half)
+    third_rows = [((rows, length, width), half) for rows in thirds(heads_here)]
+    chip_rows = ((heads_here, tokens, width), half)
     part, each = groups_here // 2, chunks // 2
     chip_half = ((2, part, tokens, width), half)
     half_stat = ((each, 1, lanes), full)
-    chip_rows = ((heads_here, tokens, width), half)
-
-    queries_other = swapped(query_matrix, "head")
-    grads_other = swapped(output_gradient, "head")
+
     own = jnp.stack([key_matrix, value_matrix])
     back_two = shifted(own, "seq", 2)
     own_sends = call(split_kernel, "split_own", [half_block] * 2, (own,))
-    own_halves = call(
-        join_own_kernel,
-        "join_own",
-        [chip_half] * 2,
-        (own, *[swapped(send, "head") for send in own_sends]),
-    )
-    back_one = [
-        shifted(block, "seq", 1, ring=index == 0) for index, block in enumerate(own_halves)
-    ]
+    (own_head,) = call(
+        join_own_kernel, "join_own", [chip_pair], (own, *[swapped(send, "head") for send in own_sends])
+    )
+    back_one = shifted(own_head, "seq", 1, ring=False)
+    sends = call(
+        split_rows_kernel,
+        "split_rows",
+        third_rows,
+        (query_matrix, output_gradient, own),
+    )
     (
         query_head, grad_head, grad_rows, first, own_max, own_total, own_out, own_weights,
         own_prob_grad,
@@ -465,7 +465,7 @@
         ],
         (
             query_head_spans, slab_offset, query_matrix, output_gradient,
-            queries_other, grads_other, *own_halves,
+            *[swapped(send, "head") for send in sends], own_head,
         ),
         scalars=2,
     )
@@ -478,10 +478,10 @@
         [stat, stat, rows_of(width, full), rows_of(tokens, full), rows_of(tokens, full), stat],
         (first, query_head, grad_head, back_two, *two_other, own_max, own_total, own_out),
     )
+    back_one, near_max = lax.optimization_barrier((back_one, near_max))
     after = near_max
     halves = []
     for index in range(2):
-        back_one[index], after = lax.optimization_barrier((back_one[index], after))
         rows, delta, factor, one_grad, one_part = call(
             functools.partial(last_kernel, index * each),
             "last_" + "ab"[index],
@@ -490,8 +490,8 @@
                 chip_half,
             ],
             (
-                first, query_head, grad_head, back_one[index], grad_rows, near_max, near_total,
-                near_out, after,
+                first, query_head, grad_head, back_one, grad_rows, near_max, near_total, near_out,
+                after,
             ),
         )
         halves.append((factor, delta, rows, one_grad, shifted(one_part, "seq", -1)))
@@ -528,10 +528,10 @@
     out_mine, query_mine, *sends = call(
         query_kernel,
         "query_grad",
-        [half_rows] * 2 + [((rows, length, width), half) for rows in thirds(heads_here)],
+        [half_rows] * 2 + third_rows,
         (
-            *own_halves, *back_one, halves[0][2], halves[1][2], halves[0][3], halves[1][3],
-            back_two, two_other[0], two_grad, own_grad, sum_token,
+            own_head, back_one, back_two, two_other[0], halves[0][2], halves[1][2], two_grad,
+            halves[0][3], halves[1][3], own_grad, sum_token,
         ),
         scratch=[pltpu.VMEM((2,) + half_rows[0], half)],
     )
@@ -542,10 +542,7 @@
         (out_mine, query_mine, *[swapped(send, "head") for send in sends]),
     )
     sum_mine, sum_send = call(
-        own_sum_kernel,
-        "sum_b",
-        [(half_pair[0], full), half_pair],
-        (own_part, first_sum, halves[1][4]),
+        own_sum_kernel, "own_sum", [(half_pair[0], full), half_pair], (own_part, first_sum, halves[1][4])
     )
     key_grad, value_grad = call(
         final_kernel,

time: 38.7 us -> 37.8 us (0.977)
  waiting for transfers between devices: 9.82 us -> 8.68 us
    ppermute x6 -> x5, waiting for transfers between devices: 7.74 us -> 5.94 us  [shifted(): return lax.ppermute(block, axis, route)]
    ppermute x12 -> x13, waiting for transfers between devices: 2.08 us -> 2.74 us  [swapped(): return lax.ppermute(block, axis, [(i, count - 1 - i) for i in range(count)])]
    ppermute x6 -> x5, starting transfers between devices: 15.2 us -> 15.4 us  [shifted(): return lax.ppermute(block, axis, route)]
    ppermute x12 -> x13, starting transfers between devices: 3.02 us -> 3.07 us  [swapped(): return lax.ppermute(block, axis, [(i, count - 1 - i) for i in range(count)])]
    pallas_call x15 -> x16, Pallas kernels: 7.94 us -> 7.97 us  [call(): pl.pallas_call(kernel, out_shape=tuple((jax.ShapeDtypeStruct(shape, kind)...]
  transfers between devices with their start and end apart: 18 -> 18, of which waited for: 8 -> 9; matrix products, arithmetic and copies ran while one was open for 3% -> 0% of each run, Pallas kernels for 19% -> 17%
where the time goes in v20:
time: 37.8 us; the launch traced here: 37.7 us
  starting transfers between devices  18.4 us (49%)
  waiting for transfers between devices  8.68 us (23%)
  Pallas kernels  7.97 us (21%)
  between operations  1.5 us (4%)
  other arithmetic  1.05 us (3%)
    ppermute x5, starting transfers between devices, shifted(): return lax.ppermute(block, axis, route)  15.4 us
    pallas_call x16, Pallas kernels, call(): pl.pallas_call(kernel, out_shape=tuple((jax.ShapeDtypeStruct(shape, kind)...  7.97 us
    ppermute x5, waiting for transfers between devices, shifted(): return lax.ppermute(block, axis, route)  5.94 us
    ppermute x13, starting transfers between devices, swapped(): return lax.ppermute(block, axis, [(i, count - 1 - i) for i in range(count)])  3.07 us
    ppermute x13, waiting for transfers between devices, swapped(): return lax.ppermute(block, axis, [(i, count - 1 - i) for i in range(count)])  2.74 us
    another operation x1, other arithmetic, shards(): own = jnp.stack([key_matrix, value_matrix])  1.05 us
  transfers between devices with their start and end apart: 18, of which 9 were waited for; matrix products, arithmetic and copies ran while one was open for 0% of the time, Pallas kernels for 17%

profile of v20, /device:TPU:0, one launch (start us, length us, event | category | flops | bytes accessed | tf_op | source)
XLA Modules:
  0.0 37.7 jit_solution(16391893668938454562)
XLA Ops:
  0.6 1.1 %pad_maximum_fusion.block.own.after = bf16[2,8,64,128]{3,2,1,0:T(8,128)(2,1)S(1)} fusion(bf16[1,8,64,128]{3,2,1,0:T(8,128)(2,1)} %bitcast.2, bf16[1,8,64,128]{3,2,1,0:T(8,128)(2,1)} %bitcast.3), kind=kLoop, calls=%fused_computation | loop fusion | flops 131072 | bytes 524288 | tf_op jit(solution)/shard_map/stack | solution.py:443
  1.7 3.0 %collective-permute-start.3 = (bf16[2,8,64,128]{3,2,1,0:T(8,128)(2,1)S(1)}, bf16[2,8,64,128]{3,2,1,0:T(8,128)(2,1)S(1)}, u32[]{:S(2)}, u32[]{:S(2)}) collective-permute-start(bf16[2,8,64,128]{3,2,1,0:T(8,128)(2,1)S(1)} %pad_maximum_fusion.block.own.after), channel_id=1, source_target_pairs={{0,2},{1,3},{2,4},{3,5},{4,6},{5,7},{6,8},{7,9},{8,10},{9,11},{10,... | collective-permute-start | bytes 786440 | tf_op jit(solution)/shard_map/ppermute | solution.py:20
  4.8 0.5 %collective-permute-start.1 = (bf16[4,64,128]{2,1,0:T(8,128)(2,1)S(1)}, bf16[4,64,128]{2,1,0:T(8,128)(2,1)S(1)}, u32[]{:S(2)}, u32[]{:S(2)}) collective-permute-start(bf16[4,64,128]{2,1,0:T(8,128)(2,1)S(1)} %get-tuple-element.61), channel_id=1, source_target_pairs={{0,16},{16,0},{1,17},{17,1},{2,18},{18,2},{3,19},{19,3},{4,20},{20... | collective-permute-start | bytes 196616 | tf_op jit(solution)/shard_map/ppermute | solution.py:25
  5.3 0.7 %collective-permute-done.other_keys = bf16[4,64,128]{2,1,0:T(8,128)(2,1)S(1)} collective-permute-done((bf16[4,64,128]{2,1,0:T(8,128)(2,1)S(1)}, bf16[4,64,128]{2,1,0:T(8,128)(2,1)S(1)}, u32[]{:S(2)}, u32[]{:S(2)}) %collective-permute-start) | collective-permute-done | bytes 65568 | tf_op jit(solution)/shard_map/ppermute | solution.py:25
  6.2 3.4 %collective-permute-start.2 = (bf16[2,4,128,128]{3,2,1,0:T(8,128)(2,1)S(1)}, bf16[2,4,128,128]{3,2,1,0:T(8,128)(2,1)S(1)}, u32[]{:S(2)}, u32[]{:S(2)}) collective-permute-start(bf16[2,4,128,128]{3,2,1,0:T(8,128)(2,1)S(1)} %join_own.1.own), channel_id=1, source_target_pairs={{0,1},{1,2},{2,3},{3,4},{4,5},{5,6},{6,7},{7,8},{8,9},{9,10},{10,1... | collective-permute-start | bytes 786440 | tf_op jit(solution)/shard_map/ppermute | solution.py:20
  11.0 0.7 %collective-permute-done.4.first_third = bf16[10,64,128]{2,1,0:T(8,128)(2,1)S(1)} collective-permute-done((bf16[10,64,128]{2,1,0:T(8,128)(2,1)S(1)}, bf16[10,64,128]{2,1,0:T(8,128)(2,1)S(1)}, u32[]{:S(2)}, u32[]{:S(2)}) %collective-permute-start.4) | collective-permute-done | bytes 163872 | tf_op jit(solution)/shard_map/ppermute | solution.py:25
  11.7 1.5 %own_block.1 = (bf16[16,128,128]{2,1,0:T(8,128)(2,1)S(1)}, bf16[16,128,128]{2,1,0:T(8,128)(2,1)S(1)}, bf16[8,128,256]{2,1,0:T(8,128)(2,1)S(1)}, s32[8,1,256]{2,1...) custom-call(s32[32]{0:T(128)S(1)} %copy-done.2, ...), custom_call_target="tpu_custom_call" | custom-call | flops 1 | tf_op jit(solution)/shard_map/own_block/pallas_call | solution.py:417
  13.3 0.8 %collective-permute-done.3.block.back_two = bf16[2,8,64,128]{3,2,1,0:T(8,128)(2,1)S(1)} collective-permute-done((bf16[2,8,64,128]{3,2,1,0:T(8,128)(2,1)S(1)}, bf16[2,8,64,128]{3,2,1,0:T(8,128)(2,1)S(1)}, u32[]{:S(2)}, u32[]{:S(2)}) %collective-permute-start.3) | collective-permute-done | bytes 262176 | tf_op jit(solution)/shard_map/ppermute | solution.py:20
  14.2 0.5 %collective-permute-start.8 = (bf16[4,64,128]{2,1,0:T(8,128)(2,1)S(1)}, bf16[4,64,128]{2,1,0:T(8,128)(2,1)S(1)}, u32[]{:S(2)}, u32[]{:S(2)}) collective-permute-start(bf16[4,64,128]{2,1,0:T(8,128)(2,1)S(1)} %get-tuple-element.71), channel_id=1, source_target_pairs={{0,16},{16,0},{1,17},{17,1},{2,18},{18,2},{3,19},{19,3},{4,20},{20... | collective-permute-start | bytes 196616 | tf_op jit(solution)/shard_map/ppermute | solution.py:25
  14.7 0.7 %collective-permute-done.7.two_keys = bf16[4,64,128]{2,1,0:T(8,128)(2,1)S(1)} collective-permute-done((bf16[4,64,128]{2,1,0:T(8,128)(2,1)S(1)}, bf16[4,64,128]{2,1,0:T(8,128)(2,1)S(1)}, u32[]{:S(2)}, u32[]{:S(2)}) %collective-permute-start.7) | collective-permute-done | bytes 65568 | tf_op jit(solution)/shard_map/ppermute | solution.py:25
  15.6 0.9 %near_forward.1 = (f32[8,1,256]{2,1,0:T(1,128)S(1)}, f32[8,1,256]{2,1,0:T(1,128)S(1)}, f32[8,128,256]{2,1,0:T(8,128)S(1)}, f32[8,128,256]{2,1,0:T(8,128)S(1)}, f...) custom-call(s32[8,1,256]{2,1,0:T(1,128)S(1)} %get-tuple-element.66.first, ...), custom_call_target="tpu_custom_call" | custom-call | flops 1 | tf_op jit(solution)/shard_map/near_forward/pallas_call | solution.py:417
  16.5 0.9 %last_a.1 = (bf16[4,128,256]{2,1,0:T(8,128)(2,1)S(1)}, f32[4,1,256]{2,1,0:T(1,128)S(1)}, f32[4,1,256]{2,1,0:T(1,128)S(1)}, bf16[4,128,256]{2,1,0:T(8,128)(2,1)S(1)}, bf16[2,2,128,128]{3,2,1,0:T(8,128)(2,1)S(1)}) custom-call(s32[8,1,256]{2,1,0:T(1,128)S(1)} %get-tuple-element.66.first, bf16[16,128,128]{2,1,0:T(8,128)(2,1)S(1)} %get-tuple-element.67.query_head, ...), custom_call_target="tpu_custom_call" | custom-call | flops 1 | tf_op jit(solution)/shard_map/last_a/pallas_call | solution.py:417
  17.4 4.4 %collective-permute-start.11 = (bf16[2,2,128,128]{3,2,1,0:T(8,128)(2,1)S(1)}, bf16[2,2,128,128]{3,2,1,0:T(8,128)(2,1)S(1)}, u32[]{:S(2)}, u32[]{:S(2)}) collective-permute-start(bf16[2,2,128,128]{3,2,1,0:T(8,128)(2,1)S(1)} %get-tuple-element.100), channel_id=1, source_target_pairs={{0,15},{1,0},{2,1},{3,2},{4,3},{5,4},{6,5},{7,6},{8,7},{9,8},{10,9... | collective-permute-start | bytes 393224 | tf_op jit(solution)/shard_map/ppermute | solution.py:20
  21.8 0.9 %last_b.1 = (bf16[4,128,256]{2,1,0:T(8,128)(2,1)S(1)}, f32[4,1,256]{2,1,0:T(1,128)S(1)}, f32[4,1,256]{2,1,0:T(1,128)S(1)}, bf16[4,128,256]{2,1,0:T(8,128)(2,1)S(1)}, bf16[2,2,128,128]{3,2,1,0:T(8,128)(2,1)S(1)}) custom-call(s32[8,1,256]{2,1,0:T(1,128)S(1)} %get-tuple-element.66.first, bf16[16,128,128]{2,1,0:T(8,128)(2,1)S(1)} %get-tuple-element.67.query_head, ...), custom_call_target="tpu_custom_call" | custom-call | flops 1 | tf_op jit(solution)/shard_map/last_b/pallas_call | solution.py:417
  22.7 0.5 %two_backward.1 = (bf16[8,128,256]{2,1,0:T(8,128)(2,1)S(1)}, bf16[2,4,64,128]{3,2,1,0:T(8,128)(2,1)S(1)}, bf16[4,64,128]{2,1,0:T(8,128)(2,1)S(1)}, bf16[4,64,128]{2,1,0:T(8,128)(2,1)S(1)}) custom-call(bf16[16,128,128]{2,1,0:T(8,128)(2,1)S(1)} %get-tuple-element.67.query_head, bf16[16,128,128]{2,1,0:T(8,128)(2,1)S(1)} %get-tuple-element.68.grad_head, ...), custom_call_target="tpu_custom_call" | custom-call | flops 1 | tf_op jit(solution)/shard_map/two_backward/pallas_call | solution.py:417
  23.3 0.5 %collective-permute-start.10 = (bf16[4,64,128]{2,1,0:T(8,128)(2,1)S(1)}, bf16[4,64,128]{2,1,0:T(8,128)(2,1)S(1)}, u32[]{:S(2)}, u32[]{:S(2)}) collective-permute-start(bf16[4,64,128]{2,1,0:T(8,128)(2,1)S(1)} %get-tuple-element.97), channel_id=1, source_target_pairs={{0,16},{16,0},{1,17},{17,1},{2,18},{18,2},{3,19},{19,3},{4,20},{20... | collective-permute-start | bytes 196616 | tf_op jit(solution)/shard_map/ppermute | solution.py:25
  23.8 4.5 %collective-permute-start.15 = (bf16[2,2,128,128]{3,2,1,0:T(8,128)(2,1)S(1)}, bf16[2,2,128,128]{3,2,1,0:T(8,128)(2,1)S(1)}, u32[]{:S(2)}, u32[]{:S(2)}) collective-permute-start(bf16[2,2,128,128]{3,2,1,0:T(8,128)(2,1)S(1)} %get-tuple-element.110), channel_id=1, source_target_pairs={{0,15},{1,0},{2,1},{3,2},{4,3},{5,4},{6,5},{7,6},{8,7},{9,8},{10,9... | collective-permute-start | bytes 393224 | tf_op jit(solution)/shard_map/ppermute | solution.py:20
  28.4 0.5 %own_backward.1 = (bf16[8,128,256]{2,1,0:T(8,128)(2,1)S(1)}, f32[2,4,128,128]{3,2,1,0:T(8,128)S(1)}) custom-call(bf16[16,128,128]{2,1,0:T(8,128)(2,1)S(1)} %get-tuple-element.67.query_head, bf16[16,128,128]{2,1,0:T(8,128)(2,1)S(1)} %get-tuple-element.68.grad_head, f32[8,128,256]{2,1,0:T(8,128)S(1)} %get-tuple-element.92.own_weights, ...), custom_call_target="tpu_custom_call" | custom-call | flops 1 | tf_op jit(solution)/shard_map/own_backward/pallas_call | solution.py:417
  28.9 0.8 %query_grad.1 = (bf16[16,64,128]{2,1,0:T(8,128)(2,1)S(1)}, bf16[16,64,128]{2,1,0:T(8,128)(2,1)S(1)}, bf16[10,64,128]{2,1,0:T(8,128)(2,1)S(1)}, bf16[11,64,128]{2,1,0:T(8,128)(2,1)S(1)}, bf16[11,64,128]{2,1,0:T(8,128)(2,1)S(1)}) custom-call(bf16[2,4,128,128]{3,2,1,0:T(8,128)(2,1)S(1)} %join_own.1.own, ...), custom_call_target="tpu_custom_call" | custom-call | flops 1 | tf_op jit(solution)/shard_map/query_grad/pallas_call | solution.py:417
  29.7 0.5 %collective-permute-start.14 = (bf16[11,64,128]{2,1,0:T(8,128)(2,1)S(1)}, bf16[11,64,128]{2,1,0:T(8,128)(2,1)S(1)}, u32[]{:S(2)}, u32[]{:S(2)}) collective-permute-start(bf16[11,64,128]{2,1,0:T(8,128)(2,1)S(1)} %get-tuple-element.106), channel_id=1, source_target_pairs={{0,16},{16,0},{1,17},{17,1},{2,18},{18,2},{3,19},{19,3},{4,20},{20... | collective-permute-start | bytes 540680 | tf_op jit(solution)/shard_map/ppermute | solution.py:25
  30.3 1.8 %collective-permute-done.15.one_total = bf16[2,2,128,128]{3,2,1,0:T(8,128)(2,1)S(1)} collective-permute-done((bf16[2,2,128,128]{3,2,1,0:T(8,128)(2,1)S(1)}, bf16[2,2,128,128]{3,2,1,0:T(8,128)(2,1)S(1)}, u32[]{:S(2)}, u32[]{:S(2)}) %collective-permute-start.15) | collective-permute-done | bytes 131104 | tf_op jit(solution)/shard_map/ppermute | solution.py:20
  32.3 1.0 %assemble.1 = (bf16[32,64,128]{2,1,0:T(8,128)(2,1)}, bf16[32,64,128]{2,1,0:T(8,128)(2,1)}, f32[8,128]{1,0:T(8,128)S(1)}) custom-call(bf16[16,64,128]{2,1,0:T(8,128)(2,1)S(1)} %get-tuple-element.102.out_mine, bf16[16,64,128]{2,1,0:T(8,128)(2,1)S(1)} %get-tuple-element.103.query_mine, bf16[10,64,128]{2,1,0:T(8,128)(2,1)S(1)} %collective-permute-done.12.first_third, ...), custom_call_target="tpu_custom_call" | custom-call | flops 1 | tf_op jit(solution)/shard_map/assemble/pallas_call | solution.py:417
  33.6 3.3 %collective-permute-done.17.two_total = bf16[2,8,64,128]{3,2,1,0:T(8,128)(2,1)S(1)} collective-permute-done((bf16[2,8,64,128]{3,2,1,0:T(8,128)(2,1)S(1)}, bf16[2,8,64,128]{3,2,1,0:T(8,128)(2,1)S(1)}, u32[]{:S(2)}, u32[]{:S(2)}) %collective-permute-start.17) | collective-permute-done | bytes 262176 | tf_op jit(solution)/shard_map/ppermute | solution.py:20
  36.9 0.7 %total.1 = (bf16[8,64,128]{2,1,0:T(8,128)(2,1)}, bf16[8,64,128]{2,1,0:T(8,128)(2,1)}) custom-call(f32[2,4,64,128]{3,2,1,0:T(8,128)S(1)} %get-tuple-element.111.sum_mine, bf16[2,4,64,128]{3,2,1,0:T(8,128)(2,1)S(1)} %collective-permute-done.16.sum_other, bf16[2,8,64,128]{3,2,1,0:T(8,128)(2,1)S(1)} %collective-permute-done.17.two_total, ...), custom_call_target="tpu_custom_call" | custom-call | flops 1 | tf_op jit(solution)/shard_map/total/pallas_call | solution.py:417
  (35 shorter events, 1.9 us)
Async XLA Ops:
  0.6 9.0 %copy-start.1 = (bf16[32,64,128]{2,1,0:T(8,128)(2,1)S(1)}, bf16[32,64,128]{2,1,0:T(8,128)(2,1)}, u32[]{:S(2)}) copy-start(bf16[32,64,128]{2,1,0:T(8,128)(2,1)} %grads.3) | copy-start | bytes 1572868
  1.7 8.0 %copy-start = (bf16[32,64,128]{2,1,0:T(8,128)(2,1)S(1)}, bf16[32,64,128]{2,1,0:T(8,128)(2,1)}, u32[]{:S(2)}) copy-start(bf16[32,64,128]{2,1,0:T(8,128)(2,1)} %queries.3) | copy-start | bytes 1572868
  1.7 12.4 %collective-permute-start.3 = (bf16[2,8,64,128]{3,2,1,0:T(8,128)(2,1)S(1)}, bf16[2,8,64,128]{3,2,1,0:T(8,128)(2,1)S(1)}, u32[]{:S(2)}, u32[]{:S(2)}) collective-permute-start(bf16[2,8,64,128]{3,2,1,0:T(8,128)(2,1)S(1)} %pad_maximum_fusion.block.own.after), channel_id=1, source_target_pairs={{0,2},{1,3},{2,4},{3,5},{4,6},{5,7},{6,8},{7,9},{8,10},{9,11},{10,... | collective-permute-start | bytes 786440 | tf_op jit(solution)/shard_map/ppermute | solution.py:20
  4.7 1.3 %collective-permute-start = (bf16[4,64,128]{2,1,0:T(8,128)(2,1)S(1)}, bf16[4,64,128]{2,1,0:T(8,128)(2,1)S(1)}, u32[]{:S(2)}, u32[]{:S(2)}) collective-permute-start(bf16[4,64,128]{2,1,0:T(8,128)(2,1)S(1)} %get-tuple-element.60), channel_id=1, source_target_pairs={{0,16},{16,0},{1,17},{17,1},{2,18},{18,2},{3,19},{19,3},{4,20},{20... | collective-permute-start | bytes 196616 | tf_op jit(solution)/shard_map/ppermute | solution.py:25
  4.8 1.4 %collective-permute-start.1 = (bf16[4,64,128]{2,1,0:T(8,128)(2,1)S(1)}, bf16[4,64,128]{2,1,0:T(8,128)(2,1)S(1)}, u32[]{:S(2)}, u32[]{:S(2)}) collective-permute-start(bf16[4,64,128]{2,1,0:T(8,128)(2,1)S(1)} %get-tuple-element.61), channel_id=1, source_target_pairs={{0,16},{16,0},{1,17},{17,1},{2,18},{18,2},{3,19},{19,3},{4,20},{20... | collective-permute-start | bytes 196616 | tf_op jit(solution)/shard_map/ppermute | solution.py:25
  6.2 10.3 %collective-permute-start.2 = (bf16[2,4,128,128]{3,2,1,0:T(8,128)(2,1)S(1)}, bf16[2,4,128,128]{3,2,1,0:T(8,128)(2,1)S(1)}, u32[]{:S(2)}, u32[]{:S(2)}) collective-permute-start(bf16[2,4,128,128]{3,2,1,0:T(8,128)(2,1)S(1)} %join_own.1.own), channel_id=1, source_target_pairs={{0,1},{1,2},{2,3},{3,4},{4,5},{5,6},{6,7},{7,8},{8,9},{9,10},{10,1... | collective-permute-start | bytes 786440 | tf_op jit(solution)/shard_map/ppermute | solution.py:20
  9.7 2.0 %collective-permute-start.5 = (bf16[11,64,128]{2,1,0:T(8,128)(2,1)S(1)}, bf16[11,64,128]{2,1,0:T(8,128)(2,1)S(1)}, u32[]{:S(2)}, u32[]{:S(2)}) collective-permute-start(bf16[11,64,128]{2,1,0:T(8,128)(2,1)S(1)} %get-tuple-element.63), channel_id=1, source_target_pairs={{0,16},{16,0},{1,17},{17,1},{2,18},{18,2},{3,19},{19,3},{4,20},{20... | collective-permute-start | bytes 540680 | tf_op jit(solution)/shard_map/ppermute | solution.py:25
  9.9 1.8 %collective-permute-start.6 = (bf16[11,64,128]{2,1,0:T(8,128)(2,1)S(1)}, bf16[11,64,128]{2,1,0:T(8,128)(2,1)S(1)}, u32[]{:S(2)}, u32[]{:S(2)}) collective-permute-start(bf16[11,64,128]{2,1,0:T(8,128)(2,1)S(1)} %get-tuple-element.64), channel_id=1, source_target_pairs={{0,16},{16,0},{1,17},{17,1},{2,18},{18,2},{3,19},{19,3},{4,20},{20... | collective-permute-start | bytes 540680 | tf_op jit(solution)/shard_map/ppermute | solution.py:25
  10.3 1.4 %copy-start.2 = (s32[32]{0:T(128)S(1)}, s32[32]{0:T(128)}, u32[]{:S(2)}) copy-start(s32[32]{0:T(128)} %spans.1) | copy-start | bytes 388
  10.3 1.4 %collective-permute-start.4 = (bf16[10,64,128]{2,1,0:T(8,128)(2,1)S(1)}, bf16[10,64,128]{2,1,0:T(8,128)(2,1)S(1)}, u32[]{:S(2)}, u32[]{:S(2)}) collective-permute-start(bf16[10,64,128]{2,1,0:T(8,128)(2,1)S(1)} %get-tuple-element.62), channel_id=1, source_target_pairs={{0,16},{16,0},{1,17},{17,1},{2,18},{18,2},{3,19},{19,3},{4,20},{20... | collective-permute-start | bytes 491528 | tf_op jit(solution)/shard_map/ppermute | solution.py:25
  14.1 1.3 %collective-permute-start.7 = (bf16[4,64,128]{2,1,0:T(8,128)(2,1)S(1)}, bf16[4,64,128]{2,1,0:T(8,128)(2,1)S(1)}, u32[]{:S(2)}, u32[]{:S(2)}) collective-permute-start(bf16[4,64,128]{2,1,0:T(8,128)(2,1)S(1)} %get-tuple-element.70), channel_id=1, source_target_pairs={{0,16},{16,0},{1,17},{17,1},{2,18},{18,2},{3,19},{19,3},{4,20},{20... | collective-permute-start | bytes 196616 | tf_op jit(solution)/shard_map/ppermute | solution.py:25
  14.2 1.4 %collective-permute-start.8 = (bf16[4,64,128]{2,1,0:T(8,128)(2,1)S(1)}, bf16[4,64,128]{2,1,0:T(8,128)(2,1)S(1)}, u32[]{:S(2)}, u32[]{:S(2)}) collective-permute-start(bf16[4,64,128]{2,1,0:T(8,128)(2,1)S(1)} %get-tuple-element.71), channel_id=1, source_target_pairs={{0,16},{16,0},{1,17},{17,1},{2,18},{18,2},{3,19},{19,3},{4,20},{20... | collective-permute-start | bytes 196616 | tf_op jit(solution)/shard_map/ppermute | solution.py:25
  17.4 11.4 %collective-permute-start.11 = (bf16[2,2,128,128]{3,2,1,0:T(8,128)(2,1)S(1)}, bf16[2,2,128,128]{3,2,1,0:T(8,128)(2,1)S(1)}, u32[]{:S(2)}, u32[]{:S(2)}) collective-permute-start(bf16[2,2,128,128]{3,2,1,0:T(8,128)(2,1)S(1)} %get-tuple-element.100), channel_id=1, source_target_pairs={{0,15},{1,0},{2,1},{3,2},{4,3},{5,4},{6,5},{7,6},{8,7},{9,8},{10,9... | collective-permute-start | bytes 393224 | tf_op jit(solution)/shard_map/ppermute | solution.py:20
  23.2 5.1 %collective-permute-start.9 = (bf16[4,64,128]{2,1,0:T(8,128)(2,1)S(1)}, bf16[4,64,128]{2,1,0:T(8,128)(2,1)S(1)}, u32[]{:S(2)}, u32[]{:S(2)}) collective-permute-start(bf16[4,64,128]{2,1,0:T(8,128)(2,1)S(1)} %get-tuple-element.96), channel_id=1, source_target_pairs={{0,16},{16,0},{1,17},{17,1},{2,18},{18,2},{3,19},{19,3},{4,20},{20... | collective-permute-start | bytes 196616 | tf_op jit(solution)/shard_map/ppermute | solution.py:25
  23.3 5.0 %collective-permute-start.10 = (bf16[4,64,128]{2,1,0:T(8,128)(2,1)S(1)}, bf16[4,64,128]{2,1,0:T(8,128)(2,1)S(1)}, u32[]{:S(2)}, u32[]{:S(2)}) collective-permute-start(bf16[4,64,128]{2,1,0:T(8,128)(2,1)S(1)} %get-tuple-element.97), channel_id=1, source_target_pairs={{0,16},{16,0},{1,17},{17,1},{2,18},{18,2},{3,19},{19,3},{4,20},{20... | collective-permute-start | bytes 196616 | tf_op jit(solution)/shard_map/ppermute | solution.py:25
  23.8 8.4 %collective-permute-start.15 = (bf16[2,2,128,128]{3,2,1,0:T(8,128)(2,1)S(1)}, bf16[2,2,128,128]{3,2,1,0:T(8,128)(2,1)S(1)}, u32[]{:S(2)}, u32[]{:S(2)}) collective-permute-start(bf16[2,2,128,128]{3,2,1,0:T(8,128)(2,1)S(1)} %get-tuple-element.110), channel_id=1, source_target_pairs={{0,15},{1,0},{2,1},{3,2},{4,3},{5,4},{6,5},{7,6},{8,7},{9,8},{10,9... | collective-permute-start | bytes 393224 | tf_op jit(solution)/shard_map/ppermute | solution.py:20
  28.3 8.6 %collective-permute-start.17 = (bf16[2,8,64,128]{3,2,1,0:T(8,128)(2,1)S(1)}, bf16[2,8,64,128]{3,2,1,0:T(8,128)(2,1)S(1)}, u32[]{:S(2)}, u32[]{:S(2)}) collective-permute-start(bf16[2,8,64,128]{3,2,1,0:T(8,128)(2,1)S(1)} %join_two.1.after), channel_id=1, source_target_pairs={{0,14},{1,15},{2,0},{3,1},{4,2},{5,3},{6,4},{7,5},{8,6},{9,7},{10,... | collective-permute-start | bytes 786440 | tf_op jit(solution)/shard_map/ppermute | solution.py:20
  29.7 2.6 %collective-permute-start.13 = (bf16[11,64,128]{2,1,0:T(8,128)(2,1)S(1)}, bf16[11,64,128]{2,1,0:T(8,128)(2,1)S(1)}, u32[]{:S(2)}, u32[]{:S(2)}) collective-permute-start(bf16[11,64,128]{2,1,0:T(8,128)(2,1)S(1)} %get-tuple-element.105), channel_id=1, source_target_pairs={{0,16},{16,0},{1,17},{17,1},{2,18},{18,2},{3,19},{19,3},{4,20},{20... | collective-permute-start | bytes 540680 | tf_op jit(solution)/shard_map/ppermute | solution.py:25
  29.7 2.6 %collective-permute-start.14 = (bf16[11,64,128]{2,1,0:T(8,128)(2,1)S(1)}, bf16[11,64,128]{2,1,0:T(8,128)(2,1)S(1)}, u32[]{:S(2)}, u32[]{:S(2)}) collective-permute-start(bf16[11,64,128]{2,1,0:T(8,128)(2,1)S(1)} %get-tuple-element.106), channel_id=1, source_target_pairs={{0,16},{16,0},{1,17},{17,1},{2,18},{18,2},{3,19},{19,3},{4,20},{20... | collective-permute-start | bytes 540680 | tf_op jit(solution)/shard_map/ppermute | solution.py:25
  30.2 2.1 %collective-permute-start.12 = (bf16[10,64,128]{2,1,0:T(8,128)(2,1)S(1)}, bf16[10,64,128]{2,1,0:T(8,128)(2,1)S(1)}, u32[]{:S(2)}, u32[]{:S(2)}) collective-permute-start(bf16[10,64,128]{2,1,0:T(8,128)(2,1)S(1)} %get-tuple-element.104), channel_id=1, source_target_pairs={{0,16},{16,0},{1,17},{17,1},{2,18},{18,2},{3,19},{19,3},{4,20},{20... | collective-permute-start | bytes 491528 | tf_op jit(solution)/shard_map/ppermute | solution.py:25
  32.2 1.4 %collective-permute-start.16 = (bf16[2,4,64,128]{3,2,1,0:T(8,128)(2,1)S(1)}, bf16[2,4,64,128]{3,2,1,0:T(8,128)(2,1)S(1)}, u32[]{:S(2)}, u32[]{:S(2)}) collective-permute-start(bf16[2,4,64,128]{3,2,1,0:T(8,128)(2,1)S(1)} %get-tuple-element.112), channel_id=1, source_target_pairs={{0,16},{16,0},{1,17},{17,1},{2,18},{18,2},{3,19},{19,3},{4,20},{20... | collective-permute-start | bytes 393224 | tf_op jit(solution)/shard_map/ppermute | solution.py:25

commit v21 on v16

--- a/solution.py
+++ b/solution.py
@@ -421,7 +421,9 @@
     chip_rows = ((heads_here, tokens, width), half)
 
     own = jnp.stack([key_matrix, value_matrix])
-    back_two = shifted(own, "seq", 2)
+    chips = lax.axis_size("seq")
+    wraps = [(chips - 2, 1), (chips - 1, 0)]
+    back_two = lax.ppermute(own, "seq", [(i, i + 2) for i in range(chips - 2)] + wraps)
     own_sends = call(split_kernel, "split_own", [half_block] * 2, (own,))
     (own_head,) = call(
         join_own_kernel, "join_own", [chip_pair], (own, *[swapped(send, "head") for send in own_sends])

time: 34.6 us -> 37.4 us (1.081)
  the two profiles are of different devices: /device:TPU:0 before, /device:TPU:4 now
where the time goes in v21:
time: 37.4 us; the launch traced here: 37.3 us
  waiting for transfers between devices  16.2 us (43%)
  starting transfers between devices  10.8 us (29%)
  Pallas kernels  7.68 us (21%)
  between operations  1.45 us (4%)
  other arithmetic  1.05 us (3%)
    ppermute x3, waiting for transfers between devices, shifted(): return lax.ppermute(block, axis, route)  12.7 us
    pallas_call x14, Pallas kernels, call(): pl.pallas_call(kernel, out_shape=tuple((jax.ShapeDtypeStruct(shape, kind)...  7.68 us
    ppermute x3, starting transfers between devices, shifted(): return lax.ppermute(block, axis, route)  6.17 us
    ppermute x13, waiting for transfers between devices, swapped(): return lax.ppermute(block, axis, [(i, count - 1 - i) for i in range(count)])  3.48 us
    ppermute x13, starting transfers between devices, swapped(): return lax.ppermute(block, axis, [(i, count - 1 - i) for i in range(count)])  3.1 us
    ppermute x1, starting transfers between devices, shards(): lax.ppermute(own, 'seq', [(i, i + 2) for i in range(chips - 2)] + wraps)  1.57 us
    another operation x1, other arithmetic, shards(): own = jnp.stack([key_matrix, value_matrix])  1.05 us
  transfers between devices with their start and end apart: 17, of which 10 were waited for; matrix products, arithmetic and copies ran while one was open for 0% of the time, Pallas kernels for 14%

profile of v21, /device:TPU:4, one launch (start us, length us, event | category | flops | bytes accessed | tf_op | source)
XLA Modules:
  0.0 37.3 jit_solution(6042042016242017448)
XLA Ops:
  0.6 1.1 %pad_maximum_fusion.block.own.after = bf16[2,8,64,128]{3,2,1,0:T(8,128)(2,1)S(1)} fusion(bf16[1,8,64,128]{3,2,1,0:T(8,128)(2,1)} %bitcast.2, bf16[1,8,64,128]{3,2,1,0:T(8,128)(2,1)} %bitcast.3), kind=kLoop, calls=%fused_computation | loop fusion | flops 131072 | bytes 524288 | tf_op jit(solution)/shard_map/stack | solution.py:423
  1.7 1.6 %collective-permute-start.3 = (bf16[2,8,64,128]{3,2,1,0:T(8,128)(2,1)S(1)}, bf16[2,8,64,128]{3,2,1,0:T(8,128)(2,1)S(1)}, u32[]{:S(2)}, u32[]{:S(2)}) collective-permute-start(bf16[2,8,64,128]{3,2,1,0:T(8,128)(2,1)S(1)} %pad_maximum_fusion.block.own.after), channel_id=1, source_target_pairs={{0,2},{1,3},{2,4},{3,5},{4,6},{5,7},{6,8},{7,9},{8,10},{9,11},{10,... | collective-permute-start | bytes 786440 | tf_op jit(solution)/shard_map/ppermute | solution.py:426
  3.4 0.5 %collective-permute-start.1 = (bf16[4,64,128]{2,1,0:T(8,128)(2,1)S(1)}, bf16[4,64,128]{2,1,0:T(8,128)(2,1)S(1)}, u32[]{:S(2)}, u32[]{:S(2)}) collective-permute-start(bf16[4,64,128]{2,1,0:T(8,128)(2,1)S(1)} %get-tuple-element.54), channel_id=1, source_target_pairs={{0,16},{16,0},{1,17},{17,1},{2,18},{18,2},{3,19},{19,3},{4,20},{20... | collective-permute-start | bytes 196616 | tf_op jit(solution)/shard_map/ppermute | solution.py:24
  3.9 0.7 %collective-permute-done.other_keys = bf16[4,64,128]{2,1,0:T(8,128)(2,1)S(1)} collective-permute-done((bf16[4,64,128]{2,1,0:T(8,128)(2,1)S(1)}, bf16[4,64,128]{2,1,0:T(8,128)(2,1)S(1)}, u32[]{:S(2)}, u32[]{:S(2)}) %collective-permute-start) | collective-permute-done | bytes 65568 | tf_op jit(solution)/shard_map/ppermute | solution.py:24
  4.8 3.4 %collective-permute-start.2 = (bf16[2,4,128,128]{3,2,1,0:T(8,128)(2,1)S(1)}, bf16[2,4,128,128]{3,2,1,0:T(8,128)(2,1)S(1)}, u32[]{:S(2)}, u32[]{:S(2)}) collective-permute-start(bf16[2,4,128,128]{3,2,1,0:T(8,128)(2,1)S(1)} %join_own.1.own), channel_id=1, source_target_pairs={{0,1},{1,2},{2,3},{3,4},{4,5},{5,6},{6,7},{7,8},{8,9},{9,10},{10,1... | collective-permute-start | bytes 786440 | tf_op jit(solution)/shard_map/ppermute | solution.py:19
  8.4 0.4 %collective-permute-start.6 = (bf16[11,64,128]{2,1,0:T(8,128)(2,1)S(1)}, bf16[11,64,128]{2,1,0:T(8,128)(2,1)S(1)}, u32[]{:S(2)}, u32[]{:S(2)}) collective-permute-start(bf16[11,64,128]{2,1,0:T(8,128)(2,1)S(1)} %get-tuple-element.57), channel_id=1, source_target_pairs={{0,16},{16,0},{1,17},{17,1},{2,18},{18,2},{3,19},{19,3},{4,20},{20... | collective-permute-start | bytes 540680 | tf_op jit(solution)/shard_map/ppermute | solution.py:24
  9.6 0.7 %collective-permute-done.4.first_third = bf16[10,64,128]{2,1,0:T(8,128)(2,1)S(1)} collective-permute-done((bf16[10,64,128]{2,1,0:T(8,128)(2,1)S(1)}, bf16[10,64,128]{2,1,0:T(8,128)(2,1)S(1)}, u32[]{:S(2)}, u32[]{:S(2)}) %collective-permute-start.4) | collective-permute-done | bytes 163872 | tf_op jit(solution)/shard_map/ppermute | solution.py:24
  10.3 1.5 %own_block.1 = (bf16[16,128,128]{2,1,0:T(8,128)(2,1)S(1)}, bf16[16,128,128]{2,1,0:T(8,128)(2,1)S(1)}, bf16[8,128,256]{2,1,0:T(8,128)(2,1)S(1)}, s32[8,1,256]{2,1...) custom-call(s32[32]{0:T(128)S(1)} %copy-done.2, ...), custom_call_target="tpu_custom_call" | custom-call | flops 1 | tf_op jit(solution)/shard_map/own_block/pallas_call | solution.py:400
  12.4 0.7 %collective-permute-done.7.two_keys = bf16[4,64,128]{2,1,0:T(8,128)(2,1)S(1)} collective-permute-done((bf16[4,64,128]{2,1,0:T(8,128)(2,1)S(1)}, bf16[4,64,128]{2,1,0:T(8,128)(2,1)S(1)}, u32[]{:S(2)}, u32[]{:S(2)}) %collective-permute-start.7) | collective-permute-done | bytes 65568 | tf_op jit(solution)/shard_map/ppermute | solution.py:24
  13.4 0.9 %near_forward.1 = (f32[8,1,256]{2,1,0:T(1,128)S(1)}, f32[8,1,256]{2,1,0:T(1,128)S(1)}, f32[8,128,256]{2,1,0:T(8,128)S(1)}, f32[8,128,256]{2,1,0:T(8,128)S(1)}, f...) custom-call(s32[8,1,256]{2,1,0:T(1,128)S(1)} %get-tuple-element.59.first, ...), custom_call_target="tpu_custom_call" | custom-call | flops 1 | tf_op jit(solution)/shard_map/near_forward/pallas_call | solution.py:400
  14.3 2.7 %collective-permute-done.2.back_one = bf16[2,4,128,128]{3,2,1,0:T(8,128)(2,1)S(1)} collective-permute-done((bf16[2,4,128,128]{3,2,1,0:T(8,128)(2,1)S(1)}, bf16[2,4,128,128]{3,2,1,0:T(8,128)(2,1)S(1)}, u32[]{:S(2)}, u32[]{:S(2)}) %collective-permute-start.2) | collective-permute-done | bytes 262176 | tf_op jit(solution)/shard_map/ppermute | solution.py:19
  17.1 1.5 %last_forward_backward.1 = (bf16[8,128,256]{2,1,0:T(8,128)(2,1)S(1)}, f32[8,1,256]{2,1,0:T(1,128)S(1)}, f32[8,1,256]{2,1,0:T(1,128)S(1)}, bf16[8,128,256]{2,1,0:T(8,128)(2,1)S(1)}, bf16[2,4,128,128]{3,2,1,0:T(8,128)(2,1)S(1)}) custom-call(s32[8,1,256]{2,1,0:T(1,128)S(1)} %get-tuple-element.59.first, bf16[16,128,128]{2,1,0:T(8,128)(2,1)S(1)} %get-tuple-element.60.query_head, ...), custom_call_target="tpu_custom_call" | custom-call | flops 1 | tf_op jit(solution)/shard_map/last_forward_backward/pallas_call | solution.py:400
  18.6 0.3 collective-permute-start.14
  19.0 0.5 %two_backward.1 = (bf16[8,128,256]{2,1,0:T(8,128)(2,1)S(1)}, bf16[2,4,64,128]{3,2,1,0:T(8,128)(2,1)S(1)}, bf16[4,64,128]{2,1,0:T(8,128)(2,1)S(1)}, bf16[4,64,128]{2,1,0:T(8,128)(2,1)S(1)}) custom-call(bf16[16,128,128]{2,1,0:T(8,128)(2,1)S(1)} %get-tuple-element.60.query_head, bf16[16,128,128]{2,1,0:T(8,128)(2,1)S(1)} %get-tuple-element.61.grad_head, ...), custom_call_target="tpu_custom_call" | custom-call | flops 1 | tf_op jit(solution)/shard_map/two_backward/pallas_call | solution.py:400
  19.6 0.4 %collective-permute-start.10 = (bf16[4,64,128]{2,1,0:T(8,128)(2,1)S(1)}, bf16[4,64,128]{2,1,0:T(8,128)(2,1)S(1)}, u32[]{:S(2)}, u32[]{:S(2)}) collective-permute-start(bf16[4,64,128]{2,1,0:T(8,128)(2,1)S(1)} %get-tuple-element.86), channel_id=1, source_target_pairs={{0,16},{16,0},{1,17},{17,1},{2,18},{18,2},{3,19},{19,3},{4,20},{20... | collective-permute-start | bytes 196616 | tf_op jit(solution)/shard_map/ppermute | solution.py:24
  20.1 0.7 %collective-permute-done.9.other_keys = bf16[4,64,128]{2,1,0:T(8,128)(2,1)S(1)} collective-permute-done((bf16[4,64,128]{2,1,0:T(8,128)(2,1)S(1)}, bf16[4,64,128]{2,1,0:T(8,128)(2,1)S(1)}, u32[]{:S(2)}, u32[]{:S(2)}) %collective-permute-start.9) | collective-permute-done | bytes 65568 | tf_op jit(solution)/shard_map/ppermute | solution.py:24
  21.0 2.4 %collective-permute-start.16 = (bf16[2,8,64,128]{3,2,1,0:T(8,128)(2,1)S(1)}, bf16[2,8,64,128]{3,2,1,0:T(8,128)(2,1)S(1)}, u32[]{:S(2)}, u32[]{:S(2)}) collective-permute-start(bf16[2,8,64,128]{3,2,1,0:T(8,128)(2,1)S(1)} %join_two.1.after), channel_id=1, source_target_pairs={{0,14},{1,15},{2,0},{3,1},{4,2},{5,3},{6,4},{7,5},{8,6},{9,7},{10,... | collective-permute-start | bytes 786440 | tf_op jit(solution)/shard_map/ppermute | solution.py:19
  23.4 0.5 %own_backward.1 = (bf16[8,128,256]{2,1,0:T(8,128)(2,1)S(1)}, f32[2,4,128,128]{3,2,1,0:T(8,128)S(1)}) custom-call(bf16[16,128,128]{2,1,0:T(8,128)(2,1)S(1)} %get-tuple-element.60.query_head, bf16[16,128,128]{2,1,0:T(8,128)(2,1)S(1)} %get-tuple-element.61.grad_head, f32[8,128,256]{2,1,0:T(8,128)S(1)} %get-tuple-element.81.own_weights, ...), custom_call_target="tpu_custom_call" | custom-call | flops 1 | tf_op jit(solution)/shard_map/own_backward/pallas_call | solution.py:400
  23.9 0.7 %query_grad.1 = (bf16[16,64,128]{2,1,0:T(8,128)(2,1)S(1)}, bf16[16,64,128]{2,1,0:T(8,128)(2,1)S(1)}, bf16[10,64,128]{2,1,0:T(8,128)(2,1)S(1)}, bf16[11,64,128]{2,1,0:T(8,128)(2,1)S(1)}, bf16[11,64,128]{2,1,0:T(8,128)(2,1)S(1)}) custom-call(bf16[2,4,128,128]{3,2,1,0:T(8,128)(2,1)S(1)} %join_own.1.own, ...), custom_call_target="tpu_custom_call" | custom-call | flops 1 | tf_op jit(solution)/shard_map/query_grad/pallas_call | solution.py:400
  24.8 0.4 %collective-permute-start.13 = (bf16[11,64,128]{2,1,0:T(8,128)(2,1)S(1)}, bf16[11,64,128]{2,1,0:T(8,128)(2,1)S(1)}, u32[]{:S(2)}, u32[]{:S(2)}) collective-permute-start(bf16[11,64,128]{2,1,0:T(8,128)(2,1)S(1)} %get-tuple-element.92), channel_id=1, source_target_pairs={{0,16},{16,0},{1,17},{17,1},{2,18},{18,2},{3,19},{19,3},{4,20},{20... | collective-permute-start | bytes 540680 | tf_op jit(solution)/shard_map/ppermute | solution.py:24
  25.3 2.4 %collective-permute-done.14.one_total = bf16[2,4,128,128]{3,2,1,0:T(8,128)(2,1)S(1)} collective-permute-done((bf16[2,4,128,128]{3,2,1,0:T(8,128)(2,1)S(1)}, bf16[2,4,128,128]{3,2,1,0:T(8,128)(2,1)S(1)}, u32[]{:S(2)}, u32[]{:S(2)}) %collective-permute-start.14) | collective-permute-done | bytes 262176 | tf_op jit(solution)/shard_map/ppermute | solution.py:19
  27.9 1.0 %assemble.1 = (bf16[32,64,128]{2,1,0:T(8,128)(2,1)}, bf16[32,64,128]{2,1,0:T(8,128)(2,1)}, f32[8,128]{1,0:T(8,128)S(1)}) custom-call(bf16[16,64,128]{2,1,0:T(8,128)(2,1)S(1)} %get-tuple-element.88.out_mine, bf16[16,64,128]{2,1,0:T(8,128)(2,1)S(1)} %get-tuple-element.89.query_mine, bf16[10,64,128]{2,1,0:T(8,128)(2,1)S(1)} %collective-permute-done.11.first_third, ...), custom_call_target="tpu_custom_call" | custom-call | flops 1 | tf_op jit(solution)/shard_map/assemble/pallas_call | solution.py:400
  28.9 7.6 %collective-permute-done.16.two_total = bf16[2,8,64,128]{3,2,1,0:T(8,128)(2,1)S(1)} collective-permute-done((bf16[2,8,64,128]{3,2,1,0:T(8,128)(2,1)S(1)}, bf16[2,8,64,128]{3,2,1,0:T(8,128)(2,1)S(1)}, u32[]{:S(2)}, u32[]{:S(2)}) %collective-permute-start.16) | collective-permute-done | bytes 262176 | tf_op jit(solution)/shard_map/ppermute | solution.py:19
  36.5 0.8 %total.1 = (bf16[8,64,128]{2,1,0:T(8,128)(2,1)}, bf16[8,64,128]{2,1,0:T(8,128)(2,1)}) custom-call(f32[2,4,64,128]{3,2,1,0:T(8,128)S(1)} %get-tuple-element.97.sum_mine, bf16[2,4,64,128]{3,2,1,0:T(8,128)(2,1)S(1)} %collective-permute-done.15.sum_other, bf16[2,8,64,128]{3,2,1,0:T(8,128)(2,1)S(1)} %collective-permute-done.16.two_total, ...), custom_call_target="tpu_custom_call" | custom-call | flops 1 | tf_op jit(solution)/shard_map/total/pallas_call | solution.py:400
  (31 shorter events, 2.1 us)
Async XLA Ops:
  0.6 7.6 %copy-start.1 = (bf16[32,64,128]{2,1,0:T(8,128)(2,1)S(1)}, bf16[32,64,128]{2,1,0:T(8,128)(2,1)}, u32[]{:S(2)}) copy-start(bf16[32,64,128]{2,1,0:T(8,128)(2,1)} %grads.3) | copy-start | bytes 1572868
  1.7 6.5 %copy-start = (bf16[32,64,128]{2,1,0:T(8,128)(2,1)S(1)}, bf16[32,64,128]{2,1,0:T(8,128)(2,1)}, u32[]{:S(2)}) copy-start(bf16[32,64,128]{2,1,0:T(8,128)(2,1)} %queries.3) | copy-start | bytes 1572868
  1.7 10.1 %collective-permute-start.3 = (bf16[2,8,64,128]{3,2,1,0:T(8,128)(2,1)S(1)}, bf16[2,8,64,128]{3,2,1,0:T(8,128)(2,1)S(1)}, u32[]{:S(2)}, u32[]{:S(2)}) collective-permute-start(bf16[2,8,64,128]{3,2,1,0:T(8,128)(2,1)S(1)} %pad_maximum_fusion.block.own.after), channel_id=1, source_target_pairs={{0,2},{1,3},{2,4},{3,5},{4,6},{5,7},{6,8},{7,9},{8,10},{9,11},{10,... | collective-permute-start | bytes 786440 | tf_op jit(solution)/shard_map/ppermute | solution.py:426
  3.3 1.3 %collective-permute-start = (bf16[4,64,128]{2,1,0:T(8,128)(2,1)S(1)}, bf16[4,64,128]{2,1,0:T(8,128)(2,1)S(1)}, u32[]{:S(2)}, u32[]{:S(2)}) collective-permute-start(bf16[4,64,128]{2,1,0:T(8,128)(2,1)S(1)} %get-tuple-element.53), channel_id=1, source_target_pairs={{0,16},{16,0},{1,17},{17,1},{2,18},{18,2},{3,19},{19,3},{4,20},{20... | collective-permute-start | bytes 196616 | tf_op jit(solution)/shard_map/ppermute | solution.py:24
  3.4 1.4 %collective-permute-start.1 = (bf16[4,64,128]{2,1,0:T(8,128)(2,1)S(1)}, bf16[4,64,128]{2,1,0:T(8,128)(2,1)S(1)}, u32[]{:S(2)}, u32[]{:S(2)}) collective-permute-start(bf16[4,64,128]{2,1,0:T(8,128)(2,1)S(1)} %get-tuple-element.54), channel_id=1, source_target_pairs={{0,16},{16,0},{1,17},{17,1},{2,18},{18,2},{3,19},{19,3},{4,20},{20... | collective-permute-start | bytes 196616 | tf_op jit(solution)/shard_map/ppermute | solution.py:24
  4.8 12.3 %collective-permute-start.2 = (bf16[2,4,128,128]{3,2,1,0:T(8,128)(2,1)S(1)}, bf16[2,4,128,128]{3,2,1,0:T(8,128)(2,1)S(1)}, u32[]{:S(2)}, u32[]{:S(2)}) collective-permute-start(bf16[2,4,128,128]{3,2,1,0:T(8,128)(2,1)S(1)} %join_own.1.own), channel_id=1, source_target_pairs={{0,1},{1,2},{2,3},{3,4},{4,5},{5,6},{6,7},{7,8},{8,9},{9,10},{10,1... | collective-permute-start | bytes 786440 | tf_op jit(solution)/shard_map/ppermute | solution.py:19
  8.3 2.0 %collective-permute-start.5 = (bf16[11,64,128]{2,1,0:T(8,128)(2,1)S(1)}, bf16[11,64,128]{2,1,0:T(8,128)(2,1)S(1)}, u32[]{:S(2)}, u32[]{:S(2)}) collective-permute-start(bf16[11,64,128]{2,1,0:T(8,128)(2,1)S(1)} %get-tuple-element.56), channel_id=1, source_target_pairs={{0,16},{16,0},{1,17},{17,1},{2,18},{18,2},{3,19},{19,3},{4,20},{20... | collective-permute-start | bytes 540680 | tf_op jit(solution)/shard_map/ppermute | solution.py:24
  8.4 1.8 %collective-permute-start.6 = (bf16[11,64,128]{2,1,0:T(8,128)(2,1)S(1)}, bf16[11,64,128]{2,1,0:T(8,128)(2,1)S(1)}, u32[]{:S(2)}, u32[]{:S(2)}) collective-permute-start(bf16[11,64,128]{2,1,0:T(8,128)(2,1)S(1)} %get-tuple-element.57), channel_id=1, source_target_pairs={{0,16},{16,0},{1,17},{17,1},{2,18},{18,2},{3,19},{19,3},{4,20},{20... | collective-permute-start | bytes 540680 | tf_op jit(solution)/shard_map/ppermute | solution.py:24
  8.9 1.4 %copy-start.2 = (s32[32]{0:T(128)S(1)}, s32[32]{0:T(128)}, u32[]{:S(2)}) copy-start(s32[32]{0:T(128)} %spans.1) | copy-start | bytes 388
  8.9 1.4 %collective-permute-start.4 = (bf16[10,64,128]{2,1,0:T(8,128)(2,1)S(1)}, bf16[10,64,128]{2,1,0:T(8,128)(2,1)S(1)}, u32[]{:S(2)}, u32[]{:S(2)}) collective-permute-start(bf16[10,64,128]{2,1,0:T(8,128)(2,1)S(1)} %get-tuple-element.55), channel_id=1, source_target_pairs={{0,16},{16,0},{1,17},{17,1},{2,18},{18,2},{3,19},{19,3},{4,20},{20... | collective-permute-start | bytes 491528 | tf_op jit(solution)/shard_map/ppermute | solution.py:24
  11.8 1.3 %collective-permute-start.7 = (bf16[4,64,128]{2,1,0:T(8,128)(2,1)S(1)}, bf16[4,64,128]{2,1,0:T(8,128)(2,1)S(1)}, u32[]{:S(2)}, u32[]{:S(2)}) collective-permute-start(bf16[4,64,128]{2,1,0:T(8,128)(2,1)S(1)} %get-tuple-element.63), channel_id=1, source_target_pairs={{0,16},{16,0},{1,17},{17,1},{2,18},{18,2},{3,19},{19,3},{4,20},{20... | collective-permute-start | bytes 196616 | tf_op jit(solution)/shard_map/ppermute | solution.py:24
  12.2 1.3 %collective-permute-start.8 = (bf16[4,64,128]{2,1,0:T(8,128)(2,1)S(1)}, bf16[4,64,128]{2,1,0:T(8,128)(2,1)S(1)}, u32[]{:S(2)}, u32[]{:S(2)}) collective-permute-start(bf16[4,64,128]{2,1,0:T(8,128)(2,1)S(1)} %get-tuple-element.64), channel_id=1, source_target_pairs={{0,16},{16,0},{1,17},{17,1},{2,18},{18,2},{3,19},{19,3},{4,20},{20... | collective-permute-start | bytes 196616 | tf_op jit(solution)/shard_map/ppermute | solution.py:24
  18.6 9.0 %collective-permute-start.14 = (bf16[2,4,128,128]{3,2,1,0:T(8,128)(2,1)S(1)}, bf16[2,4,128,128]{3,2,1,0:T(8,128)(2,1)S(1)}, u32[]{:S(2)}, u32[]{:S(2)}) collective-permute-start(bf16[2,4,128,128]{3,2,1,0:T(8,128)(2,1)S(1)} %get-tuple-element.96), channel_id=1, source_target_pairs={{0,15},{1,0},{2,1},{3,2},{4,3},{5,4},{6,5},{7,6},{8,7},{9,8},{10,9... | collective-permute-start | bytes 786440 | tf_op jit(solution)/shard_map/ppermute | solution.py:19
  19.5 1.3 %collective-permute-start.9 = (bf16[4,64,128]{2,1,0:T(8,128)(2,1)S(1)}, bf16[4,64,128]{2,1,0:T(8,128)(2,1)S(1)}, u32[]{:S(2)}, u32[]{:S(2)}) collective-permute-start(bf16[4,64,128]{2,1,0:T(8,128)(2,1)S(1)} %get-tuple-element.85), channel_id=1, source_target_pairs={{0,16},{16,0},{1,17},{17,1},{2,18},{18,2},{3,19},{19,3},{4,20},{20... | collective-permute-start | bytes 196616 | tf_op jit(solution)/shard_map/ppermute | solution.py:24
  19.6 1.3 %collective-permute-start.10 = (bf16[4,64,128]{2,1,0:T(8,128)(2,1)S(1)}, bf16[4,64,128]{2,1,0:T(8,128)(2,1)S(1)}, u32[]{:S(2)}, u32[]{:S(2)}) collective-permute-start(bf16[4,64,128]{2,1,0:T(8,128)(2,1)S(1)} %get-tuple-element.86), channel_id=1, source_target_pairs={{0,16},{16,0},{1,17},{17,1},{2,18},{18,2},{3,19},{19,3},{4,20},{20... | collective-permute-start | bytes 196616 | tf_op jit(solution)/shard_map/ppermute | solution.py:24
  21.0 15.5 %collective-permute-start.16 = (bf16[2,8,64,128]{3,2,1,0:T(8,128)(2,1)S(1)}, bf16[2,8,64,128]{3,2,1,0:T(8,128)(2,1)S(1)}, u32[]{:S(2)}, u32[]{:S(2)}) collective-permute-start(bf16[2,8,64,128]{3,2,1,0:T(8,128)(2,1)S(1)} %join_two.1.after), channel_id=1, source_target_pairs={{0,14},{1,15},{2,0},{3,1},{4,2},{5,3},{6,4},{7,5},{8,6},{9,7},{10,... | collective-permute-start | bytes 786440 | tf_op jit(solution)/shard_map/ppermute | solution.py:19
  24.6 3.2 %collective-permute-start.12 = (bf16[11,64,128]{2,1,0:T(8,128)(2,1)S(1)}, bf16[11,64,128]{2,1,0:T(8,128)(2,1)S(1)}, u32[]{:S(2)}, u32[]{:S(2)}) collective-permute-start(bf16[11,64,128]{2,1,0:T(8,128)(2,1)S(1)} %get-tuple-element.91), channel_id=1, source_target_pairs={{0,16},{16,0},{1,17},{17,1},{2,18},{18,2},{3,19},{19,3},{4,20},{20... | collective-permute-start | bytes 540680 | tf_op jit(solution)/shard_map/ppermute | solution.py:24
  24.8 3.1 %collective-permute-start.13 = (bf16[11,64,128]{2,1,0:T(8,128)(2,1)S(1)}, bf16[11,64,128]{2,1,0:T(8,128)(2,1)S(1)}, u32[]{:S(2)}, u32[]{:S(2)}) collective-permute-start(bf16[11,64,128]{2,1,0:T(8,128)(2,1)S(1)} %get-tuple-element.92), channel_id=1, source_target_pairs={{0,16},{16,0},{1,17},{17,1},{2,18},{18,2},{3,19},{19,3},{4,20},{20... | collective-permute-start | bytes 540680 | tf_op jit(solution)/shard_map/ppermute | solution.py:24
  25.2 2.6 %collective-permute-start.11 = (bf16[10,64,128]{2,1,0:T(8,128)(2,1)S(1)}, bf16[10,64,128]{2,1,0:T(8,128)(2,1)S(1)}, u32[]{:S(2)}, u32[]{:S(2)}) collective-permute-start(bf16[10,64,128]{2,1,0:T(8,128)(2,1)S(1)} %get-tuple-element.90), channel_id=1, source_target_pairs={{0,16},{16,0},{1,17},{17,1},{2,18},{18,2},{3,19},{19,3},{4,20},{20... | collective-permute-start | bytes 491528 | tf_op jit(solution)/shard_map/ppermute | solution.py:24
  27.7 8.8 %collective-permute-start.15 = (bf16[2,4,64,128]{3,2,1,0:T(8,128)(2,1)S(1)}, bf16[2,4,64,128]{3,2,1,0:T(8,128)(2,1)S(1)}, u32[]{:S(2)}, u32[]{:S(2)}) collective-permute-start(bf16[2,4,64,128]{3,2,1,0:T(8,128)(2,1)S(1)} %get-tuple-element.98), channel_id=1, source_target_pairs={{0,16},{16,0},{1,17},{17,1},{2,18},{18,2},{3,19},{19,3},{4,20},{20... | collective-permute-start | bytes 393224 | tf_op jit(solution)/shard_map/ppermute | solution.py:24

commit v22 on v21

--- a/solution.py
+++ b/solution.py
@@ -422,8 +422,13 @@
 
     own = jnp.stack([key_matrix, value_matrix])
     chips = lax.axis_size("seq")
-    wraps = [(chips - 2, 1), (chips - 1, 0)]
-    back_two = lax.ppermute(own, "seq", [(i, i + 2) for i in range(chips - 2)] + wraps)
+    route = []
+    for core in range(cores):
+        route += [(core * chips + i, core * chips + i + 2) for i in range(chips - 2)]
+        route += [
+            (core * chips + chips - 2 + i, (cores - 1 - core) * chips + i) for i in range(2)
+        ]
+    back_two = lax.ppermute(own, ("head", "seq"), route)
     own_sends = call(split_kernel, "split_own", [half_block] * 2, (own,))
     (own_head,) = call(
         join_own_kernel, "join_own", [chip_pair], (own, *[swapped(send, "head") for send in own_sends])

time: 37.4 us -> 34.6 us (0.925)
  the two profiles are of different devices: /device:TPU:4 before, /device:TPU:0 now
where the time goes in v22:
time: 34.6 us; the launch traced here: 34.4 us
  starting transfers between devices  18.1 us (52%)
  Pallas kernels  7.69 us (22%)
  waiting for transfers between devices  6.06 us (18%)
  between operations  1.45 us (4%)
  other arithmetic  1.05 us (3%)
    ppermute x3, starting transfers between devices, shifted(): return lax.ppermute(block, axis, route)  11.4 us
    pallas_call x14, Pallas kernels, call(): pl.pallas_call(kernel, out_shape=tuple((jax.ShapeDtypeStruct(shape, kind)...  7.69 us
    ppermute x13, waiting for transfers between devices, swapped(): return lax.ppermute(block, axis, [(i, count - 1 - i) for i in range(count)])  4.41 us
    ppermute x13, starting transfers between devices, swapped(): return lax.ppermute(block, axis, [(i, count - 1 - i) for i in range(count)])  3.68 us
    ppermute x1, starting transfers between devices, shards(): back_two = lax.ppermute(own, ('head', 'seq'), route)  3.02 us
    ppermute x3, waiting for transfers between devices, shifted(): return lax.ppermute(block, axis, route)  1.65 us
    another operation x1, other arithmetic, shards(): own = jnp.stack([key_matrix, value_matrix])  1.05 us
  transfers between devices with their start and end apart: 17, of which 9 were waited for; matrix products, arithmetic and copies ran while one was open for 0% of the time, Pallas kernels for 16%

profile of v22, /device:TPU:0, one launch (start us, length us, event | category | flops | bytes accessed | tf_op | source)
XLA Modules:
  0.0 34.4 jit_solution(2979684065023752853)
XLA Ops:
  0.6 1.1 %pad_maximum_fusion.block.own.after = bf16[2,8,64,128]{3,2,1,0:T(8,128)(2,1)S(1)} fusion(bf16[1,8,64,128]{3,2,1,0:T(8,128)(2,1)} %bitcast.2, bf16[1,8,64,128]{3,2,1,0:T(8,128)(2,1)} %bitcast.3), kind=kLoop, calls=%fused_computation | loop fusion | flops 131072 | bytes 524288 | tf_op jit(solution)/shard_map/stack | solution.py:423
  1.7 3.0 %collective-permute-start.3 = (bf16[2,8,64,128]{3,2,1,0:T(8,128)(2,1)S(1)}, bf16[2,8,64,128]{3,2,1,0:T(8,128)(2,1)S(1)}, u32[]{:S(2)}, u32[]{:S(2)}) collective-permute-start(bf16[2,8,64,128]{3,2,1,0:T(8,128)(2,1)S(1)} %pad_maximum_fusion.block.own.after), channel_id=1, source_target_pairs={{0,2},{1,3},{2,4},{3,5},{4,6},{5,7},{6,8},{7,9},{8,10},{9,11},{10,... | collective-permute-start | bytes 786440 | tf_op jit(solution)/shard_map/ppermute | solution.py:431
  4.8 0.5 %collective-permute-start.1 = (bf16[4,64,128]{2,1,0:T(8,128)(2,1)S(1)}, bf16[4,64,128]{2,1,0:T(8,128)(2,1)S(1)}, u32[]{:S(2)}, u32[]{:S(2)}) collective-permute-start(bf16[4,64,128]{2,1,0:T(8,128)(2,1)S(1)} %get-tuple-element.54), channel_id=1, source_target_pairs={{0,16},{16,0},{1,17},{17,1},{2,18},{18,2},{3,19},{19,3},{4,20},{20... | collective-permute-start | bytes 196616 | tf_op jit(solution)/shard_map/ppermute | solution.py:24
  5.3 0.7 %collective-permute-done.other_keys = bf16[4,64,128]{2,1,0:T(8,128)(2,1)S(1)} collective-permute-done((bf16[4,64,128]{2,1,0:T(8,128)(2,1)S(1)}, bf16[4,64,128]{2,1,0:T(8,128)(2,1)S(1)}, u32[]{:S(2)}, u32[]{:S(2)}) %collective-permute-start) | collective-permute-done | bytes 65568 | tf_op jit(solution)/shard_map/ppermute | solution.py:24
  6.2 3.4 %collective-permute-start.2 = (bf16[2,4,128,128]{3,2,1,0:T(8,128)(2,1)S(1)}, bf16[2,4,128,128]{3,2,1,0:T(8,128)(2,1)S(1)}, u32[]{:S(2)}, u32[]{:S(2)}) collective-permute-start(bf16[2,4,128,128]{3,2,1,0:T(8,128)(2,1)S(1)} %join_own.1.own), channel_id=1, source_target_pairs={{0,1},{1,2},{2,3},{3,4},{4,5},{5,6},{6,7},{7,8},{8,9},{9,10},{10,1... | collective-permute-start | bytes 786440 | tf_op jit(solution)/shard_map/ppermute | solution.py:19
  11.0 0.7 %collective-permute-done.4.first_third = bf16[10,64,128]{2,1,0:T(8,128)(2,1)S(1)} collective-permute-done((bf16[10,64,128]{2,1,0:T(8,128)(2,1)S(1)}, bf16[10,64,128]{2,1,0:T(8,128)(2,1)S(1)}, u32[]{:S(2)}, u32[]{:S(2)}) %collective-permute-start.4) | collective-permute-done | bytes 163872 | tf_op jit(solution)/shard_map/ppermute | solution.py:24
  11.7 1.5 %own_block.1 = (bf16[16,128,128]{2,1,0:T(8,128)(2,1)S(1)}, bf16[16,128,128]{2,1,0:T(8,128)(2,1)S(1)}, bf16[8,128,256]{2,1,0:T(8,128)(2,1)S(1)}, s32[8,1,256]{2,1...) custom-call(s32[32]{0:T(128)S(1)} %copy-done.2, ...), custom_call_target="tpu_custom_call" | custom-call | flops 1 | tf_op jit(solution)/shard_map/own_block/pallas_call | solution.py:400
  13.3 0.7 %collective-permute-start.7 = (bf16[4,64,128]{2,1,0:T(8,128)(2,1)S(1)}, bf16[4,64,128]{2,1,0:T(8,128)(2,1)S(1)}, u32[]{:S(2)}, u32[]{:S(2)}) collective-permute-start(bf16[4,64,128]{2,1,0:T(8,128)(2,1)S(1)} %get-tuple-element.63), channel_id=1, source_target_pairs={{0,16},{16,0},{1,17},{17,1},{2,18},{18,2},{3,19},{19,3},{4,20},{20... | collective-permute-start | bytes 196616 | tf_op jit(solution)/shard_map/ppermute | solution.py:24
  14.1 0.8 %collective-permute-done.7.two_keys = bf16[4,64,128]{2,1,0:T(8,128)(2,1)S(1)} collective-permute-done((bf16[4,64,128]{2,1,0:T(8,128)(2,1)S(1)}, bf16[4,64,128]{2,1,0:T(8,128)(2,1)S(1)}, u32[]{:S(2)}, u32[]{:S(2)}) %collective-permute-start.7) | collective-permute-done | bytes 65568 | tf_op jit(solution)/shard_map/ppermute | solution.py:24
  15.2 0.9 %near_forward.1 = (f32[8,1,256]{2,1,0:T(1,128)S(1)}, f32[8,1,256]{2,1,0:T(1,128)S(1)}, f32[8,128,256]{2,1,0:T(8,128)S(1)}, f32[8,128,256]{2,1,0:T(8,128)S(1)}, f...) custom-call(s32[8,1,256]{2,1,0:T(1,128)S(1)} %get-tuple-element.59.first, ...), custom_call_target="tpu_custom_call" | custom-call | flops 1 | tf_op jit(solution)/shard_map/near_forward/pallas_call | solution.py:400
  16.2 1.5 %last_forward_backward.1 = (bf16[8,128,256]{2,1,0:T(8,128)(2,1)S(1)}, f32[8,1,256]{2,1,0:T(1,128)S(1)}, f32[8,1,256]{2,1,0:T(1,128)S(1)}, bf16[8,128,256]{2,1,0:T(8,128)(2,1)S(1)}, bf16[2,4,128,128]{3,2,1,0:T(8,128)(2,1)S(1)}) custom-call(s32[8,1,256]{2,1,0:T(1,128)S(1)} %get-tuple-element.59.first, bf16[16,128,128]{2,1,0:T(8,128)(2,1)S(1)} %get-tuple-element.60.query_head, ...), custom_call_target="tpu_custom_call" | custom-call | flops 1 | tf_op jit(solution)/shard_map/last_forward_backward/pallas_call | solution.py:400
  17.7 4.6 %collective-permute-start.14 = (bf16[2,4,128,128]{3,2,1,0:T(8,128)(2,1)S(1)}, bf16[2,4,128,128]{3,2,1,0:T(8,128)(2,1)S(1)}, u32[]{:S(2)}, u32[]{:S(2)}) collective-permute-start(bf16[2,4,128,128]{3,2,1,0:T(8,128)(2,1)S(1)} %get-tuple-element.96), channel_id=1, source_target_pairs={{0,15},{1,0},{2,1},{3,2},{4,3},{5,4},{6,5},{7,6},{8,7},{9,8},{10,9... | collective-permute-start | bytes 786440 | tf_op jit(solution)/shard_map/ppermute | solution.py:19
  22.3 0.5 %two_backward.1 = (bf16[8,128,256]{2,1,0:T(8,128)(2,1)S(1)}, bf16[2,4,64,128]{3,2,1,0:T(8,128)(2,1)S(1)}, bf16[4,64,128]{2,1,0:T(8,128)(2,1)S(1)}, bf16[4,64,128]{2,1,0:T(8,128)(2,1)S(1)}) custom-call(bf16[16,128,128]{2,1,0:T(8,128)(2,1)S(1)} %get-tuple-element.60.query_head, bf16[16,128,128]{2,1,0:T(8,128)(2,1)S(1)} %get-tuple-element.61.grad_head, ...), custom_call_target="tpu_custom_call" | custom-call | flops 1 | tf_op jit(solution)/shard_map/two_backward/pallas_call | solution.py:400
  22.9 0.5 %collective-permute-start.10 = (bf16[4,64,128]{2,1,0:T(8,128)(2,1)S(1)}, bf16[4,64,128]{2,1,0:T(8,128)(2,1)S(1)}, u32[]{:S(2)}, u32[]{:S(2)}) collective-permute-start(bf16[4,64,128]{2,1,0:T(8,128)(2,1)S(1)} %get-tuple-element.86), channel_id=1, source_target_pairs={{0,16},{16,0},{1,17},{17,1},{2,18},{18,2},{3,19},{19,3},{4,20},{20... | collective-permute-start | bytes 196616 | tf_op jit(solution)/shard_map/ppermute | solution.py:24
  23.4 0.7 %collective-permute-done.9.other_keys = bf16[4,64,128]{2,1,0:T(8,128)(2,1)S(1)} collective-permute-done((bf16[4,64,128]{2,1,0:T(8,128)(2,1)S(1)}, bf16[4,64,128]{2,1,0:T(8,128)(2,1)S(1)}, u32[]{:S(2)}, u32[]{:S(2)}) %collective-permute-start.9) | collective-permute-done | bytes 65568 | tf_op jit(solution)/shard_map/ppermute | solution.py:24
  24.3 3.4 %collective-permute-start.16 = (bf16[2,8,64,128]{3,2,1,0:T(8,128)(2,1)S(1)}, bf16[2,8,64,128]{3,2,1,0:T(8,128)(2,1)S(1)}, u32[]{:S(2)}, u32[]{:S(2)}) collective-permute-start(bf16[2,8,64,128]{3,2,1,0:T(8,128)(2,1)S(1)} %join_two.1.after), channel_id=1, source_target_pairs={{0,14},{1,15},{2,0},{3,1},{4,2},{5,3},{6,4},{7,5},{8,6},{9,7},{10,... | collective-permute-start | bytes 786440 | tf_op jit(solution)/shard_map/ppermute | solution.py:19
  27.8 0.5 %own_backward.1 = (bf16[8,128,256]{2,1,0:T(8,128)(2,1)S(1)}, f32[2,4,128,128]{3,2,1,0:T(8,128)S(1)}) custom-call(bf16[16,128,128]{2,1,0:T(8,128)(2,1)S(1)} %get-tuple-element.60.query_head, bf16[16,128,128]{2,1,0:T(8,128)(2,1)S(1)} %get-tuple-element.61.grad_head, f32[8,128,256]{2,1,0:T(8,128)S(1)} %get-tuple-element.81.own_weights, ...), custom_call_target="tpu_custom_call" | custom-call | flops 1 | tf_op jit(solution)/shard_map/own_backward/pallas_call | solution.py:400
  28.2 0.8 %query_grad.1 = (bf16[16,64,128]{2,1,0:T(8,128)(2,1)S(1)}, bf16[16,64,128]{2,1,0:T(8,128)(2,1)S(1)}, bf16[10,64,128]{2,1,0:T(8,128)(2,1)S(1)}, bf16[11,64,128]{2,1,0:T(8,128)(2,1)S(1)}, bf16[11,64,128]{2,1,0:T(8,128)(2,1)S(1)}) custom-call(bf16[2,4,128,128]{3,2,1,0:T(8,128)(2,1)S(1)} %join_own.1.own, ...), custom_call_target="tpu_custom_call" | custom-call | flops 1 | tf_op jit(solution)/shard_map/query_grad/pallas_call | solution.py:400
  29.0 0.5 %collective-permute-start.13 = (bf16[11,64,128]{2,1,0:T(8,128)(2,1)S(1)}, bf16[11,64,128]{2,1,0:T(8,128)(2,1)S(1)}, u32[]{:S(2)}, u32[]{:S(2)}) collective-permute-start(bf16[11,64,128]{2,1,0:T(8,128)(2,1)S(1)} %get-tuple-element.92), channel_id=1, source_target_pairs={{0,16},{16,0},{1,17},{17,1},{2,18},{18,2},{3,19},{19,3},{4,20},{20... | collective-permute-start | bytes 540680 | tf_op jit(solution)/shard_map/ppermute | solution.py:24
  29.7 0.5 %collective-permute-start.15 = (bf16[2,4,64,128]{3,2,1,0:T(8,128)(2,1)S(1)}, bf16[2,4,64,128]{3,2,1,0:T(8,128)(2,1)S(1)}, u32[]{:S(2)}, u32[]{:S(2)}) collective-permute-start(bf16[2,4,64,128]{3,2,1,0:T(8,128)(2,1)S(1)} %get-tuple-element.98), channel_id=1, source_target_pairs={{0,16},{16,0},{1,17},{17,1},{2,18},{18,2},{3,19},{19,3},{4,20},{20... | collective-permute-start | bytes 393224 | tf_op jit(solution)/shard_map/ppermute | solution.py:24
  30.2 0.8 %collective-permute-done.11.first_third = bf16[10,64,128]{2,1,0:T(8,128)(2,1)S(1)} collective-permute-done((bf16[10,64,128]{2,1,0:T(8,128)(2,1)S(1)}, bf16[10,64,128]{2,1,0:T(8,128)(2,1)S(1)}, u32[]{:S(2)}, u32[]{:S(2)}) %collective-permute-start.11) | collective-permute-done | bytes 163872 | tf_op jit(solution)/shard_map/ppermute | solution.py:24
  31.0 1.0 %assemble.1 = (bf16[32,64,128]{2,1,0:T(8,128)(2,1)}, bf16[32,64,128]{2,1,0:T(8,128)(2,1)}, f32[8,128]{1,0:T(8,128)S(1)}) custom-call(bf16[16,64,128]{2,1,0:T(8,128)(2,1)S(1)} %get-tuple-element.88.out_mine, bf16[16,64,128]{2,1,0:T(8,128)(2,1)S(1)} %get-tuple-element.89.query_mine, bf16[10,64,128]{2,1,0:T(8,128)(2,1)S(1)} %collective-permute-done.11.first_third, ...), custom_call_target="tpu_custom_call" | custom-call | flops 1 | tf_op jit(solution)/shard_map/assemble/pallas_call | solution.py:400
  32.0 1.6 %collective-permute-done.16.two_total = bf16[2,8,64,128]{3,2,1,0:T(8,128)(2,1)S(1)} collective-permute-done((bf16[2,8,64,128]{3,2,1,0:T(8,128)(2,1)S(1)}, bf16[2,8,64,128]{3,2,1,0:T(8,128)(2,1)S(1)}, u32[]{:S(2)}, u32[]{:S(2)}) %collective-permute-start.16) | collective-permute-done | bytes 262176 | tf_op jit(solution)/shard_map/ppermute | solution.py:19
  33.6 0.8 %total.1 = (bf16[8,64,128]{2,1,0:T(8,128)(2,1)}, bf16[8,64,128]{2,1,0:T(8,128)(2,1)}) custom-call(f32[2,4,64,128]{3,2,1,0:T(8,128)S(1)} %get-tuple-element.97.sum_mine, bf16[2,4,64,128]{3,2,1,0:T(8,128)(2,1)S(1)} %collective-permute-done.15.sum_other, bf16[2,8,64,128]{3,2,1,0:T(8,128)(2,1)S(1)} %collective-permute-done.16.two_total, ...), custom_call_target="tpu_custom_call" | custom-call | flops 1 | tf_op jit(solution)/shard_map/total/pallas_call | solution.py:400
  (31 shorter events, 1.9 us)
Async XLA Ops:
  0.6 9.0 %copy-start.1 = (bf16[32,64,128]{2,1,0:T(8,128)(2,1)S(1)}, bf16[32,64,128]{2,1,0:T(8,128)(2,1)}, u32[]{:S(2)}) copy-start(bf16[32,64,128]{2,1,0:T(8,128)(2,1)} %grads.3) | copy-start | bytes 1572868
  1.7 8.0 %copy-start = (bf16[32,64,128]{2,1,0:T(8,128)(2,1)S(1)}, bf16[32,64,128]{2,1,0:T(8,128)(2,1)}, u32[]{:S(2)}) copy-start(bf16[32,64,128]{2,1,0:T(8,128)(2,1)} %queries.3) | copy-start | bytes 1572868
  1.7 11.6 %collective-permute-start.3 = (bf16[2,8,64,128]{3,2,1,0:T(8,128)(2,1)S(1)}, bf16[2,8,64,128]{3,2,1,0:T(8,128)(2,1)S(1)}, u32[]{:S(2)}, u32[]{:S(2)}) collective-permute-start(bf16[2,8,64,128]{3,2,1,0:T(8,128)(2,1)S(1)} %pad_maximum_fusion.block.own.after), channel_id=1, source_target_pairs={{0,2},{1,3},{2,4},{3,5},{4,6},{5,7},{6,8},{7,9},{8,10},{9,11},{10,... | collective-permute-start | bytes 786440 | tf_op jit(solution)/shard_map/ppermute | solution.py:431
  4.7 1.3 %collective-permute-start = (bf16[4,64,128]{2,1,0:T(8,128)(2,1)S(1)}, bf16[4,64,128]{2,1,0:T(8,128)(2,1)S(1)}, u32[]{:S(2)}, u32[]{:S(2)}) collective-permute-start(bf16[4,64,128]{2,1,0:T(8,128)(2,1)S(1)} %get-tuple-element.53), channel_id=1, source_target_pairs={{0,16},{16,0},{1,17},{17,1},{2,18},{18,2},{3,19},{19,3},{4,20},{20... | collective-permute-start | bytes 196616 | tf_op jit(solution)/shard_map/ppermute | solution.py:24
  4.8 1.4 %collective-permute-start.1 = (bf16[4,64,128]{2,1,0:T(8,128)(2,1)S(1)}, bf16[4,64,128]{2,1,0:T(8,128)(2,1)S(1)}, u32[]{:S(2)}, u32[]{:S(2)}) collective-permute-start(bf16[4,64,128]{2,1,0:T(8,128)(2,1)S(1)} %get-tuple-element.54), channel_id=1, source_target_pairs={{0,16},{16,0},{1,17},{17,1},{2,18},{18,2},{3,19},{19,3},{4,20},{20... | collective-permute-start | bytes 196616 | tf_op jit(solution)/shard_map/ppermute | solution.py:24
  6.2 9.9 %collective-permute-start.2 = (bf16[2,4,128,128]{3,2,1,0:T(8,128)(2,1)S(1)}, bf16[2,4,128,128]{3,2,1,0:T(8,128)(2,1)S(1)}, u32[]{:S(2)}, u32[]{:S(2)}) collective-permute-start(bf16[2,4,128,128]{3,2,1,0:T(8,128)(2,1)S(1)} %join_own.1.own), channel_id=1, source_target_pairs={{0,1},{1,2},{2,3},{3,4},{4,5},{5,6},{6,7},{7,8},{8,9},{9,10},{10,1... | collective-permute-start | bytes 786440 | tf_op jit(solution)/shard_map/ppermute | solution.py:19
  9.7 2.0 %collective-permute-start.5 = (bf16[11,64,128]{2,1,0:T(8,128)(2,1)S(1)}, bf16[11,64,128]{2,1,0:T(8,128)(2,1)S(1)}, u32[]{:S(2)}, u32[]{:S(2)}) collective-permute-start(bf16[11,64,128]{2,1,0:T(8,128)(2,1)S(1)} %get-tuple-element.56), channel_id=1, source_target_pairs={{0,16},{16,0},{1,17},{17,1},{2,18},{18,2},{3,19},{19,3},{4,20},{20... | collective-permute-start | bytes 540680 | tf_op jit(solution)/shard_map/ppermute | solution.py:24
  9.9 1.8 %collective-permute-start.6 = (bf16[11,64,128]{2,1,0:T(8,128)(2,1)S(1)}, bf16[11,64,128]{2,1,0:T(8,128)(2,1)S(1)}, u32[]{:S(2)}, u32[]{:S(2)}) collective-permute-start(bf16[11,64,128]{2,1,0:T(8,128)(2,1)S(1)} %get-tuple-element.57), channel_id=1, source_target_pairs={{0,16},{16,0},{1,17},{17,1},{2,18},{18,2},{3,19},{19,3},{4,20},{20... | collective-permute-start | bytes 540680 | tf_op jit(solution)/shard_map/ppermute | solution.py:24
  10.3 1.4 %copy-start.2 = (s32[32]{0:T(128)S(1)}, s32[32]{0:T(128)}, u32[]{:S(2)}) copy-start(s32[32]{0:T(128)} %spans.1) | copy-start | bytes 388
  10.3 1.4 %collective-permute-start.4 = (bf16[10,64,128]{2,1,0:T(8,128)(2,1)S(1)}, bf16[10,64,128]{2,1,0:T(8,128)(2,1)S(1)}, u32[]{:S(2)}, u32[]{:S(2)}) collective-permute-start(bf16[10,64,128]{2,1,0:T(8,128)(2,1)S(1)} %get-tuple-element.55), channel_id=1, source_target_pairs={{0,16},{16,0},{1,17},{17,1},{2,18},{18,2},{3,19},{19,3},{4,20},{20... | collective-permute-start | bytes 491528 | tf_op jit(solution)/shard_map/ppermute | solution.py:24
  13.3 1.6 %collective-permute-start.7 = (bf16[4,64,128]{2,1,0:T(8,128)(2,1)S(1)}, bf16[4,64,128]{2,1,0:T(8,128)(2,1)S(1)}, u32[]{:S(2)}, u32[]{:S(2)}) collective-permute-start(bf16[4,64,128]{2,1,0:T(8,128)(2,1)S(1)} %get-tuple-element.63), channel_id=1, source_target_pairs={{0,16},{16,0},{1,17},{17,1},{2,18},{18,2},{3,19},{19,3},{4,20},{20... | collective-permute-start | bytes 196616 | tf_op jit(solution)/shard_map/ppermute | solution.py:24
  14.0 1.3 %collective-permute-start.8 = (bf16[4,64,128]{2,1,0:T(8,128)(2,1)S(1)}, bf16[4,64,128]{2,1,0:T(8,128)(2,1)S(1)}, u32[]{:S(2)}, u32[]{:S(2)}) collective-permute-start(bf16[4,64,128]{2,1,0:T(8,128)(2,1)S(1)} %get-tuple-element.64), channel_id=1, source_target_pairs={{0,16},{16,0},{1,17},{17,1},{2,18},{18,2},{3,19},{19,3},{4,20},{20... | collective-permute-start | bytes 196616 | tf_op jit(solution)/shard_map/ppermute | solution.py:24
  17.7 11.9 %collective-permute-start.14 = (bf16[2,4,128,128]{3,2,1,0:T(8,128)(2,1)S(1)}, bf16[2,4,128,128]{3,2,1,0:T(8,128)(2,1)S(1)}, u32[]{:S(2)}, u32[]{:S(2)}) collective-permute-start(bf16[2,4,128,128]{3,2,1,0:T(8,128)(2,1)S(1)} %get-tuple-element.96), channel_id=1, source_target_pairs={{0,15},{1,0},{2,1},{3,2},{4,3},{5,4},{6,5},{7,6},{8,7},{9,8},{10,9... | collective-permute-start | bytes 786440 | tf_op jit(solution)/shard_map/ppermute | solution.py:19
  22.8 1.3 %collective-permute-start.9 = (bf16[4,64,128]{2,1,0:T(8,128)(2,1)S(1)}, bf16[4,64,128]{2,1,0:T(8,128)(2,1)S(1)}, u32[]{:S(2)}, u32[]{:S(2)}) collective-permute-start(bf16[4,64,128]{2,1,0:T(8,128)(2,1)S(1)} %get-tuple-element.85), channel_id=1, source_target_pairs={{0,16},{16,0},{1,17},{17,1},{2,18},{18,2},{3,19},{19,3},{4,20},{20... | collective-permute-start | bytes 196616 | tf_op jit(solution)/shard_map/ppermute | solution.py:24
  22.9 1.4 %collective-permute-start.10 = (bf16[4,64,128]{2,1,0:T(8,128)(2,1)S(1)}, bf16[4,64,128]{2,1,0:T(8,128)(2,1)S(1)}, u32[]{:S(2)}, u32[]{:S(2)}) collective-permute-start(bf16[4,64,128]{2,1,0:T(8,128)(2,1)S(1)} %get-tuple-element.86), channel_id=1, source_target_pairs={{0,16},{16,0},{1,17},{17,1},{2,18},{18,2},{3,19},{19,3},{4,20},{20... | collective-permute-start | bytes 196616 | tf_op jit(solution)/shard_map/ppermute | solution.py:24
  24.3 9.3 %collective-permute-start.16 = (bf16[2,8,64,128]{3,2,1,0:T(8,128)(2,1)S(1)}, bf16[2,8,64,128]{3,2,1,0:T(8,128)(2,1)S(1)}, u32[]{:S(2)}, u32[]{:S(2)}) collective-permute-start(bf16[2,8,64,128]{3,2,1,0:T(8,128)(2,1)S(1)} %join_two.1.after), channel_id=1, source_target_pairs={{0,14},{1,15},{2,0},{3,1},{4,2},{5,3},{6,4},{7,5},{8,6},{9,7},{10,... | collective-permute-start | bytes 786440 | tf_op jit(solution)/shard_map/ppermute | solution.py:19
  29.0 2.0 %collective-permute-start.12 = (bf16[11,64,128]{2,1,0:T(8,128)(2,1)S(1)}, bf16[11,64,128]{2,1,0:T(8,128)(2,1)S(1)}, u32[]{:S(2)}, u32[]{:S(2)}) collective-permute-start(bf16[11,64,128]{2,1,0:T(8,128)(2,1)S(1)} %get-tuple-element.91), channel_id=1, source_target_pairs={{0,16},{16,0},{1,17},{17,1},{2,18},{18,2},{3,19},{19,3},{4,20},{20... | collective-permute-start | bytes 540680 | tf_op jit(solution)/shard_map/ppermute | solution.py:24
  29.0 1.9 %collective-permute-start.13 = (bf16[11,64,128]{2,1,0:T(8,128)(2,1)S(1)}, bf16[11,64,128]{2,1,0:T(8,128)(2,1)S(1)}, u32[]{:S(2)}, u32[]{:S(2)}) collective-permute-start(bf16[11,64,128]{2,1,0:T(8,128)(2,1)S(1)} %get-tuple-element.92), channel_id=1, source_target_pairs={{0,16},{16,0},{1,17},{17,1},{2,18},{18,2},{3,19},{19,3},{4,20},{20... | collective-permute-start | bytes 540680 | tf_op jit(solution)/shard_map/ppermute | solution.py:24
  29.5 1.4 %collective-permute-start.11 = (bf16[10,64,128]{2,1,0:T(8,128)(2,1)S(1)}, bf16[10,64,128]{2,1,0:T(8,128)(2,1)S(1)}, u32[]{:S(2)}, u32[]{:S(2)}) collective-permute-start(bf16[10,64,128]{2,1,0:T(8,128)(2,1)S(1)} %get-tuple-element.90), channel_id=1, source_target_pairs={{0,16},{16,0},{1,17},{17,1},{2,18},{18,2},{3,19},{19,3},{4,20},{20... | collective-permute-start | bytes 491528 | tf_op jit(solution)/shard_map/ppermute | solution.py:24
  29.7 4.0 %collective-permute-start.15 = (bf16[2,4,64,128]{3,2,1,0:T(8,128)(2,1)S(1)}, bf16[2,4,64,128]{3,2,1,0:T(8,128)(2,1)S(1)}, u32[]{:S(2)}, u32[]{:S(2)}) collective-permute-start(bf16[2,4,64,128]{3,2,1,0:T(8,128)(2,1)S(1)} %get-tuple-element.98), channel_id=1, source_target_pairs={{0,16},{16,0},{1,17},{17,1},{2,18},{18,2},{3,19},{19,3},{4,20},{20... | collective-permute-start | bytes 393224 | tf_op jit(solution)/shard_map/ppermute | solution.py:24

commit v23 on v16

--- a/solution.py
+++ b/solution.py
@@ -281,7 +281,7 @@
 
 def two_backward_kernel(
     query_head, grad_head, near_weights, near_prob_grad, near_factor, row_delta,
-    two_grad, two_mine, send_keys, send_values,
+    two_grad, two_mine, two_send,
 ):
     chunks = near_weights.shape[0]
     groups, length, width = two_mine.shape[1:]
@@ -293,11 +293,9 @@
         return score_grad, prob.astype(jnp.bfloat16)
 
     def store(g, key_part, value_part):
-        for index, (part, send) in enumerate(
-            ((key_part * width ** (-0.5), send_keys), (value_part, send_values))
-        ):
+        for index, part in enumerate((key_part * width ** (-0.5), value_part)):
             two_mine[index, g] = part[:length].astype(jnp.bfloat16)
-            send[g] = part[length:].astype(jnp.bfloat16)
+            two_send[index, g] = part[length:].astype(jnp.bfloat16)
 
     accumulate = accumulator(query_head, grad_head, chunks, groups, store)
     pipelined(chunks, differentiate, accumulate)
@@ -324,11 +322,10 @@
     pipelined(chunks, differentiate, accumulate)
 
 
-def join_two_kernel(two_mine, other_keys, other_values, two_part):
+def join_two_kernel(two_mine, two_other, two_part):
     groups = two_mine.shape[1]
     two_part[:, my_heads(groups)] = two_mine[...]
-    two_part[0, other_heads(groups)] = other_keys[...]
-    two_part[1, other_heads(groups)] = other_values[...]
+    two_part[:, other_heads(groups)] = two_other[...]
 
 
 def query_kernel(
@@ -466,17 +463,17 @@
         (first, query_head, grad_head, back_one, grad_rows, near_max, near_total, near_out),
     )
     one_total = shifted(one_part, "seq", -1)
-    two_grad, part_mine, *part_sends = call(
+    two_grad, part_mine, part_send = call(
         two_backward_kernel,
         "two_backward",
-        [rows_of(tokens, half), half_pair, half_block, half_block],
+        [rows_of(tokens, half), half_pair, half_pair],
         (query_head, grad_head, near_weights, near_prob_grad, near_factor, row_delta),
     )
     (two_part,) = call(
         join_two_kernel,
         "join_two",
         [whole_pair],
-        (part_mine, *[swapped(send, "head") for send in part_sends]),
+        (part_mine, swapped(part_send, "head")),
     )
     two_total = shifted(two_part, "seq", -2)
     own_grad, own_part = call(

time: 34.6 us -> 34.5 us (level)
  starting transfers between devices: 17.6 us -> 16.9 us
  waiting for transfers between devices: 6.59 us -> 7.21 us
    ppermute x13 -> x12, starting transfers between devices: 3.5 us -> 3.01 us  [swapped(): return lax.ppermute(block, axis, [(i, count - 1 - i) for i in range(count)])]
    ppermute x13 -> x12, waiting for transfers between devices: 4.14 us -> 4.57 us  [swapped(): return lax.ppermute(block, axis, [(i, count - 1 - i) for i in range(count)])]
  transfers between devices with their start and end apart: 17 -> 16, of which waited for: 10 -> 9; matrix products, arithmetic and copies ran while one was open for 0% -> 0% of each run, Pallas kernels for 16% -> 16%
where the time goes in v23:
time: 34.5 us; the launch traced here: 34.3 us
  starting transfers between devices  16.9 us (49%)
  Pallas kernels  7.68 us (22%)
  waiting for transfers between devices  7.21 us (21%)
  between operations  1.44 us (4%)
  other arithmetic  1.05 us (3%)
    ppermute x4, starting transfers between devices, shifted(): return lax.ppermute(block, axis, route)  13.9 us
    pallas_call x14, Pallas kernels, call(): pl.pallas_call(kernel, out_shape=tuple((jax.ShapeDtypeStruct(shape, kind)...  7.68 us
    ppermute x12, waiting for transfers between devices, swapped(): return lax.ppermute(block, axis, [(i, count - 1 - i) for i in range(count)])  4.57 us
    ppermute x12, starting transfers between devices, swapped(): return lax.ppermute(block, axis, [(i, count - 1 - i) for i in range(count)])  3.01 us
    ppermute x4, waiting for transfers between devices, shifted(): return lax.ppermute(block, axis, route)  2.64 us
    another operation x1, other arithmetic, shards(): own = jnp.stack([key_matrix, value_matrix])  1.05 us
  transfers between devices with their start and end apart: 16, of which 9 were waited for; matrix products, arithmetic and copies ran while one was open for 0% of the time, Pallas kernels for 16%

profile of v23, /device:TPU:0, one launch (start us, length us, event | category | flops | bytes accessed | tf_op | source)
XLA Modules:
  0.0 34.3 jit_solution(16793603928137292796)
XLA Ops:
  0.6 1.1 %pad_maximum_fusion.block.own.after = bf16[2,8,64,128]{3,2,1,0:T(8,128)(2,1)S(1)} fusion(bf16[1,8,64,128]{3,2,1,0:T(8,128)(2,1)} %bitcast.2, bf16[1,8,64,128]{3,2,1,0:T(8,128)(2,1)} %bitcast.3), kind=kLoop, calls=%fused_computation | loop fusion | flops 131072 | bytes 524288 | tf_op jit(solution)/shard_map/stack | solution.py:420
  1.7 3.0 %collective-permute-start.3 = (bf16[2,8,64,128]{3,2,1,0:T(8,128)(2,1)S(1)}, bf16[2,8,64,128]{3,2,1,0:T(8,128)(2,1)S(1)}, u32[]{:S(2)}, u32[]{:S(2)}) collective-permute-start(bf16[2,8,64,128]{3,2,1,0:T(8,128)(2,1)S(1)} %pad_maximum_fusion.block.own.after), channel_id=1, source_target_pairs={{0,2},{1,3},{2,4},{3,5},{4,6},{5,7},{6,8},{7,9},{8,10},{9,11},{10,... | collective-permute-start | bytes 786440 | tf_op jit(solution)/shard_map/ppermute | solution.py:19
  4.8 0.5 %collective-permute-start.1 = (bf16[4,64,128]{2,1,0:T(8,128)(2,1)S(1)}, bf16[4,64,128]{2,1,0:T(8,128)(2,1)S(1)}, u32[]{:S(2)}, u32[]{:S(2)}) collective-permute-start(bf16[4,64,128]{2,1,0:T(8,128)(2,1)S(1)} %get-tuple-element.53), channel_id=1, source_target_pairs={{0,16},{16,0},{1,17},{17,1},{2,18},{18,2},{3,19},{19,3},{4,20},{20... | collective-permute-start | bytes 196616 | tf_op jit(solution)/shard_map/ppermute | solution.py:24
  5.3 0.7 %collective-permute-done.other_keys = bf16[4,64,128]{2,1,0:T(8,128)(2,1)S(1)} collective-permute-done((bf16[4,64,128]{2,1,0:T(8,128)(2,1)S(1)}, bf16[4,64,128]{2,1,0:T(8,128)(2,1)S(1)}, u32[]{:S(2)}, u32[]{:S(2)}) %collective-permute-start) | collective-permute-done | bytes 65568 | tf_op jit(solution)/shard_map/ppermute | solution.py:24
  6.2 3.4 %collective-permute-start.2 = (bf16[2,4,128,128]{3,2,1,0:T(8,128)(2,1)S(1)}, bf16[2,4,128,128]{3,2,1,0:T(8,128)(2,1)S(1)}, u32[]{:S(2)}, u32[]{:S(2)}) collective-permute-start(bf16[2,4,128,128]{3,2,1,0:T(8,128)(2,1)S(1)} %join_own.1.own), channel_id=1, source_target_pairs={{0,1},{1,2},{2,3},{3,4},{4,5},{5,6},{6,7},{7,8},{8,9},{9,10},{10,1... | collective-permute-start | bytes 786440 | tf_op jit(solution)/shard_map/ppermute | solution.py:19
  11.0 0.7 %collective-permute-done.4.first_third = bf16[10,64,128]{2,1,0:T(8,128)(2,1)S(1)} collective-permute-done((bf16[10,64,128]{2,1,0:T(8,128)(2,1)S(1)}, bf16[10,64,128]{2,1,0:T(8,128)(2,1)S(1)}, u32[]{:S(2)}, u32[]{:S(2)}) %collective-permute-start.4) | collective-permute-done | bytes 163872 | tf_op jit(solution)/shard_map/ppermute | solution.py:24
  11.7 1.5 %own_block.1 = (bf16[16,128,128]{2,1,0:T(8,128)(2,1)S(1)}, bf16[16,128,128]{2,1,0:T(8,128)(2,1)S(1)}, bf16[8,128,256]{2,1,0:T(8,128)(2,1)S(1)}, s32[8,1,256]{2,1...) custom-call(s32[32]{0:T(128)S(1)} %copy-done.2, ...), custom_call_target="tpu_custom_call" | custom-call | flops 1 | tf_op jit(solution)/shard_map/own_block/pallas_call | solution.py:397
  13.3 0.8 %collective-permute-done.3.block.back_two = bf16[2,8,64,128]{3,2,1,0:T(8,128)(2,1)S(1)} collective-permute-done((bf16[2,8,64,128]{3,2,1,0:T(8,128)(2,1)S(1)}, bf16[2,8,64,128]{3,2,1,0:T(8,128)(2,1)S(1)}, u32[]{:S(2)}, u32[]{:S(2)}) %collective-permute-start.3) | collective-permute-done | bytes 262176 | tf_op jit(solution)/shard_map/ppermute | solution.py:19
  14.2 0.5 %collective-permute-start.8 = (bf16[4,64,128]{2,1,0:T(8,128)(2,1)S(1)}, bf16[4,64,128]{2,1,0:T(8,128)(2,1)S(1)}, u32[]{:S(2)}, u32[]{:S(2)}) collective-permute-start(bf16[4,64,128]{2,1,0:T(8,128)(2,1)S(1)} %get-tuple-element.63), channel_id=1, source_target_pairs={{0,16},{16,0},{1,17},{17,1},{2,18},{18,2},{3,19},{19,3},{4,20},{20... | collective-permute-start | bytes 196616 | tf_op jit(solution)/shard_map/ppermute | solution.py:24
  14.7 0.7 %collective-permute-done.7.two_keys = bf16[4,64,128]{2,1,0:T(8,128)(2,1)S(1)} collective-permute-done((bf16[4,64,128]{2,1,0:T(8,128)(2,1)S(1)}, bf16[4,64,128]{2,1,0:T(8,128)(2,1)S(1)}, u32[]{:S(2)}, u32[]{:S(2)}) %collective-permute-start.7) | collective-permute-done | bytes 65568 | tf_op jit(solution)/shard_map/ppermute | solution.py:24
  15.6 0.9 %near_forward.1 = (f32[8,1,256]{2,1,0:T(1,128)S(1)}, f32[8,1,256]{2,1,0:T(1,128)S(1)}, f32[8,128,256]{2,1,0:T(8,128)S(1)}, f32[8,128,256]{2,1,0:T(8,128)S(1)}, f...) custom-call(s32[8,1,256]{2,1,0:T(1,128)S(1)} %get-tuple-element.58.first, ...), custom_call_target="tpu_custom_call" | custom-call | flops 1 | tf_op jit(solution)/shard_map/near_forward/pallas_call | solution.py:397
  16.5 1.5 %last_forward_backward.1 = (bf16[8,128,256]{2,1,0:T(8,128)(2,1)S(1)}, f32[8,1,256]{2,1,0:T(1,128)S(1)}, f32[8,1,256]{2,1,0:T(1,128)S(1)}, bf16[8,128,256]{2,1,0:T(8,128)(2,1)S(1)}, bf16[2,4,128,128]{3,2,1,0:T(8,128)(2,1)S(1)}) custom-call(s32[8,1,256]{2,1,0:T(1,128)S(1)} %get-tuple-element.58.first, bf16[16,128,128]{2,1,0:T(8,128)(2,1)S(1)} %get-tuple-element.59.query_head, ...), custom_call_target="tpu_custom_call" | custom-call | flops 1 | tf_op jit(solution)/shard_map/last_forward_backward/pallas_call | solution.py:397
  18.1 4.4 %collective-permute-start.13 = (bf16[2,4,128,128]{3,2,1,0:T(8,128)(2,1)S(1)}, bf16[2,4,128,128]{3,2,1,0:T(8,128)(2,1)S(1)}, u32[]{:S(2)}, u32[]{:S(2)}) collective-permute-start(bf16[2,4,128,128]{3,2,1,0:T(8,128)(2,1)S(1)} %get-tuple-element.94), channel_id=1, source_target_pairs={{0,15},{1,0},{2,1},{3,2},{4,3},{5,4},{6,5},{7,6},{8,7},{9,8},{10,9... | collective-permute-start | bytes 786440 | tf_op jit(solution)/shard_map/ppermute | solution.py:19
  22.4 0.5 %two_backward.1 = (bf16[8,128,256]{2,1,0:T(8,128)(2,1)S(1)}, bf16[2,4,64,128]{3,2,1,0:T(8,128)(2,1)S(1)}, bf16[2,4,64,128]{3,2,1,0:T(8,128)(2,1)S(1)}) custom-call(bf16[16,128,128]{2,1,0:T(8,128)(2,1)S(1)} %get-tuple-element.59.query_head, bf16[16,128,128]{2,1,0:T(8,128)(2,1)S(1)} %get-tuple-element.60.grad_head, ...), custom_call_target="tpu_custom_call" | custom-call | flops 1 | tf_op jit(solution)/shard_map/two_backward/pallas_call | solution.py:397
  23.0 1.3 %collective-permute-done.9.two_other = bf16[2,4,64,128]{3,2,1,0:T(8,128)(2,1)S(1)} collective-permute-done((bf16[2,4,64,128]{3,2,1,0:T(8,128)(2,1)S(1)}, bf16[2,4,64,128]{3,2,1,0:T(8,128)(2,1)S(1)}, u32[]{:S(2)}, u32[]{:S(2)}) %collective-permute-start.9) | collective-permute-done | bytes 131104 | tf_op jit(solution)/shard_map/ppermute | solution.py:24
  24.4 3.1 %collective-permute-start.15 = (bf16[2,8,64,128]{3,2,1,0:T(8,128)(2,1)S(1)}, bf16[2,8,64,128]{3,2,1,0:T(8,128)(2,1)S(1)}, u32[]{:S(2)}, u32[]{:S(2)}) collective-permute-start(bf16[2,8,64,128]{3,2,1,0:T(8,128)(2,1)S(1)} %join_two.1.after), channel_id=1, source_target_pairs={{0,14},{1,15},{2,0},{3,1},{4,2},{5,3},{6,4},{7,5},{8,6},{9,7},{10,... | collective-permute-start | bytes 786440 | tf_op jit(solution)/shard_map/ppermute | solution.py:19
  27.5 0.5 %own_backward.1 = (bf16[8,128,256]{2,1,0:T(8,128)(2,1)S(1)}, f32[2,4,128,128]{3,2,1,0:T(8,128)S(1)}) custom-call(bf16[16,128,128]{2,1,0:T(8,128)(2,1)S(1)} %get-tuple-element.59.query_head, bf16[16,128,128]{2,1,0:T(8,128)(2,1)S(1)} %get-tuple-element.60.grad_head, f32[8,128,256]{2,1,0:T(8,128)S(1)} %get-tuple-element.80.own_weights, ...), custom_call_target="tpu_custom_call" | custom-call | flops 1 | tf_op jit(solution)/shard_map/own_backward/pallas_call | solution.py:397
  28.0 0.8 %query_grad.1 = (bf16[16,64,128]{2,1,0:T(8,128)(2,1)S(1)}, bf16[16,64,128]{2,1,0:T(8,128)(2,1)S(1)}, bf16[10,64,128]{2,1,0:T(8,128)(2,1)S(1)}, bf16[11,64,128]{2,1,0:T(8,128)(2,1)S(1)}, bf16[11,64,128]{2,1,0:T(8,128)(2,1)S(1)}) custom-call(bf16[2,4,128,128]{3,2,1,0:T(8,128)(2,1)S(1)} %join_own.1.own, ...), custom_call_target="tpu_custom_call" | custom-call | flops 1 | tf_op jit(solution)/shard_map/query_grad/pallas_call | solution.py:397
  28.8 0.4 %collective-permute-start.12 = (bf16[11,64,128]{2,1,0:T(8,128)(2,1)S(1)}, bf16[11,64,128]{2,1,0:T(8,128)(2,1)S(1)}, u32[]{:S(2)}, u32[]{:S(2)}) collective-permute-start(bf16[11,64,128]{2,1,0:T(8,128)(2,1)S(1)} %get-tuple-element.90), channel_id=1, source_target_pairs={{0,16},{16,0},{1,17},{17,1},{2,18},{18,2},{3,19},{19,3},{4,20},{20... | collective-permute-start | bytes 540680 | tf_op jit(solution)/shard_map/ppermute | solution.py:24
  29.4 0.5 %collective-permute-start.14 = (bf16[2,4,64,128]{3,2,1,0:T(8,128)(2,1)S(1)}, bf16[2,4,64,128]{3,2,1,0:T(8,128)(2,1)S(1)}, u32[]{:S(2)}, u32[]{:S(2)}) collective-permute-start(bf16[2,4,64,128]{3,2,1,0:T(8,128)(2,1)S(1)} %get-tuple-element.96), channel_id=1, source_target_pairs={{0,16},{16,0},{1,17},{17,1},{2,18},{18,2},{3,19},{19,3},{4,20},{20... | collective-permute-start | bytes 393224 | tf_op jit(solution)/shard_map/ppermute | solution.py:24
  29.9 0.8 %collective-permute-done.10.first_third = bf16[10,64,128]{2,1,0:T(8,128)(2,1)S(1)} collective-permute-done((bf16[10,64,128]{2,1,0:T(8,128)(2,1)S(1)}, bf16[10,64,128]{2,1,0:T(8,128)(2,1)S(1)}, u32[]{:S(2)}, u32[]{:S(2)}) %collective-permute-start.10) | collective-permute-done | bytes 163872 | tf_op jit(solution)/shard_map/ppermute | solution.py:24
  30.7 1.0 %assemble.1 = (bf16[32,64,128]{2,1,0:T(8,128)(2,1)}, bf16[32,64,128]{2,1,0:T(8,128)(2,1)}, f32[8,128]{1,0:T(8,128)S(1)}) custom-call(bf16[16,64,128]{2,1,0:T(8,128)(2,1)S(1)} %get-tuple-element.86.out_mine, bf16[16,64,128]{2,1,0:T(8,128)(2,1)S(1)} %get-tuple-element.87.query_mine, bf16[10,64,128]{2,1,0:T(8,128)(2,1)S(1)} %collective-permute-done.10.first_third, ...), custom_call_target="tpu_custom_call" | custom-call | flops 1 | tf_op jit(solution)/shard_map/assemble/pallas_call | solution.py:397
  31.8 1.8 %collective-permute-done.15.two_total = bf16[2,8,64,128]{3,2,1,0:T(8,128)(2,1)S(1)} collective-permute-done((bf16[2,8,64,128]{3,2,1,0:T(8,128)(2,1)S(1)}, bf16[2,8,64,128]{3,2,1,0:T(8,128)(2,1)S(1)}, u32[]{:S(2)}, u32[]{:S(2)}) %collective-permute-start.15) | collective-permute-done | bytes 262176 | tf_op jit(solution)/shard_map/ppermute | solution.py:19
  33.6 0.7 %total.1 = (bf16[8,64,128]{2,1,0:T(8,128)(2,1)}, bf16[8,64,128]{2,1,0:T(8,128)(2,1)}) custom-call(f32[2,4,64,128]{3,2,1,0:T(8,128)S(1)} %get-tuple-element.95.sum_mine, bf16[2,4,64,128]{3,2,1,0:T(8,128)(2,1)S(1)} %collective-permute-done.14.sum_other, bf16[2,8,64,128]{3,2,1,0:T(8,128)(2,1)S(1)} %collective-permute-done.15.two_total, ...), custom_call_target="tpu_custom_call" | custom-call | flops 1 | tf_op jit(solution)/shard_map/total/pallas_call | solution.py:397
  (29 shorter events, 1.6 us)
Async XLA Ops:
  0.6 9.0 %copy-start.1 = (bf16[32,64,128]{2,1,0:T(8,128)(2,1)S(1)}, bf16[32,64,128]{2,1,0:T(8,128)(2,1)}, u32[]{:S(2)}) copy-start(bf16[32,64,128]{2,1,0:T(8,128)(2,1)} %grads.3) | copy-start | bytes 1572868
  1.7 8.0 %copy-start = (bf16[32,64,128]{2,1,0:T(8,128)(2,1)S(1)}, bf16[32,64,128]{2,1,0:T(8,128)(2,1)}, u32[]{:S(2)}) copy-start(bf16[32,64,128]{2,1,0:T(8,128)(2,1)} %queries.3) | copy-start | bytes 1572868
  1.7 12.4 %collective-permute-start.3 = (bf16[2,8,64,128]{3,2,1,0:T(8,128)(2,1)S(1)}, bf16[2,8,64,128]{3,2,1,0:T(8,128)(2,1)S(1)}, u32[]{:S(2)}, u32[]{:S(2)}) collective-permute-start(bf16[2,8,64,128]{3,2,1,0:T(8,128)(2,1)S(1)} %pad_maximum_fusion.block.own.after), channel_id=1, source_target_pairs={{0,2},{1,3},{2,4},{3,5},{4,6},{5,7},{6,8},{7,9},{8,10},{9,11},{10,... | collective-permute-start | bytes 786440 | tf_op jit(solution)/shard_map/ppermute | solution.py:19
  4.7 1.3 %collective-permute-start = (bf16[4,64,128]{2,1,0:T(8,128)(2,1)S(1)}, bf16[4,64,128]{2,1,0:T(8,128)(2,1)S(1)}, u32[]{:S(2)}, u32[]{:S(2)}) collective-permute-start(bf16[4,64,128]{2,1,0:T(8,128)(2,1)S(1)} %get-tuple-element.52), channel_id=1, source_target_pairs={{0,16},{16,0},{1,17},{17,1},{2,18},{18,2},{3,19},{19,3},{4,20},{20... | collective-permute-start | bytes 196616 | tf_op jit(solution)/shard_map/ppermute | solution.py:24
  4.8 1.4 %collective-permute-start.1 = (bf16[4,64,128]{2,1,0:T(8,128)(2,1)S(1)}, bf16[4,64,128]{2,1,0:T(8,128)(2,1)S(1)}, u32[]{:S(2)}, u32[]{:S(2)}) collective-permute-start(bf16[4,64,128]{2,1,0:T(8,128)(2,1)S(1)} %get-tuple-element.53), channel_id=1, source_target_pairs={{0,16},{16,0},{1,17},{17,1},{2,18},{18,2},{3,19},{19,3},{4,20},{20... | collective-permute-start | bytes 196616 | tf_op jit(solution)/shard_map/ppermute | solution.py:24
  6.2 10.3 %collective-permute-start.2 = (bf16[2,4,128,128]{3,2,1,0:T(8,128)(2,1)S(1)}, bf16[2,4,128,128]{3,2,1,0:T(8,128)(2,1)S(1)}, u32[]{:S(2)}, u32[]{:S(2)}) collective-permute-start(bf16[2,4,128,128]{3,2,1,0:T(8,128)(2,1)S(1)} %join_own.1.own), channel_id=1, source_target_pairs={{0,1},{1,2},{2,3},{3,4},{4,5},{5,6},{6,7},{7,8},{8,9},{9,10},{10,1... | collective-permute-start | bytes 786440 | tf_op jit(solution)/shard_map/ppermute | solution.py:19
  9.7 2.0 %collective-permute-start.5 = (bf16[11,64,128]{2,1,0:T(8,128)(2,1)S(1)}, bf16[11,64,128]{2,1,0:T(8,128)(2,1)S(1)}, u32[]{:S(2)}, u32[]{:S(2)}) collective-permute-start(bf16[11,64,128]{2,1,0:T(8,128)(2,1)S(1)} %get-tuple-element.55), channel_id=1, source_target_pairs={{0,16},{16,0},{1,17},{17,1},{2,18},{18,2},{3,19},{19,3},{4,20},{20... | collective-permute-start | bytes 540680 | tf_op jit(solution)/shard_map/ppermute | solution.py:24
  9.9 1.8 %collective-permute-start.6 = (bf16[11,64,128]{2,1,0:T(8,128)(2,1)S(1)}, bf16[11,64,128]{2,1,0:T(8,128)(2,1)S(1)}, u32[]{:S(2)}, u32[]{:S(2)}) collective-permute-start(bf16[11,64,128]{2,1,0:T(8,128)(2,1)S(1)} %get-tuple-element.56), channel_id=1, source_target_pairs={{0,16},{16,0},{1,17},{17,1},{2,18},{18,2},{3,19},{19,3},{4,20},{20... | collective-permute-start | bytes 540680 | tf_op jit(solution)/shard_map/ppermute | solution.py:24
  10.3 1.4 %copy-start.2 = (s32[32]{0:T(128)S(1)}, s32[32]{0:T(128)}, u32[]{:S(2)}) copy-start(s32[32]{0:T(128)} %spans.1) | copy-start | bytes 388
  10.3 1.4 %collective-permute-start.4 = (bf16[10,64,128]{2,1,0:T(8,128)(2,1)S(1)}, bf16[10,64,128]{2,1,0:T(8,128)(2,1)S(1)}, u32[]{:S(2)}, u32[]{:S(2)}) collective-permute-start(bf16[10,64,128]{2,1,0:T(8,128)(2,1)S(1)} %get-tuple-element.54), channel_id=1, source_target_pairs={{0,16},{16,0},{1,17},{17,1},{2,18},{18,2},{3,19},{19,3},{4,20},{20... | collective-permute-start | bytes 491528 | tf_op jit(solution)/shard_map/ppermute | solution.py:24
  14.1 1.3 %collective-permute-start.7 = (bf16[4,64,128]{2,1,0:T(8,128)(2,1)S(1)}, bf16[4,64,128]{2,1,0:T(8,128)(2,1)S(1)}, u32[]{:S(2)}, u32[]{:S(2)}) collective-permute-start(bf16[4,64,128]{2,1,0:T(8,128)(2,1)S(1)} %get-tuple-element.62), channel_id=1, source_target_pairs={{0,16},{16,0},{1,17},{17,1},{2,18},{18,2},{3,19},{19,3},{4,20},{20... | collective-permute-start | bytes 196616 | tf_op jit(solution)/shard_map/ppermute | solution.py:24
  14.2 1.4 %collective-permute-start.8 = (bf16[4,64,128]{2,1,0:T(8,128)(2,1)S(1)}, bf16[4,64,128]{2,1,0:T(8,128)(2,1)S(1)}, u32[]{:S(2)}, u32[]{:S(2)}) collective-permute-start(bf16[4,64,128]{2,1,0:T(8,128)(2,1)S(1)} %get-tuple-element.63), channel_id=1, source_target_pairs={{0,16},{16,0},{1,17},{17,1},{2,18},{18,2},{3,19},{19,3},{4,20},{20... | collective-permute-start | bytes 196616 | tf_op jit(solution)/shard_map/ppermute | solution.py:24
  18.1 11.3 %collective-permute-start.13 = (bf16[2,4,128,128]{3,2,1,0:T(8,128)(2,1)S(1)}, bf16[2,4,128,128]{3,2,1,0:T(8,128)(2,1)S(1)}, u32[]{:S(2)}, u32[]{:S(2)}) collective-permute-start(bf16[2,4,128,128]{3,2,1,0:T(8,128)(2,1)S(1)} %get-tuple-element.94), channel_id=1, source_target_pairs={{0,15},{1,0},{2,1},{3,2},{4,3},{5,4},{6,5},{7,6},{8,7},{9,8},{10,9... | collective-permute-start | bytes 786440 | tf_op jit(solution)/shard_map/ppermute | solution.py:19
  22.9 1.4 %collective-permute-start.9 = (bf16[2,4,64,128]{3,2,1,0:T(8,128)(2,1)S(1)}, bf16[2,4,64,128]{3,2,1,0:T(8,128)(2,1)S(1)}, u32[]{:S(2)}, u32[]{:S(2)}) collective-permute-start(bf16[2,4,64,128]{3,2,1,0:T(8,128)(2,1)S(1)} %get-tuple-element.84), channel_id=1, source_target_pairs={{0,16},{16,0},{1,17},{17,1},{2,18},{18,2},{3,19},{19,3},{4,20},{20... | collective-permute-start | bytes 393224 | tf_op jit(solution)/shard_map/ppermute | solution.py:24
  24.4 9.2 %collective-permute-start.15 = (bf16[2,8,64,128]{3,2,1,0:T(8,128)(2,1)S(1)}, bf16[2,8,64,128]{3,2,1,0:T(8,128)(2,1)S(1)}, u32[]{:S(2)}, u32[]{:S(2)}) collective-permute-start(bf16[2,8,64,128]{3,2,1,0:T(8,128)(2,1)S(1)} %join_two.1.after), channel_id=1, source_target_pairs={{0,14},{1,15},{2,0},{3,1},{4,2},{5,3},{6,4},{7,5},{8,6},{9,7},{10,... | collective-permute-start | bytes 786440 | tf_op jit(solution)/shard_map/ppermute | solution.py:19
  28.7 2.0 %collective-permute-start.11 = (bf16[11,64,128]{2,1,0:T(8,128)(2,1)S(1)}, bf16[11,64,128]{2,1,0:T(8,128)(2,1)S(1)}, u32[]{:S(2)}, u32[]{:S(2)}) collective-permute-start(bf16[11,64,128]{2,1,0:T(8,128)(2,1)S(1)} %get-tuple-element.89), channel_id=1, source_target_pairs={{0,16},{16,0},{1,17},{17,1},{2,18},{18,2},{3,19},{19,3},{4,20},{20... | collective-permute-start | bytes 540680 | tf_op jit(solution)/shard_map/ppermute | solution.py:24
  28.8 1.9 %collective-permute-start.12 = (bf16[11,64,128]{2,1,0:T(8,128)(2,1)S(1)}, bf16[11,64,128]{2,1,0:T(8,128)(2,1)S(1)}, u32[]{:S(2)}, u32[]{:S(2)}) collective-permute-start(bf16[11,64,128]{2,1,0:T(8,128)(2,1)S(1)} %get-tuple-element.90), channel_id=1, source_target_pairs={{0,16},{16,0},{1,17},{17,1},{2,18},{18,2},{3,19},{19,3},{4,20},{20... | collective-permute-start | bytes 540680 | tf_op jit(solution)/shard_map/ppermute | solution.py:24
  29.3 1.4 %collective-permute-start.10 = (bf16[10,64,128]{2,1,0:T(8,128)(2,1)S(1)}, bf16[10,64,128]{2,1,0:T(8,128)(2,1)S(1)}, u32[]{:S(2)}, u32[]{:S(2)}) collective-permute-start(bf16[10,64,128]{2,1,0:T(8,128)(2,1)S(1)} %get-tuple-element.88), channel_id=1, source_target_pairs={{0,16},{16,0},{1,17},{17,1},{2,18},{18,2},{3,19},{19,3},{4,20},{20... | collective-permute-start | bytes 491528 | tf_op jit(solution)/shard_map/ppermute | solution.py:24
  29.4 2.3 %collective-permute-start.14 = (bf16[2,4,64,128]{3,2,1,0:T(8,128)(2,1)S(1)}, bf16[2,4,64,128]{3,2,1,0:T(8,128)(2,1)S(1)}, u32[]{:S(2)}, u32[]{:S(2)}) collective-permute-start(bf16[2,4,64,128]{3,2,1,0:T(8,128)(2,1)S(1)} %get-tuple-element.96), channel_id=1, source_target_pairs={{0,16},{16,0},{1,17},{17,1},{2,18},{18,2},{3,19},{19,3},{4,20},{20... | collective-permute-start | bytes 393224 | tf_op jit(solution)/shard_map/ppermute | solution.py:24

commit v24 on v16

--- a/solution.py
+++ b/solution.py
@@ -256,7 +256,7 @@
 def pipelined(chunks, *stages):
     ready = [{} for _ in range(len(stages) + 1)]
     for step in range(chunks + len(stages) - 1):
-        for depth, stage in enumerate(stages):
+        for depth, stage in reversed(list(enumerate(stages))):
             n = step - depth
             if 0 <= n < chunks:
                 ready[depth + 1][n] = stage(n, *ready[depth].pop(n, ())) or ()

time: 34.6 us -> 34.9 us (level)
  Pallas kernels: 7.69 us -> 8.25 us
    pallas_call x14, Pallas kernels: 7.69 us -> 8.25 us  [call(): pl.pallas_call(kernel, out_shape=tuple((jax.ShapeDtypeStruct(shape, kind)...]
  transfers between devices with their start and end apart: 17 -> 17, of which waited for: 10 -> 10; matrix products, arithmetic and copies ran while one was open for 0% -> 0% of each run, Pallas kernels for 16% -> 17%
where the time goes in v24:
time: 34.9 us; the launch traced here: 34.7 us
  starting transfers between devices  17.6 us (50%)
  Pallas kernels  8.25 us (24%)
  waiting for transfers between devices  6.35 us (18%)
  between operations  1.44 us (4%)
  other arithmetic  1.05 us (3%)
    ppermute x4, starting transfers between devices, shifted(): return lax.ppermute(block, axis, route)  14.1 us
    pallas_call x14, Pallas kernels, call(): pl.pallas_call(kernel, out_shape=tuple((jax.ShapeDtypeStruct(shape, kind)...  8.25 us
    ppermute x13, waiting for transfers between devices, swapped(): return lax.ppermute(block, axis, [(i, count - 1 - i) for i in range(count)])  4.14 us
    ppermute x13, starting transfers between devices, swapped(): return lax.ppermute(block, axis, [(i, count - 1 - i) for i in range(count)])  3.5 us
    ppermute x4, waiting for transfers between devices, shifted(): return lax.ppermute(block, axis, route)  2.21 us
    another operation x1, other arithmetic, shards(): own = jnp.stack([key_matrix, value_matrix])  1.05 us
  transfers between devices with their start and end apart: 17, of which 10 were waited for; matrix products, arithmetic and copies ran while one was open for 0% of the time, Pallas kernels for 17%

profile of v24, /device:TPU:0, one launch (start us, length us, event | category | flops | bytes accessed | tf_op | source)
XLA Modules:
  0.0 34.7 jit_solution(8201159636981343149)
XLA Ops:
  0.6 1.1 %pad_maximum_fusion.block.own.after = bf16[2,8,64,128]{3,2,1,0:T(8,128)(2,1)S(1)} fusion(bf16[1,8,64,128]{3,2,1,0:T(8,128)(2,1)} %bitcast.2, bf16[1,8,64,128]{3,2,1,0:T(8,128)(2,1)} %bitcast.3), kind=kLoop, calls=%fused_computation | loop fusion | flops 131072 | bytes 524288 | tf_op jit(solution)/shard_map/stack | solution.py:423
  1.7 3.0 %collective-permute-start.3 = (bf16[2,8,64,128]{3,2,1,0:T(8,128)(2,1)S(1)}, bf16[2,8,64,128]{3,2,1,0:T(8,128)(2,1)S(1)}, u32[]{:S(2)}, u32[]{:S(2)}) collective-permute-start(bf16[2,8,64,128]{3,2,1,0:T(8,128)(2,1)S(1)} %pad_maximum_fusion.block.own.after), channel_id=1, source_target_pairs={{0,2},{1,3},{2,4},{3,5},{4,6},{5,7},{6,8},{7,9},{8,10},{9,11},{10,... | collective-permute-start | bytes 786440 | tf_op jit(solution)/shard_map/ppermute | solution.py:19
  4.8 0.5 %collective-permute-start.1 = (bf16[4,64,128]{2,1,0:T(8,128)(2,1)S(1)}, bf16[4,64,128]{2,1,0:T(8,128)(2,1)S(1)}, u32[]{:S(2)}, u32[]{:S(2)}) collective-permute-start(bf16[4,64,128]{2,1,0:T(8,128)(2,1)S(1)} %get-tuple-element.54), channel_id=1, source_target_pairs={{0,16},{16,0},{1,17},{17,1},{2,18},{18,2},{3,19},{19,3},{4,20},{20... | collective-permute-start | bytes 196616 | tf_op jit(solution)/shard_map/ppermute | solution.py:24
  5.3 0.7 %collective-permute-done.other_keys = bf16[4,64,128]{2,1,0:T(8,128)(2,1)S(1)} collective-permute-done((bf16[4,64,128]{2,1,0:T(8,128)(2,1)S(1)}, bf16[4,64,128]{2,1,0:T(8,128)(2,1)S(1)}, u32[]{:S(2)}, u32[]{:S(2)}) %collective-permute-start) | collective-permute-done | bytes 65568 | tf_op jit(solution)/shard_map/ppermute | solution.py:24
  6.2 3.4 %collective-permute-start.2 = (bf16[2,4,128,128]{3,2,1,0:T(8,128)(2,1)S(1)}, bf16[2,4,128,128]{3,2,1,0:T(8,128)(2,1)S(1)}, u32[]{:S(2)}, u32[]{:S(2)}) collective-permute-start(bf16[2,4,128,128]{3,2,1,0:T(8,128)(2,1)S(1)} %join_own.1.own), channel_id=1, source_target_pairs={{0,1},{1,2},{2,3},{3,4},{4,5},{5,6},{6,7},{7,8},{8,9},{9,10},{10,1... | collective-permute-start | bytes 786440 | tf_op jit(solution)/shard_map/ppermute | solution.py:19
  11.0 0.7 %collective-permute-done.4.first_third = bf16[10,64,128]{2,1,0:T(8,128)(2,1)S(1)} collective-permute-done((bf16[10,64,128]{2,1,0:T(8,128)(2,1)S(1)}, bf16[10,64,128]{2,1,0:T(8,128)(2,1)S(1)}, u32[]{:S(2)}, u32[]{:S(2)}) %collective-permute-start.4) | collective-permute-done | bytes 163872 | tf_op jit(solution)/shard_map/ppermute | solution.py:24
  11.7 1.8 %own_block.1 = (bf16[16,128,128]{2,1,0:T(8,128)(2,1)S(1)}, bf16[16,128,128]{2,1,0:T(8,128)(2,1)S(1)}, bf16[8,128,256]{2,1,0:T(8,128)(2,1)S(1)}, s32[8,1,256]{2,1...) custom-call(s32[32]{0:T(128)S(1)} %copy-done.2, ...), custom_call_target="tpu_custom_call" | custom-call | flops 1 | tf_op jit(solution)/shard_map/own_block/pallas_call | solution.py:400
  13.5 0.6 %collective-permute-done.3.block.back_two = bf16[2,8,64,128]{3,2,1,0:T(8,128)(2,1)S(1)} collective-permute-done((bf16[2,8,64,128]{3,2,1,0:T(8,128)(2,1)S(1)}, bf16[2,8,64,128]{3,2,1,0:T(8,128)(2,1)S(1)}, u32[]{:S(2)}, u32[]{:S(2)}) %collective-permute-start.3) | collective-permute-done | bytes 262176 | tf_op jit(solution)/shard_map/ppermute | solution.py:19
  14.2 0.5 %collective-permute-start.8 = (bf16[4,64,128]{2,1,0:T(8,128)(2,1)S(1)}, bf16[4,64,128]{2,1,0:T(8,128)(2,1)S(1)}, u32[]{:S(2)}, u32[]{:S(2)}) collective-permute-start(bf16[4,64,128]{2,1,0:T(8,128)(2,1)S(1)} %get-tuple-element.64), channel_id=1, source_target_pairs={{0,16},{16,0},{1,17},{17,1},{2,18},{18,2},{3,19},{19,3},{4,20},{20... | collective-permute-start | bytes 196616 | tf_op jit(solution)/shard_map/ppermute | solution.py:24
  14.7 0.7 %collective-permute-done.7.two_keys = bf16[4,64,128]{2,1,0:T(8,128)(2,1)S(1)} collective-permute-done((bf16[4,64,128]{2,1,0:T(8,128)(2,1)S(1)}, bf16[4,64,128]{2,1,0:T(8,128)(2,1)S(1)}, u32[]{:S(2)}, u32[]{:S(2)}) %collective-permute-start.7) | collective-permute-done | bytes 65568 | tf_op jit(solution)/shard_map/ppermute | solution.py:24
  15.6 1.2 %near_forward.1 = (f32[8,1,256]{2,1,0:T(1,128)S(1)}, f32[8,1,256]{2,1,0:T(1,128)S(1)}, f32[8,128,256]{2,1,0:T(8,128)S(1)}, f32[8,128,256]{2,1,0:T(8,128)S(1)}, f...) custom-call(s32[8,1,256]{2,1,0:T(1,128)S(1)} %get-tuple-element.59.first, ...), custom_call_target="tpu_custom_call" | custom-call | flops 1 | tf_op jit(solution)/shard_map/near_forward/pallas_call | solution.py:400
  16.7 1.6 %last_forward_backward.1 = (bf16[8,128,256]{2,1,0:T(8,128)(2,1)S(1)}, f32[8,1,256]{2,1,0:T(1,128)S(1)}, f32[8,1,256]{2,1,0:T(1,128)S(1)}, bf16[8,128,256]{2,1,0:T(8,128)(2,1)S(1)}, bf16[2,4,128,128]{3,2,1,0:T(8,128)(2,1)S(1)}) custom-call(s32[8,1,256]{2,1,0:T(1,128)S(1)} %get-tuple-element.59.first, bf16[16,128,128]{2,1,0:T(8,128)(2,1)S(1)} %get-tuple-element.60.query_head, ...), custom_call_target="tpu_custom_call" | custom-call | flops 1 | tf_op jit(solution)/shard_map/last_forward_backward/pallas_call | solution.py:400
  18.4 4.1 %collective-permute-start.14 = (bf16[2,4,128,128]{3,2,1,0:T(8,128)(2,1)S(1)}, bf16[2,4,128,128]{3,2,1,0:T(8,128)(2,1)S(1)}, u32[]{:S(2)}, u32[]{:S(2)}) collective-permute-start(bf16[2,4,128,128]{3,2,1,0:T(8,128)(2,1)S(1)} %get-tuple-element.96), channel_id=1, source_target_pairs={{0,15},{1,0},{2,1},{3,2},{4,3},{5,4},{6,5},{7,6},{8,7},{9,8},{10,9... | collective-permute-start | bytes 786440 | tf_op jit(solution)/shard_map/ppermute | solution.py:19
  22.5 0.5 %two_backward.1 = (bf16[8,128,256]{2,1,0:T(8,128)(2,1)S(1)}, bf16[2,4,64,128]{3,2,1,0:T(8,128)(2,1)S(1)}, bf16[4,64,128]{2,1,0:T(8,128)(2,1)S(1)}, bf16[4,64,128]{2,1,0:T(8,128)(2,1)S(1)}) custom-call(bf16[16,128,128]{2,1,0:T(8,128)(2,1)S(1)} %get-tuple-element.60.query_head, bf16[16,128,128]{2,1,0:T(8,128)(2,1)S(1)} %get-tuple-element.61.grad_head, ...), custom_call_target="tpu_custom_call" | custom-call | flops 1 | tf_op jit(solution)/shard_map/two_backward/pallas_call | solution.py:400
  23.1 0.5 %collective-permute-start.10 = (bf16[4,64,128]{2,1,0:T(8,128)(2,1)S(1)}, bf16[4,64,128]{2,1,0:T(8,128)(2,1)S(1)}, u32[]{:S(2)}, u32[]{:S(2)}) collective-permute-start(bf16[4,64,128]{2,1,0:T(8,128)(2,1)S(1)} %get-tuple-element.86), channel_id=1, source_target_pairs={{0,16},{16,0},{1,17},{17,1},{2,18},{18,2},{3,19},{19,3},{4,20},{20... | collective-permute-start | bytes 196616 | tf_op jit(solution)/shard_map/ppermute | solution.py:24
  23.6 0.7 %collective-permute-done.9.other_keys = bf16[4,64,128]{2,1,0:T(8,128)(2,1)S(1)} collective-permute-done((bf16[4,64,128]{2,1,0:T(8,128)(2,1)S(1)}, bf16[4,64,128]{2,1,0:T(8,128)(2,1)S(1)}, u32[]{:S(2)}, u32[]{:S(2)}) %collective-permute-start.9) | collective-permute-done | bytes 65568 | tf_op jit(solution)/shard_map/ppermute | solution.py:24
  24.5 3.5 %collective-permute-start.16 = (bf16[2,8,64,128]{3,2,1,0:T(8,128)(2,1)S(1)}, bf16[2,8,64,128]{3,2,1,0:T(8,128)(2,1)S(1)}, u32[]{:S(2)}, u32[]{:S(2)}) collective-permute-start(bf16[2,8,64,128]{3,2,1,0:T(8,128)(2,1)S(1)} %join_two.1.after), channel_id=1, source_target_pairs={{0,14},{1,15},{2,0},{3,1},{4,2},{5,3},{6,4},{7,5},{8,6},{9,7},{10,... | collective-permute-start | bytes 786440 | tf_op jit(solution)/shard_map/ppermute | solution.py:19
  28.5 0.8 %query_grad.1 = (bf16[16,64,128]{2,1,0:T(8,128)(2,1)S(1)}, bf16[16,64,128]{2,1,0:T(8,128)(2,1)S(1)}, bf16[10,64,128]{2,1,0:T(8,128)(2,1)S(1)}, bf16[11,64,128]{2,1,0:T(8,128)(2,1)S(1)}, bf16[11,64,128]{2,1,0:T(8,128)(2,1)S(1)}) custom-call(bf16[2,4,128,128]{3,2,1,0:T(8,128)(2,1)S(1)} %join_own.1.own, ...), custom_call_target="tpu_custom_call" | custom-call | flops 1 | tf_op jit(solution)/shard_map/query_grad/pallas_call | solution.py:400
  29.4 0.5 %collective-permute-start.13 = (bf16[11,64,128]{2,1,0:T(8,128)(2,1)S(1)}, bf16[11,64,128]{2,1,0:T(8,128)(2,1)S(1)}, u32[]{:S(2)}, u32[]{:S(2)}) collective-permute-start(bf16[11,64,128]{2,1,0:T(8,128)(2,1)S(1)} %get-tuple-element.92), channel_id=1, source_target_pairs={{0,16},{16,0},{1,17},{17,1},{2,18},{18,2},{3,19},{19,3},{4,20},{20... | collective-permute-start | bytes 540680 | tf_op jit(solution)/shard_map/ppermute | solution.py:24
  30.0 0.5 %collective-permute-start.15 = (bf16[2,4,64,128]{3,2,1,0:T(8,128)(2,1)S(1)}, bf16[2,4,64,128]{3,2,1,0:T(8,128)(2,1)S(1)}, u32[]{:S(2)}, u32[]{:S(2)}) collective-permute-start(bf16[2,4,64,128]{3,2,1,0:T(8,128)(2,1)S(1)} %get-tuple-element.98), channel_id=1, source_target_pairs={{0,16},{16,0},{1,17},{17,1},{2,18},{18,2},{3,19},{19,3},{4,20},{20... | collective-permute-start | bytes 393224 | tf_op jit(solution)/shard_map/ppermute | solution.py:24
  30.5 0.8 %collective-permute-done.11.first_third = bf16[10,64,128]{2,1,0:T(8,128)(2,1)S(1)} collective-permute-done((bf16[10,64,128]{2,1,0:T(8,128)(2,1)S(1)}, bf16[10,64,128]{2,1,0:T(8,128)(2,1)S(1)}, u32[]{:S(2)}, u32[]{:S(2)}) %collective-permute-start.11) | collective-permute-done | bytes 163872 | tf_op jit(solution)/shard_map/ppermute | solution.py:24
  31.3 1.0 %assemble.1 = (bf16[32,64,128]{2,1,0:T(8,128)(2,1)}, bf16[32,64,128]{2,1,0:T(8,128)(2,1)}, f32[8,128]{1,0:T(8,128)S(1)}) custom-call(bf16[16,64,128]{2,1,0:T(8,128)(2,1)S(1)} %get-tuple-element.88.out_mine, bf16[16,64,128]{2,1,0:T(8,128)(2,1)S(1)} %get-tuple-element.89.query_mine, bf16[10,64,128]{2,1,0:T(8,128)(2,1)S(1)} %collective-permute-done.11.first_third, ...), custom_call_target="tpu_custom_call" | custom-call | flops 1 | tf_op jit(solution)/shard_map/assemble/pallas_call | solution.py:400
  32.3 1.6 %collective-permute-done.16.two_total = bf16[2,8,64,128]{3,2,1,0:T(8,128)(2,1)S(1)} collective-permute-done((bf16[2,8,64,128]{3,2,1,0:T(8,128)(2,1)S(1)}, bf16[2,8,64,128]{3,2,1,0:T(8,128)(2,1)S(1)}, u32[]{:S(2)}, u32[]{:S(2)}) %collective-permute-start.16) | collective-permute-done | bytes 262176 | tf_op jit(solution)/shard_map/ppermute | solution.py:19
  34.0 0.8 %total.1 = (bf16[8,64,128]{2,1,0:T(8,128)(2,1)}, bf16[8,64,128]{2,1,0:T(8,128)(2,1)}) custom-call(f32[2,4,64,128]{3,2,1,0:T(8,128)S(1)} %get-tuple-element.97.sum_mine, bf16[2,4,64,128]{3,2,1,0:T(8,128)(2,1)S(1)} %collective-permute-done.15.sum_other, bf16[2,8,64,128]{3,2,1,0:T(8,128)(2,1)S(1)} %collective-permute-done.16.two_total, ...), custom_call_target="tpu_custom_call" | custom-call | flops 1 | tf_op jit(solution)/shard_map/total/pallas_call | solution.py:400
  (31 shorter events, 2.1 us)
Async XLA Ops:
  0.6 9.0 %copy-start.1 = (bf16[32,64,128]{2,1,0:T(8,128)(2,1)S(1)}, bf16[32,64,128]{2,1,0:T(8,128)(2,1)}, u32[]{:S(2)}) copy-start(bf16[32,64,128]{2,1,0:T(8,128)(2,1)} %grads.3) | copy-start | bytes 1572868
  1.7 8.0 %copy-start = (bf16[32,64,128]{2,1,0:T(8,128)(2,1)S(1)}, bf16[32,64,128]{2,1,0:T(8,128)(2,1)}, u32[]{:S(2)}) copy-start(bf16[32,64,128]{2,1,0:T(8,128)(2,1)} %queries.3) | copy-start | bytes 1572868
  1.7 12.4 %collective-permute-start.3 = (bf16[2,8,64,128]{3,2,1,0:T(8,128)(2,1)S(1)}, bf16[2,8,64,128]{3,2,1,0:T(8,128)(2,1)S(1)}, u32[]{:S(2)}, u32[]{:S(2)}) collective-permute-start(bf16[2,8,64,128]{3,2,1,0:T(8,128)(2,1)S(1)} %pad_maximum_fusion.block.own.after), channel_id=1, source_target_pairs={{0,2},{1,3},{2,4},{3,5},{4,6},{5,7},{6,8},{7,9},{8,10},{9,11},{10,... | collective-permute-start | bytes 786440 | tf_op jit(solution)/shard_map/ppermute | solution.py:19
  4.7 1.3 %collective-permute-start = (bf16[4,64,128]{2,1,0:T(8,128)(2,1)S(1)}, bf16[4,64,128]{2,1,0:T(8,128)(2,1)S(1)}, u32[]{:S(2)}, u32[]{:S(2)}) collective-permute-start(bf16[4,64,128]{2,1,0:T(8,128)(2,1)S(1)} %get-tuple-element.53), channel_id=1, source_target_pairs={{0,16},{16,0},{1,17},{17,1},{2,18},{18,2},{3,19},{19,3},{4,20},{20... | collective-permute-start | bytes 196616 | tf_op jit(solution)/shard_map/ppermute | solution.py:24
  4.8 1.4 %collective-permute-start.1 = (bf16[4,64,128]{2,1,0:T(8,128)(2,1)S(1)}, bf16[4,64,128]{2,1,0:T(8,128)(2,1)S(1)}, u32[]{:S(2)}, u32[]{:S(2)}) collective-permute-start(bf16[4,64,128]{2,1,0:T(8,128)(2,1)S(1)} %get-tuple-element.54), channel_id=1, source_target_pairs={{0,16},{16,0},{1,17},{17,1},{2,18},{18,2},{3,19},{19,3},{4,20},{20... | collective-permute-start | bytes 196616 | tf_op jit(solution)/shard_map/ppermute | solution.py:24
  6.2 10.5 %collective-permute-start.2 = (bf16[2,4,128,128]{3,2,1,0:T(8,128)(2,1)S(1)}, bf16[2,4,128,128]{3,2,1,0:T(8,128)(2,1)S(1)}, u32[]{:S(2)}, u32[]{:S(2)}) collective-permute-start(bf16[2,4,128,128]{3,2,1,0:T(8,128)(2,1)S(1)} %join_own.1.own), channel_id=1, source_target_pairs={{0,1},{1,2},{2,3},{3,4},{4,5},{5,6},{6,7},{7,8},{8,9},{9,10},{10,1... | collective-permute-start | bytes 786440 | tf_op jit(solution)/shard_map/ppermute | solution.py:19
  9.7 2.0 %collective-permute-start.5 = (bf16[11,64,128]{2,1,0:T(8,128)(2,1)S(1)}, bf16[11,64,128]{2,1,0:T(8,128)(2,1)S(1)}, u32[]{:S(2)}, u32[]{:S(2)}) collective-permute-start(bf16[11,64,128]{2,1,0:T(8,128)(2,1)S(1)} %get-tuple-element.56), channel_id=1, source_target_pairs={{0,16},{16,0},{1,17},{17,1},{2,18},{18,2},{3,19},{19,3},{4,20},{20... | collective-permute-start | bytes 540680 | tf_op jit(solution)/shard_map/ppermute | solution.py:24
  9.9 1.8 %collective-permute-start.6 = (bf16[11,64,128]{2,1,0:T(8,128)(2,1)S(1)}, bf16[11,64,128]{2,1,0:T(8,128)(2,1)S(1)}, u32[]{:S(2)}, u32[]{:S(2)}) collective-permute-start(bf16[11,64,128]{2,1,0:T(8,128)(2,1)S(1)} %get-tuple-element.57), channel_id=1, source_target_pairs={{0,16},{16,0},{1,17},{17,1},{2,18},{18,2},{3,19},{19,3},{4,20},{20... | collective-permute-start | bytes 540680 | tf_op jit(solution)/shard_map/ppermute | solution.py:24
  10.3 1.4 %copy-start.2 = (s32[32]{0:T(128)S(1)}, s32[32]{0:T(128)}, u32[]{:S(2)}) copy-start(s32[32]{0:T(128)} %spans.1) | copy-start | bytes 388
  10.3 1.4 %collective-permute-start.4 = (bf16[10,64,128]{2,1,0:T(8,128)(2,1)S(1)}, bf16[10,64,128]{2,1,0:T(8,128)(2,1)S(1)}, u32[]{:S(2)}, u32[]{:S(2)}) collective-permute-start(bf16[10,64,128]{2,1,0:T(8,128)(2,1)S(1)} %get-tuple-element.55), channel_id=1, source_target_pairs={{0,16},{16,0},{1,17},{17,1},{2,18},{18,2},{3,19},{19,3},{4,20},{20... | collective-permute-start | bytes 491528 | tf_op jit(solution)/shard_map/ppermute | solution.py:24
  14.1 1.3 %collective-permute-start.7 = (bf16[4,64,128]{2,1,0:T(8,128)(2,1)S(1)}, bf16[4,64,128]{2,1,0:T(8,128)(2,1)S(1)}, u32[]{:S(2)}, u32[]{:S(2)}) collective-permute-start(bf16[4,64,128]{2,1,0:T(8,128)(2,1)S(1)} %get-tuple-element.63), channel_id=1, source_target_pairs={{0,16},{16,0},{1,17},{17,1},{2,18},{18,2},{3,19},{19,3},{4,20},{20... | collective-permute-start | bytes 196616 | tf_op jit(solution)/shard_map/ppermute | solution.py:24
  14.2 1.4 %collective-permute-start.8 = (bf16[4,64,128]{2,1,0:T(8,128)(2,1)S(1)}, bf16[4,64,128]{2,1,0:T(8,128)(2,1)S(1)}, u32[]{:S(2)}, u32[]{:S(2)}) collective-permute-start(bf16[4,64,128]{2,1,0:T(8,128)(2,1)S(1)} %get-tuple-element.64), channel_id=1, source_target_pairs={{0,16},{16,0},{1,17},{17,1},{2,18},{18,2},{3,19},{19,3},{4,20},{20... | collective-permute-start | bytes 196616 | tf_op jit(solution)/shard_map/ppermute | solution.py:24
  18.4 11.6 %collective-permute-start.14 = (bf16[2,4,128,128]{3,2,1,0:T(8,128)(2,1)S(1)}, bf16[2,4,128,128]{3,2,1,0:T(8,128)(2,1)S(1)}, u32[]{:S(2)}, u32[]{:S(2)}) collective-permute-start(bf16[2,4,128,128]{3,2,1,0:T(8,128)(2,1)S(1)} %get-tuple-element.96), channel_id=1, source_target_pairs={{0,15},{1,0},{2,1},{3,2},{4,3},{5,4},{6,5},{7,6},{8,7},{9,8},{10,9... | collective-permute-start | bytes 786440 | tf_op jit(solution)/shard_map/ppermute | solution.py:19
  23.0 1.3 %collective-permute-start.9 = (bf16[4,64,128]{2,1,0:T(8,128)(2,1)S(1)}, bf16[4,64,128]{2,1,0:T(8,128)(2,1)S(1)}, u32[]{:S(2)}, u32[]{:S(2)}) collective-permute-start(bf16[4,64,128]{2,1,0:T(8,128)(2,1)S(1)} %get-tuple-element.85), channel_id=1, source_target_pairs={{0,16},{16,0},{1,17},{17,1},{2,18},{18,2},{3,19},{19,3},{4,20},{20... | collective-permute-start | bytes 196616 | tf_op jit(solution)/shard_map/ppermute | solution.py:24
  23.1 1.4 %collective-permute-start.10 = (bf16[4,64,128]{2,1,0:T(8,128)(2,1)S(1)}, bf16[4,64,128]{2,1,0:T(8,128)(2,1)S(1)}, u32[]{:S(2)}, u32[]{:S(2)}) collective-permute-start(bf16[4,64,128]{2,1,0:T(8,128)(2,1)S(1)} %get-tuple-element.86), channel_id=1, source_target_pairs={{0,16},{16,0},{1,17},{17,1},{2,18},{18,2},{3,19},{19,3},{4,20},{20... | collective-permute-start | bytes 196616 | tf_op jit(solution)/shard_map/ppermute | solution.py:24
  24.5 9.4 %collective-permute-start.16 = (bf16[2,8,64,128]{3,2,1,0:T(8,128)(2,1)S(1)}, bf16[2,8,64,128]{3,2,1,0:T(8,128)(2,1)S(1)}, u32[]{:S(2)}, u32[]{:S(2)}) collective-permute-start(bf16[2,8,64,128]{3,2,1,0:T(8,128)(2,1)S(1)} %join_two.1.after), channel_id=1, source_target_pairs={{0,14},{1,15},{2,0},{3,1},{4,2},{5,3},{6,4},{7,5},{8,6},{9,7},{10,... | collective-permute-start | bytes 786440 | tf_op jit(solution)/shard_map/ppermute | solution.py:19
  29.3 2.0 %collective-permute-start.12 = (bf16[11,64,128]{2,1,0:T(8,128)(2,1)S(1)}, bf16[11,64,128]{2,1,0:T(8,128)(2,1)S(1)}, u32[]{:S(2)}, u32[]{:S(2)}) collective-permute-start(bf16[11,64,128]{2,1,0:T(8,128)(2,1)S(1)} %get-tuple-element.91), channel_id=1, source_target_pairs={{0,16},{16,0},{1,17},{17,1},{2,18},{18,2},{3,19},{19,3},{4,20},{20... | collective-permute-start | bytes 540680 | tf_op jit(solution)/shard_map/ppermute | solution.py:24
  29.4 1.9 %collective-permute-start.13 = (bf16[11,64,128]{2,1,0:T(8,128)(2,1)S(1)}, bf16[11,64,128]{2,1,0:T(8,128)(2,1)S(1)}, u32[]{:S(2)}, u32[]{:S(2)}) collective-permute-start(bf16[11,64,128]{2,1,0:T(8,128)(2,1)S(1)} %get-tuple-element.92), channel_id=1, source_target_pairs={{0,16},{16,0},{1,17},{17,1},{2,18},{18,2},{3,19},{19,3},{4,20},{20... | collective-permute-start | bytes 540680 | tf_op jit(solution)/shard_map/ppermute | solution.py:24
  29.9 1.4 %collective-permute-start.11 = (bf16[10,64,128]{2,1,0:T(8,128)(2,1)S(1)}, bf16[10,64,128]{2,1,0:T(8,128)(2,1)S(1)}, u32[]{:S(2)}, u32[]{:S(2)}) collective-permute-start(bf16[10,64,128]{2,1,0:T(8,128)(2,1)S(1)} %get-tuple-element.90), channel_id=1, source_target_pairs={{0,16},{16,0},{1,17},{17,1},{2,18},{18,2},{3,19},{19,3},{4,20},{20... | collective-permute-start | bytes 491528 | tf_op jit(solution)/shard_map/ppermute | solution.py:24
  30.0 4.0 %collective-permute-start.15 = (bf16[2,4,64,128]{3,2,1,0:T(8,128)(2,1)S(1)}, bf16[2,4,64,128]{3,2,1,0:T(8,128)(2,1)S(1)}, u32[]{:S(2)}, u32[]{:S(2)}) collective-permute-start(bf16[2,4,64,128]{3,2,1,0:T(8,128)(2,1)S(1)} %get-tuple-element.98), channel_id=1, source_target_pairs={{0,16},{16,0},{1,17},{17,1},{2,18},{18,2},{3,19},{19,3},{4,20},{20... | collective-permute-start | bytes 393224 | tf_op jit(solution)/shard_map/ppermute | solution.py:24

commit v25 on v16

--- a/solution.py
+++ b/solution.py
@@ -250,7 +250,11 @@
         one_part[1, g] = value_part.astype(jnp.bfloat16)
 
     accumulate = accumulator(query_head, grad_head, chunks, groups, store)
-    pipelined(chunks, products, softmax, differentiate, accumulate)
+    pipelined(chunks, products, wait, softmax, differentiate, accumulate)
+
+
+def wait(n, *values):
+    return values
 
 
 def pipelined(chunks, *stages):

time: 34.6 us -> 34.4 us (level)
  no operation moved by 1% of the time
where the time goes in v25:
time: 34.4 us; the launch traced here: 34.2 us
  starting transfers between devices  17.6 us (51%)
  Pallas kernels  7.51 us (22%)
  waiting for transfers between devices  6.59 us (19%)
  between operations  1.44 us (4%)
  other arithmetic  1.05 us (3%)
    ppermute x4, starting transfers between devices, shifted(): return lax.ppermute(block, axis, route)  14.1 us
    pallas_call x14, Pallas kernels, call(): pl.pallas_call(kernel, out_shape=tuple((jax.ShapeDtypeStruct(shape, kind)...  7.51 us
    ppermute x13, waiting for transfers between devices, swapped(): return lax.ppermute(block, axis, [(i, count - 1 - i) for i in range(count)])  4.14 us
    ppermute x13, starting transfers between devices, swapped(): return lax.ppermute(block, axis, [(i, count - 1 - i) for i in range(count)])  3.5 us
    ppermute x4, waiting for transfers between devices, shifted(): return lax.ppermute(block, axis, route)  2.45 us
    another operation x1, other arithmetic, shards(): own = jnp.stack([key_matrix, value_matrix])  1.05 us
  transfers between devices with their start and end apart: 17, of which 10 were waited for; matrix products, arithmetic and copies ran while one was open for 0% of the time, Pallas kernels for 16%

profile of v25, /device:TPU:0, one launch (start us, length us, event | category | flops | bytes accessed | tf_op | source)
XLA Modules:
  0.0 34.2 jit_solution(9905608801494273848)
XLA Ops:
  0.6 1.1 %pad_maximum_fusion.block.own.after = bf16[2,8,64,128]{3,2,1,0:T(8,128)(2,1)S(1)} fusion(bf16[1,8,64,128]{3,2,1,0:T(8,128)(2,1)} %bitcast.2, bf16[1,8,64,128]{3,2,1,0:T(8,128)(2,1)} %bitcast.3), kind=kLoop, calls=%fused_computation | loop fusion | flops 131072 | bytes 524288 | tf_op jit(solution)/shard_map/stack | solution.py:427
  1.7 3.0 %collective-permute-start.3 = (bf16[2,8,64,128]{3,2,1,0:T(8,128)(2,1)S(1)}, bf16[2,8,64,128]{3,2,1,0:T(8,128)(2,1)S(1)}, u32[]{:S(2)}, u32[]{:S(2)}) collective-permute-start(bf16[2,8,64,128]{3,2,1,0:T(8,128)(2,1)S(1)} %pad_maximum_fusion.block.own.after), channel_id=1, source_target_pairs={{0,2},{1,3},{2,4},{3,5},{4,6},{5,7},{6,8},{7,9},{8,10},{9,11},{10,... | collective-permute-start | bytes 786440 | tf_op jit(solution)/shard_map/ppermute | solution.py:19
  4.8 0.5 %collective-permute-start.1 = (bf16[4,64,128]{2,1,0:T(8,128)(2,1)S(1)}, bf16[4,64,128]{2,1,0:T(8,128)(2,1)S(1)}, u32[]{:S(2)}, u32[]{:S(2)}) collective-permute-start(bf16[4,64,128]{2,1,0:T(8,128)(2,1)S(1)} %get-tuple-element.54), channel_id=1, source_target_pairs={{0,16},{16,0},{1,17},{17,1},{2,18},{18,2},{3,19},{19,3},{4,20},{20... | collective-permute-start | bytes 196616 | tf_op jit(solution)/shard_map/ppermute | solution.py:24
  5.3 0.7 %collective-permute-done.other_keys = bf16[4,64,128]{2,1,0:T(8,128)(2,1)S(1)} collective-permute-done((bf16[4,64,128]{2,1,0:T(8,128)(2,1)S(1)}, bf16[4,64,128]{2,1,0:T(8,128)(2,1)S(1)}, u32[]{:S(2)}, u32[]{:S(2)}) %collective-permute-start) | collective-permute-done | bytes 65568 | tf_op jit(solution)/shard_map/ppermute | solution.py:24
  6.2 3.4 %collective-permute-start.2 = (bf16[2,4,128,128]{3,2,1,0:T(8,128)(2,1)S(1)}, bf16[2,4,128,128]{3,2,1,0:T(8,128)(2,1)S(1)}, u32[]{:S(2)}, u32[]{:S(2)}) collective-permute-start(bf16[2,4,128,128]{3,2,1,0:T(8,128)(2,1)S(1)} %join_own.1.own), channel_id=1, source_target_pairs={{0,1},{1,2},{2,3},{3,4},{4,5},{5,6},{6,7},{7,8},{8,9},{9,10},{10,1... | collective-permute-start | bytes 786440 | tf_op jit(solution)/shard_map/ppermute | solution.py:19
  11.0 0.7 %collective-permute-done.4.first_third = bf16[10,64,128]{2,1,0:T(8,128)(2,1)S(1)} collective-permute-done((bf16[10,64,128]{2,1,0:T(8,128)(2,1)S(1)}, bf16[10,64,128]{2,1,0:T(8,128)(2,1)S(1)}, u32[]{:S(2)}, u32[]{:S(2)}) %collective-permute-start.4) | collective-permute-done | bytes 163872 | tf_op jit(solution)/shard_map/ppermute | solution.py:24
  11.7 1.5 %own_block.1 = (bf16[16,128,128]{2,1,0:T(8,128)(2,1)S(1)}, bf16[16,128,128]{2,1,0:T(8,128)(2,1)S(1)}, bf16[8,128,256]{2,1,0:T(8,128)(2,1)S(1)}, s32[8,1,256]{2,1...) custom-call(s32[32]{0:T(128)S(1)} %copy-done.2, ...), custom_call_target="tpu_custom_call" | custom-call | flops 1 | tf_op jit(solution)/shard_map/own_block/pallas_call | solution.py:404
  13.3 0.8 %collective-permute-done.3.block.back_two = bf16[2,8,64,128]{3,2,1,0:T(8,128)(2,1)S(1)} collective-permute-done((bf16[2,8,64,128]{3,2,1,0:T(8,128)(2,1)S(1)}, bf16[2,8,64,128]{3,2,1,0:T(8,128)(2,1)S(1)}, u32[]{:S(2)}, u32[]{:S(2)}) %collective-permute-start.3) | collective-permute-done | bytes 262176 | tf_op jit(solution)/shard_map/ppermute | solution.py:19
  14.2 0.5 %collective-permute-start.8 = (bf16[4,64,128]{2,1,0:T(8,128)(2,1)S(1)}, bf16[4,64,128]{2,1,0:T(8,128)(2,1)S(1)}, u32[]{:S(2)}, u32[]{:S(2)}) collective-permute-start(bf16[4,64,128]{2,1,0:T(8,128)(2,1)S(1)} %get-tuple-element.64), channel_id=1, source_target_pairs={{0,16},{16,0},{1,17},{17,1},{2,18},{18,2},{3,19},{19,3},{4,20},{20... | collective-permute-start | bytes 196616 | tf_op jit(solution)/shard_map/ppermute | solution.py:24
  14.7 0.7 %collective-permute-done.7.two_keys = bf16[4,64,128]{2,1,0:T(8,128)(2,1)S(1)} collective-permute-done((bf16[4,64,128]{2,1,0:T(8,128)(2,1)S(1)}, bf16[4,64,128]{2,1,0:T(8,128)(2,1)S(1)}, u32[]{:S(2)}, u32[]{:S(2)}) %collective-permute-start.7) | collective-permute-done | bytes 65568 | tf_op jit(solution)/shard_map/ppermute | solution.py:24
  15.6 0.9 %near_forward.1 = (f32[8,1,256]{2,1,0:T(1,128)S(1)}, f32[8,1,256]{2,1,0:T(1,128)S(1)}, f32[8,128,256]{2,1,0:T(8,128)S(1)}, f32[8,128,256]{2,1,0:T(8,128)S(1)}, f...) custom-call(s32[8,1,256]{2,1,0:T(1,128)S(1)} %get-tuple-element.59.first, ...), custom_call_target="tpu_custom_call" | custom-call | flops 1 | tf_op jit(solution)/shard_map/near_forward/pallas_call | solution.py:404
  16.5 1.4 %last_forward_backward.1 = (bf16[8,128,256]{2,1,0:T(8,128)(2,1)S(1)}, f32[8,1,256]{2,1,0:T(1,128)S(1)}, f32[8,1,256]{2,1,0:T(1,128)S(1)}, bf16[8,128,256]{2,1,0:T(8,128)(2,1)S(1)}, bf16[2,4,128,128]{3,2,1,0:T(8,128)(2,1)S(1)}) custom-call(s32[8,1,256]{2,1,0:T(1,128)S(1)} %get-tuple-element.59.first, bf16[16,128,128]{2,1,0:T(8,128)(2,1)S(1)} %get-tuple-element.60.query_head, ...), custom_call_target="tpu_custom_call" | custom-call | flops 1 | tf_op jit(solution)/shard_map/last_forward_backward/pallas_call | solution.py:404
  17.9 4.4 %collective-permute-start.14 = (bf16[2,4,128,128]{3,2,1,0:T(8,128)(2,1)S(1)}, bf16[2,4,128,128]{3,2,1,0:T(8,128)(2,1)S(1)}, u32[]{:S(2)}, u32[]{:S(2)}) collective-permute-start(bf16[2,4,128,128]{3,2,1,0:T(8,128)(2,1)S(1)} %get-tuple-element.96), channel_id=1, source_target_pairs={{0,15},{1,0},{2,1},{3,2},{4,3},{5,4},{6,5},{7,6},{8,7},{9,8},{10,9... | collective-permute-start | bytes 786440 | tf_op jit(solution)/shard_map/ppermute | solution.py:19
  22.2 0.5 %two_backward.1 = (bf16[8,128,256]{2,1,0:T(8,128)(2,1)S(1)}, bf16[2,4,64,128]{3,2,1,0:T(8,128)(2,1)S(1)}, bf16[4,64,128]{2,1,0:T(8,128)(2,1)S(1)}, bf16[4,64,128]{2,1,0:T(8,128)(2,1)S(1)}) custom-call(bf16[16,128,128]{2,1,0:T(8,128)(2,1)S(1)} %get-tuple-element.60.query_head, bf16[16,128,128]{2,1,0:T(8,128)(2,1)S(1)} %get-tuple-element.61.grad_head, ...), custom_call_target="tpu_custom_call" | custom-call | flops 1 | tf_op jit(solution)/shard_map/two_backward/pallas_call | solution.py:404
  22.8 0.5 %collective-permute-start.10 = (bf16[4,64,128]{2,1,0:T(8,128)(2,1)S(1)}, bf16[4,64,128]{2,1,0:T(8,128)(2,1)S(1)}, u32[]{:S(2)}, u32[]{:S(2)}) collective-permute-start(bf16[4,64,128]{2,1,0:T(8,128)(2,1)S(1)} %get-tuple-element.86), channel_id=1, source_target_pairs={{0,16},{16,0},{1,17},{17,1},{2,18},{18,2},{3,19},{19,3},{4,20},{20... | collective-permute-start | bytes 196616 | tf_op jit(solution)/shard_map/ppermute | solution.py:24
  23.3 0.7 %collective-permute-done.9.other_keys = bf16[4,64,128]{2,1,0:T(8,128)(2,1)S(1)} collective-permute-done((bf16[4,64,128]{2,1,0:T(8,128)(2,1)S(1)}, bf16[4,64,128]{2,1,0:T(8,128)(2,1)S(1)}, u32[]{:S(2)}, u32[]{:S(2)}) %collective-permute-start.9) | collective-permute-done | bytes 65568 | tf_op jit(solution)/shard_map/ppermute | solution.py:24
  24.3 3.3 %collective-permute-start.16 = (bf16[2,8,64,128]{3,2,1,0:T(8,128)(2,1)S(1)}, bf16[2,8,64,128]{3,2,1,0:T(8,128)(2,1)S(1)}, u32[]{:S(2)}, u32[]{:S(2)}) collective-permute-start(bf16[2,8,64,128]{3,2,1,0:T(8,128)(2,1)S(1)} %join_two.1.after), channel_id=1, source_target_pairs={{0,14},{1,15},{2,0},{3,1},{4,2},{5,3},{6,4},{7,5},{8,6},{9,7},{10,... | collective-permute-start | bytes 786440 | tf_op jit(solution)/shard_map/ppermute | solution.py:19
  28.0 0.8 %query_grad.1 = (bf16[16,64,128]{2,1,0:T(8,128)(2,1)S(1)}, bf16[16,64,128]{2,1,0:T(8,128)(2,1)S(1)}, bf16[10,64,128]{2,1,0:T(8,128)(2,1)S(1)}, bf16[11,64,128]{2,1,0:T(8,128)(2,1)S(1)}, bf16[11,64,128]{2,1,0:T(8,128)(2,1)S(1)}) custom-call(bf16[2,4,128,128]{3,2,1,0:T(8,128)(2,1)S(1)} %join_own.1.own, ...), custom_call_target="tpu_custom_call" | custom-call | flops 1 | tf_op jit(solution)/shard_map/query_grad/pallas_call | solution.py:404
  28.9 0.5 %collective-permute-start.13 = (bf16[11,64,128]{2,1,0:T(8,128)(2,1)S(1)}, bf16[11,64,128]{2,1,0:T(8,128)(2,1)S(1)}, u32[]{:S(2)}, u32[]{:S(2)}) collective-permute-start(bf16[11,64,128]{2,1,0:T(8,128)(2,1)S(1)} %get-tuple-element.92), channel_id=1, source_target_pairs={{0,16},{16,0},{1,17},{17,1},{2,18},{18,2},{3,19},{19,3},{4,20},{20... | collective-permute-start | bytes 540680 | tf_op jit(solution)/shard_map/ppermute | solution.py:24
  29.5 0.5 %collective-permute-start.15 = (bf16[2,4,64,128]{3,2,1,0:T(8,128)(2,1)S(1)}, bf16[2,4,64,128]{3,2,1,0:T(8,128)(2,1)S(1)}, u32[]{:S(2)}, u32[]{:S(2)}) collective-permute-start(bf16[2,4,64,128]{3,2,1,0:T(8,128)(2,1)S(1)} %get-tuple-element.98), channel_id=1, source_target_pairs={{0,16},{16,0},{1,17},{17,1},{2,18},{18,2},{3,19},{19,3},{4,20},{20... | collective-permute-start | bytes 393224 | tf_op jit(solution)/shard_map/ppermute | solution.py:24
  30.0 0.8 %collective-permute-done.11.first_third = bf16[10,64,128]{2,1,0:T(8,128)(2,1)S(1)} collective-permute-done((bf16[10,64,128]{2,1,0:T(8,128)(2,1)S(1)}, bf16[10,64,128]{2,1,0:T(8,128)(2,1)S(1)}, u32[]{:S(2)}, u32[]{:S(2)}) %collective-permute-start.11) | collective-permute-done | bytes 163872 | tf_op jit(solution)/shard_map/ppermute | solution.py:24
  30.8 1.0 %assemble.1 = (bf16[32,64,128]{2,1,0:T(8,128)(2,1)}, bf16[32,64,128]{2,1,0:T(8,128)(2,1)}, f32[8,128]{1,0:T(8,128)S(1)}) custom-call(bf16[16,64,128]{2,1,0:T(8,128)(2,1)S(1)} %get-tuple-element.88.out_mine, bf16[16,64,128]{2,1,0:T(8,128)(2,1)S(1)} %get-tuple-element.89.query_mine, bf16[10,64,128]{2,1,0:T(8,128)(2,1)S(1)} %collective-permute-done.11.first_third, ...), custom_call_target="tpu_custom_call" | custom-call | flops 1 | tf_op jit(solution)/shard_map/assemble/pallas_call | solution.py:404
  31.8 1.6 %collective-permute-done.16.two_total = bf16[2,8,64,128]{3,2,1,0:T(8,128)(2,1)S(1)} collective-permute-done((bf16[2,8,64,128]{3,2,1,0:T(8,128)(2,1)S(1)}, bf16[2,8,64,128]{3,2,1,0:T(8,128)(2,1)S(1)}, u32[]{:S(2)}, u32[]{:S(2)}) %collective-permute-start.16) | collective-permute-done | bytes 262176 | tf_op jit(solution)/shard_map/ppermute | solution.py:19
  33.5 0.8 %total.1 = (bf16[8,64,128]{2,1,0:T(8,128)(2,1)}, bf16[8,64,128]{2,1,0:T(8,128)(2,1)}) custom-call(f32[2,4,64,128]{3,2,1,0:T(8,128)S(1)} %get-tuple-element.97.sum_mine, bf16[2,4,64,128]{3,2,1,0:T(8,128)(2,1)S(1)} %collective-permute-done.15.sum_other, bf16[2,8,64,128]{3,2,1,0:T(8,128)(2,1)S(1)} %collective-permute-done.16.two_total, ...), custom_call_target="tpu_custom_call" | custom-call | flops 1 | tf_op jit(solution)/shard_map/total/pallas_call | solution.py:404
  (31 shorter events, 2.1 us)
Async XLA Ops:
  0.6 9.0 %copy-start.1 = (bf16[32,64,128]{2,1,0:T(8,128)(2,1)S(1)}, bf16[32,64,128]{2,1,0:T(8,128)(2,1)}, u32[]{:S(2)}) copy-start(bf16[32,64,128]{2,1,0:T(8,128)(2,1)} %grads.3) | copy-start | bytes 1572868
  1.7 8.0 %copy-start = (bf16[32,64,128]{2,1,0:T(8,128)(2,1)S(1)}, bf16[32,64,128]{2,1,0:T(8,128)(2,1)}, u32[]{:S(2)}) copy-start(bf16[32,64,128]{2,1,0:T(8,128)(2,1)} %queries.3) | copy-start | bytes 1572868
  1.7 12.4 %collective-permute-start.3 = (bf16[2,8,64,128]{3,2,1,0:T(8,128)(2,1)S(1)}, bf16[2,8,64,128]{3,2,1,0:T(8,128)(2,1)S(1)}, u32[]{:S(2)}, u32[]{:S(2)}) collective-permute-start(bf16[2,8,64,128]{3,2,1,0:T(8,128)(2,1)S(1)} %pad_maximum_fusion.block.own.after), channel_id=1, source_target_pairs={{0,2},{1,3},{2,4},{3,5},{4,6},{5,7},{6,8},{7,9},{8,10},{9,11},{10,... | collective-permute-start | bytes 786440 | tf_op jit(solution)/shard_map/ppermute | solution.py:19
  4.7 1.3 %collective-permute-start = (bf16[4,64,128]{2,1,0:T(8,128)(2,1)S(1)}, bf16[4,64,128]{2,1,0:T(8,128)(2,1)S(1)}, u32[]{:S(2)}, u32[]{:S(2)}) collective-permute-start(bf16[4,64,128]{2,1,0:T(8,128)(2,1)S(1)} %get-tuple-element.53), channel_id=1, source_target_pairs={{0,16},{16,0},{1,17},{17,1},{2,18},{18,2},{3,19},{19,3},{4,20},{20... | collective-permute-start | bytes 196616 | tf_op jit(solution)/shard_map/ppermute | solution.py:24
  4.8 1.4 %collective-permute-start.1 = (bf16[4,64,128]{2,1,0:T(8,128)(2,1)S(1)}, bf16[4,64,128]{2,1,0:T(8,128)(2,1)S(1)}, u32[]{:S(2)}, u32[]{:S(2)}) collective-permute-start(bf16[4,64,128]{2,1,0:T(8,128)(2,1)S(1)} %get-tuple-element.54), channel_id=1, source_target_pairs={{0,16},{16,0},{1,17},{17,1},{2,18},{18,2},{3,19},{19,3},{4,20},{20... | collective-permute-start | bytes 196616 | tf_op jit(solution)/shard_map/ppermute | solution.py:24
  6.2 10.3 %collective-permute-start.2 = (bf16[2,4,128,128]{3,2,1,0:T(8,128)(2,1)S(1)}, bf16[2,4,128,128]{3,2,1,0:T(8,128)(2,1)S(1)}, u32[]{:S(2)}, u32[]{:S(2)}) collective-permute-start(bf16[2,4,128,128]{3,2,1,0:T(8,128)(2,1)S(1)} %join_own.1.own), channel_id=1, source_target_pairs={{0,1},{1,2},{2,3},{3,4},{4,5},{5,6},{6,7},{7,8},{8,9},{9,10},{10,1... | collective-permute-start | bytes 786440 | tf_op jit(solution)/shard_map/ppermute | solution.py:19
  9.7 2.0 %collective-permute-start.5 = (bf16[11,64,128]{2,1,0:T(8,128)(2,1)S(1)}, bf16[11,64,128]{2,1,0:T(8,128)(2,1)S(1)}, u32[]{:S(2)}, u32[]{:S(2)}) collective-permute-start(bf16[11,64,128]{2,1,0:T(8,128)(2,1)S(1)} %get-tuple-element.56), channel_id=1, source_target_pairs={{0,16},{16,0},{1,17},{17,1},{2,18},{18,2},{3,19},{19,3},{4,20},{20... | collective-permute-start | bytes 540680 | tf_op jit(solution)/shard_map/ppermute | solution.py:24
  9.9 1.8 %collective-permute-start.6 = (bf16[11,64,128]{2,1,0:T(8,128)(2,1)S(1)}, bf16[11,64,128]{2,1,0:T(8,128)(2,1)S(1)}, u32[]{:S(2)}, u32[]{:S(2)}) collective-permute-start(bf16[11,64,128]{2,1,0:T(8,128)(2,1)S(1)} %get-tuple-element.57), channel_id=1, source_target_pairs={{0,16},{16,0},{1,17},{17,1},{2,18},{18,2},{3,19},{19,3},{4,20},{20... | collective-permute-start | bytes 540680 | tf_op jit(solution)/shard_map/ppermute | solution.py:24
  10.3 1.4 %copy-start.2 = (s32[32]{0:T(128)S(1)}, s32[32]{0:T(128)}, u32[]{:S(2)}) copy-start(s32[32]{0:T(128)} %spans.1) | copy-start | bytes 388
  10.3 1.4 %collective-permute-start.4 = (bf16[10,64,128]{2,1,0:T(8,128)(2,1)S(1)}, bf16[10,64,128]{2,1,0:T(8,128)(2,1)S(1)}, u32[]{:S(2)}, u32[]{:S(2)}) collective-permute-start(bf16[10,64,128]{2,1,0:T(8,128)(2,1)S(1)} %get-tuple-element.55), channel_id=1, source_target_pairs={{0,16},{16,0},{1,17},{17,1},{2,18},{18,2},{3,19},{19,3},{4,20},{20... | collective-permute-start | bytes 491528 | tf_op jit(solution)/shard_map/ppermute | solution.py:24
  14.1 1.3 %collective-permute-start.7 = (bf16[4,64,128]{2,1,0:T(8,128)(2,1)S(1)}, bf16[4,64,128]{2,1,0:T(8,128)(2,1)S(1)}, u32[]{:S(2)}, u32[]{:S(2)}) collective-permute-start(bf16[4,64,128]{2,1,0:T(8,128)(2,1)S(1)} %get-tuple-element.63), channel_id=1, source_target_pairs={{0,16},{16,0},{1,17},{17,1},{2,18},{18,2},{3,19},{19,3},{4,20},{20... | collective-permute-start | bytes 196616 | tf_op jit(solution)/shard_map/ppermute | solution.py:24
  14.2 1.4 %collective-permute-start.8 = (bf16[4,64,128]{2,1,0:T(8,128)(2,1)S(1)}, bf16[4,64,128]{2,1,0:T(8,128)(2,1)S(1)}, u32[]{:S(2)}, u32[]{:S(2)}) collective-permute-start(bf16[4,64,128]{2,1,0:T(8,128)(2,1)S(1)} %get-tuple-element.64), channel_id=1, source_target_pairs={{0,16},{16,0},{1,17},{17,1},{2,18},{18,2},{3,19},{19,3},{4,20},{20... | collective-permute-start | bytes 196616 | tf_op jit(solution)/shard_map/ppermute | solution.py:24
  17.9 11.6 %collective-permute-start.14 = (bf16[2,4,128,128]{3,2,1,0:T(8,128)(2,1)S(1)}, bf16[2,4,128,128]{3,2,1,0:T(8,128)(2,1)S(1)}, u32[]{:S(2)}, u32[]{:S(2)}) collective-permute-start(bf16[2,4,128,128]{3,2,1,0:T(8,128)(2,1)S(1)} %get-tuple-element.96), channel_id=1, source_target_pairs={{0,15},{1,0},{2,1},{3,2},{4,3},{5,4},{6,5},{7,6},{8,7},{9,8},{10,9... | collective-permute-start | bytes 786440 | tf_op jit(solution)/shard_map/ppermute | solution.py:19
  22.8 1.3 %collective-permute-start.9 = (bf16[4,64,128]{2,1,0:T(8,128)(2,1)S(1)}, bf16[4,64,128]{2,1,0:T(8,128)(2,1)S(1)}, u32[]{:S(2)}, u32[]{:S(2)}) collective-permute-start(bf16[4,64,128]{2,1,0:T(8,128)(2,1)S(1)} %get-tuple-element.85), channel_id=1, source_target_pairs={{0,16},{16,0},{1,17},{17,1},{2,18},{18,2},{3,19},{19,3},{4,20},{20... | collective-permute-start | bytes 196616 | tf_op jit(solution)/shard_map/ppermute | solution.py:24
  22.8 1.4 %collective-permute-start.10 = (bf16[4,64,128]{2,1,0:T(8,128)(2,1)S(1)}, bf16[4,64,128]{2,1,0:T(8,128)(2,1)S(1)}, u32[]{:S(2)}, u32[]{:S(2)}) collective-permute-start(bf16[4,64,128]{2,1,0:T(8,128)(2,1)S(1)} %get-tuple-element.86), channel_id=1, source_target_pairs={{0,16},{16,0},{1,17},{17,1},{2,18},{18,2},{3,19},{19,3},{4,20},{20... | collective-permute-start | bytes 196616 | tf_op jit(solution)/shard_map/ppermute | solution.py:24
  24.3 9.2 %collective-permute-start.16 = (bf16[2,8,64,128]{3,2,1,0:T(8,128)(2,1)S(1)}, bf16[2,8,64,128]{3,2,1,0:T(8,128)(2,1)S(1)}, u32[]{:S(2)}, u32[]{:S(2)}) collective-permute-start(bf16[2,8,64,128]{3,2,1,0:T(8,128)(2,1)S(1)} %join_two.1.after), channel_id=1, source_target_pairs={{0,14},{1,15},{2,0},{3,1},{4,2},{5,3},{6,4},{7,5},{8,6},{9,7},{10,... | collective-permute-start | bytes 786440 | tf_op jit(solution)/shard_map/ppermute | solution.py:19
  28.8 2.0 %collective-permute-start.12 = (bf16[11,64,128]{2,1,0:T(8,128)(2,1)S(1)}, bf16[11,64,128]{2,1,0:T(8,128)(2,1)S(1)}, u32[]{:S(2)}, u32[]{:S(2)}) collective-permute-start(bf16[11,64,128]{2,1,0:T(8,128)(2,1)S(1)} %get-tuple-element.91), channel_id=1, source_target_pairs={{0,16},{16,0},{1,17},{17,1},{2,18},{18,2},{3,19},{19,3},{4,20},{20... | collective-permute-start | bytes 540680 | tf_op jit(solution)/shard_map/ppermute | solution.py:24
  28.9 1.9 %collective-permute-start.13 = (bf16[11,64,128]{2,1,0:T(8,128)(2,1)S(1)}, bf16[11,64,128]{2,1,0:T(8,128)(2,1)S(1)}, u32[]{:S(2)}, u32[]{:S(2)}) collective-permute-start(bf16[11,64,128]{2,1,0:T(8,128)(2,1)S(1)} %get-tuple-element.92), channel_id=1, source_target_pairs={{0,16},{16,0},{1,17},{17,1},{2,18},{18,2},{3,19},{19,3},{4,20},{20... | collective-permute-start | bytes 540680 | tf_op jit(solution)/shard_map/ppermute | solution.py:24
  29.4 1.4 %collective-permute-start.11 = (bf16[10,64,128]{2,1,0:T(8,128)(2,1)S(1)}, bf16[10,64,128]{2,1,0:T(8,128)(2,1)S(1)}, u32[]{:S(2)}, u32[]{:S(2)}) collective-permute-start(bf16[10,64,128]{2,1,0:T(8,128)(2,1)S(1)} %get-tuple-element.90), channel_id=1, source_target_pairs={{0,16},{16,0},{1,17},{17,1},{2,18},{18,2},{3,19},{19,3},{4,20},{20... | collective-permute-start | bytes 491528 | tf_op jit(solution)/shard_map/ppermute | solution.py:24
  29.5 3.9 %collective-permute-start.15 = (bf16[2,4,64,128]{3,2,1,0:T(8,128)(2,1)S(1)}, bf16[2,4,64,128]{3,2,1,0:T(8,128)(2,1)S(1)}, u32[]{:S(2)}, u32[]{:S(2)}) collective-permute-start(bf16[2,4,64,128]{3,2,1,0:T(8,128)(2,1)S(1)} %get-tuple-element.98), channel_id=1, source_target_pairs={{0,16},{16,0},{1,17},{17,1},{2,18},{18,2},{3,19},{19,3},{4,20},{20... | collective-permute-start | bytes 393224 | tf_op jit(solution)/shard_map/ppermute | solution.py:24

commit v26 on v25

--- a/solution.py
+++ b/solution.py
@@ -161,7 +161,7 @@
         own_out[n] = matmul(own[1, n * groups // chunks], halves, (0, 0))
         grad_rows[n] = grouped(grad_head, n, count).T
 
-    pipelined(chunks, products, softmax, weigh)
+    pipelined(chunks, products, wait, softmax, weigh)
 
 
 def two_back(back_two, two_other, index, g):
@@ -202,7 +202,7 @@
         values = two_back(back_two, two_other, 1, n * groups // chunks)
         near_out[n] = own_out[n] * rescale + matmul(values, halves, (0, 0))
 
-    pipelined(chunks, products, softmax, weigh)
+    pipelined(chunks, products, wait, softmax, weigh)
 
 
 def last_kernel(
@@ -250,7 +250,7 @@
         one_part[1, g] = value_part.astype(jnp.bfloat16)
 
     accumulate = accumulator(query_head, grad_head, chunks, groups, store)
-    pipelined(chunks, products, wait, softmax, differentiate, accumulate)
+    pipelined(chunks, products, wait, softmax, wait, differentiate, accumulate)
 
 
 def wait(n, *values):

time: 34.4 us -> 34.3 us (level)
  transfers between devices with their start and end apart: 17 -> 17, of which waited for: 10 -> 10; matrix products, arithmetic and copies ran while one was open for 0% -> 0% of each run, Pallas kernels for 16% -> 15%
where the time goes in v26:
time: 34.3 us; the launch traced here: 34.1 us
  starting transfers between devices  17.6 us (51%)
  Pallas kernels  7.27 us (21%)
  waiting for transfers between devices  6.7 us (20%)
  between operations  1.44 us (4%)
  other arithmetic  1.05 us (3%)
    ppermute x4, starting transfers between devices, shifted(): return lax.ppermute(block, axis, route)  14.1 us
    pallas_call x14, Pallas kernels, call(): pl.pallas_call(kernel, out_shape=tuple((jax.ShapeDtypeStruct(shape, kind)...  7.27 us
    ppermute x13, waiting for transfers between devices, swapped(): return lax.ppermute(block, axis, [(i, count - 1 - i) for i in range(count)])  4.14 us
    ppermute x13, starting transfers between devices, swapped(): return lax.ppermute(block, axis, [(i, count - 1 - i) for i in range(count)])  3.5 us
    ppermute x4, waiting for transfers between devices, shifted(): return lax.ppermute(block, axis, route)  2.56 us
    another operation x1, other arithmetic, shards(): own = jnp.stack([key_matrix, value_matrix])  1.05 us
  transfers between devices with their start and end apart: 17, of which 10 were waited for; matrix products, arithmetic and copies ran while one was open for 0% of the time, Pallas kernels for 15%

profile of v26, /device:TPU:0, one launch (start us, length us, event | category | flops | bytes accessed | tf_op | source)
XLA Modules:
  0.0 34.1 jit_solution(12067798221930012081)
XLA Ops:
  0.6 1.1 %pad_maximum_fusion.block.own.after = bf16[2,8,64,128]{3,2,1,0:T(8,128)(2,1)S(1)} fusion(bf16[1,8,64,128]{3,2,1,0:T(8,128)(2,1)} %bitcast.2, bf16[1,8,64,128]{3,2,1,0:T(8,128)(2,1)} %bitcast.3), kind=kLoop, calls=%fused_computation | loop fusion | flops 131072 | bytes 524288 | tf_op jit(solution)/shard_map/stack | solution.py:427
  1.7 3.0 %collective-permute-start.3 = (bf16[2,8,64,128]{3,2,1,0:T(8,128)(2,1)S(1)}, bf16[2,8,64,128]{3,2,1,0:T(8,128)(2,1)S(1)}, u32[]{:S(2)}, u32[]{:S(2)}) collective-permute-start(bf16[2,8,64,128]{3,2,1,0:T(8,128)(2,1)S(1)} %pad_maximum_fusion.block.own.after), channel_id=1, source_target_pairs={{0,2},{1,3},{2,4},{3,5},{4,6},{5,7},{6,8},{7,9},{8,10},{9,11},{10,... | collective-permute-start | bytes 786440 | tf_op jit(solution)/shard_map/ppermute | solution.py:19
  4.8 0.5 %collective-permute-start.1 = (bf16[4,64,128]{2,1,0:T(8,128)(2,1)S(1)}, bf16[4,64,128]{2,1,0:T(8,128)(2,1)S(1)}, u32[]{:S(2)}, u32[]{:S(2)}) collective-permute-start(bf16[4,64,128]{2,1,0:T(8,128)(2,1)S(1)} %get-tuple-element.54), channel_id=1, source_target_pairs={{0,16},{16,0},{1,17},{17,1},{2,18},{18,2},{3,19},{19,3},{4,20},{20... | collective-permute-start | bytes 196616 | tf_op jit(solution)/shard_map/ppermute | solution.py:24
  5.3 0.7 %collective-permute-done.other_keys = bf16[4,64,128]{2,1,0:T(8,128)(2,1)S(1)} collective-permute-done((bf16[4,64,128]{2,1,0:T(8,128)(2,1)S(1)}, bf16[4,64,128]{2,1,0:T(8,128)(2,1)S(1)}, u32[]{:S(2)}, u32[]{:S(2)}) %collective-permute-start) | collective-permute-done | bytes 65568 | tf_op jit(solution)/shard_map/ppermute | solution.py:24
  6.2 3.4 %collective-permute-start.2 = (bf16[2,4,128,128]{3,2,1,0:T(8,128)(2,1)S(1)}, bf16[2,4,128,128]{3,2,1,0:T(8,128)(2,1)S(1)}, u32[]{:S(2)}, u32[]{:S(2)}) collective-permute-start(bf16[2,4,128,128]{3,2,1,0:T(8,128)(2,1)S(1)} %join_own.1.own), channel_id=1, source_target_pairs={{0,1},{1,2},{2,3},{3,4},{4,5},{5,6},{6,7},{7,8},{8,9},{9,10},{10,1... | collective-permute-start | bytes 786440 | tf_op jit(solution)/shard_map/ppermute | solution.py:19
  11.0 0.7 %collective-permute-done.4.first_third = bf16[10,64,128]{2,1,0:T(8,128)(2,1)S(1)} collective-permute-done((bf16[10,64,128]{2,1,0:T(8,128)(2,1)S(1)}, bf16[10,64,128]{2,1,0:T(8,128)(2,1)S(1)}, u32[]{:S(2)}, u32[]{:S(2)}) %collective-permute-start.4) | collective-permute-done | bytes 163872 | tf_op jit(solution)/shard_map/ppermute | solution.py:24
  11.7 1.4 %own_block.1 = (bf16[16,128,128]{2,1,0:T(8,128)(2,1)S(1)}, bf16[16,128,128]{2,1,0:T(8,128)(2,1)S(1)}, bf16[8,128,256]{2,1,0:T(8,128)(2,1)S(1)}, s32[8,1,256]{2,1...) custom-call(s32[32]{0:T(128)S(1)} %copy-done.2, ...), custom_call_target="tpu_custom_call" | custom-call | flops 1 | tf_op jit(solution)/shard_map/own_block/pallas_call | solution.py:404
  13.2 0.9 %collective-permute-done.3.block.back_two = bf16[2,8,64,128]{3,2,1,0:T(8,128)(2,1)S(1)} collective-permute-done((bf16[2,8,64,128]{3,2,1,0:T(8,128)(2,1)S(1)}, bf16[2,8,64,128]{3,2,1,0:T(8,128)(2,1)S(1)}, u32[]{:S(2)}, u32[]{:S(2)}) %collective-permute-start.3) | collective-permute-done | bytes 262176 | tf_op jit(solution)/shard_map/ppermute | solution.py:19
  14.2 0.5 %collective-permute-start.8 = (bf16[4,64,128]{2,1,0:T(8,128)(2,1)S(1)}, bf16[4,64,128]{2,1,0:T(8,128)(2,1)S(1)}, u32[]{:S(2)}, u32[]{:S(2)}) collective-permute-start(bf16[4,64,128]{2,1,0:T(8,128)(2,1)S(1)} %get-tuple-element.64), channel_id=1, source_target_pairs={{0,16},{16,0},{1,17},{17,1},{2,18},{18,2},{3,19},{19,3},{4,20},{20... | collective-permute-start | bytes 196616 | tf_op jit(solution)/shard_map/ppermute | solution.py:24
  14.7 0.7 %collective-permute-done.7.two_keys = bf16[4,64,128]{2,1,0:T(8,128)(2,1)S(1)} collective-permute-done((bf16[4,64,128]{2,1,0:T(8,128)(2,1)S(1)}, bf16[4,64,128]{2,1,0:T(8,128)(2,1)S(1)}, u32[]{:S(2)}, u32[]{:S(2)}) %collective-permute-start.7) | collective-permute-done | bytes 65568 | tf_op jit(solution)/shard_map/ppermute | solution.py:24
  15.6 0.8 %near_forward.1 = (f32[8,1,256]{2,1,0:T(1,128)S(1)}, f32[8,1,256]{2,1,0:T(1,128)S(1)}, f32[8,128,256]{2,1,0:T(8,128)S(1)}, f32[8,128,256]{2,1,0:T(8,128)S(1)}, f...) custom-call(s32[8,1,256]{2,1,0:T(1,128)S(1)} %get-tuple-element.59.first, ...), custom_call_target="tpu_custom_call" | custom-call | flops 1 | tf_op jit(solution)/shard_map/near_forward/pallas_call | solution.py:404
  16.4 1.4 %last_forward_backward.1 = (bf16[8,128,256]{2,1,0:T(8,128)(2,1)S(1)}, f32[8,1,256]{2,1,0:T(1,128)S(1)}, f32[8,1,256]{2,1,0:T(1,128)S(1)}, bf16[8,128,256]{2,1,0:T(8,128)(2,1)S(1)}, bf16[2,4,128,128]{3,2,1,0:T(8,128)(2,1)S(1)}) custom-call(s32[8,1,256]{2,1,0:T(1,128)S(1)} %get-tuple-element.59.first, bf16[16,128,128]{2,1,0:T(8,128)(2,1)S(1)} %get-tuple-element.60.query_head, ...), custom_call_target="tpu_custom_call" | custom-call | flops 1 | tf_op jit(solution)/shard_map/last_forward_backward/pallas_call | solution.py:404
  17.7 4.5 %collective-permute-start.14 = (bf16[2,4,128,128]{3,2,1,0:T(8,128)(2,1)S(1)}, bf16[2,4,128,128]{3,2,1,0:T(8,128)(2,1)S(1)}, u32[]{:S(2)}, u32[]{:S(2)}) collective-permute-start(bf16[2,4,128,128]{3,2,1,0:T(8,128)(2,1)S(1)} %get-tuple-element.96), channel_id=1, source_target_pairs={{0,15},{1,0},{2,1},{3,2},{4,3},{5,4},{6,5},{7,6},{8,7},{9,8},{10,9... | collective-permute-start | bytes 786440 | tf_op jit(solution)/shard_map/ppermute | solution.py:19
  22.2 0.5 %two_backward.1 = (bf16[8,128,256]{2,1,0:T(8,128)(2,1)S(1)}, bf16[2,4,64,128]{3,2,1,0:T(8,128)(2,1)S(1)}, bf16[4,64,128]{2,1,0:T(8,128)(2,1)S(1)}, bf16[4,64,128]{2,1,0:T(8,128)(2,1)S(1)}) custom-call(bf16[16,128,128]{2,1,0:T(8,128)(2,1)S(1)} %get-tuple-element.60.query_head, bf16[16,128,128]{2,1,0:T(8,128)(2,1)S(1)} %get-tuple-element.61.grad_head, ...), custom_call_target="tpu_custom_call" | custom-call | flops 1 | tf_op jit(solution)/shard_map/two_backward/pallas_call | solution.py:404
  22.8 0.5 %collective-permute-start.10 = (bf16[4,64,128]{2,1,0:T(8,128)(2,1)S(1)}, bf16[4,64,128]{2,1,0:T(8,128)(2,1)S(1)}, u32[]{:S(2)}, u32[]{:S(2)}) collective-permute-start(bf16[4,64,128]{2,1,0:T(8,128)(2,1)S(1)} %get-tuple-element.86), channel_id=1, source_target_pairs={{0,16},{16,0},{1,17},{17,1},{2,18},{18,2},{3,19},{19,3},{4,20},{20... | collective-permute-start | bytes 196616 | tf_op jit(solution)/shard_map/ppermute | solution.py:24
  23.3 0.7 %collective-permute-done.9.other_keys = bf16[4,64,128]{2,1,0:T(8,128)(2,1)S(1)} collective-permute-done((bf16[4,64,128]{2,1,0:T(8,128)(2,1)S(1)}, bf16[4,64,128]{2,1,0:T(8,128)(2,1)S(1)}, u32[]{:S(2)}, u32[]{:S(2)}) %collective-permute-start.9) | collective-permute-done | bytes 65568 | tf_op jit(solution)/shard_map/ppermute | solution.py:24
  24.3 3.2 %collective-permute-start.16 = (bf16[2,8,64,128]{3,2,1,0:T(8,128)(2,1)S(1)}, bf16[2,8,64,128]{3,2,1,0:T(8,128)(2,1)S(1)}, u32[]{:S(2)}, u32[]{:S(2)}) collective-permute-start(bf16[2,8,64,128]{3,2,1,0:T(8,128)(2,1)S(1)} %join_two.1.after), channel_id=1, source_target_pairs={{0,14},{1,15},{2,0},{3,1},{4,2},{5,3},{6,4},{7,5},{8,6},{9,7},{10,... | collective-permute-start | bytes 786440 | tf_op jit(solution)/shard_map/ppermute | solution.py:19
  27.9 0.8 %query_grad.1 = (bf16[16,64,128]{2,1,0:T(8,128)(2,1)S(1)}, bf16[16,64,128]{2,1,0:T(8,128)(2,1)S(1)}, bf16[10,64,128]{2,1,0:T(8,128)(2,1)S(1)}, bf16[11,64,128]{2,1,0:T(8,128)(2,1)S(1)}, bf16[11,64,128]{2,1,0:T(8,128)(2,1)S(1)}) custom-call(bf16[2,4,128,128]{3,2,1,0:T(8,128)(2,1)S(1)} %join_own.1.own, ...), custom_call_target="tpu_custom_call" | custom-call | flops 1 | tf_op jit(solution)/shard_map/query_grad/pallas_call | solution.py:404
  28.7 0.5 %collective-permute-start.13 = (bf16[11,64,128]{2,1,0:T(8,128)(2,1)S(1)}, bf16[11,64,128]{2,1,0:T(8,128)(2,1)S(1)}, u32[]{:S(2)}, u32[]{:S(2)}) collective-permute-start(bf16[11,64,128]{2,1,0:T(8,128)(2,1)S(1)} %get-tuple-element.92), channel_id=1, source_target_pairs={{0,16},{16,0},{1,17},{17,1},{2,18},{18,2},{3,19},{19,3},{4,20},{20... | collective-permute-start | bytes 540680 | tf_op jit(solution)/shard_map/ppermute | solution.py:24
  29.4 0.5 %collective-permute-start.15 = (bf16[2,4,64,128]{3,2,1,0:T(8,128)(2,1)S(1)}, bf16[2,4,64,128]{3,2,1,0:T(8,128)(2,1)S(1)}, u32[]{:S(2)}, u32[]{:S(2)}) collective-permute-start(bf16[2,4,64,128]{3,2,1,0:T(8,128)(2,1)S(1)} %get-tuple-element.98), channel_id=1, source_target_pairs={{0,16},{16,0},{1,17},{17,1},{2,18},{18,2},{3,19},{19,3},{4,20},{20... | collective-permute-start | bytes 393224 | tf_op jit(solution)/shard_map/ppermute | solution.py:24
  29.9 0.8 %collective-permute-done.11.first_third = bf16[10,64,128]{2,1,0:T(8,128)(2,1)S(1)} collective-permute-done((bf16[10,64,128]{2,1,0:T(8,128)(2,1)S(1)}, bf16[10,64,128]{2,1,0:T(8,128)(2,1)S(1)}, u32[]{:S(2)}, u32[]{:S(2)}) %collective-permute-start.11) | collective-permute-done | bytes 163872 | tf_op jit(solution)/shard_map/ppermute | solution.py:24
  30.6 1.0 %assemble.1 = (bf16[32,64,128]{2,1,0:T(8,128)(2,1)}, bf16[32,64,128]{2,1,0:T(8,128)(2,1)}, f32[8,128]{1,0:T(8,128)S(1)}) custom-call(bf16[16,64,128]{2,1,0:T(8,128)(2,1)S(1)} %get-tuple-element.88.out_mine, bf16[16,64,128]{2,1,0:T(8,128)(2,1)S(1)} %get-tuple-element.89.query_mine, bf16[10,64,128]{2,1,0:T(8,128)(2,1)S(1)} %collective-permute-done.11.first_third, ...), custom_call_target="tpu_custom_call" | custom-call | flops 1 | tf_op jit(solution)/shard_map/assemble/pallas_call | solution.py:404
  31.7 1.6 %collective-permute-done.16.two_total = bf16[2,8,64,128]{3,2,1,0:T(8,128)(2,1)S(1)} collective-permute-done((bf16[2,8,64,128]{3,2,1,0:T(8,128)(2,1)S(1)}, bf16[2,8,64,128]{3,2,1,0:T(8,128)(2,1)S(1)}, u32[]{:S(2)}, u32[]{:S(2)}) %collective-permute-start.16) | collective-permute-done | bytes 262176 | tf_op jit(solution)/shard_map/ppermute | solution.py:19
  33.3 0.8 %total.1 = (bf16[8,64,128]{2,1,0:T(8,128)(2,1)}, bf16[8,64,128]{2,1,0:T(8,128)(2,1)}) custom-call(f32[2,4,64,128]{3,2,1,0:T(8,128)S(1)} %get-tuple-element.97.sum_mine, bf16[2,4,64,128]{3,2,1,0:T(8,128)(2,1)S(1)} %collective-permute-done.15.sum_other, bf16[2,8,64,128]{3,2,1,0:T(8,128)(2,1)S(1)} %collective-permute-done.16.two_total, ...), custom_call_target="tpu_custom_call" | custom-call | flops 1 | tf_op jit(solution)/shard_map/total/pallas_call | solution.py:404
  (31 shorter events, 2.1 us)
Async XLA Ops:
  0.6 9.0 %copy-start.1 = (bf16[32,64,128]{2,1,0:T(8,128)(2,1)S(1)}, bf16[32,64,128]{2,1,0:T(8,128)(2,1)}, u32[]{:S(2)}) copy-start(bf16[32,64,128]{2,1,0:T(8,128)(2,1)} %grads.3) | copy-start | bytes 1572868
  1.7 8.0 %copy-start = (bf16[32,64,128]{2,1,0:T(8,128)(2,1)S(1)}, bf16[32,64,128]{2,1,0:T(8,128)(2,1)}, u32[]{:S(2)}) copy-start(bf16[32,64,128]{2,1,0:T(8,128)(2,1)} %queries.3) | copy-start | bytes 1572868
  1.7 12.4 %collective-permute-start.3 = (bf16[2,8,64,128]{3,2,1,0:T(8,128)(2,1)S(1)}, bf16[2,8,64,128]{3,2,1,0:T(8,128)(2,1)S(1)}, u32[]{:S(2)}, u32[]{:S(2)}) collective-permute-start(bf16[2,8,64,128]{3,2,1,0:T(8,128)(2,1)S(1)} %pad_maximum_fusion.block.own.after), channel_id=1, source_target_pairs={{0,2},{1,3},{2,4},{3,5},{4,6},{5,7},{6,8},{7,9},{8,10},{9,11},{10,... | collective-permute-start | bytes 786440 | tf_op jit(solution)/shard_map/ppermute | solution.py:19
  4.7 1.3 %collective-permute-start = (bf16[4,64,128]{2,1,0:T(8,128)(2,1)S(1)}, bf16[4,64,128]{2,1,0:T(8,128)(2,1)S(1)}, u32[]{:S(2)}, u32[]{:S(2)}) collective-permute-start(bf16[4,64,128]{2,1,0:T(8,128)(2,1)S(1)} %get-tuple-element.53), channel_id=1, source_target_pairs={{0,16},{16,0},{1,17},{17,1},{2,18},{18,2},{3,19},{19,3},{4,20},{20... | collective-permute-start | bytes 196616 | tf_op jit(solution)/shard_map/ppermute | solution.py:24
  4.8 1.4 %collective-permute-start.1 = (bf16[4,64,128]{2,1,0:T(8,128)(2,1)S(1)}, bf16[4,64,128]{2,1,0:T(8,128)(2,1)S(1)}, u32[]{:S(2)}, u32[]{:S(2)}) collective-permute-start(bf16[4,64,128]{2,1,0:T(8,128)(2,1)S(1)} %get-tuple-element.54), channel_id=1, source_target_pairs={{0,16},{16,0},{1,17},{17,1},{2,18},{18,2},{3,19},{19,3},{4,20},{20... | collective-permute-start | bytes 196616 | tf_op jit(solution)/shard_map/ppermute | solution.py:24
  6.2 10.1 %collective-permute-start.2 = (bf16[2,4,128,128]{3,2,1,0:T(8,128)(2,1)S(1)}, bf16[2,4,128,128]{3,2,1,0:T(8,128)(2,1)S(1)}, u32[]{:S(2)}, u32[]{:S(2)}) collective-permute-start(bf16[2,4,128,128]{3,2,1,0:T(8,128)(2,1)S(1)} %join_own.1.own), channel_id=1, source_target_pairs={{0,1},{1,2},{2,3},{3,4},{4,5},{5,6},{6,7},{7,8},{8,9},{9,10},{10,1... | collective-permute-start | bytes 786440 | tf_op jit(solution)/shard_map/ppermute | solution.py:19
  9.7 2.0 %collective-permute-start.5 = (bf16[11,64,128]{2,1,0:T(8,128)(2,1)S(1)}, bf16[11,64,128]{2,1,0:T(8,128)(2,1)S(1)}, u32[]{:S(2)}, u32[]{:S(2)}) collective-permute-start(bf16[11,64,128]{2,1,0:T(8,128)(2,1)S(1)} %get-tuple-element.56), channel_id=1, source_target_pairs={{0,16},{16,0},{1,17},{17,1},{2,18},{18,2},{3,19},{19,3},{4,20},{20... | collective-permute-start | bytes 540680 | tf_op jit(solution)/shard_map/ppermute | solution.py:24
  9.9 1.8 %collective-permute-start.6 = (bf16[11,64,128]{2,1,0:T(8,128)(2,1)S(1)}, bf16[11,64,128]{2,1,0:T(8,128)(2,1)S(1)}, u32[]{:S(2)}, u32[]{:S(2)}) collective-permute-start(bf16[11,64,128]{2,1,0:T(8,128)(2,1)S(1)} %get-tuple-element.57), channel_id=1, source_target_pairs={{0,16},{16,0},{1,17},{17,1},{2,18},{18,2},{3,19},{19,3},{4,20},{20... | collective-permute-start | bytes 540680 | tf_op jit(solution)/shard_map/ppermute | solution.py:24
  10.3 1.4 %copy-start.2 = (s32[32]{0:T(128)S(1)}, s32[32]{0:T(128)}, u32[]{:S(2)}) copy-start(s32[32]{0:T(128)} %spans.1) | copy-start | bytes 388
  10.3 1.4 %collective-permute-start.4 = (bf16[10,64,128]{2,1,0:T(8,128)(2,1)S(1)}, bf16[10,64,128]{2,1,0:T(8,128)(2,1)S(1)}, u32[]{:S(2)}, u32[]{:S(2)}) collective-permute-start(bf16[10,64,128]{2,1,0:T(8,128)(2,1)S(1)} %get-tuple-element.55), channel_id=1, source_target_pairs={{0,16},{16,0},{1,17},{17,1},{2,18},{18,2},{3,19},{19,3},{4,20},{20... | collective-permute-start | bytes 491528 | tf_op jit(solution)/shard_map/ppermute | solution.py:24
  14.1 1.3 %collective-permute-start.7 = (bf16[4,64,128]{2,1,0:T(8,128)(2,1)S(1)}, bf16[4,64,128]{2,1,0:T(8,128)(2,1)S(1)}, u32[]{:S(2)}, u32[]{:S(2)}) collective-permute-start(bf16[4,64,128]{2,1,0:T(8,128)(2,1)S(1)} %get-tuple-element.63), channel_id=1, source_target_pairs={{0,16},{16,0},{1,17},{17,1},{2,18},{18,2},{3,19},{19,3},{4,20},{20... | collective-permute-start | bytes 196616 | tf_op jit(solution)/shard_map/ppermute | solution.py:24
  14.2 1.4 %collective-permute-start.8 = (bf16[4,64,128]{2,1,0:T(8,128)(2,1)S(1)}, bf16[4,64,128]{2,1,0:T(8,128)(2,1)S(1)}, u32[]{:S(2)}, u32[]{:S(2)}) collective-permute-start(bf16[4,64,128]{2,1,0:T(8,128)(2,1)S(1)} %get-tuple-element.64), channel_id=1, source_target_pairs={{0,16},{16,0},{1,17},{17,1},{2,18},{18,2},{3,19},{19,3},{4,20},{20... | collective-permute-start | bytes 196616 | tf_op jit(solution)/shard_map/ppermute | solution.py:24
  17.7 11.6 %collective-permute-start.14 = (bf16[2,4,128,128]{3,2,1,0:T(8,128)(2,1)S(1)}, bf16[2,4,128,128]{3,2,1,0:T(8,128)(2,1)S(1)}, u32[]{:S(2)}, u32[]{:S(2)}) collective-permute-start(bf16[2,4,128,128]{3,2,1,0:T(8,128)(2,1)S(1)} %get-tuple-element.96), channel_id=1, source_target_pairs={{0,15},{1,0},{2,1},{3,2},{4,3},{5,4},{6,5},{7,6},{8,7},{9,8},{10,9... | collective-permute-start | bytes 786440 | tf_op jit(solution)/shard_map/ppermute | solution.py:19
  22.8 1.3 %collective-permute-start.9 = (bf16[4,64,128]{2,1,0:T(8,128)(2,1)S(1)}, bf16[4,64,128]{2,1,0:T(8,128)(2,1)S(1)}, u32[]{:S(2)}, u32[]{:S(2)}) collective-permute-start(bf16[4,64,128]{2,1,0:T(8,128)(2,1)S(1)} %get-tuple-element.85), channel_id=1, source_target_pairs={{0,16},{16,0},{1,17},{17,1},{2,18},{18,2},{3,19},{19,3},{4,20},{20... | collective-permute-start | bytes 196616 | tf_op jit(solution)/shard_map/ppermute | solution.py:24
  22.8 1.4 %collective-permute-start.10 = (bf16[4,64,128]{2,1,0:T(8,128)(2,1)S(1)}, bf16[4,64,128]{2,1,0:T(8,128)(2,1)S(1)}, u32[]{:S(2)}, u32[]{:S(2)}) collective-permute-start(bf16[4,64,128]{2,1,0:T(8,128)(2,1)S(1)} %get-tuple-element.86), channel_id=1, source_target_pairs={{0,16},{16,0},{1,17},{17,1},{2,18},{18,2},{3,19},{19,3},{4,20},{20... | collective-permute-start | bytes 196616 | tf_op jit(solution)/shard_map/ppermute | solution.py:24
  24.3 9.1 %collective-permute-start.16 = (bf16[2,8,64,128]{3,2,1,0:T(8,128)(2,1)S(1)}, bf16[2,8,64,128]{3,2,1,0:T(8,128)(2,1)S(1)}, u32[]{:S(2)}, u32[]{:S(2)}) collective-permute-start(bf16[2,8,64,128]{3,2,1,0:T(8,128)(2,1)S(1)} %join_two.1.after), channel_id=1, source_target_pairs={{0,14},{1,15},{2,0},{3,1},{4,2},{5,3},{6,4},{7,5},{8,6},{9,7},{10,... | collective-permute-start | bytes 786440 | tf_op jit(solution)/shard_map/ppermute | solution.py:19
  28.7 2.0 %collective-permute-start.12 = (bf16[11,64,128]{2,1,0:T(8,128)(2,1)S(1)}, bf16[11,64,128]{2,1,0:T(8,128)(2,1)S(1)}, u32[]{:S(2)}, u32[]{:S(2)}) collective-permute-start(bf16[11,64,128]{2,1,0:T(8,128)(2,1)S(1)} %get-tuple-element.91), channel_id=1, source_target_pairs={{0,16},{16,0},{1,17},{17,1},{2,18},{18,2},{3,19},{19,3},{4,20},{20... | collective-permute-start | bytes 540680 | tf_op jit(solution)/shard_map/ppermute | solution.py:24
  28.7 1.9 %collective-permute-start.13 = (bf16[11,64,128]{2,1,0:T(8,128)(2,1)S(1)}, bf16[11,64,128]{2,1,0:T(8,128)(2,1)S(1)}, u32[]{:S(2)}, u32[]{:S(2)}) collective-permute-start(bf16[11,64,128]{2,1,0:T(8,128)(2,1)S(1)} %get-tuple-element.92), channel_id=1, source_target_pairs={{0,16},{16,0},{1,17},{17,1},{2,18},{18,2},{3,19},{19,3},{4,20},{20... | collective-permute-start | bytes 540680 | tf_op jit(solution)/shard_map/ppermute | solution.py:24
  29.2 1.4 %collective-permute-start.11 = (bf16[10,64,128]{2,1,0:T(8,128)(2,1)S(1)}, bf16[10,64,128]{2,1,0:T(8,128)(2,1)S(1)}, u32[]{:S(2)}, u32[]{:S(2)}) collective-permute-start(bf16[10,64,128]{2,1,0:T(8,128)(2,1)S(1)} %get-tuple-element.90), channel_id=1, source_target_pairs={{0,16},{16,0},{1,17},{17,1},{2,18},{18,2},{3,19},{19,3},{4,20},{20... | collective-permute-start | bytes 491528 | tf_op jit(solution)/shard_map/ppermute | solution.py:24
  29.4 4.0 %collective-permute-start.15 = (bf16[2,4,64,128]{3,2,1,0:T(8,128)(2,1)S(1)}, bf16[2,4,64,128]{3,2,1,0:T(8,128)(2,1)S(1)}, u32[]{:S(2)}, u32[]{:S(2)}) collective-permute-start(bf16[2,4,64,128]{3,2,1,0:T(8,128)(2,1)S(1)} %get-tuple-element.98), channel_id=1, source_target_pairs={{0,16},{16,0},{1,17},{17,1},{2,18},{18,2},{3,19},{19,3},{4,20},{20... | collective-permute-start | bytes 393224 | tf_op jit(solution)/shard_map/ppermute | solution.py:24

commit v27 on v26

--- a/solution.py
+++ b/solution.py
@@ -250,7 +250,7 @@
         one_part[1, g] = value_part.astype(jnp.bfloat16)
 
     accumulate = accumulator(query_head, grad_head, chunks, groups, store)
-    pipelined(chunks, products, wait, softmax, wait, differentiate, accumulate)
+    pipelined(chunks, products, wait, softmax, differentiate, wait, accumulate)
 
 
 def wait(n, *values):

time: 34.3 us -> 34.3 us (level)
  no operation moved by 1% of the time
where the time goes in v27:
time: 34.3 us; the launch traced here: 34.1 us
  starting transfers between devices  17.6 us (51%)
  Pallas kernels  7.27 us (21%)
  waiting for transfers between devices  6.7 us (20%)
  between operations  1.44 us (4%)
  other arithmetic  1.05 us (3%)
    ppermute x4, starting transfers between devices, shifted(): return lax.ppermute(block, axis, route)  14.1 us
    pallas_call x14, Pallas kernels, call(): pl.pallas_call(kernel, out_shape=tuple((jax.ShapeDtypeStruct(shape, kind)...  7.27 us
    ppermute x13, waiting for transfers between devices, swapped(): return lax.ppermute(block, axis, [(i, count - 1 - i) for i in range(count)])  4.14 us
    ppermute x13, starting transfers between devices, swapped(): return lax.ppermute(block, axis, [(i, count - 1 - i) for i in range(count)])  3.5 us
    ppermute x4, waiting for transfers between devices, shifted(): return lax.ppermute(block, axis, route)  2.56 us
    another operation x1, other arithmetic, shards(): own = jnp.stack([key_matrix, value_matrix])  1.05 us
  transfers between devices with their start and end apart: 17, of which 10 were waited for; matrix products, arithmetic and copies ran while one was open for 0% of the time, Pallas kernels for 15%

profile of v27, /device:TPU:0, one launch (start us, length us, event | category | flops | bytes accessed | tf_op | source)
XLA Modules:
  0.0 34.1 jit_solution(12067798221930012081)
XLA Ops:
  0.6 1.1 %pad_maximum_fusion.block.own.after = bf16[2,8,64,128]{3,2,1,0:T(8,128)(2,1)S(1)} fusion(bf16[1,8,64,128]{3,2,1,0:T(8,128)(2,1)} %bitcast.2, bf16[1,8,64,128]{3,2,1,0:T(8,128)(2,1)} %bitcast.3), kind=kLoop, calls=%fused_computation | loop fusion | flops 131072 | bytes 524288 | tf_op jit(solution)/shard_map/stack | solution.py:427
  1.7 3.0 %collective-permute-start.3 = (bf16[2,8,64,128]{3,2,1,0:T(8,128)(2,1)S(1)}, bf16[2,8,64,128]{3,2,1,0:T(8,128)(2,1)S(1)}, u32[]{:S(2)}, u32[]{:S(2)}) collective-permute-start(bf16[2,8,64,128]{3,2,1,0:T(8,128)(2,1)S(1)} %pad_maximum_fusion.block.own.after), channel_id=1, source_target_pairs={{0,2},{1,3},{2,4},{3,5},{4,6},{5,7},{6,8},{7,9},{8,10},{9,11},{10,... | collective-permute-start | bytes 786440 | tf_op jit(solution)/shard_map/ppermute | solution.py:19
  4.8 0.5 %collective-permute-start.1 = (bf16[4,64,128]{2,1,0:T(8,128)(2,1)S(1)}, bf16[4,64,128]{2,1,0:T(8,128)(2,1)S(1)}, u32[]{:S(2)}, u32[]{:S(2)}) collective-permute-start(bf16[4,64,128]{2,1,0:T(8,128)(2,1)S(1)} %get-tuple-element.54), channel_id=1, source_target_pairs={{0,16},{16,0},{1,17},{17,1},{2,18},{18,2},{3,19},{19,3},{4,20},{20... | collective-permute-start | bytes 196616 | tf_op jit(solution)/shard_map/ppermute | solution.py:24
  5.3 0.7 %collective-permute-done.other_keys = bf16[4,64,128]{2,1,0:T(8,128)(2,1)S(1)} collective-permute-done((bf16[4,64,128]{2,1,0:T(8,128)(2,1)S(1)}, bf16[4,64,128]{2,1,0:T(8,128)(2,1)S(1)}, u32[]{:S(2)}, u32[]{:S(2)}) %collective-permute-start) | collective-permute-done | bytes 65568 | tf_op jit(solution)/shard_map/ppermute | solution.py:24
  6.2 3.4 %collective-permute-start.2 = (bf16[2,4,128,128]{3,2,1,0:T(8,128)(2,1)S(1)}, bf16[2,4,128,128]{3,2,1,0:T(8,128)(2,1)S(1)}, u32[]{:S(2)}, u32[]{:S(2)}) collective-permute-start(bf16[2,4,128,128]{3,2,1,0:T(8,128)(2,1)S(1)} %join_own.1.own), channel_id=1, source_target_pairs={{0,1},{1,2},{2,3},{3,4},{4,5},{5,6},{6,7},{7,8},{8,9},{9,10},{10,1... | collective-permute-start | bytes 786440 | tf_op jit(solution)/shard_map/ppermute | solution.py:19
  11.0 0.7 %collective-permute-done.4.first_third = bf16[10,64,128]{2,1,0:T(8,128)(2,1)S(1)} collective-permute-done((bf16[10,64,128]{2,1,0:T(8,128)(2,1)S(1)}, bf16[10,64,128]{2,1,0:T(8,128)(2,1)S(1)}, u32[]{:S(2)}, u32[]{:S(2)}) %collective-permute-start.4) | collective-permute-done | bytes 163872 | tf_op jit(solution)/shard_map/ppermute | solution.py:24
  11.7 1.4 %own_block.1 = (bf16[16,128,128]{2,1,0:T(8,128)(2,1)S(1)}, bf16[16,128,128]{2,1,0:T(8,128)(2,1)S(1)}, bf16[8,128,256]{2,1,0:T(8,128)(2,1)S(1)}, s32[8,1,256]{2,1...) custom-call(s32[32]{0:T(128)S(1)} %copy-done.2, ...), custom_call_target="tpu_custom_call" | custom-call | flops 1 | tf_op jit(solution)/shard_map/own_block/pallas_call | solution.py:404
  13.2 0.9 %collective-permute-done.3.block.back_two = bf16[2,8,64,128]{3,2,1,0:T(8,128)(2,1)S(1)} collective-permute-done((bf16[2,8,64,128]{3,2,1,0:T(8,128)(2,1)S(1)}, bf16[2,8,64,128]{3,2,1,0:T(8,128)(2,1)S(1)}, u32[]{:S(2)}, u32[]{:S(2)}) %collective-permute-start.3) | collective-permute-done | bytes 262176 | tf_op jit(solution)/shard_map/ppermute | solution.py:19
  14.2 0.5 %collective-permute-start.8 = (bf16[4,64,128]{2,1,0:T(8,128)(2,1)S(1)}, bf16[4,64,128]{2,1,0:T(8,128)(2,1)S(1)}, u32[]{:S(2)}, u32[]{:S(2)}) collective-permute-start(bf16[4,64,128]{2,1,0:T(8,128)(2,1)S(1)} %get-tuple-element.64), channel_id=1, source_target_pairs={{0,16},{16,0},{1,17},{17,1},{2,18},{18,2},{3,19},{19,3},{4,20},{20... | collective-permute-start | bytes 196616 | tf_op jit(solution)/shard_map/ppermute | solution.py:24
  14.7 0.7 %collective-permute-done.7.two_keys = bf16[4,64,128]{2,1,0:T(8,128)(2,1)S(1)} collective-permute-done((bf16[4,64,128]{2,1,0:T(8,128)(2,1)S(1)}, bf16[4,64,128]{2,1,0:T(8,128)(2,1)S(1)}, u32[]{:S(2)}, u32[]{:S(2)}) %collective-permute-start.7) | collective-permute-done | bytes 65568 | tf_op jit(solution)/shard_map/ppermute | solution.py:24
  15.6 0.8 %near_forward.1 = (f32[8,1,256]{2,1,0:T(1,128)S(1)}, f32[8,1,256]{2,1,0:T(1,128)S(1)}, f32[8,128,256]{2,1,0:T(8,128)S(1)}, f32[8,128,256]{2,1,0:T(8,128)S(1)}, f...) custom-call(s32[8,1,256]{2,1,0:T(1,128)S(1)} %get-tuple-element.59.first, ...), custom_call_target="tpu_custom_call" | custom-call | flops 1 | tf_op jit(solution)/shard_map/near_forward/pallas_call | solution.py:404
  16.4 1.4 %last_forward_backward.1 = (bf16[8,128,256]{2,1,0:T(8,128)(2,1)S(1)}, f32[8,1,256]{2,1,0:T(1,128)S(1)}, f32[8,1,256]{2,1,0:T(1,128)S(1)}, bf16[8,128,256]{2,1,0:T(8,128)(2,1)S(1)}, bf16[2,4,128,128]{3,2,1,0:T(8,128)(2,1)S(1)}) custom-call(s32[8,1,256]{2,1,0:T(1,128)S(1)} %get-tuple-element.59.first, bf16[16,128,128]{2,1,0:T(8,128)(2,1)S(1)} %get-tuple-element.60.query_head, ...), custom_call_target="tpu_custom_call" | custom-call | flops 1 | tf_op jit(solution)/shard_map/last_forward_backward/pallas_call | solution.py:404
  17.7 4.5 %collective-permute-start.14 = (bf16[2,4,128,128]{3,2,1,0:T(8,128)(2,1)S(1)}, bf16[2,4,128,128]{3,2,1,0:T(8,128)(2,1)S(1)}, u32[]{:S(2)}, u32[]{:S(2)}) collective-permute-start(bf16[2,4,128,128]{3,2,1,0:T(8,128)(2,1)S(1)} %get-tuple-element.96), channel_id=1, source_target_pairs={{0,15},{1,0},{2,1},{3,2},{4,3},{5,4},{6,5},{7,6},{8,7},{9,8},{10,9... | collective-permute-start | bytes 786440 | tf_op jit(solution)/shard_map/ppermute | solution.py:19
  22.2 0.5 %two_backward.1 = (bf16[8,128,256]{2,1,0:T(8,128)(2,1)S(1)}, bf16[2,4,64,128]{3,2,1,0:T(8,128)(2,1)S(1)}, bf16[4,64,128]{2,1,0:T(8,128)(2,1)S(1)}, bf16[4,64,128]{2,1,0:T(8,128)(2,1)S(1)}) custom-call(bf16[16,128,128]{2,1,0:T(8,128)(2,1)S(1)} %get-tuple-element.60.query_head, bf16[16,128,128]{2,1,0:T(8,128)(2,1)S(1)} %get-tuple-element.61.grad_head, ...), custom_call_target="tpu_custom_call" | custom-call | flops 1 | tf_op jit(solution)/shard_map/two_backward/pallas_call | solution.py:404
  22.8 0.5 %collective-permute-start.10 = (bf16[4,64,128]{2,1,0:T(8,128)(2,1)S(1)}, bf16[4,64,128]{2,1,0:T(8,128)(2,1)S(1)}, u32[]{:S(2)}, u32[]{:S(2)}) collective-permute-start(bf16[4,64,128]{2,1,0:T(8,128)(2,1)S(1)} %get-tuple-element.86), channel_id=1, source_target_pairs={{0,16},{16,0},{1,17},{17,1},{2,18},{18,2},{3,19},{19,3},{4,20},{20... | collective-permute-start | bytes 196616 | tf_op jit(solution)/shard_map/ppermute | solution.py:24
  23.3 0.7 %collective-permute-done.9.other_keys = bf16[4,64,128]{2,1,0:T(8,128)(2,1)S(1)} collective-permute-done((bf16[4,64,128]{2,1,0:T(8,128)(2,1)S(1)}, bf16[4,64,128]{2,1,0:T(8,128)(2,1)S(1)}, u32[]{:S(2)}, u32[]{:S(2)}) %collective-permute-start.9) | collective-permute-done | bytes 65568 | tf_op jit(solution)/shard_map/ppermute | solution.py:24
  24.3 3.2 %collective-permute-start.16 = (bf16[2,8,64,128]{3,2,1,0:T(8,128)(2,1)S(1)}, bf16[2,8,64,128]{3,2,1,0:T(8,128)(2,1)S(1)}, u32[]{:S(2)}, u32[]{:S(2)}) collective-permute-start(bf16[2,8,64,128]{3,2,1,0:T(8,128)(2,1)S(1)} %join_two.1.after), channel_id=1, source_target_pairs={{0,14},{1,15},{2,0},{3,1},{4,2},{5,3},{6,4},{7,5},{8,6},{9,7},{10,... | collective-permute-start | bytes 786440 | tf_op jit(solution)/shard_map/ppermute | solution.py:19
  27.9 0.8 %query_grad.1 = (bf16[16,64,128]{2,1,0:T(8,128)(2,1)S(1)}, bf16[16,64,128]{2,1,0:T(8,128)(2,1)S(1)}, bf16[10,64,128]{2,1,0:T(8,128)(2,1)S(1)}, bf16[11,64,128]{2,1,0:T(8,128)(2,1)S(1)}, bf16[11,64,128]{2,1,0:T(8,128)(2,1)S(1)}) custom-call(bf16[2,4,128,128]{3,2,1,0:T(8,128)(2,1)S(1)} %join_own.1.own, ...), custom_call_target="tpu_custom_call" | custom-call | flops 1 | tf_op jit(solution)/shard_map/query_grad/pallas_call | solution.py:404
  28.7 0.5 %collective-permute-start.13 = (bf16[11,64,128]{2,1,0:T(8,128)(2,1)S(1)}, bf16[11,64,128]{2,1,0:T(8,128)(2,1)S(1)}, u32[]{:S(2)}, u32[]{:S(2)}) collective-permute-start(bf16[11,64,128]{2,1,0:T(8,128)(2,1)S(1)} %get-tuple-element.92), channel_id=1, source_target_pairs={{0,16},{16,0},{1,17},{17,1},{2,18},{18,2},{3,19},{19,3},{4,20},{20... | collective-permute-start | bytes 540680 | tf_op jit(solution)/shard_map/ppermute | solution.py:24
  29.4 0.5 %collective-permute-start.15 = (bf16[2,4,64,128]{3,2,1,0:T(8,128)(2,1)S(1)}, bf16[2,4,64,128]{3,2,1,0:T(8,128)(2,1)S(1)}, u32[]{:S(2)}, u32[]{:S(2)}) collective-permute-start(bf16[2,4,64,128]{3,2,1,0:T(8,128)(2,1)S(1)} %get-tuple-element.98), channel_id=1, source_target_pairs={{0,16},{16,0},{1,17},{17,1},{2,18},{18,2},{3,19},{19,3},{4,20},{20... | collective-permute-start | bytes 393224 | tf_op jit(solution)/shard_map/ppermute | solution.py:24
  29.9 0.8 %collective-permute-done.11.first_third = bf16[10,64,128]{2,1,0:T(8,128)(2,1)S(1)} collective-permute-done((bf16[10,64,128]{2,1,0:T(8,128)(2,1)S(1)}, bf16[10,64,128]{2,1,0:T(8,128)(2,1)S(1)}, u32[]{:S(2)}, u32[]{:S(2)}) %collective-permute-start.11) | collective-permute-done | bytes 163872 | tf_op jit(solution)/shard_map/ppermute | solution.py:24
  30.6 1.0 %assemble.1 = (bf16[32,64,128]{2,1,0:T(8,128)(2,1)}, bf16[32,64,128]{2,1,0:T(8,128)(2,1)}, f32[8,128]{1,0:T(8,128)S(1)}) custom-call(bf16[16,64,128]{2,1,0:T(8,128)(2,1)S(1)} %get-tuple-element.88.out_mine, bf16[16,64,128]{2,1,0:T(8,128)(2,1)S(1)} %get-tuple-element.89.query_mine, bf16[10,64,128]{2,1,0:T(8,128)(2,1)S(1)} %collective-permute-done.11.first_third, ...), custom_call_target="tpu_custom_call" | custom-call | flops 1 | tf_op jit(solution)/shard_map/assemble/pallas_call | solution.py:404
  31.7 1.6 %collective-permute-done.16.two_total = bf16[2,8,64,128]{3,2,1,0:T(8,128)(2,1)S(1)} collective-permute-done((bf16[2,8,64,128]{3,2,1,0:T(8,128)(2,1)S(1)}, bf16[2,8,64,128]{3,2,1,0:T(8,128)(2,1)S(1)}, u32[]{:S(2)}, u32[]{:S(2)}) %collective-permute-start.16) | collective-permute-done | bytes 262176 | tf_op jit(solution)/shard_map/ppermute | solution.py:19
  33.3 0.8 %total.1 = (bf16[8,64,128]{2,1,0:T(8,128)(2,1)}, bf16[8,64,128]{2,1,0:T(8,128)(2,1)}) custom-call(f32[2,4,64,128]{3,2,1,0:T(8,128)S(1)} %get-tuple-element.97.sum_mine, bf16[2,4,64,128]{3,2,1,0:T(8,128)(2,1)S(1)} %collective-permute-done.15.sum_other, bf16[2,8,64,128]{3,2,1,0:T(8,128)(2,1)S(1)} %collective-permute-done.16.two_total, ...), custom_call_target="tpu_custom_call" | custom-call | flops 1 | tf_op jit(solution)/shard_map/total/pallas_call | solution.py:404
  (31 shorter events, 2.1 us)
Async XLA Ops:
  0.6 9.0 %copy-start.1 = (bf16[32,64,128]{2,1,0:T(8,128)(2,1)S(1)}, bf16[32,64,128]{2,1,0:T(8,128)(2,1)}, u32[]{:S(2)}) copy-start(bf16[32,64,128]{2,1,0:T(8,128)(2,1)} %grads.3) | copy-start | bytes 1572868
  1.7 8.0 %copy-start = (bf16[32,64,128]{2,1,0:T(8,128)(2,1)S(1)}, bf16[32,64,128]{2,1,0:T(8,128)(2,1)}, u32[]{:S(2)}) copy-start(bf16[32,64,128]{2,1,0:T(8,128)(2,1)} %queries.3) | copy-start | bytes 1572868
  1.7 12.4 %collective-permute-start.3 = (bf16[2,8,64,128]{3,2,1,0:T(8,128)(2,1)S(1)}, bf16[2,8,64,128]{3,2,1,0:T(8,128)(2,1)S(1)}, u32[]{:S(2)}, u32[]{:S(2)}) collective-permute-start(bf16[2,8,64,128]{3,2,1,0:T(8,128)(2,1)S(1)} %pad_maximum_fusion.block.own.after), channel_id=1, source_target_pairs={{0,2},{1,3},{2,4},{3,5},{4,6},{5,7},{6,8},{7,9},{8,10},{9,11},{10,... | collective-permute-start | bytes 786440 | tf_op jit(solution)/shard_map/ppermute | solution.py:19
  4.7 1.3 %collective-permute-start = (bf16[4,64,128]{2,1,0:T(8,128)(2,1)S(1)}, bf16[4,64,128]{2,1,0:T(8,128)(2,1)S(1)}, u32[]{:S(2)}, u32[]{:S(2)}) collective-permute-start(bf16[4,64,128]{2,1,0:T(8,128)(2,1)S(1)} %get-tuple-element.53), channel_id=1, source_target_pairs={{0,16},{16,0},{1,17},{17,1},{2,18},{18,2},{3,19},{19,3},{4,20},{20... | collective-permute-start | bytes 196616 | tf_op jit(solution)/shard_map/ppermute | solution.py:24
  4.8 1.4 %collective-permute-start.1 = (bf16[4,64,128]{2,1,0:T(8,128)(2,1)S(1)}, bf16[4,64,128]{2,1,0:T(8,128)(2,1)S(1)}, u32[]{:S(2)}, u32[]{:S(2)}) collective-permute-start(bf16[4,64,128]{2,1,0:T(8,128)(2,1)S(1)} %get-tuple-element.54), channel_id=1, source_target_pairs={{0,16},{16,0},{1,17},{17,1},{2,18},{18,2},{3,19},{19,3},{4,20},{20... | collective-permute-start | bytes 196616 | tf_op jit(solution)/shard_map/ppermute | solution.py:24
  6.2 10.1 %collective-permute-start.2 = (bf16[2,4,128,128]{3,2,1,0:T(8,128)(2,1)S(1)}, bf16[2,4,128,128]{3,2,1,0:T(8,128)(2,1)S(1)}, u32[]{:S(2)}, u32[]{:S(2)}) collective-permute-start(bf16[2,4,128,128]{3,2,1,0:T(8,128)(2,1)S(1)} %join_own.1.own), channel_id=1, source_target_pairs={{0,1},{1,2},{2,3},{3,4},{4,5},{5,6},{6,7},{7,8},{8,9},{9,10},{10,1... | collective-permute-start | bytes 786440 | tf_op jit(solution)/shard_map/ppermute | solution.py:19
  9.7 2.0 %collective-permute-start.5 = (bf16[11,64,128]{2,1,0:T(8,128)(2,1)S(1)}, bf16[11,64,128]{2,1,0:T(8,128)(2,1)S(1)}, u32[]{:S(2)}, u32[]{:S(2)}) collective-permute-start(bf16[11,64,128]{2,1,0:T(8,128)(2,1)S(1)} %get-tuple-element.56), channel_id=1, source_target_pairs={{0,16},{16,0},{1,17},{17,1},{2,18},{18,2},{3,19},{19,3},{4,20},{20... | collective-permute-start | bytes 540680 | tf_op jit(solution)/shard_map/ppermute | solution.py:24
  9.9 1.8 %collective-permute-start.6 = (bf16[11,64,128]{2,1,0:T(8,128)(2,1)S(1)}, bf16[11,64,128]{2,1,0:T(8,128)(2,1)S(1)}, u32[]{:S(2)}, u32[]{:S(2)}) collective-permute-start(bf16[11,64,128]{2,1,0:T(8,128)(2,1)S(1)} %get-tuple-element.57), channel_id=1, source_target_pairs={{0,16},{16,0},{1,17},{17,1},{2,18},{18,2},{3,19},{19,3},{4,20},{20... | collective-permute-start | bytes 540680 | tf_op jit(solution)/shard_map/ppermute | solution.py:24
  10.3 1.4 %copy-start.2 = (s32[32]{0:T(128)S(1)}, s32[32]{0:T(128)}, u32[]{:S(2)}) copy-start(s32[32]{0:T(128)} %spans.1) | copy-start | bytes 388
  10.3 1.4 %collective-permute-start.4 = (bf16[10,64,128]{2,1,0:T(8,128)(2,1)S(1)}, bf16[10,64,128]{2,1,0:T(8,128)(2,1)S(1)}, u32[]{:S(2)}, u32[]{:S(2)}) collective-permute-start(bf16[10,64,128]{2,1,0:T(8,128)(2,1)S(1)} %get-tuple-element.55), channel_id=1, source_target_pairs={{0,16},{16,0},{1,17},{17,1},{2,18},{18,2},{3,19},{19,3},{4,20},{20... | collective-permute-start | bytes 491528 | tf_op jit(solution)/shard_map/ppermute | solution.py:24
  14.1 1.3 %collective-permute-start.7 = (bf16[4,64,128]{2,1,0:T(8,128)(2,1)S(1)}, bf16[4,64,128]{2,1,0:T(8,128)(2,1)S(1)}, u32[]{:S(2)}, u32[]{:S(2)}) collective-permute-start(bf16[4,64,128]{2,1,0:T(8,128)(2,1)S(1)} %get-tuple-element.63), channel_id=1, source_target_pairs={{0,16},{16,0},{1,17},{17,1},{2,18},{18,2},{3,19},{19,3},{4,20},{20... | collective-permute-start | bytes 196616 | tf_op jit(solution)/shard_map/ppermute | solution.py:24
  14.2 1.4 %collective-permute-start.8 = (bf16[4,64,128]{2,1,0:T(8,128)(2,1)S(1)}, bf16[4,64,128]{2,1,0:T(8,128)(2,1)S(1)}, u32[]{:S(2)}, u32[]{:S(2)}) collective-permute-start(bf16[4,64,128]{2,1,0:T(8,128)(2,1)S(1)} %get-tuple-element.64), channel_id=1, source_target_pairs={{0,16},{16,0},{1,17},{17,1},{2,18},{18,2},{3,19},{19,3},{4,20},{20... | collective-permute-start | bytes 196616 | tf_op jit(solution)/shard_map/ppermute | solution.py:24
  17.7 11.6 %collective-permute-start.14 = (bf16[2,4,128,128]{3,2,1,0:T(8,128)(2,1)S(1)}, bf16[2,4,128,128]{3,2,1,0:T(8,128)(2,1)S(1)}, u32[]{:S(2)}, u32[]{:S(2)}) collective-permute-start(bf16[2,4,128,128]{3,2,1,0:T(8,128)(2,1)S(1)} %get-tuple-element.96), channel_id=1, source_target_pairs={{0,15},{1,0},{2,1},{3,2},{4,3},{5,4},{6,5},{7,6},{8,7},{9,8},{10,9... | collective-permute-start | bytes 786440 | tf_op jit(solution)/shard_map/ppermute | solution.py:19
  22.8 1.3 %collective-permute-start.9 = (bf16[4,64,128]{2,1,0:T(8,128)(2,1)S(1)}, bf16[4,64,128]{2,1,0:T(8,128)(2,1)S(1)}, u32[]{:S(2)}, u32[]{:S(2)}) collective-permute-start(bf16[4,64,128]{2,1,0:T(8,128)(2,1)S(1)} %get-tuple-element.85), channel_id=1, source_target_pairs={{0,16},{16,0},{1,17},{17,1},{2,18},{18,2},{3,19},{19,3},{4,20},{20... | collective-permute-start | bytes 196616 | tf_op jit(solution)/shard_map/ppermute | solution.py:24
  22.8 1.4 %collective-permute-start.10 = (bf16[4,64,128]{2,1,0:T(8,128)(2,1)S(1)}, bf16[4,64,128]{2,1,0:T(8,128)(2,1)S(1)}, u32[]{:S(2)}, u32[]{:S(2)}) collective-permute-start(bf16[4,64,128]{2,1,0:T(8,128)(2,1)S(1)} %get-tuple-element.86), channel_id=1, source_target_pairs={{0,16},{16,0},{1,17},{17,1},{2,18},{18,2},{3,19},{19,3},{4,20},{20... | collective-permute-start | bytes 196616 | tf_op jit(solution)/shard_map/ppermute | solution.py:24
  24.3 9.1 %collective-permute-start.16 = (bf16[2,8,64,128]{3,2,1,0:T(8,128)(2,1)S(1)}, bf16[2,8,64,128]{3,2,1,0:T(8,128)(2,1)S(1)}, u32[]{:S(2)}, u32[]{:S(2)}) collective-permute-start(bf16[2,8,64,128]{3,2,1,0:T(8,128)(2,1)S(1)} %join_two.1.after), channel_id=1, source_target_pairs={{0,14},{1,15},{2,0},{3,1},{4,2},{5,3},{6,4},{7,5},{8,6},{9,7},{10,... | collective-permute-start | bytes 786440 | tf_op jit(solution)/shard_map/ppermute | solution.py:19
  28.7 2.0 %collective-permute-start.12 = (bf16[11,64,128]{2,1,0:T(8,128)(2,1)S(1)}, bf16[11,64,128]{2,1,0:T(8,128)(2,1)S(1)}, u32[]{:S(2)}, u32[]{:S(2)}) collective-permute-start(bf16[11,64,128]{2,1,0:T(8,128)(2,1)S(1)} %get-tuple-element.91), channel_id=1, source_target_pairs={{0,16},{16,0},{1,17},{17,1},{2,18},{18,2},{3,19},{19,3},{4,20},{20... | collective-permute-start | bytes 540680 | tf_op jit(solution)/shard_map/ppermute | solution.py:24
  28.7 1.9 %collective-permute-start.13 = (bf16[11,64,128]{2,1,0:T(8,128)(2,1)S(1)}, bf16[11,64,128]{2,1,0:T(8,128)(2,1)S(1)}, u32[]{:S(2)}, u32[]{:S(2)}) collective-permute-start(bf16[11,64,128]{2,1,0:T(8,128)(2,1)S(1)} %get-tuple-element.92), channel_id=1, source_target_pairs={{0,16},{16,0},{1,17},{17,1},{2,18},{18,2},{3,19},{19,3},{4,20},{20... | collective-permute-start | bytes 540680 | tf_op jit(solution)/shard_map/ppermute | solution.py:24
  29.2 1.4 %collective-permute-start.11 = (bf16[10,64,128]{2,1,0:T(8,128)(2,1)S(1)}, bf16[10,64,128]{2,1,0:T(8,128)(2,1)S(1)}, u32[]{:S(2)}, u32[]{:S(2)}) collective-permute-start(bf16[10,64,128]{2,1,0:T(8,128)(2,1)S(1)} %get-tuple-element.90), channel_id=1, source_target_pairs={{0,16},{16,0},{1,17},{17,1},{2,18},{18,2},{3,19},{19,3},{4,20},{20... | collective-permute-start | bytes 491528 | tf_op jit(solution)/shard_map/ppermute | solution.py:24
  29.4 4.0 %collective-permute-start.15 = (bf16[2,4,64,128]{3,2,1,0:T(8,128)(2,1)S(1)}, bf16[2,4,64,128]{3,2,1,0:T(8,128)(2,1)S(1)}, u32[]{:S(2)}, u32[]{:S(2)}) collective-permute-start(bf16[2,4,64,128]{3,2,1,0:T(8,128)(2,1)S(1)} %get-tuple-element.98), channel_id=1, source_target_pairs={{0,16},{16,0},{1,17},{17,1},{2,18},{18,2},{3,19},{19,3},{4,20},{20... | collective-permute-start | bytes 393224 | tf_op jit(solution)/shard_map/ppermute | solution.py:24
